TPU v7x, 32 devices: a whole 2x2x4 slice. The times are simulated.
32 devices in a mesh: grp: 2 (over y), blk: 4 (over z), cls: 2 (over x), rot: 2 (over core).
Axes of the slice: x: 2, y: 2, z: 4, core: 2. Of those that a mesh axis runs over, the one named last changes fastest.
Arguments:
- particles: bfloat16 [2304, 128, 128], P(('grp', 'blk'), 'rot'), parts along dimension 0, may hold values from -48 to 48
- references: bfloat16 [16, 128, 128], P(('grp', 'blk', 'cls'), 'rot'), parts along dimension 0, may hold values from -6 to 6
- noise_inv: float32 [64], replicated, may hold values from 0.5 to 2
- prior_rot: int32 [2304], P(('grp', 'blk')), parts along dimension 0, may hold values from 0 to 255
Outputs:
- class_means: float32 [16, 128, 128], P(('grp', 'blk', 'cls'), 'rot'), parts along dimension 0
- log_evidence: float32 [2304], P(('grp', 'blk', 'rot')), parts along dimension 0
There are 2 independent parts, one for each index of `grp`. A program takes and returns all parts, laid end to end along the dimension named above; an argument that names none is the same for every part. Nothing has to cross between parts.
All inputs are finite; a program needn't handle non-finite values.
Results may differ from a plain program's by a relative error of at most 0.0036.
Values may be sent and summed in bfloat16 or wider, within the bound.
No kernel may reach another device: no remote copies, remote signals or barrier semaphores. Data moves between devices by JAX's collectives and lax.ppermute only.
A program may use at most 128 MiB of HBM per device.

v0:
```python
import math

import jax
import jax.numpy as jnp
from jax import lax
from jax.sharding import PartitionSpec as P

ANG = 256
ITERS = 2
SIGMA = 32


shrinkage = 1.0


def freq_scale(freq):
    return jnp.where(freq == 0, 1.0, 2.0).astype(jnp.float32) / ANG


def turn_angle(first, second):
    product = first[:, None] * second[None, :] % ANG
    return product.astype(jnp.float32) * (2.0 * math.pi / ANG)


def pair_up(images, radii):
    flipped = jnp.concatenate([-images[..., radii:], images[..., :radii]], -1)
    return jnp.stack([images, flipped], 1)


def shards(particles, references, noise_inv, prior_rot):
    batch = particles.shape[0]
    half_freq = particles.shape[1]
    depth = particles.shape[2]
    radii = depth // 2
    groups = lax.axis_size("rot")
    group_index = lax.axis_index("rot")
    blocks_blk = lax.axis_size("blk")
    owned = references.shape[0]
    visible = owned * blocks_blk
    own_turns = ANG // groups
    first_turn = group_index * own_turns
    first_freq = group_index * half_freq
    share = batch // groups
    first_row = group_index * share
    doubled = jnp.concatenate([noise_inv, noise_inv])
    every_turn = jnp.arange(ANG, dtype=jnp.int32)
    own_freq = first_freq + jnp.arange(half_freq, dtype=jnp.int32)
    all_rows = jnp.arange(groups * 2 * half_freq, dtype=jnp.int32)
    row_freq = all_rows // (2 * half_freq) * half_freq + all_rows % half_freq
    row_kind = all_rows // half_freq % 2
    own_cols = first_turn + jnp.arange(own_turns, dtype=jnp.int32)
    angles = turn_angle(row_freq, own_cols)
    scale = freq_scale(row_freq)[:, None]
    inverse = jnp.where(row_kind[:, None] == 0, scale * jnp.cos(angles), -scale * jnp.sin(angles))
    back_angles = turn_angle(every_turn, own_freq)
    forward = jnp.concatenate([jnp.cos(back_angles), jnp.sin(back_angles)], 1)
    offset = jnp.abs(own_cols[None, :] - prior_rot[:, None])
    distance = jnp.minimum(offset, ANG - offset).astype(jnp.float32)
    prior_term = -distance * distance / (2.0 * SIGMA * SIGMA)
    paired = pair_up(particles, radii)
    spectra = particles.reshape(batch, 1, half_freq, depth)
    scale_freq = freq_scale(own_freq)
    rows_here = spectra.shape[0]
    freq_blocks = spectra.shape[1]
    block_freq = spectra.shape[2]
    current = references
    for step in range(ITERS):
        source = current
        piece = lax.all_gather(source, "blk", axis=0, tiled=True)
        size = piece.shape[0]
        weighted = (piece.astype(jnp.float32) * doubled).astype(jnp.bfloat16)
        turned = jnp.concatenate([-weighted[..., radii:], weighted[..., :radii]], -1)
        stacked = jnp.stack([weighted, turned], 1).reshape(size, 2, freq_blocks, block_freq, depth)
        partial_value = jnp.einsum(
            "pgfd,kcgfd->pkgcf", spectra, stacked, preferred_element_type=jnp.float32
        )
        partial_value = partial_value.reshape(rows_here, size, freq_blocks * 2 * block_freq)
        correlation = partial_value
        squares = piece.astype(jnp.float32) ** 2 * doubled
        piece_energy = jnp.sum(squares * scale_freq[None, :, None], axis=(1, 2))
        energy = piece_energy
        correlation, energy = (correlation, energy)
        correlation, energy_parts = (
            lax.all_gather(correlation, "rot", axis=2, tiled=True),
            lax.all_gather(energy, "rot", axis=0, tiled=True),
        )
        energy = jnp.sum(energy_parts.reshape(groups, visible), 0)
        inner = jnp.dot(
            correlation.reshape(batch * visible, groups * 2 * half_freq),
            inverse,
            precision=lax.Precision.HIGHEST,
            preferred_element_type=jnp.float32,
        )
        scores = (
            inner.reshape(batch, visible, own_turns)
            - 0.5 * energy[None, :, None]
            + prior_term[:, None, :]
        )
        local_peak = jnp.max(scores, axis=(1, 2))
        summit = lax.pmax(local_peak, ("cls", "rot"))
        weight_sum = lax.psum(
            jnp.sum(jnp.exp(scores - summit[:, None, None]), axis=(1, 2)), ("cls", "rot")
        )
        evidence = summit + jnp.log(weight_sum)
        posterior = jnp.exp(scores - evidence[:, None, None])
        local_counts = jnp.sum(posterior, axis=(0, 2))
        rounded = posterior.astype(jnp.bfloat16)
        every = lax.all_gather(rounded, "rot", axis=2, tiled=True)
        spectrum = jnp.dot(
            every.reshape(batch * visible, ANG).astype(jnp.float32),
            forward,
            precision=lax.Precision.HIGHEST,
            preferred_element_type=jnp.float32,
        )
        spectrum = spectrum.astype(jnp.bfloat16).reshape(batch, visible, 2, half_freq)
        totals = lax.psum_scatter(
            jnp.einsum("pkcf,pcfd->kfd", spectrum, paired, preferred_element_type=jnp.float32),
            "blk",
            scatter_dimension=0,
            tiled=True,
        )
        own_evidence = lax.dynamic_slice_in_dim(evidence, first_row, share, 0)
        counts = lax.psum(local_counts, ("blk", "rot"))
        own_counts = lax.dynamic_slice_in_dim(counts, lax.axis_index("blk") * owned, owned, 0)
        means = totals / (own_counts + shrinkage)[:, None, None]
        current = means.astype(jnp.bfloat16)
    return (means, own_evidence)


def solution(mesh):
    in_specs = (
        P(("grp", "blk"), "rot", None),
        P(("grp", "blk", "cls"), "rot", None),
        P(),
        P(("grp", "blk")),
    )
    out_specs = (P(("grp", "blk", "cls"), "rot", None), P(("grp", "blk", "rot")))
    return jax.shard_map(shards, mesh=mesh, in_specs=in_specs, out_specs=out_specs, check_vma=False)
```

profile of v0, /device:TPU:0, one launch (start us, length us, event | category | flops | bytes accessed | tf_op | source)
XLA Modules:
  0.0 187.3 jit_solution(1432716370018008471)
XLA Ops:
  7.2 0.8 pad_maximum_fusion.11
  8.0 15.1 %all_gather.24 = bf16[4,64,128]{2,1,0:T(8,128)(2,1)S(1)} all-gather(bf16[1,64,128]{2,1,0:T(8,128)(2,1)} %param.5), channel_id=1, replica_groups=mesh['grp'=2,'blk'=4,'cls'=2,'rot'=2] {'blk'}, dimensions={0}, use_global_device_ids=true | all-gather | bytes 81920 | tf_op jit(solution)/shard_map/all_gather | solution.py:69
  23.6 7.5 %fusion.6 = f32[288,4,1,2,64]{0,1,3,4,2:T(4,128)S(1)} fusion(bf16[288,64,128,1]{2,1,0,3:T(8,128)(2,1)} %bitcast.53, bf16[4,1,64,128]{3,0,1,2:T(4,128)(2,1)S(1)} %maximum_bitcast_fusion.1, bf16[4,1,64,128]{3,0,1,2:T(4,128)(2,1)S(1)} %bitcast.60), kind=kOutput, calls=%fused_computation.11 | convolution fusion | flops 38010880 | bytes 5439488 | tf_op jit(solution)/shard_map/pgfd,kcgfd->pkgcf/dot_general | solution.py:74
  31.3 1.1 copy.41
  34.0 2.6 %all-reduce = f32[8]{0:T(128)S(1)} all-reduce(f32[8]{0:T(128)S(1)} %dynamic-update-slice), channel_id=1, replica_groups=mesh['grp'=2,'blk'=4,'cls'=2,'rot'=2] {'rot'}, use_global_device_ids=true, to_apply=%add | all-reduce | flops 8 | bytes 64
  36.9 5.4 %copy.77 = bf16[288,64,128]{2,0,1:T(8,128)(2,1)S(1)} copy(bf16[288,64,128]{2,1,0:T(8,128)(2,1)} %param.4) | data formatting | bytes 9437184 | tf_op args[0]
  42.9 4.2 %slice_negate_fusion = (bf16[288,64,64]{2,0,1:T(8,128)(2,1)S(1)}, bf16[288,64,64]{2,0,1:T(8,128)(2,1)}) fusion(bf16[288,64,128]{2,0,1:T(8,128)(2,1)S(1)} %copy.77), kind=kLoop, calls=%fused_computation.3 | loop fusion | flops 1179648 | bytes 9437184 | tf_op jit(solution)/shard_map/neg | solution.py:26
  47.1 7.2 %maximum_bitcast_fusion = bf16[288,1,64,128]{3,0,1,2:T(8,128)(2,1)} fusion(bf16[288,64,64]{2,0,1:T(8,128)(2,1)} %get-tuple-element.9, bf16[288,64,64]{2,0,1:T(8,128)(2,1)S(1)} %get-tuple-element.8), kind=kLoop, calls=%fused_computation.4 | loop fusion | flops 9437184 | bytes 9437184 | tf_op jit(solution)/shard_map/stack | solution.py:27
  54.3 3.1 %fusion.70 = (f32[288]{0:T(512)S(1)}, f32[288,4,128]{2,0,1:T(8,128)S(1)}) fusion(f32[288,128]{1,0:T(8,128)S(1)} %fusion.21, f32[4]{0:T(128)S(1)} %broadcast_multiply_fusion.1, f32[288,4,256]{2,0,1:T(8,128)} %all-gather.3.cloned.1.call-done, f32[256]{0:T(256)S(1)} %get-tuple-element.29, s32[128]{0:T(128)S(1)} %iota_add_fusion.1, s32[256]{0:T(256)S(1)} %fusion.49, ...), kind=kOutput, calls=%fused_computation.121 | convolution fusion | flops 453983968 | bytes 1921936 | tf_op jit(solution)/shard_map/dot_general | solution.py:88
  57.4 6.9 %pmax.14 = f32[288]{0:T(512)S(1)} all-reduce(f32[288]{0:T(512)S(1)} %get-tuple-element.24), channel_id=1, replica_groups=mesh['grp'=2,'blk'=4,'cls'=2,'rot'=2] {'cls','rot'}, use_global_device_ids=true, to_apply=%region_3.4 | all-reduce | flops 288 | bytes 2304 | tf_op jit(solution)/shard_map/pmax | solution.py:100
  64.6 5.9 %psum.28 = f32[288]{0:T(512)S(1)} all-reduce(f32[288]{0:T(512)S(1)} %exponential_reduce_fusion.1), channel_id=1, replica_groups=mesh['grp'=2,'blk'=4,'cls'=2,'rot'=2] {'cls','rot'}, use_global_device_ids=true, to_apply=%region_5.6 | all-reduce | flops 288 | bytes 2304 | tf_op jit(solution)/shard_map/psum | solution.py:101
  70.8 2.4 %all_gather.27 = bf16[288,4,256]{2,0,1:T(8,128)(2,1)S(1)} all-gather(bf16[288,4,128]{2,0,1:T(8,128)(2,1)S(1)} %get-tuple-element.13), channel_id=1, replica_groups=mesh['grp'=2,'blk'=4,'cls'=2,'rot'=2] {'rot'}, dimensions={2}, use_global_device_ids=true | all-gather | bytes 884736 | tf_op jit(solution)/shard_map/all_gather | solution.py:108
  74.8 0.9 copy.43
  75.7 5.4 %fusion.14 = f32[4,64,128]{2,0,1:T(4,128)S(1)} fusion(bf16[288,4,2,64]{0,1,2,3:T(4,128)(2,1)S(1)} %copy.43, bf16[288,1,64,128]{3,0,1,2:T(8,128)(2,1)} %maximum_bitcast_fusion, bf16[288,1,64,128]{3,0,1,2:T(8,128)(2,1)} %bitcast.55), kind=kOutput, calls=%fused_computation.17 | convolution fusion | flops 42467328 | bytes 9863168 | tf_op jit(solution)/shard_map/pkcf,pcfd->kfd/dot_general | solution.py:117
  81.9 16.8 %psum.29 = f32[4]{0:T(128)S(1)} all-reduce(f32[4]{0:T(128)S(1)} %get-tuple-element.12), channel_id=1, replica_groups=mesh['grp'=2,'blk'=4,'cls'=2,'rot'=2] {'blk','rot'}, use_global_device_ids=true, to_apply=%region_8.9 | all-reduce | flops 4 | bytes 32 | tf_op jit(solution)/shard_map/psum | solution.py:123
  100.0 1.4 reduce-scatter.3.cloned.1.call-done
  101.4 0.8 divide_convert_fusion
  102.1 13.1 %all_gather.28 = bf16[4,64,128]{2,1,0:T(8,128)(2,1)S(1)} all-gather(bf16[1,64,128]{2,1,0:T(8,128)(2,1)S(1)} %divide_convert_fusion), channel_id=1, replica_groups=mesh['grp'=2,'blk'=4,'cls'=2,'rot'=2] {'blk'}, dimensions={0}, use_global_device_ids=true | all-gather | bytes 81920 | tf_op jit(solution)/shard_map/all_gather | solution.py:69
  115.7 7.5 %fusion.9 = f32[288,4,1,2,64]{0,1,3,4,2:T(4,128)S(1)} fusion(bf16[288,64,128,1]{2,1,0,3:T(8,128)(2,1)} %bitcast.54, bf16[4,1,64,128]{3,0,2,1:T(4,128)(2,1)S(1)} %maximum_bitcast_fusion.2, bf16[4,1,64,128]{3,0,2,1:T(4,128)(2,1)S(1)} %bitcast.59), kind=kOutput, calls=%fused_computation.12 | convolution fusion | flops 37814272 | bytes 5439488 | tf_op jit(solution)/shard_map/pgfd,kcgfd->pkgcf/dot_general | solution.py:74
  123.4 1.1 copy.49
  124.8 2.4 %all-reduce.1 = f32[8]{0:T(128)S(1)} all-reduce(f32[8]{0:T(128)S(1)} %dynamic-update-slice.1), channel_id=1, replica_groups=mesh['grp'=2,'blk'=4,'cls'=2,'rot'=2] {'rot'}, use_global_device_ids=true, to_apply=%add.1 | all-reduce | flops 8 | bytes 64
  127.4 4.6 %all-gather.5.cloned.1.call-done = f32[288,4,256]{2,0,1:T(8,128)} async-done(((f32[288,4,128]{2,0,1:T(8,128)}), f32[288,4,256]{2,0,1:T(8,128)}) %all-gather.5.cloned.1.call-update) | async-done | bytes 1179664 | tf_op jit(solution)/shard_map/all_gather | solution.py:84
  132.0 3.1 %fusion.71 = (f32[288]{0:T(512)S(1)}, f32[288,4,128]{2,0,1:T(8,128)S(1)}) fusion(f32[288,128]{1,0:T(8,128)S(1)} %fusion.21, f32[4]{0:T(128)S(1)} %broadcast_multiply_fusion, f32[288,4,256]{2,0,1:T(8,128)} %all-gather.5.cloned.1.call-done, f32[256]{0:T(256)S(1)} %get-tuple-element.29, s32[128]{0:T(128)S(1)} %iota_add_fusion.1, s32[256]{0:T(256)S(1)} %fusion.49, ...), kind=kOutput, calls=%fused_computation.122 | convolution fusion | flops 453983968 | bytes 1921936 | tf_op jit(solution)/shard_map/dot_general | solution.py:88
  135.1 7.5 %pmax.15 = f32[288]{0:T(512)S(1)} all-reduce(f32[288]{0:T(512)S(1)} %get-tuple-element.26), channel_id=1, replica_groups=mesh['grp'=2,'blk'=4,'cls'=2,'rot'=2] {'cls','rot'}, use_global_device_ids=true, to_apply=%region_12.13 | all-reduce | flops 288 | bytes 2304 | tf_op jit(solution)/shard_map/pmax | solution.py:100
  142.9 5.8 %psum.30 = f32[288]{0:T(512)S(1)} all-reduce(f32[288]{0:T(512)S(1)} %exponential_reduce_fusion), channel_id=1, replica_groups=mesh['grp'=2,'blk'=4,'cls'=2,'rot'=2] {'cls','rot'}, use_global_device_ids=true, to_apply=%region_14.15 | all-reduce | flops 288 | bytes 2304 | tf_op jit(solution)/shard_map/psum | solution.py:101
  149.0 2.2 %all_gather.31 = bf16[288,4,256]{2,0,1:T(8,128)(2,1)S(1)} all-gather(bf16[288,4,128]{2,0,1:T(8,128)(2,1)S(1)} %get-tuple-element.11), channel_id=1, replica_groups=mesh['grp'=2,'blk'=4,'cls'=2,'rot'=2] {'rot'}, dimensions={2}, use_global_device_ids=true | all-gather | bytes 884736 | tf_op jit(solution)/shard_map/all_gather | solution.py:108
  151.8 0.7 convolution_convert_fusion
  152.8 0.9 copy.51
  153.8 5.4 %fusion.15 = f32[4,64,128]{2,0,1:T(4,128)S(1)} fusion(bf16[288,4,2,64]{0,1,2,3:T(4,128)(2,1)S(1)} %copy.51, bf16[288,1,64,128]{3,0,1,2:T(8,128)(2,1)} %maximum_bitcast_fusion, bf16[288,1,64,128]{3,0,1,2:T(8,128)(2,1)} %bitcast.56), kind=kOutput, calls=%fused_computation.18 | convolution fusion | flops 42467328 | bytes 9863168 | tf_op jit(solution)/shard_map/pkcf,pcfd->kfd/dot_general | solution.py:117
  159.8 16.8 %psum.31 = f32[4]{0:T(128)S(1)} all-reduce(f32[4]{0:T(128)S(1)} %get-tuple-element.10), channel_id=1, replica_groups=mesh['grp'=2,'blk'=4,'cls'=2,'rot'=2] {'blk','rot'}, use_global_device_ids=true, to_apply=%region_17.18 | all-reduce | flops 4 | bytes 32 | tf_op jit(solution)/shard_map/psum | solution.py:123
  178.6 0.9 reduce-scatter.5.cloned.1.call-done
  179.4 1.4 broadcast_divide_fusion
  (60 shorter events, 10.2 us)
Async XLA Ops:
  7.2 47.1 %all-gather.3.cloned.1.call-start = ((), (), s32[]{:S(2)}) async-start(), calls=%async_computation.2 | async-start | bytes 1769472 | tf_op jit(solution)/shard_map/all_gather | solution.py:84
  23.5 9.0 %copy-start.2 = (u32[32]{0:T(128)S(1)}, u32[32]{0:T(128)}, u32[]{:S(2)}) copy-start(u32[32]{0:T(128)} %constant.128) | copy-start | bytes 388
  23.5 13.2 %copy-start.1 = (s32[288]{0:T(512)S(1)}, s32[288]{0:T(512)}, u32[]{:S(2)}) copy-start(s32[288]{0:T(512)} %param.7) | copy-start | bytes 3460
  32.4 69.0 %reduce-scatter.3.cloned.1.call-start = ((), (), s32[]{:S(2)}) async-start(), calls=%async_computation.3 | async-start | bytes 163840 | tf_op jit(solution)/shard_map/reduce_scatter | solution.py:116
  42.3 4.8 %copy-start = (bf16[288,64,128]{2,0,1:T(8,128)(2,1)}, bf16[288,64,128]{2,0,1:T(8,128)(2,1)S(1)}, u32[]{:S(2)}) copy-start(bf16[288,64,128]{2,0,1:T(8,128)(2,1)S(1)} %copy.77) | copy-start | bytes 14155780
  81.8 50.2 %all-gather.5.cloned.1.call-start = ((), (), s32[]{:S(2)}) async-start(), calls=%async_computation.4 | async-start | bytes 1769472 | tf_op jit(solution)/shard_map/all_gather | solution.py:84
  124.5 54.9 %reduce-scatter.5.cloned.1.call-start = ((), (), s32[]{:S(2)}) async-start(), calls=%async_computation.5 | async-start | bytes 163840 | tf_op jit(solution)/shard_map/reduce_scatter | solution.py:116
Sparse Core Ops, SparseCore 0:
  32.5 10.2 all-gather.2
  82.0 19.3 reduce-scatter.2
  124.7 7.3 all-gather.4
  160.0 19.4 reduce-scatter.4
where the time goes:
time: 188 us; the launch traced here: 187 us
  blocking collectives  97.8 us (52%)
  matrix products  33.4 us (18%)
  other arithmetic  17.2 us (9%)
  between operations  16 us (9%)
  local copies, waits for them, and re-layouts  15.9 us (8%)
  waiting for transfers between devices  6.99 us (4%)
    psum x2, blocking collectives, shards(): counts = lax.psum(local_counts, ('blk', 'rot'))  33.7 us
    all_gather x2, blocking collectives, shards(): piece = lax.all_gather(source, 'blk', axis=0, tiled=True)  28.2 us
    dot_general x2, matrix products, shards(): jnp.einsum('pgfd,kcgfd->pkgcf', spectra, stacked, preferred_element_type=...  15 us
    pmax x2, blocking collectives, shards(): summit = lax.pmax(local_peak, ('cls', 'rot'))  14.5 us
    psum x2, blocking collectives, shards(): lax.psum(jnp.sum(jnp.exp(scores - summit[:, None, None]), axis=(1, 2)), (...  11.7 us
    dot_general x2, matrix products, shards(): jnp.einsum('pkcf,pcfd->kfd', spectrum, paired, preferred_element_type=jnp...  10.8 us
    another operation x1, other arithmetic, pair_up(): return jnp.stack([images, flipped], 1)  7.22 us
    unnamed x12, local copies, waits for them, and re-layouts  6.46 us
  transfers between devices with their start and end apart: 4, of which 3 were waited for; matrix products, arithmetic and copies ran while one was open for 11% of the time, Pallas kernels for 0%

commit v1 on v0

v1 whole, which is shorter than its diff:
```python
import functools
import math

import jax
import jax.numpy as jnp
import numpy as np
from jax import lax
from jax.experimental import pallas as pl
from jax.experimental.pallas import tpu as pltpu
from jax.sharding import PartitionSpec as P

ANG = 256
ITERS = 2
SIGMA = 32

shrinkage = 1.0

F32 = jnp.float32
BF16 = jnp.bfloat16
PAD = 16


def tables(freqs):
    freq = np.arange(freqs)
    turn = np.arange(ANG)
    angle = (turn[:, None] * freq[None, :] % ANG) * (2.0 * math.pi / ANG)
    scale = np.where(freq == 0, 1.0, 2.0) / ANG
    inverse = np.concatenate([scale * np.cos(angle), -scale * np.sin(angle)], 1).astype(np.float32)
    forward = np.concatenate([np.cos(angle), np.sin(angle)], 1).T.astype(np.float32)

    def split(x):
        high = x.astype(BF16)
        return high, (x - high.astype(np.float32)).astype(BF16)

    return split(inverse) + split(forward)


def loop(count, body, unroll):
    while count % unroll:
        unroll -= 1
    if unroll == count:
        for i in range(count):
            body(i)
        return

    def step(outer, carry):
        for inner in range(unroll):
            body(outer * unroll + inner)
        return carry

    lax.fori_loop(0, count // unroll, step, 0)


def params(*shapes):
    total = 0
    for shape, dtype in shapes:
        size = jnp.dtype(dtype).itemsize
        dims = [1, 1, *shape]
        rows = -(-dims[-2] // 16) * 16
        lanes = -(-dims[-1] // 128) * 128
        total += math.prod(dims[:-2]) * rows * lanes * size
    return pltpu.CompilerParams(vmem_limit_bytes=min(total + (4 << 20), 62 << 20))


def vmem(count):
    return [pl.BlockSpec(memory_space=pltpu.VMEM)] * count


def prep_kernel(share, groups, start_ref, particles_ref, *rest):
    outs, (held, wide, sems) = rest[:groups], rest[groups:]
    freqs = particles_ref.shape[1]
    copies = []
    for g in range(groups):
        rows = pl.ds(start_ref[g], share)
        copy = pltpu.make_async_copy(particles_ref.at[rows], held.at[g], sems.at[g])
        copy.start()
        copies.append(copy)
    for g in reversed(range(groups)):
        copies[g].wait()

        def widen(p, g=g):
            wide[pl.ds(pl.multiple_of(p * freqs, 8), freqs), :] = held[g, p].astype(F32)

        loop(share, widen, 8)

        def turn(f, g=g):
            outs[g][f] = wide[pl.ds(f, share, stride=freqs), :].astype(BF16)

        loop(freqs, turn, 8)


def prep(particles, start, share, groups):
    _, freqs, depth = particles.shape
    shape = (freqs, share, depth)
    return pl.pallas_call(
        functools.partial(prep_kernel, share, groups),
        out_shape=[jax.ShapeDtypeStruct(shape, BF16)] * groups,
        in_specs=[pl.BlockSpec(memory_space=pltpu.SMEM), pl.BlockSpec(memory_space=pl.ANY)],
        out_specs=vmem(groups),
        scratch_shapes=[
            pltpu.VMEM((groups, share, freqs, depth), BF16),
            pltpu.VMEM((share * freqs, depth), F32),
            pltpu.SemaphoreType.DMA((groups,)),
        ],
        compiler_params=params(*[(shape, BF16)] * (2 * groups), ((share * freqs, depth), F32)),
        cost_estimate=pl.CostEstimate(
            flops=0, bytes_accessed=4 * groups * math.prod(shape), transcendentals=0
        ),
    )(start, particles)


def em_kernel(groups, sides, blocks, send_type, *refs):
    peers = sides * groups
    refs = list(refs)
    take = lambda n: [refs.pop(0) for _ in range(n)]
    (index_ref,) = take(1)
    particles = take(groups)
    pieces = take(peers)
    doubled_ref, prior_ref, inv_hi, inv_lo, fwd_hi, fwd_lo = take(6)
    outs = take(peers)
    (evidence_ref,) = take(1)
    image, field, energy_ref, count_ref = take(4)
    freqs, share, depth = particles[0].shape
    every = freqs * groups
    classes = sides * blocks
    radii = depth // 2
    start = [
        pl.multiple_of(lax.rem(index_ref[0] + g, groups) * freqs, freqs) for g in range(groups)
    ]
    lane = lax.broadcasted_iota(jnp.int32, (freqs, depth), 1)
    sign = jnp.where(lane < radii, -1.0, 1.0).astype(F32)
    doubled = doubled_ref[...]
    row = lax.broadcasted_iota(jnp.int32, (freqs, depth), 0)

    for side in range(sides):

        def weigh(i, side=side):
            k = side * blocks + i
            energy = jnp.zeros((freqs, depth), F32)
            for g in range(groups):
                plain = pieces[side * groups + g][i].astype(F32)
                scale = jnp.where(row + start[g] == 0, 1.0 / ANG, 2.0 / ANG).astype(F32)
                energy = energy + plain * plain * doubled * scale
                weighted = (plain * doubled).astype(BF16).astype(F32)
                base = k * 2 * every + start[g]
                image[pl.ds(pl.multiple_of(base, 8), freqs), :] = weighted
                image[pl.ds(pl.multiple_of(base + every, 8), freqs), :] = sign * pltpu.roll(
                    weighted, radii, 1
                )
            total = jnp.sum(jnp.sum(energy, axis=0, keepdims=True), axis=1, keepdims=True)
            energy_ref[pl.ds(k, 1), :] = jnp.broadcast_to(total, (1, share))

        loop(blocks, weigh, 4)

    for g in range(groups):

        def correlate(f, g=g):
            rows = pl.ds(start[g] + f, 2 * classes, stride=every)
            field[rows, :] = lax.dot_general(
                image[rows, :].astype(BF16),
                particles[g][f],
                (((1,), (1,)), ((), ())),
                preferred_element_type=F32,
            )

        loop(freqs, correlate, 16)

    turns = lax.broadcasted_iota(jnp.int32, (ANG, share), 0)
    offset = jnp.abs(turns - prior_ref[...])
    distance = jnp.minimum(offset, ANG - offset).astype(F32)
    prior_term = -distance * distance / (2.0 * SIGMA * SIGMA)
    dot = functools.partial(jnp.dot, preferred_element_type=F32)

    def class_rows(k):
        return pl.ds(pl.multiple_of(k * ANG, ANG), ANG)

    def score(k, peak):
        value = field[class_rows(k), :]
        high = value.astype(BF16)
        low = (value - high.astype(F32)).astype(BF16)
        inner = dot(inv_hi[...], high) + (dot(inv_hi[...], low) + dot(inv_lo[...], high))
        scores = inner - 0.5 * energy_ref[pl.ds(k, 1), :] + prior_term
        field[class_rows(k), :] = scores
        return jnp.maximum(peak, jnp.max(scores, axis=0, keepdims=True))

    def weight(k, total):
        value = jnp.exp(field[class_rows(k), :] - peak)
        field[class_rows(k), :] = value
        return total + jnp.sum(value, axis=0, keepdims=True)

    def spectrum(k, carry):
        value = field[class_rows(k), :] * inverse_total
        count = jnp.sum(jnp.sum(value, axis=0, keepdims=True), axis=1, keepdims=True)
        count_ref[pl.ds(k, 1), :] = jnp.broadcast_to(count, (1, depth))
        rounded = value.astype(BF16)
        turned = dot(fwd_hi[...], rounded) + dot(fwd_lo[...], rounded)
        field[class_rows(k), :] = turned
        return carry

    def each(body, init):
        if classes <= 8:
            for k in range(classes):
                init = body(k, init)
            return init
        return lax.fori_loop(0, classes, body, init)

    peak = each(score, jnp.full((1, share), -jnp.inf, F32))
    total = each(weight, jnp.zeros((1, share), F32))
    evidence_ref[...] = peak + jnp.log(total)
    inverse_total = 1.0 / total
    each(spectrum, 0)

    for g in range(groups):

        def accumulate(f, g=g):
            rows = pl.ds(start[g] + f, 2 * classes, stride=every)
            image[rows, :] = dot(field[rows, :].astype(BF16), particles[g][f])

        loop(freqs, accumulate, 16)

    for side in range(sides):

        def finish(i, side=side):
            k = side * blocks + i
            count = count_ref[pl.ds(k, 1), :]
            high = count.astype(BF16).astype(F32)
            spare = lax.broadcasted_iota(jnp.int32, (PAD, depth), 0)
            for g in range(groups):
                out = outs[side * groups + g]
                base = k * 2 * every + start[g]
                plain = image[pl.ds(pl.multiple_of(base, 8), freqs), :]
                other = image[pl.ds(pl.multiple_of(base + every, 8), freqs), :]
                value = plain + sign * pltpu.roll(other, radii, 1)
                out[i, pl.ds(0, freqs), :] = value.astype(out.dtype)
                tail = jnp.where(spare == 0, high, jnp.where(spare == 1, count - high, 0.0))
                out[i, pl.ds(freqs, PAD), :] = tail.astype(out.dtype)

        loop(blocks, finish, 4)


def em(index, particles, pieces, doubled, prior, constants, sides, send_type):
    groups = len(particles)
    freqs, share, depth = particles[0].shape
    blocks = pieces[0].shape[0]
    classes = sides * blocks
    every = freqs * groups
    piece = (blocks, freqs + PAD, depth)
    kinds = [F32] + [send_type] * (sides * groups - 1)
    scratch = [
        ((2 * every * classes, depth), F32),
        ((2 * every * classes, share), F32),
        ((classes, share), F32),
        ((classes, depth), F32),
    ]
    buffers = scratch + [(x.shape, x.dtype) for x in (*particles, *pieces, *constants)]
    return pl.pallas_call(
        functools.partial(em_kernel, groups, sides, blocks, send_type),
        out_shape=[jax.ShapeDtypeStruct(piece, kind) for kind in kinds]
        + [jax.ShapeDtypeStruct((1, share), F32)],
        in_specs=[pl.BlockSpec(memory_space=pltpu.SMEM)]
        + vmem(groups + len(pieces) + 2 + len(constants)),
        out_specs=vmem(len(kinds) + 1),
        scratch_shapes=[pltpu.VMEM(*entry) for entry in scratch],
        compiler_params=params(*buffers, *[(piece, kind) for kind in kinds]),
        cost_estimate=pl.CostEstimate(
            flops=8 * classes * share * every * (depth + 3 * ANG),
            bytes_accessed=2 * every * share * depth,
            transcendentals=classes * share * ANG,
        ),
    )(index, *particles, *pieces, doubled, prior, *constants)


def combine_kernel(count, *refs):
    ins, outs = refs[:count], refs[count:]
    for i, out in enumerate(outs):
        total = ins[0][i].astype(F32)
        for ref in ins[1:]:
            total = total + ref[i].astype(F32)
        out[...] = total


def combine(parts):
    blocks, rows, depth = parts[0].shape
    return pl.pallas_call(
        functools.partial(combine_kernel, len(parts)),
        out_shape=[jax.ShapeDtypeStruct((rows, depth), F32)] * blocks,
        in_specs=vmem(len(parts)),
        out_specs=vmem(blocks),
        compiler_params=params(*[(x.shape, F32) for x in parts], (parts[0].shape, F32)),
    )(*parts)


def means_kernel(count, freqs, *refs):
    ins, (out,) = refs[:count], refs[count:]
    total = ins[0][...]
    for ref in ins[1:]:
        total = total + ref[...]
    counts = total[freqs : freqs + 1, :] + total[freqs + 1 : freqs + 2, :]
    out[0] = (total[:freqs, :] / (counts + shrinkage)).astype(out.dtype)


def class_means(parts, dtype):
    rows, depth = parts[0].shape
    freqs = rows - PAD
    return pl.pallas_call(
        functools.partial(means_kernel, len(parts), freqs),
        out_shape=jax.ShapeDtypeStruct((1, freqs, depth), dtype),
        in_specs=vmem(len(parts)),
        out_specs=pl.BlockSpec(memory_space=pltpu.VMEM),
        compiler_params=params(*[(x.shape, F32) for x in parts], (parts[0].shape, F32)),
    )(*parts)


def shift(value, axes, sizes, step):
    if not any(step):
        return value
    pairs = []
    for there in np.ndindex(*sizes):
        here = tuple((t - s) % n for t, s, n in zip(there, step, sizes))
        pairs.append((int(np.ravel_multi_index(there, sizes)), int(np.ravel_multi_index(here, sizes))))
    return lax.ppermute(value, axes, pairs)


def shards(particles, references, noise_inv, prior_rot):
    batch, freqs, depth = particles.shape
    sides = lax.axis_size("cls")
    groups = lax.axis_size("rot")
    blocks = lax.axis_size("blk")
    side = lax.axis_index("cls")
    group = lax.axis_index("rot")
    half = batch // groups
    share = half // sides
    axes, sizes = ("cls", "rot"), (sides, groups)
    steps = list(np.ndindex(*sizes))

    constants = [jnp.asarray(x) for x in tables(freqs * groups)]
    doubled = jnp.concatenate([noise_inv, noise_inv]).reshape(1, depth)
    index = group.astype(jnp.int32).reshape(1)
    start = (group + jnp.arange(groups, dtype=jnp.int32)) % groups * half + side * share
    prior = lax.dynamic_slice_in_dim(prior_rot, start[0], share, 0).reshape(1, share)

    cut = prep(particles, start, share, groups)
    own = [cut[0]]
    for g in range(1, groups):
        own.append(shift(cut[-g % groups], ("rot",), (groups,), (g,)))

    current = references
    for step in range(ITERS):
        last = step == ITERS - 1
        column = [shift(current, ("blk",), (blocks,), (i,)) for i in range(blocks)]
        column = jnp.concatenate(column, 0)
        pieces = [shift(column, axes, sizes, s) for s in steps]
        *sums, evidence = em(
            index, own, pieces, doubled, prior, constants, sides, F32 if last else BF16
        )
        parts = [shift(x, axes, sizes, tuple(-i for i in s)) for x, s in zip(sums, steps)]
        mine = combine(parts)
        mine = [shift(x, ("blk",), (blocks,), (-i,)) for i, x in enumerate(mine)]
        current = class_means(mine, F32 if last else BF16)
    gathered = jnp.concatenate([shift(evidence, ("cls",), (sides,), (i,)) for i in range(sides)], 0)
    evidence = jnp.roll(gathered, side, 0).reshape(half)
    return current, evidence


def solution(mesh):
    in_specs = (
        P(("grp", "blk"), "rot", None),
        P(("grp", "blk", "cls"), "rot", None),
        P(),
        P(("grp", "blk")),
    )
    out_specs = (P(("grp", "blk", "cls"), "rot", None), P(("grp", "blk", "rot")))
    return jax.shard_map(shards, mesh=mesh, in_specs=in_specs, out_specs=out_specs, check_vma=False)
```

time: 188 us -> 82.8 us (0.44)
  blocking collectives: 97.8 us -> 0 us
  matrix products: 33.4 us -> 0 us
  starting transfers between devices: 0.16 us -> 26.7 us
  waiting for transfers between devices: 6.99 us -> 32.1 us
  Pallas kernels: 0 us -> 19.7 us
  other arithmetic: 17.2 us -> 0.11 us
  between operations: 16 us -> 0.91 us
  local copies, waits for them, and re-layouts: 15.9 us -> 3.12 us
    psum x4 -> x0, blocking collectives: 45.4 us -> none  [the longest x2 33.7 us: shards(): counts = lax.psum(local_counts, ('blk', 'rot'))]
    dot_general x8 -> x0, matrix products: 33.4 us -> none  [the longest x2 15 us: shards(): jnp.einsum('pgfd,kcgfd->pkgcf', spectra, stacked, preferred_element_type=...]
    all_gather x4 -> x0, blocking collectives: 32.9 us -> none  [the longest x2 28.2 us: shards(): piece = lax.all_gather(source, 'blk', axis=0, tiled=True)]
    ppermute x0 -> x26, waiting for transfers between devices: none -> 32.1 us  [shift(): return lax.ppermute(value, axes, pairs)]
    ppermute x0 -> x26, starting transfers between devices: none -> 26.7 us  [shift(): return lax.ppermute(value, axes, pairs)]
    pallas_call x0 -> x7, Pallas kernels: none -> 19.7 us  [the longest x2 13.6 us: em(): pl.pallas_call(functools.partial(em_kernel, groups, sides, blocks, send_t...]
    pmax x2 -> x0, blocking collectives: 14.5 us -> none  [shards(): summit = lax.pmax(local_peak, ('cls', 'rot'))]
    another operation x3 -> x0, other arithmetic: 7.45 us -> none  [the longest x1 7.22 us: pair_up(): return jnp.stack([images, flipped], 1)]
  transfers between devices with their start and end apart: 4 -> 26, of which waited for: 3 -> 18; matrix products, arithmetic and copies ran while one was open for 11% -> 1% of each run, Pallas kernels for 0% -> 0%
where the time goes in v1:
time: 82.8 us; the launch traced here: 82.7 us
  waiting for transfers between devices  32.1 us (39%)
  starting transfers between devices  26.7 us (32%)
  Pallas kernels  19.7 us (24%)
  local copies, waits for them, and re-layouts  3.12 us (4%)
  between operations  0.91 us (1%)
    ppermute x26, waiting for transfers between devices, shift(): return lax.ppermute(value, axes, pairs)  32.1 us
    ppermute x26, starting transfers between devices, shift(): return lax.ppermute(value, axes, pairs)  26.7 us
    pallas_call x2, Pallas kernels, em(): pl.pallas_call(functools.partial(em_kernel, groups, sides, blocks, send_t...  13.6 us
    pallas_call x1, Pallas kernels, prep(): pl.pallas_call(functools.partial(prep_kernel, share, groups), out_shape=[...  5.35 us
    unnamed x19, local copies, waits for them, and re-layouts  2.39 us
  transfers between devices with their start and end apart: 26, of which 18 were waited for; matrix products, arithmetic and copies ran while one was open for 1% of the time, Pallas kernels for 0%

profile of v1, /device:TPU:0, one launch (start us, length us, event | category | flops | bytes accessed | tf_op | source)
XLA Modules:
  0.0 82.7 jit_solution(7500298724345514842)
XLA Ops:
  0.7 2.3 %copy-done.1 = bf16[288,64,128]{2,1,0:T(8,128)(2,1)S(1)} copy-done((bf16[288,64,128]{2,1,0:T(8,128)(2,1)S(1)}, bf16[288,64,128]{2,1,0:T(8,128)(2,1)}, u32[]{:S(2)}) %copy-start.1) | copy-done | bytes 4718616
  3.0 5.3 %shard_map.95 = (bf16[64,72,128]{2,1,0:T(8,128)(2,1)S(1)}, bf16[64,72,128]{2,1,0:T(8,128)(2,1)}) custom-call(s32[2]{0:T(128)S(1)} %fusion.1.start_ref, bf16[288,64,128]{2,1,0:T(8,128)(2,1)S(1)} %copy-done.1), custom_call_target="tpu_custom_call" | custom-call | bytes 4718592 | tf_op jit(solution)/shard_map/pallas_call | solution.py:95
  8.9 4.7 %collective-permute-start.1 = (bf16[1,64,128]{2,1,0:T(8,128)(2,1)S(1)}, bf16[1,64,128]{2,1,0:T(8,128)(2,1)S(1)}, u32[]{:S(2)}, u32[]{:S(2)}) collective-permute-start(bf16[1,64,128]{2,1,0:T(8,128)(2,1)S(1)} %copy-done.6), channel_id=1, source_target_pairs={{0,12},{4,0},{8,4},{12,8},{1,13},{5,1},{9,5},{13,9},{2,14},{6,2},{... | collective-permute-start | bytes 49160 | tf_op jit(solution)/shard_map/ppermute | solution.py:321
  13.6 1.0 %collective-permute-start.3 = (bf16[1,64,128]{2,1,0:T(8,128)(2,1)S(1)}, bf16[1,64,128]{2,1,0:T(8,128)(2,1)S(1)}, u32[]{:S(2)}, u32[]{:S(2)}) collective-permute-start(bf16[1,64,128]{2,1,0:T(8,128)(2,1)S(1)} %copy-done.6), channel_id=1, source_target_pairs={{0,4},{4,8},{8,12},{12,0},{1,5},{5,9},{9,13},{13,1},{2,6},{6,10},{... | collective-permute-start | bytes 49160 | tf_op jit(solution)/shard_map/ppermute | solution.py:321
  15.0 3.2 %collective-permute-done.2 = bf16[1,64,128]{2,1,0:T(8,128)(2,1)S(1)} collective-permute-done((bf16[1,64,128]{2,1,0:T(8,128)(2,1)S(1)}, bf16[1,64,128]{2,1,0:T(8,128)(2,1)S(1)}, u32[]{:S(2)}, u32[]{:S(2)}) %collective-permute-start.2) | collective-permute-done | bytes 16416 | tf_op jit(solution)/shard_map/ppermute | solution.py:321
  18.2 0.9 %collective-permute-done.3 = bf16[1,64,128]{2,1,0:T(8,128)(2,1)S(1)} collective-permute-done((bf16[1,64,128]{2,1,0:T(8,128)(2,1)S(1)}, bf16[1,64,128]{2,1,0:T(8,128)(2,1)S(1)}, u32[]{:S(2)}, u32[]{:S(2)}) %collective-permute-start.3) | collective-permute-done | bytes 16416 | tf_op jit(solution)/shard_map/ppermute | solution.py:321
  19.1 1.5 %collective-permute-start.5 = (bf16[4,64,128]{2,1,0:T(8,128)(2,1)S(1)}, bf16[4,64,128]{2,1,0:T(8,128)(2,1)S(1)}, u32[]{:S(2)}, u32[]{:S(2)}) collective-permute-start(bf16[4,64,128]{2,1,0:T(8,128)(2,1)S(1)} %constant_dynamic-update-slice_fusion.refs_3_), channel_id=1, source_target_pairs={{0,2},{1,3},{2,0},{3,1},{4,6},{5,7},{6,4},{7,5},{8,10},{9,11},{10,... | collective-permute-start | bytes 196616 | tf_op jit(solution)/shard_map/ppermute | solution.py:321
  21.1 2.6 %collective-permute-done.5.refs_5_ = bf16[4,64,128]{2,1,0:T(8,128)(2,1)S(1)} collective-permute-done((bf16[4,64,128]{2,1,0:T(8,128)(2,1)S(1)}, bf16[4,64,128]{2,1,0:T(8,128)(2,1)S(1)}, u32[]{:S(2)}, u32[]{:S(2)}) %collective-permute-start.5) | collective-permute-done | bytes 65568 | tf_op jit(solution)/shard_map/ppermute | solution.py:321
  23.6 1.2 %collective-permute-done.6.refs_6_ = bf16[4,64,128]{2,1,0:T(8,128)(2,1)S(1)} collective-permute-done((bf16[4,64,128]{2,1,0:T(8,128)(2,1)S(1)}, bf16[4,64,128]{2,1,0:T(8,128)(2,1)S(1)}, u32[]{:S(2)}, u32[]{:S(2)}) %collective-permute-start.6) | collective-permute-done | bytes 65568 | tf_op jit(solution)/shard_map/ppermute | solution.py:321
  24.9 6.9 %shard_map.96 = (f32[4,80,128]{2,1,0:T(8,128)S(1)}, bf16[4,80,128]{2,1,0:T(8,128)(2,1)S(1)}, bf16[4,80,128]{2,1,0:T(8,128)(2,1)S(1)}, bf16[4,80,128]{2,1,0:T(8,128)(2,1)S(1)}, f32[1,72]{1,0:T(1,128)}) custom-call(s32[1]{0:T(128)} %bitcast.refs_0_, bf16[64,72,128]{2,1,0:T(8,128)(2,1)S(1)} %get-tuple-element.21.refs_1_, ...), custom_call_target="tpu_custom_call" | custom-call | flops 528482304 | bytes 2359296 | tf_op jit(solution)/shard_map/pallas_call | solution.py:256
  31.8 1.4 %collective-permute-start.8 = (bf16[4,80,128]{2,1,0:T(8,128)(2,1)S(1)}, bf16[4,80,128]{2,1,0:T(8,128)(2,1)S(1)}, u32[]{:S(2)}, u32[]{:S(2)}) collective-permute-start(bf16[4,80,128]{2,1,0:T(8,128)(2,1)S(1)} %get-tuple-element.25), channel_id=1, source_target_pairs={{0,2},{1,3},{2,0},{3,1},{4,6},{5,7},{6,4},{7,5},{8,10},{9,11},{10,... | collective-permute-start | bytes 245768 | tf_op jit(solution)/shard_map/ppermute | solution.py:321
  33.6 3.4 %collective-permute-done.8.refs_2_ = bf16[4,80,128]{2,1,0:T(8,128)(2,1)S(1)} collective-permute-done((bf16[4,80,128]{2,1,0:T(8,128)(2,1)S(1)}, bf16[4,80,128]{2,1,0:T(8,128)(2,1)S(1)}, u32[]{:S(2)}, u32[]{:S(2)}) %collective-permute-start.8) | collective-permute-done | bytes 81952 | tf_op jit(solution)/shard_map/ppermute | solution.py:321
  36.9 1.0 %collective-permute-done.9.refs_3_ = bf16[4,80,128]{2,1,0:T(8,128)(2,1)S(1)} collective-permute-done((bf16[4,80,128]{2,1,0:T(8,128)(2,1)S(1)}, bf16[4,80,128]{2,1,0:T(8,128)(2,1)S(1)}, u32[]{:S(2)}, u32[]{:S(2)}) %collective-permute-start.9) | collective-permute-done | bytes 81952 | tf_op jit(solution)/shard_map/ppermute | solution.py:321
  38.1 1.2 %collective-permute-start.11 = (f32[80,128]{1,0:T(8,128)S(1)}, f32[80,128]{1,0:T(8,128)S(1)}, u32[]{:S(2)}, u32[]{:S(2)}) collective-permute-start(f32[80,128]{1,0:T(8,128)S(1)} %get-tuple-element.29), channel_id=1, source_target_pairs={{0,8},{4,12},{8,0},{12,4},{1,9},{5,13},{9,1},{13,5},{2,10},{6,14},... | collective-permute-start | bytes 122888 | tf_op jit(solution)/shard_map/ppermute | solution.py:321
  39.3 2.8 %collective-permute-start.12 = (f32[80,128]{1,0:T(8,128)S(1)}, f32[80,128]{1,0:T(8,128)S(1)}, u32[]{:S(2)}, u32[]{:S(2)}) collective-permute-start(f32[80,128]{1,0:T(8,128)S(1)} %get-tuple-element.30), channel_id=1, source_target_pairs={{0,12},{4,0},{8,4},{12,8},{1,13},{5,1},{9,5},{13,9},{2,14},{6,2},{... | collective-permute-start | bytes 122888 | tf_op jit(solution)/shard_map/ppermute | solution.py:321
  42.1 2.2 %collective-permute-done.10.refs_1_ = f32[80,128]{1,0:T(8,128)S(1)} collective-permute-done((f32[80,128]{1,0:T(8,128)S(1)}, f32[80,128]{1,0:T(8,128)S(1)}, u32[]{:S(2)}, u32[]{:S(2)}) %collective-permute-start.10) | collective-permute-done | bytes 40992 | tf_op jit(solution)/shard_map/ppermute | solution.py:321
  45.0 1.6 %collective-permute-start.15 = (bf16[1,64,128]{2,1,0:T(8,128)(2,1)S(1)}, bf16[1,64,128]{2,1,0:T(8,128)(2,1)S(1)}, u32[]{:S(2)}, u32[]{:S(2)}) collective-permute-start(bf16[1,64,128]{2,1,0:T(8,128)(2,1)S(1)} %shard_map.98), channel_id=1, source_target_pairs={{0,4},{4,8},{8,12},{12,0},{1,5},{5,9},{9,13},{13,1},{2,6},{6,10},{... | collective-permute-start | bytes 49160 | tf_op jit(solution)/shard_map/ppermute | solution.py:321
  46.5 2.0 %collective-permute-start.14 = (bf16[1,64,128]{2,1,0:T(8,128)(2,1)S(1)}, bf16[1,64,128]{2,1,0:T(8,128)(2,1)S(1)}, u32[]{:S(2)}, u32[]{:S(2)}) collective-permute-start(bf16[1,64,128]{2,1,0:T(8,128)(2,1)S(1)} %shard_map.98), channel_id=1, source_target_pairs={{0,8},{4,12},{8,0},{12,4},{1,9},{5,13},{9,1},{13,5},{2,10},{6,14},... | collective-permute-start | bytes 49160 | tf_op jit(solution)/shard_map/ppermute | solution.py:321
  49.0 1.6 %collective-permute-done.15 = bf16[1,64,128]{2,1,0:T(8,128)(2,1)S(1)} collective-permute-done((bf16[1,64,128]{2,1,0:T(8,128)(2,1)S(1)}, bf16[1,64,128]{2,1,0:T(8,128)(2,1)S(1)}, u32[]{:S(2)}, u32[]{:S(2)}) %collective-permute-start.15) | collective-permute-done | bytes 16416 | tf_op jit(solution)/shard_map/ppermute | solution.py:321
  51.2 1.1 %collective-permute-done.13 = bf16[1,64,128]{2,1,0:T(8,128)(2,1)S(1)} collective-permute-done((bf16[1,64,128]{2,1,0:T(8,128)(2,1)S(1)}, bf16[1,64,128]{2,1,0:T(8,128)(2,1)S(1)}, u32[]{:S(2)}, u32[]{:S(2)}) %collective-permute-start.13) | collective-permute-done | bytes 16416 | tf_op jit(solution)/shard_map/ppermute | solution.py:321
  52.4 1.0 %collective-permute-start.17 = (bf16[4,64,128]{2,1,0:T(8,128)(2,1)S(1)}, bf16[4,64,128]{2,1,0:T(8,128)(2,1)S(1)}, u32[]{:S(2)}, u32[]{:S(2)}) collective-permute-start(bf16[4,64,128]{2,1,0:T(8,128)(2,1)S(1)} %pad_maximum_fusion.refs_3_), channel_id=1, source_target_pairs={{0,2},{1,3},{2,0},{3,1},{4,6},{5,7},{6,4},{7,5},{8,10},{9,11},{10,... | collective-permute-start | bytes 196616 | tf_op jit(solution)/shard_map/ppermute | solution.py:321
  53.4 0.9 %collective-permute-start.18 = (bf16[4,64,128]{2,1,0:T(8,128)(2,1)S(1)}, bf16[4,64,128]{2,1,0:T(8,128)(2,1)S(1)}, u32[]{:S(2)}, u32[]{:S(2)}) collective-permute-start(bf16[4,64,128]{2,1,0:T(8,128)(2,1)S(1)} %pad_maximum_fusion.refs_3_), channel_id=1, source_target_pairs={{0,3},{1,2},{2,1},{3,0},{4,7},{5,6},{6,5},{7,4},{8,11},{9,10},{10,... | collective-permute-start | bytes 196616 | tf_op jit(solution)/shard_map/ppermute | solution.py:321
  54.3 3.1 %collective-permute-done.17.refs_5_ = bf16[4,64,128]{2,1,0:T(8,128)(2,1)S(1)} collective-permute-done((bf16[4,64,128]{2,1,0:T(8,128)(2,1)S(1)}, bf16[4,64,128]{2,1,0:T(8,128)(2,1)S(1)}, u32[]{:S(2)}, u32[]{:S(2)}) %collective-permute-start.17) | collective-permute-done | bytes 65568 | tf_op jit(solution)/shard_map/ppermute | solution.py:321
  57.9 6.8 %shard_map.99 = (f32[4,80,128]{2,1,0:T(8,128)S(1)}, f32[4,80,128]{2,1,0:T(8,128)S(1)}, f32[4,80,128]{2,1,0:T(8,128)S(1)}, f32[4,80,128]{2,1,0:T(8,128)S(1)}, f32[1,72]{1,0:T(1,128)S(1)}) custom-call(s32[1]{0:T(128)} %bitcast.refs_0_, bf16[64,72,128]{2,1,0:T(8,128)(2,1)S(1)} %get-tuple-element.21.refs_1_, ...), custom_call_target="tpu_custom_call" | custom-call | flops 528482304 | bytes 2359296 | tf_op jit(solution)/shard_map/pallas_call | solution.py:256
  65.0 0.9 %collective-permute-start.20 = (f32[4,80,128]{2,1,0:T(8,128)S(1)}, f32[4,80,128]{2,1,0:T(8,128)S(1)}, u32[]{:S(2)}, u32[]{:S(2)}) collective-permute-start(f32[4,80,128]{2,1,0:T(8,128)S(1)} %get-tuple-element.33), channel_id=1, source_target_pairs={{0,2},{1,3},{2,0},{3,1},{4,6},{5,7},{6,4},{7,5},{8,10},{9,11},{10,... | collective-permute-start | bytes 491528 | tf_op jit(solution)/shard_map/ppermute | solution.py:321
  66.6 1.0 %collective-permute-start.25 = (f32[1,72]{1,0:T(1,128)S(1)}, f32[1,72]{1,0:T(1,128)S(1)}, u32[]{:S(2)}, u32[]{:S(2)}) collective-permute-start(f32[1,72]{1,0:T(1,128)S(1)} %get-tuple-element.39), channel_id=1, source_target_pairs={{0,2},{2,0},{1,3},{3,1},{4,6},{6,4},{5,7},{7,5},{8,10},{10,8},{9,1... | collective-permute-start | bytes 872 | tf_op jit(solution)/shard_map/ppermute | solution.py:321
  67.5 7.3 %collective-permute-done.25 = f32[1,72]{1,0:T(1,128)S(1)} collective-permute-done((f32[1,72]{1,0:T(1,128)S(1)}, f32[1,72]{1,0:T(1,128)S(1)}, u32[]{:S(2)}, u32[]{:S(2)}) %collective-permute-start.25) | collective-permute-done | bytes 320 | tf_op jit(solution)/shard_map/ppermute | solution.py:321
  74.9 0.9 %collective-permute-start.22 = (f32[80,128]{1,0:T(8,128)S(1)}, f32[80,128]{1,0:T(8,128)S(1)}, u32[]{:S(2)}, u32[]{:S(2)}) collective-permute-start(f32[80,128]{1,0:T(8,128)S(1)} %get-tuple-element.36), channel_id=1, source_target_pairs={{0,4},{4,8},{8,12},{12,0},{1,5},{5,9},{9,13},{13,1},{2,6},{6,10},{... | collective-permute-start | bytes 122888 | tf_op jit(solution)/shard_map/ppermute | solution.py:321
  75.8 2.0 %collective-permute-start.23 = (f32[80,128]{1,0:T(8,128)S(1)}, f32[80,128]{1,0:T(8,128)S(1)}, u32[]{:S(2)}, u32[]{:S(2)}) collective-permute-start(f32[80,128]{1,0:T(8,128)S(1)} %get-tuple-element.37), channel_id=1, source_target_pairs={{0,8},{4,12},{8,0},{12,4},{1,9},{5,13},{9,1},{13,5},{2,10},{6,14},... | collective-permute-start | bytes 122888 | tf_op jit(solution)/shard_map/ppermute | solution.py:321
  77.8 1.0 %collective-permute-start.24 = (f32[80,128]{1,0:T(8,128)S(1)}, f32[80,128]{1,0:T(8,128)S(1)}, u32[]{:S(2)}, u32[]{:S(2)}) collective-permute-start(f32[80,128]{1,0:T(8,128)S(1)} %get-tuple-element.38), channel_id=1, source_target_pairs={{0,12},{4,0},{8,4},{12,8},{1,13},{5,1},{9,5},{13,9},{2,14},{6,2},{... | collective-permute-start | bytes 122888 | tf_op jit(solution)/shard_map/ppermute | solution.py:321
  79.4 1.5 %collective-permute-done.22.refs_1_ = f32[80,128]{1,0:T(8,128)S(1)} collective-permute-done((f32[80,128]{1,0:T(8,128)S(1)}, f32[80,128]{1,0:T(8,128)S(1)}, u32[]{:S(2)}, u32[]{:S(2)}) %collective-permute-start.22) | collective-permute-done | bytes 40992 | tf_op jit(solution)/shard_map/ppermute | solution.py:321
  80.9 0.9 %collective-permute-done.23.refs_2_ = f32[80,128]{1,0:T(8,128)S(1)} collective-permute-done((f32[80,128]{1,0:T(8,128)S(1)}, f32[80,128]{1,0:T(8,128)S(1)}, u32[]{:S(2)}, u32[]{:S(2)}) %collective-permute-start.23) | collective-permute-done | bytes 40992 | tf_op jit(solution)/shard_map/ppermute | solution.py:321
  (54 shorter events, 6.6 us)
Async XLA Ops:
  0.6 20.4 %copy-start = (s32[288]{0:T(512)S(1)}, s32[288]{0:T(512)}, u32[]{:S(2)}) copy-start(s32[288]{0:T(512)} %param.11) | copy-start | bytes 3460
  3.0 11.6 %copy-start.7 = (f32[64]{0:T(128)S(1)}, f32[64]{0:T(128)}, u32[]{:S(2)}) copy-start(f32[64]{0:T(128)} %param.10) | copy-start | bytes 772
  3.0 21.8 %copy-start.2 = (bf16[256,256]{1,0:T(8,128)(2,1)S(1)}, bf16[256,256]{1,0:T(8,128)(2,1)}, u32[]{:S(2)}) copy-start(bf16[256,256]{1,0:T(8,128)(2,1)} %constant.52.clone.refs_9_) | copy-start | bytes 393220
  3.0 21.8 %copy-start.3 = (bf16[256,256]{1,0:T(8,128)(2,1)S(1)}, bf16[256,256]{1,0:T(8,128)(2,1)}, u32[]{:S(2)}) copy-start(bf16[256,256]{1,0:T(8,128)(2,1)} %constant.53.clone.refs_10_) | copy-start | bytes 393220
  3.0 21.8 %copy-start.4 = (bf16[256,256]{1,0:T(8,128)(2,1)S(1)}, bf16[256,256]{1,0:T(8,128)(2,1)}, u32[]{:S(2)}) copy-start(bf16[256,256]{1,0:T(8,128)(2,1)} %constant.54.clone.refs_11_) | copy-start | bytes 393220
  3.0 21.8 %copy-start.5 = (bf16[256,256]{1,0:T(8,128)(2,1)S(1)}, bf16[256,256]{1,0:T(8,128)(2,1)}, u32[]{:S(2)}) copy-start(bf16[256,256]{1,0:T(8,128)(2,1)} %constant.55.clone.refs_12_) | copy-start | bytes 393220
  8.4 16.4 %collective-permute-start = (bf16[64,72,128]{2,1,0:T(8,128)(2,1)}, bf16[64,72,128]{2,1,0:T(8,128)(2,1)S(1)}, u32[]{:S(2)}, u32[]{:S(2)}) collective-permute-start(bf16[64,72,128]{2,1,0:T(8,128)(2,1)} %get-tuple-element.22), channel_id=1, source_target_pairs={{0,1},{1,0},{2,3},{3,2},{4,5},{5,4},{6,7},{7,6},{8,9},{9,8},{10,11... | collective-permute-start | bytes 3538952 | tf_op jit(solution)/shard_map/ppermute | solution.py:321
  8.9 6.1 %collective-permute-start.1 = (bf16[1,64,128]{2,1,0:T(8,128)(2,1)S(1)}, bf16[1,64,128]{2,1,0:T(8,128)(2,1)S(1)}, u32[]{:S(2)}, u32[]{:S(2)}) collective-permute-start(bf16[1,64,128]{2,1,0:T(8,128)(2,1)S(1)} %copy-done.6), channel_id=1, source_target_pairs={{0,12},{4,0},{8,4},{12,8},{1,13},{5,1},{9,5},{13,9},{2,14},{6,2},{... | collective-permute-start | bytes 49160 | tf_op jit(solution)/shard_map/ppermute | solution.py:321
  13.6 4.6 %collective-permute-start.2 = (bf16[1,64,128]{2,1,0:T(8,128)(2,1)S(1)}, bf16[1,64,128]{2,1,0:T(8,128)(2,1)S(1)}, u32[]{:S(2)}, u32[]{:S(2)}) collective-permute-start(bf16[1,64,128]{2,1,0:T(8,128)(2,1)S(1)} %copy-done.6), channel_id=1, source_target_pairs={{0,8},{4,12},{8,0},{12,4},{1,9},{5,13},{9,1},{13,5},{2,10},{6,14},... | collective-permute-start | bytes 49160 | tf_op jit(solution)/shard_map/ppermute | solution.py:321
  13.6 5.5 %collective-permute-start.3 = (bf16[1,64,128]{2,1,0:T(8,128)(2,1)S(1)}, bf16[1,64,128]{2,1,0:T(8,128)(2,1)S(1)}, u32[]{:S(2)}, u32[]{:S(2)}) collective-permute-start(bf16[1,64,128]{2,1,0:T(8,128)(2,1)S(1)} %copy-done.6), channel_id=1, source_target_pairs={{0,4},{4,8},{8,12},{12,0},{1,5},{5,9},{9,13},{13,1},{2,6},{6,10},{... | collective-permute-start | bytes 49160 | tf_op jit(solution)/shard_map/ppermute | solution.py:321
  19.1 1.9 %collective-permute-start.4 = (bf16[4,64,128]{2,1,0:T(8,128)(2,1)S(1)}, bf16[4,64,128]{2,1,0:T(8,128)(2,1)S(1)}, u32[]{:S(2)}, u32[]{:S(2)}) collective-permute-start(bf16[4,64,128]{2,1,0:T(8,128)(2,1)S(1)} %constant_dynamic-update-slice_fusion.refs_3_), channel_id=1, source_target_pairs={{0,1},{1,0},{2,3},{3,2},{4,5},{5,4},{6,7},{7,6},{8,9},{9,8},{10,11... | collective-permute-start | bytes 196616 | tf_op jit(solution)/shard_map/ppermute | solution.py:321
  19.1 4.5 %collective-permute-start.5 = (bf16[4,64,128]{2,1,0:T(8,128)(2,1)S(1)}, bf16[4,64,128]{2,1,0:T(8,128)(2,1)S(1)}, u32[]{:S(2)}, u32[]{:S(2)}) collective-permute-start(bf16[4,64,128]{2,1,0:T(8,128)(2,1)S(1)} %constant_dynamic-update-slice_fusion.refs_3_), channel_id=1, source_target_pairs={{0,2},{1,3},{2,0},{3,1},{4,6},{5,7},{6,4},{7,5},{8,10},{9,11},{10,... | collective-permute-start | bytes 196616 | tf_op jit(solution)/shard_map/ppermute | solution.py:321
  20.7 4.1 %collective-permute-start.6 = (bf16[4,64,128]{2,1,0:T(8,128)(2,1)S(1)}, bf16[4,64,128]{2,1,0:T(8,128)(2,1)S(1)}, u32[]{:S(2)}, u32[]{:S(2)}) collective-permute-start(bf16[4,64,128]{2,1,0:T(8,128)(2,1)S(1)} %constant_dynamic-update-slice_fusion.refs_3_), channel_id=1, source_target_pairs={{0,3},{1,2},{2,1},{3,0},{4,7},{5,6},{6,5},{7,4},{8,11},{9,10},{10,... | collective-permute-start | bytes 196616 | tf_op jit(solution)/shard_map/ppermute | solution.py:321
  31.7 1.9 %collective-permute-start.7 = (bf16[4,80,128]{2,1,0:T(8,128)(2,1)S(1)}, bf16[4,80,128]{2,1,0:T(8,128)(2,1)S(1)}, u32[]{:S(2)}, u32[]{:S(2)}) collective-permute-start(bf16[4,80,128]{2,1,0:T(8,128)(2,1)S(1)} %get-tuple-element.24), channel_id=1, source_target_pairs={{0,1},{1,0},{2,3},{3,2},{4,5},{5,4},{6,7},{7,6},{8,9},{9,8},{10,11... | collective-permute-start | bytes 245768 | tf_op jit(solution)/shard_map/ppermute | solution.py:321
  31.8 5.1 %collective-permute-start.8 = (bf16[4,80,128]{2,1,0:T(8,128)(2,1)S(1)}, bf16[4,80,128]{2,1,0:T(8,128)(2,1)S(1)}, u32[]{:S(2)}, u32[]{:S(2)}) collective-permute-start(bf16[4,80,128]{2,1,0:T(8,128)(2,1)S(1)} %get-tuple-element.25), channel_id=1, source_target_pairs={{0,2},{1,3},{2,0},{3,1},{4,6},{5,7},{6,4},{7,5},{8,10},{9,11},{10,... | collective-permute-start | bytes 245768 | tf_op jit(solution)/shard_map/ppermute | solution.py:321
  33.3 4.7 %collective-permute-start.9 = (bf16[4,80,128]{2,1,0:T(8,128)(2,1)S(1)}, bf16[4,80,128]{2,1,0:T(8,128)(2,1)S(1)}, u32[]{:S(2)}, u32[]{:S(2)}) collective-permute-start(bf16[4,80,128]{2,1,0:T(8,128)(2,1)S(1)} %get-tuple-element.26), channel_id=1, source_target_pairs={{0,3},{1,2},{2,1},{3,0},{4,7},{5,6},{6,5},{7,4},{8,11},{9,10},{10,... | collective-permute-start | bytes 245768 | tf_op jit(solution)/shard_map/ppermute | solution.py:321
  38.0 6.3 %collective-permute-start.10 = (f32[80,128]{1,0:T(8,128)S(1)}, f32[80,128]{1,0:T(8,128)S(1)}, u32[]{:S(2)}, u32[]{:S(2)}) collective-permute-start(f32[80,128]{1,0:T(8,128)S(1)} %get-tuple-element.28), channel_id=1, source_target_pairs={{0,4},{4,8},{8,12},{12,0},{1,5},{5,9},{9,13},{13,1},{2,6},{6,10},{... | collective-permute-start | bytes 122888 | tf_op jit(solution)/shard_map/ppermute | solution.py:321
  38.1 6.9 %collective-permute-start.11 = (f32[80,128]{1,0:T(8,128)S(1)}, f32[80,128]{1,0:T(8,128)S(1)}, u32[]{:S(2)}, u32[]{:S(2)}) collective-permute-start(f32[80,128]{1,0:T(8,128)S(1)} %get-tuple-element.29), channel_id=1, source_target_pairs={{0,8},{4,12},{8,0},{12,4},{1,9},{5,13},{9,1},{13,5},{2,10},{6,14},... | collective-permute-start | bytes 122888 | tf_op jit(solution)/shard_map/ppermute | solution.py:321
  39.3 5.7 %collective-permute-start.12 = (f32[80,128]{1,0:T(8,128)S(1)}, f32[80,128]{1,0:T(8,128)S(1)}, u32[]{:S(2)}, u32[]{:S(2)}) collective-permute-start(f32[80,128]{1,0:T(8,128)S(1)} %get-tuple-element.30), channel_id=1, source_target_pairs={{0,12},{4,0},{8,4},{12,8},{1,13},{5,1},{9,5},{13,9},{2,14},{6,2},{... | collective-permute-start | bytes 122888 | tf_op jit(solution)/shard_map/ppermute | solution.py:321
  45.0 5.6 %collective-permute-start.15 = (bf16[1,64,128]{2,1,0:T(8,128)(2,1)S(1)}, bf16[1,64,128]{2,1,0:T(8,128)(2,1)S(1)}, u32[]{:S(2)}, u32[]{:S(2)}) collective-permute-start(bf16[1,64,128]{2,1,0:T(8,128)(2,1)S(1)} %shard_map.98), channel_id=1, source_target_pairs={{0,4},{4,8},{8,12},{12,0},{1,5},{5,9},{9,13},{13,1},{2,6},{6,10},{... | collective-permute-start | bytes 49160 | tf_op jit(solution)/shard_map/ppermute | solution.py:321
  46.5 4.6 %collective-permute-start.14 = (bf16[1,64,128]{2,1,0:T(8,128)(2,1)S(1)}, bf16[1,64,128]{2,1,0:T(8,128)(2,1)S(1)}, u32[]{:S(2)}, u32[]{:S(2)}) collective-permute-start(bf16[1,64,128]{2,1,0:T(8,128)(2,1)S(1)} %shard_map.98), channel_id=1, source_target_pairs={{0,8},{4,12},{8,0},{12,4},{1,9},{5,13},{9,1},{13,5},{2,10},{6,14},... | collective-permute-start | bytes 49160 | tf_op jit(solution)/shard_map/ppermute | solution.py:321
  48.6 3.7 %collective-permute-start.13 = (bf16[1,64,128]{2,1,0:T(8,128)(2,1)S(1)}, bf16[1,64,128]{2,1,0:T(8,128)(2,1)S(1)}, u32[]{:S(2)}, u32[]{:S(2)}) collective-permute-start(bf16[1,64,128]{2,1,0:T(8,128)(2,1)S(1)} %shard_map.98), channel_id=1, source_target_pairs={{0,12},{4,0},{8,4},{12,8},{1,13},{5,1},{9,5},{13,9},{2,14},{6,2},{... | collective-permute-start | bytes 49160 | tf_op jit(solution)/shard_map/ppermute | solution.py:321
  52.3 1.9 %collective-permute-start.16 = (bf16[4,64,128]{2,1,0:T(8,128)(2,1)S(1)}, bf16[4,64,128]{2,1,0:T(8,128)(2,1)S(1)}, u32[]{:S(2)}, u32[]{:S(2)}) collective-permute-start(bf16[4,64,128]{2,1,0:T(8,128)(2,1)S(1)} %pad_maximum_fusion.refs_3_), channel_id=1, source_target_pairs={{0,1},{1,0},{2,3},{3,2},{4,5},{5,4},{6,7},{7,6},{8,9},{9,8},{10,11... | collective-permute-start | bytes 196616 | tf_op jit(solution)/shard_map/ppermute | solution.py:321
  52.4 5.0 %collective-permute-start.17 = (bf16[4,64,128]{2,1,0:T(8,128)(2,1)S(1)}, bf16[4,64,128]{2,1,0:T(8,128)(2,1)S(1)}, u32[]{:S(2)}, u32[]{:S(2)}) collective-permute-start(bf16[4,64,128]{2,1,0:T(8,128)(2,1)S(1)} %pad_maximum_fusion.refs_3_), channel_id=1, source_target_pairs={{0,2},{1,3},{2,0},{3,1},{4,6},{5,7},{6,4},{7,5},{8,10},{9,11},{10,... | collective-permute-start | bytes 196616 | tf_op jit(solution)/shard_map/ppermute | solution.py:321
  53.4 4.5 %collective-permute-start.18 = (bf16[4,64,128]{2,1,0:T(8,128)(2,1)S(1)}, bf16[4,64,128]{2,1,0:T(8,128)(2,1)S(1)}, u32[]{:S(2)}, u32[]{:S(2)}) collective-permute-start(bf16[4,64,128]{2,1,0:T(8,128)(2,1)S(1)} %pad_maximum_fusion.refs_3_), channel_id=1, source_target_pairs={{0,3},{1,2},{2,1},{3,0},{4,7},{5,6},{6,5},{7,4},{8,11},{9,10},{10,... | collective-permute-start | bytes 196616 | tf_op jit(solution)/shard_map/ppermute | solution.py:321
  64.6 10.2 %collective-permute-start.19 = (f32[4,80,128]{2,1,0:T(8,128)S(1)}, f32[4,80,128]{2,1,0:T(8,128)S(1)}, u32[]{:S(2)}, u32[]{:S(2)}) collective-permute-start(f32[4,80,128]{2,1,0:T(8,128)S(1)} %get-tuple-element.32), channel_id=1, source_target_pairs={{0,1},{1,0},{2,3},{3,2},{4,5},{5,4},{6,7},{7,6},{8,9},{9,8},{10,11... | collective-permute-start | bytes 491528 | tf_op jit(solution)/shard_map/ppermute | solution.py:321
  65.0 9.9 %collective-permute-start.20 = (f32[4,80,128]{2,1,0:T(8,128)S(1)}, f32[4,80,128]{2,1,0:T(8,128)S(1)}, u32[]{:S(2)}, u32[]{:S(2)}) collective-permute-start(f32[4,80,128]{2,1,0:T(8,128)S(1)} %get-tuple-element.33), channel_id=1, source_target_pairs={{0,2},{1,3},{2,0},{3,1},{4,6},{5,7},{6,4},{7,5},{8,10},{9,11},{10,... | collective-permute-start | bytes 491528 | tf_op jit(solution)/shard_map/ppermute | solution.py:321
  65.9 8.9 %collective-permute-start.21 = (f32[4,80,128]{2,1,0:T(8,128)S(1)}, f32[4,80,128]{2,1,0:T(8,128)S(1)}, u32[]{:S(2)}, u32[]{:S(2)}) collective-permute-start(f32[4,80,128]{2,1,0:T(8,128)S(1)} %get-tuple-element.34), channel_id=1, source_target_pairs={{0,3},{1,2},{2,1},{3,0},{4,7},{5,6},{6,5},{7,4},{8,11},{9,10},{10,... | collective-permute-start | bytes 491528 | tf_op jit(solution)/shard_map/ppermute | solution.py:321
  66.6 8.2 %collective-permute-start.25 = (f32[1,72]{1,0:T(1,128)S(1)}, f32[1,72]{1,0:T(1,128)S(1)}, u32[]{:S(2)}, u32[]{:S(2)}) collective-permute-start(f32[1,72]{1,0:T(1,128)S(1)} %get-tuple-element.39), channel_id=1, source_target_pairs={{0,2},{2,0},{1,3},{3,1},{4,6},{6,4},{5,7},{7,5},{8,10},{10,8},{9,1... | collective-permute-start | bytes 872 | tf_op jit(solution)/shard_map/ppermute | solution.py:321
  74.9 6.0 %collective-permute-start.22 = (f32[80,128]{1,0:T(8,128)S(1)}, f32[80,128]{1,0:T(8,128)S(1)}, u32[]{:S(2)}, u32[]{:S(2)}) collective-permute-start(f32[80,128]{1,0:T(8,128)S(1)} %get-tuple-element.36), channel_id=1, source_target_pairs={{0,4},{4,8},{8,12},{12,0},{1,5},{5,9},{9,13},{13,1},{2,6},{6,10},{... | collective-permute-start | bytes 122888 | tf_op jit(solution)/shard_map/ppermute | solution.py:321
  75.8 6.0 %collective-permute-start.23 = (f32[80,128]{1,0:T(8,128)S(1)}, f32[80,128]{1,0:T(8,128)S(1)}, u32[]{:S(2)}, u32[]{:S(2)}) collective-permute-start(f32[80,128]{1,0:T(8,128)S(1)} %get-tuple-element.37), channel_id=1, source_target_pairs={{0,8},{4,12},{8,0},{12,4},{1,9},{5,13},{9,1},{13,5},{2,10},{6,14},... | collective-permute-start | bytes 122888 | tf_op jit(solution)/shard_map/ppermute | solution.py:321
  77.8 4.2 %collective-permute-start.24 = (f32[80,128]{1,0:T(8,128)S(1)}, f32[80,128]{1,0:T(8,128)S(1)}, u32[]{:S(2)}, u32[]{:S(2)}) collective-permute-start(f32[80,128]{1,0:T(8,128)S(1)} %get-tuple-element.38), channel_id=1, source_target_pairs={{0,12},{4,0},{8,4},{12,8},{1,13},{5,1},{9,5},{13,9},{2,14},{6,2},{... | collective-permute-start | bytes 122888 | tf_op jit(solution)/shard_map/ppermute | solution.py:321
  (2 other events, 8.3 us)

commit v2 on v1

v2 whole, which is shorter than its diff:
```python
import functools
import math

import jax
import jax.numpy as jnp
import numpy as np
from jax import lax
from jax.experimental import pallas as pl
from jax.experimental.pallas import tpu as pltpu
from jax.sharding import PartitionSpec as P

ANG = 256
ITERS = 2
SIGMA = 32

shrinkage = 1.0

F32 = jnp.float32
BF16 = jnp.bfloat16


def tables(freqs):
    freq = np.arange(freqs)
    turn = np.arange(ANG)
    angle = (turn[:, None] * freq[None, :] % ANG) * (2.0 * math.pi / ANG)
    scale = np.where(freq == 0, 1.0, 2.0) / ANG
    inverse = np.concatenate([scale * np.cos(angle), -scale * np.sin(angle)], 1).astype(np.float32)
    forward = np.concatenate([np.cos(angle), np.sin(angle)], 1).T.astype(np.float32)

    def split(x):
        high = x.astype(BF16)
        return high, (x - high.astype(np.float32)).astype(BF16)

    return split(inverse) + split(forward)


def loop(count, body, unroll):
    while count % unroll:
        unroll -= 1
    if unroll == count:
        for i in range(count):
            body(i)
        return

    def step(outer, carry):
        for inner in range(unroll):
            body(outer * unroll + inner)
        return carry

    lax.fori_loop(0, count // unroll, step, 0)


def params(*shapes):
    total = 0
    for shape, dtype in shapes:
        size = jnp.dtype(dtype).itemsize
        dims = [1, 1, *shape]
        rows = -(-dims[-2] // 16) * 16
        lanes = -(-dims[-1] // 128) * 128
        total += math.prod(dims[:-2]) * rows * lanes * size
    return pltpu.CompilerParams(vmem_limit_bytes=min(total + (4 << 20), 62 << 20))


def vmem(count):
    return [pl.BlockSpec(memory_space=pltpu.VMEM)] * count


def prep_kernel(share, groups, start_ref, particles_ref, *rest):
    outs, (held, wide, sems) = rest[:groups], rest[groups:]
    freqs, depth = held.shape[2:]
    pitch = wide.shape[0] // share
    copies = []
    for g in reversed(range(groups)):
        rows = pl.ds(start_ref[g], share)
        copy = pltpu.make_async_copy(particles_ref.at[rows], held.at[g], sems.at[g])
        copy.start()
        copies.append((g, copy))
    for g, copy in copies:
        copy.wait()

        def widen(p, g=g):
            wide[pl.ds(pl.multiple_of(p * pitch, 8), freqs), :] = held[g, p].astype(F32)

        loop(share, widen, 8)

        def turn(f, g=g):
            for part in range(2):
                rows = pl.ds(2 * f + part, share, stride=pitch)
                outs[g][f, :, pl.ds(part * depth, depth)] = wide[rows, :].astype(BF16)

        loop(freqs // 2, turn, 8)


def prep(particles, start, share, groups):
    _, freqs, depth = particles.shape
    shape = (freqs // 2, share, 2 * depth)
    held = (groups, share, freqs, depth)
    wide = (share * (freqs + 8), depth)
    return pl.pallas_call(
        functools.partial(prep_kernel, share, groups),
        out_shape=[jax.ShapeDtypeStruct(shape, BF16)] * groups,
        in_specs=[
            pl.BlockSpec(memory_space=pltpu.SMEM),
            pl.BlockSpec(memory_space=pltpu.MemorySpace.HBM),
        ],
        out_specs=vmem(groups),
        scratch_shapes=[
            pltpu.VMEM(held, BF16),
            pltpu.VMEM(wide, F32),
            pltpu.SemaphoreType.DMA((groups,)),
        ],
        compiler_params=params(*[(shape, BF16)] * groups, (held, BF16), (wide, F32)),
        cost_estimate=pl.CostEstimate(
            flops=0, bytes_accessed=4 * groups * math.prod(shape), transcendentals=0
        ),
    )(start, particles)


def em_kernel(groups, sides, blocks, *refs):
    refs = list(refs)
    take = lambda n: [refs.pop(0) for _ in range(n)]
    (index_ref,) = take(1)
    particles = take(groups)
    pieces_ref, doubled_ref, prior_ref, inv_hi, inv_lo, fwd_hi, fwd_lo = take(7)
    out, evidence_ref = take(2)
    image, field, energy_ref, count_ref = take(4)
    pairs, share, twice = particles[0].shape
    freqs, depth = 2 * pairs, twice // 2
    every = freqs * groups
    classes = sides * blocks
    radii = depth // 2
    pitch = image.shape[0] // (2 * classes)
    start = [
        pl.multiple_of(lax.rem(index_ref[0] + g, groups) * freqs, freqs) for g in range(groups)
    ]
    lane = lax.broadcasted_iota(jnp.int32, (freqs, depth), 1)
    sign = jnp.where(lane < radii, -1.0, 1.0).astype(F32)
    doubled = doubled_ref[...]
    row = lax.broadcasted_iota(jnp.int32, (freqs, depth), 0)
    dot = functools.partial(jnp.dot, preferred_element_type=F32)

    def rows(base, count):
        return pl.ds(pl.multiple_of(base, 8), count)

    def weigh(k):
        energy = jnp.zeros((freqs, depth), F32)
        for g in range(groups):
            plain = pieces_ref[k * groups + g].astype(F32)
            scale = jnp.where(row + g * freqs == 0, 1.0 / ANG, 2.0 / ANG).astype(F32)
            energy = energy + plain * plain * doubled * scale
            weighted = (plain * doubled).astype(BF16).astype(F32)
            base = k * 2 * pitch + g * freqs
            image[rows(base, freqs), :] = weighted
            image[rows(base + pitch, freqs), :] = sign * pltpu.roll(weighted, radii, 1)
        total = jnp.sum(jnp.sum(energy, axis=0, keepdims=True), axis=1, keepdims=True)
        energy_ref[pl.ds(k, 1), :] = jnp.broadcast_to(total, (1, share))

    loop(classes, weigh, 8)

    none = jnp.zeros((2 * classes, depth), BF16)
    for g in range(groups):

        def correlate(f, g=g):
            where = [
                pl.ds(start[g] + 2 * f + part, 2 * classes, stride=pitch) for part in range(2)
            ]
            first, second = [image[at, :].astype(BF16) for at in where]
            left = jnp.concatenate(
                [
                    jnp.concatenate([first, none], 1),
                    jnp.concatenate([none, second], 1),
                ],
                0,
            )
            value = lax.dot_general(
                left, particles[g][f], (((1,), (1,)), ((), ())), preferred_element_type=F32
            )
            for part, at in enumerate(where):
                field[at, :] = value[part * 2 * classes : (part + 1) * 2 * classes]

        loop(pairs, correlate, 8)

    turns = lax.broadcasted_iota(jnp.int32, (ANG, share), 0)
    offset = jnp.abs(turns - prior_ref[...])
    distance = jnp.minimum(offset, ANG - offset).astype(F32)
    prior_term = -distance * distance / (2.0 * SIGMA * SIGMA)

    def load(k):
        return jnp.concatenate(
            [field[rows((2 * k + part) * pitch, every), :] for part in range(2)], 0
        )

    def store(k, value):
        for part in range(2):
            field[rows((2 * k + part) * pitch, every), :] = value[part * every : (part + 1) * every]

    def score(k, peak):
        value = load(k)
        high = value.astype(BF16)
        low = (value - high.astype(F32)).astype(BF16)
        inner = dot(inv_hi[...], high) + (dot(inv_hi[...], low) + dot(inv_lo[...], high))
        scores = inner - 0.5 * energy_ref[pl.ds(k, 1), :] + prior_term
        store(k, scores)
        return jnp.maximum(peak, jnp.max(scores, axis=0, keepdims=True))

    def weight(k, total):
        value = jnp.exp(load(k) - peak)
        store(k, value)
        return total + jnp.sum(value, axis=0, keepdims=True)

    def spectrum(k, carry):
        value = load(k) * inverse_total
        count = jnp.sum(jnp.sum(value, axis=0, keepdims=True), axis=1, keepdims=True)
        count_ref[pl.ds(k, 1), :] = jnp.broadcast_to(count, (1, depth))
        rounded = value.astype(BF16)
        store(k, dot(fwd_hi[...], rounded) + dot(fwd_lo[...], rounded))
        return carry

    def each(body, init):
        if classes <= 8:
            for k in range(classes):
                init = body(k, init)
            return init
        return lax.fori_loop(0, classes, body, init)

    peak = each(score, jnp.full((1, share), -jnp.inf, F32))
    total = each(weight, jnp.zeros((1, share), F32))
    evidence = peak + jnp.log(total)
    evidence_ref[...] = evidence
    inverse_total = 1.0 / total
    each(spectrum, 0)

    for g in range(groups):

        def accumulate(f, g=g):
            where = [
                pl.ds(start[g] + 2 * f + part, 2 * classes, stride=pitch) for part in range(2)
            ]
            left = jnp.concatenate([field[at, :].astype(BF16) for at in where], 0)
            value = dot(left, particles[g][f])
            for part, at in enumerate(where):
                image[at, :] = value[
                    part * 2 * classes : (part + 1) * 2 * classes,
                    part * depth : (part + 1) * depth,
                ]

        loop(pairs, accumulate, 8)

    spare = lax.broadcasted_iota(jnp.int32, (out.shape[2] - freqs, depth), 0)
    for side in range(sides):

        def finish(i, side=side):
            k = i * sides + side
            count = count_ref[pl.ds(k, 1), :]
            high = count.astype(BF16).astype(F32)
            tail = jnp.where(spare == 0, high, jnp.where(spare == 1, count - high, 0.0))
            for g in range(groups):
                base = k * 2 * pitch + g * freqs
                other = pltpu.roll(image[rows(base + pitch, freqs), :], radii, 1)
                value = image[rows(base, freqs), :] + sign * other
                out[side * groups + g, i, pl.ds(0, freqs), :] = value.astype(out.dtype)
                out[side * groups + g, i, pl.ds(freqs, tail.shape[0]), :] = tail.astype(out.dtype)

        loop(blocks, finish, 4)


def em(index, particles, pieces, doubled, prior, constants, sides, send_type):
    groups = len(particles)
    pairs, share, twice = particles[0].shape
    freqs, depth = 2 * pairs, twice // 2
    classes = pieces.shape[0] // groups
    blocks = classes // sides
    every = freqs * groups
    sums = (sides * groups, blocks, freqs + (8 if send_type == F32 else 16), depth)
    scratch = [
        ((2 * (every + 8) * classes, depth), F32),
        ((2 * (every + 8) * classes, share), F32),
        ((classes, share), F32),
        ((classes, depth), F32),
    ]
    buffers = scratch + [(x.shape, x.dtype) for x in (*particles, pieces, *constants)]
    return pl.pallas_call(
        functools.partial(em_kernel, groups, sides, blocks),
        out_shape=[jax.ShapeDtypeStruct(sums, send_type), jax.ShapeDtypeStruct((1, share), F32)],
        in_specs=[pl.BlockSpec(memory_space=pltpu.SMEM)] + vmem(groups + 3 + len(constants)),
        out_specs=vmem(2),
        scratch_shapes=[pltpu.VMEM(*entry) for entry in scratch],
        compiler_params=params(*buffers, (sums, send_type)),
        cost_estimate=pl.CostEstimate(
            flops=8 * classes * share * every * (depth + 3 * ANG),
            bytes_accessed=2 * every * share * depth,
            transcendentals=classes * share * ANG,
        ),
    )(index, *particles, pieces, doubled, prior, *constants)


def combine_kernel(parts_ref, out):
    rows = out.shape[1]
    for i in range(out.shape[0]):
        total = parts_ref[0, i].astype(F32)
        for j in range(1, parts_ref.shape[0]):
            total = total + parts_ref[j, i].astype(F32)
        out[i] = total[:rows]


def combine(parts, freqs):
    _, blocks, _, depth = parts.shape
    shape = (blocks, freqs + 8, depth)
    return pl.pallas_call(
        combine_kernel,
        out_shape=jax.ShapeDtypeStruct(shape, F32),
        in_specs=vmem(1),
        out_specs=pl.BlockSpec(memory_space=pltpu.VMEM),
        compiler_params=params((parts.shape, F32), (shape, F32)),
    )(parts)


def means_kernel(parts_ref, out):
    freqs = out.shape[1]
    total = parts_ref[0]
    for i in range(1, parts_ref.shape[0]):
        total = total + parts_ref[i]
    counts = total[freqs : freqs + 1, :] + total[freqs + 1 : freqs + 2, :]
    value = (total[:freqs, :] / (counts + shrinkage)).astype(out.dtype)
    for i in range(out.shape[0]):
        out[i] = value


def class_means(parts, copies, dtype):
    _, rows, depth = parts.shape
    shape = (copies, rows - 8, depth)
    return pl.pallas_call(
        means_kernel,
        out_shape=jax.ShapeDtypeStruct(shape, dtype),
        in_specs=vmem(1),
        out_specs=pl.BlockSpec(memory_space=pltpu.VMEM),
        compiler_params=params((parts.shape, F32), (shape, dtype)),
    )(parts)


def shift(value, axes, sizes, step):
    if not any(step):
        return value
    pairs = []
    for there in np.ndindex(*sizes):
        here = tuple((t - s) % n for t, s, n in zip(there, step, sizes))
        pairs.append((int(np.ravel_multi_index(there, sizes)), int(np.ravel_multi_index(here, sizes))))
    return lax.ppermute(value, axes, pairs)


def shards(particles, references, noise_inv, prior_rot):
    batch, freqs, depth = particles.shape
    sides = lax.axis_size("cls")
    groups = lax.axis_size("rot")
    blocks = lax.axis_size("blk")
    side = lax.axis_index("cls")
    group = lax.axis_index("rot")
    half = batch // groups
    share = half // sides
    members = blocks * sides * groups

    constants = [jnp.asarray(x) for x in tables(freqs * groups)]
    doubled = jnp.concatenate([noise_inv, noise_inv]).reshape(1, depth)
    index = group.astype(jnp.int32).reshape(1)
    start = (group + jnp.arange(groups, dtype=jnp.int32)) % groups * half + side * share
    prior = lax.dynamic_slice_in_dim(prior_rot, start[0], share, 0).reshape(1, share)

    cut = prep(particles, start, share, groups)
    own = [cut[0]]
    for g in range(1, groups):
        own.append(shift(cut[-g % groups], ("rot",), (groups,), (g,)))

    exchange = functools.partial(lax.all_to_all, split_axis=0, concat_axis=0, tiled=True)
    current = jnp.broadcast_to(references, (members, freqs, depth))
    for step in range(ITERS):
        last = step == ITERS - 1
        pieces = exchange(current, ("blk", "cls", "rot"))
        sums, evidence = em(
            index, own, pieces, doubled, prior, constants, sides, F32 if last else BF16
        )
        if last:
            gathered = [shift(evidence, ("cls",), (sides,), (i,)) for i in range(sides)]
        mine = combine(exchange(sums, ("cls", "rot")), freqs)
        mine = exchange(mine, "blk")
        current = class_means(mine, 1, F32) if last else class_means(mine, members, BF16)
    evidence = jnp.roll(jnp.concatenate(gathered, 0), side, 0).reshape(half)
    return current, evidence


def solution(mesh):
    in_specs = (
        P(("grp", "blk"), "rot", None),
        P(("grp", "blk", "cls"), "rot", None),
        P(),
        P(("grp", "blk")),
    )
    out_specs = (P(("grp", "blk", "cls"), "rot", None), P(("grp", "blk", "rot")))
    return jax.shard_map(shards, mesh=mesh, in_specs=in_specs, out_specs=out_specs, check_vma=False)
```

time: 82.8 us -> 92.3 us (1.11)
  blocking collectives: 0 us -> 30.8 us
  starting transfers between devices: 26.7 us -> 16.3 us
  waiting for transfers between devices: 32.1 us -> 22.8 us
  Pallas kernels: 19.7 us -> 17 us
    ppermute x26 -> x2, waiting for transfers between devices: 32.1 us -> 0.01 us  [shift(): return lax.ppermute(value, axes, pairs)]
    all_to_all x0 -> x3, blocking collectives: none -> 30.8 us  [the longest x1 12.6 us: shards(): pieces = exchange(current, ('blk', 'cls', 'rot'))]
    ppermute x26 -> x2, starting transfers between devices: 26.7 us -> 2.49 us  [shift(): return lax.ppermute(value, axes, pairs)]
    all_to_all x0 -> x3, waiting for transfers between devices: none -> 22.8 us  [the longest x1 9.78 us: shards(): pieces = exchange(current, ('blk', 'cls', 'rot'))]
    all_to_all x0 -> x3, starting transfers between devices: none -> 13.8 us  [the longest x1 7.02 us: shards(): pieces = exchange(current, ('blk', 'cls', 'rot'))]
    pallas_call x1, Pallas kernels: 5.35 us -> 3.3 us  [prep(): pl.pallas_call(functools.partial(prep_kernel, share, groups), out_shape=[...]
    unnamed x19 -> x16, local copies, waits for them, and re-layouts: 2.39 us -> 2.37 us
  transfers between devices with their start and end apart: 26 -> 5, of which waited for: 18 -> 3; matrix products, arithmetic and copies ran while one was open for 1% -> 2% of each run, Pallas kernels for 0% -> 1%
where the time goes in v2:
time: 92.3 us; the launch traced here: 91.8 us
  blocking collectives  30.8 us (33%)
  waiting for transfers between devices  22.8 us (25%)
  Pallas kernels  17 us (18%)
  starting transfers between devices  16.3 us (18%)
  local copies, waits for them, and re-layouts  3.86 us (4%)
    all_to_all x1, blocking collectives, shards(): pieces = exchange(current, ('blk', 'cls', 'rot'))  12.6 us
    pallas_call x2, Pallas kernels, em(): pl.pallas_call(functools.partial(em_kernel, groups, sides, blocks), out_s...  12.3 us
    all_to_all x1, waiting for transfers between devices, shards(): pieces = exchange(current, ('blk', 'cls', 'rot'))  9.78 us
    all_to_all x1, blocking collectives, shards(): mine = combine(exchange(sums, ('cls', 'rot')), freqs)  9.1 us
    all_to_all x1, blocking collectives, shards(): mine = exchange(mine, 'blk')  9.04 us
    all_to_all x1, waiting for transfers between devices, shards(): mine = combine(exchange(sums, ('cls', 'rot')), freqs)  7.53 us
    all_to_all x1, starting transfers between devices, shards(): pieces = exchange(current, ('blk', 'cls', 'rot'))  7.02 us
    all_to_all x1, waiting for transfers between devices, shards(): mine = exchange(mine, 'blk')  5.53 us
  transfers between devices with their start and end apart: 5, of which 3 were waited for; matrix products, arithmetic and copies ran while one was open for 2% of the time, Pallas kernels for 1%

profile of v2, /device:TPU:0, one launch (start us, length us, event | category | flops | bytes accessed | tf_op | source)
XLA Modules:
  0.0 91.8 jit_solution(1656769255399101593)
XLA Ops:
  0.6 0.0 copy-start
  0.7 0.0 copy-start.1
  0.7 2.3 %copy-done.1 = bf16[288,64,128]{2,1,0:T(8,128)(2,1)S(1)} copy-done((bf16[288,64,128]{2,1,0:T(8,128)(2,1)S(1)}, bf16[288,64,128]{2,1,0:T(8,128)(2,1)}, u32[]{:S(2)}) %copy-start.1) | copy-done | bytes 4718616
  3.0 0.0 copy-start.4
  3.0 0.0 copy-start.5
  3.0 3.3 %shard_map.95 = (bf16[32,72,256]{2,1,0:T(8,128)(2,1)S(1)}, bf16[32,72,256]{2,1,0:T(8,128)(2,1)}) custom-call(s32[2]{0:T(128)S(1)} %fusion.1.start_ref, bf16[288,64,128]{2,1,0:T(8,128)(2,1)S(1)} %copy-done.1), custom_call_target="tpu_custom_call" | custom-call | bytes 4718592 | tf_op jit(solution)/shard_map/pallas_call | solution.py:99
  6.4 0.5 collective-permute-start
  6.9 0.0 copy-done.6
  6.9 0.8 broadcast_in_dim.8
  7.6 7.0 %all-to-all-start = ((bf16[16,64,128]{2,1,0:T(8,128)(2,1)}), bf16[16,64,128]{2,1,0:T(8,128)(2,1)S(1)}, u32[]{:S(2)}, u32[]{:S(2)}) async-start(bf16[16,64,128]{2,1,0:T(8,128)(2,1)} %broadcast_in_dim.8), calls=%async_computation | async-start | bytes 524288 | tf_op jit(solution)/shard_map/all_to_all | solution.py:377
  14.8 0.0 copy-done.7
  14.8 0.1 maximum_bitcast_fusion.refs_4_
  14.9 0.0 copy-done
  14.9 0.1 dynamic-slice_bitcast_fusion.refs_5_
  14.9 9.8 %all-to-all-done.refs_3_ = bf16[16,64,128]{2,1,0:T(8,128)(2,1)S(1)} async-done(((bf16[16,64,128]{2,1,0:T(8,128)(2,1)}), bf16[16,64,128]{2,1,0:T(8,128)(2,1)S(1)}, u32[]{:S(2)}, u32[]{:S(2)}) %all-to-all-start) | async-done | bytes 262176 | tf_op jit(solution)/shard_map/all_to_all | solution.py:377
  24.7 0.0 collective-permute-done.refs_2_
  24.7 0.0 copy-done.2
  24.7 0.0 copy-done.3
  24.7 5.8 %shard_map.96 = (bf16[4,4,80,128]{3,2,1,0:T(8,128)(2,1)S(1)}, f32[1,72]{1,0:T(1,128)}) custom-call(s32[1]{0:T(128)} %bitcast.refs_0_, bf16[32,72,256]{2,1,0:T(8,128)(2,1)S(1)} %get-tuple-element.7.refs_1_, bf16[32,72,256]{2,1,0:T(8,128)(2,1)S(1)} %collective-permute-done.refs_2_, bf16[16,64,128]{2,1,0:T(8,128)(2,1)S(1)} %all-to-all-done.refs_3_, ...), custom_call_target="tpu_custom_call" | custom-call | flops 528482304 | bytes 2359296 | tf_op jit(solution)/shard_map/pallas_call | solution.py:282
  30.5 9.1 %all_to_all.30.parts_ref = bf16[4,4,80,128]{3,2,1,0:T(8,128)(2,1)S(1)} all-to-all(bf16[4,4,80,128]{3,2,1,0:T(8,128)(2,1)S(1)} %get-tuple-element.9), channel_id=1, replica_groups=mesh['grp'=2,'blk'=4,'cls'=2,'rot'=2] {'cls','rot'}, dimensions={0} | all-to-all | bytes 655360 | tf_op jit(solution)/shard_map/all_to_all | solution.py:383
  39.7 9.0 %all_to_all.31.parts_ref = f32[4,72,128]{2,1,0:T(8,128)S(1)} all-to-all(f32[4,72,128]{2,1,0:T(8,128)S(1)} %shard_map.97), channel_id=1, replica_groups=mesh['grp'=2,'blk'=4,'cls'=2,'rot'=2] {'blk'}, dimensions={0} | all-to-all | bytes 294912 | tf_op jit(solution)/shard_map/all_to_all | solution.py:384
  48.8 12.6 %all_to_all.32.refs_3_ = bf16[16,64,128]{2,1,0:T(8,128)(2,1)S(1)} all-to-all(bf16[16,64,128]{2,1,0:T(8,128)(2,1)S(1)} %shard_map.98), channel_id=1, replica_groups=mesh['grp'=2,'blk'=4,'cls'=2,'rot'=2] {'blk','cls','rot'}, dimensions={0} | all-to-all | bytes 524288 | tf_op jit(solution)/shard_map/all_to_all | solution.py:377
  61.4 6.5 %shard_map.99 = (f32[4,4,72,128]{3,2,1,0:T(8,128)}, f32[1,72]{1,0:T(1,128)S(1)}) custom-call(s32[1]{0:T(128)} %bitcast.refs_0_, bf16[32,72,256]{2,1,0:T(8,128)(2,1)S(1)} %get-tuple-element.7.refs_1_, bf16[32,72,256]{2,1,0:T(8,128)(2,1)S(1)} %collective-permute-done.refs_2_, bf16[16,64,128]{2,1,0:T(8,128)(2,1)S(1)} %all_to_all.32.refs_3_, ...), custom_call_target="tpu_custom_call" | custom-call | flops 528482304 | bytes 2359296 | tf_op jit(solution)/shard_map/pallas_call | solution.py:282
  67.9 3.5 %all-to-all-start.4 = ((f32[4,4,72,128]{3,2,1,0:T(8,128)}), f32[4,4,72,128]{3,2,1,0:T(8,128)S(1)}, u32[]{:S(2)}, u32[]{:S(2)}) async-start(f32[4,4,72,128]{3,2,1,0:T(8,128)} %get-tuple-element.10), calls=%async_computation.4 | async-start | bytes 1179648 | tf_op jit(solution)/shard_map/all_to_all | solution.py:383
  71.4 2.0 %collective-permute-start.1 = (f32[1,72]{1,0:T(1,128)S(1)}, f32[1,72]{1,0:T(1,128)S(1)}, u32[]{:S(2)}, u32[]{:S(2)}) collective-permute-start(f32[1,72]{1,0:T(1,128)S(1)} %get-tuple-element.11), channel_id=1, source_target_pairs={{0,2},{2,0},{1,3},{3,1},{4,6},{6,4},{5,7},{7,5},{8,10},{10,8},{9,1... | collective-permute-start | bytes 872 | tf_op jit(solution)/shard_map/ppermute | solution.py:348
  73.4 7.5 %all-to-all-done.4.parts_ref = f32[4,4,72,128]{3,2,1,0:T(8,128)S(1)} async-done(((f32[4,4,72,128]{3,2,1,0:T(8,128)}), f32[4,4,72,128]{3,2,1,0:T(8,128)S(1)}, u32[]{:S(2)}, u32[]{:S(2)}) %all-to-all-start.4) | async-done | bytes 589856 | tf_op jit(solution)/shard_map/all_to_all | solution.py:383
  80.9 0.7 shard_map.100
  81.6 3.3 %all-to-all-start.5 = ((f32[4,72,128]{2,1,0:T(8,128)}), f32[4,72,128]{2,1,0:T(8,128)S(1)}, u32[]{:S(2)}, u32[]{:S(2)}) async-start(f32[4,72,128]{2,1,0:T(8,128)} %shard_map.100), calls=%async_computation.5 | async-start | bytes 294912 | tf_op jit(solution)/shard_map/all_to_all | solution.py:384
  84.9 0.0 collective-permute-done.1
  85.0 0.6 reshape.19
  85.6 5.5 %all-to-all-done.5.parts_ref = f32[4,72,128]{2,1,0:T(8,128)S(1)} async-done(((f32[4,72,128]{2,1,0:T(8,128)}), f32[4,72,128]{2,1,0:T(8,128)S(1)}, u32[]{:S(2)}, u32[]{:S(2)}) %all-to-all-start.5) | async-done | bytes 147488 | tf_op jit(solution)/shard_map/all_to_all | solution.py:384
  91.2 0.6 shard_map.101
  (11 shorter events, 0.1 us)
Async XLA Ops:
  0.6 14.2 %copy-start = (s32[288]{0:T(512)S(1)}, s32[288]{0:T(512)}, u32[]{:S(2)}) copy-start(s32[288]{0:T(512)} %param.11) | copy-start | bytes 3460
  0.7 2.3 %copy-start.1 = (bf16[288,64,128]{2,1,0:T(8,128)(2,1)S(1)}, bf16[288,64,128]{2,1,0:T(8,128)(2,1)}, u32[]{:S(2)}) copy-start(bf16[288,64,128]{2,1,0:T(8,128)(2,1)} %particles_ref.1) | copy-start | bytes 14155780
  3.0 3.9 %copy-start.6 = (bf16[1,64,128]{2,1,0:T(8,128)(2,1)S(1)}, bf16[1,64,128]{2,1,0:T(8,128)(2,1)}, u32[]{:S(2)}) copy-start(bf16[1,64,128]{2,1,0:T(8,128)(2,1)} %param.9) | copy-start | bytes 49156
  3.0 11.8 %copy-start.7 = (f32[64]{0:T(128)S(1)}, f32[64]{0:T(128)}, u32[]{:S(2)}) copy-start(f32[64]{0:T(128)} %param.10) | copy-start | bytes 772
  3.0 21.7 %copy-start.2 = (bf16[256,256]{1,0:T(8,128)(2,1)S(1)}, bf16[256,256]{1,0:T(8,128)(2,1)}, u32[]{:S(2)}) copy-start(bf16[256,256]{1,0:T(8,128)(2,1)} %constant.52.clone.refs_6_) | copy-start | bytes 393220
  3.0 21.7 %copy-start.3 = (bf16[256,256]{1,0:T(8,128)(2,1)S(1)}, bf16[256,256]{1,0:T(8,128)(2,1)}, u32[]{:S(2)}) copy-start(bf16[256,256]{1,0:T(8,128)(2,1)} %constant.53.clone.refs_7_) | copy-start | bytes 393220
  3.0 21.7 %copy-start.4 = (bf16[256,256]{1,0:T(8,128)(2,1)S(1)}, bf16[256,256]{1,0:T(8,128)(2,1)}, u32[]{:S(2)}) copy-start(bf16[256,256]{1,0:T(8,128)(2,1)} %constant.54.clone.refs_8_) | copy-start | bytes 393220
  3.0 21.7 %copy-start.5 = (bf16[256,256]{1,0:T(8,128)(2,1)S(1)}, bf16[256,256]{1,0:T(8,128)(2,1)}, u32[]{:S(2)}) copy-start(bf16[256,256]{1,0:T(8,128)(2,1)} %constant.55.clone.refs_9_) | copy-start | bytes 393220
  6.4 18.4 %collective-permute-start = (bf16[32,72,256]{2,1,0:T(8,128)(2,1)}, bf16[32,72,256]{2,1,0:T(8,128)(2,1)S(1)}, u32[]{:S(2)}, u32[]{:S(2)}) collective-permute-start(bf16[32,72,256]{2,1,0:T(8,128)(2,1)} %get-tuple-element.8), channel_id=1, source_target_pairs={{0,1},{1,0},{2,3},{3,2},{4,5},{5,4},{6,7},{7,6},{8,9},{9,8},{10,11... | collective-permute-start | bytes 3538952 | tf_op jit(solution)/shard_map/ppermute | solution.py:348
  7.6 17.1 %all-to-all-start = ((bf16[16,64,128]{2,1,0:T(8,128)(2,1)}), bf16[16,64,128]{2,1,0:T(8,128)(2,1)S(1)}, u32[]{:S(2)}, u32[]{:S(2)}) async-start(bf16[16,64,128]{2,1,0:T(8,128)(2,1)} %broadcast_in_dim.8), calls=%async_computation | async-start | bytes 524288 | tf_op jit(solution)/shard_map/all_to_all | solution.py:377
  67.9 13.0 %all-to-all-start.4 = ((f32[4,4,72,128]{3,2,1,0:T(8,128)}), f32[4,4,72,128]{3,2,1,0:T(8,128)S(1)}, u32[]{:S(2)}, u32[]{:S(2)}) async-start(f32[4,4,72,128]{3,2,1,0:T(8,128)} %get-tuple-element.10), calls=%async_computation.4 | async-start | bytes 1179648 | tf_op jit(solution)/shard_map/all_to_all | solution.py:383
  71.4 13.6 %collective-permute-start.1 = (f32[1,72]{1,0:T(1,128)S(1)}, f32[1,72]{1,0:T(1,128)S(1)}, u32[]{:S(2)}, u32[]{:S(2)}) collective-permute-start(f32[1,72]{1,0:T(1,128)S(1)} %get-tuple-element.11), channel_id=1, source_target_pairs={{0,2},{2,0},{1,3},{3,1},{4,6},{6,4},{5,7},{7,5},{8,10},{10,8},{9,1... | collective-permute-start | bytes 872 | tf_op jit(solution)/shard_map/ppermute | solution.py:348
  81.6 9.6 %all-to-all-start.5 = ((f32[4,72,128]{2,1,0:T(8,128)}), f32[4,72,128]{2,1,0:T(8,128)S(1)}, u32[]{:S(2)}, u32[]{:S(2)}) async-start(f32[4,72,128]{2,1,0:T(8,128)} %shard_map.100), calls=%async_computation.5 | async-start | bytes 294912 | tf_op jit(solution)/shard_map/all_to_all | solution.py:384

commit v3 on v0

v3 whole, which is shorter than its diff:
```python
import functools
import math

import jax
import jax.numpy as jnp
import numpy as np
from jax import lax
from jax.experimental import pallas as pl
from jax.experimental.pallas import tpu as pltpu
from jax.sharding import PartitionSpec as P

ANG = 256
ITERS = 2
SIGMA = 32

shrinkage = 1.0

F32 = jnp.float32
BF16 = jnp.bfloat16
SPARE = 8
LONG_SPARE = 16

dot = functools.partial(jnp.dot, preferred_element_type=F32)


def split(x):
    high = x.astype(BF16)
    return high, (x - high.astype(F32)).astype(BF16)


def tables(half_freq):
    turn = np.arange(ANG)
    inverse, forward = [], []
    for group in range(2):
        sides = {}
        for which in range(2):
            freq = which * half_freq + np.arange(half_freq)
            angle = (turn[:, None] * freq[None, :] % ANG) * (2.0 * math.pi / ANG)
            scale = np.where(freq == 0, 1.0, 2.0) / ANG
            sides[which] = (
                np.concatenate([scale * np.cos(angle), -scale * np.sin(angle)], 1),
                np.concatenate([np.cos(angle), np.sin(angle)], 1).T,
            )
        inverse.append(np.concatenate([sides[group][0], sides[1 - group][0]], 1))
        forward.append(np.concatenate([sides[1 - group][1], sides[group][1]], 0))
    result = []
    for table in (inverse, forward):
        table = np.stack(table).astype(np.float32)
        high = table.astype(BF16)
        result += [high, (table - high.astype(np.float32)).astype(BF16)]
    return [jnp.asarray(x) for x in result]


def loop(count, body, unroll):
    while count % unroll:
        unroll -= 1
    if unroll == count:
        for i in range(count):
            body(i)
        return

    def step(outer, carry):
        for inner in range(unroll):
            body(outer * unroll + inner)
        return carry

    lax.fori_loop(0, count // unroll, step, 0)


def each(count, body, init):
    if count <= 8:
        for k in range(count):
            init = body(k, init)
        return init
    return lax.fori_loop(0, count, body, init)


def rows(base, count):
    return pl.ds(pl.multiple_of(base, 8), count)


def call(kernel, ins, outs, scratch=(), flops=0, scalar=False):
    total = 0
    buffers = [(x.shape, x.dtype) for x in ins] + list(outs) + list(scratch)
    for shape, dtype in buffers:
        dims = [1, 1, *shape]
        lines = -(-dims[-2] // 16) * 16
        lanes = -(-dims[-1] // 128) * 128
        total += math.prod(dims[:-2]) * lines * lanes * jnp.dtype(dtype).itemsize
    kinds = [pltpu.SMEM if scalar and i == 0 else pltpu.VMEM for i in range(len(ins))]
    return pl.pallas_call(
        kernel,
        out_shape=[jax.ShapeDtypeStruct(*x) for x in outs],
        in_specs=[pl.BlockSpec(memory_space=kind) for kind in kinds],
        out_specs=[pl.BlockSpec(memory_space=pltpu.VMEM)] * len(outs),
        scratch_shapes=[pltpu.VMEM(*x) for x in scratch],
        compiler_params=pltpu.CompilerParams(
            vmem_limit_bytes=min(total + (4 << 20), 62 << 20)
        ),
        cost_estimate=pl.CostEstimate(flops=flops, bytes_accessed=total, transcendentals=0),
    )(*ins)


def prep_kernel(share, start_ref, particles_ref, out, wide):
    freqs, depth = particles_ref.shape[1:]
    pitch = wide.shape[0] // share
    first = start_ref[0]

    def widen(p):
        wide[rows(p * pitch, freqs), :] = particles_ref[first + p].astype(F32)

    loop(share, widen, 8)

    def turn(f):
        for part in range(2):
            at = pl.ds(2 * f + part, share, stride=pitch)
            out[f, :, pl.ds(part * depth, depth)] = wide[at, :].astype(BF16)

    loop(freqs // 2, turn, 8)


def prep(particles, start, share):
    _, freqs, depth = particles.shape
    return call(
        functools.partial(prep_kernel, share),
        [start.reshape(1), particles],
        [((freqs // 2, share, 2 * depth), BF16)],
        [((share * (freqs + SPARE), depth), F32)],
        flops=1 << 30,
        scalar=True,
    )[0]


def weigh_kernel(fresh, positions, *refs):
    index_ref, first_ref, second_ref, doubled_ref, particles, out, energy_ref, left_ref, image = refs
    pairs, share, twice = particles.shape
    freqs, depth = 2 * pairs, twice // 2
    classes, lanes = energy_ref.shape
    pitch = freqs + SPARE
    radii = depth // 2
    lane = lax.broadcasted_iota(jnp.int32, (freqs, depth), 1)
    sign = jnp.where(lane < radii, -1.0, 1.0).astype(F32)
    doubled = doubled_ref[...]
    row = lax.broadcasted_iota(jnp.int32, (freqs, depth), 0) + index_ref[0] * freqs
    scale = jnp.where(row == 0, 1.0 / ANG, 2.0 / ANG).astype(F32) * doubled

    for k in range(classes):
        if fresh:
            half = classes // 2
            plain = (first_ref if k < half else second_ref)[k % half].astype(F32)
        else:
            total = first_ref[k].astype(F32) + second_ref[positions[k]].astype(F32)
            counts = total[freqs : freqs + 1, :] + total[freqs + 1 : freqs + 2, :]
            plain = (total[:freqs, :] / (counts + shrinkage)).astype(BF16).astype(F32)
        weighted = (plain * doubled).astype(BF16).astype(F32)
        image[rows(2 * k * pitch, freqs), :] = weighted
        image[rows((2 * k + 1) * pitch, freqs), :] = sign * pltpu.roll(weighted, radii, 1)
        energy = jnp.sum(plain * plain * scale, axis=0, keepdims=True)
        energy = jnp.broadcast_to(jnp.sum(energy, axis=1, keepdims=True), (SPARE, lanes))
        energy_ref[pl.ds(k, 1), :] = energy[:1]
        out[0, rows(2 * k * pitch + freqs, SPARE), :] = energy[:, : out.shape[2]]

    none = jnp.zeros((2 * classes, depth), BF16)

    def correlate(f):
        first, second = [
            image[pl.ds(2 * f + part, 2 * classes, stride=pitch), :].astype(BF16)
            for part in range(2)
        ]
        left = jnp.concatenate(
            [jnp.concatenate([first, none], 1), jnp.concatenate([none, second], 1)], 0
        )
        left_ref[f] = left
        place(out, f, times(left, particles[f]), classes, pitch)

    loop(pairs, correlate, 8)


def times(left, particles):
    return lax.dot_general(left, particles, (((1,), (1,)), ((), ())), preferred_element_type=F32)


def place(out, f, value, classes, pitch):
    tiles, _, width = out.shape
    spare = jnp.zeros((value.shape[0], tiles * width - value.shape[1]), F32)
    value = jnp.concatenate([value, spare], 1) if spare.size else value
    for part in range(2):
        at = pl.ds(2 * f + part, 2 * classes, stride=pitch)
        for tile in range(tiles):
            out[tile, at, :] = value[
                part * 2 * classes : (part + 1) * 2 * classes, tile * width : (tile + 1) * width
            ]


def lane_tiles(share):
    return -(-share // 128)


def weigh(index, first, second, doubled, particles, fresh, positions):
    pairs, share, twice = particles.shape
    classes = len(positions)
    lines = 2 * classes * (2 * pairs + SPARE)
    tiles = lane_tiles(share)
    return call(
        functools.partial(weigh_kernel, fresh, positions),
        [index, first, second, doubled, particles],
        [
            ((tiles, lines, 128), F32),
            ((classes, tiles * 128), F32),
            ((pairs, 4 * classes, twice), BF16),
        ],
        [((lines, twice // 2), F32)],
        flops=8 * classes * share * pairs * twice * 4,
        scalar=True,
    )


def correlate_kernel(left_ref, particles, out):
    pairs = left_ref.shape[0]
    classes = left_ref.shape[1] // 4

    def body(f):
        place(out, f, times(left_ref[f], particles[f]), classes, 2 * pairs + SPARE)

    loop(pairs, body, 8)


def correlate(left, particles):
    pairs, share, twice = particles.shape
    lines = left.shape[1] // 2 * (2 * pairs + SPARE)
    return call(
        correlate_kernel,
        [left, particles],
        [((lane_tiles(share), lines, 128), F32)],
        flops=2 * left.shape[1] * share * pairs * twice * 8,
    )[0]


def across(ref, at):
    return jnp.concatenate([ref[tile, at, :] for tile in range(ref.shape[0])], 1)


def score_kernel(index_ref, own, other, energy_ref, prior_ref, inv_hi, inv_lo, *refs):
    weights, peaks, sums, field = refs
    classes, share = energy_ref.shape
    tiles, lines, width = own.shape
    pitch = lines // (2 * classes)
    freqs = pitch - SPARE
    which = index_ref[0]
    turns = lax.broadcasted_iota(jnp.int32, (ANG, share), 0)
    offset = jnp.abs(turns - prior_ref[...])
    distance = jnp.minimum(offset, ANG - offset).astype(F32)
    prior_term = -distance * distance / (2.0 * SIGMA * SIGMA)

    def score(k, peak):
        value = jnp.concatenate(
            [
                across(ref, rows((2 * k + part) * pitch, freqs))
                for ref in (own, other)
                for part in (0, 1)
            ],
            0,
        )
        high, low = split(value)
        inner = dot(inv_hi[which], high) + (dot(inv_hi[which], low) + dot(inv_lo[which], high))
        far = other[0, rows(2 * k * pitch + freqs, SPARE), :][:1]
        energy = energy_ref[pl.ds(k, 1), :] + jnp.concatenate([far] * tiles, 1)
        scores = inner - 0.5 * energy + prior_term
        field[rows(k * ANG, ANG), :] = scores
        return jnp.maximum(peak, jnp.max(scores, axis=0, keepdims=True))

    peak = each(classes, score, jnp.full((1, share), -jnp.inf, F32))

    def weight(k, total):
        value = jnp.exp(field[rows(k * ANG, ANG), :] - peak)
        weights[k] = value.astype(BF16)
        part = jnp.sum(value, axis=0, keepdims=True)
        sums[pl.ds(k, 1), :] = part
        return total + part

    total = each(classes, weight, jnp.zeros((1, share), F32))
    line = lax.broadcasted_iota(jnp.int32, peaks.shape, 0)
    peaks[...] = jnp.where(line == 0, peak, total)


def scores(index, own, other, energy, prior, inv_hi, inv_lo):
    classes, share = energy.shape
    return call(
        score_kernel,
        [index, own, other, energy, prior, inv_hi, inv_lo],
        [((classes, ANG, share), BF16), ((8, share), F32), ((classes, share), F32)],
        [((classes * ANG, share), F32)],
        flops=6 * classes * share * ANG * ANG,
        scalar=True,
    )


def merge(first, second):
    top = jnp.maximum(first[0:1], second[0:1])
    total = first[1:2] * jnp.exp(first[0:1] - top) + second[1:2] * jnp.exp(second[0:1] - top)
    return top, total


def merge_kernel(first, second, out):
    top, total = merge(first[...], second[...])
    line = lax.broadcasted_iota(jnp.int32, out.shape, 0)
    out[...] = jnp.where(line == 0, top, total)


def turn_kernel(index_ref, weights, fwd_hi, fwd_lo, other, own):
    classes = weights.shape[0]
    tiles, lines, width = own.shape
    pitch = lines // (2 * classes)
    freqs = pitch - SPARE
    which = index_ref[0]

    def body(k, carry):
        value = dot(fwd_hi[which], weights[k]) + dot(fwd_lo[which], weights[k])
        for i, ref in enumerate((other, own)):
            for part in range(2):
                start = (2 * i + part) * freqs
                for tile in range(tiles):
                    ref[tile, rows((2 * k + part) * pitch, freqs), :] = value[
                        start : start + freqs, tile * width : (tile + 1) * width
                    ]
        return carry

    each(classes, body, 0)


def turn(index, weights, fwd_hi, fwd_lo, freqs):
    classes, _, share = weights.shape
    shape = (share // 128, 2 * classes * (freqs + SPARE), 128)
    return call(
        turn_kernel,
        [index, weights, fwd_hi, fwd_lo],
        [(shape, F32), (shape, F32)],
        flops=4 * classes * share * ANG * ANG,
        scalar=True,
    )


def scale_kernel(here, first, second, sums, other, own, send, keep, evidence_ref):
    classes, lanes = sums.shape
    share = evidence_ref.shape[1]
    pitch = own.shape[1] // (2 * classes)
    pairs = (pitch - SPARE) // 2
    top, total = merge(first[...], second[...])
    evidence_ref[...] = (top + jnp.log(total))[:, :share]
    factor = jnp.exp(here[0:1, :] - top) / total
    lane = lax.broadcasted_iota(jnp.int32, (1, lanes), 1)
    factor = jnp.where(lane < share, factor, 0.0)

    def body(f):
        for ref, out in ((other, send), (own, keep)):
            parts = [
                across(ref, pl.ds(2 * f + part, 2 * classes, stride=pitch)) * factor
                for part in range(2)
            ]
            out[f] = jnp.concatenate(parts, 0).astype(BF16)[:, :share]

    loop(pairs, body, 8)
    counts = jnp.sum(sums[...] * factor, axis=1, keepdims=True)
    high = counts.astype(BF16).astype(F32)
    column = jnp.concatenate([high, counts - high, high, high], 0)
    column = jnp.broadcast_to(column, (4 * classes, share)).astype(BF16)
    send[pairs] = column
    keep[pairs] = column


def scale(here, first, second, sums, other, own, share):
    classes = sums.shape[0]
    pairs = (own.shape[1] // (2 * classes) - SPARE) // 2
    shape = (pairs + 1, 4 * classes, share)
    return call(
        scale_kernel,
        [here, first, second, sums, other, own],
        [(shape, BF16), (shape, BF16), ((1, share), F32)],
    )


def gather_kernel(spectrum, particles, image):
    pairs, _, twice = particles.shape
    classes = spectrum.shape[1] // 4

    def body(f):
        value = dot(spectrum[f], particles[f])
        take_in(image, f, value, classes, False)

    loop(pairs, body, 8)


def take_in(image, f, value, classes, add):
    lines, depth = image.shape
    for part in range(2):
        at = pl.ds(2 * f + part, 2 * classes, stride=lines // (2 * classes))
        new = value[
            part * 2 * classes : (part + 1) * 2 * classes, part * depth : (part + 1) * depth
        ]
        image[at, :] = image[at, :] + new if add else new


def gather(spectrum, particles):
    pairs, _, twice = particles.shape
    lines = spectrum.shape[1] // 2 * (2 * pairs + SPARE)
    return call(
        gather_kernel,
        [spectrum, particles],
        [((lines, twice // 2), F32)],
        flops=2 * math.prod(spectrum.shape) * twice * 8,
    )[0]


def finish_kernel(image, mine, spectrum, particles, *refs):
    outs, held = refs[:-1], refs[-1]
    pairs, _, twice = particles.shape
    classes = spectrum.shape[1] // 4
    freqs, depth = 2 * pairs, twice // 2
    radii = depth // 2
    pitch = freqs + SPARE

    def body(f):
        value = dot(spectrum[f], particles[f])
        take_in(held, f, value, classes, False)

    loop(pairs, body, 8)
    counts = mine[pairs].astype(F32) + spectrum[pairs].astype(F32)
    lane = lax.broadcasted_iota(jnp.int32, (freqs, depth), 1)
    sign = jnp.where(lane < radii, -1.0, 1.0).astype(F32)
    each_out = classes // len(outs)
    for k in range(classes):
        out = outs[k // each_out]
        plain, turned = [
            image[rows((2 * k + part) * pitch, freqs), :]
            + held[rows((2 * k + part) * pitch, freqs), :]
            for part in range(2)
        ]
        value = plain + sign * pltpu.roll(turned, radii, 1)
        out[k % each_out, pl.ds(0, freqs), :] = value.astype(out.dtype)
        count = counts[k : k + 1, :depth] + counts[classes + k : classes + k + 1, :depth]
        out[k % each_out, pl.ds(freqs, out.shape[1] - freqs), :] = tail(count, freqs, out)


def tail(count, freqs, out):
    shape = (out.shape[1] - freqs, out.shape[2])
    line = lax.broadcasted_iota(jnp.int32, shape, 0)
    high = count.astype(BF16).astype(F32)
    return jnp.where(line == 0, high, jnp.where(line == 1, count - high, 0.0)).astype(out.dtype)


def finish(image, mine, spectrum, particles, last):
    pairs, _, twice = particles.shape
    classes = spectrum.shape[1] // 4
    depth = twice // 2
    if last:
        outs = [((classes // 2, 2 * pairs + SPARE, depth), F32)] * 2
    else:
        outs = [((classes, 2 * pairs + LONG_SPARE, depth), BF16)]
    return call(
        finish_kernel,
        [image, mine, spectrum, particles],
        outs,
        [(image.shape, F32)],
        flops=2 * math.prod(spectrum.shape) * twice * 8,
    )


def add_kernel(positions, freqs, own, other, out):
    for k, position in enumerate(positions):
        total = own[k].astype(F32) + other[position].astype(F32)
        count = total[freqs : freqs + 1, :] + total[freqs + 1 : freqs + 2, :]
        out[k, pl.ds(0, freqs), :] = total[:freqs, :].astype(out.dtype)
        out[k, pl.ds(freqs, out.shape[1] - freqs), :] = tail(count, freqs, out)


def halve_kernel(own, other, keep, send):
    half = keep.shape[0]
    for k in range(half):
        keep[k] = own[k] + other[k]
        send[k] = own[half + k] + other[half + k]


def means_kernel(own, other, out):
    freqs = out.shape[1]
    total = own[0] + other[0]
    counts = total[freqs : freqs + 1, :] + total[freqs + 1 : freqs + 2, :]
    out[0] = total[:freqs, :] / (counts + shrinkage)


def swap(value, axis, size, bit):
    return lax.ppermute(value, axis, [(i, i ^ bit) for i in range(size)])


def bits(size):
    assert size > 1 and size & (size - 1) == 0
    return [1 << i for i in range(size.bit_length() - 1)]


def shards(particles, references, noise_inv, prior_rot):
    batch, freqs, depth = particles.shape
    sides = lax.axis_size("cls")
    groups = lax.axis_size("rot")
    blocks = lax.axis_size("blk")
    assert groups == 2 and 2 * groups * freqs == ANG
    group = lax.axis_index("rot").astype(jnp.int32)
    share = batch // groups
    order = [0]
    for bit in reversed(bits(blocks)):
        order = order + [o ^ bit for o in order]
    inv_hi, inv_lo, fwd_hi, fwd_lo = tables(freqs)
    doubled = jnp.concatenate([noise_inv, noise_inv]).reshape(1, depth)
    index = group.reshape(1)
    prior = lax.dynamic_slice_in_dim(prior_rot, group * share, share, 0)
    prior = jnp.pad(prior, (0, -share % 128)).reshape(1, -1)

    other_images = prep(particles, (1 - group) * share, share)
    own_images = prep(particles, group * share, share)
    first = references
    for bit in reversed(bits(blocks)):
        second = swap(first, "blk", blocks, bit)
        if bit > 1:
            first = jnp.concatenate([first, second], 0)
    positions = list(range(blocks))
    for step in range(ITERS):
        last = step == ITERS - 1
        message, energy, left = weigh(
            index, first, second, doubled, other_images, step == 0, positions
        )
        message = swap(message, "rot", groups, 1)
        own = correlate(left, own_images)
        weights, here, sums = scores(index, own, message, energy, prior, inv_hi, inv_lo)
        first = here
        for bit in bits(sides):
            second = swap(first, "cls", sides, bit)
            if 2 * bit < sides:
                (first,) = call(merge_kernel, [first, second], [(here.shape, F32)])
        other, own = turn(index, weights, fwd_hi, fwd_lo, freqs)
        send, keep, evidence = scale(here, first, second, sums, other, own, share)
        message = swap(send, "rot", groups, 1)
        image = gather(keep, own_images)
        if not last:
            (first,) = finish(image, keep, message, other_images, last)
            for bit in bits(blocks):
                second = swap(first, "blk", blocks, bit)
                positions = [order.index(o ^ bit) for o in order]
                if 2 * bit < blocks:
                    (first,) = call(
                        functools.partial(add_kernel, positions, freqs),
                        [first, second],
                        [(first.shape, first.dtype)],
                    )
        else:
            first, second = finish(image, keep, message, other_images, last)
            for bit in bits(blocks):
                second = swap(second, "blk", blocks, bit)
                if 2 * bit < blocks:
                    shape = (first.shape[0] // 2, *first.shape[1:])
                    first, second = call(halve_kernel, [first, second], [(shape, F32)] * 2)
    (means,) = call(means_kernel, [first, second], [((1, freqs, depth), F32)])
    return means, evidence.reshape(share)


def solution(mesh):
    in_specs = (
        P(("grp", "blk"), "rot", None),
        P(("grp", "blk", "cls"), "rot", None),
        P(),
        P(("grp", "blk")),
    )
    out_specs = (P(("grp", "blk", "cls"), "rot", None), P(("grp", "blk", "rot")))
    return jax.shard_map(shards, mesh=mesh, in_specs=in_specs, out_specs=out_specs, check_vma=False)
```

time: 188 us -> 59.2 us (0.31)
  blocking collectives: 97.8 us -> 0 us
  matrix products: 33.4 us -> 0 us
  other arithmetic: 17.2 us -> 0.8 us
  Pallas kernels: 0 us -> 16.2 us
  between operations: 16 us -> 0.78 us
  waiting for transfers between devices: 6.99 us -> 21.3 us
  starting transfers between devices: 0.16 us -> 14.4 us
  local copies, waits for them, and re-layouts: 15.9 us -> 5.55 us
    psum x4 -> x0, blocking collectives: 45.4 us -> none  [the longest x2 33.7 us: shards(): counts = lax.psum(local_counts, ('blk', 'rot'))]
    dot_general x8 -> x0, matrix products: 33.4 us -> none  [the longest x2 15 us: shards(): jnp.einsum('pgfd,kcgfd->pkgcf', spectra, stacked, preferred_element_type=...]
    all_gather x4 -> x0, blocking collectives: 32.9 us -> none  [the longest x2 28.2 us: shards(): piece = lax.all_gather(source, 'blk', axis=0, tiled=True)]
    ppermute x0 -> x12, waiting for transfers between devices: none -> 21.3 us  [swap(): return lax.ppermute(value, axis, [(i, i ^ bit) for i in range(size)])]
    pallas_call x0 -> x19, Pallas kernels: none -> 16.2 us  [call(): pl.pallas_call(kernel, out_shape=[jax.ShapeDtypeStruct(*x) for x in outs]...]
    pmax x2 -> x0, blocking collectives: 14.5 us -> none  [shards(): summit = lax.pmax(local_peak, ('cls', 'rot'))]
    ppermute x0 -> x12, starting transfers between devices: none -> 14.4 us  [swap(): return lax.ppermute(value, axis, [(i, i ^ bit) for i in range(size)])]
    another operation x3 -> x0, other arithmetic: 7.45 us -> none  [the longest x1 7.22 us: pair_up(): return jnp.stack([images, flipped], 1)]
  transfers between devices with their start and end apart: 4 -> 12, of which waited for: 3 -> 10; matrix products, arithmetic and copies ran while one was open for 11% -> 3% of each run, Pallas kernels for 0% -> 12%
where the time goes in v3:
time: 59.2 us; the launch traced here: 59 us
  waiting for transfers between devices  21.3 us (36%)
  Pallas kernels  16.2 us (27%)
  starting transfers between devices  14.4 us (24%)
  local copies, waits for them, and re-layouts  5.55 us (9%)
  other arithmetic  0.8 us (1%)
  between operations  0.78 us (1%)
    ppermute x12, waiting for transfers between devices, swap(): return lax.ppermute(value, axis, [(i, i ^ bit) for i in range(size)])  21.3 us
    pallas_call x19, Pallas kernels, call(): pl.pallas_call(kernel, out_shape=[jax.ShapeDtypeStruct(*x) for x in outs]...  16.2 us
    ppermute x12, starting transfers between devices, swap(): return lax.ppermute(value, axis, [(i, i ^ bit) for i in range(size)])  14.4 us
    unnamed x15, local copies, waits for them, and re-layouts  5.46 us
  transfers between devices with their start and end apart: 12, of which 10 were waited for; matrix products, arithmetic and copies ran while one was open for 3% of the time, Pallas kernels for 12%

profile of v3, /device:TPU:0, one launch (start us, length us, event | category | flops | bytes accessed | tf_op | source)
XLA Modules:
  0.0 59.0 jit_solution(1749106222627541962)
XLA Ops:
  0.6 4.1 %collective-permute-start = (bf16[1,64,128]{2,1,0:T(8,128)(2,1)}, bf16[1,64,128]{2,1,0:T(8,128)(2,1)S(1)}, u32[]{:S(2)}, u32[]{:S(2)}) collective-permute-start(bf16[1,64,128]{2,1,0:T(8,128)(2,1)} %param.9), channel_id=1, source_target_pairs={{0,8},{4,12},{8,0},{12,4},{1,9},{5,13},{9,1},{13,5},{2,10},{6,14},... | collective-permute-start | bytes 49160 | tf_op jit(solution)/shard_map/ppermute | solution.py:491
  5.5 0.8 %maximum_bitcast_fusion.refs_3_ = f32[1,128]{1,0:T(1,128)S(1)} fusion(f32[64]{0:T(128)} %param.10), kind=kLoop, calls=%fused_computation.2 | loop fusion | flops 128 | bytes 768 | tf_op jit(solution)/shard_map/reshape | solution.py:511
  6.7 1.9 %collective-permute-start.1 = (bf16[2,64,128]{2,1,0:T(8,128)(2,1)S(1)}, bf16[2,64,128]{2,1,0:T(8,128)(2,1)S(1)}, u32[]{:S(2)}, u32[]{:S(2)}) collective-permute-start(bf16[2,64,128]{2,1,0:T(8,128)(2,1)S(1)} %constant_dynamic-update-slice_fusion.refs_1_), channel_id=1, source_target_pairs={{0,4},{4,0},{8,12},{12,8},{1,5},{5,1},{9,13},{13,9},{2,6},{6,2},{1... | collective-permute-start | bytes 98312 | tf_op jit(solution)/shard_map/ppermute | solution.py:491
  8.6 2.3 %copy-done = bf16[288,64,128]{2,1,0:T(8,128)(2,1)S(1)} copy-done((bf16[288,64,128]{2,1,0:T(8,128)(2,1)S(1)}, bf16[288,64,128]{2,1,0:T(8,128)(2,1)}, u32[]{:S(2)}) %copy-start) | copy-done | bytes 4718616
  10.9 1.3 %shard_map.95.refs_4_.particles = bf16[32,144,256]{2,1,0:T(8,128)(2,1)S(1)} custom-call(s32[1]{0:T(128)} %bitcast.2.start_ref, bf16[288,64,128]{2,1,0:T(8,128)(2,1)S(1)} %copy-done), custom_call_target="tpu_custom_call" | custom-call | flops 1073741824 | bytes 12394496 | tf_op jit(solution)/shard_map/pallas_call | solution.py:91
  12.3 2.1 %shard_map.96 = (f32[2,576,128]{2,1,0:T(8,128)}, f32[4,256]{1,0:T(4,128)S(1)}, bf16[32,16,256]{2,1,0:T(8,128)(2,1)S(1)}) custom-call(s32[1]{0:T(128)} %bitcast.refs_0_.index_ref, bf16[2,64,128]{2,1,0:T(8,128)(2,1)S(1)} %constant_dynamic-update-slice_fusion.refs_1_, bf16[2,64,128]{2,1,0:T(8,128)(2,1)S(1)} %collective-permute-done.1.refs_2_, ...), custom_call_target="tpu_custom_call" | custom-call | flops 150994944 | bytes 3604480 | tf_op jit(solution)/shard_map/pallas_call | solution.py:91
  14.4 2.3 %copy-done.1 = bf16[288,64,128]{2,1,0:T(8,128)(2,1)S(1)} copy-done((bf16[288,64,128]{2,1,0:T(8,128)(2,1)S(1)}, bf16[288,64,128]{2,1,0:T(8,128)(2,1)}, u32[]{:S(2)}) %copy-start.1) | copy-done | bytes 4718616
  16.8 1.3 %shard_map.97.particles = bf16[32,144,256]{2,1,0:T(8,128)(2,1)S(1)} custom-call(s32[1]{0:T(128)} %bitcast.3.start_ref, bf16[288,64,128]{2,1,0:T(8,128)(2,1)S(1)} %copy-done.1), custom_call_target="tpu_custom_call" | custom-call | flops 1073741824 | bytes 12394496 | tf_op jit(solution)/shard_map/pallas_call | solution.py:91
  18.1 1.1 %shard_map.98.own = f32[2,576,128]{2,1,0:T(8,128)S(1)} custom-call(bf16[32,16,256]{2,1,0:T(8,128)(2,1)S(1)} %get-tuple-element.27.left_ref, bf16[32,144,256]{2,1,0:T(8,128)(2,1)S(1)} %shard_map.97.particles), custom_call_target="tpu_custom_call" | custom-call | flops 301989888 | bytes 3211264 | tf_op jit(solution)/shard_map/pallas_call | solution.py:91
  19.2 0.9 %shard_map.99 = (bf16[4,256,256]{2,1,0:T(8,128)(2,1)S(1)}, f32[8,256]{1,0:T(8,128)S(1)}, f32[4,256]{1,0:T(4,128)S(1)}) custom-call(s32[1]{0:T(128)} %bitcast.refs_0_.index_ref, f32[2,576,128]{2,1,0:T(8,128)S(1)} %shard_map.98.own, f32[2,576,128]{2,1,0:T(8,128)S(1)} %collective-permute-done.2.other, f32[4,256]{1,0:T(4,128)S(1)} %get-tuple-element.29.energy_ref, ...), custom_call_target="tpu_custom_call" | custom-call | flops 402653184 | bytes 3350528 | tf_op jit(solution)/shard_map/pallas_call | solution.py:91
  20.1 1.6 %collective-permute-start.3 = (f32[8,256]{1,0:T(8,128)S(1)}, f32[8,256]{1,0:T(8,128)S(1)}, u32[]{:S(2)}, u32[]{:S(2)}) collective-permute-start(f32[8,256]{1,0:T(8,128)S(1)} %get-tuple-element.30.here.first), channel_id=1, source_target_pairs={{0,2},{2,0},{1,3},{3,1},{4,6},{6,4},{5,7},{7,5},{8,10},{10,8},{9,1... | collective-permute-start | bytes 24584 | tf_op jit(solution)/shard_map/ppermute | solution.py:491
  22.1 1.7 %collective-permute-done.3.second = f32[8,256]{1,0:T(8,128)S(1)} collective-permute-done((f32[8,256]{1,0:T(8,128)S(1)}, f32[8,256]{1,0:T(8,128)S(1)}, u32[]{:S(2)}, u32[]{:S(2)}) %collective-permute-start.3) | collective-permute-done | bytes 8224 | tf_op jit(solution)/shard_map/ppermute | solution.py:491
  23.8 0.8 %shard_map.101 = (bf16[33,16,144]{2,1,0:T(8,128)(2,1)S(1)}, bf16[33,16,144]{2,1,0:T(8,128)(2,1)S(1)}, f32[1,144]{1,0:T(1,128)}) custom-call(f32[8,256]{1,0:T(8,128)S(1)} %get-tuple-element.30.here.first, f32[8,256]{1,0:T(8,128)S(1)} %get-tuple-element.30.here.first, f32[8,256]{1,0:T(8,128)S(1)} %collective-permute-done.3.second, ...), custom_call_target="tpu_custom_call" | custom-call | bytes 1802240 | tf_op jit(solution)/shard_map/pallas_call | solution.py:91
  24.6 0.8 %shard_map.102.image = f32[576,128]{1,0:T(8,128)S(1)} custom-call(bf16[33,16,144]{2,1,0:T(8,128)(2,1)S(1)} %get-tuple-element.35.spectrum.mine, bf16[32,144,256]{2,1,0:T(8,128)(2,1)S(1)} %shard_map.97.particles), custom_call_target="tpu_custom_call" | custom-call | flops 311427072 | bytes 2924544 | tf_op jit(solution)/shard_map/pallas_call | solution.py:91
  25.4 0.8 %collective-permute-done.4.spectrum = bf16[33,16,144]{2,1,0:T(8,128)(2,1)S(1)} collective-permute-done((bf16[33,16,144]{2,1,0:T(8,128)(2,1)S(1)}, bf16[33,16,144]{2,1,0:T(8,128)(2,1)S(1)}, u32[]{:S(2)}, u32[]{:S(2)}) %collective-permute-start.4) | collective-permute-done | bytes 152096 | tf_op jit(solution)/shard_map/ppermute | solution.py:491
  26.1 0.9 %shard_map.103.own = bf16[4,80,128]{2,1,0:T(8,128)(2,1)S(1)} custom-call(f32[576,128]{1,0:T(8,128)S(1)} %shard_map.102.image, bf16[33,16,144]{2,1,0:T(8,128)(2,1)S(1)} %get-tuple-element.35.spectrum.mine, bf16[33,16,144]{2,1,0:T(8,128)(2,1)S(1)} %collective-permute-done.4.spectrum, bf16[32,144,256]{2,1,0:T(8,128)(2,1)S(1)} %shard_map.95.refs_4_.particles), custom_call_target="tpu_custom_call" | custom-call | flops 311427072 | bytes 3571712 | tf_op jit(solution)/shard_map/pallas_call | solution.py:91
  27.3 4.3 %collective-permute-done.5.other = bf16[4,80,128]{2,1,0:T(8,128)(2,1)S(1)} collective-permute-done((bf16[4,80,128]{2,1,0:T(8,128)(2,1)S(1)}, bf16[4,80,128]{2,1,0:T(8,128)(2,1)S(1)}, u32[]{:S(2)}, u32[]{:S(2)}) %collective-permute-start.5) | collective-permute-done | bytes 81952 | tf_op jit(solution)/shard_map/ppermute | solution.py:491
  31.6 2.7 %collective-permute-start.6 = (bf16[4,80,128]{2,1,0:T(8,128)(2,1)S(1)}, bf16[4,80,128]{2,1,0:T(8,128)(2,1)S(1)}, u32[]{:S(2)}, u32[]{:S(2)}) collective-permute-start(bf16[4,80,128]{2,1,0:T(8,128)(2,1)S(1)} %shard_map.104.refs_1_), channel_id=1, source_target_pairs={{0,8},{4,12},{8,0},{12,4},{1,9},{5,13},{9,1},{13,5},{2,10},{6,14},... | collective-permute-start | bytes 245768 | tf_op jit(solution)/shard_map/ppermute | solution.py:491
  34.3 3.5 %collective-permute-done.6.refs_2_ = bf16[4,80,128]{2,1,0:T(8,128)(2,1)S(1)} collective-permute-done((bf16[4,80,128]{2,1,0:T(8,128)(2,1)S(1)}, bf16[4,80,128]{2,1,0:T(8,128)(2,1)S(1)}, u32[]{:S(2)}, u32[]{:S(2)}) %collective-permute-start.6) | collective-permute-done | bytes 81952 | tf_op jit(solution)/shard_map/ppermute | solution.py:491
  37.8 1.2 %shard_map.105 = (f32[2,576,128]{2,1,0:T(8,128)S(1)}, f32[4,256]{1,0:T(4,128)S(1)}, bf16[32,16,256]{2,1,0:T(8,128)(2,1)S(1)}) custom-call(s32[1]{0:T(128)} %bitcast.refs_0_.index_ref, bf16[4,80,128]{2,1,0:T(8,128)(2,1)S(1)} %shard_map.104.refs_1_, bf16[4,80,128]{2,1,0:T(8,128)(2,1)S(1)} %collective-permute-done.6.refs_2_, ...), custom_call_target="tpu_custom_call" | custom-call | flops 150994944 | bytes 3702784 | tf_op jit(solution)/shard_map/pallas_call | solution.py:91
  39.1 1.1 %shard_map.106.own = f32[2,576,128]{2,1,0:T(8,128)S(1)} custom-call(bf16[32,16,256]{2,1,0:T(8,128)(2,1)S(1)} %get-tuple-element.37.left_ref, bf16[32,144,256]{2,1,0:T(8,128)(2,1)S(1)} %shard_map.97.particles), custom_call_target="tpu_custom_call" | custom-call | flops 301989888 | bytes 3211264 | tf_op jit(solution)/shard_map/pallas_call | solution.py:91
  40.2 0.9 %collective-permute-done.7.other = f32[2,576,128]{2,1,0:T(8,128)S(1)} collective-permute-done((f32[2,576,128]{2,1,0:T(8,128)S(1)}, f32[2,576,128]{2,1,0:T(8,128)S(1)}, u32[]{:S(2)}, u32[]{:S(2)}) %collective-permute-start.7) | collective-permute-done | bytes 589856 | tf_op jit(solution)/shard_map/ppermute | solution.py:491
  41.1 0.9 %shard_map.107 = (bf16[4,256,256]{2,1,0:T(8,128)(2,1)S(1)}, f32[8,256]{1,0:T(8,128)S(1)}, f32[4,256]{1,0:T(4,128)S(1)}) custom-call(s32[1]{0:T(128)} %bitcast.refs_0_.index_ref, f32[2,576,128]{2,1,0:T(8,128)S(1)} %shard_map.106.own, f32[2,576,128]{2,1,0:T(8,128)S(1)} %collective-permute-done.7.other, f32[4,256]{1,0:T(4,128)S(1)} %get-tuple-element.39.energy_ref, ...), custom_call_target="tpu_custom_call" | custom-call | flops 402653184 | bytes 3350528 | tf_op jit(solution)/shard_map/pallas_call | solution.py:91
  42.0 1.7 %collective-permute-start.8 = (f32[8,256]{1,0:T(8,128)S(1)}, f32[8,256]{1,0:T(8,128)S(1)}, u32[]{:S(2)}, u32[]{:S(2)}) collective-permute-start(f32[8,256]{1,0:T(8,128)S(1)} %get-tuple-element.40.here.first), channel_id=1, source_target_pairs={{0,2},{2,0},{1,3},{3,1},{4,6},{6,4},{5,7},{7,5},{8,10},{10,8},{9,1... | collective-permute-start | bytes 24584 | tf_op jit(solution)/shard_map/ppermute | solution.py:491
  44.1 1.6 %collective-permute-done.8.second = f32[8,256]{1,0:T(8,128)S(1)} collective-permute-done((f32[8,256]{1,0:T(8,128)S(1)}, f32[8,256]{1,0:T(8,128)S(1)}, u32[]{:S(2)}, u32[]{:S(2)}) %collective-permute-start.8) | collective-permute-done | bytes 8224 | tf_op jit(solution)/shard_map/ppermute | solution.py:491
  45.7 0.8 %shard_map.109 = (bf16[33,16,144]{2,1,0:T(8,128)(2,1)S(1)}, bf16[33,16,144]{2,1,0:T(8,128)(2,1)S(1)}, f32[1,144]{1,0:T(1,128)}) custom-call(f32[8,256]{1,0:T(8,128)S(1)} %get-tuple-element.40.here.first, f32[8,256]{1,0:T(8,128)S(1)} %get-tuple-element.40.here.first, f32[8,256]{1,0:T(8,128)S(1)} %collective-permute-done.8.second, ...), custom_call_target="tpu_custom_call" | custom-call | bytes 1802240 | tf_op jit(solution)/shard_map/pallas_call | solution.py:91
  46.5 0.8 %shard_map.110.image = f32[576,128]{1,0:T(8,128)S(1)} custom-call(bf16[33,16,144]{2,1,0:T(8,128)(2,1)S(1)} %get-tuple-element.45.spectrum.mine, bf16[32,144,256]{2,1,0:T(8,128)(2,1)S(1)} %shard_map.97.particles), custom_call_target="tpu_custom_call" | custom-call | flops 311427072 | bytes 2924544 | tf_op jit(solution)/shard_map/pallas_call | solution.py:91
  47.2 0.8 %collective-permute-done.9.spectrum = bf16[33,16,144]{2,1,0:T(8,128)(2,1)S(1)} collective-permute-done((bf16[33,16,144]{2,1,0:T(8,128)(2,1)S(1)}, bf16[33,16,144]{2,1,0:T(8,128)(2,1)S(1)}, u32[]{:S(2)}, u32[]{:S(2)}) %collective-permute-start.9) | collective-permute-done | bytes 152096 | tf_op jit(solution)/shard_map/ppermute | solution.py:491
  48.0 0.9 %shard_map.111 = (f32[2,72,128]{2,1,0:T(8,128)S(1)}, f32[2,72,128]{2,1,0:T(8,128)S(1)}) custom-call(f32[576,128]{1,0:T(8,128)S(1)} %shard_map.110.image, bf16[33,16,144]{2,1,0:T(8,128)(2,1)S(1)} %get-tuple-element.45.spectrum.mine, bf16[33,16,144]{2,1,0:T(8,128)(2,1)S(1)} %collective-permute-done.9.spectrum, ...), custom_call_target="tpu_custom_call" | custom-call | flops 311427072 | bytes 3653632 | tf_op jit(solution)/shard_map/pallas_call | solution.py:91
  49.0 4.3 %collective-permute-done.10.other = f32[2,72,128]{2,1,0:T(8,128)S(1)} collective-permute-done((f32[2,72,128]{2,1,0:T(8,128)S(1)}, f32[2,72,128]{2,1,0:T(8,128)S(1)}, u32[]{:S(2)}, u32[]{:S(2)}) %collective-permute-start.10) | collective-permute-done | bytes 73760 | tf_op jit(solution)/shard_map/ppermute | solution.py:491
  53.3 2.0 %collective-permute-start.11 = (f32[1,72,128]{2,1,0:T(8,128)S(1)}, f32[1,72,128]{2,1,0:T(8,128)S(1)}, u32[]{:S(2)}, u32[]{:S(2)}) collective-permute-start(f32[1,72,128]{2,1,0:T(8,128)S(1)} %get-tuple-element.50), channel_id=1, source_target_pairs={{0,8},{4,12},{8,0},{12,4},{1,9},{5,13},{9,1},{13,5},{2,10},{6,14},... | collective-permute-start | bytes 110600 | tf_op jit(solution)/shard_map/ppermute | solution.py:491
  55.3 3.0 %collective-permute-done.11.other = f32[1,72,128]{2,1,0:T(8,128)S(1)} collective-permute-done((f32[1,72,128]{2,1,0:T(8,128)S(1)}, f32[1,72,128]{2,1,0:T(8,128)S(1)}, u32[]{:S(2)}, u32[]{:S(2)}) %collective-permute-start.11) | collective-permute-done | bytes 36896 | tf_op jit(solution)/shard_map/ppermute | solution.py:491
  (30 shorter events, 3.2 us)
Async XLA Ops:
  0.6 6.0 %collective-permute-start = (bf16[1,64,128]{2,1,0:T(8,128)(2,1)}, bf16[1,64,128]{2,1,0:T(8,128)(2,1)S(1)}, u32[]{:S(2)}, u32[]{:S(2)}) collective-permute-start(bf16[1,64,128]{2,1,0:T(8,128)(2,1)} %param.9), channel_id=1, source_target_pairs={{0,8},{4,12},{8,0},{12,4},{1,9},{5,13},{9,1},{13,5},{2,10},{6,14},... | collective-permute-start | bytes 49160 | tf_op jit(solution)/shard_map/ppermute | solution.py:491
  6.7 5.6 %collective-permute-start.1 = (bf16[2,64,128]{2,1,0:T(8,128)(2,1)S(1)}, bf16[2,64,128]{2,1,0:T(8,128)(2,1)S(1)}, u32[]{:S(2)}, u32[]{:S(2)}) collective-permute-start(bf16[2,64,128]{2,1,0:T(8,128)(2,1)S(1)} %constant_dynamic-update-slice_fusion.refs_1_), channel_id=1, source_target_pairs={{0,4},{4,0},{8,12},{12,8},{1,5},{5,1},{9,13},{13,9},{2,6},{6,2},{1... | collective-permute-start | bytes 98312 | tf_op jit(solution)/shard_map/ppermute | solution.py:491
  8.6 2.3 %copy-start = (bf16[288,64,128]{2,1,0:T(8,128)(2,1)S(1)}, bf16[288,64,128]{2,1,0:T(8,128)(2,1)}, u32[]{:S(2)}) copy-start(bf16[288,64,128]{2,1,0:T(8,128)(2,1)} %particles_ref.3) | copy-start | bytes 14155780
  12.2 2.1 %copy-start.6 = (s32[288]{0:T(512)S(1)}, s32[288]{0:T(512)}, u32[]{:S(2)}) copy-start(s32[288]{0:T(512)} %param.11) | copy-start | bytes 3460
  14.3 4.9 %collective-permute-start.2 = (f32[2,576,128]{2,1,0:T(8,128)}, f32[2,576,128]{2,1,0:T(8,128)S(1)}, u32[]{:S(2)}, u32[]{:S(2)}) collective-permute-start(f32[2,576,128]{2,1,0:T(8,128)} %get-tuple-element.28), channel_id=1, source_target_pairs={{0,1},{1,0},{2,3},{3,2},{4,5},{5,4},{6,7},{7,6},{8,9},{9,8},{10,11... | collective-permute-start | bytes 1769480 | tf_op jit(solution)/shard_map/ppermute | solution.py:491
  14.4 2.3 %copy-start.1 = (bf16[288,64,128]{2,1,0:T(8,128)(2,1)S(1)}, bf16[288,64,128]{2,1,0:T(8,128)(2,1)}, u32[]{:S(2)}) copy-start(bf16[288,64,128]{2,1,0:T(8,128)(2,1)} %particles_ref.3) | copy-start | bytes 14155780
  18.1 1.2 %copy-start.4 = (bf16[2,256,256]{2,1,0:T(8,128)(2,1)S(1)}, bf16[2,256,256]{2,1,0:T(8,128)(2,1)}, u32[]{:S(2)}) copy-start(bf16[2,256,256]{2,1,0:T(8,128)(2,1)} %constant.20.clone.inv_hi) | copy-start | bytes 786436
  18.1 1.1 %copy-start.5 = (bf16[2,256,256]{2,1,0:T(8,128)(2,1)S(1)}, bf16[2,256,256]{2,1,0:T(8,128)(2,1)}, u32[]{:S(2)}) copy-start(bf16[2,256,256]{2,1,0:T(8,128)(2,1)} %constant.21.clone.inv_lo) | copy-start | bytes 786436
  18.1 3.6 %copy-start.2 = (bf16[2,256,256]{2,1,0:T(8,128)(2,1)S(1)}, bf16[2,256,256]{2,1,0:T(8,128)(2,1)}, u32[]{:S(2)}) copy-start(bf16[2,256,256]{2,1,0:T(8,128)(2,1)} %constant.22.clone.fwd_hi) | copy-start | bytes 786436
  18.1 3.6 %copy-start.3 = (bf16[2,256,256]{2,1,0:T(8,128)(2,1)S(1)}, bf16[2,256,256]{2,1,0:T(8,128)(2,1)}, u32[]{:S(2)}) copy-start(bf16[2,256,256]{2,1,0:T(8,128)(2,1)} %constant.23.clone.fwd_lo) | copy-start | bytes 786436
  20.1 3.7 %collective-permute-start.3 = (f32[8,256]{1,0:T(8,128)S(1)}, f32[8,256]{1,0:T(8,128)S(1)}, u32[]{:S(2)}, u32[]{:S(2)}) collective-permute-start(f32[8,256]{1,0:T(8,128)S(1)} %get-tuple-element.30.here.first), channel_id=1, source_target_pairs={{0,2},{2,0},{1,3},{3,1},{4,6},{6,4},{5,7},{7,5},{8,10},{10,8},{9,1... | collective-permute-start | bytes 24584 | tf_op jit(solution)/shard_map/ppermute | solution.py:491
  24.6 1.5 %collective-permute-start.4 = (bf16[33,16,144]{2,1,0:T(8,128)(2,1)S(1)}, bf16[33,16,144]{2,1,0:T(8,128)(2,1)S(1)}, u32[]{:S(2)}, u32[]{:S(2)}) collective-permute-start(bf16[33,16,144]{2,1,0:T(8,128)(2,1)S(1)} %get-tuple-element.36), channel_id=1, source_target_pairs={{0,1},{1,0},{2,3},{3,2},{4,5},{5,4},{6,7},{7,6},{8,9},{9,8},{10,11... | collective-permute-start | bytes 456200 | tf_op jit(solution)/shard_map/ppermute | solution.py:491
  27.0 4.6 %collective-permute-start.5 = (bf16[4,80,128]{2,1,0:T(8,128)(2,1)S(1)}, bf16[4,80,128]{2,1,0:T(8,128)(2,1)S(1)}, u32[]{:S(2)}, u32[]{:S(2)}) collective-permute-start(bf16[4,80,128]{2,1,0:T(8,128)(2,1)S(1)} %shard_map.103.own), channel_id=1, source_target_pairs={{0,4},{4,0},{8,12},{12,8},{1,5},{5,1},{9,13},{13,9},{2,6},{6,2},{1... | collective-permute-start | bytes 245768 | tf_op jit(solution)/shard_map/ppermute | solution.py:491
  31.6 6.2 %collective-permute-start.6 = (bf16[4,80,128]{2,1,0:T(8,128)(2,1)S(1)}, bf16[4,80,128]{2,1,0:T(8,128)(2,1)S(1)}, u32[]{:S(2)}, u32[]{:S(2)}) collective-permute-start(bf16[4,80,128]{2,1,0:T(8,128)(2,1)S(1)} %shard_map.104.refs_1_), channel_id=1, source_target_pairs={{0,8},{4,12},{8,0},{12,4},{1,9},{5,13},{9,1},{13,5},{2,10},{6,14},... | collective-permute-start | bytes 245768 | tf_op jit(solution)/shard_map/ppermute | solution.py:491
  39.1 2.1 %collective-permute-start.7 = (f32[2,576,128]{2,1,0:T(8,128)S(1)}, f32[2,576,128]{2,1,0:T(8,128)S(1)}, u32[]{:S(2)}, u32[]{:S(2)}) collective-permute-start(f32[2,576,128]{2,1,0:T(8,128)S(1)} %get-tuple-element.38), channel_id=1, source_target_pairs={{0,1},{1,0},{2,3},{3,2},{4,5},{5,4},{6,7},{7,6},{8,9},{9,8},{10,11... | collective-permute-start | bytes 1769480 | tf_op jit(solution)/shard_map/ppermute | solution.py:491
  42.0 3.7 %collective-permute-start.8 = (f32[8,256]{1,0:T(8,128)S(1)}, f32[8,256]{1,0:T(8,128)S(1)}, u32[]{:S(2)}, u32[]{:S(2)}) collective-permute-start(f32[8,256]{1,0:T(8,128)S(1)} %get-tuple-element.40.here.first), channel_id=1, source_target_pairs={{0,2},{2,0},{1,3},{3,1},{4,6},{6,4},{5,7},{7,5},{8,10},{10,8},{9,1... | collective-permute-start | bytes 24584 | tf_op jit(solution)/shard_map/ppermute | solution.py:491
  46.5 1.5 %collective-permute-start.9 = (bf16[33,16,144]{2,1,0:T(8,128)(2,1)S(1)}, bf16[33,16,144]{2,1,0:T(8,128)(2,1)S(1)}, u32[]{:S(2)}, u32[]{:S(2)}) collective-permute-start(bf16[33,16,144]{2,1,0:T(8,128)(2,1)S(1)} %get-tuple-element.46), channel_id=1, source_target_pairs={{0,1},{1,0},{2,3},{3,2},{4,5},{5,4},{6,7},{7,6},{8,9},{9,8},{10,11... | collective-permute-start | bytes 456200 | tf_op jit(solution)/shard_map/ppermute | solution.py:491
  48.9 4.4 %collective-permute-start.10 = (f32[2,72,128]{2,1,0:T(8,128)S(1)}, f32[2,72,128]{2,1,0:T(8,128)S(1)}, u32[]{:S(2)}, u32[]{:S(2)}) collective-permute-start(f32[2,72,128]{2,1,0:T(8,128)S(1)} %get-tuple-element.48), channel_id=1, source_target_pairs={{0,4},{4,0},{8,12},{12,8},{1,5},{5,1},{9,13},{13,9},{2,6},{6,2},{1... | collective-permute-start | bytes 221192 | tf_op jit(solution)/shard_map/ppermute | solution.py:491
  53.3 5.0 %collective-permute-start.11 = (f32[1,72,128]{2,1,0:T(8,128)S(1)}, f32[1,72,128]{2,1,0:T(8,128)S(1)}, u32[]{:S(2)}, u32[]{:S(2)}) collective-permute-start(f32[1,72,128]{2,1,0:T(8,128)S(1)} %get-tuple-element.50), channel_id=1, source_target_pairs={{0,8},{4,12},{8,0},{12,4},{1,9},{5,13},{9,1},{13,5},{2,10},{6,14},... | collective-permute-start | bytes 110600 | tf_op jit(solution)/shard_map/ppermute | solution.py:491

commit v4 on v3

v4 whole, which is shorter than its diff:
```python
import functools
import math

import jax
import jax.numpy as jnp
import numpy as np
from jax import lax
from jax.experimental import pallas as pl
from jax.experimental.pallas import tpu as pltpu
from jax.sharding import PartitionSpec as P

ANG = 256
ITERS = 2
SIGMA = 32

shrinkage = 1.0

F32 = jnp.float32
BF16 = jnp.bfloat16
SPARE = 8

dot = functools.partial(jnp.dot, preferred_element_type=F32)


def split(x):
    high = x.astype(BF16)
    return high, (x - high.astype(F32)).astype(BF16)


def tables(half_freq):
    turn = np.arange(ANG)
    inverse, forward = [], []
    for group in range(2):
        sides = {}
        for which in range(2):
            freq = which * half_freq + np.arange(half_freq)
            angle = (turn[:, None] * freq[None, :] % ANG) * (2.0 * math.pi / ANG)
            scale = np.where(freq == 0, 1.0, 2.0) / ANG
            sides[which] = (
                np.concatenate([scale * np.cos(angle), -scale * np.sin(angle)], 1),
                np.concatenate([np.cos(angle), np.sin(angle)], 1).T,
            )
        inverse.append(np.concatenate([sides[group][0], sides[1 - group][0]], 1))
        forward.append(np.concatenate([sides[1 - group][1], sides[group][1]], 0))
    result = []
    for table in (inverse, forward):
        table = np.stack(table).astype(np.float32)
        high = table.astype(BF16)
        result += [high, (table - high.astype(np.float32)).astype(BF16)]
    return [jnp.asarray(x.reshape(-1, ANG)) for x in result]


def loop(count, body, unroll):
    while count % unroll:
        unroll -= 1
    if unroll == count:
        for i in range(count):
            body(i)
        return

    def step(outer, carry):
        for inner in range(unroll):
            body(outer * unroll + inner)
        return carry

    lax.fori_loop(0, count // unroll, step, 0)


def each(count, body, init):
    if count <= 8:
        for k in range(count):
            init = body(k, init)
        return init
    return lax.fori_loop(0, count, body, init)


def rows(base, count):
    return pl.ds(pl.multiple_of(base, 8), count)


def call(kernel, ins, outs, scratch=(), flops=0, scalar=False, far=(), room=4 << 20):
    total = 0
    buffers = [(x.shape, x.dtype) for i, x in enumerate(ins) if i not in far]
    for shape, dtype in buffers + list(outs) + [x for x in scratch if isinstance(x, tuple)]:
        dims = [1, 1, *shape]
        lines = -(-dims[-2] // 16) * 16
        lanes = -(-dims[-1] // 128) * 128
        total += math.prod(dims[:-2]) * lines * lanes * jnp.dtype(dtype).itemsize
    kinds = [pltpu.VMEM] * len(ins)
    if scalar:
        kinds[0] = pltpu.SMEM
    for i in far:
        kinds[i] = pltpu.MemorySpace.HBM
    return pl.pallas_call(
        kernel,
        out_shape=[jax.ShapeDtypeStruct(*x) for x in outs],
        in_specs=[pl.BlockSpec(memory_space=kind) for kind in kinds],
        out_specs=[pl.BlockSpec(memory_space=pltpu.VMEM)] * len(outs),
        scratch_shapes=[pltpu.VMEM(*x) if isinstance(x, tuple) else x for x in scratch],
        compiler_params=pltpu.CompilerParams(vmem_limit_bytes=min(total + room, 56 << 20)),
        cost_estimate=pl.CostEstimate(flops=flops, bytes_accessed=total, transcendentals=0),
    )(*ins)


def prep_kernel(share, start_ref, particles_ref, other, own, held, wide, sems):
    chunk, freqs, depth = held.shape[1:]
    pitch = wide.shape[0] // chunk
    steps = share // chunk
    copies = []
    for i in range(2 * steps):
        first = start_ref[i // steps] + i % steps * chunk
        copy = pltpu.make_async_copy(particles_ref.at[pl.ds(first, chunk)], held.at[i], sems.at[i])
        copy.start()
        copies.append(copy)
    for i in range(2 * steps):
        out = (other, own)[i // steps]
        to = pl.ds(i % steps * chunk, chunk)
        copies[i].wait()

        def widen(p):
            wide[rows(p * pitch, freqs), :] = held[i, p].astype(F32)

        loop(chunk, widen, 8)

        def turn(f):
            for part in range(2):
                at = pl.ds(2 * f + part, chunk, stride=pitch)
                out[f, to, pl.ds(part * depth, depth)] = wide[at, :].astype(BF16)

        loop(freqs // 2, turn, 8)


def prep(particles, start, share):
    _, freqs, depth = particles.shape
    chunk = max([n for n in (16, 32, 48) if share % n == 0], default=share)
    steps = 2 * share // chunk
    return call(
        functools.partial(prep_kernel, share),
        [start, particles],
        [((freqs // 2, share, 2 * depth), BF16)] * 2,
        [
            ((steps, chunk, freqs, depth), BF16),
            ((chunk * (freqs + SPARE), depth), F32),
            pltpu.SemaphoreType.DMA((steps,)),
        ],
        flops=1 << 31,
        scalar=True,
        far=(1,),
        room=56 << 20,
    )


def tree(values):
    values = list(values)
    while len(values) > 1:
        values = [a + b for a, b in zip(values[::2], values[1::2])]
    return values[0]


def weigh_kernel(fresh, count, *refs):
    index_ref, *sources = refs[: count + 1]
    doubled_ref, particles, out, energy_ref, left_ref, image = refs[count + 1 :]
    pairs, share, twice = particles.shape
    freqs, depth = 2 * pairs, twice // 2
    classes, lanes = energy_ref.shape
    pitch = freqs + SPARE
    radii = depth // 2
    lane = lax.broadcasted_iota(jnp.int32, (freqs, depth), 1)
    sign = jnp.where(lane < radii, -1.0, 1.0).astype(F32)
    doubled = jnp.concatenate([doubled_ref[...]] * 2, 1)
    row = lax.broadcasted_iota(jnp.int32, (freqs, depth), 0) + index_ref[0] * freqs
    scale = jnp.where(row == 0, 1.0 / ANG, 2.0 / ANG).astype(F32) * doubled

    for k in range(classes):
        if fresh:
            plain = sources[k][0].astype(F32)
        else:
            sums, highs, lows = [
                tree(
                    source[pl.ds(base + (k ^ i) * step, step), :].astype(F32)
                    for i, source in enumerate(sources)
                )
                for base, step in ((0, freqs), (classes * freqs, 1), (classes * (freqs + 1), 1))
            ]
            plain = (sums / (highs + lows + shrinkage)).astype(BF16).astype(F32)
        weighted = (plain * doubled).astype(BF16).astype(F32)
        image[rows(2 * k * pitch, freqs), :] = weighted
        image[rows((2 * k + 1) * pitch, freqs), :] = sign * pltpu.roll(weighted, radii, 1)
        energy = jnp.sum(plain * plain * scale, axis=0, keepdims=True)
        energy = jnp.broadcast_to(jnp.sum(energy, axis=1, keepdims=True), (SPARE, lanes))
        energy_ref[pl.ds(k, 1), :] = energy[:1]
        out[0, rows(2 * k * pitch + freqs, SPARE), :] = energy[:, : out.shape[2]]

    none = jnp.zeros((2 * classes, depth), BF16)

    def correlate(f):
        first, second = [
            image[pl.ds(2 * f + part, 2 * classes, stride=pitch), :].astype(BF16)
            for part in range(2)
        ]
        left = jnp.concatenate(
            [jnp.concatenate([first, none], 1), jnp.concatenate([none, second], 1)], 0
        )
        left_ref[f] = left
        place(out, f, times(left, particles[f]), classes, pitch)

    loop(pairs, correlate, 8)


def times(left, particles):
    return lax.dot_general(left, particles, (((1,), (1,)), ((), ())), preferred_element_type=F32)


def place(out, f, value, classes, pitch):
    tiles, _, width = out.shape
    spare = jnp.zeros((value.shape[0], tiles * width - value.shape[1]), F32)
    value = jnp.concatenate([value, spare], 1) if spare.size else value
    for part in range(2):
        at = pl.ds(2 * f + part, 2 * classes, stride=pitch)
        for tile in range(tiles):
            out[tile, at, :] = value[
                part * 2 * classes : (part + 1) * 2 * classes, tile * width : (tile + 1) * width
            ]


def lane_tiles(share):
    return -(-share // 128)


def weigh(index, sources, inverse_noise, particles, fresh):
    pairs, share, twice = particles.shape
    classes = len(sources)
    lines = 2 * classes * (2 * pairs + SPARE)
    tiles = lane_tiles(share)
    return call(
        functools.partial(weigh_kernel, fresh, classes),
        [index, *sources, inverse_noise, particles],
        [
            ((tiles, lines, 128), F32),
            ((classes, tiles * 128), F32),
            ((pairs, 4 * classes, twice), BF16),
        ],
        [((lines, twice // 2), F32)],
        flops=8 * classes * share * pairs * twice * 4,
        scalar=True,
    )


def correlate_kernel(left_ref, particles, out):
    pairs = left_ref.shape[0]
    classes = left_ref.shape[1] // 4

    def body(f):
        place(out, f, times(left_ref[f], particles[f]), classes, 2 * pairs + SPARE)

    loop(pairs, body, 8)


def correlate(left, particles):
    pairs, share, twice = particles.shape
    lines = left.shape[1] // 2 * (2 * pairs + SPARE)
    return call(
        correlate_kernel,
        [left, particles],
        [((lane_tiles(share), lines, 128), F32)],
        flops=2 * left.shape[1] * share * pairs * twice * 8,
    )[0]


def across(ref, at):
    return jnp.concatenate([ref[tile, at, :] for tile in range(ref.shape[0])], 1)


def table_rows(index_ref, base, count):
    return pl.ds(pl.multiple_of(index_ref[0] * ANG + base, 128), count)


def score_kernel(index_ref, own, other, energy_ref, prior_ref, inv_hi, inv_lo, *refs):
    weights, peaks = refs
    classes, share = energy_ref.shape
    tiles, lines, width = own.shape
    pitch = lines // (2 * classes)
    freqs = pitch - SPARE
    which = table_rows(index_ref, 0, ANG)
    turns = lax.broadcasted_iota(jnp.int32, (ANG, share), 0)
    offset = jnp.abs(turns - prior_ref[...])
    distance = jnp.minimum(offset, ANG - offset).astype(F32)
    prior_term = -distance * distance / (2.0 * SIGMA * SIGMA)

    def score(k, peak):
        value = jnp.concatenate(
            [
                across(ref, rows((2 * k + part) * pitch, freqs))
                for ref in (own, other)
                for part in (0, 1)
            ],
            0,
        )
        high, low = split(value)
        inner = dot(inv_hi[which, :], high) + (
            dot(inv_hi[which, :], low) + dot(inv_lo[which, :], high)
        )
        far = other[0, rows(2 * k * pitch + freqs, SPARE), :][:1]
        energy = energy_ref[pl.ds(k, 1), :] + jnp.concatenate([far] * tiles, 1)
        scores = inner - 0.5 * energy + prior_term
        weights[k] = scores
        return jnp.maximum(peak, jnp.max(scores, axis=0, keepdims=True))

    peak = each(classes, score, jnp.full((1, share), -jnp.inf, F32))

    def weight(k, total):
        value = jnp.exp(weights[k] - peak)
        weights[k] = value
        return total + jnp.sum(value, axis=0, keepdims=True)

    total = each(classes, weight, jnp.zeros((1, share), F32))
    line = lax.broadcasted_iota(jnp.int32, peaks.shape, 0)
    peaks[...] = jnp.where(line == 0, peak, total)


def scores(index, own, other, energy, prior, inv_hi, inv_lo):
    classes, share = energy.shape
    return call(
        score_kernel,
        [index, own, other, energy, prior, inv_hi, inv_lo],
        [((classes, ANG, share), F32), ((8, share), F32)],
        flops=6 * classes * share * ANG * ANG,
        scalar=True,
    )


def merge(first, second):
    top = jnp.maximum(first[0:1], second[0:1])
    total = first[1:2] * jnp.exp(first[0:1] - top) + second[1:2] * jnp.exp(second[0:1] - top)
    return top, total


def merge_kernel(first, second, out):
    top, total = merge(first[...], second[...])
    line = lax.broadcasted_iota(jnp.int32, out.shape, 0)
    out[...] = jnp.where(line == 0, top, total)


def turn_kernel(index_ref, weights, here, first, second, fwd_hi, fwd_lo, *refs):
    rounded_ref, send, evidence_ref, held = refs
    classes, _, lanes = weights.shape
    share = evidence_ref.shape[1]
    pairs = send.shape[0] - 1
    top, total = merge(first[...], second[...])
    evidence_ref[...] = (top + jnp.log(total))[:, :share]
    factor = jnp.exp(here[0:1, :] - top) / total
    lane = lax.broadcasted_iota(jnp.int32, (1, lanes), 1)
    factor = jnp.where(lane < share, factor, 0.0)
    which = table_rows(index_ref, 0, ANG // 2)
    line = lax.broadcasted_iota(jnp.int32, (4 * classes, share), 0)

    def body(k, column):
        value = weights[k] * factor
        count = jnp.sum(jnp.sum(value, axis=0, keepdims=True), axis=1, keepdims=True)
        rounded = value.astype(BF16)
        rounded_ref[k] = rounded
        spread(held, k, dot(fwd_hi[which, :], rounded) + dot(fwd_lo[which, :], rounded))
        high = count.astype(BF16).astype(F32)
        return jnp.where(line == k, high, jnp.where(line == classes + k, count - high, column))

    column = each(classes, body, jnp.zeros((4 * classes, share), F32))
    send[pairs] = column.astype(BF16)

    def rearrange(f):
        send[f] = pick(held, f, classes, share)

    loop(pairs, rearrange, 8)


def spread(held, k, value):
    tiles, lines, width = held.shape
    freqs = value.shape[0] // 2
    for part in range(2):
        for tile in range(tiles):
            held[tile, rows((2 * k + part) * (freqs + SPARE), freqs), :] = value[
                part * freqs : (part + 1) * freqs, tile * width : (tile + 1) * width
            ]


def pick(held, f, classes, share):
    pitch = held.shape[1] // (2 * classes)
    parts = [
        across(held, pl.ds(2 * f + part, 2 * classes, stride=pitch)).astype(BF16)
        for part in range(2)
    ]
    return jnp.concatenate(parts, 0)[:, :share]


def turn(index, weights, here, first, second, fwd_hi, fwd_lo, freqs, share):
    classes, _, lanes = weights.shape
    return call(
        turn_kernel,
        [index, weights, here, first, second, fwd_hi, fwd_lo],
        [
            ((classes, ANG, lanes), BF16),
            ((freqs // 2 + 1, 4 * classes, share), BF16),
            ((1, share), F32),
        ],
        [((lanes // 128, 2 * classes * (freqs + SPARE), 128), F32)],
        flops=4 * classes * lanes * ANG * ANG,
        scalar=True,
    )


def gather_kernel(index_ref, rounded_ref, fwd_hi, fwd_lo, particles, image, held):
    classes = rounded_ref.shape[0]
    pairs, share, _ = particles.shape
    which = table_rows(index_ref, ANG // 2, ANG // 2)

    def body(k, carry):
        rounded = rounded_ref[k]
        spread(held, k, dot(fwd_hi[which, :], rounded) + dot(fwd_lo[which, :], rounded))
        return carry

    each(classes, body, 0)

    def accumulate(f):
        take_in(image, f, dot(pick(held, f, classes, share), particles[f]), classes)

    loop(pairs, accumulate, 8)


def gather(index, rounded, fwd_hi, fwd_lo, particles):
    pairs, share, twice = particles.shape
    classes, _, lanes = rounded.shape
    lines = 2 * classes * (2 * pairs + SPARE)
    return call(
        gather_kernel,
        [index, rounded, fwd_hi, fwd_lo, particles],
        [((lines, twice // 2), F32)],
        [((lanes // 128, lines, 128), F32)],
        flops=4 * classes * lanes * ANG * ANG,
        scalar=True,
    )[0]


def take_in(image, f, value, classes):
    lines, depth = image.shape
    for part in range(2):
        at = pl.ds(2 * f + part, 2 * classes, stride=lines // (2 * classes))
        image[at, :] = value[
            part * 2 * classes : (part + 1) * 2 * classes, part * depth : (part + 1) * depth
        ]


def finish_kernel(image, mine, spectrum, particles, *refs):
    outs, held = refs[:-1], refs[-1]
    pairs, _, twice = particles.shape
    classes = spectrum.shape[1] // 4
    freqs, depth = 2 * pairs, twice // 2
    radii = depth // 2
    pitch = freqs + SPARE

    def body(f):
        take_in(held, f, dot(spectrum[f], particles[f]), classes)

    loop(pairs, body, 8)
    counts = (mine[pairs].astype(F32) + spectrum[pairs].astype(F32))[:, :depth]
    counts = counts[:classes] + counts[classes : 2 * classes]
    lane = lax.broadcasted_iota(jnp.int32, (freqs, depth), 1)
    sign = jnp.where(lane < radii, -1.0, 1.0).astype(F32)
    for k in range(classes):
        plain, turned = [
            image[rows((2 * k + part) * pitch, freqs), :]
            + held[rows((2 * k + part) * pitch, freqs), :]
            for part in range(2)
        ]
        value = plain + sign * pltpu.roll(turned, radii, 1)
        if len(outs) == 1:
            outs[0][pl.ds(k * freqs, freqs), :] = value.astype(BF16)
        else:
            outs[k][pl.ds(0, freqs), :] = value
            outs[k][pl.ds(freqs, SPARE), :] = jnp.broadcast_to(counts[k : k + 1], (SPARE, depth))
    if len(outs) == 1:
        end = outs[0].shape[0] - classes * freqs
        high, low = split(counts)
        spare = [jnp.zeros((end - 2 * classes, depth), F32)] if end > 2 * classes else []
        tail = jnp.concatenate([high.astype(F32), low.astype(F32), *spare], 0)
        outs[0][pl.ds(classes * freqs, end), :] = tail.astype(BF16)


def finish(image, mine, spectrum, particles, last):
    pairs, _, twice = particles.shape
    classes = spectrum.shape[1] // 4
    freqs, depth = 2 * pairs, twice // 2
    if last:
        outs = [((freqs + SPARE, depth), F32)] * classes
    else:
        outs = [((classes * freqs + -(-2 * classes // 16) * 16, depth), BF16)]
    return call(
        finish_kernel,
        [image, mine, spectrum, particles],
        outs,
        [(image.shape, F32)],
        flops=2 * math.prod(spectrum.shape) * twice * 8,
    )


def means_kernel(*refs):
    parts, out = refs[:-1], refs[-1]
    freqs = out.shape[1]
    total = tree(ref[...] for ref in parts)
    out[0] = total[:freqs, :] / (total[freqs : freqs + 1, :] + shrinkage)


def swap(value, axis, size, bit):
    if not bit:
        return value
    return lax.ppermute(value, axis, [(i, i ^ bit) for i in range(size)])


def bits(size):
    assert size > 1 and size & (size - 1) == 0
    return [1 << i for i in range(size.bit_length() - 1)]


def shards(particles, references, noise_inv, prior_rot):
    batch, freqs, depth = particles.shape
    sides = lax.axis_size("cls")
    groups = lax.axis_size("rot")
    blocks = lax.axis_size("blk")
    assert groups == 2 and 2 * groups * freqs == ANG
    group = lax.axis_index("rot").astype(jnp.int32)
    share = batch // groups
    inv_hi, inv_lo, fwd_hi, fwd_lo = tables(freqs)
    inverse_noise = noise_inv.reshape(1, depth // 2)
    index = group.reshape(1)
    prior = lax.dynamic_slice_in_dim(prior_rot, group * share, share, 0)
    prior = jnp.pad(prior, (0, -share % 128)).reshape(1, -1)
    assert blocks & (blocks - 1) == 0

    sources = [swap(references, "blk", blocks, i) for i in range(blocks)]
    other_images, own_images = prep(particles, jnp.stack([1 - group, group]) * share, share)
    for step in range(ITERS):
        last = step == ITERS - 1
        message, energy, left = weigh(index, sources, inverse_noise, other_images, step == 0)
        message = swap(message, "rot", groups, 1)
        own = correlate(left, own_images)
        weights, here = scores(index, own, message, energy, prior, inv_hi, inv_lo)
        first = here
        for bit in bits(sides):
            second = swap(first, "cls", sides, bit)
            if 2 * bit < sides:
                (first,) = call(merge_kernel, [first, second], [(here.shape, F32)])
        rounded, send, evidence = turn(
            index, weights, here, first, second, fwd_hi, fwd_lo, freqs, share
        )
        message = swap(send, "rot", groups, 1)
        image = gather(index, rounded, fwd_hi, fwd_lo, own_images)
        sums = finish(image, send, message, other_images, last)
        sums = sums if last else sums * blocks
        sources = [swap(x, "blk", blocks, i) for i, x in enumerate(sums)]
    (means,) = call(means_kernel, sources, [((1, freqs, depth), F32)])
    return means, evidence.reshape(share)


def solution(mesh):
    in_specs = (
        P(("grp", "blk"), "rot", None),
        P(("grp", "blk", "cls"), "rot", None),
        P(),
        P(("grp", "blk")),
    )
    out_specs = (P(("grp", "blk", "cls"), "rot", None), P(("grp", "blk", "rot")))
    return jax.shard_map(shards, mesh=mesh, in_specs=in_specs, out_specs=out_specs, check_vma=False)
```

time: 59.2 us -> 59.1 us (level)
  waiting for transfers between devices: 21.3 us -> 15.6 us
  Pallas kernels: 16.2 us -> 20.4 us
  starting transfers between devices: 14.4 us -> 18.1 us
  local copies, waits for them, and re-layouts: 5.55 us -> 3.42 us
    ppermute x12 -> x15, waiting for transfers between devices: 21.3 us -> 15.6 us  [swap(): return lax.ppermute(value, axis, [(i, i ^ bit) for i in range(size)])]
    pallas_call x19 -> x14, Pallas kernels: 16.2 us -> 20.4 us  [call(): pl.pallas_call(kernel, out_shape=[jax.ShapeDtypeStruct(*x) for x in outs]...]
    ppermute x12 -> x15, starting transfers between devices: 14.4 us -> 18.1 us  [swap(): return lax.ppermute(value, axis, [(i, i ^ bit) for i in range(size)])]
    unnamed x15 -> x24, local copies, waits for them, and re-layouts: 5.46 us -> 3.34 us
    reshape x1 -> x0, other arithmetic: 0.8 us -> none  [shards(): doubled = jnp.concatenate([noise_inv, noise_inv]).reshape(1, depth)]
  transfers between devices with their start and end apart: 12 -> 15, of which waited for: 10 -> 11; matrix products, arithmetic and copies ran while one was open for 3% -> 1% of each run, Pallas kernels for 12% -> 19%
where the time goes in v4:
time: 59.1 us; the launch traced here: 58.8 us
  Pallas kernels  20.4 us (35%)
  starting transfers between devices  18.1 us (31%)
  waiting for transfers between devices  15.6 us (26%)
  local copies, waits for them, and re-layouts  3.42 us (6%)
  between operations  0.74 us (1%)
    pallas_call x14, Pallas kernels, call(): pl.pallas_call(kernel, out_shape=[jax.ShapeDtypeStruct(*x) for x in outs]...  20.4 us
    ppermute x15, starting transfers between devices, swap(): return lax.ppermute(value, axis, [(i, i ^ bit) for i in range(size)])  18.1 us
    ppermute x15, waiting for transfers between devices, swap(): return lax.ppermute(value, axis, [(i, i ^ bit) for i in range(size)])  15.6 us
    unnamed x24, local copies, waits for them, and re-layouts  3.34 us
  transfers between devices with their start and end apart: 15, of which 11 were waited for; matrix products, arithmetic and copies ran while one was open for 1% of the time, Pallas kernels for 19%

profile of v4, /device:TPU:0, one launch (start us, length us, event | category | flops | bytes accessed | tf_op | source)
XLA Modules:
  0.0 58.8 jit_solution(17406634287445367997)
XLA Ops:
  0.6 4.1 %collective-permute-start.1 = (bf16[1,64,128]{2,1,0:T(8,128)(2,1)}, bf16[1,64,128]{2,1,0:T(8,128)(2,1)S(1)}, u32[]{:S(2)}, u32[]{:S(2)}) collective-permute-start(bf16[1,64,128]{2,1,0:T(8,128)(2,1)} %refs_1_.1), channel_id=1, source_target_pairs={{0,8},{4,12},{8,0},{12,4},{1,9},{5,13},{9,1},{13,5},{2,10},{6,14},... | collective-permute-start | bytes 49160 | tf_op jit(solution)/shard_map/ppermute | solution.py:514
  4.7 1.6 %collective-permute-start = (bf16[1,64,128]{2,1,0:T(8,128)(2,1)}, bf16[1,64,128]{2,1,0:T(8,128)(2,1)S(1)}, u32[]{:S(2)}, u32[]{:S(2)}) collective-permute-start(bf16[1,64,128]{2,1,0:T(8,128)(2,1)} %refs_1_.1), channel_id=1, source_target_pairs={{0,4},{4,0},{8,12},{12,8},{1,5},{5,1},{9,13},{13,9},{2,6},{6,2},{1... | collective-permute-start | bytes 49160 | tf_op jit(solution)/shard_map/ppermute | solution.py:514
  6.9 6.7 %shard_map.95 = (bf16[32,144,256]{2,1,0:T(8,128)(2,1)}, bf16[32,144,256]{2,1,0:T(8,128)(2,1)}) custom-call(s32[2]{0:T(128)} %add_multiply_fusion.start_ref, bf16[288,64,128]{2,1,0:T(8,128)(2,1)} %particles_ref.1), custom_call_target="tpu_custom_call" | custom-call | flops 2147483648 | bytes 11214848 | tf_op jit(solution)/shard_map/pallas_call | solution.py:94
  13.7 1.7 %copy-done = bf16[32,144,256]{2,1,0:T(8,128)(2,1)S(1)} copy-done((bf16[32,144,256]{2,1,0:T(8,128)(2,1)S(1)}, bf16[32,144,256]{2,1,0:T(8,128)(2,1)}, u32[]{:S(2)}) %copy-start) | copy-done | bytes 2359320
  15.3 2.1 %shard_map.96 = (f32[2,576,128]{2,1,0:T(8,128)}, f32[4,256]{1,0:T(4,128)S(1)}, bf16[32,16,256]{2,1,0:T(8,128)(2,1)S(1)}) custom-call(s32[1]{0:T(128)} %bitcast.refs_0_.index_ref, bf16[1,64,128]{2,1,0:T(8,128)(2,1)S(1)} %copy-done.9, bf16[1,64,128]{2,1,0:T(8,128)(2,1)S(1)} %collective-permute-done.refs_2_, ...), custom_call_target="tpu_custom_call" | custom-call | flops 150994944 | bytes 3604480 | tf_op jit(solution)/shard_map/pallas_call | solution.py:94
  17.4 0.7 %copy-done.7 = bf16[32,16,256]{2,1,0:T(8,128)(2,1)} copy-done((bf16[32,16,256]{2,1,0:T(8,128)(2,1)}, bf16[32,16,256]{2,1,0:T(8,128)(2,1)S(1)}, u32[]{:S(2)}) %copy-start.7) | copy-done | bytes 262168
  18.2 0.9 %copy-done.8 = bf16[32,16,256]{2,1,0:T(8,128)(2,1)S(1)} copy-done((bf16[32,16,256]{2,1,0:T(8,128)(2,1)S(1)}, bf16[32,16,256]{2,1,0:T(8,128)(2,1)}, u32[]{:S(2)}) %copy-start.8) | copy-done | bytes 262168
  19.2 1.1 %shard_map.97.own = f32[2,576,128]{2,1,0:T(8,128)S(1)} custom-call(bf16[32,16,256]{2,1,0:T(8,128)(2,1)S(1)} %copy-done.8, bf16[32,144,256]{2,1,0:T(8,128)(2,1)S(1)} %copy-done.2), custom_call_target="tpu_custom_call" | custom-call | flops 301989888 | bytes 3211264 | tf_op jit(solution)/shard_map/pallas_call | solution.py:94
  20.4 0.8 %shard_map.98 = (f32[4,256,256]{2,1,0:T(8,128)S(1)}, f32[8,256]{1,0:T(8,128)S(1)}) custom-call(s32[1]{0:T(128)} %bitcast.refs_0_.index_ref, f32[2,576,128]{2,1,0:T(8,128)S(1)} %shard_map.97.own, f32[2,576,128]{2,1,0:T(8,128)S(1)} %collective-permute-done.3.other, f32[4,256]{1,0:T(4,128)S(1)} %get-tuple-element.27.energy_ref, s32[1,256]{1,0:T(1,128)S(1)} %bitcast.5, ...), custom_call_target="tpu_custom_call" | custom-call | flops 402653184 | bytes 2809856 | tf_op jit(solution)/shard_map/pallas_call | solution.py:94
  21.2 1.8 %collective-permute-start.4 = (f32[8,256]{1,0:T(8,128)S(1)}, f32[8,256]{1,0:T(8,128)S(1)}, u32[]{:S(2)}, u32[]{:S(2)}) collective-permute-start(f32[8,256]{1,0:T(8,128)S(1)} %get-tuple-element.29.here.first), channel_id=1, source_target_pairs={{0,2},{2,0},{1,3},{3,1},{4,6},{6,4},{5,7},{7,5},{8,10},{10,8},{9,1... | collective-permute-start | bytes 24584 | tf_op jit(solution)/shard_map/ppermute | solution.py:514
  22.9 1.9 %collective-permute-done.4.second = f32[8,256]{1,0:T(8,128)S(1)} collective-permute-done((f32[8,256]{1,0:T(8,128)S(1)}, f32[8,256]{1,0:T(8,128)S(1)}, u32[]{:S(2)}, u32[]{:S(2)}) %collective-permute-start.4) | collective-permute-done | bytes 8224 | tf_op jit(solution)/shard_map/ppermute | solution.py:514
  24.9 1.0 %shard_map.99 = (bf16[4,256,256]{2,1,0:T(8,128)(2,1)S(1)}, bf16[33,16,144]{2,1,0:T(8,128)(2,1)S(1)}, f32[1,144]{1,0:T(1,128)}) custom-call(s32[1]{0:T(128)} %bitcast.refs_0_.index_ref, f32[4,256,256]{2,1,0:T(8,128)S(1)} %get-tuple-element.28.weights, f32[8,256]{1,0:T(8,128)S(1)} %get-tuple-element.29.here.first, f32[8,256]{1,0:T(8,128)S(1)} %get-tuple-element.29.here.first, ...), custom_call_target="tpu_custom_call" | custom-call | flops 268435456 | bytes 3031040 | tf_op jit(solution)/shard_map/pallas_call | solution.py:94
  25.9 1.1 %shard_map.100.image = f32[576,128]{1,0:T(8,128)S(1)} custom-call(s32[1]{0:T(128)} %bitcast.refs_0_.index_ref, bf16[4,256,256]{2,1,0:T(8,128)(2,1)S(1)} %get-tuple-element.30.rounded_ref, bf16[512,256]{1,0:T(8,128)(2,1)S(1)} %copy-done.4, bf16[512,256]{1,0:T(8,128)(2,1)S(1)} %copy-done.3, bf16[32,144,256]{2,1,0:T(8,128)(2,1)S(1)} %copy-done.2), custom_call_target="tpu_custom_call" | custom-call | flops 268435456 | bytes 4300800 | tf_op jit(solution)/shard_map/pallas_call | solution.py:94
  27.5 0.9 %shard_map.101.refs_1_ = bf16[272,128]{1,0:T(8,128)(2,1)S(1)} custom-call(f32[576,128]{1,0:T(8,128)S(1)} %shard_map.100.image, bf16[33,16,144]{2,1,0:T(8,128)(2,1)S(1)} %get-tuple-element.31.mine, bf16[33,16,144]{2,1,0:T(8,128)(2,1)S(1)} %collective-permute-done.5.spectrum, bf16[32,144,256]{2,1,0:T(8,128)(2,1)S(1)} %copy-done.1), custom_call_target="tpu_custom_call" | custom-call | flops 311427072 | bytes 3559424 | tf_op jit(solution)/shard_map/pallas_call | solution.py:94
  28.3 3.9 %collective-permute-start.8 = (bf16[272,128]{1,0:T(8,128)(2,1)S(1)}, bf16[272,128]{1,0:T(8,128)(2,1)S(1)}, u32[]{:S(2)}, u32[]{:S(2)}) collective-permute-start(bf16[272,128]{1,0:T(8,128)(2,1)S(1)} %shard_map.101.refs_1_), channel_id=1, source_target_pairs={{0,12},{4,8},{8,4},{12,0},{1,13},{5,9},{9,5},{13,1},{2,14},{6,10},... | collective-permute-start | bytes 208904 | tf_op jit(solution)/shard_map/ppermute | solution.py:514
  32.2 0.6 %collective-permute-start.6 = (bf16[272,128]{1,0:T(8,128)(2,1)S(1)}, bf16[272,128]{1,0:T(8,128)(2,1)S(1)}, u32[]{:S(2)}, u32[]{:S(2)}) collective-permute-start(bf16[272,128]{1,0:T(8,128)(2,1)S(1)} %shard_map.101.refs_1_), channel_id=1, source_target_pairs={{0,4},{4,0},{8,12},{12,8},{1,5},{5,1},{9,13},{13,9},{2,6},{6,2},{1... | collective-permute-start | bytes 208904 | tf_op jit(solution)/shard_map/ppermute | solution.py:514
  32.9 2.3 %collective-permute-done.8.refs_4_ = bf16[272,128]{1,0:T(8,128)(2,1)S(1)} collective-permute-done((bf16[272,128]{1,0:T(8,128)(2,1)S(1)}, bf16[272,128]{1,0:T(8,128)(2,1)S(1)}, u32[]{:S(2)}, u32[]{:S(2)}) %collective-permute-start.8) | collective-permute-done | bytes 69664 | tf_op jit(solution)/shard_map/ppermute | solution.py:514
  35.2 2.6 %collective-permute-done.7.refs_3_ = bf16[272,128]{1,0:T(8,128)(2,1)S(1)} collective-permute-done((bf16[272,128]{1,0:T(8,128)(2,1)S(1)}, bf16[272,128]{1,0:T(8,128)(2,1)S(1)}, u32[]{:S(2)}, u32[]{:S(2)}) %collective-permute-start.7) | collective-permute-done | bytes 69664 | tf_op jit(solution)/shard_map/ppermute | solution.py:514
  38.0 1.3 %shard_map.102 = (f32[2,576,128]{2,1,0:T(8,128)S(1)}, f32[4,256]{1,0:T(4,128)S(1)}, bf16[32,16,256]{2,1,0:T(8,128)(2,1)S(1)}) custom-call(s32[1]{0:T(128)} %bitcast.refs_0_.index_ref, bf16[272,128]{1,0:T(8,128)(2,1)S(1)} %shard_map.101.refs_1_, bf16[272,128]{1,0:T(8,128)(2,1)S(1)} %collective-permute-done.6.refs_2_, ...), custom_call_target="tpu_custom_call" | custom-call | flops 150994944 | bytes 3817472 | tf_op jit(solution)/shard_map/pallas_call | solution.py:94
  39.4 1.1 %shard_map.103.own = f32[2,576,128]{2,1,0:T(8,128)S(1)} custom-call(bf16[32,16,256]{2,1,0:T(8,128)(2,1)S(1)} %get-tuple-element.32.left_ref, bf16[32,144,256]{2,1,0:T(8,128)(2,1)S(1)} %copy-done.2), custom_call_target="tpu_custom_call" | custom-call | flops 301989888 | bytes 3211264 | tf_op jit(solution)/shard_map/pallas_call | solution.py:94
  40.4 0.9 %collective-permute-done.9.other = f32[2,576,128]{2,1,0:T(8,128)S(1)} collective-permute-done((f32[2,576,128]{2,1,0:T(8,128)S(1)}, f32[2,576,128]{2,1,0:T(8,128)S(1)}, u32[]{:S(2)}, u32[]{:S(2)}) %collective-permute-start.9) | collective-permute-done | bytes 589856 | tf_op jit(solution)/shard_map/ppermute | solution.py:514
  41.4 0.8 %shard_map.104 = (f32[4,256,256]{2,1,0:T(8,128)S(1)}, f32[8,256]{1,0:T(8,128)S(1)}) custom-call(s32[1]{0:T(128)} %bitcast.refs_0_.index_ref, f32[2,576,128]{2,1,0:T(8,128)S(1)} %shard_map.103.own, f32[2,576,128]{2,1,0:T(8,128)S(1)} %collective-permute-done.9.other, f32[4,256]{1,0:T(4,128)S(1)} %get-tuple-element.34.energy_ref, s32[1,256]{1,0:T(1,128)S(1)} %bitcast.6, ...), custom_call_target="tpu_custom_call" | custom-call | flops 402653184 | bytes 2809856 | tf_op jit(solution)/shard_map/pallas_call | solution.py:94
  42.2 1.6 %collective-permute-start.10 = (f32[8,256]{1,0:T(8,128)S(1)}, f32[8,256]{1,0:T(8,128)S(1)}, u32[]{:S(2)}, u32[]{:S(2)}) collective-permute-start(f32[8,256]{1,0:T(8,128)S(1)} %get-tuple-element.36.here.first), channel_id=1, source_target_pairs={{0,2},{2,0},{1,3},{3,1},{4,6},{6,4},{5,7},{7,5},{8,10},{10,8},{9,1... | collective-permute-start | bytes 24584 | tf_op jit(solution)/shard_map/ppermute | solution.py:514
  43.8 2.1 %collective-permute-done.10.second = f32[8,256]{1,0:T(8,128)S(1)} collective-permute-done((f32[8,256]{1,0:T(8,128)S(1)}, f32[8,256]{1,0:T(8,128)S(1)}, u32[]{:S(2)}, u32[]{:S(2)}) %collective-permute-start.10) | collective-permute-done | bytes 8224 | tf_op jit(solution)/shard_map/ppermute | solution.py:514
  45.9 1.0 %shard_map.105 = (bf16[4,256,256]{2,1,0:T(8,128)(2,1)S(1)}, bf16[33,16,144]{2,1,0:T(8,128)(2,1)S(1)}, f32[1,144]{1,0:T(1,128)}) custom-call(s32[1]{0:T(128)} %bitcast.refs_0_.index_ref, f32[4,256,256]{2,1,0:T(8,128)S(1)} %get-tuple-element.35.weights, f32[8,256]{1,0:T(8,128)S(1)} %get-tuple-element.36.here.first, f32[8,256]{1,0:T(8,128)S(1)} %get-tuple-element.36.here.first, ...), custom_call_target="tpu_custom_call" | custom-call | flops 268435456 | bytes 3031040 | tf_op jit(solution)/shard_map/pallas_call | solution.py:94
  46.9 1.1 %shard_map.106.image = f32[576,128]{1,0:T(8,128)S(1)} custom-call(s32[1]{0:T(128)} %bitcast.refs_0_.index_ref, bf16[4,256,256]{2,1,0:T(8,128)(2,1)S(1)} %get-tuple-element.37.rounded_ref, bf16[512,256]{1,0:T(8,128)(2,1)S(1)} %copy-done.4, bf16[512,256]{1,0:T(8,128)(2,1)S(1)} %copy-done.3, bf16[32,144,256]{2,1,0:T(8,128)(2,1)S(1)} %copy-done.2), custom_call_target="tpu_custom_call" | custom-call | flops 268435456 | bytes 4300800 | tf_op jit(solution)/shard_map/pallas_call | solution.py:94
  48.5 0.9 %shard_map.107 = (f32[72,128]{1,0:T(8,128)S(1)}, f32[72,128]{1,0:T(8,128)S(1)}, f32[72,128]{1,0:T(8,128)S(1)}, f32[72,128]{1,0:T(8,128)S(1)}) custom-call(f32[576,128]{1,0:T(8,128)S(1)} %shard_map.106.image, bf16[33,16,144]{2,1,0:T(8,128)(2,1)S(1)} %get-tuple-element.38.mine, bf16[33,16,144]{2,1,0:T(8,128)(2,1)S(1)} %collective-permute-done.11.spectrum, ...), custom_call_target="tpu_custom_call" | custom-call | flops 311427072 | bytes 3653632 | tf_op jit(solution)/shard_map/pallas_call | solution.py:94
  49.3 1.5 %collective-permute-start.12 = (f32[72,128]{1,0:T(8,128)S(1)}, f32[72,128]{1,0:T(8,128)S(1)}, u32[]{:S(2)}, u32[]{:S(2)}) collective-permute-start(f32[72,128]{1,0:T(8,128)S(1)} %get-tuple-element.40), channel_id=1, source_target_pairs={{0,4},{4,0},{8,12},{12,8},{1,5},{5,1},{9,13},{13,9},{2,6},{6,2},{1... | collective-permute-start | bytes 110600 | tf_op jit(solution)/shard_map/ppermute | solution.py:514
  50.9 1.6 %collective-permute-start.13 = (f32[72,128]{1,0:T(8,128)S(1)}, f32[72,128]{1,0:T(8,128)S(1)}, u32[]{:S(2)}, u32[]{:S(2)}) collective-permute-start(f32[72,128]{1,0:T(8,128)S(1)} %get-tuple-element.41), channel_id=1, source_target_pairs={{0,8},{4,12},{8,0},{12,4},{1,9},{5,13},{9,1},{13,5},{2,10},{6,14},... | collective-permute-start | bytes 110600 | tf_op jit(solution)/shard_map/ppermute | solution.py:514
  52.4 1.4 %collective-permute-start.14 = (f32[72,128]{1,0:T(8,128)S(1)}, f32[72,128]{1,0:T(8,128)S(1)}, u32[]{:S(2)}, u32[]{:S(2)}) collective-permute-start(f32[72,128]{1,0:T(8,128)S(1)} %get-tuple-element.42), channel_id=1, source_target_pairs={{0,12},{4,8},{8,4},{12,0},{1,13},{5,9},{9,5},{13,1},{2,14},{6,10},... | collective-permute-start | bytes 110600 | tf_op jit(solution)/shard_map/ppermute | solution.py:514
  53.8 2.4 %collective-permute-done.13.refs_2_ = f32[72,128]{1,0:T(8,128)S(1)} collective-permute-done((f32[72,128]{1,0:T(8,128)S(1)}, f32[72,128]{1,0:T(8,128)S(1)}, u32[]{:S(2)}, u32[]{:S(2)}) %collective-permute-start.13) | collective-permute-done | bytes 36896 | tf_op jit(solution)/shard_map/ppermute | solution.py:514
  56.2 2.0 %collective-permute-done.14.refs_3_ = f32[72,128]{1,0:T(8,128)S(1)} collective-permute-done((f32[72,128]{1,0:T(8,128)S(1)}, f32[72,128]{1,0:T(8,128)S(1)}, u32[]{:S(2)}, u32[]{:S(2)}) %collective-permute-start.14) | collective-permute-done | bytes 36896 | tf_op jit(solution)/shard_map/ppermute | solution.py:514
  (39 shorter events, 2.7 us)
Async XLA Ops:
  0.6 13.0 %collective-permute-start.1 = (bf16[1,64,128]{2,1,0:T(8,128)(2,1)}, bf16[1,64,128]{2,1,0:T(8,128)(2,1)S(1)}, u32[]{:S(2)}, u32[]{:S(2)}) collective-permute-start(bf16[1,64,128]{2,1,0:T(8,128)(2,1)} %refs_1_.1), channel_id=1, source_target_pairs={{0,8},{4,12},{8,0},{12,4},{1,9},{5,13},{9,1},{13,5},{2,10},{6,14},... | collective-permute-start | bytes 49160 | tf_op jit(solution)/shard_map/ppermute | solution.py:514
  4.7 8.9 %collective-permute-start = (bf16[1,64,128]{2,1,0:T(8,128)(2,1)}, bf16[1,64,128]{2,1,0:T(8,128)(2,1)S(1)}, u32[]{:S(2)}, u32[]{:S(2)}) collective-permute-start(bf16[1,64,128]{2,1,0:T(8,128)(2,1)} %refs_1_.1), channel_id=1, source_target_pairs={{0,4},{4,0},{8,12},{12,8},{1,5},{5,1},{9,13},{13,9},{2,6},{6,2},{1... | collective-permute-start | bytes 49160 | tf_op jit(solution)/shard_map/ppermute | solution.py:514
  6.3 7.3 %collective-permute-start.2 = (bf16[1,64,128]{2,1,0:T(8,128)(2,1)}, bf16[1,64,128]{2,1,0:T(8,128)(2,1)S(1)}, u32[]{:S(2)}, u32[]{:S(2)}) collective-permute-start(bf16[1,64,128]{2,1,0:T(8,128)(2,1)} %refs_1_.1), channel_id=1, source_target_pairs={{0,12},{4,8},{8,4},{12,0},{1,13},{5,9},{9,5},{13,1},{2,14},{6,10},... | collective-permute-start | bytes 49160 | tf_op jit(solution)/shard_map/ppermute | solution.py:514
  6.9 6.8 %copy-start.9 = (bf16[1,64,128]{2,1,0:T(8,128)(2,1)S(1)}, bf16[1,64,128]{2,1,0:T(8,128)(2,1)}, u32[]{:S(2)}) copy-start(bf16[1,64,128]{2,1,0:T(8,128)(2,1)} %refs_1_.1) | copy-start | bytes 49156
  6.9 6.8 %copy-start.10 = (f32[64]{0:T(128)S(1)}, f32[64]{0:T(128)}, u32[]{:S(2)}) copy-start(f32[64]{0:T(128)} %param.10) | copy-start | bytes 772
  13.6 4.6 %copy-start.11 = (s32[288]{0:T(512)S(1)}, s32[288]{0:T(512)}, u32[]{:S(2)}) copy-start(s32[288]{0:T(512)} %param.11) | copy-start | bytes 3460
  13.7 1.7 %copy-start = (bf16[32,144,256]{2,1,0:T(8,128)(2,1)S(1)}, bf16[32,144,256]{2,1,0:T(8,128)(2,1)}, u32[]{:S(2)}) copy-start(bf16[32,144,256]{2,1,0:T(8,128)(2,1)} %get-tuple-element.23.refs_6_.particles) | copy-start | bytes 7077892
  15.3 2.9 %copy-start.2 = (bf16[32,144,256]{2,1,0:T(8,128)(2,1)S(1)}, bf16[32,144,256]{2,1,0:T(8,128)(2,1)}, u32[]{:S(2)}) copy-start(bf16[32,144,256]{2,1,0:T(8,128)(2,1)} %get-tuple-element.25.particles) | copy-start | bytes 7077892
  15.3 5.0 %copy-start.5 = (bf16[512,256]{1,0:T(8,128)(2,1)S(1)}, bf16[512,256]{1,0:T(8,128)(2,1)}, u32[]{:S(2)}) copy-start(bf16[512,256]{1,0:T(8,128)(2,1)} %constant.22.clone.inv_lo) | copy-start | bytes 786436
  15.3 5.0 %copy-start.6 = (bf16[512,256]{1,0:T(8,128)(2,1)S(1)}, bf16[512,256]{1,0:T(8,128)(2,1)}, u32[]{:S(2)}) copy-start(bf16[512,256]{1,0:T(8,128)(2,1)} %constant.8.clone.inv_hi) | copy-start | bytes 786436
  17.4 0.7 %copy-start.7 = (bf16[32,16,256]{2,1,0:T(8,128)(2,1)}, bf16[32,16,256]{2,1,0:T(8,128)(2,1)S(1)}, u32[]{:S(2)}) copy-start(bf16[32,16,256]{2,1,0:T(8,128)(2,1)S(1)} %get-tuple-element.24.left_ref) | copy-start | bytes 786436
  18.1 2.2 %collective-permute-start.3 = (f32[2,576,128]{2,1,0:T(8,128)}, f32[2,576,128]{2,1,0:T(8,128)S(1)}, u32[]{:S(2)}, u32[]{:S(2)}) collective-permute-start(f32[2,576,128]{2,1,0:T(8,128)} %get-tuple-element.26), channel_id=1, source_target_pairs={{0,1},{1,0},{2,3},{3,2},{4,5},{5,4},{6,7},{7,6},{8,9},{9,8},{10,11... | collective-permute-start | bytes 1769480 | tf_op jit(solution)/shard_map/ppermute | solution.py:514
  18.2 1.0 %copy-start.8 = (bf16[32,16,256]{2,1,0:T(8,128)(2,1)S(1)}, bf16[32,16,256]{2,1,0:T(8,128)(2,1)}, u32[]{:S(2)}) copy-start(bf16[32,16,256]{2,1,0:T(8,128)(2,1)} %copy-done.7) | copy-start | bytes 786436
  19.2 5.7 %copy-start.3 = (bf16[512,256]{1,0:T(8,128)(2,1)S(1)}, bf16[512,256]{1,0:T(8,128)(2,1)}, u32[]{:S(2)}) copy-start(bf16[512,256]{1,0:T(8,128)(2,1)} %constant.24.clone.fwd_lo) | copy-start | bytes 786436
  19.2 5.7 %copy-start.4 = (bf16[512,256]{1,0:T(8,128)(2,1)S(1)}, bf16[512,256]{1,0:T(8,128)(2,1)}, u32[]{:S(2)}) copy-start(bf16[512,256]{1,0:T(8,128)(2,1)} %constant.23.clone.fwd_hi) | copy-start | bytes 786436
  21.2 3.7 %collective-permute-start.4 = (f32[8,256]{1,0:T(8,128)S(1)}, f32[8,256]{1,0:T(8,128)S(1)}, u32[]{:S(2)}, u32[]{:S(2)}) collective-permute-start(f32[8,256]{1,0:T(8,128)S(1)} %get-tuple-element.29.here.first), channel_id=1, source_target_pairs={{0,2},{2,0},{1,3},{3,1},{4,6},{6,4},{5,7},{7,5},{8,10},{10,8},{9,1... | collective-permute-start | bytes 24584 | tf_op jit(solution)/shard_map/ppermute | solution.py:514
  24.9 2.6 %copy-start.1 = (bf16[32,144,256]{2,1,0:T(8,128)(2,1)S(1)}, bf16[32,144,256]{2,1,0:T(8,128)(2,1)}, u32[]{:S(2)}) copy-start(bf16[32,144,256]{2,1,0:T(8,128)(2,1)} %get-tuple-element.23.refs_6_.particles) | copy-start | bytes 7077892
  25.9 1.5 %collective-permute-start.5 = (bf16[33,16,144]{2,1,0:T(8,128)(2,1)S(1)}, bf16[33,16,144]{2,1,0:T(8,128)(2,1)S(1)}, u32[]{:S(2)}, u32[]{:S(2)}) collective-permute-start(bf16[33,16,144]{2,1,0:T(8,128)(2,1)S(1)} %get-tuple-element.31.mine), channel_id=1, source_target_pairs={{0,1},{1,0},{2,3},{3,2},{4,5},{5,4},{6,7},{7,6},{8,9},{9,8},{10,11... | collective-permute-start | bytes 456200 | tf_op jit(solution)/shard_map/ppermute | solution.py:514
  28.3 6.9 %collective-permute-start.8 = (bf16[272,128]{1,0:T(8,128)(2,1)S(1)}, bf16[272,128]{1,0:T(8,128)(2,1)S(1)}, u32[]{:S(2)}, u32[]{:S(2)}) collective-permute-start(bf16[272,128]{1,0:T(8,128)(2,1)S(1)} %shard_map.101.refs_1_), channel_id=1, source_target_pairs={{0,12},{4,8},{8,4},{12,0},{1,13},{5,9},{9,5},{13,1},{2,14},{6,10},... | collective-permute-start | bytes 208904 | tf_op jit(solution)/shard_map/ppermute | solution.py:514
  32.2 5.6 %collective-permute-start.7 = (bf16[272,128]{1,0:T(8,128)(2,1)S(1)}, bf16[272,128]{1,0:T(8,128)(2,1)S(1)}, u32[]{:S(2)}, u32[]{:S(2)}) collective-permute-start(bf16[272,128]{1,0:T(8,128)(2,1)S(1)} %shard_map.101.refs_1_), channel_id=1, source_target_pairs={{0,8},{4,12},{8,0},{12,4},{1,9},{5,13},{9,1},{13,5},{2,10},{6,14},... | collective-permute-start | bytes 208904 | tf_op jit(solution)/shard_map/ppermute | solution.py:514
  32.2 5.8 %collective-permute-start.6 = (bf16[272,128]{1,0:T(8,128)(2,1)S(1)}, bf16[272,128]{1,0:T(8,128)(2,1)S(1)}, u32[]{:S(2)}, u32[]{:S(2)}) collective-permute-start(bf16[272,128]{1,0:T(8,128)(2,1)S(1)} %shard_map.101.refs_1_), channel_id=1, source_target_pairs={{0,4},{4,0},{8,12},{12,8},{1,5},{5,1},{9,13},{13,9},{2,6},{6,2},{1... | collective-permute-start | bytes 208904 | tf_op jit(solution)/shard_map/ppermute | solution.py:514
  39.3 2.1 %collective-permute-start.9 = (f32[2,576,128]{2,1,0:T(8,128)S(1)}, f32[2,576,128]{2,1,0:T(8,128)S(1)}, u32[]{:S(2)}, u32[]{:S(2)}) collective-permute-start(f32[2,576,128]{2,1,0:T(8,128)S(1)} %get-tuple-element.33), channel_id=1, source_target_pairs={{0,1},{1,0},{2,3},{3,2},{4,5},{5,4},{6,7},{7,6},{8,9},{9,8},{10,11... | collective-permute-start | bytes 1769480 | tf_op jit(solution)/shard_map/ppermute | solution.py:514
  42.2 3.7 %collective-permute-start.10 = (f32[8,256]{1,0:T(8,128)S(1)}, f32[8,256]{1,0:T(8,128)S(1)}, u32[]{:S(2)}, u32[]{:S(2)}) collective-permute-start(f32[8,256]{1,0:T(8,128)S(1)} %get-tuple-element.36.here.first), channel_id=1, source_target_pairs={{0,2},{2,0},{1,3},{3,1},{4,6},{6,4},{5,7},{7,5},{8,10},{10,8},{9,1... | collective-permute-start | bytes 24584 | tf_op jit(solution)/shard_map/ppermute | solution.py:514
  46.9 1.5 %collective-permute-start.11 = (bf16[33,16,144]{2,1,0:T(8,128)(2,1)S(1)}, bf16[33,16,144]{2,1,0:T(8,128)(2,1)S(1)}, u32[]{:S(2)}, u32[]{:S(2)}) collective-permute-start(bf16[33,16,144]{2,1,0:T(8,128)(2,1)S(1)} %get-tuple-element.38.mine), channel_id=1, source_target_pairs={{0,1},{1,0},{2,3},{3,2},{4,5},{5,4},{6,7},{7,6},{8,9},{9,8},{10,11... | collective-permute-start | bytes 456200 | tf_op jit(solution)/shard_map/ppermute | solution.py:514
  49.3 4.5 %collective-permute-start.12 = (f32[72,128]{1,0:T(8,128)S(1)}, f32[72,128]{1,0:T(8,128)S(1)}, u32[]{:S(2)}, u32[]{:S(2)}) collective-permute-start(f32[72,128]{1,0:T(8,128)S(1)} %get-tuple-element.40), channel_id=1, source_target_pairs={{0,4},{4,0},{8,12},{12,8},{1,5},{5,1},{9,13},{13,9},{2,6},{6,2},{1... | collective-permute-start | bytes 110600 | tf_op jit(solution)/shard_map/ppermute | solution.py:514
  50.9 5.3 %collective-permute-start.13 = (f32[72,128]{1,0:T(8,128)S(1)}, f32[72,128]{1,0:T(8,128)S(1)}, u32[]{:S(2)}, u32[]{:S(2)}) collective-permute-start(f32[72,128]{1,0:T(8,128)S(1)} %get-tuple-element.41), channel_id=1, source_target_pairs={{0,8},{4,12},{8,0},{12,4},{1,9},{5,13},{9,1},{13,5},{2,10},{6,14},... | collective-permute-start | bytes 110600 | tf_op jit(solution)/shard_map/ppermute | solution.py:514
  52.4 5.8 %collective-permute-start.14 = (f32[72,128]{1,0:T(8,128)S(1)}, f32[72,128]{1,0:T(8,128)S(1)}, u32[]{:S(2)}, u32[]{:S(2)}) collective-permute-start(f32[72,128]{1,0:T(8,128)S(1)} %get-tuple-element.42), channel_id=1, source_target_pairs={{0,12},{4,8},{8,4},{12,0},{1,13},{5,9},{9,5},{13,1},{2,14},{6,10},... | collective-permute-start | bytes 110600 | tf_op jit(solution)/shard_map/ppermute | solution.py:514

commit v5 on v4

--- a/solution.py
+++ b/solution.py
@@ -78,7 +78,7 @@
     return pl.ds(pl.multiple_of(base, 8), count)
 
 
-def call(kernel, ins, outs, scratch=(), flops=0, scalar=False, far=(), room=4 << 20):
+def call(kernel, ins, outs, scratch=(), flops=0, far=(), room=4 << 20):
     total = 0
     buffers = [(x.shape, x.dtype) for i, x in enumerate(ins) if i not in far]
     for shape, dtype in buffers + list(outs) + [x for x in scratch if isinstance(x, tuple)]:
@@ -87,8 +87,6 @@
         lanes = -(-dims[-1] // 128) * 128
         total += math.prod(dims[:-2]) * lines * lanes * jnp.dtype(dtype).itemsize
     kinds = [pltpu.VMEM] * len(ins)
-    if scalar:
-        kinds[0] = pltpu.SMEM
     for i in far:
         kinds[i] = pltpu.MemorySpace.HBM
     return pl.pallas_call(
@@ -102,13 +100,14 @@
     )(*ins)
 
 
-def prep_kernel(share, start_ref, particles_ref, other, own, held, wide, sems):
+def prep_kernel(share, particles_ref, other, own, held, wide, sems):
     chunk, freqs, depth = held.shape[1:]
     pitch = wide.shape[0] // chunk
     steps = share // chunk
+    group = lax.axis_index("rot")
     copies = []
     for i in range(2 * steps):
-        first = start_ref[i // steps] + i % steps * chunk
+        first = jnp.where(i < steps, 1 - group, group) * share + i % steps * chunk
         copy = pltpu.make_async_copy(particles_ref.at[pl.ds(first, chunk)], held.at[i], sems.at[i])
         copy.start()
         copies.append(copy)
@@ -130,13 +129,13 @@
         loop(freqs // 2, turn, 8)
 
 
-def prep(particles, start, share):
+def prep(particles, share):
     _, freqs, depth = particles.shape
     chunk = max([n for n in (16, 32, 48) if share % n == 0], default=share)
     steps = 2 * share // chunk
     return call(
         functools.partial(prep_kernel, share),
-        [start, particles],
+        [particles],
         [((freqs // 2, share, 2 * depth), BF16)] * 2,
         [
             ((steps, chunk, freqs, depth), BF16),
@@ -144,9 +143,8 @@
             pltpu.SemaphoreType.DMA((steps,)),
         ],
         flops=1 << 31,
-        scalar=True,
-        far=(1,),
-        room=56 << 20,
+        far=(0,),
+        room=36 << 20,
     )
 
 
@@ -158,8 +156,8 @@
 
 
 def weigh_kernel(fresh, count, *refs):
-    index_ref, *sources = refs[: count + 1]
-    doubled_ref, particles, out, energy_ref, left_ref, image = refs[count + 1 :]
+    sources = refs[:count]
+    doubled_ref, particles, out, energy_ref, left_ref, image = refs[count:]
     pairs, share, twice = particles.shape
     freqs, depth = 2 * pairs, twice // 2
     classes, lanes = energy_ref.shape
@@ -168,7 +166,7 @@
     lane = lax.broadcasted_iota(jnp.int32, (freqs, depth), 1)
     sign = jnp.where(lane < radii, -1.0, 1.0).astype(F32)
     doubled = jnp.concatenate([doubled_ref[...]] * 2, 1)
-    row = lax.broadcasted_iota(jnp.int32, (freqs, depth), 0) + index_ref[0] * freqs
+    row = lax.broadcasted_iota(jnp.int32, (freqs, depth), 0) + lax.axis_index("rot") * freqs
     scale = jnp.where(row == 0, 1.0 / ANG, 2.0 / ANG).astype(F32) * doubled
 
     for k in range(classes):
@@ -227,14 +225,14 @@
     return -(-share // 128)
 
 
-def weigh(index, sources, inverse_noise, particles, fresh):
+def weigh(sources, inverse_noise, particles, fresh):
     pairs, share, twice = particles.shape
     classes = len(sources)
     lines = 2 * classes * (2 * pairs + SPARE)
     tiles = lane_tiles(share)
     return call(
         functools.partial(weigh_kernel, fresh, classes),
-        [index, *sources, inverse_noise, particles],
+        [*sources, inverse_noise, particles],
         [
             ((tiles, lines, 128), F32),
             ((classes, tiles * 128), F32),
@@ -242,7 +240,6 @@
         ],
         [((lines, twice // 2), F32)],
         flops=8 * classes * share * pairs * twice * 4,
-        scalar=True,
     )
 
 
@@ -271,17 +268,17 @@
     return jnp.concatenate([ref[tile, at, :] for tile in range(ref.shape[0])], 1)
 
 
-def table_rows(index_ref, base, count):
-    return pl.ds(pl.multiple_of(index_ref[0] * ANG + base, 128), count)
-
-
-def score_kernel(index_ref, own, other, energy_ref, prior_ref, inv_hi, inv_lo, *refs):
+def table_rows(base, count):
+    return pl.ds(pl.multiple_of(lax.axis_index("rot") * ANG + base, 128), count)
+
+
+def score_kernel(own, other, energy_ref, prior_ref, inv_hi, inv_lo, *refs):
     weights, peaks = refs
     classes, share = energy_ref.shape
     tiles, lines, width = own.shape
     pitch = lines // (2 * classes)
     freqs = pitch - SPARE
-    which = table_rows(index_ref, 0, ANG)
+    which = table_rows(0, ANG)
     turns = lax.broadcasted_iota(jnp.int32, (ANG, share), 0)
     offset = jnp.abs(turns - prior_ref[...])
     distance = jnp.minimum(offset, ANG - offset).astype(F32)
@@ -318,14 +315,13 @@
     peaks[...] = jnp.where(line == 0, peak, total)
 
 
-def scores(index, own, other, energy, prior, inv_hi, inv_lo):
+def scores(own, other, energy, prior, inv_hi, inv_lo):
     classes, share = energy.shape
     return call(
         score_kernel,
-        [index, own, other, energy, prior, inv_hi, inv_lo],
+        [own, other, energy, prior, inv_hi, inv_lo],
         [((classes, ANG, share), F32), ((8, share), F32)],
         flops=6 * classes * share * ANG * ANG,
-        scalar=True,
     )
 
 
@@ -341,7 +337,7 @@
     out[...] = jnp.where(line == 0, top, total)
 
 
-def turn_kernel(index_ref, weights, here, first, second, fwd_hi, fwd_lo, *refs):
+def turn_kernel(weights, here, first, second, fwd_hi, fwd_lo, *refs):
     rounded_ref, send, evidence_ref, held = refs
     classes, _, lanes = weights.shape
     share = evidence_ref.shape[1]
@@ -351,7 +347,7 @@
     factor = jnp.exp(here[0:1, :] - top) / total
     lane = lax.broadcasted_iota(jnp.int32, (1, lanes), 1)
     factor = jnp.where(lane < share, factor, 0.0)
-    which = table_rows(index_ref, 0, ANG // 2)
+    which = table_rows(0, ANG // 2)
     line = lax.broadcasted_iota(jnp.int32, (4 * classes, share), 0)
 
     def body(k, column):
@@ -391,11 +387,11 @@
     return jnp.concatenate(parts, 0)[:, :share]
 
 
-def turn(index, weights, here, first, second, fwd_hi, fwd_lo, freqs, share):
+def turn(weights, here, first, second, fwd_hi, fwd_lo, freqs, share):
     classes, _, lanes = weights.shape
     return call(
         turn_kernel,
-        [index, weights, here, first, second, fwd_hi, fwd_lo],
+        [weights, here, first, second, fwd_hi, fwd_lo],
         [
             ((classes, ANG, lanes), BF16),
             ((freqs // 2 + 1, 4 * classes, share), BF16),
@@ -403,14 +399,13 @@
         ],
         [((lanes // 128, 2 * classes * (freqs + SPARE), 128), F32)],
         flops=4 * classes * lanes * ANG * ANG,
-        scalar=True,
-    )
-
-
-def gather_kernel(index_ref, rounded_ref, fwd_hi, fwd_lo, particles, image, held):
+    )
+
+
+def gather_kernel(rounded_ref, fwd_hi, fwd_lo, particles, image, held):
     classes = rounded_ref.shape[0]
     pairs, share, _ = particles.shape
-    which = table_rows(index_ref, ANG // 2, ANG // 2)
+    which = table_rows(ANG // 2, ANG // 2)
 
     def body(k, carry):
         rounded = rounded_ref[k]
@@ -425,17 +420,16 @@
     loop(pairs, accumulate, 8)
 
 
-def gather(index, rounded, fwd_hi, fwd_lo, particles):
+def gather(rounded, fwd_hi, fwd_lo, particles):
     pairs, share, twice = particles.shape
     classes, _, lanes = rounded.shape
     lines = 2 * classes * (2 * pairs + SPARE)
     return call(
         gather_kernel,
-        [index, rounded, fwd_hi, fwd_lo, particles],
+        [rounded, fwd_hi, fwd_lo, particles],
         [((lines, twice // 2), F32)],
         [((lanes // 128, lines, 128), F32)],
         flops=4 * classes * lanes * ANG * ANG,
-        scalar=True,
     )[0]
 
 
@@ -502,7 +496,8 @@
 
 
 def means_kernel(*refs):
-    parts, out = refs[:-1], refs[-1]
+    *parts, evidence_ref, out, last_ref = refs
+    last_ref[...] = evidence_ref[...]
     freqs = out.shape[1]
     total = tree(ref[...] for ref in parts)
     out[0] = total[:freqs, :] / (total[freqs : freqs + 1, :] + shrinkage)
@@ -529,33 +524,32 @@
     share = batch // groups
     inv_hi, inv_lo, fwd_hi, fwd_lo = tables(freqs)
     inverse_noise = noise_inv.reshape(1, depth // 2)
-    index = group.reshape(1)
     prior = lax.dynamic_slice_in_dim(prior_rot, group * share, share, 0)
     prior = jnp.pad(prior, (0, -share % 128)).reshape(1, -1)
     assert blocks & (blocks - 1) == 0
 
     sources = [swap(references, "blk", blocks, i) for i in range(blocks)]
-    other_images, own_images = prep(particles, jnp.stack([1 - group, group]) * share, share)
+    other_images, own_images = prep(particles, share)
     for step in range(ITERS):
         last = step == ITERS - 1
-        message, energy, left = weigh(index, sources, inverse_noise, other_images, step == 0)
+        message, energy, left = weigh(sources, inverse_noise, other_images, step == 0)
         message = swap(message, "rot", groups, 1)
         own = correlate(left, own_images)
-        weights, here = scores(index, own, message, energy, prior, inv_hi, inv_lo)
+        weights, here = scores(own, message, energy, prior, inv_hi, inv_lo)
         first = here
         for bit in bits(sides):
             second = swap(first, "cls", sides, bit)
             if 2 * bit < sides:
                 (first,) = call(merge_kernel, [first, second], [(here.shape, F32)])
-        rounded, send, evidence = turn(
-            index, weights, here, first, second, fwd_hi, fwd_lo, freqs, share
-        )
+        rounded, send, evidence = turn(weights, here, first, second, fwd_hi, fwd_lo, freqs, share)
         message = swap(send, "rot", groups, 1)
-        image = gather(index, rounded, fwd_hi, fwd_lo, own_images)
+        image = gather(rounded, fwd_hi, fwd_lo, own_images)
         sums = finish(image, send, message, other_images, last)
         sums = sums if last else sums * blocks
         sources = [swap(x, "blk", blocks, i) for i, x in enumerate(sums)]
-    (means,) = call(means_kernel, sources, [((1, freqs, depth), F32)])
+    means, evidence = call(
+        means_kernel, [*sources, evidence], [((1, freqs, depth), F32), (evidence.shape, F32)]
+    )
     return means, evidence.reshape(share)
 
 

time: 59.1 us -> 55.6 us (0.941)
  Pallas kernels: 20.4 us -> 17 us
  waiting for transfers between devices: 15.6 us -> 16.7 us
    pallas_call x14, Pallas kernels: 20.4 us -> 17 us  [call(): pl.pallas_call(kernel, out_shape=[jax.ShapeDtypeStruct(*x) for x in outs]...]
    ppermute x15, waiting for transfers between devices: 15.6 us -> 16.7 us  [swap(): return lax.ppermute(value, axis, [(i, i ^ bit) for i in range(size)])]
    unnamed x24 -> x22, local copies, waits for them, and re-layouts: 3.34 us -> 3.1 us
  transfers between devices with their start and end apart: 15 -> 15, of which waited for: 11 -> 11; matrix products, arithmetic and copies ran while one was open for 1% -> 0% of each run, Pallas kernels for 19% -> 15%
where the time goes in v5:
time: 55.6 us; the launch traced here: 55.4 us
  starting transfers between devices  17.8 us (32%)
  Pallas kernels  17 us (31%)
  waiting for transfers between devices  16.7 us (30%)
  local copies, waits for them, and re-layouts  3.18 us (6%)
  between operations  0.74 us (1%)
    ppermute x15, starting transfers between devices, swap(): return lax.ppermute(value, axis, [(i, i ^ bit) for i in range(size)])  17.8 us
    pallas_call x14, Pallas kernels, call(): pl.pallas_call(kernel, out_shape=[jax.ShapeDtypeStruct(*x) for x in outs]...  17 us
    ppermute x15, waiting for transfers between devices, swap(): return lax.ppermute(value, axis, [(i, i ^ bit) for i in range(size)])  16.7 us
    unnamed x22, local copies, waits for them, and re-layouts  3.1 us
  transfers between devices with their start and end apart: 15, of which 11 were waited for; matrix products, arithmetic and copies ran while one was open for 0% of the time, Pallas kernels for 15%

profile of v5, /device:TPU:0, one launch (start us, length us, event | category | flops | bytes accessed | tf_op | source)
XLA Modules:
  0.0 55.4 jit_solution(17590563493098436852)
XLA Ops:
  0.6 4.1 %collective-permute-start.1 = (bf16[1,64,128]{2,1,0:T(8,128)(2,1)}, bf16[1,64,128]{2,1,0:T(8,128)(2,1)S(1)}, u32[]{:S(2)}, u32[]{:S(2)}) collective-permute-start(bf16[1,64,128]{2,1,0:T(8,128)(2,1)} %refs_0_.1), channel_id=1, source_target_pairs={{0,8},{4,12},{8,0},{12,4},{1,9},{5,13},{9,1},{13,5},{2,10},{6,14},... | collective-permute-start | bytes 49160 | tf_op jit(solution)/shard_map/ppermute | solution.py:509
  4.8 1.6 %collective-permute-start = (bf16[1,64,128]{2,1,0:T(8,128)(2,1)}, bf16[1,64,128]{2,1,0:T(8,128)(2,1)S(1)}, u32[]{:S(2)}, u32[]{:S(2)}) collective-permute-start(bf16[1,64,128]{2,1,0:T(8,128)(2,1)} %refs_0_.1), channel_id=1, source_target_pairs={{0,4},{4,0},{8,12},{12,8},{1,5},{5,1},{9,13},{13,9},{2,6},{6,2},{1... | collective-permute-start | bytes 49160 | tf_op jit(solution)/shard_map/ppermute | solution.py:509
  6.3 3.8 %shard_map.95 = (bf16[32,144,256]{2,1,0:T(8,128)(2,1)S(1)}, bf16[32,144,256]{2,1,0:T(8,128)(2,1)S(1)}) custom-call(bf16[288,64,128]{2,1,0:T(8,128)(2,1)} %particles_ref.1), custom_call_target="tpu_custom_call" | custom-call | flops 2147483648 | bytes 11206656 | tf_op jit(solution)/shard_map/pallas_call | solution.py:92
  10.2 1.9 %collective-permute-done.2.refs_3_ = bf16[1,64,128]{2,1,0:T(8,128)(2,1)S(1)} collective-permute-done((bf16[1,64,128]{2,1,0:T(8,128)(2,1)}, bf16[1,64,128]{2,1,0:T(8,128)(2,1)S(1)}, u32[]{:S(2)}, u32[]{:S(2)}) %collective-permute-start.2) | collective-permute-done | bytes 16416 | tf_op jit(solution)/shard_map/ppermute | solution.py:509
  12.1 2.1 %shard_map.96 = (f32[2,576,128]{2,1,0:T(8,128)}, f32[4,256]{1,0:T(4,128)S(1)}, bf16[32,16,256]{2,1,0:T(8,128)(2,1)S(1)}) custom-call(bf16[1,64,128]{2,1,0:T(8,128)(2,1)S(1)} %copy-done.8, bf16[1,64,128]{2,1,0:T(8,128)(2,1)S(1)} %collective-permute-done.refs_1_, bf16[1,64,128]{2,1,0:T(8,128)(2,1)S(1)} %collective-permute-done.1.refs_2_, ...), custom_call_target="tpu_custom_call" | custom-call | flops 150994944 | bytes 3596288 | tf_op jit(solution)/shard_map/pallas_call | solution.py:92
  14.2 1.4 %copy-done = bf16[32,144,256]{2,1,0:T(8,128)(2,1)} copy-done((bf16[32,144,256]{2,1,0:T(8,128)(2,1)}, bf16[32,144,256]{2,1,0:T(8,128)(2,1)S(1)}, u32[]{:S(2)}) %copy-start) | copy-done | bytes 2359320
  15.6 0.7 %copy-done.6 = bf16[32,16,256]{2,1,0:T(8,128)(2,1)} copy-done((bf16[32,16,256]{2,1,0:T(8,128)(2,1)}, bf16[32,16,256]{2,1,0:T(8,128)(2,1)S(1)}, u32[]{:S(2)}) %copy-start.6) | copy-done | bytes 262168
  16.4 0.9 %copy-done.7 = bf16[32,16,256]{2,1,0:T(8,128)(2,1)S(1)} copy-done((bf16[32,16,256]{2,1,0:T(8,128)(2,1)S(1)}, bf16[32,16,256]{2,1,0:T(8,128)(2,1)}, u32[]{:S(2)}) %copy-start.7) | copy-done | bytes 262168
  17.4 1.1 %shard_map.97.own = f32[2,576,128]{2,1,0:T(8,128)S(1)} custom-call(bf16[32,16,256]{2,1,0:T(8,128)(2,1)S(1)} %copy-done.7, bf16[32,144,256]{2,1,0:T(8,128)(2,1)S(1)} %get-tuple-element.27.particles), custom_call_target="tpu_custom_call" | custom-call | flops 301989888 | bytes 3211264 | tf_op jit(solution)/shard_map/pallas_call | solution.py:92
  18.5 0.8 %shard_map.98 = (f32[4,256,256]{2,1,0:T(8,128)S(1)}, f32[8,256]{1,0:T(8,128)S(1)}) custom-call(f32[2,576,128]{2,1,0:T(8,128)S(1)} %shard_map.97.own, f32[2,576,128]{2,1,0:T(8,128)S(1)} %collective-permute-done.3.other, f32[4,256]{1,0:T(4,128)S(1)} %get-tuple-element.29.energy_ref, s32[1,256]{1,0:T(1,128)S(1)} %bitcast.3, bf16[512,256]{1,0:T(8,128)(2,1)S(1)} %copy-done.5, ...), custom_call_target="tpu_custom_call" | custom-call | flops 402653184 | bytes 2801664 | tf_op jit(solution)/shard_map/pallas_call | solution.py:92
  19.4 1.6 %collective-permute-start.4 = (f32[8,256]{1,0:T(8,128)S(1)}, f32[8,256]{1,0:T(8,128)S(1)}, u32[]{:S(2)}, u32[]{:S(2)}) collective-permute-start(f32[8,256]{1,0:T(8,128)S(1)} %get-tuple-element.31.here.first), channel_id=1, source_target_pairs={{0,2},{2,0},{1,3},{3,1},{4,6},{6,4},{5,7},{7,5},{8,10},{10,8},{9,1... | collective-permute-start | bytes 24584 | tf_op jit(solution)/shard_map/ppermute | solution.py:509
  20.9 2.2 %collective-permute-done.4.second = f32[8,256]{1,0:T(8,128)S(1)} collective-permute-done((f32[8,256]{1,0:T(8,128)S(1)}, f32[8,256]{1,0:T(8,128)S(1)}, u32[]{:S(2)}, u32[]{:S(2)}) %collective-permute-start.4) | collective-permute-done | bytes 8224 | tf_op jit(solution)/shard_map/ppermute | solution.py:509
  23.1 1.0 %shard_map.99 = (bf16[4,256,256]{2,1,0:T(8,128)(2,1)S(1)}, bf16[33,16,144]{2,1,0:T(8,128)(2,1)S(1)}, f32[1,144]{1,0:T(1,128)}) custom-call(f32[4,256,256]{2,1,0:T(8,128)S(1)} %get-tuple-element.30.weights, f32[8,256]{1,0:T(8,128)S(1)} %get-tuple-element.31.here.first, f32[8,256]{1,0:T(8,128)S(1)} %get-tuple-element.31.here.first, ...), custom_call_target="tpu_custom_call" | custom-call | flops 268435456 | bytes 3022848 | tf_op jit(solution)/shard_map/pallas_call | solution.py:92
  24.1 1.1 %shard_map.100.image = f32[576,128]{1,0:T(8,128)S(1)} custom-call(bf16[4,256,256]{2,1,0:T(8,128)(2,1)S(1)} %get-tuple-element.32.rounded_ref, bf16[512,256]{1,0:T(8,128)(2,1)S(1)} %copy-done.3, bf16[512,256]{1,0:T(8,128)(2,1)S(1)} %copy-done.2, bf16[32,144,256]{2,1,0:T(8,128)(2,1)S(1)} %get-tuple-element.27.particles), custom_call_target="tpu_custom_call" | custom-call | flops 268435456 | bytes 4292608 | tf_op jit(solution)/shard_map/pallas_call | solution.py:92
  25.6 0.9 %shard_map.101.refs_0_ = bf16[272,128]{1,0:T(8,128)(2,1)S(1)} custom-call(f32[576,128]{1,0:T(8,128)S(1)} %shard_map.100.image, bf16[33,16,144]{2,1,0:T(8,128)(2,1)S(1)} %get-tuple-element.33.mine, bf16[33,16,144]{2,1,0:T(8,128)(2,1)S(1)} %collective-permute-done.5.spectrum, bf16[32,144,256]{2,1,0:T(8,128)(2,1)S(1)} %copy-done.1), custom_call_target="tpu_custom_call" | custom-call | flops 311427072 | bytes 3559424 | tf_op jit(solution)/shard_map/pallas_call | solution.py:92
  26.5 2.0 %collective-permute-start.8 = (bf16[272,128]{1,0:T(8,128)(2,1)S(1)}, bf16[272,128]{1,0:T(8,128)(2,1)S(1)}, u32[]{:S(2)}, u32[]{:S(2)}) collective-permute-start(bf16[272,128]{1,0:T(8,128)(2,1)S(1)} %shard_map.101.refs_0_), channel_id=1, source_target_pairs={{0,12},{4,8},{8,4},{12,0},{1,13},{5,9},{9,5},{13,1},{2,14},{6,10},... | collective-permute-start | bytes 208904 | tf_op jit(solution)/shard_map/ppermute | solution.py:509
  28.6 2.4 %collective-permute-start.6 = (bf16[272,128]{1,0:T(8,128)(2,1)S(1)}, bf16[272,128]{1,0:T(8,128)(2,1)S(1)}, u32[]{:S(2)}, u32[]{:S(2)}) collective-permute-start(bf16[272,128]{1,0:T(8,128)(2,1)S(1)} %shard_map.101.refs_0_), channel_id=1, source_target_pairs={{0,4},{4,0},{8,12},{12,8},{1,5},{5,1},{9,13},{13,9},{2,6},{6,2},{1... | collective-permute-start | bytes 208904 | tf_op jit(solution)/shard_map/ppermute | solution.py:509
  31.0 2.5 %collective-permute-done.8.refs_3_ = bf16[272,128]{1,0:T(8,128)(2,1)S(1)} collective-permute-done((bf16[272,128]{1,0:T(8,128)(2,1)S(1)}, bf16[272,128]{1,0:T(8,128)(2,1)S(1)}, u32[]{:S(2)}, u32[]{:S(2)}) %collective-permute-start.8) | collective-permute-done | bytes 69664 | tf_op jit(solution)/shard_map/ppermute | solution.py:509
  33.5 2.1 %collective-permute-done.7.refs_2_ = bf16[272,128]{1,0:T(8,128)(2,1)S(1)} collective-permute-done((bf16[272,128]{1,0:T(8,128)(2,1)S(1)}, bf16[272,128]{1,0:T(8,128)(2,1)S(1)}, u32[]{:S(2)}, u32[]{:S(2)}) %collective-permute-start.7) | collective-permute-done | bytes 69664 | tf_op jit(solution)/shard_map/ppermute | solution.py:509
  35.6 1.3 %shard_map.102 = (f32[2,576,128]{2,1,0:T(8,128)S(1)}, f32[4,256]{1,0:T(4,128)S(1)}, bf16[32,16,256]{2,1,0:T(8,128)(2,1)S(1)}) custom-call(bf16[272,128]{1,0:T(8,128)(2,1)S(1)} %shard_map.101.refs_0_, bf16[272,128]{1,0:T(8,128)(2,1)S(1)} %collective-permute-done.6.refs_1_, bf16[272,128]{1,0:T(8,128)(2,1)S(1)} %collective-permute-done.7.refs_2_, ...), custom_call_target="tpu_custom_call" | custom-call | flops 150994944 | bytes 3809280 | tf_op jit(solution)/shard_map/pallas_call | solution.py:92
  36.9 1.1 %shard_map.103.own = f32[2,576,128]{2,1,0:T(8,128)S(1)} custom-call(bf16[32,16,256]{2,1,0:T(8,128)(2,1)S(1)} %get-tuple-element.34.left_ref, bf16[32,144,256]{2,1,0:T(8,128)(2,1)S(1)} %get-tuple-element.27.particles), custom_call_target="tpu_custom_call" | custom-call | flops 301989888 | bytes 3211264 | tf_op jit(solution)/shard_map/pallas_call | solution.py:92
  38.0 0.9 %collective-permute-done.9.other = f32[2,576,128]{2,1,0:T(8,128)S(1)} collective-permute-done((f32[2,576,128]{2,1,0:T(8,128)S(1)}, f32[2,576,128]{2,1,0:T(8,128)S(1)}, u32[]{:S(2)}, u32[]{:S(2)}) %collective-permute-start.9) | collective-permute-done | bytes 589856 | tf_op jit(solution)/shard_map/ppermute | solution.py:509
  38.9 0.8 %shard_map.104 = (f32[4,256,256]{2,1,0:T(8,128)S(1)}, f32[8,256]{1,0:T(8,128)S(1)}) custom-call(f32[2,576,128]{2,1,0:T(8,128)S(1)} %shard_map.103.own, f32[2,576,128]{2,1,0:T(8,128)S(1)} %collective-permute-done.9.other, f32[4,256]{1,0:T(4,128)S(1)} %get-tuple-element.36.energy_ref, s32[1,256]{1,0:T(1,128)S(1)} %bitcast.4, bf16[512,256]{1,0:T(8,128)(2,1)S(1)} %copy-done.5, ...), custom_call_target="tpu_custom_call" | custom-call | flops 402653184 | bytes 2801664 | tf_op jit(solution)/shard_map/pallas_call | solution.py:92
  39.8 1.6 %collective-permute-start.10 = (f32[8,256]{1,0:T(8,128)S(1)}, f32[8,256]{1,0:T(8,128)S(1)}, u32[]{:S(2)}, u32[]{:S(2)}) collective-permute-start(f32[8,256]{1,0:T(8,128)S(1)} %get-tuple-element.38.here.first), channel_id=1, source_target_pairs={{0,2},{2,0},{1,3},{3,1},{4,6},{6,4},{5,7},{7,5},{8,10},{10,8},{9,1... | collective-permute-start | bytes 24584 | tf_op jit(solution)/shard_map/ppermute | solution.py:509
  41.3 2.2 %collective-permute-done.10.second = f32[8,256]{1,0:T(8,128)S(1)} collective-permute-done((f32[8,256]{1,0:T(8,128)S(1)}, f32[8,256]{1,0:T(8,128)S(1)}, u32[]{:S(2)}, u32[]{:S(2)}) %collective-permute-start.10) | collective-permute-done | bytes 8224 | tf_op jit(solution)/shard_map/ppermute | solution.py:509
  44.0 1.1 %shard_map.106.image = f32[576,128]{1,0:T(8,128)S(1)} custom-call(bf16[4,256,256]{2,1,0:T(8,128)(2,1)S(1)} %get-tuple-element.39.rounded_ref, bf16[512,256]{1,0:T(8,128)(2,1)S(1)} %copy-done.3, bf16[512,256]{1,0:T(8,128)(2,1)S(1)} %copy-done.2, bf16[32,144,256]{2,1,0:T(8,128)(2,1)S(1)} %get-tuple-element.27.particles), custom_call_target="tpu_custom_call" | custom-call | flops 268435456 | bytes 4292608 | tf_op jit(solution)/shard_map/pallas_call | solution.py:92
  45.6 0.9 %shard_map.107 = (f32[72,128]{1,0:T(8,128)S(1)}, f32[72,128]{1,0:T(8,128)S(1)}, f32[72,128]{1,0:T(8,128)S(1)}, f32[72,128]{1,0:T(8,128)S(1)}) custom-call(f32[576,128]{1,0:T(8,128)S(1)} %shard_map.106.image, bf16[33,16,144]{2,1,0:T(8,128)(2,1)S(1)} %get-tuple-element.40.mine, bf16[33,16,144]{2,1,0:T(8,128)(2,1)S(1)} %collective-permute-done.11.spectrum, ...), custom_call_target="tpu_custom_call" | custom-call | flops 311427072 | bytes 3653632 | tf_op jit(solution)/shard_map/pallas_call | solution.py:92
  46.7 2.4 %collective-permute-start.13 = (f32[72,128]{1,0:T(8,128)S(1)}, f32[72,128]{1,0:T(8,128)S(1)}, u32[]{:S(2)}, u32[]{:S(2)}) collective-permute-start(f32[72,128]{1,0:T(8,128)S(1)} %get-tuple-element.43), channel_id=1, source_target_pairs={{0,8},{4,12},{8,0},{12,4},{1,9},{5,13},{9,1},{13,5},{2,10},{6,14},... | collective-permute-start | bytes 110600 | tf_op jit(solution)/shard_map/ppermute | solution.py:509
  49.0 1.8 %collective-permute-start.14 = (f32[72,128]{1,0:T(8,128)S(1)}, f32[72,128]{1,0:T(8,128)S(1)}, u32[]{:S(2)}, u32[]{:S(2)}) collective-permute-start(f32[72,128]{1,0:T(8,128)S(1)} %get-tuple-element.44), channel_id=1, source_target_pairs={{0,12},{4,8},{8,4},{12,0},{1,13},{5,9},{9,5},{13,1},{2,14},{6,10},... | collective-permute-start | bytes 110600 | tf_op jit(solution)/shard_map/ppermute | solution.py:509
  50.9 1.3 %collective-permute-done.13.refs_2_ = f32[72,128]{1,0:T(8,128)S(1)} collective-permute-done((f32[72,128]{1,0:T(8,128)S(1)}, f32[72,128]{1,0:T(8,128)S(1)}, u32[]{:S(2)}, u32[]{:S(2)}) %collective-permute-start.13) | collective-permute-done | bytes 36896 | tf_op jit(solution)/shard_map/ppermute | solution.py:509
  52.2 2.6 %collective-permute-done.14.refs_3_ = f32[72,128]{1,0:T(8,128)S(1)} collective-permute-done((f32[72,128]{1,0:T(8,128)S(1)}, f32[72,128]{1,0:T(8,128)S(1)}, u32[]{:S(2)}, u32[]{:S(2)}) %collective-permute-start.14) | collective-permute-done | bytes 36896 | tf_op jit(solution)/shard_map/ppermute | solution.py:509
  54.8 0.6 %shard_map.108 = (f32[1,64,128]{2,1,0:T(8,128)}, f32[1,144]{1,0:T(1,128)}) custom-call(f32[72,128]{1,0:T(8,128)S(1)} %get-tuple-element.41.refs_0_, f32[72,128]{1,0:T(8,128)S(1)} %collective-permute-done.12.refs_1_, f32[72,128]{1,0:T(8,128)S(1)} %collective-permute-done.13.refs_2_, f32[72,128]{1,0:T(8,128)S(1)} %collective-permute-done.14.refs_3_, ...), custom_call_target="tpu_custom_call" | custom-call | bytes 229376 | tf_op jit(solution)/shard_map/pallas_call | solution.py:92
  (36 shorter events, 2.0 us)
Async XLA Ops:
  0.6 11.4 %copy-start.8 = (bf16[1,64,128]{2,1,0:T(8,128)(2,1)S(1)}, bf16[1,64,128]{2,1,0:T(8,128)(2,1)}, u32[]{:S(2)}) copy-start(bf16[1,64,128]{2,1,0:T(8,128)(2,1)} %refs_0_.1) | copy-start | bytes 49156
  0.6 11.4 %copy-start.9 = (f32[64]{0:T(128)S(1)}, f32[64]{0:T(128)}, u32[]{:S(2)}) copy-start(f32[64]{0:T(128)} %param.10) | copy-start | bytes 772
  0.6 9.5 %collective-permute-start.1 = (bf16[1,64,128]{2,1,0:T(8,128)(2,1)}, bf16[1,64,128]{2,1,0:T(8,128)(2,1)S(1)}, u32[]{:S(2)}, u32[]{:S(2)}) collective-permute-start(bf16[1,64,128]{2,1,0:T(8,128)(2,1)} %refs_0_.1), channel_id=1, source_target_pairs={{0,8},{4,12},{8,0},{12,4},{1,9},{5,13},{9,1},{13,5},{2,10},{6,14},... | collective-permute-start | bytes 49160 | tf_op jit(solution)/shard_map/ppermute | solution.py:509
  4.8 5.4 %collective-permute-start = (bf16[1,64,128]{2,1,0:T(8,128)(2,1)}, bf16[1,64,128]{2,1,0:T(8,128)(2,1)S(1)}, u32[]{:S(2)}, u32[]{:S(2)}) collective-permute-start(bf16[1,64,128]{2,1,0:T(8,128)(2,1)} %refs_0_.1), channel_id=1, source_target_pairs={{0,4},{4,0},{8,12},{12,8},{1,5},{5,1},{9,13},{13,9},{2,6},{6,2},{1... | collective-permute-start | bytes 49160 | tf_op jit(solution)/shard_map/ppermute | solution.py:509
  6.3 5.7 %collective-permute-start.2 = (bf16[1,64,128]{2,1,0:T(8,128)(2,1)}, bf16[1,64,128]{2,1,0:T(8,128)(2,1)S(1)}, u32[]{:S(2)}, u32[]{:S(2)}) collective-permute-start(bf16[1,64,128]{2,1,0:T(8,128)(2,1)} %refs_0_.1), channel_id=1, source_target_pairs={{0,12},{4,8},{8,4},{12,0},{1,13},{5,9},{9,5},{13,1},{2,14},{6,10},... | collective-permute-start | bytes 49160 | tf_op jit(solution)/shard_map/ppermute | solution.py:509
  10.2 6.2 %copy-start.10 = (s32[288]{0:T(512)S(1)}, s32[288]{0:T(512)}, u32[]{:S(2)}) copy-start(s32[288]{0:T(512)} %param.11) | copy-start | bytes 3460
  12.1 6.5 %copy-start.4 = (bf16[512,256]{1,0:T(8,128)(2,1)S(1)}, bf16[512,256]{1,0:T(8,128)(2,1)}, u32[]{:S(2)}) copy-start(bf16[512,256]{1,0:T(8,128)(2,1)} %constant.19.clone.inv_lo) | copy-start | bytes 786436
  12.1 6.5 %copy-start.5 = (bf16[512,256]{1,0:T(8,128)(2,1)S(1)}, bf16[512,256]{1,0:T(8,128)(2,1)}, u32[]{:S(2)}) copy-start(bf16[512,256]{1,0:T(8,128)(2,1)} %constant.18.clone.inv_hi) | copy-start | bytes 786436
  14.2 1.4 %copy-start = (bf16[32,144,256]{2,1,0:T(8,128)(2,1)}, bf16[32,144,256]{2,1,0:T(8,128)(2,1)S(1)}, u32[]{:S(2)}) copy-start(bf16[32,144,256]{2,1,0:T(8,128)(2,1)S(1)} %get-tuple-element.25.refs_5_.particles) | copy-start | bytes 7077892
  15.6 0.7 %copy-start.6 = (bf16[32,16,256]{2,1,0:T(8,128)(2,1)}, bf16[32,16,256]{2,1,0:T(8,128)(2,1)S(1)}, u32[]{:S(2)}) copy-start(bf16[32,16,256]{2,1,0:T(8,128)(2,1)S(1)} %get-tuple-element.26.left_ref) | copy-start | bytes 786436
  16.3 2.2 %collective-permute-start.3 = (f32[2,576,128]{2,1,0:T(8,128)}, f32[2,576,128]{2,1,0:T(8,128)S(1)}, u32[]{:S(2)}, u32[]{:S(2)}) collective-permute-start(f32[2,576,128]{2,1,0:T(8,128)} %get-tuple-element.28), channel_id=1, source_target_pairs={{0,1},{1,0},{2,3},{3,2},{4,5},{5,4},{6,7},{7,6},{8,9},{9,8},{10,11... | collective-permute-start | bytes 1769480 | tf_op jit(solution)/shard_map/ppermute | solution.py:509
  16.4 1.0 %copy-start.7 = (bf16[32,16,256]{2,1,0:T(8,128)(2,1)S(1)}, bf16[32,16,256]{2,1,0:T(8,128)(2,1)}, u32[]{:S(2)}) copy-start(bf16[32,16,256]{2,1,0:T(8,128)(2,1)} %copy-done.6) | copy-start | bytes 786436
  17.4 5.7 %copy-start.2 = (bf16[512,256]{1,0:T(8,128)(2,1)S(1)}, bf16[512,256]{1,0:T(8,128)(2,1)}, u32[]{:S(2)}) copy-start(bf16[512,256]{1,0:T(8,128)(2,1)} %constant.21.clone.fwd_lo) | copy-start | bytes 786436
  17.4 5.7 %copy-start.3 = (bf16[512,256]{1,0:T(8,128)(2,1)S(1)}, bf16[512,256]{1,0:T(8,128)(2,1)}, u32[]{:S(2)}) copy-start(bf16[512,256]{1,0:T(8,128)(2,1)} %constant.20.clone.fwd_hi) | copy-start | bytes 786436
  19.4 3.7 %collective-permute-start.4 = (f32[8,256]{1,0:T(8,128)S(1)}, f32[8,256]{1,0:T(8,128)S(1)}, u32[]{:S(2)}, u32[]{:S(2)}) collective-permute-start(f32[8,256]{1,0:T(8,128)S(1)} %get-tuple-element.31.here.first), channel_id=1, source_target_pairs={{0,2},{2,0},{1,3},{3,1},{4,6},{6,4},{5,7},{7,5},{8,10},{10,8},{9,1... | collective-permute-start | bytes 24584 | tf_op jit(solution)/shard_map/ppermute | solution.py:509
  23.1 2.6 %copy-start.1 = (bf16[32,144,256]{2,1,0:T(8,128)(2,1)S(1)}, bf16[32,144,256]{2,1,0:T(8,128)(2,1)}, u32[]{:S(2)}) copy-start(bf16[32,144,256]{2,1,0:T(8,128)(2,1)} %copy-done) | copy-start | bytes 7077892
  24.1 1.5 %collective-permute-start.5 = (bf16[33,16,144]{2,1,0:T(8,128)(2,1)S(1)}, bf16[33,16,144]{2,1,0:T(8,128)(2,1)S(1)}, u32[]{:S(2)}, u32[]{:S(2)}) collective-permute-start(bf16[33,16,144]{2,1,0:T(8,128)(2,1)S(1)} %get-tuple-element.33.mine), channel_id=1, source_target_pairs={{0,1},{1,0},{2,3},{3,2},{4,5},{5,4},{6,7},{7,6},{8,9},{9,8},{10,11... | collective-permute-start | bytes 456200 | tf_op jit(solution)/shard_map/ppermute | solution.py:509
  26.5 6.9 %collective-permute-start.8 = (bf16[272,128]{1,0:T(8,128)(2,1)S(1)}, bf16[272,128]{1,0:T(8,128)(2,1)S(1)}, u32[]{:S(2)}, u32[]{:S(2)}) collective-permute-start(bf16[272,128]{1,0:T(8,128)(2,1)S(1)} %shard_map.101.refs_0_), channel_id=1, source_target_pairs={{0,12},{4,8},{8,4},{12,0},{1,13},{5,9},{9,5},{13,1},{2,14},{6,10},... | collective-permute-start | bytes 208904 | tf_op jit(solution)/shard_map/ppermute | solution.py:509
  28.6 7.0 %collective-permute-start.7 = (bf16[272,128]{1,0:T(8,128)(2,1)S(1)}, bf16[272,128]{1,0:T(8,128)(2,1)S(1)}, u32[]{:S(2)}, u32[]{:S(2)}) collective-permute-start(bf16[272,128]{1,0:T(8,128)(2,1)S(1)} %shard_map.101.refs_0_), channel_id=1, source_target_pairs={{0,8},{4,12},{8,0},{12,4},{1,9},{5,13},{9,1},{13,5},{2,10},{6,14},... | collective-permute-start | bytes 208904 | tf_op jit(solution)/shard_map/ppermute | solution.py:509
  28.6 7.0 %collective-permute-start.6 = (bf16[272,128]{1,0:T(8,128)(2,1)S(1)}, bf16[272,128]{1,0:T(8,128)(2,1)S(1)}, u32[]{:S(2)}, u32[]{:S(2)}) collective-permute-start(bf16[272,128]{1,0:T(8,128)(2,1)S(1)} %shard_map.101.refs_0_), channel_id=1, source_target_pairs={{0,4},{4,0},{8,12},{12,8},{1,5},{5,1},{9,13},{13,9},{2,6},{6,2},{1... | collective-permute-start | bytes 208904 | tf_op jit(solution)/shard_map/ppermute | solution.py:509
  36.9 2.1 %collective-permute-start.9 = (f32[2,576,128]{2,1,0:T(8,128)S(1)}, f32[2,576,128]{2,1,0:T(8,128)S(1)}, u32[]{:S(2)}, u32[]{:S(2)}) collective-permute-start(f32[2,576,128]{2,1,0:T(8,128)S(1)} %get-tuple-element.35), channel_id=1, source_target_pairs={{0,1},{1,0},{2,3},{3,2},{4,5},{5,4},{6,7},{7,6},{8,9},{9,8},{10,11... | collective-permute-start | bytes 1769480 | tf_op jit(solution)/shard_map/ppermute | solution.py:509
  39.8 3.7 %collective-permute-start.10 = (f32[8,256]{1,0:T(8,128)S(1)}, f32[8,256]{1,0:T(8,128)S(1)}, u32[]{:S(2)}, u32[]{:S(2)}) collective-permute-start(f32[8,256]{1,0:T(8,128)S(1)} %get-tuple-element.38.here.first), channel_id=1, source_target_pairs={{0,2},{2,0},{1,3},{3,1},{4,6},{6,4},{5,7},{7,5},{8,10},{10,8},{9,1... | collective-permute-start | bytes 24584 | tf_op jit(solution)/shard_map/ppermute | solution.py:509
  43.9 1.6 %collective-permute-start.11 = (bf16[33,16,144]{2,1,0:T(8,128)(2,1)S(1)}, bf16[33,16,144]{2,1,0:T(8,128)(2,1)S(1)}, u32[]{:S(2)}, u32[]{:S(2)}) collective-permute-start(bf16[33,16,144]{2,1,0:T(8,128)(2,1)S(1)} %get-tuple-element.40.mine), channel_id=1, source_target_pairs={{0,1},{1,0},{2,3},{3,2},{4,5},{5,4},{6,7},{7,6},{8,9},{9,8},{10,11... | collective-permute-start | bytes 456200 | tf_op jit(solution)/shard_map/ppermute | solution.py:509
  46.4 4.5 %collective-permute-start.12 = (f32[72,128]{1,0:T(8,128)S(1)}, f32[72,128]{1,0:T(8,128)S(1)}, u32[]{:S(2)}, u32[]{:S(2)}) collective-permute-start(f32[72,128]{1,0:T(8,128)S(1)} %get-tuple-element.42), channel_id=1, source_target_pairs={{0,4},{4,0},{8,12},{12,8},{1,5},{5,1},{9,13},{13,9},{2,6},{6,2},{1... | collective-permute-start | bytes 110600 | tf_op jit(solution)/shard_map/ppermute | solution.py:509
  46.7 5.5 %collective-permute-start.13 = (f32[72,128]{1,0:T(8,128)S(1)}, f32[72,128]{1,0:T(8,128)S(1)}, u32[]{:S(2)}, u32[]{:S(2)}) collective-permute-start(f32[72,128]{1,0:T(8,128)S(1)} %get-tuple-element.43), channel_id=1, source_target_pairs={{0,8},{4,12},{8,0},{12,4},{1,9},{5,13},{9,1},{13,5},{2,10},{6,14},... | collective-permute-start | bytes 110600 | tf_op jit(solution)/shard_map/ppermute | solution.py:509
  49.0 5.8 %collective-permute-start.14 = (f32[72,128]{1,0:T(8,128)S(1)}, f32[72,128]{1,0:T(8,128)S(1)}, u32[]{:S(2)}, u32[]{:S(2)}) collective-permute-start(f32[72,128]{1,0:T(8,128)S(1)} %get-tuple-element.44), channel_id=1, source_target_pairs={{0,12},{4,8},{8,4},{12,0},{1,13},{5,9},{9,5},{13,1},{2,14},{6,10},... | collective-permute-start | bytes 110600 | tf_op jit(solution)/shard_map/ppermute | solution.py:509

commit v6 on v5

--- a/solution.py
+++ b/solution.py
@@ -100,10 +100,9 @@
     )(*ins)
 
 
-def prep_kernel(share, particles_ref, other, own, held, wide, sems):
-    chunk, freqs, depth = held.shape[1:]
-    pitch = wide.shape[0] // chunk
-    steps = share // chunk
+def prep_kernel(share, particles_ref, other, own, held, sems):
+    steps, chunk, freqs, depth = held.shape
+    steps //= 2
     group = lax.axis_index("rot")
     copies = []
     for i in range(2 * steps):
@@ -111,40 +110,44 @@
         copy = pltpu.make_async_copy(particles_ref.at[pl.ds(first, chunk)], held.at[i], sems.at[i])
         copy.start()
         copies.append(copy)
+    to = lax.broadcasted_iota(jnp.int32, (256, 256), 0)
+    at = lax.broadcasted_iota(jnp.int32, (256, 256), 1)
+    permutation = ((to // 16 == at % 16) & (to % 16 == at // 16)).astype(F32).astype(BF16)
     for i in range(2 * steps):
         out = (other, own)[i // steps]
-        to = pl.ds(i % steps * chunk, chunk)
         copies[i].wait()
-
-        def widen(p):
-            wide[rows(p * pitch, freqs), :] = held[i, p].astype(F32)
-
-        loop(chunk, widen, 8)
-
-        def turn(f):
-            for part in range(2):
-                at = pl.ds(2 * f + part, chunk, stride=pitch)
-                out[f, to, pl.ds(part * depth, depth)] = wide[at, :].astype(BF16)
-
-        loop(freqs // 2, turn, 8)
+        for p in range(0, chunk, 16):
+            for f in range(0, freqs, 32):
+                blocks = [
+                    jnp.concatenate(
+                        [held[i, p + j, pl.ds(f + half, 16), :] for j in range(16)], 0
+                    )
+                    for half in (0, 16)
+                ]
+                turned = dot(permutation, jnp.concatenate(blocks, 1)).astype(BF16)
+                for half in range(2):
+                    for j in range(16):
+                        pair, part = divmod(f + 16 * half + j, 2)
+                        out[
+                            pair,
+                            pl.ds(i % steps * chunk + p, 16),
+                            pl.ds(part * depth, depth),
+                        ] = turned[16 * j : 16 * j + 16, half * depth : (half + 1) * depth]
 
 
 def prep(particles, share):
     _, freqs, depth = particles.shape
-    chunk = max([n for n in (16, 32, 48) if share % n == 0], default=share)
+    assert share % 16 == 0 and freqs % 32 == 0
+    chunk = max(n for n in (16, 32, 48) if share % n == 0)
     steps = 2 * share // chunk
     return call(
         functools.partial(prep_kernel, share),
         [particles],
         [((freqs // 2, share, 2 * depth), BF16)] * 2,
-        [
-            ((steps, chunk, freqs, depth), BF16),
-            ((chunk * (freqs + SPARE), depth), F32),
-            pltpu.SemaphoreType.DMA((steps,)),
-        ],
+        [((steps, chunk, freqs, depth), BF16), pltpu.SemaphoreType.DMA((steps,))],
         flops=1 << 31,
         far=(0,),
-        room=36 << 20,
+        room=38 << 20,
     )
 
 
@@ -280,7 +283,14 @@
     freqs = pitch - SPARE
     which = table_rows(0, ANG)
     turns = lax.broadcasted_iota(jnp.int32, (ANG, share), 0)
-    offset = jnp.abs(turns - prior_ref[...])
+    lane = lax.broadcasted_iota(jnp.int32, (1, share), 1)
+    priors = prior_ref[...].reshape(1, -1)
+    half = priors.shape[1] // 2
+    first, second = [
+        jnp.concatenate([priors[:, i * half : (i + 1) * half], lane[:, half:]], 1)
+        for i in range(2)
+    ]
+    offset = jnp.abs(turns - jnp.where(lax.axis_index("rot") == 0, first, second))
     distance = jnp.minimum(offset, ANG - offset).astype(F32)
     prior_term = -distance * distance / (2.0 * SIGMA * SIGMA)
 
@@ -338,12 +348,13 @@
 
 
 def turn_kernel(weights, here, first, second, fwd_hi, fwd_lo, *refs):
-    rounded_ref, send, evidence_ref, held = refs
+    rounded_ref, send, *evidence_ref, held = refs
     classes, _, lanes = weights.shape
-    share = evidence_ref.shape[1]
+    share = send.shape[2]
     pairs = send.shape[0] - 1
     top, total = merge(first[...], second[...])
-    evidence_ref[...] = (top + jnp.log(total))[:, :share]
+    for ref in evidence_ref:
+        ref[...] = (top + jnp.log(total))[:, :share]
     factor = jnp.exp(here[0:1, :] - top) / total
     lane = lax.broadcasted_iota(jnp.int32, (1, lanes), 1)
     factor = jnp.where(lane < share, factor, 0.0)
@@ -387,7 +398,7 @@
     return jnp.concatenate(parts, 0)[:, :share]
 
 
-def turn(weights, here, first, second, fwd_hi, fwd_lo, freqs, share):
+def turn(weights, here, first, second, fwd_hi, fwd_lo, freqs, share, last):
     classes, _, lanes = weights.shape
     return call(
         turn_kernel,
@@ -395,7 +406,7 @@
         [
             ((classes, ANG, lanes), BF16),
             ((freqs // 2 + 1, 4 * classes, share), BF16),
-            ((1, share), F32),
+            *([((1, share), F32)] if last else []),
         ],
         [((lanes // 128, 2 * classes * (freqs + SPARE), 128), F32)],
         flops=4 * classes * lanes * ANG * ANG,
@@ -520,12 +531,9 @@
     groups = lax.axis_size("rot")
     blocks = lax.axis_size("blk")
     assert groups == 2 and 2 * groups * freqs == ANG
-    group = lax.axis_index("rot").astype(jnp.int32)
     share = batch // groups
     inv_hi, inv_lo, fwd_hi, fwd_lo = tables(freqs)
     inverse_noise = noise_inv.reshape(1, depth // 2)
-    prior = lax.dynamic_slice_in_dim(prior_rot, group * share, share, 0)
-    prior = jnp.pad(prior, (0, -share % 128)).reshape(1, -1)
     assert blocks & (blocks - 1) == 0
 
     sources = [swap(references, "blk", blocks, i) for i in range(blocks)]
@@ -535,20 +543,22 @@
         message, energy, left = weigh(sources, inverse_noise, other_images, step == 0)
         message = swap(message, "rot", groups, 1)
         own = correlate(left, own_images)
-        weights, here = scores(own, message, energy, prior, inv_hi, inv_lo)
+        weights, here = scores(own, message, energy, prior_rot, inv_hi, inv_lo)
         first = here
         for bit in bits(sides):
             second = swap(first, "cls", sides, bit)
             if 2 * bit < sides:
                 (first,) = call(merge_kernel, [first, second], [(here.shape, F32)])
-        rounded, send, evidence = turn(weights, here, first, second, fwd_hi, fwd_lo, freqs, share)
+        rounded, send, *evidence = turn(
+            weights, here, first, second, fwd_hi, fwd_lo, freqs, share, last
+        )
         message = swap(send, "rot", groups, 1)
         image = gather(rounded, fwd_hi, fwd_lo, own_images)
         sums = finish(image, send, message, other_images, last)
         sums = sums if last else sums * blocks
-        sources = [swap(x, "blk", blocks, i) for i, x in enumerate(sums)]
+        sources = [swap(sums[i], "blk", blocks, i) for i in reversed(range(blocks))][::-1]
     means, evidence = call(
-        means_kernel, [*sources, evidence], [((1, freqs, depth), F32), (evidence.shape, F32)]
+        means_kernel, [*sources[::-1], *evidence], [((1, freqs, depth), F32), ((1, share), F32)]
     )
     return means, evidence.reshape(share)
 

time: 55.6 us -> 50.7 us (0.912)
  local copies, waits for them, and re-layouts: 3.18 us -> 0.04 us
  Pallas kernels: 17 us -> 15.2 us
    unnamed x22 -> x14, local copies, waits for them, and re-layouts: 3.1 us -> 0.04 us
    pallas_call x14, Pallas kernels: 17 us -> 15.2 us  [call(): pl.pallas_call(kernel, out_shape=[jax.ShapeDtypeStruct(*x) for x in outs]...]
  transfers between devices with their start and end apart: 15 -> 15, of which waited for: 11 -> 12; matrix products, arithmetic and copies ran while one was open for 0% -> 0% of each run, Pallas kernels for 15% -> 15%
where the time goes in v6:
time: 50.7 us; the launch traced here: 50.6 us
  starting transfers between devices  18 us (36%)
  waiting for transfers between devices  16.6 us (33%)
  Pallas kernels  15.2 us (30%)
  between operations  0.77 us (2%)
    ppermute x15, starting transfers between devices, swap(): return lax.ppermute(value, axis, [(i, i ^ bit) for i in range(size)])  18 us
    ppermute x15, waiting for transfers between devices, swap(): return lax.ppermute(value, axis, [(i, i ^ bit) for i in range(size)])  16.6 us
    pallas_call x14, Pallas kernels, call(): pl.pallas_call(kernel, out_shape=[jax.ShapeDtypeStruct(*x) for x in outs]...  15.2 us
  transfers between devices with their start and end apart: 15, of which 12 were waited for; matrix products, arithmetic and copies ran while one was open for 0% of the time, Pallas kernels for 15%

profile of v6, /device:TPU:0, one launch (start us, length us, event | category | flops | bytes accessed | tf_op | source)
XLA Modules:
  0.0 50.6 jit_solution(9069550330900691943)
XLA Ops:
  0.6 4.1 %collective-permute-start.1 = (bf16[1,64,128]{2,1,0:T(8,128)(2,1)}, bf16[1,64,128]{2,1,0:T(8,128)(2,1)S(1)}, u32[]{:S(2)}, u32[]{:S(2)}) collective-permute-start(bf16[1,64,128]{2,1,0:T(8,128)(2,1)} %refs_0_.1), channel_id=1, source_target_pairs={{0,8},{4,12},{8,0},{12,4},{1,9},{5,13},{9,1},{13,5},{2,10},{6,14},... | collective-permute-start | bytes 49160 | tf_op jit(solution)/shard_map/ppermute | solution.py:520
  4.8 1.6 %collective-permute-start = (bf16[1,64,128]{2,1,0:T(8,128)(2,1)}, bf16[1,64,128]{2,1,0:T(8,128)(2,1)S(1)}, u32[]{:S(2)}, u32[]{:S(2)}) collective-permute-start(bf16[1,64,128]{2,1,0:T(8,128)(2,1)} %refs_0_.1), channel_id=1, source_target_pairs={{0,4},{4,0},{8,12},{12,8},{1,5},{5,1},{9,13},{13,9},{2,6},{6,2},{1... | collective-permute-start | bytes 49160 | tf_op jit(solution)/shard_map/ppermute | solution.py:520
  6.3 3.4 %shard_map.95 = (bf16[32,144,256]{2,1,0:T(8,128)(2,1)S(1)}, bf16[32,144,256]{2,1,0:T(8,128)(2,1)S(1)}) custom-call(bf16[288,64,128]{2,1,0:T(8,128)(2,1)} %particles_ref.1), custom_call_target="tpu_custom_call" | custom-call | flops 2147483648 | bytes 9437184 | tf_op jit(solution)/shard_map/pallas_call | solution.py:92
  9.8 2.3 %collective-permute-done.2.refs_3_ = bf16[1,64,128]{2,1,0:T(8,128)(2,1)S(1)} collective-permute-done((bf16[1,64,128]{2,1,0:T(8,128)(2,1)}, bf16[1,64,128]{2,1,0:T(8,128)(2,1)S(1)}, u32[]{:S(2)}, u32[]{:S(2)}) %collective-permute-start.2) | collective-permute-done | bytes 16416 | tf_op jit(solution)/shard_map/ppermute | solution.py:520
  12.1 1.3 %shard_map.96 = (f32[2,576,128]{2,1,0:T(8,128)S(1)}, f32[4,256]{1,0:T(4,128)S(1)}, bf16[32,16,256]{2,1,0:T(8,128)(2,1)S(1)}) custom-call(bf16[1,64,128]{2,1,0:T(8,128)(2,1)S(1)} %copy-done.4, bf16[1,64,128]{2,1,0:T(8,128)(2,1)S(1)} %collective-permute-done.refs_1_, bf16[1,64,128]{2,1,0:T(8,128)(2,1)S(1)} %collective-permute-done.1.refs_2_, ...), custom_call_target="tpu_custom_call" | custom-call | flops 150994944 | bytes 3596288 | tf_op jit(solution)/shard_map/pallas_call | solution.py:92
  13.5 1.1 %shard_map.97.own = f32[2,576,128]{2,1,0:T(8,128)S(1)} custom-call(bf16[32,16,256]{2,1,0:T(8,128)(2,1)S(1)} %get-tuple-element.26.left_ref, bf16[32,144,256]{2,1,0:T(8,128)(2,1)S(1)} %get-tuple-element.27.particles), custom_call_target="tpu_custom_call" | custom-call | flops 301989888 | bytes 3211264 | tf_op jit(solution)/shard_map/pallas_call | solution.py:92
  14.5 0.9 %collective-permute-done.3.other = f32[2,576,128]{2,1,0:T(8,128)S(1)} collective-permute-done((f32[2,576,128]{2,1,0:T(8,128)S(1)}, f32[2,576,128]{2,1,0:T(8,128)S(1)}, u32[]{:S(2)}, u32[]{:S(2)}) %collective-permute-start.3) | collective-permute-done | bytes 589856 | tf_op jit(solution)/shard_map/ppermute | solution.py:520
  15.4 0.8 %shard_map.98 = (f32[4,256,256]{2,1,0:T(8,128)S(1)}, f32[8,256]{1,0:T(8,128)S(1)}) custom-call(f32[2,576,128]{2,1,0:T(8,128)S(1)} %shard_map.97.own, f32[2,576,128]{2,1,0:T(8,128)S(1)} %collective-permute-done.3.other, f32[4,256]{1,0:T(4,128)S(1)} %get-tuple-element.29.energy_ref, s32[288]{0:T(512)S(1)} %copy-done.5, bf16[512,256]{1,0:T(8,128)(2,1)S(1)} %copy-done.3, ...), custom_call_target="tpu_custom_call" | custom-call | flops 402653184 | bytes 2809856 | tf_op jit(solution)/shard_map/pallas_call | solution.py:92
  16.3 1.6 %collective-permute-start.4 = (f32[8,256]{1,0:T(8,128)S(1)}, f32[8,256]{1,0:T(8,128)S(1)}, u32[]{:S(2)}, u32[]{:S(2)}) collective-permute-start(f32[8,256]{1,0:T(8,128)S(1)} %get-tuple-element.31.here.first), channel_id=1, source_target_pairs={{0,2},{2,0},{1,3},{3,1},{4,6},{6,4},{5,7},{7,5},{8,10},{10,8},{9,1... | collective-permute-start | bytes 24584 | tf_op jit(solution)/shard_map/ppermute | solution.py:520
  17.8 2.2 %collective-permute-done.4.second = f32[8,256]{1,0:T(8,128)S(1)} collective-permute-done((f32[8,256]{1,0:T(8,128)S(1)}, f32[8,256]{1,0:T(8,128)S(1)}, u32[]{:S(2)}, u32[]{:S(2)}) %collective-permute-start.4) | collective-permute-done | bytes 8224 | tf_op jit(solution)/shard_map/ppermute | solution.py:520
  20.0 0.5 shard_map.99
  20.5 1.1 %shard_map.100.image = f32[576,128]{1,0:T(8,128)S(1)} custom-call(bf16[4,256,256]{2,1,0:T(8,128)(2,1)S(1)} %get-tuple-element.32.rounded_ref, bf16[512,256]{1,0:T(8,128)(2,1)S(1)} %copy-done.1, bf16[512,256]{1,0:T(8,128)(2,1)S(1)} %copy-done, bf16[32,144,256]{2,1,0:T(8,128)(2,1)S(1)} %get-tuple-element.27.particles), custom_call_target="tpu_custom_call" | custom-call | flops 268435456 | bytes 4292608 | tf_op jit(solution)/shard_map/pallas_call | solution.py:92
  21.6 0.5 collective-permute-done.5.spectrum
  22.1 0.9 %shard_map.101.refs_0_ = bf16[272,128]{1,0:T(8,128)(2,1)S(1)} custom-call(f32[576,128]{1,0:T(8,128)S(1)} %shard_map.100.image, bf16[33,16,144]{2,1,0:T(8,128)(2,1)S(1)} %get-tuple-element.33.mine, bf16[33,16,144]{2,1,0:T(8,128)(2,1)S(1)} %collective-permute-done.5.spectrum, bf16[32,144,256]{2,1,0:T(8,128)(2,1)S(1)} %get-tuple-element.25.refs_5_.particles), custom_call_target="tpu_custom_call" | custom-call | flops 311427072 | bytes 3559424 | tf_op jit(solution)/shard_map/pallas_call | solution.py:92
  22.9 1.6 %collective-permute-start.8 = (bf16[272,128]{1,0:T(8,128)(2,1)S(1)}, bf16[272,128]{1,0:T(8,128)(2,1)S(1)}, u32[]{:S(2)}, u32[]{:S(2)}) collective-permute-start(bf16[272,128]{1,0:T(8,128)(2,1)S(1)} %shard_map.101.refs_0_), channel_id=1, source_target_pairs={{0,12},{4,8},{8,4},{12,0},{1,13},{5,9},{9,5},{13,1},{2,14},{6,10},... | collective-permute-start | bytes 208904 | tf_op jit(solution)/shard_map/ppermute | solution.py:520
  24.6 2.8 %collective-permute-start.6 = (bf16[272,128]{1,0:T(8,128)(2,1)S(1)}, bf16[272,128]{1,0:T(8,128)(2,1)S(1)}, u32[]{:S(2)}, u32[]{:S(2)}) collective-permute-start(bf16[272,128]{1,0:T(8,128)(2,1)S(1)} %shard_map.101.refs_0_), channel_id=1, source_target_pairs={{0,4},{4,0},{8,12},{12,8},{1,5},{5,1},{9,13},{13,9},{2,6},{6,2},{1... | collective-permute-start | bytes 208904 | tf_op jit(solution)/shard_map/ppermute | solution.py:520
  27.4 2.5 %collective-permute-done.8.refs_3_ = bf16[272,128]{1,0:T(8,128)(2,1)S(1)} collective-permute-done((bf16[272,128]{1,0:T(8,128)(2,1)S(1)}, bf16[272,128]{1,0:T(8,128)(2,1)S(1)}, u32[]{:S(2)}, u32[]{:S(2)}) %collective-permute-start.8) | collective-permute-done | bytes 69664 | tf_op jit(solution)/shard_map/ppermute | solution.py:520
  29.9 2.1 %collective-permute-done.7.refs_2_ = bf16[272,128]{1,0:T(8,128)(2,1)S(1)} collective-permute-done((bf16[272,128]{1,0:T(8,128)(2,1)S(1)}, bf16[272,128]{1,0:T(8,128)(2,1)S(1)}, u32[]{:S(2)}, u32[]{:S(2)}) %collective-permute-start.7) | collective-permute-done | bytes 69664 | tf_op jit(solution)/shard_map/ppermute | solution.py:520
  32.0 1.3 %shard_map.102 = (f32[2,576,128]{2,1,0:T(8,128)S(1)}, f32[4,256]{1,0:T(4,128)S(1)}, bf16[32,16,256]{2,1,0:T(8,128)(2,1)S(1)}) custom-call(bf16[272,128]{1,0:T(8,128)(2,1)S(1)} %shard_map.101.refs_0_, bf16[272,128]{1,0:T(8,128)(2,1)S(1)} %collective-permute-done.6.refs_1_, bf16[272,128]{1,0:T(8,128)(2,1)S(1)} %collective-permute-done.7.refs_2_, ...), custom_call_target="tpu_custom_call" | custom-call | flops 150994944 | bytes 3809280 | tf_op jit(solution)/shard_map/pallas_call | solution.py:92
  33.4 1.1 %shard_map.103.own = f32[2,576,128]{2,1,0:T(8,128)S(1)} custom-call(bf16[32,16,256]{2,1,0:T(8,128)(2,1)S(1)} %get-tuple-element.34.left_ref, bf16[32,144,256]{2,1,0:T(8,128)(2,1)S(1)} %get-tuple-element.27.particles), custom_call_target="tpu_custom_call" | custom-call | flops 301989888 | bytes 3211264 | tf_op jit(solution)/shard_map/pallas_call | solution.py:92
  34.4 0.9 %collective-permute-done.9.other = f32[2,576,128]{2,1,0:T(8,128)S(1)} collective-permute-done((f32[2,576,128]{2,1,0:T(8,128)S(1)}, f32[2,576,128]{2,1,0:T(8,128)S(1)}, u32[]{:S(2)}, u32[]{:S(2)}) %collective-permute-start.9) | collective-permute-done | bytes 589856 | tf_op jit(solution)/shard_map/ppermute | solution.py:520
  35.3 0.8 %shard_map.104 = (f32[4,256,256]{2,1,0:T(8,128)S(1)}, f32[8,256]{1,0:T(8,128)S(1)}) custom-call(f32[2,576,128]{2,1,0:T(8,128)S(1)} %shard_map.103.own, f32[2,576,128]{2,1,0:T(8,128)S(1)} %collective-permute-done.9.other, f32[4,256]{1,0:T(4,128)S(1)} %get-tuple-element.36.energy_ref, s32[288]{0:T(512)S(1)} %copy-done.5, bf16[512,256]{1,0:T(8,128)(2,1)S(1)} %copy-done.3, ...), custom_call_target="tpu_custom_call" | custom-call | flops 402653184 | bytes 2809856 | tf_op jit(solution)/shard_map/pallas_call | solution.py:92
  36.2 1.6 %collective-permute-start.10 = (f32[8,256]{1,0:T(8,128)S(1)}, f32[8,256]{1,0:T(8,128)S(1)}, u32[]{:S(2)}, u32[]{:S(2)}) collective-permute-start(f32[8,256]{1,0:T(8,128)S(1)} %get-tuple-element.38.here.first), channel_id=1, source_target_pairs={{0,2},{2,0},{1,3},{3,1},{4,6},{6,4},{5,7},{7,5},{8,10},{10,8},{9,1... | collective-permute-start | bytes 24584 | tf_op jit(solution)/shard_map/ppermute | solution.py:520
  37.7 2.2 %collective-permute-done.10.second = f32[8,256]{1,0:T(8,128)S(1)} collective-permute-done((f32[8,256]{1,0:T(8,128)S(1)}, f32[8,256]{1,0:T(8,128)S(1)}, u32[]{:S(2)}, u32[]{:S(2)}) %collective-permute-start.10) | collective-permute-done | bytes 8224 | tf_op jit(solution)/shard_map/ppermute | solution.py:520
  39.9 0.5 shard_map.105
  40.4 1.1 %shard_map.106.image = f32[576,128]{1,0:T(8,128)S(1)} custom-call(bf16[4,256,256]{2,1,0:T(8,128)(2,1)S(1)} %get-tuple-element.39.rounded_ref, bf16[512,256]{1,0:T(8,128)(2,1)S(1)} %copy-done.1, bf16[512,256]{1,0:T(8,128)(2,1)S(1)} %copy-done, bf16[32,144,256]{2,1,0:T(8,128)(2,1)S(1)} %get-tuple-element.27.particles), custom_call_target="tpu_custom_call" | custom-call | flops 268435456 | bytes 4292608 | tf_op jit(solution)/shard_map/pallas_call | solution.py:92
  42.0 0.9 %shard_map.107 = (f32[72,128]{1,0:T(8,128)S(1)}, f32[72,128]{1,0:T(8,128)S(1)}, f32[72,128]{1,0:T(8,128)S(1)}, f32[72,128]{1,0:T(8,128)S(1)}) custom-call(f32[576,128]{1,0:T(8,128)S(1)} %shard_map.106.image, bf16[33,16,144]{2,1,0:T(8,128)(2,1)S(1)} %get-tuple-element.40.mine, bf16[33,16,144]{2,1,0:T(8,128)(2,1)S(1)} %collective-permute-done.11.spectrum, ...), custom_call_target="tpu_custom_call" | custom-call | flops 311427072 | bytes 3653632 | tf_op jit(solution)/shard_map/pallas_call | solution.py:92
  42.9 1.6 %collective-permute-start.12 = (f32[72,128]{1,0:T(8,128)S(1)}, f32[72,128]{1,0:T(8,128)S(1)}, u32[]{:S(2)}, u32[]{:S(2)}) collective-permute-start(f32[72,128]{1,0:T(8,128)S(1)} %get-tuple-element.41), channel_id=1, source_target_pairs={{0,12},{4,8},{8,4},{12,0},{1,13},{5,9},{9,5},{13,1},{2,14},{6,10},... | collective-permute-start | bytes 110600 | tf_op jit(solution)/shard_map/ppermute | solution.py:520
  44.5 2.8 %collective-permute-start.14 = (f32[72,128]{1,0:T(8,128)S(1)}, f32[72,128]{1,0:T(8,128)S(1)}, u32[]{:S(2)}, u32[]{:S(2)}) collective-permute-start(f32[72,128]{1,0:T(8,128)S(1)} %get-tuple-element.43), channel_id=1, source_target_pairs={{0,4},{4,0},{8,12},{12,8},{1,5},{5,1},{9,13},{13,9},{2,6},{6,2},{1... | collective-permute-start | bytes 110600 | tf_op jit(solution)/shard_map/ppermute | solution.py:520
  47.3 1.4 %collective-permute-done.12.refs_0_ = f32[72,128]{1,0:T(8,128)S(1)} collective-permute-done((f32[72,128]{1,0:T(8,128)S(1)}, f32[72,128]{1,0:T(8,128)S(1)}, u32[]{:S(2)}, u32[]{:S(2)}) %collective-permute-start.12) | collective-permute-done | bytes 36896 | tf_op jit(solution)/shard_map/ppermute | solution.py:520
  48.7 1.2 %collective-permute-done.13.refs_1_ = f32[72,128]{1,0:T(8,128)S(1)} collective-permute-done((f32[72,128]{1,0:T(8,128)S(1)}, f32[72,128]{1,0:T(8,128)S(1)}, u32[]{:S(2)}, u32[]{:S(2)}) %collective-permute-start.13) | collective-permute-done | bytes 36896 | tf_op jit(solution)/shard_map/ppermute | solution.py:520
  49.9 0.6 %shard_map.108 = (f32[1,64,128]{2,1,0:T(8,128)}, f32[1,144]{1,0:T(1,128)}) custom-call(f32[72,128]{1,0:T(8,128)S(1)} %collective-permute-done.12.refs_0_, f32[72,128]{1,0:T(8,128)S(1)} %collective-permute-done.13.refs_1_, f32[72,128]{1,0:T(8,128)S(1)} %collective-permute-done.14.refs_2_, f32[72,128]{1,0:T(8,128)S(1)} %get-tuple-element.44.refs_3_, ...), custom_call_target="tpu_custom_call" | custom-call | bytes 229376 | tf_op jit(solution)/shard_map/pallas_call | solution.py:92
  (26 shorter events, 0.8 us)
Async XLA Ops:
  0.6 11.4 %copy-start.4 = (bf16[1,64,128]{2,1,0:T(8,128)(2,1)S(1)}, bf16[1,64,128]{2,1,0:T(8,128)(2,1)}, u32[]{:S(2)}) copy-start(bf16[1,64,128]{2,1,0:T(8,128)(2,1)} %refs_0_.1) | copy-start | bytes 49156
  0.6 11.4 %copy-start.6 = (f32[64]{0:T(128)S(1)}, f32[64]{0:T(128)}, u32[]{:S(2)}) copy-start(f32[64]{0:T(128)} %param.10) | copy-start | bytes 772
  0.6 9.1 %collective-permute-start.1 = (bf16[1,64,128]{2,1,0:T(8,128)(2,1)}, bf16[1,64,128]{2,1,0:T(8,128)(2,1)S(1)}, u32[]{:S(2)}, u32[]{:S(2)}) collective-permute-start(bf16[1,64,128]{2,1,0:T(8,128)(2,1)} %refs_0_.1), channel_id=1, source_target_pairs={{0,8},{4,12},{8,0},{12,4},{1,9},{5,13},{9,1},{13,5},{2,10},{6,14},... | collective-permute-start | bytes 49160 | tf_op jit(solution)/shard_map/ppermute | solution.py:520
  4.8 5.0 %collective-permute-start = (bf16[1,64,128]{2,1,0:T(8,128)(2,1)}, bf16[1,64,128]{2,1,0:T(8,128)(2,1)S(1)}, u32[]{:S(2)}, u32[]{:S(2)}) collective-permute-start(bf16[1,64,128]{2,1,0:T(8,128)(2,1)} %refs_0_.1), channel_id=1, source_target_pairs={{0,4},{4,0},{8,12},{12,8},{1,5},{5,1},{9,13},{13,9},{2,6},{6,2},{1... | collective-permute-start | bytes 49160 | tf_op jit(solution)/shard_map/ppermute | solution.py:520
  6.3 5.7 %collective-permute-start.2 = (bf16[1,64,128]{2,1,0:T(8,128)(2,1)}, bf16[1,64,128]{2,1,0:T(8,128)(2,1)S(1)}, u32[]{:S(2)}, u32[]{:S(2)}) collective-permute-start(bf16[1,64,128]{2,1,0:T(8,128)(2,1)} %refs_0_.1), channel_id=1, source_target_pairs={{0,12},{4,8},{8,4},{12,0},{1,13},{5,9},{9,5},{13,1},{2,14},{6,10},... | collective-permute-start | bytes 49160 | tf_op jit(solution)/shard_map/ppermute | solution.py:520
  12.1 3.4 %copy-start.2 = (bf16[512,256]{1,0:T(8,128)(2,1)S(1)}, bf16[512,256]{1,0:T(8,128)(2,1)}, u32[]{:S(2)}) copy-start(bf16[512,256]{1,0:T(8,128)(2,1)} %constant.9.clone.inv_lo) | copy-start | bytes 786436
  12.1 3.4 %copy-start.3 = (bf16[512,256]{1,0:T(8,128)(2,1)S(1)}, bf16[512,256]{1,0:T(8,128)(2,1)}, u32[]{:S(2)}) copy-start(bf16[512,256]{1,0:T(8,128)(2,1)} %constant.8.clone.inv_hi) | copy-start | bytes 786436
  12.1 3.3 %copy-start.5 = (s32[288]{0:T(512)S(1)}, s32[288]{0:T(512)}, u32[]{:S(2)}) copy-start(s32[288]{0:T(512)} %prior_ref.3) | copy-start | bytes 3460
  13.4 2.1 %collective-permute-start.3 = (f32[2,576,128]{2,1,0:T(8,128)S(1)}, f32[2,576,128]{2,1,0:T(8,128)S(1)}, u32[]{:S(2)}, u32[]{:S(2)}) collective-permute-start(f32[2,576,128]{2,1,0:T(8,128)S(1)} %get-tuple-element.28), channel_id=1, source_target_pairs={{0,1},{1,0},{2,3},{3,2},{4,5},{5,4},{6,7},{7,6},{8,9},{9,8},{10,11... | collective-permute-start | bytes 1769480 | tf_op jit(solution)/shard_map/ppermute | solution.py:520
  13.4 6.5 %copy-start = (bf16[512,256]{1,0:T(8,128)(2,1)S(1)}, bf16[512,256]{1,0:T(8,128)(2,1)}, u32[]{:S(2)}) copy-start(bf16[512,256]{1,0:T(8,128)(2,1)} %constant.11.clone.fwd_lo) | copy-start | bytes 786436
  13.5 6.5 %copy-start.1 = (bf16[512,256]{1,0:T(8,128)(2,1)S(1)}, bf16[512,256]{1,0:T(8,128)(2,1)}, u32[]{:S(2)}) copy-start(bf16[512,256]{1,0:T(8,128)(2,1)} %constant.10.clone.fwd_hi) | copy-start | bytes 786436
  16.3 3.7 %collective-permute-start.4 = (f32[8,256]{1,0:T(8,128)S(1)}, f32[8,256]{1,0:T(8,128)S(1)}, u32[]{:S(2)}, u32[]{:S(2)}) collective-permute-start(f32[8,256]{1,0:T(8,128)S(1)} %get-tuple-element.31.here.first), channel_id=1, source_target_pairs={{0,2},{2,0},{1,3},{3,1},{4,6},{6,4},{5,7},{7,5},{8,10},{10,8},{9,1... | collective-permute-start | bytes 24584 | tf_op jit(solution)/shard_map/ppermute | solution.py:520
  20.4 1.6 %collective-permute-start.5 = (bf16[33,16,144]{2,1,0:T(8,128)(2,1)S(1)}, bf16[33,16,144]{2,1,0:T(8,128)(2,1)S(1)}, u32[]{:S(2)}, u32[]{:S(2)}) collective-permute-start(bf16[33,16,144]{2,1,0:T(8,128)(2,1)S(1)} %get-tuple-element.33.mine), channel_id=1, source_target_pairs={{0,1},{1,0},{2,3},{3,2},{4,5},{5,4},{6,7},{7,6},{8,9},{9,8},{10,11... | collective-permute-start | bytes 456200 | tf_op jit(solution)/shard_map/ppermute | solution.py:520
  22.9 6.9 %collective-permute-start.8 = (bf16[272,128]{1,0:T(8,128)(2,1)S(1)}, bf16[272,128]{1,0:T(8,128)(2,1)S(1)}, u32[]{:S(2)}, u32[]{:S(2)}) collective-permute-start(bf16[272,128]{1,0:T(8,128)(2,1)S(1)} %shard_map.101.refs_0_), channel_id=1, source_target_pairs={{0,12},{4,8},{8,4},{12,0},{1,13},{5,9},{9,5},{13,1},{2,14},{6,10},... | collective-permute-start | bytes 208904 | tf_op jit(solution)/shard_map/ppermute | solution.py:520
  24.6 7.4 %collective-permute-start.7 = (bf16[272,128]{1,0:T(8,128)(2,1)S(1)}, bf16[272,128]{1,0:T(8,128)(2,1)S(1)}, u32[]{:S(2)}, u32[]{:S(2)}) collective-permute-start(bf16[272,128]{1,0:T(8,128)(2,1)S(1)} %shard_map.101.refs_0_), channel_id=1, source_target_pairs={{0,8},{4,12},{8,0},{12,4},{1,9},{5,13},{9,1},{13,5},{2,10},{6,14},... | collective-permute-start | bytes 208904 | tf_op jit(solution)/shard_map/ppermute | solution.py:520
  24.6 7.4 %collective-permute-start.6 = (bf16[272,128]{1,0:T(8,128)(2,1)S(1)}, bf16[272,128]{1,0:T(8,128)(2,1)S(1)}, u32[]{:S(2)}, u32[]{:S(2)}) collective-permute-start(bf16[272,128]{1,0:T(8,128)(2,1)S(1)} %shard_map.101.refs_0_), channel_id=1, source_target_pairs={{0,4},{4,0},{8,12},{12,8},{1,5},{5,1},{9,13},{13,9},{2,6},{6,2},{1... | collective-permute-start | bytes 208904 | tf_op jit(solution)/shard_map/ppermute | solution.py:520
  33.3 2.1 %collective-permute-start.9 = (f32[2,576,128]{2,1,0:T(8,128)S(1)}, f32[2,576,128]{2,1,0:T(8,128)S(1)}, u32[]{:S(2)}, u32[]{:S(2)}) collective-permute-start(f32[2,576,128]{2,1,0:T(8,128)S(1)} %get-tuple-element.35), channel_id=1, source_target_pairs={{0,1},{1,0},{2,3},{3,2},{4,5},{5,4},{6,7},{7,6},{8,9},{9,8},{10,11... | collective-permute-start | bytes 1769480 | tf_op jit(solution)/shard_map/ppermute | solution.py:520
  36.2 3.7 %collective-permute-start.10 = (f32[8,256]{1,0:T(8,128)S(1)}, f32[8,256]{1,0:T(8,128)S(1)}, u32[]{:S(2)}, u32[]{:S(2)}) collective-permute-start(f32[8,256]{1,0:T(8,128)S(1)} %get-tuple-element.38.here.first), channel_id=1, source_target_pairs={{0,2},{2,0},{1,3},{3,1},{4,6},{6,4},{5,7},{7,5},{8,10},{10,8},{9,1... | collective-permute-start | bytes 24584 | tf_op jit(solution)/shard_map/ppermute | solution.py:520
  40.4 1.6 %collective-permute-start.11 = (bf16[33,16,144]{2,1,0:T(8,128)(2,1)S(1)}, bf16[33,16,144]{2,1,0:T(8,128)(2,1)S(1)}, u32[]{:S(2)}, u32[]{:S(2)}) collective-permute-start(bf16[33,16,144]{2,1,0:T(8,128)(2,1)S(1)} %get-tuple-element.40.mine), channel_id=1, source_target_pairs={{0,1},{1,0},{2,3},{3,2},{4,5},{5,4},{6,7},{7,6},{8,9},{9,8},{10,11... | collective-permute-start | bytes 456200 | tf_op jit(solution)/shard_map/ppermute | solution.py:520
  42.9 5.9 %collective-permute-start.12 = (f32[72,128]{1,0:T(8,128)S(1)}, f32[72,128]{1,0:T(8,128)S(1)}, u32[]{:S(2)}, u32[]{:S(2)}) collective-permute-start(f32[72,128]{1,0:T(8,128)S(1)} %get-tuple-element.41), channel_id=1, source_target_pairs={{0,12},{4,8},{8,4},{12,0},{1,13},{5,9},{9,5},{13,1},{2,14},{6,10},... | collective-permute-start | bytes 110600 | tf_op jit(solution)/shard_map/ppermute | solution.py:520
  44.5 5.4 %collective-permute-start.13 = (f32[72,128]{1,0:T(8,128)S(1)}, f32[72,128]{1,0:T(8,128)S(1)}, u32[]{:S(2)}, u32[]{:S(2)}) collective-permute-start(f32[72,128]{1,0:T(8,128)S(1)} %get-tuple-element.42), channel_id=1, source_target_pairs={{0,8},{4,12},{8,0},{12,4},{1,9},{5,13},{9,1},{13,5},{2,10},{6,14},... | collective-permute-start | bytes 110600 | tf_op jit(solution)/shard_map/ppermute | solution.py:520
  44.5 5.4 %collective-permute-start.14 = (f32[72,128]{1,0:T(8,128)S(1)}, f32[72,128]{1,0:T(8,128)S(1)}, u32[]{:S(2)}, u32[]{:S(2)}) collective-permute-start(f32[72,128]{1,0:T(8,128)S(1)} %get-tuple-element.43), channel_id=1, source_target_pairs={{0,4},{4,0},{8,12},{12,8},{1,5},{5,1},{9,13},{13,9},{2,6},{6,2},{1... | collective-permute-start | bytes 110600 | tf_op jit(solution)/shard_map/ppermute | solution.py:520

commit v7 on v6

--- a/solution.py
+++ b/solution.py
@@ -100,27 +100,34 @@
     )(*ins)
 
 
-def prep_kernel(share, particles_ref, other, own, held, sems):
-    steps, chunk, freqs, depth = held.shape
-    steps //= 2
+def prior_kernel(prior_ref, references_ref, prior_term, out):
+    out[...] = references_ref[...]
+    turns = lax.broadcasted_iota(jnp.int32, prior_term.shape, 0)
+    lane = lax.broadcasted_iota(jnp.int32, (1, prior_term.shape[1]), 1)
+    priors = prior_ref[...].reshape(1, -1)
+    half = priors.shape[1] // 2
+    first, second = [
+        jnp.concatenate([priors[:, i * half : (i + 1) * half], lane[:, half:]], 1)
+        for i in range(2)
+    ]
+    offset = jnp.abs(turns - jnp.where(lax.axis_index("rot") == 0, first, second))
+    distance = jnp.minimum(offset, ANG - offset).astype(F32)
+    prior_term[...] = -distance * distance / (2.0 * SIGMA * SIGMA)
+
+
+def prep_kernel(share, particles_ref, other, own):
+    freqs, depth = particles_ref.shape[1:]
     group = lax.axis_index("rot")
-    copies = []
-    for i in range(2 * steps):
-        first = jnp.where(i < steps, 1 - group, group) * share + i % steps * chunk
-        copy = pltpu.make_async_copy(particles_ref.at[pl.ds(first, chunk)], held.at[i], sems.at[i])
-        copy.start()
-        copies.append(copy)
     to = lax.broadcasted_iota(jnp.int32, (256, 256), 0)
     at = lax.broadcasted_iota(jnp.int32, (256, 256), 1)
     permutation = ((to // 16 == at % 16) & (to % 16 == at // 16)).astype(F32).astype(BF16)
-    for i in range(2 * steps):
-        out = (other, own)[i // steps]
-        copies[i].wait()
-        for p in range(0, chunk, 16):
+    for out, first in ((other, (1 - group) * share), (own, group * share)):
+        for p in range(0, share, 16):
             for f in range(0, freqs, 32):
                 blocks = [
                     jnp.concatenate(
-                        [held[i, p + j, pl.ds(f + half, 16), :] for j in range(16)], 0
+                        [particles_ref[first + p + j, pl.ds(f + half, 16), :] for j in range(16)],
+                        0,
                     )
                     for half in (0, 16)
                 ]
@@ -128,26 +135,19 @@
                 for half in range(2):
                     for j in range(16):
                         pair, part = divmod(f + 16 * half + j, 2)
-                        out[
-                            pair,
-                            pl.ds(i % steps * chunk + p, 16),
-                            pl.ds(part * depth, depth),
-                        ] = turned[16 * j : 16 * j + 16, half * depth : (half + 1) * depth]
+                        out[pair, pl.ds(p, 16), pl.ds(part * depth, depth)] = turned[
+                            16 * j : 16 * j + 16, half * depth : (half + 1) * depth
+                        ]
 
 
 def prep(particles, share):
     _, freqs, depth = particles.shape
     assert share % 16 == 0 and freqs % 32 == 0
-    chunk = max(n for n in (16, 32, 48) if share % n == 0)
-    steps = 2 * share // chunk
     return call(
         functools.partial(prep_kernel, share),
         [particles],
         [((freqs // 2, share, 2 * depth), BF16)] * 2,
-        [((steps, chunk, freqs, depth), BF16), pltpu.SemaphoreType.DMA((steps,))],
         flops=1 << 31,
-        far=(0,),
-        room=38 << 20,
     )
 
 
@@ -275,25 +275,13 @@
     return pl.ds(pl.multiple_of(lax.axis_index("rot") * ANG + base, 128), count)
 
 
-def score_kernel(own, other, energy_ref, prior_ref, inv_hi, inv_lo, *refs):
+def score_kernel(own, other, energy_ref, prior_term, inv_hi, inv_lo, *refs):
     weights, peaks = refs
     classes, share = energy_ref.shape
     tiles, lines, width = own.shape
     pitch = lines // (2 * classes)
     freqs = pitch - SPARE
     which = table_rows(0, ANG)
-    turns = lax.broadcasted_iota(jnp.int32, (ANG, share), 0)
-    lane = lax.broadcasted_iota(jnp.int32, (1, share), 1)
-    priors = prior_ref[...].reshape(1, -1)
-    half = priors.shape[1] // 2
-    first, second = [
-        jnp.concatenate([priors[:, i * half : (i + 1) * half], lane[:, half:]], 1)
-        for i in range(2)
-    ]
-    offset = jnp.abs(turns - jnp.where(lax.axis_index("rot") == 0, first, second))
-    distance = jnp.minimum(offset, ANG - offset).astype(F32)
-    prior_term = -distance * distance / (2.0 * SIGMA * SIGMA)
-
     def score(k, peak):
         value = jnp.concatenate(
             [
@@ -309,7 +297,7 @@
         )
         far = other[0, rows(2 * k * pitch + freqs, SPARE), :][:1]
         energy = energy_ref[pl.ds(k, 1), :] + jnp.concatenate([far] * tiles, 1)
-        scores = inner - 0.5 * energy + prior_term
+        scores = inner - 0.5 * energy + prior_term[...]
         weights[k] = scores
         return jnp.maximum(peak, jnp.max(scores, axis=0, keepdims=True))
 
@@ -325,11 +313,11 @@
     peaks[...] = jnp.where(line == 0, peak, total)
 
 
-def scores(own, other, energy, prior, inv_hi, inv_lo):
+def scores(own, other, energy, prior_term, inv_hi, inv_lo):
     classes, share = energy.shape
     return call(
         score_kernel,
-        [own, other, energy, prior, inv_hi, inv_lo],
+        [own, other, energy, prior_term, inv_hi, inv_lo],
         [((classes, ANG, share), F32), ((8, share), F32)],
         flops=6 * classes * share * ANG * ANG,
     )
@@ -536,14 +524,20 @@
     inverse_noise = noise_inv.reshape(1, depth // 2)
     assert blocks & (blocks - 1) == 0
 
-    sources = [swap(references, "blk", blocks, i) for i in range(blocks)]
+    prior_term, first = call(
+        prior_kernel,
+        [prior_rot, references],
+        [((ANG, lane_tiles(share) * 128), F32), (references.shape, BF16)],
+        flops=1 << 32,
+    )
+    sources = [swap(first, "blk", blocks, i) for i in reversed(range(blocks))][::-1]
     other_images, own_images = prep(particles, share)
     for step in range(ITERS):
         last = step == ITERS - 1
         message, energy, left = weigh(sources, inverse_noise, other_images, step == 0)
         message = swap(message, "rot", groups, 1)
         own = correlate(left, own_images)
-        weights, here = scores(own, message, energy, prior_rot, inv_hi, inv_lo)
+        weights, here = scores(own, message, energy, prior_term, inv_hi, inv_lo)
         first = here
         for bit in bits(sides):
             second = swap(first, "cls", sides, bit)

time: 50.7 us -> 51.5 us (1.016)
  Pallas kernels: 15.2 us -> 13.4 us
  local copies, waits for them, and re-layouts: 0.04 us -> 1.78 us
  waiting for transfers between devices: 16.6 us -> 17.3 us
    pallas_call x14 -> x15, Pallas kernels: 15.2 us -> 13.4 us  [call(): pl.pallas_call(kernel, out_shape=[jax.ShapeDtypeStruct(*x) for x in outs]...]
    unnamed x14 -> x16, local copies, waits for them, and re-layouts: 0.04 us -> 1.78 us
    ppermute x15, waiting for transfers between devices: 16.6 us -> 17.3 us  [swap(): return lax.ppermute(value, axis, [(i, i ^ bit) for i in range(size)])]
  transfers between devices with their start and end apart: 15 -> 15, of which waited for: 12 -> 11; matrix products, arithmetic and copies ran while one was open for 0% -> 0% of each run, Pallas kernels for 15% -> 11%
where the time goes in v7:
time: 51.5 us; the launch traced here: 51.3 us
  starting transfers between devices  18 us (35%)
  waiting for transfers between devices  17.3 us (34%)
  Pallas kernels  13.4 us (26%)
  local copies, waits for them, and re-layouts  1.78 us (3%)
  between operations  0.77 us (1%)
    ppermute x15, starting transfers between devices, swap(): return lax.ppermute(value, axis, [(i, i ^ bit) for i in range(size)])  18 us
    ppermute x15, waiting for transfers between devices, swap(): return lax.ppermute(value, axis, [(i, i ^ bit) for i in range(size)])  17.3 us
    pallas_call x15, Pallas kernels, call(): pl.pallas_call(kernel, out_shape=[jax.ShapeDtypeStruct(*x) for x in outs]...  13.4 us
    unnamed x16, local copies, waits for them, and re-layouts  1.78 us
  transfers between devices with their start and end apart: 15, of which 11 were waited for; matrix products, arithmetic and copies ran while one was open for 0% of the time, Pallas kernels for 11%

profile of v7, /device:TPU:0, one launch (start us, length us, event | category | flops | bytes accessed | tf_op | source)
XLA Modules:
  0.0 51.3 jit_solution(17881864708985657590)
XLA Ops:
  0.6 0.9 %copy-done.6 = bf16[1,64,128]{2,1,0:T(8,128)(2,1)S(1)} copy-done((bf16[1,64,128]{2,1,0:T(8,128)(2,1)S(1)}, bf16[1,64,128]{2,1,0:T(8,128)(2,1)}, u32[]{:S(2)}) %copy-start.6) | copy-done | bytes 16408
  1.5 0.9 %copy-done.7 = s32[288]{0:T(512)S(1)} copy-done((s32[288]{0:T(512)S(1)}, s32[288]{0:T(512)}, u32[]{:S(2)}) %copy-start.7) | copy-done | bytes 1176
  2.6 5.1 %collective-permute-start.2 = (bf16[1,64,128]{2,1,0:T(8,128)(2,1)S(1)}, bf16[1,64,128]{2,1,0:T(8,128)(2,1)S(1)}, u32[]{:S(2)}, u32[]{:S(2)}) collective-permute-start(bf16[1,64,128]{2,1,0:T(8,128)(2,1)S(1)} %get-tuple-element.27.refs_0_), channel_id=1, source_target_pairs={{0,12},{4,8},{8,4},{12,0},{1,13},{5,9},{9,5},{13,1},{2,14},{6,10},... | collective-permute-start | bytes 49160 | tf_op jit(solution)/shard_map/ppermute | solution.py:508
  7.7 0.6 %collective-permute-start = (bf16[1,64,128]{2,1,0:T(8,128)(2,1)S(1)}, bf16[1,64,128]{2,1,0:T(8,128)(2,1)S(1)}, u32[]{:S(2)}, u32[]{:S(2)}) collective-permute-start(bf16[1,64,128]{2,1,0:T(8,128)(2,1)S(1)} %get-tuple-element.27.refs_0_), channel_id=1, source_target_pairs={{0,4},{4,0},{8,12},{12,8},{1,5},{5,1},{9,13},{13,9},{2,6},{6,2},{1... | collective-permute-start | bytes 49160 | tf_op jit(solution)/shard_map/ppermute | solution.py:508
  8.4 1.4 %shard_map.96 = (bf16[32,144,256]{2,1,0:T(8,128)(2,1)S(1)}, bf16[32,144,256]{2,1,0:T(8,128)(2,1)S(1)}) custom-call(bf16[288,64,128]{2,1,0:T(8,128)(2,1)S(1)} %copy-done.5), custom_call_target="tpu_custom_call" | custom-call | flops 2147483648 | bytes 9437184 | tf_op jit(solution)/shard_map/pallas_call | solution.py:92
  9.8 2.6 %collective-permute-done.1.refs_2_ = bf16[1,64,128]{2,1,0:T(8,128)(2,1)S(1)} collective-permute-done((bf16[1,64,128]{2,1,0:T(8,128)(2,1)S(1)}, bf16[1,64,128]{2,1,0:T(8,128)(2,1)S(1)}, u32[]{:S(2)}, u32[]{:S(2)}) %collective-permute-start.1) | collective-permute-done | bytes 16416 | tf_op jit(solution)/shard_map/ppermute | solution.py:508
  12.4 1.3 %shard_map.97 = (f32[2,576,128]{2,1,0:T(8,128)S(1)}, f32[4,256]{1,0:T(4,128)S(1)}, bf16[32,16,256]{2,1,0:T(8,128)(2,1)S(1)}) custom-call(bf16[1,64,128]{2,1,0:T(8,128)(2,1)S(1)} %get-tuple-element.27.refs_0_, bf16[1,64,128]{2,1,0:T(8,128)(2,1)S(1)} %collective-permute-done.refs_1_, bf16[1,64,128]{2,1,0:T(8,128)(2,1)S(1)} %collective-permute-done.1.refs_2_, ...), custom_call_target="tpu_custom_call" | custom-call | flops 150994944 | bytes 3596288 | tf_op jit(solution)/shard_map/pallas_call | solution.py:92
  13.7 1.1 %shard_map.98.own = f32[2,576,128]{2,1,0:T(8,128)S(1)} custom-call(bf16[32,16,256]{2,1,0:T(8,128)(2,1)S(1)} %get-tuple-element.29.left_ref, bf16[32,144,256]{2,1,0:T(8,128)(2,1)S(1)} %get-tuple-element.30.particles), custom_call_target="tpu_custom_call" | custom-call | flops 301989888 | bytes 3211264 | tf_op jit(solution)/shard_map/pallas_call | solution.py:92
  14.8 0.9 %collective-permute-done.3.other = f32[2,576,128]{2,1,0:T(8,128)S(1)} collective-permute-done((f32[2,576,128]{2,1,0:T(8,128)S(1)}, f32[2,576,128]{2,1,0:T(8,128)S(1)}, u32[]{:S(2)}, u32[]{:S(2)}) %collective-permute-start.3) | collective-permute-done | bytes 589856 | tf_op jit(solution)/shard_map/ppermute | solution.py:508
  15.7 0.8 %shard_map.99 = (f32[4,256,256]{2,1,0:T(8,128)S(1)}, f32[8,256]{1,0:T(8,128)S(1)}) custom-call(f32[2,576,128]{2,1,0:T(8,128)S(1)} %shard_map.98.own, f32[2,576,128]{2,1,0:T(8,128)S(1)} %collective-permute-done.3.other, f32[4,256]{1,0:T(4,128)S(1)} %get-tuple-element.32.energy_ref, f32[256,256]{1,0:T(8,128)S(1)} %get-tuple-element.33.prior_term, ...), custom_call_target="tpu_custom_call" | custom-call | flops 402653184 | bytes 3047424 | tf_op jit(solution)/shard_map/pallas_call | solution.py:92
  16.5 1.6 %collective-permute-start.4 = (f32[8,256]{1,0:T(8,128)S(1)}, f32[8,256]{1,0:T(8,128)S(1)}, u32[]{:S(2)}, u32[]{:S(2)}) collective-permute-start(f32[8,256]{1,0:T(8,128)S(1)} %get-tuple-element.35.here.first), channel_id=1, source_target_pairs={{0,2},{2,0},{1,3},{3,1},{4,6},{6,4},{5,7},{7,5},{8,10},{10,8},{9,1... | collective-permute-start | bytes 24584 | tf_op jit(solution)/shard_map/ppermute | solution.py:508
  18.1 2.2 %collective-permute-done.4.second = f32[8,256]{1,0:T(8,128)S(1)} collective-permute-done((f32[8,256]{1,0:T(8,128)S(1)}, f32[8,256]{1,0:T(8,128)S(1)}, u32[]{:S(2)}, u32[]{:S(2)}) %collective-permute-start.4) | collective-permute-done | bytes 8224 | tf_op jit(solution)/shard_map/ppermute | solution.py:508
  20.8 1.1 %shard_map.101.image = f32[576,128]{1,0:T(8,128)S(1)} custom-call(bf16[4,256,256]{2,1,0:T(8,128)(2,1)S(1)} %get-tuple-element.36.rounded_ref, bf16[512,256]{1,0:T(8,128)(2,1)S(1)} %copy-done.1, bf16[512,256]{1,0:T(8,128)(2,1)S(1)} %copy-done, bf16[32,144,256]{2,1,0:T(8,128)(2,1)S(1)} %get-tuple-element.30.particles), custom_call_target="tpu_custom_call" | custom-call | flops 268435456 | bytes 4292608 | tf_op jit(solution)/shard_map/pallas_call | solution.py:92
  22.3 0.9 %shard_map.102.refs_0_ = bf16[272,128]{1,0:T(8,128)(2,1)S(1)} custom-call(f32[576,128]{1,0:T(8,128)S(1)} %shard_map.101.image, bf16[33,16,144]{2,1,0:T(8,128)(2,1)S(1)} %get-tuple-element.37.mine, bf16[33,16,144]{2,1,0:T(8,128)(2,1)S(1)} %collective-permute-done.5.spectrum, bf16[32,144,256]{2,1,0:T(8,128)(2,1)S(1)} %get-tuple-element.28.refs_5_.particles), custom_call_target="tpu_custom_call" | custom-call | flops 311427072 | bytes 3559424 | tf_op jit(solution)/shard_map/pallas_call | solution.py:92
  23.2 1.5 %collective-permute-start.8 = (bf16[272,128]{1,0:T(8,128)(2,1)S(1)}, bf16[272,128]{1,0:T(8,128)(2,1)S(1)}, u32[]{:S(2)}, u32[]{:S(2)}) collective-permute-start(bf16[272,128]{1,0:T(8,128)(2,1)S(1)} %shard_map.102.refs_0_), channel_id=1, source_target_pairs={{0,12},{4,8},{8,4},{12,0},{1,13},{5,9},{9,5},{13,1},{2,14},{6,10},... | collective-permute-start | bytes 208904 | tf_op jit(solution)/shard_map/ppermute | solution.py:508
  24.7 0.6 %collective-permute-start.7 = (bf16[272,128]{1,0:T(8,128)(2,1)S(1)}, bf16[272,128]{1,0:T(8,128)(2,1)S(1)}, u32[]{:S(2)}, u32[]{:S(2)}) collective-permute-start(bf16[272,128]{1,0:T(8,128)(2,1)S(1)} %shard_map.102.refs_0_), channel_id=1, source_target_pairs={{0,8},{4,12},{8,0},{12,4},{1,9},{5,13},{9,1},{13,5},{2,10},{6,14},... | collective-permute-start | bytes 208904 | tf_op jit(solution)/shard_map/ppermute | solution.py:508
  25.4 2.3 %collective-permute-start.6 = (bf16[272,128]{1,0:T(8,128)(2,1)S(1)}, bf16[272,128]{1,0:T(8,128)(2,1)S(1)}, u32[]{:S(2)}, u32[]{:S(2)}) collective-permute-start(bf16[272,128]{1,0:T(8,128)(2,1)S(1)} %shard_map.102.refs_0_), channel_id=1, source_target_pairs={{0,4},{4,0},{8,12},{12,8},{1,5},{5,1},{9,13},{13,9},{2,6},{6,2},{1... | collective-permute-start | bytes 208904 | tf_op jit(solution)/shard_map/ppermute | solution.py:508
  27.7 2.5 %collective-permute-done.8.refs_3_ = bf16[272,128]{1,0:T(8,128)(2,1)S(1)} collective-permute-done((bf16[272,128]{1,0:T(8,128)(2,1)S(1)}, bf16[272,128]{1,0:T(8,128)(2,1)S(1)}, u32[]{:S(2)}, u32[]{:S(2)}) %collective-permute-start.8) | collective-permute-done | bytes 69664 | tf_op jit(solution)/shard_map/ppermute | solution.py:508
  30.1 2.1 %collective-permute-done.7.refs_2_ = bf16[272,128]{1,0:T(8,128)(2,1)S(1)} collective-permute-done((bf16[272,128]{1,0:T(8,128)(2,1)S(1)}, bf16[272,128]{1,0:T(8,128)(2,1)S(1)}, u32[]{:S(2)}, u32[]{:S(2)}) %collective-permute-start.7) | collective-permute-done | bytes 69664 | tf_op jit(solution)/shard_map/ppermute | solution.py:508
  32.3 1.3 %shard_map.103 = (f32[2,576,128]{2,1,0:T(8,128)S(1)}, f32[4,256]{1,0:T(4,128)S(1)}, bf16[32,16,256]{2,1,0:T(8,128)(2,1)S(1)}) custom-call(bf16[272,128]{1,0:T(8,128)(2,1)S(1)} %shard_map.102.refs_0_, bf16[272,128]{1,0:T(8,128)(2,1)S(1)} %collective-permute-done.6.refs_1_, bf16[272,128]{1,0:T(8,128)(2,1)S(1)} %collective-permute-done.7.refs_2_, ...), custom_call_target="tpu_custom_call" | custom-call | flops 150994944 | bytes 3809280 | tf_op jit(solution)/shard_map/pallas_call | solution.py:92
  33.6 1.1 %shard_map.104.own = f32[2,576,128]{2,1,0:T(8,128)S(1)} custom-call(bf16[32,16,256]{2,1,0:T(8,128)(2,1)S(1)} %get-tuple-element.38.left_ref, bf16[32,144,256]{2,1,0:T(8,128)(2,1)S(1)} %get-tuple-element.30.particles), custom_call_target="tpu_custom_call" | custom-call | flops 301989888 | bytes 3211264 | tf_op jit(solution)/shard_map/pallas_call | solution.py:92
  34.7 0.9 %collective-permute-done.9.other = f32[2,576,128]{2,1,0:T(8,128)S(1)} collective-permute-done((f32[2,576,128]{2,1,0:T(8,128)S(1)}, f32[2,576,128]{2,1,0:T(8,128)S(1)}, u32[]{:S(2)}, u32[]{:S(2)}) %collective-permute-start.9) | collective-permute-done | bytes 589856 | tf_op jit(solution)/shard_map/ppermute | solution.py:508
  35.6 0.8 %shard_map.105 = (f32[4,256,256]{2,1,0:T(8,128)S(1)}, f32[8,256]{1,0:T(8,128)S(1)}) custom-call(f32[2,576,128]{2,1,0:T(8,128)S(1)} %shard_map.104.own, f32[2,576,128]{2,1,0:T(8,128)S(1)} %collective-permute-done.9.other, f32[4,256]{1,0:T(4,128)S(1)} %get-tuple-element.40.energy_ref, f32[256,256]{1,0:T(8,128)S(1)} %get-tuple-element.33.prior_term, ...), custom_call_target="tpu_custom_call" | custom-call | flops 402653184 | bytes 3047424 | tf_op jit(solution)/shard_map/pallas_call | solution.py:92
  36.4 1.6 %collective-permute-start.10 = (f32[8,256]{1,0:T(8,128)S(1)}, f32[8,256]{1,0:T(8,128)S(1)}, u32[]{:S(2)}, u32[]{:S(2)}) collective-permute-start(f32[8,256]{1,0:T(8,128)S(1)} %get-tuple-element.42.here.first), channel_id=1, source_target_pairs={{0,2},{2,0},{1,3},{3,1},{4,6},{6,4},{5,7},{7,5},{8,10},{10,8},{9,1... | collective-permute-start | bytes 24584 | tf_op jit(solution)/shard_map/ppermute | solution.py:508
  37.9 2.2 %collective-permute-done.10.second = f32[8,256]{1,0:T(8,128)S(1)} collective-permute-done((f32[8,256]{1,0:T(8,128)S(1)}, f32[8,256]{1,0:T(8,128)S(1)}, u32[]{:S(2)}, u32[]{:S(2)}) %collective-permute-start.10) | collective-permute-done | bytes 8224 | tf_op jit(solution)/shard_map/ppermute | solution.py:508
  40.7 1.1 %shard_map.107.image = f32[576,128]{1,0:T(8,128)S(1)} custom-call(bf16[4,256,256]{2,1,0:T(8,128)(2,1)S(1)} %get-tuple-element.43.rounded_ref, bf16[512,256]{1,0:T(8,128)(2,1)S(1)} %copy-done.1, bf16[512,256]{1,0:T(8,128)(2,1)S(1)} %copy-done, bf16[32,144,256]{2,1,0:T(8,128)(2,1)S(1)} %get-tuple-element.30.particles), custom_call_target="tpu_custom_call" | custom-call | flops 268435456 | bytes 4292608 | tf_op jit(solution)/shard_map/pallas_call | solution.py:92
  42.2 0.9 %shard_map.108 = (f32[72,128]{1,0:T(8,128)S(1)}, f32[72,128]{1,0:T(8,128)S(1)}, f32[72,128]{1,0:T(8,128)S(1)}, f32[72,128]{1,0:T(8,128)S(1)}) custom-call(f32[576,128]{1,0:T(8,128)S(1)} %shard_map.107.image, bf16[33,16,144]{2,1,0:T(8,128)(2,1)S(1)} %get-tuple-element.44.mine, bf16[33,16,144]{2,1,0:T(8,128)(2,1)S(1)} %collective-permute-done.11.spectrum, ...), custom_call_target="tpu_custom_call" | custom-call | flops 311427072 | bytes 3653632 | tf_op jit(solution)/shard_map/pallas_call | solution.py:92
  43.1 2.7 %collective-permute-start.12 = (f32[72,128]{1,0:T(8,128)S(1)}, f32[72,128]{1,0:T(8,128)S(1)}, u32[]{:S(2)}, u32[]{:S(2)}) collective-permute-start(f32[72,128]{1,0:T(8,128)S(1)} %get-tuple-element.45), channel_id=1, source_target_pairs={{0,12},{4,8},{8,4},{12,0},{1,13},{5,9},{9,5},{13,1},{2,14},{6,10},... | collective-permute-start | bytes 110600 | tf_op jit(solution)/shard_map/ppermute | solution.py:508
  45.8 1.8 %collective-permute-start.14 = (f32[72,128]{1,0:T(8,128)S(1)}, f32[72,128]{1,0:T(8,128)S(1)}, u32[]{:S(2)}, u32[]{:S(2)}) collective-permute-start(f32[72,128]{1,0:T(8,128)S(1)} %get-tuple-element.47), channel_id=1, source_target_pairs={{0,4},{4,0},{8,12},{12,8},{1,5},{5,1},{9,13},{13,9},{2,6},{6,2},{1... | collective-permute-start | bytes 110600 | tf_op jit(solution)/shard_map/ppermute | solution.py:508
  47.5 1.5 %collective-permute-done.12.refs_0_ = f32[72,128]{1,0:T(8,128)S(1)} collective-permute-done((f32[72,128]{1,0:T(8,128)S(1)}, f32[72,128]{1,0:T(8,128)S(1)}, u32[]{:S(2)}, u32[]{:S(2)}) %collective-permute-start.12) | collective-permute-done | bytes 36896 | tf_op jit(solution)/shard_map/ppermute | solution.py:508
  49.0 1.6 %collective-permute-done.13.refs_1_ = f32[72,128]{1,0:T(8,128)S(1)} collective-permute-done((f32[72,128]{1,0:T(8,128)S(1)}, f32[72,128]{1,0:T(8,128)S(1)}, u32[]{:S(2)}, u32[]{:S(2)}) %collective-permute-start.13) | collective-permute-done | bytes 36896 | tf_op jit(solution)/shard_map/ppermute | solution.py:508
  50.6 0.6 %shard_map.109 = (f32[1,64,128]{2,1,0:T(8,128)}, f32[1,144]{1,0:T(1,128)}) custom-call(f32[72,128]{1,0:T(8,128)S(1)} %collective-permute-done.12.refs_0_, f32[72,128]{1,0:T(8,128)S(1)} %collective-permute-done.13.refs_1_, f32[72,128]{1,0:T(8,128)S(1)} %collective-permute-done.14.refs_2_, f32[72,128]{1,0:T(8,128)S(1)} %get-tuple-element.48.refs_3_, ...), custom_call_target="tpu_custom_call" | custom-call | bytes 229376 | tf_op jit(solution)/shard_map/pallas_call | solution.py:92
  (29 shorter events, 2.4 us)
Async XLA Ops:
  0.6 7.7 %copy-start.5 = (bf16[288,64,128]{2,1,0:T(8,128)(2,1)S(1)}, bf16[288,64,128]{2,1,0:T(8,128)(2,1)}, u32[]{:S(2)}) copy-start(bf16[288,64,128]{2,1,0:T(8,128)(2,1)} %particles_ref.1) | copy-start | bytes 14155780
  0.6 0.9 %copy-start.6 = (bf16[1,64,128]{2,1,0:T(8,128)(2,1)S(1)}, bf16[1,64,128]{2,1,0:T(8,128)(2,1)}, u32[]{:S(2)}) copy-start(bf16[1,64,128]{2,1,0:T(8,128)(2,1)} %references_ref.1) | copy-start | bytes 49156
  1.5 0.9 %copy-start.7 = (s32[288]{0:T(512)S(1)}, s32[288]{0:T(512)}, u32[]{:S(2)}) copy-start(s32[288]{0:T(512)} %prior_ref.1) | copy-start | bytes 3460
  2.6 9.8 %copy-start.4 = (f32[64]{0:T(128)S(1)}, f32[64]{0:T(128)}, u32[]{:S(2)}) copy-start(f32[64]{0:T(128)} %param.10) | copy-start | bytes 772
  2.6 7.2 %collective-permute-start.2 = (bf16[1,64,128]{2,1,0:T(8,128)(2,1)S(1)}, bf16[1,64,128]{2,1,0:T(8,128)(2,1)S(1)}, u32[]{:S(2)}, u32[]{:S(2)}) collective-permute-start(bf16[1,64,128]{2,1,0:T(8,128)(2,1)S(1)} %get-tuple-element.27.refs_0_), channel_id=1, source_target_pairs={{0,12},{4,8},{8,4},{12,0},{1,13},{5,9},{9,5},{13,1},{2,14},{6,10},... | collective-permute-start | bytes 49160 | tf_op jit(solution)/shard_map/ppermute | solution.py:508
  7.7 4.6 %collective-permute-start.1 = (bf16[1,64,128]{2,1,0:T(8,128)(2,1)S(1)}, bf16[1,64,128]{2,1,0:T(8,128)(2,1)S(1)}, u32[]{:S(2)}, u32[]{:S(2)}) collective-permute-start(bf16[1,64,128]{2,1,0:T(8,128)(2,1)S(1)} %get-tuple-element.27.refs_0_), channel_id=1, source_target_pairs={{0,8},{4,12},{8,0},{12,4},{1,9},{5,13},{9,1},{13,5},{2,10},{6,14},... | collective-permute-start | bytes 49160 | tf_op jit(solution)/shard_map/ppermute | solution.py:508
  7.7 4.6 %collective-permute-start = (bf16[1,64,128]{2,1,0:T(8,128)(2,1)S(1)}, bf16[1,64,128]{2,1,0:T(8,128)(2,1)S(1)}, u32[]{:S(2)}, u32[]{:S(2)}) collective-permute-start(bf16[1,64,128]{2,1,0:T(8,128)(2,1)S(1)} %get-tuple-element.27.refs_0_), channel_id=1, source_target_pairs={{0,4},{4,0},{8,12},{12,8},{1,5},{5,1},{9,13},{13,9},{2,6},{6,2},{1... | collective-permute-start | bytes 49160 | tf_op jit(solution)/shard_map/ppermute | solution.py:508
  12.4 3.3 %copy-start.2 = (bf16[512,256]{1,0:T(8,128)(2,1)S(1)}, bf16[512,256]{1,0:T(8,128)(2,1)}, u32[]{:S(2)}) copy-start(bf16[512,256]{1,0:T(8,128)(2,1)} %constant.9.clone.inv_lo) | copy-start | bytes 786436
  12.4 3.3 %copy-start.3 = (bf16[512,256]{1,0:T(8,128)(2,1)S(1)}, bf16[512,256]{1,0:T(8,128)(2,1)}, u32[]{:S(2)}) copy-start(bf16[512,256]{1,0:T(8,128)(2,1)} %constant.8.clone.inv_hi) | copy-start | bytes 786436
  13.7 2.1 %collective-permute-start.3 = (f32[2,576,128]{2,1,0:T(8,128)S(1)}, f32[2,576,128]{2,1,0:T(8,128)S(1)}, u32[]{:S(2)}, u32[]{:S(2)}) collective-permute-start(f32[2,576,128]{2,1,0:T(8,128)S(1)} %get-tuple-element.31), channel_id=1, source_target_pairs={{0,1},{1,0},{2,3},{3,2},{4,5},{5,4},{6,7},{7,6},{8,9},{9,8},{10,11... | collective-permute-start | bytes 1769480 | tf_op jit(solution)/shard_map/ppermute | solution.py:508
  13.7 6.5 %copy-start = (bf16[512,256]{1,0:T(8,128)(2,1)S(1)}, bf16[512,256]{1,0:T(8,128)(2,1)}, u32[]{:S(2)}) copy-start(bf16[512,256]{1,0:T(8,128)(2,1)} %constant.11.clone.fwd_lo) | copy-start | bytes 786436
  13.7 6.5 %copy-start.1 = (bf16[512,256]{1,0:T(8,128)(2,1)S(1)}, bf16[512,256]{1,0:T(8,128)(2,1)}, u32[]{:S(2)}) copy-start(bf16[512,256]{1,0:T(8,128)(2,1)} %constant.10.clone.fwd_hi) | copy-start | bytes 786436
  16.5 3.7 %collective-permute-start.4 = (f32[8,256]{1,0:T(8,128)S(1)}, f32[8,256]{1,0:T(8,128)S(1)}, u32[]{:S(2)}, u32[]{:S(2)}) collective-permute-start(f32[8,256]{1,0:T(8,128)S(1)} %get-tuple-element.35.here.first), channel_id=1, source_target_pairs={{0,2},{2,0},{1,3},{3,1},{4,6},{6,4},{5,7},{7,5},{8,10},{10,8},{9,1... | collective-permute-start | bytes 24584 | tf_op jit(solution)/shard_map/ppermute | solution.py:508
  20.7 1.6 %collective-permute-start.5 = (bf16[33,16,144]{2,1,0:T(8,128)(2,1)S(1)}, bf16[33,16,144]{2,1,0:T(8,128)(2,1)S(1)}, u32[]{:S(2)}, u32[]{:S(2)}) collective-permute-start(bf16[33,16,144]{2,1,0:T(8,128)(2,1)S(1)} %get-tuple-element.37.mine), channel_id=1, source_target_pairs={{0,1},{1,0},{2,3},{3,2},{4,5},{5,4},{6,7},{7,6},{8,9},{9,8},{10,11... | collective-permute-start | bytes 456200 | tf_op jit(solution)/shard_map/ppermute | solution.py:508
  23.2 6.9 %collective-permute-start.8 = (bf16[272,128]{1,0:T(8,128)(2,1)S(1)}, bf16[272,128]{1,0:T(8,128)(2,1)S(1)}, u32[]{:S(2)}, u32[]{:S(2)}) collective-permute-start(bf16[272,128]{1,0:T(8,128)(2,1)S(1)} %shard_map.102.refs_0_), channel_id=1, source_target_pairs={{0,12},{4,8},{8,4},{12,0},{1,13},{5,9},{9,5},{13,1},{2,14},{6,10},... | collective-permute-start | bytes 208904 | tf_op jit(solution)/shard_map/ppermute | solution.py:508
  24.7 7.6 %collective-permute-start.7 = (bf16[272,128]{1,0:T(8,128)(2,1)S(1)}, bf16[272,128]{1,0:T(8,128)(2,1)S(1)}, u32[]{:S(2)}, u32[]{:S(2)}) collective-permute-start(bf16[272,128]{1,0:T(8,128)(2,1)S(1)} %shard_map.102.refs_0_), channel_id=1, source_target_pairs={{0,8},{4,12},{8,0},{12,4},{1,9},{5,13},{9,1},{13,5},{2,10},{6,14},... | collective-permute-start | bytes 208904 | tf_op jit(solution)/shard_map/ppermute | solution.py:508
  25.4 6.9 %collective-permute-start.6 = (bf16[272,128]{1,0:T(8,128)(2,1)S(1)}, bf16[272,128]{1,0:T(8,128)(2,1)S(1)}, u32[]{:S(2)}, u32[]{:S(2)}) collective-permute-start(bf16[272,128]{1,0:T(8,128)(2,1)S(1)} %shard_map.102.refs_0_), channel_id=1, source_target_pairs={{0,4},{4,0},{8,12},{12,8},{1,5},{5,1},{9,13},{13,9},{2,6},{6,2},{1... | collective-permute-start | bytes 208904 | tf_op jit(solution)/shard_map/ppermute | solution.py:508
  33.6 2.1 %collective-permute-start.9 = (f32[2,576,128]{2,1,0:T(8,128)S(1)}, f32[2,576,128]{2,1,0:T(8,128)S(1)}, u32[]{:S(2)}, u32[]{:S(2)}) collective-permute-start(f32[2,576,128]{2,1,0:T(8,128)S(1)} %get-tuple-element.39), channel_id=1, source_target_pairs={{0,1},{1,0},{2,3},{3,2},{4,5},{5,4},{6,7},{7,6},{8,9},{9,8},{10,11... | collective-permute-start | bytes 1769480 | tf_op jit(solution)/shard_map/ppermute | solution.py:508
  36.4 3.7 %collective-permute-start.10 = (f32[8,256]{1,0:T(8,128)S(1)}, f32[8,256]{1,0:T(8,128)S(1)}, u32[]{:S(2)}, u32[]{:S(2)}) collective-permute-start(f32[8,256]{1,0:T(8,128)S(1)} %get-tuple-element.42.here.first), channel_id=1, source_target_pairs={{0,2},{2,0},{1,3},{3,1},{4,6},{6,4},{5,7},{7,5},{8,10},{10,8},{9,1... | collective-permute-start | bytes 24584 | tf_op jit(solution)/shard_map/ppermute | solution.py:508
  40.6 1.6 %collective-permute-start.11 = (bf16[33,16,144]{2,1,0:T(8,128)(2,1)S(1)}, bf16[33,16,144]{2,1,0:T(8,128)(2,1)S(1)}, u32[]{:S(2)}, u32[]{:S(2)}) collective-permute-start(bf16[33,16,144]{2,1,0:T(8,128)(2,1)S(1)} %get-tuple-element.44.mine), channel_id=1, source_target_pairs={{0,1},{1,0},{2,3},{3,2},{4,5},{5,4},{6,7},{7,6},{8,9},{9,8},{10,11... | collective-permute-start | bytes 456200 | tf_op jit(solution)/shard_map/ppermute | solution.py:508
  43.1 5.9 %collective-permute-start.12 = (f32[72,128]{1,0:T(8,128)S(1)}, f32[72,128]{1,0:T(8,128)S(1)}, u32[]{:S(2)}, u32[]{:S(2)}) collective-permute-start(f32[72,128]{1,0:T(8,128)S(1)} %get-tuple-element.45), channel_id=1, source_target_pairs={{0,12},{4,8},{8,4},{12,0},{1,13},{5,9},{9,5},{13,1},{2,14},{6,10},... | collective-permute-start | bytes 110600 | tf_op jit(solution)/shard_map/ppermute | solution.py:508
  45.8 4.9 %collective-permute-start.13 = (f32[72,128]{1,0:T(8,128)S(1)}, f32[72,128]{1,0:T(8,128)S(1)}, u32[]{:S(2)}, u32[]{:S(2)}) collective-permute-start(f32[72,128]{1,0:T(8,128)S(1)} %get-tuple-element.46), channel_id=1, source_target_pairs={{0,8},{4,12},{8,0},{12,4},{1,9},{5,13},{9,1},{13,5},{2,10},{6,14},... | collective-permute-start | bytes 110600 | tf_op jit(solution)/shard_map/ppermute | solution.py:508
  45.8 4.9 %collective-permute-start.14 = (f32[72,128]{1,0:T(8,128)S(1)}, f32[72,128]{1,0:T(8,128)S(1)}, u32[]{:S(2)}, u32[]{:S(2)}) collective-permute-start(f32[72,128]{1,0:T(8,128)S(1)} %get-tuple-element.47), channel_id=1, source_target_pairs={{0,4},{4,0},{8,12},{12,8},{1,5},{5,1},{9,13},{13,9},{2,6},{6,2},{1... | collective-permute-start | bytes 110600 | tf_op jit(solution)/shard_map/ppermute | solution.py:508

commit v8 on v7

--- a/solution.py
+++ b/solution.py
@@ -100,8 +100,13 @@
     )(*ins)
 
 
-def prior_kernel(prior_ref, references_ref, prior_term, out):
-    out[...] = references_ref[...]
+def permutation_kernel(out):
+    to = lax.broadcasted_iota(jnp.int32, out.shape, 0)
+    at = lax.broadcasted_iota(jnp.int32, out.shape, 1)
+    out[...] = ((to // 16 == at % 16) & (to % 16 == at // 16)).astype(F32).astype(BF16)
+
+
+def prior_kernel(prior_ref, prior_term):
     turns = lax.broadcasted_iota(jnp.int32, prior_term.shape, 0)
     lane = lax.broadcasted_iota(jnp.int32, (1, prior_term.shape[1]), 1)
     priors = prior_ref[...].reshape(1, -1)
@@ -115,12 +120,10 @@
     prior_term[...] = -distance * distance / (2.0 * SIGMA * SIGMA)
 
 
-def prep_kernel(share, particles_ref, other, own):
+def prep_kernel(share, particles_ref, permutation_ref, other, own):
     freqs, depth = particles_ref.shape[1:]
     group = lax.axis_index("rot")
-    to = lax.broadcasted_iota(jnp.int32, (256, 256), 0)
-    at = lax.broadcasted_iota(jnp.int32, (256, 256), 1)
-    permutation = ((to // 16 == at % 16) & (to % 16 == at // 16)).astype(F32).astype(BF16)
+    permutation = permutation_ref[...]
     for out, first in ((other, (1 - group) * share), (own, group * share)):
         for p in range(0, share, 16):
             for f in range(0, freqs, 32):
@@ -140,12 +143,12 @@
                         ]
 
 
-def prep(particles, share):
+def prep(particles, permutation, share):
     _, freqs, depth = particles.shape
     assert share % 16 == 0 and freqs % 32 == 0
     return call(
         functools.partial(prep_kernel, share),
-        [particles],
+        [particles, permutation],
         [((freqs // 2, share, 2 * depth), BF16)] * 2,
         flops=1 << 31,
     )
@@ -524,14 +527,13 @@
     inverse_noise = noise_inv.reshape(1, depth // 2)
     assert blocks & (blocks - 1) == 0
 
-    prior_term, first = call(
-        prior_kernel,
-        [prior_rot, references],
-        [((ANG, lane_tiles(share) * 128), F32), (references.shape, BF16)],
-        flops=1 << 32,
+    (permutation,) = call(permutation_kernel, [], [((256, 256), BF16)], flops=1 << 32)
+    first, permutation = lax.optimization_barrier((references, permutation))
+    (prior_term,) = call(
+        prior_kernel, [prior_rot], [((ANG, lane_tiles(share) * 128), F32)], flops=1 << 26
     )
     sources = [swap(first, "blk", blocks, i) for i in reversed(range(blocks))][::-1]
-    other_images, own_images = prep(particles, share)
+    other_images, own_images = prep(particles, permutation, share)
     for step in range(ITERS):
         last = step == ITERS - 1
         message, energy, left = weigh(sources, inverse_noise, other_images, step == 0)

time: 51.5 us -> 50.2 us (0.975)
  local copies, waits for them, and re-layouts: 1.78 us -> 0.68 us
    unnamed x16, local copies, waits for them, and re-layouts: 1.78 us -> 0.68 us
    pallas_call x15 -> x16, Pallas kernels: 13.4 us -> 13.4 us  [call(): pl.pallas_call(kernel, out_shape=[jax.ShapeDtypeStruct(*x) for x in outs]...]
  transfers between devices with their start and end apart: 15 -> 15, of which waited for: 11 -> 11; matrix products, arithmetic and copies ran while one was open for 0% -> 0% of each run, Pallas kernels for 11% -> 12%
where the time goes in v8:
time: 50.2 us; the launch traced here: 49.9 us
  starting transfers between devices  17.9 us (36%)
  waiting for transfers between devices  17.2 us (34%)
  Pallas kernels  13.4 us (27%)
  between operations  0.78 us (2%)
  local copies, waits for them, and re-layouts  0.68 us (1%)
    ppermute x15, starting transfers between devices, swap(): return lax.ppermute(value, axis, [(i, i ^ bit) for i in range(size)])  17.9 us
    ppermute x15, waiting for transfers between devices, swap(): return lax.ppermute(value, axis, [(i, i ^ bit) for i in range(size)])  17.2 us
    pallas_call x16, Pallas kernels, call(): pl.pallas_call(kernel, out_shape=[jax.ShapeDtypeStruct(*x) for x in outs]...  13.4 us
  transfers between devices with their start and end apart: 15, of which 11 were waited for; matrix products, arithmetic and copies ran while one was open for 0% of the time, Pallas kernels for 12%

profile of v8, /device:TPU:0, one launch (start us, length us, event | category | flops | bytes accessed | tf_op | source)
XLA Modules:
  0.0 49.9 jit_solution(6112061750631678916)
XLA Ops:
  0.7 0.6 %copy-done.4 = bf16[1,64,128]{2,1,0:T(8,128)(2,1)S(1)} copy-done((bf16[1,64,128]{2,1,0:T(8,128)(2,1)S(1)}, bf16[1,64,128]{2,1,0:T(8,128)(2,1)}, u32[]{:S(2)}) %copy-start.4) | copy-done | bytes 16408
  1.4 5.0 %collective-permute-start.2 = (bf16[1,64,128]{2,1,0:T(8,128)(2,1)S(1)}, bf16[1,64,128]{2,1,0:T(8,128)(2,1)S(1)}, u32[]{:S(2)}, u32[]{:S(2)}) collective-permute-start(bf16[1,64,128]{2,1,0:T(8,128)(2,1)S(1)} %copy-done.4), channel_id=1, source_target_pairs={{0,12},{4,8},{8,4},{12,0},{1,13},{5,9},{9,5},{13,1},{2,14},{6,10},... | collective-permute-start | bytes 49160 | tf_op jit(solution)/shard_map/ppermute | solution.py:511
  6.4 0.6 %collective-permute-start = (bf16[1,64,128]{2,1,0:T(8,128)(2,1)S(1)}, bf16[1,64,128]{2,1,0:T(8,128)(2,1)S(1)}, u32[]{:S(2)}, u32[]{:S(2)}) collective-permute-start(bf16[1,64,128]{2,1,0:T(8,128)(2,1)S(1)} %copy-done.4), channel_id=1, source_target_pairs={{0,4},{4,0},{8,12},{12,8},{1,5},{5,1},{9,13},{13,9},{2,6},{6,2},{1... | collective-permute-start | bytes 49160 | tf_op jit(solution)/shard_map/ppermute | solution.py:511
  7.0 1.4 %shard_map.96 = (bf16[32,144,256]{2,1,0:T(8,128)(2,1)S(1)}, bf16[32,144,256]{2,1,0:T(8,128)(2,1)S(1)}) custom-call(bf16[288,64,128]{2,1,0:T(8,128)(2,1)S(1)} %copy-done.7, bf16[256,256]{1,0:T(8,128)(2,1)S(1)} %shard_map.95.permutation_ref), custom_call_target="tpu_custom_call" | custom-call | flops 2147483648 | bytes 9568256 | tf_op jit(solution)/shard_map/pallas_call | solution.py:92
  8.4 2.6 %collective-permute-done.1.refs_2_ = bf16[1,64,128]{2,1,0:T(8,128)(2,1)S(1)} collective-permute-done((bf16[1,64,128]{2,1,0:T(8,128)(2,1)S(1)}, bf16[1,64,128]{2,1,0:T(8,128)(2,1)S(1)}, u32[]{:S(2)}, u32[]{:S(2)}) %collective-permute-start.1) | collective-permute-done | bytes 16416 | tf_op jit(solution)/shard_map/ppermute | solution.py:511
  11.1 1.3 %shard_map.97 = (f32[2,576,128]{2,1,0:T(8,128)S(1)}, f32[4,256]{1,0:T(4,128)S(1)}, bf16[32,16,256]{2,1,0:T(8,128)(2,1)S(1)}) custom-call(bf16[1,64,128]{2,1,0:T(8,128)(2,1)S(1)} %copy-done.4, bf16[1,64,128]{2,1,0:T(8,128)(2,1)S(1)} %collective-permute-done.refs_1_, bf16[1,64,128]{2,1,0:T(8,128)(2,1)S(1)} %collective-permute-done.1.refs_2_, ...), custom_call_target="tpu_custom_call" | custom-call | flops 150994944 | bytes 3596288 | tf_op jit(solution)/shard_map/pallas_call | solution.py:92
  12.6 1.1 %shard_map.98.own = f32[2,576,128]{2,1,0:T(8,128)S(1)} custom-call(bf16[32,16,256]{2,1,0:T(8,128)(2,1)S(1)} %get-tuple-element.30.left_ref, bf16[32,144,256]{2,1,0:T(8,128)(2,1)S(1)} %get-tuple-element.31.particles), custom_call_target="tpu_custom_call" | custom-call | flops 301989888 | bytes 3211264 | tf_op jit(solution)/shard_map/pallas_call | solution.py:92
  13.7 0.7 %collective-permute-done.3.other = f32[2,576,128]{2,1,0:T(8,128)S(1)} collective-permute-done((f32[2,576,128]{2,1,0:T(8,128)S(1)}, f32[2,576,128]{2,1,0:T(8,128)S(1)}, u32[]{:S(2)}, u32[]{:S(2)}) %collective-permute-start.3) | collective-permute-done | bytes 589856 | tf_op jit(solution)/shard_map/ppermute | solution.py:511
  14.4 0.8 %shard_map.100 = (f32[4,256,256]{2,1,0:T(8,128)S(1)}, f32[8,256]{1,0:T(8,128)S(1)}) custom-call(f32[2,576,128]{2,1,0:T(8,128)S(1)} %shard_map.98.own, f32[2,576,128]{2,1,0:T(8,128)S(1)} %collective-permute-done.3.other, f32[4,256]{1,0:T(4,128)S(1)} %get-tuple-element.33.energy_ref, f32[256,256]{1,0:T(8,128)S(1)} %shard_map.99.prior_term, ...), custom_call_target="tpu_custom_call" | custom-call | flops 402653184 | bytes 3047424 | tf_op jit(solution)/shard_map/pallas_call | solution.py:92
  15.2 1.5 %collective-permute-start.4 = (f32[8,256]{1,0:T(8,128)S(1)}, f32[8,256]{1,0:T(8,128)S(1)}, u32[]{:S(2)}, u32[]{:S(2)}) collective-permute-start(f32[8,256]{1,0:T(8,128)S(1)} %get-tuple-element.35.here.first), channel_id=1, source_target_pairs={{0,2},{2,0},{1,3},{3,1},{4,6},{6,4},{5,7},{7,5},{8,10},{10,8},{9,1... | collective-permute-start | bytes 24584 | tf_op jit(solution)/shard_map/ppermute | solution.py:511
  16.7 2.2 %collective-permute-done.4.second = f32[8,256]{1,0:T(8,128)S(1)} collective-permute-done((f32[8,256]{1,0:T(8,128)S(1)}, f32[8,256]{1,0:T(8,128)S(1)}, u32[]{:S(2)}, u32[]{:S(2)}) %collective-permute-start.4) | collective-permute-done | bytes 8224 | tf_op jit(solution)/shard_map/ppermute | solution.py:511
  18.9 0.5 shard_map.101
  19.5 1.1 %shard_map.102.image = f32[576,128]{1,0:T(8,128)S(1)} custom-call(bf16[4,256,256]{2,1,0:T(8,128)(2,1)S(1)} %get-tuple-element.36.rounded_ref, bf16[512,256]{1,0:T(8,128)(2,1)S(1)} %copy-done.1, bf16[512,256]{1,0:T(8,128)(2,1)S(1)} %copy-done, bf16[32,144,256]{2,1,0:T(8,128)(2,1)S(1)} %get-tuple-element.31.particles), custom_call_target="tpu_custom_call" | custom-call | flops 268435456 | bytes 4292608 | tf_op jit(solution)/shard_map/pallas_call | solution.py:92
  21.0 0.9 %shard_map.103.refs_0_ = bf16[272,128]{1,0:T(8,128)(2,1)S(1)} custom-call(f32[576,128]{1,0:T(8,128)S(1)} %shard_map.102.image, bf16[33,16,144]{2,1,0:T(8,128)(2,1)S(1)} %get-tuple-element.37.mine, bf16[33,16,144]{2,1,0:T(8,128)(2,1)S(1)} %collective-permute-done.5.spectrum, bf16[32,144,256]{2,1,0:T(8,128)(2,1)S(1)} %get-tuple-element.29.refs_5_.particles), custom_call_target="tpu_custom_call" | custom-call | flops 311427072 | bytes 3559424 | tf_op jit(solution)/shard_map/pallas_call | solution.py:92
  21.9 1.5 %collective-permute-start.8 = (bf16[272,128]{1,0:T(8,128)(2,1)S(1)}, bf16[272,128]{1,0:T(8,128)(2,1)S(1)}, u32[]{:S(2)}, u32[]{:S(2)}) collective-permute-start(bf16[272,128]{1,0:T(8,128)(2,1)S(1)} %shard_map.103.refs_0_), channel_id=1, source_target_pairs={{0,12},{4,8},{8,4},{12,0},{1,13},{5,9},{9,5},{13,1},{2,14},{6,10},... | collective-permute-start | bytes 208904 | tf_op jit(solution)/shard_map/ppermute | solution.py:511
  23.4 0.6 %collective-permute-start.7 = (bf16[272,128]{1,0:T(8,128)(2,1)S(1)}, bf16[272,128]{1,0:T(8,128)(2,1)S(1)}, u32[]{:S(2)}, u32[]{:S(2)}) collective-permute-start(bf16[272,128]{1,0:T(8,128)(2,1)S(1)} %shard_map.103.refs_0_), channel_id=1, source_target_pairs={{0,8},{4,12},{8,0},{12,4},{1,9},{5,13},{9,1},{13,5},{2,10},{6,14},... | collective-permute-start | bytes 208904 | tf_op jit(solution)/shard_map/ppermute | solution.py:511
  24.0 2.3 %collective-permute-start.6 = (bf16[272,128]{1,0:T(8,128)(2,1)S(1)}, bf16[272,128]{1,0:T(8,128)(2,1)S(1)}, u32[]{:S(2)}, u32[]{:S(2)}) collective-permute-start(bf16[272,128]{1,0:T(8,128)(2,1)S(1)} %shard_map.103.refs_0_), channel_id=1, source_target_pairs={{0,4},{4,0},{8,12},{12,8},{1,5},{5,1},{9,13},{13,9},{2,6},{6,2},{1... | collective-permute-start | bytes 208904 | tf_op jit(solution)/shard_map/ppermute | solution.py:511
  26.3 2.5 %collective-permute-done.8.refs_3_ = bf16[272,128]{1,0:T(8,128)(2,1)S(1)} collective-permute-done((bf16[272,128]{1,0:T(8,128)(2,1)S(1)}, bf16[272,128]{1,0:T(8,128)(2,1)S(1)}, u32[]{:S(2)}, u32[]{:S(2)}) %collective-permute-start.8) | collective-permute-done | bytes 69664 | tf_op jit(solution)/shard_map/ppermute | solution.py:511
  28.8 2.1 %collective-permute-done.7.refs_2_ = bf16[272,128]{1,0:T(8,128)(2,1)S(1)} collective-permute-done((bf16[272,128]{1,0:T(8,128)(2,1)S(1)}, bf16[272,128]{1,0:T(8,128)(2,1)S(1)}, u32[]{:S(2)}, u32[]{:S(2)}) %collective-permute-start.7) | collective-permute-done | bytes 69664 | tf_op jit(solution)/shard_map/ppermute | solution.py:511
  31.0 1.3 %shard_map.104 = (f32[2,576,128]{2,1,0:T(8,128)S(1)}, f32[4,256]{1,0:T(4,128)S(1)}, bf16[32,16,256]{2,1,0:T(8,128)(2,1)S(1)}) custom-call(bf16[272,128]{1,0:T(8,128)(2,1)S(1)} %shard_map.103.refs_0_, bf16[272,128]{1,0:T(8,128)(2,1)S(1)} %collective-permute-done.6.refs_1_, bf16[272,128]{1,0:T(8,128)(2,1)S(1)} %collective-permute-done.7.refs_2_, ...), custom_call_target="tpu_custom_call" | custom-call | flops 150994944 | bytes 3809280 | tf_op jit(solution)/shard_map/pallas_call | solution.py:92
  32.3 1.1 %shard_map.105.own = f32[2,576,128]{2,1,0:T(8,128)S(1)} custom-call(bf16[32,16,256]{2,1,0:T(8,128)(2,1)S(1)} %get-tuple-element.38.left_ref, bf16[32,144,256]{2,1,0:T(8,128)(2,1)S(1)} %get-tuple-element.31.particles), custom_call_target="tpu_custom_call" | custom-call | flops 301989888 | bytes 3211264 | tf_op jit(solution)/shard_map/pallas_call | solution.py:92
  33.4 0.9 %collective-permute-done.9.other = f32[2,576,128]{2,1,0:T(8,128)S(1)} collective-permute-done((f32[2,576,128]{2,1,0:T(8,128)S(1)}, f32[2,576,128]{2,1,0:T(8,128)S(1)}, u32[]{:S(2)}, u32[]{:S(2)}) %collective-permute-start.9) | collective-permute-done | bytes 589856 | tf_op jit(solution)/shard_map/ppermute | solution.py:511
  34.3 0.8 %shard_map.106 = (f32[4,256,256]{2,1,0:T(8,128)S(1)}, f32[8,256]{1,0:T(8,128)S(1)}) custom-call(f32[2,576,128]{2,1,0:T(8,128)S(1)} %shard_map.105.own, f32[2,576,128]{2,1,0:T(8,128)S(1)} %collective-permute-done.9.other, f32[4,256]{1,0:T(4,128)S(1)} %get-tuple-element.40.energy_ref, f32[256,256]{1,0:T(8,128)S(1)} %shard_map.99.prior_term, ...), custom_call_target="tpu_custom_call" | custom-call | flops 402653184 | bytes 3047424 | tf_op jit(solution)/shard_map/pallas_call | solution.py:92
  35.1 1.5 %collective-permute-start.10 = (f32[8,256]{1,0:T(8,128)S(1)}, f32[8,256]{1,0:T(8,128)S(1)}, u32[]{:S(2)}, u32[]{:S(2)}) collective-permute-start(f32[8,256]{1,0:T(8,128)S(1)} %get-tuple-element.42.here.first), channel_id=1, source_target_pairs={{0,2},{2,0},{1,3},{3,1},{4,6},{6,4},{5,7},{7,5},{8,10},{10,8},{9,1... | collective-permute-start | bytes 24584 | tf_op jit(solution)/shard_map/ppermute | solution.py:511
  36.6 2.2 %collective-permute-done.10.second = f32[8,256]{1,0:T(8,128)S(1)} collective-permute-done((f32[8,256]{1,0:T(8,128)S(1)}, f32[8,256]{1,0:T(8,128)S(1)}, u32[]{:S(2)}, u32[]{:S(2)}) %collective-permute-start.10) | collective-permute-done | bytes 8224 | tf_op jit(solution)/shard_map/ppermute | solution.py:511
  39.3 1.1 %shard_map.108.image = f32[576,128]{1,0:T(8,128)S(1)} custom-call(bf16[4,256,256]{2,1,0:T(8,128)(2,1)S(1)} %get-tuple-element.43.rounded_ref, bf16[512,256]{1,0:T(8,128)(2,1)S(1)} %copy-done.1, bf16[512,256]{1,0:T(8,128)(2,1)S(1)} %copy-done, bf16[32,144,256]{2,1,0:T(8,128)(2,1)S(1)} %get-tuple-element.31.particles), custom_call_target="tpu_custom_call" | custom-call | flops 268435456 | bytes 4292608 | tf_op jit(solution)/shard_map/pallas_call | solution.py:92
  40.9 0.9 %shard_map.109 = (f32[72,128]{1,0:T(8,128)S(1)}, f32[72,128]{1,0:T(8,128)S(1)}, f32[72,128]{1,0:T(8,128)S(1)}, f32[72,128]{1,0:T(8,128)S(1)}) custom-call(f32[576,128]{1,0:T(8,128)S(1)} %shard_map.108.image, bf16[33,16,144]{2,1,0:T(8,128)(2,1)S(1)} %get-tuple-element.44.mine, bf16[33,16,144]{2,1,0:T(8,128)(2,1)S(1)} %collective-permute-done.11.spectrum, ...), custom_call_target="tpu_custom_call" | custom-call | flops 311427072 | bytes 3653632 | tf_op jit(solution)/shard_map/pallas_call | solution.py:92
  41.8 2.7 %collective-permute-start.12 = (f32[72,128]{1,0:T(8,128)S(1)}, f32[72,128]{1,0:T(8,128)S(1)}, u32[]{:S(2)}, u32[]{:S(2)}) collective-permute-start(f32[72,128]{1,0:T(8,128)S(1)} %get-tuple-element.45), channel_id=1, source_target_pairs={{0,12},{4,8},{8,4},{12,0},{1,13},{5,9},{9,5},{13,1},{2,14},{6,10},... | collective-permute-start | bytes 110600 | tf_op jit(solution)/shard_map/ppermute | solution.py:511
  44.4 1.8 %collective-permute-start.14 = (f32[72,128]{1,0:T(8,128)S(1)}, f32[72,128]{1,0:T(8,128)S(1)}, u32[]{:S(2)}, u32[]{:S(2)}) collective-permute-start(f32[72,128]{1,0:T(8,128)S(1)} %get-tuple-element.47), channel_id=1, source_target_pairs={{0,4},{4,0},{8,12},{12,8},{1,5},{5,1},{9,13},{13,9},{2,6},{6,2},{1... | collective-permute-start | bytes 110600 | tf_op jit(solution)/shard_map/ppermute | solution.py:511
  46.2 1.5 %collective-permute-done.12.refs_0_ = f32[72,128]{1,0:T(8,128)S(1)} collective-permute-done((f32[72,128]{1,0:T(8,128)S(1)}, f32[72,128]{1,0:T(8,128)S(1)}, u32[]{:S(2)}, u32[]{:S(2)}) %collective-permute-start.12) | collective-permute-done | bytes 36896 | tf_op jit(solution)/shard_map/ppermute | solution.py:511
  47.7 1.6 %collective-permute-done.13.refs_1_ = f32[72,128]{1,0:T(8,128)S(1)} collective-permute-done((f32[72,128]{1,0:T(8,128)S(1)}, f32[72,128]{1,0:T(8,128)S(1)}, u32[]{:S(2)}, u32[]{:S(2)}) %collective-permute-start.13) | collective-permute-done | bytes 36896 | tf_op jit(solution)/shard_map/ppermute | solution.py:511
  49.3 0.6 %shard_map.110 = (f32[1,64,128]{2,1,0:T(8,128)}, f32[1,144]{1,0:T(1,128)}) custom-call(f32[72,128]{1,0:T(8,128)S(1)} %collective-permute-done.12.refs_0_, f32[72,128]{1,0:T(8,128)S(1)} %collective-permute-done.13.refs_1_, f32[72,128]{1,0:T(8,128)S(1)} %collective-permute-done.14.refs_2_, f32[72,128]{1,0:T(8,128)S(1)} %get-tuple-element.48.refs_3_, ...), custom_call_target="tpu_custom_call" | custom-call | bytes 229376 | tf_op jit(solution)/shard_map/pallas_call | solution.py:92
  (30 shorter events, 2.0 us)
Async XLA Ops:
  0.6 0.7 %copy-start.4 = (bf16[1,64,128]{2,1,0:T(8,128)(2,1)S(1)}, bf16[1,64,128]{2,1,0:T(8,128)(2,1)}, u32[]{:S(2)}) copy-start(bf16[1,64,128]{2,1,0:T(8,128)(2,1)} %refs_0_) | copy-start | bytes 49156
  0.6 6.3 %copy-start.7 = (bf16[288,64,128]{2,1,0:T(8,128)(2,1)S(1)}, bf16[288,64,128]{2,1,0:T(8,128)(2,1)}, u32[]{:S(2)}) copy-start(bf16[288,64,128]{2,1,0:T(8,128)(2,1)} %particles_ref.1) | copy-start | bytes 14155780
  1.3 9.7 %copy-start.6 = (f32[64]{0:T(128)S(1)}, f32[64]{0:T(128)}, u32[]{:S(2)}) copy-start(f32[64]{0:T(128)} %param.10) | copy-start | bytes 772
  1.4 7.0 %collective-permute-start.2 = (bf16[1,64,128]{2,1,0:T(8,128)(2,1)S(1)}, bf16[1,64,128]{2,1,0:T(8,128)(2,1)S(1)}, u32[]{:S(2)}, u32[]{:S(2)}) collective-permute-start(bf16[1,64,128]{2,1,0:T(8,128)(2,1)S(1)} %copy-done.4), channel_id=1, source_target_pairs={{0,12},{4,8},{8,4},{12,0},{1,13},{5,9},{9,5},{13,1},{2,14},{6,10},... | collective-permute-start | bytes 49160 | tf_op jit(solution)/shard_map/ppermute | solution.py:511
  6.4 4.6 %collective-permute-start.1 = (bf16[1,64,128]{2,1,0:T(8,128)(2,1)S(1)}, bf16[1,64,128]{2,1,0:T(8,128)(2,1)S(1)}, u32[]{:S(2)}, u32[]{:S(2)}) collective-permute-start(bf16[1,64,128]{2,1,0:T(8,128)(2,1)S(1)} %copy-done.4), channel_id=1, source_target_pairs={{0,8},{4,12},{8,0},{12,4},{1,9},{5,13},{9,1},{13,5},{2,10},{6,14},... | collective-permute-start | bytes 49160 | tf_op jit(solution)/shard_map/ppermute | solution.py:511
  6.4 4.6 %collective-permute-start = (bf16[1,64,128]{2,1,0:T(8,128)(2,1)S(1)}, bf16[1,64,128]{2,1,0:T(8,128)(2,1)S(1)}, u32[]{:S(2)}, u32[]{:S(2)}) collective-permute-start(bf16[1,64,128]{2,1,0:T(8,128)(2,1)S(1)} %copy-done.4), channel_id=1, source_target_pairs={{0,4},{4,0},{8,12},{12,8},{1,5},{5,1},{9,13},{13,9},{2,6},{6,2},{1... | collective-permute-start | bytes 49160 | tf_op jit(solution)/shard_map/ppermute | solution.py:511
  8.4 4.0 %copy-start.5 = (s32[288]{0:T(512)S(1)}, s32[288]{0:T(512)}, u32[]{:S(2)}) copy-start(s32[288]{0:T(512)} %prior_ref.1) | copy-start | bytes 3460
  11.0 3.3 %copy-start.2 = (bf16[512,256]{1,0:T(8,128)(2,1)S(1)}, bf16[512,256]{1,0:T(8,128)(2,1)}, u32[]{:S(2)}) copy-start(bf16[512,256]{1,0:T(8,128)(2,1)} %constant.9.clone.inv_lo) | copy-start | bytes 786436
  11.0 3.3 %copy-start.3 = (bf16[512,256]{1,0:T(8,128)(2,1)S(1)}, bf16[512,256]{1,0:T(8,128)(2,1)}, u32[]{:S(2)}) copy-start(bf16[512,256]{1,0:T(8,128)(2,1)} %constant.8.clone.inv_hi) | copy-start | bytes 786436
  12.3 2.1 %collective-permute-start.3 = (f32[2,576,128]{2,1,0:T(8,128)S(1)}, f32[2,576,128]{2,1,0:T(8,128)S(1)}, u32[]{:S(2)}, u32[]{:S(2)}) collective-permute-start(f32[2,576,128]{2,1,0:T(8,128)S(1)} %get-tuple-element.32), channel_id=1, source_target_pairs={{0,1},{1,0},{2,3},{3,2},{4,5},{5,4},{6,7},{7,6},{8,9},{9,8},{10,11... | collective-permute-start | bytes 1769480 | tf_op jit(solution)/shard_map/ppermute | solution.py:511
  12.6 6.3 %copy-start = (bf16[512,256]{1,0:T(8,128)(2,1)S(1)}, bf16[512,256]{1,0:T(8,128)(2,1)}, u32[]{:S(2)}) copy-start(bf16[512,256]{1,0:T(8,128)(2,1)} %constant.11.clone.fwd_lo) | copy-start | bytes 786436
  12.6 6.3 %copy-start.1 = (bf16[512,256]{1,0:T(8,128)(2,1)S(1)}, bf16[512,256]{1,0:T(8,128)(2,1)}, u32[]{:S(2)}) copy-start(bf16[512,256]{1,0:T(8,128)(2,1)} %constant.10.clone.fwd_hi) | copy-start | bytes 786436
  15.2 3.7 %collective-permute-start.4 = (f32[8,256]{1,0:T(8,128)S(1)}, f32[8,256]{1,0:T(8,128)S(1)}, u32[]{:S(2)}, u32[]{:S(2)}) collective-permute-start(f32[8,256]{1,0:T(8,128)S(1)} %get-tuple-element.35.here.first), channel_id=1, source_target_pairs={{0,2},{2,0},{1,3},{3,1},{4,6},{6,4},{5,7},{7,5},{8,10},{10,8},{9,1... | collective-permute-start | bytes 24584 | tf_op jit(solution)/shard_map/ppermute | solution.py:511
  19.4 1.6 %collective-permute-start.5 = (bf16[33,16,144]{2,1,0:T(8,128)(2,1)S(1)}, bf16[33,16,144]{2,1,0:T(8,128)(2,1)S(1)}, u32[]{:S(2)}, u32[]{:S(2)}) collective-permute-start(bf16[33,16,144]{2,1,0:T(8,128)(2,1)S(1)} %get-tuple-element.37.mine), channel_id=1, source_target_pairs={{0,1},{1,0},{2,3},{3,2},{4,5},{5,4},{6,7},{7,6},{8,9},{9,8},{10,11... | collective-permute-start | bytes 456200 | tf_op jit(solution)/shard_map/ppermute | solution.py:511
  21.9 6.9 %collective-permute-start.8 = (bf16[272,128]{1,0:T(8,128)(2,1)S(1)}, bf16[272,128]{1,0:T(8,128)(2,1)S(1)}, u32[]{:S(2)}, u32[]{:S(2)}) collective-permute-start(bf16[272,128]{1,0:T(8,128)(2,1)S(1)} %shard_map.103.refs_0_), channel_id=1, source_target_pairs={{0,12},{4,8},{8,4},{12,0},{1,13},{5,9},{9,5},{13,1},{2,14},{6,10},... | collective-permute-start | bytes 208904 | tf_op jit(solution)/shard_map/ppermute | solution.py:511
  23.4 7.6 %collective-permute-start.7 = (bf16[272,128]{1,0:T(8,128)(2,1)S(1)}, bf16[272,128]{1,0:T(8,128)(2,1)S(1)}, u32[]{:S(2)}, u32[]{:S(2)}) collective-permute-start(bf16[272,128]{1,0:T(8,128)(2,1)S(1)} %shard_map.103.refs_0_), channel_id=1, source_target_pairs={{0,8},{4,12},{8,0},{12,4},{1,9},{5,13},{9,1},{13,5},{2,10},{6,14},... | collective-permute-start | bytes 208904 | tf_op jit(solution)/shard_map/ppermute | solution.py:511
  24.0 6.9 %collective-permute-start.6 = (bf16[272,128]{1,0:T(8,128)(2,1)S(1)}, bf16[272,128]{1,0:T(8,128)(2,1)S(1)}, u32[]{:S(2)}, u32[]{:S(2)}) collective-permute-start(bf16[272,128]{1,0:T(8,128)(2,1)S(1)} %shard_map.103.refs_0_), channel_id=1, source_target_pairs={{0,4},{4,0},{8,12},{12,8},{1,5},{5,1},{9,13},{13,9},{2,6},{6,2},{1... | collective-permute-start | bytes 208904 | tf_op jit(solution)/shard_map/ppermute | solution.py:511
  32.2 2.1 %collective-permute-start.9 = (f32[2,576,128]{2,1,0:T(8,128)S(1)}, f32[2,576,128]{2,1,0:T(8,128)S(1)}, u32[]{:S(2)}, u32[]{:S(2)}) collective-permute-start(f32[2,576,128]{2,1,0:T(8,128)S(1)} %get-tuple-element.39), channel_id=1, source_target_pairs={{0,1},{1,0},{2,3},{3,2},{4,5},{5,4},{6,7},{7,6},{8,9},{9,8},{10,11... | collective-permute-start | bytes 1769480 | tf_op jit(solution)/shard_map/ppermute | solution.py:511
  35.1 3.7 %collective-permute-start.10 = (f32[8,256]{1,0:T(8,128)S(1)}, f32[8,256]{1,0:T(8,128)S(1)}, u32[]{:S(2)}, u32[]{:S(2)}) collective-permute-start(f32[8,256]{1,0:T(8,128)S(1)} %get-tuple-element.42.here.first), channel_id=1, source_target_pairs={{0,2},{2,0},{1,3},{3,1},{4,6},{6,4},{5,7},{7,5},{8,10},{10,8},{9,1... | collective-permute-start | bytes 24584 | tf_op jit(solution)/shard_map/ppermute | solution.py:511
  39.3 1.6 %collective-permute-start.11 = (bf16[33,16,144]{2,1,0:T(8,128)(2,1)S(1)}, bf16[33,16,144]{2,1,0:T(8,128)(2,1)S(1)}, u32[]{:S(2)}, u32[]{:S(2)}) collective-permute-start(bf16[33,16,144]{2,1,0:T(8,128)(2,1)S(1)} %get-tuple-element.44.mine), channel_id=1, source_target_pairs={{0,1},{1,0},{2,3},{3,2},{4,5},{5,4},{6,7},{7,6},{8,9},{9,8},{10,11... | collective-permute-start | bytes 456200 | tf_op jit(solution)/shard_map/ppermute | solution.py:511
  41.8 5.9 %collective-permute-start.12 = (f32[72,128]{1,0:T(8,128)S(1)}, f32[72,128]{1,0:T(8,128)S(1)}, u32[]{:S(2)}, u32[]{:S(2)}) collective-permute-start(f32[72,128]{1,0:T(8,128)S(1)} %get-tuple-element.45), channel_id=1, source_target_pairs={{0,12},{4,8},{8,4},{12,0},{1,13},{5,9},{9,5},{13,1},{2,14},{6,10},... | collective-permute-start | bytes 110600 | tf_op jit(solution)/shard_map/ppermute | solution.py:511
  44.4 4.9 %collective-permute-start.13 = (f32[72,128]{1,0:T(8,128)S(1)}, f32[72,128]{1,0:T(8,128)S(1)}, u32[]{:S(2)}, u32[]{:S(2)}) collective-permute-start(f32[72,128]{1,0:T(8,128)S(1)} %get-tuple-element.46), channel_id=1, source_target_pairs={{0,8},{4,12},{8,0},{12,4},{1,9},{5,13},{9,1},{13,5},{2,10},{6,14},... | collective-permute-start | bytes 110600 | tf_op jit(solution)/shard_map/ppermute | solution.py:511
  44.4 4.9 %collective-permute-start.14 = (f32[72,128]{1,0:T(8,128)S(1)}, f32[72,128]{1,0:T(8,128)S(1)}, u32[]{:S(2)}, u32[]{:S(2)}) collective-permute-start(f32[72,128]{1,0:T(8,128)S(1)} %get-tuple-element.47), channel_id=1, source_target_pairs={{0,4},{4,0},{8,12},{12,8},{1,5},{5,1},{9,13},{13,9},{2,6},{6,2},{1... | collective-permute-start | bytes 110600 | tf_op jit(solution)/shard_map/ppermute | solution.py:511

commit v9 on v8

--- a/solution.py
+++ b/solution.py
@@ -163,7 +163,7 @@
 
 def weigh_kernel(fresh, count, *refs):
     sources = refs[:count]
-    doubled_ref, particles, out, energy_ref, left_ref, image = refs[count:]
+    doubled_ref, particles, out, energy_ref, left_ref, image, *rest = refs[count:]
     pairs, share, twice = particles.shape
     freqs, depth = 2 * pairs, twice // 2
     classes, lanes = energy_ref.shape
@@ -193,7 +193,7 @@
         energy = jnp.sum(plain * plain * scale, axis=0, keepdims=True)
         energy = jnp.broadcast_to(jnp.sum(energy, axis=1, keepdims=True), (SPARE, lanes))
         energy_ref[pl.ds(k, 1), :] = energy[:1]
-        out[0, rows(2 * k * pitch + freqs, SPARE), :] = energy[:, : out.shape[2]]
+        out[rows(2 * k * pitch + freqs, SPARE), :] = energy[:, : out.shape[1]]
 
     none = jnp.zeros((2 * classes, depth), BF16)
 
@@ -206,24 +206,31 @@
             [jnp.concatenate([first, none], 1), jnp.concatenate([none, second], 1)], 0
         )
         left_ref[f] = left
-        place(out, f, times(left, particles[f]), classes, pitch)
+        place([out, *rest], f, times(left, particles[f]), classes, pitch)
 
     loop(pairs, correlate, 8)
+    for ref in rest:
+        width = share - 128
+        for pack in range(-(-2 * classes * width // 128)):
+            total = 0.0
+            for i in range(min(128 // width, 2 * classes - pack * (128 // width))):
+                group = ref[rows((pack * (128 // width) + i) * pitch, pitch), :]
+                total = total + (pltpu.roll(group, i * width, 1) if i else group)
+            out[rows((2 * classes + pack) * pitch, pitch), :] = total
 
 
 def times(left, particles):
     return lax.dot_general(left, particles, (((1,), (1,)), ((), ())), preferred_element_type=F32)
 
 
-def place(out, f, value, classes, pitch):
-    tiles, _, width = out.shape
-    spare = jnp.zeros((value.shape[0], tiles * width - value.shape[1]), F32)
+def place(outs, f, value, classes, pitch):
+    spare = jnp.zeros((value.shape[0], len(outs) * 128 - value.shape[1]), F32)
     value = jnp.concatenate([value, spare], 1) if spare.size else value
     for part in range(2):
         at = pl.ds(2 * f + part, 2 * classes, stride=pitch)
-        for tile in range(tiles):
-            out[tile, at, :] = value[
-                part * 2 * classes : (part + 1) * 2 * classes, tile * width : (tile + 1) * width
+        for tile, out in enumerate(outs):
+            out[at, :] = value[
+                part * 2 * classes : (part + 1) * 2 * classes, tile * 128 : (tile + 1) * 128
             ]
 
 
@@ -234,17 +241,20 @@
 def weigh(sources, inverse_noise, particles, fresh):
     pairs, share, twice = particles.shape
     classes = len(sources)
-    lines = 2 * classes * (2 * pairs + SPARE)
+    pitch = 2 * pairs + SPARE
     tiles = lane_tiles(share)
+    assert tiles == 1 or tiles == 2 and 128 % (share - 128) == 0
+    packs = -(-2 * classes * (share - 128) // 128) if tiles == 2 else 0
     return call(
         functools.partial(weigh_kernel, fresh, classes),
         [*sources, inverse_noise, particles],
         [
-            ((tiles, lines, 128), F32),
+            (((2 * classes + packs) * pitch, 128), F32),
             ((classes, tiles * 128), F32),
             ((pairs, 4 * classes, twice), BF16),
         ],
-        [((lines, twice // 2), F32)],
+        [((2 * classes * pitch, twice // 2), F32)]
+        + [((2 * classes * pitch, 128), F32)] * (tiles - 1),
         flops=8 * classes * share * pairs * twice * 4,
     )
 
@@ -254,7 +264,8 @@
     classes = left_ref.shape[1] // 4
 
     def body(f):
-        place(out, f, times(left_ref[f], particles[f]), classes, 2 * pairs + SPARE)
+        outs = [out.at[tile] for tile in range(out.shape[0])]
+        place(outs, f, times(left_ref[f], particles[f]), classes, 2 * pairs + SPARE)
 
     loop(pairs, body, 8)
 
@@ -278,27 +289,32 @@
     return pl.ds(pl.multiple_of(lax.axis_index("rot") * ANG + base, 128), count)
 
 
-def score_kernel(own, other, energy_ref, prior_term, inv_hi, inv_lo, *refs):
+def score_kernel(particles, own, other, energy_ref, prior_term, inv_hi, inv_lo, *refs):
     weights, peaks = refs
     classes, share = energy_ref.shape
     tiles, lines, width = own.shape
     pitch = lines // (2 * classes)
     freqs = pitch - SPARE
     which = table_rows(0, ANG)
+    def unpacked(group):
+        first = other[rows(group * pitch, freqs), :]
+        if tiles == 1:
+            return first
+        width = particles - 128
+        bundle = 128 // width
+        packed = other[rows((2 * classes + group // bundle) * pitch, freqs), :]
+        back = (bundle - group % bundle) % bundle * width
+        return jnp.concatenate([first, pltpu.roll(packed, back, 1)], 1)
+
     def score(k, peak):
-        value = jnp.concatenate(
-            [
-                across(ref, rows((2 * k + part) * pitch, freqs))
-                for ref in (own, other)
-                for part in (0, 1)
-            ],
-            0,
-        )
+        near = [across(own, rows((2 * k + part) * pitch, freqs)) for part in range(2)]
+        far = [unpacked(2 * k + part) for part in range(2)]
+        value = jnp.concatenate(near + far, 0)
         high, low = split(value)
         inner = dot(inv_hi[which, :], high) + (
             dot(inv_hi[which, :], low) + dot(inv_lo[which, :], high)
         )
-        far = other[0, rows(2 * k * pitch + freqs, SPARE), :][:1]
+        far = other[rows(2 * k * pitch + freqs, SPARE), :][:1]
         energy = energy_ref[pl.ds(k, 1), :] + jnp.concatenate([far] * tiles, 1)
         scores = inner - 0.5 * energy + prior_term[...]
         weights[k] = scores
@@ -316,10 +332,10 @@
     peaks[...] = jnp.where(line == 0, peak, total)
 
 
-def scores(own, other, energy, prior_term, inv_hi, inv_lo):
+def scores(own, other, energy, prior_term, inv_hi, inv_lo, particles):
     classes, share = energy.shape
     return call(
-        score_kernel,
+        functools.partial(score_kernel, particles),
         [own, other, energy, prior_term, inv_hi, inv_lo],
         [((classes, ANG, share), F32), ((8, share), F32)],
         flops=6 * classes * share * ANG * ANG,
@@ -338,11 +354,10 @@
     out[...] = jnp.where(line == 0, top, total)
 
 
-def turn_kernel(weights, here, first, second, fwd_hi, fwd_lo, *refs):
+def turn_kernel(share, weights, here, first, second, fwd_hi, fwd_lo, *refs):
     rounded_ref, send, *evidence_ref, held = refs
     classes, _, lanes = weights.shape
-    share = send.shape[2]
-    pairs = send.shape[0] - 1
+    pairs = (held.shape[1] // (2 * classes) - SPARE) // 2
     top, total = merge(first[...], second[...])
     for ref in evidence_ref:
         ref[...] = (top + jnp.log(total))[:, :share]
@@ -350,7 +365,7 @@
     lane = lax.broadcasted_iota(jnp.int32, (1, lanes), 1)
     factor = jnp.where(lane < share, factor, 0.0)
     which = table_rows(0, ANG // 2)
-    line = lax.broadcasted_iota(jnp.int32, (4 * classes, share), 0)
+    line = lax.broadcasted_iota(jnp.int32, (4 * classes, 128), 0)
 
     def body(k, column):
         value = weights[k] * factor
@@ -361,13 +376,27 @@
         high = count.astype(BF16).astype(F32)
         return jnp.where(line == k, high, jnp.where(line == classes + k, count - high, column))
 
-    column = each(classes, body, jnp.zeros((4 * classes, share), F32))
-    send[pairs] = column.astype(BF16)
-
-    def rearrange(f):
-        send[f] = pick(held, f, classes, share)
-
-    loop(pairs, rearrange, 8)
+    column = each(classes, body, jnp.zeros((4 * classes, 128), F32))
+    send[send.shape[0] - 1] = column.astype(BF16)
+    bundle, width = bundles(pairs, share)
+
+    def rearrange(j):
+        packed = 0.0
+        for i in range(bundle):
+            value = pick(held, j * bundle + i, classes)
+            send[j * bundle + i] = value[:, :128].astype(BF16)
+            if width:
+                packed = packed + (pltpu.roll(value[:, 128:], i * width, 1) if i else value[:, 128:])
+        if width:
+            send[pairs + j] = packed.astype(BF16)
+
+    loop(pairs // bundle, rearrange, 1)
+
+
+def bundles(pairs, share):
+    if lane_tiles(share) == 1:
+        return min(8, pairs), 0
+    return min(128 // (share - 128), pairs), share - 128
 
 
 def spread(held, k, value):
@@ -380,23 +409,24 @@
             ]
 
 
-def pick(held, f, classes, share):
+def pick(held, f, classes):
     pitch = held.shape[1] // (2 * classes)
     parts = [
-        across(held, pl.ds(2 * f + part, 2 * classes, stride=pitch)).astype(BF16)
-        for part in range(2)
+        across(held, pl.ds(2 * f + part, 2 * classes, stride=pitch)) for part in range(2)
     ]
-    return jnp.concatenate(parts, 0)[:, :share]
+    return jnp.concatenate(parts, 0)
 
 
 def turn(weights, here, first, second, fwd_hi, fwd_lo, freqs, share, last):
     classes, _, lanes = weights.shape
+    bundle, width = bundles(freqs // 2, share)
+    entries = freqs // 2 + (freqs // 2 // bundle if width else 0) + 1
     return call(
-        turn_kernel,
+        functools.partial(turn_kernel, share),
         [weights, here, first, second, fwd_hi, fwd_lo],
         [
             ((classes, ANG, lanes), BF16),
-            ((freqs // 2 + 1, 4 * classes, share), BF16),
+            ((entries, 4 * classes, 128), BF16),
             *([((1, share), F32)] if last else []),
         ],
         [((lanes // 128, 2 * classes * (freqs + SPARE), 128), F32)],
@@ -417,7 +447,8 @@
     each(classes, body, 0)
 
     def accumulate(f):
-        take_in(image, f, dot(pick(held, f, classes, share), particles[f]), classes)
+        left = pick(held, f, classes).astype(BF16)[:, :share]
+        take_in(image, f, dot(left, particles[f]), classes)
 
     loop(pairs, accumulate, 8)
 
@@ -446,17 +477,26 @@
 
 def finish_kernel(image, mine, spectrum, particles, *refs):
     outs, held = refs[:-1], refs[-1]
-    pairs, _, twice = particles.shape
+    pairs, share, twice = particles.shape
     classes = spectrum.shape[1] // 4
     freqs, depth = 2 * pairs, twice // 2
     radii = depth // 2
     pitch = freqs + SPARE
-
-    def body(f):
-        take_in(held, f, dot(spectrum[f], particles[f]), classes)
-
-    loop(pairs, body, 8)
-    counts = (mine[pairs].astype(F32) + spectrum[pairs].astype(F32))[:, :depth]
+    bundle, width = bundles(pairs, share)
+
+    def body(j):
+        packed = spectrum[pairs + j].astype(F32) if width else None
+        for i in range(bundle):
+            f = j * bundle + i
+            left = spectrum[f]
+            if width:
+                rest = pltpu.roll(packed, 128 - i * width, 1) if i else packed
+                left = jnp.concatenate([left, rest.astype(BF16)], 1)
+            take_in(held, f, dot(left[:, :share], particles[f]), classes)
+
+    loop(pairs // bundle, body, 1)
+    end = spectrum.shape[0] - 1
+    counts = mine[end].astype(F32) + spectrum[end].astype(F32)
     counts = counts[:classes] + counts[classes : 2 * classes]
     lane = lax.broadcasted_iota(jnp.int32, (freqs, depth), 1)
     sign = jnp.where(lane < radii, -1.0, 1.0).astype(F32)
@@ -532,14 +572,16 @@
     (prior_term,) = call(
         prior_kernel, [prior_rot], [((ANG, lane_tiles(share) * 128), F32)], flops=1 << 26
     )
-    sources = [swap(first, "blk", blocks, i) for i in reversed(range(blocks))][::-1]
+    sources = [
+        swap(first if i else references, "blk", blocks, i ^ (blocks - 1)) for i in range(blocks)
+    ][::-1]
     other_images, own_images = prep(particles, permutation, share)
     for step in range(ITERS):
         last = step == ITERS - 1
         message, energy, left = weigh(sources, inverse_noise, other_images, step == 0)
         message = swap(message, "rot", groups, 1)
         own = correlate(left, own_images)
-        weights, here = scores(own, message, energy, prior_term, inv_hi, inv_lo)
+        weights, here = scores(own, message, energy, prior_term, inv_hi, inv_lo, share)
         first = here
         for bit in bits(sides):
             second = swap(first, "cls", sides, bit)

time: 50.2 us -> 49.9 us (level)
  waiting for transfers between devices: 17.2 us -> 15.7 us
  Pallas kernels: 13.4 us -> 14.6 us
  local copies, waits for them, and re-layouts: 0.68 us -> 0.05 us
  starting transfers between devices: 17.9 us -> 18.5 us
    ppermute x15, waiting for transfers between devices: 17.2 us -> 15.7 us  [swap(): return lax.ppermute(value, axis, [(i, i ^ bit) for i in range(size)])]
    pallas_call x16, Pallas kernels: 13.4 us -> 14.6 us  [call(): pl.pallas_call(kernel, out_shape=[jax.ShapeDtypeStruct(*x) for x in outs]...]
    ppermute x15, starting transfers between devices: 17.9 us -> 18.5 us  [swap(): return lax.ppermute(value, axis, [(i, i ^ bit) for i in range(size)])]
    unnamed x16, local copies, waits for them, and re-layouts: 0.68 us -> 0.05 us
where the time goes in v9:
time: 49.9 us; the launch traced here: 49.7 us
  starting transfers between devices  18.5 us (37%)
  waiting for transfers between devices  15.7 us (31%)
  Pallas kernels  14.6 us (29%)
  between operations  0.8 us (2%)
    ppermute x15, starting transfers between devices, swap(): return lax.ppermute(value, axis, [(i, i ^ bit) for i in range(size)])  18.5 us
    ppermute x15, waiting for transfers between devices, swap(): return lax.ppermute(value, axis, [(i, i ^ bit) for i in range(size)])  15.7 us
    pallas_call x16, Pallas kernels, call(): pl.pallas_call(kernel, out_shape=[jax.ShapeDtypeStruct(*x) for x in outs]...  14.6 us
  transfers between devices with their start and end apart: 15, of which 11 were waited for; matrix products, arithmetic and copies ran while one was open for 0% of the time, Pallas kernels for 12%

profile of v9, /device:TPU:0, one launch (start us, length us, event | category | flops | bytes accessed | tf_op | source)
XLA Modules:
  0.0 49.7 jit_solution(16140152528397693357)
XLA Ops:
  0.6 5.1 %collective-permute-start.2 = (bf16[1,64,128]{2,1,0:T(8,128)(2,1)}, bf16[1,64,128]{2,1,0:T(8,128)(2,1)S(1)}, u32[]{:S(2)}, u32[]{:S(2)}) collective-permute-start(bf16[1,64,128]{2,1,0:T(8,128)(2,1)} %refs_0_), channel_id=1, source_target_pairs={{0,12},{4,8},{8,4},{12,0},{1,13},{5,9},{9,5},{13,1},{2,14},{6,10},... | collective-permute-start | bytes 49160 | tf_op jit(solution)/shard_map/ppermute | solution.py:551
  5.9 1.0 %collective-permute-start = (bf16[1,64,128]{2,1,0:T(8,128)(2,1)S(1)}, bf16[1,64,128]{2,1,0:T(8,128)(2,1)S(1)}, u32[]{:S(2)}, u32[]{:S(2)}) collective-permute-start(bf16[1,64,128]{2,1,0:T(8,128)(2,1)S(1)} %copy-done.4), channel_id=1, source_target_pairs={{0,4},{4,0},{8,12},{12,8},{1,5},{5,1},{9,13},{13,9},{2,6},{6,2},{1... | collective-permute-start | bytes 49160 | tf_op jit(solution)/shard_map/ppermute | solution.py:551
  7.0 1.4 %shard_map.96 = (bf16[32,144,256]{2,1,0:T(8,128)(2,1)S(1)}, bf16[32,144,256]{2,1,0:T(8,128)(2,1)S(1)}) custom-call(bf16[288,64,128]{2,1,0:T(8,128)(2,1)S(1)} %copy-done.7, bf16[256,256]{1,0:T(8,128)(2,1)S(1)} %shard_map.95.permutation_ref), custom_call_target="tpu_custom_call" | custom-call | flops 2147483648 | bytes 9568256 | tf_op jit(solution)/shard_map/pallas_call | solution.py:92
  8.4 2.2 %collective-permute-done.1.refs_2_ = bf16[1,64,128]{2,1,0:T(8,128)(2,1)S(1)} collective-permute-done((bf16[1,64,128]{2,1,0:T(8,128)(2,1)S(1)}, bf16[1,64,128]{2,1,0:T(8,128)(2,1)S(1)}, u32[]{:S(2)}, u32[]{:S(2)}) %collective-permute-start.1) | collective-permute-done | bytes 16416 | tf_op jit(solution)/shard_map/ppermute | solution.py:551
  10.6 1.4 %shard_map.97 = (f32[648,128]{1,0:T(8,128)S(1)}, f32[4,256]{1,0:T(4,128)S(1)}, bf16[32,16,256]{2,1,0:T(8,128)(2,1)S(1)}) custom-call(bf16[1,64,128]{2,1,0:T(8,128)(2,1)S(1)} %copy-done.4, bf16[1,64,128]{2,1,0:T(8,128)(2,1)S(1)} %collective-permute-done.refs_1_, bf16[1,64,128]{2,1,0:T(8,128)(2,1)S(1)} %collective-permute-done.1.refs_2_, ...), custom_call_target="tpu_custom_call" | custom-call | flops 150994944 | bytes 3637248 | tf_op jit(solution)/shard_map/pallas_call | solution.py:92
  12.3 1.1 %shard_map.98.own = f32[2,576,128]{2,1,0:T(8,128)S(1)} custom-call(bf16[32,16,256]{2,1,0:T(8,128)(2,1)S(1)} %get-tuple-element.30.left_ref, bf16[32,144,256]{2,1,0:T(8,128)(2,1)S(1)} %get-tuple-element.31.particles), custom_call_target="tpu_custom_call" | custom-call | flops 301989888 | bytes 3211264 | tf_op jit(solution)/shard_map/pallas_call | solution.py:92
  13.4 0.3 collective-permute-done.3.other
  13.7 0.8 %shard_map.100 = (f32[4,256,256]{2,1,0:T(8,128)S(1)}, f32[8,256]{1,0:T(8,128)S(1)}) custom-call(f32[2,576,128]{2,1,0:T(8,128)S(1)} %shard_map.98.own, f32[648,128]{1,0:T(8,128)S(1)} %collective-permute-done.3.other, f32[4,256]{1,0:T(4,128)S(1)} %get-tuple-element.33.energy_ref, f32[256,256]{1,0:T(8,128)S(1)} %shard_map.99.prior_term, ...), custom_call_target="tpu_custom_call" | custom-call | flops 402653184 | bytes 2793472 | tf_op jit(solution)/shard_map/pallas_call | solution.py:92
  14.5 1.6 %collective-permute-start.4 = (f32[8,256]{1,0:T(8,128)S(1)}, f32[8,256]{1,0:T(8,128)S(1)}, u32[]{:S(2)}, u32[]{:S(2)}) collective-permute-start(f32[8,256]{1,0:T(8,128)S(1)} %get-tuple-element.35.here.first), channel_id=1, source_target_pairs={{0,2},{2,0},{1,3},{3,1},{4,6},{6,4},{5,7},{7,5},{8,10},{10,8},{9,1... | collective-permute-start | bytes 24584 | tf_op jit(solution)/shard_map/ppermute | solution.py:551
  16.1 2.2 %collective-permute-done.4.second = f32[8,256]{1,0:T(8,128)S(1)} collective-permute-done((f32[8,256]{1,0:T(8,128)S(1)}, f32[8,256]{1,0:T(8,128)S(1)}, u32[]{:S(2)}, u32[]{:S(2)}) %collective-permute-start.4) | collective-permute-done | bytes 8224 | tf_op jit(solution)/shard_map/ppermute | solution.py:551
  18.3 0.7 %shard_map.101 = (bf16[4,256,256]{2,1,0:T(8,128)(2,1)S(1)}, bf16[37,16,128]{2,1,0:T(8,128)(2,1)S(1)}) custom-call(f32[4,256,256]{2,1,0:T(8,128)S(1)} %get-tuple-element.34.weights, f32[8,256]{1,0:T(8,128)S(1)} %get-tuple-element.35.here.first, f32[8,256]{1,0:T(8,128)S(1)} %get-tuple-element.35.here.first, f32[8,256]{1,0:T(8,128)S(1)} %collective-permute-done.4.second, ...), custom_call_target="tpu_custom_call" | custom-call | flops 268435456 | bytes 2887680 | tf_op jit(solution)/shard_map/pallas_call | solution.py:92
  19.0 1.1 %shard_map.102.image = f32[576,128]{1,0:T(8,128)S(1)} custom-call(bf16[4,256,256]{2,1,0:T(8,128)(2,1)S(1)} %get-tuple-element.36.rounded_ref, bf16[512,256]{1,0:T(8,128)(2,1)S(1)} %copy-done.1, bf16[512,256]{1,0:T(8,128)(2,1)S(1)} %copy-done, bf16[32,144,256]{2,1,0:T(8,128)(2,1)S(1)} %get-tuple-element.31.particles), custom_call_target="tpu_custom_call" | custom-call | flops 268435456 | bytes 4292608 | tf_op jit(solution)/shard_map/pallas_call | solution.py:92
  20.4 1.1 %shard_map.103.refs_0_ = bf16[272,128]{1,0:T(8,128)(2,1)S(1)} custom-call(f32[576,128]{1,0:T(8,128)S(1)} %shard_map.102.image, bf16[37,16,128]{2,1,0:T(8,128)(2,1)S(1)} %get-tuple-element.37.mine, bf16[37,16,128]{2,1,0:T(8,128)(2,1)S(1)} %collective-permute-done.5.spectrum, bf16[32,144,256]{2,1,0:T(8,128)(2,1)S(1)} %get-tuple-element.29.refs_5_.particles), custom_call_target="tpu_custom_call" | custom-call | flops 310378496 | bytes 3321856 | tf_op jit(solution)/shard_map/pallas_call | solution.py:92
  21.5 1.5 %collective-permute-start.8 = (bf16[272,128]{1,0:T(8,128)(2,1)S(1)}, bf16[272,128]{1,0:T(8,128)(2,1)S(1)}, u32[]{:S(2)}, u32[]{:S(2)}) collective-permute-start(bf16[272,128]{1,0:T(8,128)(2,1)S(1)} %shard_map.103.refs_0_), channel_id=1, source_target_pairs={{0,12},{4,8},{8,4},{12,0},{1,13},{5,9},{9,5},{13,1},{2,14},{6,10},... | collective-permute-start | bytes 208904 | tf_op jit(solution)/shard_map/ppermute | solution.py:551
  23.0 0.6 %collective-permute-start.7 = (bf16[272,128]{1,0:T(8,128)(2,1)S(1)}, bf16[272,128]{1,0:T(8,128)(2,1)S(1)}, u32[]{:S(2)}, u32[]{:S(2)}) collective-permute-start(bf16[272,128]{1,0:T(8,128)(2,1)S(1)} %shard_map.103.refs_0_), channel_id=1, source_target_pairs={{0,8},{4,12},{8,0},{12,4},{1,9},{5,13},{9,1},{13,5},{2,10},{6,14},... | collective-permute-start | bytes 208904 | tf_op jit(solution)/shard_map/ppermute | solution.py:551
  23.6 2.3 %collective-permute-start.6 = (bf16[272,128]{1,0:T(8,128)(2,1)S(1)}, bf16[272,128]{1,0:T(8,128)(2,1)S(1)}, u32[]{:S(2)}, u32[]{:S(2)}) collective-permute-start(bf16[272,128]{1,0:T(8,128)(2,1)S(1)} %shard_map.103.refs_0_), channel_id=1, source_target_pairs={{0,4},{4,0},{8,12},{12,8},{1,5},{5,1},{9,13},{13,9},{2,6},{6,2},{1... | collective-permute-start | bytes 208904 | tf_op jit(solution)/shard_map/ppermute | solution.py:551
  25.9 2.5 %collective-permute-done.8.refs_3_ = bf16[272,128]{1,0:T(8,128)(2,1)S(1)} collective-permute-done((bf16[272,128]{1,0:T(8,128)(2,1)S(1)}, bf16[272,128]{1,0:T(8,128)(2,1)S(1)}, u32[]{:S(2)}, u32[]{:S(2)}) %collective-permute-start.8) | collective-permute-done | bytes 69664 | tf_op jit(solution)/shard_map/ppermute | solution.py:551
  28.4 2.2 %collective-permute-done.7.refs_2_ = bf16[272,128]{1,0:T(8,128)(2,1)S(1)} collective-permute-done((bf16[272,128]{1,0:T(8,128)(2,1)S(1)}, bf16[272,128]{1,0:T(8,128)(2,1)S(1)}, u32[]{:S(2)}, u32[]{:S(2)}) %collective-permute-start.7) | collective-permute-done | bytes 69664 | tf_op jit(solution)/shard_map/ppermute | solution.py:551
  30.6 1.4 %shard_map.104 = (f32[648,128]{1,0:T(8,128)S(1)}, f32[4,256]{1,0:T(4,128)S(1)}, bf16[32,16,256]{2,1,0:T(8,128)(2,1)S(1)}) custom-call(bf16[272,128]{1,0:T(8,128)(2,1)S(1)} %shard_map.103.refs_0_, bf16[272,128]{1,0:T(8,128)(2,1)S(1)} %collective-permute-done.6.refs_1_, bf16[272,128]{1,0:T(8,128)(2,1)S(1)} %collective-permute-done.7.refs_2_, ...), custom_call_target="tpu_custom_call" | custom-call | flops 150994944 | bytes 3850240 | tf_op jit(solution)/shard_map/pallas_call | solution.py:92
  32.1 1.1 %shard_map.105.own = f32[2,576,128]{2,1,0:T(8,128)S(1)} custom-call(bf16[32,16,256]{2,1,0:T(8,128)(2,1)S(1)} %get-tuple-element.38.left_ref, bf16[32,144,256]{2,1,0:T(8,128)(2,1)S(1)} %get-tuple-element.31.particles), custom_call_target="tpu_custom_call" | custom-call | flops 301989888 | bytes 3211264 | tf_op jit(solution)/shard_map/pallas_call | solution.py:92
  33.2 0.5 %collective-permute-done.9.other = f32[648,128]{1,0:T(8,128)S(1)} collective-permute-done((f32[648,128]{1,0:T(8,128)S(1)}, f32[648,128]{1,0:T(8,128)S(1)}, u32[]{:S(2)}, u32[]{:S(2)}) %collective-permute-start.9) | collective-permute-done | bytes 331808 | tf_op jit(solution)/shard_map/ppermute | solution.py:551
  33.8 0.8 %shard_map.106 = (f32[4,256,256]{2,1,0:T(8,128)S(1)}, f32[8,256]{1,0:T(8,128)S(1)}) custom-call(f32[2,576,128]{2,1,0:T(8,128)S(1)} %shard_map.105.own, f32[648,128]{1,0:T(8,128)S(1)} %collective-permute-done.9.other, f32[4,256]{1,0:T(4,128)S(1)} %get-tuple-element.40.energy_ref, f32[256,256]{1,0:T(8,128)S(1)} %shard_map.99.prior_term, ...), custom_call_target="tpu_custom_call" | custom-call | flops 402653184 | bytes 2793472 | tf_op jit(solution)/shard_map/pallas_call | solution.py:92
  34.6 1.6 %collective-permute-start.10 = (f32[8,256]{1,0:T(8,128)S(1)}, f32[8,256]{1,0:T(8,128)S(1)}, u32[]{:S(2)}, u32[]{:S(2)}) collective-permute-start(f32[8,256]{1,0:T(8,128)S(1)} %get-tuple-element.42.here.first), channel_id=1, source_target_pairs={{0,2},{2,0},{1,3},{3,1},{4,6},{6,4},{5,7},{7,5},{8,10},{10,8},{9,1... | collective-permute-start | bytes 24584 | tf_op jit(solution)/shard_map/ppermute | solution.py:551
  36.1 2.2 %collective-permute-done.10.second = f32[8,256]{1,0:T(8,128)S(1)} collective-permute-done((f32[8,256]{1,0:T(8,128)S(1)}, f32[8,256]{1,0:T(8,128)S(1)}, u32[]{:S(2)}, u32[]{:S(2)}) %collective-permute-start.10) | collective-permute-done | bytes 8224 | tf_op jit(solution)/shard_map/ppermute | solution.py:551
  38.3 0.7 %shard_map.107 = (bf16[4,256,256]{2,1,0:T(8,128)(2,1)S(1)}, bf16[37,16,128]{2,1,0:T(8,128)(2,1)S(1)}, f32[1,144]{1,0:T(1,128)S(1)}) custom-call(f32[4,256,256]{2,1,0:T(8,128)S(1)} %get-tuple-element.41.weights, f32[8,256]{1,0:T(8,128)S(1)} %get-tuple-element.42.here.first, f32[8,256]{1,0:T(8,128)S(1)} %get-tuple-element.42.here.first, ...), custom_call_target="tpu_custom_call" | custom-call | flops 268435456 | bytes 2904064 | tf_op jit(solution)/shard_map/pallas_call | solution.py:92
  39.1 1.1 %shard_map.108.image = f32[576,128]{1,0:T(8,128)S(1)} custom-call(bf16[4,256,256]{2,1,0:T(8,128)(2,1)S(1)} %get-tuple-element.43.rounded_ref, bf16[512,256]{1,0:T(8,128)(2,1)S(1)} %copy-done.1, bf16[512,256]{1,0:T(8,128)(2,1)S(1)} %copy-done, bf16[32,144,256]{2,1,0:T(8,128)(2,1)S(1)} %get-tuple-element.31.particles), custom_call_target="tpu_custom_call" | custom-call | flops 268435456 | bytes 4292608 | tf_op jit(solution)/shard_map/pallas_call | solution.py:92
  40.4 1.1 %shard_map.109 = (f32[72,128]{1,0:T(8,128)S(1)}, f32[72,128]{1,0:T(8,128)S(1)}, f32[72,128]{1,0:T(8,128)S(1)}, f32[72,128]{1,0:T(8,128)S(1)}) custom-call(f32[576,128]{1,0:T(8,128)S(1)} %shard_map.108.image, bf16[37,16,128]{2,1,0:T(8,128)(2,1)S(1)} %get-tuple-element.44.mine, bf16[37,16,128]{2,1,0:T(8,128)(2,1)S(1)} %collective-permute-done.11.spectrum, ...), custom_call_target="tpu_custom_call" | custom-call | flops 310378496 | bytes 3416064 | tf_op jit(solution)/shard_map/pallas_call | solution.py:92
  41.5 2.7 %collective-permute-start.12 = (f32[72,128]{1,0:T(8,128)S(1)}, f32[72,128]{1,0:T(8,128)S(1)}, u32[]{:S(2)}, u32[]{:S(2)}) collective-permute-start(f32[72,128]{1,0:T(8,128)S(1)} %get-tuple-element.45), channel_id=1, source_target_pairs={{0,12},{4,8},{8,4},{12,0},{1,13},{5,9},{9,5},{13,1},{2,14},{6,10},... | collective-permute-start | bytes 110600 | tf_op jit(solution)/shard_map/ppermute | solution.py:551
  44.2 1.8 %collective-permute-start.14 = (f32[72,128]{1,0:T(8,128)S(1)}, f32[72,128]{1,0:T(8,128)S(1)}, u32[]{:S(2)}, u32[]{:S(2)}) collective-permute-start(f32[72,128]{1,0:T(8,128)S(1)} %get-tuple-element.47), channel_id=1, source_target_pairs={{0,4},{4,0},{8,12},{12,8},{1,5},{5,1},{9,13},{13,9},{2,6},{6,2},{1... | collective-permute-start | bytes 110600 | tf_op jit(solution)/shard_map/ppermute | solution.py:551
  46.0 1.5 %collective-permute-done.12.refs_0_ = f32[72,128]{1,0:T(8,128)S(1)} collective-permute-done((f32[72,128]{1,0:T(8,128)S(1)}, f32[72,128]{1,0:T(8,128)S(1)}, u32[]{:S(2)}, u32[]{:S(2)}) %collective-permute-start.12) | collective-permute-done | bytes 36896 | tf_op jit(solution)/shard_map/ppermute | solution.py:551
  47.5 1.6 %collective-permute-done.13.refs_1_ = f32[72,128]{1,0:T(8,128)S(1)} collective-permute-done((f32[72,128]{1,0:T(8,128)S(1)}, f32[72,128]{1,0:T(8,128)S(1)}, u32[]{:S(2)}, u32[]{:S(2)}) %collective-permute-start.13) | collective-permute-done | bytes 36896 | tf_op jit(solution)/shard_map/ppermute | solution.py:551
  49.1 0.6 %shard_map.110 = (f32[1,64,128]{2,1,0:T(8,128)}, f32[1,144]{1,0:T(1,128)}) custom-call(f32[72,128]{1,0:T(8,128)S(1)} %collective-permute-done.12.refs_0_, f32[72,128]{1,0:T(8,128)S(1)} %collective-permute-done.13.refs_1_, f32[72,128]{1,0:T(8,128)S(1)} %collective-permute-done.14.refs_2_, f32[72,128]{1,0:T(8,128)S(1)} %get-tuple-element.48.refs_3_, ...), custom_call_target="tpu_custom_call" | custom-call | bytes 229376 | tf_op jit(solution)/shard_map/pallas_call | solution.py:92
  (30 shorter events, 1.2 us)
Async XLA Ops:
  0.6 5.2 %copy-start.4 = (bf16[1,64,128]{2,1,0:T(8,128)(2,1)S(1)}, bf16[1,64,128]{2,1,0:T(8,128)(2,1)}, u32[]{:S(2)}) copy-start(bf16[1,64,128]{2,1,0:T(8,128)(2,1)} %refs_0_) | copy-start | bytes 49156
  0.6 6.3 %copy-start.7 = (bf16[288,64,128]{2,1,0:T(8,128)(2,1)S(1)}, bf16[288,64,128]{2,1,0:T(8,128)(2,1)}, u32[]{:S(2)}) copy-start(bf16[288,64,128]{2,1,0:T(8,128)(2,1)} %particles_ref.1) | copy-start | bytes 14155780
  0.6 7.7 %collective-permute-start.2 = (bf16[1,64,128]{2,1,0:T(8,128)(2,1)}, bf16[1,64,128]{2,1,0:T(8,128)(2,1)S(1)}, u32[]{:S(2)}, u32[]{:S(2)}) collective-permute-start(bf16[1,64,128]{2,1,0:T(8,128)(2,1)} %refs_0_), channel_id=1, source_target_pairs={{0,12},{4,8},{8,4},{12,0},{1,13},{5,9},{9,5},{13,1},{2,14},{6,10},... | collective-permute-start | bytes 49160 | tf_op jit(solution)/shard_map/ppermute | solution.py:551
  5.8 4.7 %copy-start.6 = (f32[64]{0:T(128)S(1)}, f32[64]{0:T(128)}, u32[]{:S(2)}) copy-start(f32[64]{0:T(128)} %param.10) | copy-start | bytes 772
  5.8 4.7 %collective-permute-start.1 = (bf16[1,64,128]{2,1,0:T(8,128)(2,1)S(1)}, bf16[1,64,128]{2,1,0:T(8,128)(2,1)S(1)}, u32[]{:S(2)}, u32[]{:S(2)}) collective-permute-start(bf16[1,64,128]{2,1,0:T(8,128)(2,1)S(1)} %copy-done.4), channel_id=1, source_target_pairs={{0,8},{4,12},{8,0},{12,4},{1,9},{5,13},{9,1},{13,5},{2,10},{6,14},... | collective-permute-start | bytes 49160 | tf_op jit(solution)/shard_map/ppermute | solution.py:551
  5.9 4.6 %collective-permute-start = (bf16[1,64,128]{2,1,0:T(8,128)(2,1)S(1)}, bf16[1,64,128]{2,1,0:T(8,128)(2,1)S(1)}, u32[]{:S(2)}, u32[]{:S(2)}) collective-permute-start(bf16[1,64,128]{2,1,0:T(8,128)(2,1)S(1)} %copy-done.4), channel_id=1, source_target_pairs={{0,4},{4,0},{8,12},{12,8},{1,5},{5,1},{9,13},{13,9},{2,6},{6,2},{1... | collective-permute-start | bytes 49160 | tf_op jit(solution)/shard_map/ppermute | solution.py:551
  8.4 3.7 %copy-start.5 = (s32[288]{0:T(512)S(1)}, s32[288]{0:T(512)}, u32[]{:S(2)}) copy-start(s32[288]{0:T(512)} %prior_ref.1) | copy-start | bytes 3460
  10.5 3.1 %copy-start.2 = (bf16[512,256]{1,0:T(8,128)(2,1)S(1)}, bf16[512,256]{1,0:T(8,128)(2,1)}, u32[]{:S(2)}) copy-start(bf16[512,256]{1,0:T(8,128)(2,1)} %constant.9.clone.inv_lo) | copy-start | bytes 786436
  10.6 3.1 %copy-start.3 = (bf16[512,256]{1,0:T(8,128)(2,1)S(1)}, bf16[512,256]{1,0:T(8,128)(2,1)}, u32[]{:S(2)}) copy-start(bf16[512,256]{1,0:T(8,128)(2,1)} %constant.8.clone.inv_hi) | copy-start | bytes 786436
  12.0 1.7 %collective-permute-start.3 = (f32[648,128]{1,0:T(8,128)S(1)}, f32[648,128]{1,0:T(8,128)S(1)}, u32[]{:S(2)}, u32[]{:S(2)}) collective-permute-start(f32[648,128]{1,0:T(8,128)S(1)} %get-tuple-element.32), channel_id=1, source_target_pairs={{0,1},{1,0},{2,3},{3,2},{4,5},{5,4},{6,7},{7,6},{8,9},{9,8},{10,11... | collective-permute-start | bytes 995336 | tf_op jit(solution)/shard_map/ppermute | solution.py:551
  12.3 6.0 %copy-start = (bf16[512,256]{1,0:T(8,128)(2,1)S(1)}, bf16[512,256]{1,0:T(8,128)(2,1)}, u32[]{:S(2)}) copy-start(bf16[512,256]{1,0:T(8,128)(2,1)} %constant.11.clone.fwd_lo) | copy-start | bytes 786436
  12.3 6.0 %copy-start.1 = (bf16[512,256]{1,0:T(8,128)(2,1)S(1)}, bf16[512,256]{1,0:T(8,128)(2,1)}, u32[]{:S(2)}) copy-start(bf16[512,256]{1,0:T(8,128)(2,1)} %constant.10.clone.fwd_hi) | copy-start | bytes 786436
  14.5 3.7 %collective-permute-start.4 = (f32[8,256]{1,0:T(8,128)S(1)}, f32[8,256]{1,0:T(8,128)S(1)}, u32[]{:S(2)}, u32[]{:S(2)}) collective-permute-start(f32[8,256]{1,0:T(8,128)S(1)} %get-tuple-element.35.here.first), channel_id=1, source_target_pairs={{0,2},{2,0},{1,3},{3,1},{4,6},{6,4},{5,7},{7,5},{8,10},{10,8},{9,1... | collective-permute-start | bytes 24584 | tf_op jit(solution)/shard_map/ppermute | solution.py:551
  19.0 1.4 %collective-permute-start.5 = (bf16[37,16,128]{2,1,0:T(8,128)(2,1)S(1)}, bf16[37,16,128]{2,1,0:T(8,128)(2,1)S(1)}, u32[]{:S(2)}, u32[]{:S(2)}) collective-permute-start(bf16[37,16,128]{2,1,0:T(8,128)(2,1)S(1)} %get-tuple-element.37.mine), channel_id=1, source_target_pairs={{0,1},{1,0},{2,3},{3,2},{4,5},{5,4},{6,7},{7,6},{8,9},{9,8},{10,11... | collective-permute-start | bytes 454664 | tf_op jit(solution)/shard_map/ppermute | solution.py:551
  21.5 6.9 %collective-permute-start.8 = (bf16[272,128]{1,0:T(8,128)(2,1)S(1)}, bf16[272,128]{1,0:T(8,128)(2,1)S(1)}, u32[]{:S(2)}, u32[]{:S(2)}) collective-permute-start(bf16[272,128]{1,0:T(8,128)(2,1)S(1)} %shard_map.103.refs_0_), channel_id=1, source_target_pairs={{0,12},{4,8},{8,4},{12,0},{1,13},{5,9},{9,5},{13,1},{2,14},{6,10},... | collective-permute-start | bytes 208904 | tf_op jit(solution)/shard_map/ppermute | solution.py:551
  23.0 7.6 %collective-permute-start.7 = (bf16[272,128]{1,0:T(8,128)(2,1)S(1)}, bf16[272,128]{1,0:T(8,128)(2,1)S(1)}, u32[]{:S(2)}, u32[]{:S(2)}) collective-permute-start(bf16[272,128]{1,0:T(8,128)(2,1)S(1)} %shard_map.103.refs_0_), channel_id=1, source_target_pairs={{0,8},{4,12},{8,0},{12,4},{1,9},{5,13},{9,1},{13,5},{2,10},{6,14},... | collective-permute-start | bytes 208904 | tf_op jit(solution)/shard_map/ppermute | solution.py:551
  23.6 7.0 %collective-permute-start.6 = (bf16[272,128]{1,0:T(8,128)(2,1)S(1)}, bf16[272,128]{1,0:T(8,128)(2,1)S(1)}, u32[]{:S(2)}, u32[]{:S(2)}) collective-permute-start(bf16[272,128]{1,0:T(8,128)(2,1)S(1)} %shard_map.103.refs_0_), channel_id=1, source_target_pairs={{0,4},{4,0},{8,12},{12,8},{1,5},{5,1},{9,13},{13,9},{2,6},{6,2},{1... | collective-permute-start | bytes 208904 | tf_op jit(solution)/shard_map/ppermute | solution.py:551
  32.1 1.7 %collective-permute-start.9 = (f32[648,128]{1,0:T(8,128)S(1)}, f32[648,128]{1,0:T(8,128)S(1)}, u32[]{:S(2)}, u32[]{:S(2)}) collective-permute-start(f32[648,128]{1,0:T(8,128)S(1)} %get-tuple-element.39), channel_id=1, source_target_pairs={{0,1},{1,0},{2,3},{3,2},{4,5},{5,4},{6,7},{7,6},{8,9},{9,8},{10,11... | collective-permute-start | bytes 995336 | tf_op jit(solution)/shard_map/ppermute | solution.py:551
  34.6 3.7 %collective-permute-start.10 = (f32[8,256]{1,0:T(8,128)S(1)}, f32[8,256]{1,0:T(8,128)S(1)}, u32[]{:S(2)}, u32[]{:S(2)}) collective-permute-start(f32[8,256]{1,0:T(8,128)S(1)} %get-tuple-element.42.here.first), channel_id=1, source_target_pairs={{0,2},{2,0},{1,3},{3,1},{4,6},{6,4},{5,7},{7,5},{8,10},{10,8},{9,1... | collective-permute-start | bytes 24584 | tf_op jit(solution)/shard_map/ppermute | solution.py:551
  39.0 1.4 %collective-permute-start.11 = (bf16[37,16,128]{2,1,0:T(8,128)(2,1)S(1)}, bf16[37,16,128]{2,1,0:T(8,128)(2,1)S(1)}, u32[]{:S(2)}, u32[]{:S(2)}) collective-permute-start(bf16[37,16,128]{2,1,0:T(8,128)(2,1)S(1)} %get-tuple-element.44.mine), channel_id=1, source_target_pairs={{0,1},{1,0},{2,3},{3,2},{4,5},{5,4},{6,7},{7,6},{8,9},{9,8},{10,11... | collective-permute-start | bytes 454664 | tf_op jit(solution)/shard_map/ppermute | solution.py:551
  41.5 5.9 %collective-permute-start.12 = (f32[72,128]{1,0:T(8,128)S(1)}, f32[72,128]{1,0:T(8,128)S(1)}, u32[]{:S(2)}, u32[]{:S(2)}) collective-permute-start(f32[72,128]{1,0:T(8,128)S(1)} %get-tuple-element.45), channel_id=1, source_target_pairs={{0,12},{4,8},{8,4},{12,0},{1,13},{5,9},{9,5},{13,1},{2,14},{6,10},... | collective-permute-start | bytes 110600 | tf_op jit(solution)/shard_map/ppermute | solution.py:551
  44.2 4.9 %collective-permute-start.13 = (f32[72,128]{1,0:T(8,128)S(1)}, f32[72,128]{1,0:T(8,128)S(1)}, u32[]{:S(2)}, u32[]{:S(2)}) collective-permute-start(f32[72,128]{1,0:T(8,128)S(1)} %get-tuple-element.46), channel_id=1, source_target_pairs={{0,8},{4,12},{8,0},{12,4},{1,9},{5,13},{9,1},{13,5},{2,10},{6,14},... | collective-permute-start | bytes 110600 | tf_op jit(solution)/shard_map/ppermute | solution.py:551
  44.2 4.9 %collective-permute-start.14 = (f32[72,128]{1,0:T(8,128)S(1)}, f32[72,128]{1,0:T(8,128)S(1)}, u32[]{:S(2)}, u32[]{:S(2)}) collective-permute-start(f32[72,128]{1,0:T(8,128)S(1)} %get-tuple-element.47), channel_id=1, source_target_pairs={{0,4},{4,0},{8,12},{12,8},{1,5},{5,1},{9,13},{13,9},{2,6},{6,2},{1... | collective-permute-start | bytes 110600 | tf_op jit(solution)/shard_map/ppermute | solution.py:551

commit v10 on v9

--- a/solution.py
+++ b/solution.py
@@ -208,7 +208,7 @@
         left_ref[f] = left
         place([out, *rest], f, times(left, particles[f]), classes, pitch)
 
-    loop(pairs, correlate, 8)
+    loop(pairs, correlate, 32)
     for ref in rest:
         width = share - 128
         for pack in range(-(-2 * classes * width // 128)):
@@ -267,7 +267,7 @@
         outs = [out.at[tile] for tile in range(out.shape[0])]
         place(outs, f, times(left_ref[f], particles[f]), classes, 2 * pairs + SPARE)
 
-    loop(pairs, body, 8)
+    loop(pairs, body, 32)
 
 
 def correlate(left, particles):
@@ -365,7 +365,7 @@
     lane = lax.broadcasted_iota(jnp.int32, (1, lanes), 1)
     factor = jnp.where(lane < share, factor, 0.0)
     which = table_rows(0, ANG // 2)
-    line = lax.broadcasted_iota(jnp.int32, (4 * classes, 128), 0)
+    line = lax.broadcasted_iota(jnp.int32, (4 * classes, share), 0)
 
     def body(k, column):
         value = weights[k] * factor
@@ -376,27 +376,13 @@
         high = count.astype(BF16).astype(F32)
         return jnp.where(line == k, high, jnp.where(line == classes + k, count - high, column))
 
-    column = each(classes, body, jnp.zeros((4 * classes, 128), F32))
-    send[send.shape[0] - 1] = column.astype(BF16)
-    bundle, width = bundles(pairs, share)
-
-    def rearrange(j):
-        packed = 0.0
-        for i in range(bundle):
-            value = pick(held, j * bundle + i, classes)
-            send[j * bundle + i] = value[:, :128].astype(BF16)
-            if width:
-                packed = packed + (pltpu.roll(value[:, 128:], i * width, 1) if i else value[:, 128:])
-        if width:
-            send[pairs + j] = packed.astype(BF16)
-
-    loop(pairs // bundle, rearrange, 1)
-
-
-def bundles(pairs, share):
-    if lane_tiles(share) == 1:
-        return min(8, pairs), 0
-    return min(128 // (share - 128), pairs), share - 128
+    column = each(classes, body, jnp.zeros((4 * classes, share), F32))
+    send[pairs] = column.astype(BF16)
+
+    def rearrange(f):
+        send[f] = pick(held, f, classes, share)
+
+    loop(pairs, rearrange, 32)
 
 
 def spread(held, k, value):
@@ -409,24 +395,23 @@
             ]
 
 
-def pick(held, f, classes):
+def pick(held, f, classes, share):
     pitch = held.shape[1] // (2 * classes)
     parts = [
-        across(held, pl.ds(2 * f + part, 2 * classes, stride=pitch)) for part in range(2)
+        across(held, pl.ds(2 * f + part, 2 * classes, stride=pitch)).astype(BF16)
+        for part in range(2)
     ]
-    return jnp.concatenate(parts, 0)
+    return jnp.concatenate(parts, 0)[:, :share]
 
 
 def turn(weights, here, first, second, fwd_hi, fwd_lo, freqs, share, last):
     classes, _, lanes = weights.shape
-    bundle, width = bundles(freqs // 2, share)
-    entries = freqs // 2 + (freqs // 2 // bundle if width else 0) + 1
     return call(
         functools.partial(turn_kernel, share),
         [weights, here, first, second, fwd_hi, fwd_lo],
         [
             ((classes, ANG, lanes), BF16),
-            ((entries, 4 * classes, 128), BF16),
+            ((freqs // 2 + 1, 4 * classes, share), BF16),
             *([((1, share), F32)] if last else []),
         ],
         [((lanes // 128, 2 * classes * (freqs + SPARE), 128), F32)],
@@ -447,10 +432,9 @@
     each(classes, body, 0)
 
     def accumulate(f):
-        left = pick(held, f, classes).astype(BF16)[:, :share]
-        take_in(image, f, dot(left, particles[f]), classes)
-
-    loop(pairs, accumulate, 8)
+        take_in(image, f, dot(pick(held, f, classes, share), particles[f]), classes)
+
+    loop(pairs, accumulate, 32)
 
 
 def gather(rounded, fwd_hi, fwd_lo, particles):
@@ -477,26 +461,17 @@
 
 def finish_kernel(image, mine, spectrum, particles, *refs):
     outs, held = refs[:-1], refs[-1]
-    pairs, share, twice = particles.shape
+    pairs, _, twice = particles.shape
     classes = spectrum.shape[1] // 4
     freqs, depth = 2 * pairs, twice // 2
     radii = depth // 2
     pitch = freqs + SPARE
-    bundle, width = bundles(pairs, share)
-
-    def body(j):
-        packed = spectrum[pairs + j].astype(F32) if width else None
-        for i in range(bundle):
-            f = j * bundle + i
-            left = spectrum[f]
-            if width:
-                rest = pltpu.roll(packed, 128 - i * width, 1) if i else packed
-                left = jnp.concatenate([left, rest.astype(BF16)], 1)
-            take_in(held, f, dot(left[:, :share], particles[f]), classes)
-
-    loop(pairs // bundle, body, 1)
-    end = spectrum.shape[0] - 1
-    counts = mine[end].astype(F32) + spectrum[end].astype(F32)
+
+    def body(f):
+        take_in(held, f, dot(spectrum[f], particles[f]), classes)
+
+    loop(pairs, body, 32)
+    counts = (mine[pairs].astype(F32) + spectrum[pairs].astype(F32))[:, :depth]
     counts = counts[:classes] + counts[classes : 2 * classes]
     lane = lax.broadcasted_iota(jnp.int32, (freqs, depth), 1)
     sign = jnp.where(lane < radii, -1.0, 1.0).astype(F32)

time: 49.9 us -> 47.3 us (0.948)
  Pallas kernels: 14.6 us -> 10.5 us
  waiting for transfers between devices: 15.7 us -> 17.4 us
    pallas_call x16, Pallas kernels: 14.6 us -> 10.5 us  [call(): pl.pallas_call(kernel, out_shape=[jax.ShapeDtypeStruct(*x) for x in outs]...]
    ppermute x15, waiting for transfers between devices: 15.7 us -> 17.4 us  [swap(): return lax.ppermute(value, axis, [(i, i ^ bit) for i in range(size)])]
  transfers between devices with their start and end apart: 15 -> 15, of which waited for: 11 -> 11; matrix products, arithmetic and copies ran while one was open for 0% -> 0% of each run, Pallas kernels for 12% -> 9%
where the time goes in v10:
time: 47.3 us; the launch traced here: 47.2 us
  starting transfers between devices  18.4 us (39%)
  waiting for transfers between devices  17.4 us (37%)
  Pallas kernels  10.5 us (22%)
  between operations  0.8 us (2%)
    ppermute x15, starting transfers between devices, swap(): return lax.ppermute(value, axis, [(i, i ^ bit) for i in range(size)])  18.4 us
    ppermute x15, waiting for transfers between devices, swap(): return lax.ppermute(value, axis, [(i, i ^ bit) for i in range(size)])  17.4 us
    pallas_call x16, Pallas kernels, call(): pl.pallas_call(kernel, out_shape=[jax.ShapeDtypeStruct(*x) for x in outs]...  10.5 us
  transfers between devices with their start and end apart: 15, of which 11 were waited for; matrix products, arithmetic and copies ran while one was open for 0% of the time, Pallas kernels for 9%

profile of v10, /device:TPU:0, one launch (start us, length us, event | category | flops | bytes accessed | tf_op | source)
XLA Modules:
  0.0 47.2 jit_solution(4411173496173486627)
XLA Ops:
  0.6 5.1 %collective-permute-start.2 = (bf16[1,64,128]{2,1,0:T(8,128)(2,1)}, bf16[1,64,128]{2,1,0:T(8,128)(2,1)S(1)}, u32[]{:S(2)}, u32[]{:S(2)}) collective-permute-start(bf16[1,64,128]{2,1,0:T(8,128)(2,1)} %refs_0_), channel_id=1, source_target_pairs={{0,12},{4,8},{8,4},{12,0},{1,13},{5,9},{9,5},{13,1},{2,14},{6,10},... | collective-permute-start | bytes 49160 | tf_op jit(solution)/shard_map/ppermute | solution.py:526
  5.9 1.0 %collective-permute-start = (bf16[1,64,128]{2,1,0:T(8,128)(2,1)S(1)}, bf16[1,64,128]{2,1,0:T(8,128)(2,1)S(1)}, u32[]{:S(2)}, u32[]{:S(2)}) collective-permute-start(bf16[1,64,128]{2,1,0:T(8,128)(2,1)S(1)} %copy-done.4), channel_id=1, source_target_pairs={{0,4},{4,0},{8,12},{12,8},{1,5},{5,1},{9,13},{13,9},{2,6},{6,2},{1... | collective-permute-start | bytes 49160 | tf_op jit(solution)/shard_map/ppermute | solution.py:526
  7.0 1.4 %shard_map.96 = (bf16[32,144,256]{2,1,0:T(8,128)(2,1)S(1)}, bf16[32,144,256]{2,1,0:T(8,128)(2,1)S(1)}) custom-call(bf16[288,64,128]{2,1,0:T(8,128)(2,1)S(1)} %copy-done.7, bf16[256,256]{1,0:T(8,128)(2,1)S(1)} %shard_map.95.permutation_ref), custom_call_target="tpu_custom_call" | custom-call | flops 2147483648 | bytes 9568256 | tf_op jit(solution)/shard_map/pallas_call | solution.py:92
  8.4 2.2 %collective-permute-done.1.refs_2_ = bf16[1,64,128]{2,1,0:T(8,128)(2,1)S(1)} collective-permute-done((bf16[1,64,128]{2,1,0:T(8,128)(2,1)S(1)}, bf16[1,64,128]{2,1,0:T(8,128)(2,1)S(1)}, u32[]{:S(2)}, u32[]{:S(2)}) %collective-permute-start.1) | collective-permute-done | bytes 16416 | tf_op jit(solution)/shard_map/ppermute | solution.py:526
  10.6 0.9 %shard_map.97 = (f32[648,128]{1,0:T(8,128)S(1)}, f32[4,256]{1,0:T(4,128)S(1)}, bf16[32,16,256]{2,1,0:T(8,128)(2,1)S(1)}) custom-call(bf16[1,64,128]{2,1,0:T(8,128)(2,1)S(1)} %copy-done.4, bf16[1,64,128]{2,1,0:T(8,128)(2,1)S(1)} %collective-permute-done.refs_1_, bf16[1,64,128]{2,1,0:T(8,128)(2,1)S(1)} %collective-permute-done.1.refs_2_, ...), custom_call_target="tpu_custom_call" | custom-call | flops 150994944 | bytes 3637248 | tf_op jit(solution)/shard_map/pallas_call | solution.py:92
  11.8 0.7 %shard_map.98.own = f32[2,576,128]{2,1,0:T(8,128)S(1)} custom-call(bf16[32,16,256]{2,1,0:T(8,128)(2,1)S(1)} %get-tuple-element.30.left_ref, bf16[32,144,256]{2,1,0:T(8,128)(2,1)S(1)} %get-tuple-element.31.particles), custom_call_target="tpu_custom_call" | custom-call | flops 301989888 | bytes 3211264 | tf_op jit(solution)/shard_map/pallas_call | solution.py:92
  12.5 0.7 %collective-permute-done.3.other = f32[648,128]{1,0:T(8,128)S(1)} collective-permute-done((f32[648,128]{1,0:T(8,128)S(1)}, f32[648,128]{1,0:T(8,128)S(1)}, u32[]{:S(2)}, u32[]{:S(2)}) %collective-permute-start.3) | collective-permute-done | bytes 331808 | tf_op jit(solution)/shard_map/ppermute | solution.py:526
  13.2 0.8 %shard_map.100 = (f32[4,256,256]{2,1,0:T(8,128)S(1)}, f32[8,256]{1,0:T(8,128)S(1)}) custom-call(f32[2,576,128]{2,1,0:T(8,128)S(1)} %shard_map.98.own, f32[648,128]{1,0:T(8,128)S(1)} %collective-permute-done.3.other, f32[4,256]{1,0:T(4,128)S(1)} %get-tuple-element.33.energy_ref, f32[256,256]{1,0:T(8,128)S(1)} %shard_map.99.prior_term, ...), custom_call_target="tpu_custom_call" | custom-call | flops 402653184 | bytes 2793472 | tf_op jit(solution)/shard_map/pallas_call | solution.py:92
  14.0 1.6 %collective-permute-start.4 = (f32[8,256]{1,0:T(8,128)S(1)}, f32[8,256]{1,0:T(8,128)S(1)}, u32[]{:S(2)}, u32[]{:S(2)}) collective-permute-start(f32[8,256]{1,0:T(8,128)S(1)} %get-tuple-element.35.here.first), channel_id=1, source_target_pairs={{0,2},{2,0},{1,3},{3,1},{4,6},{6,4},{5,7},{7,5},{8,10},{10,8},{9,1... | collective-permute-start | bytes 24584 | tf_op jit(solution)/shard_map/ppermute | solution.py:526
  15.5 2.2 %collective-permute-done.4.second = f32[8,256]{1,0:T(8,128)S(1)} collective-permute-done((f32[8,256]{1,0:T(8,128)S(1)}, f32[8,256]{1,0:T(8,128)S(1)}, u32[]{:S(2)}, u32[]{:S(2)}) %collective-permute-start.4) | collective-permute-done | bytes 8224 | tf_op jit(solution)/shard_map/ppermute | solution.py:526
  18.2 0.7 %shard_map.102.image = f32[576,128]{1,0:T(8,128)S(1)} custom-call(bf16[4,256,256]{2,1,0:T(8,128)(2,1)S(1)} %get-tuple-element.36.rounded_ref, bf16[512,256]{1,0:T(8,128)(2,1)S(1)} %copy-done.1, bf16[512,256]{1,0:T(8,128)(2,1)S(1)} %copy-done, bf16[32,144,256]{2,1,0:T(8,128)(2,1)S(1)} %get-tuple-element.31.particles), custom_call_target="tpu_custom_call" | custom-call | flops 268435456 | bytes 4292608 | tf_op jit(solution)/shard_map/pallas_call | solution.py:92
  18.9 0.8 %collective-permute-done.5.spectrum = bf16[33,16,144]{2,1,0:T(8,128)(2,1)S(1)} collective-permute-done((bf16[33,16,144]{2,1,0:T(8,128)(2,1)S(1)}, bf16[33,16,144]{2,1,0:T(8,128)(2,1)S(1)}, u32[]{:S(2)}, u32[]{:S(2)}) %collective-permute-start.5) | collective-permute-done | bytes 152096 | tf_op jit(solution)/shard_map/ppermute | solution.py:526
  19.8 0.5 %shard_map.103.refs_0_ = bf16[272,128]{1,0:T(8,128)(2,1)S(1)} custom-call(f32[576,128]{1,0:T(8,128)S(1)} %shard_map.102.image, bf16[33,16,144]{2,1,0:T(8,128)(2,1)S(1)} %get-tuple-element.37.mine, bf16[33,16,144]{2,1,0:T(8,128)(2,1)S(1)} %collective-permute-done.5.spectrum, bf16[32,144,256]{2,1,0:T(8,128)(2,1)S(1)} %get-tuple-element.29.refs_5_.particles), custom_call_target="tpu_custom_call" | custom-call | flops 311427072 | bytes 3559424 | tf_op jit(solution)/shard_map/pallas_call | solution.py:92
  20.3 1.5 %collective-permute-start.8 = (bf16[272,128]{1,0:T(8,128)(2,1)S(1)}, bf16[272,128]{1,0:T(8,128)(2,1)S(1)}, u32[]{:S(2)}, u32[]{:S(2)}) collective-permute-start(bf16[272,128]{1,0:T(8,128)(2,1)S(1)} %shard_map.103.refs_0_), channel_id=1, source_target_pairs={{0,12},{4,8},{8,4},{12,0},{1,13},{5,9},{9,5},{13,1},{2,14},{6,10},... | collective-permute-start | bytes 208904 | tf_op jit(solution)/shard_map/ppermute | solution.py:526
  21.8 0.6 %collective-permute-start.7 = (bf16[272,128]{1,0:T(8,128)(2,1)S(1)}, bf16[272,128]{1,0:T(8,128)(2,1)S(1)}, u32[]{:S(2)}, u32[]{:S(2)}) collective-permute-start(bf16[272,128]{1,0:T(8,128)(2,1)S(1)} %shard_map.103.refs_0_), channel_id=1, source_target_pairs={{0,8},{4,12},{8,0},{12,4},{1,9},{5,13},{9,1},{13,5},{2,10},{6,14},... | collective-permute-start | bytes 208904 | tf_op jit(solution)/shard_map/ppermute | solution.py:526
  22.4 2.3 %collective-permute-start.6 = (bf16[272,128]{1,0:T(8,128)(2,1)S(1)}, bf16[272,128]{1,0:T(8,128)(2,1)S(1)}, u32[]{:S(2)}, u32[]{:S(2)}) collective-permute-start(bf16[272,128]{1,0:T(8,128)(2,1)S(1)} %shard_map.103.refs_0_), channel_id=1, source_target_pairs={{0,4},{4,0},{8,12},{12,8},{1,5},{5,1},{9,13},{13,9},{2,6},{6,2},{1... | collective-permute-start | bytes 208904 | tf_op jit(solution)/shard_map/ppermute | solution.py:526
  24.7 2.5 %collective-permute-done.8.refs_3_ = bf16[272,128]{1,0:T(8,128)(2,1)S(1)} collective-permute-done((bf16[272,128]{1,0:T(8,128)(2,1)S(1)}, bf16[272,128]{1,0:T(8,128)(2,1)S(1)}, u32[]{:S(2)}, u32[]{:S(2)}) %collective-permute-start.8) | collective-permute-done | bytes 69664 | tf_op jit(solution)/shard_map/ppermute | solution.py:526
  27.2 2.1 %collective-permute-done.7.refs_2_ = bf16[272,128]{1,0:T(8,128)(2,1)S(1)} collective-permute-done((bf16[272,128]{1,0:T(8,128)(2,1)S(1)}, bf16[272,128]{1,0:T(8,128)(2,1)S(1)}, u32[]{:S(2)}, u32[]{:S(2)}) %collective-permute-start.7) | collective-permute-done | bytes 69664 | tf_op jit(solution)/shard_map/ppermute | solution.py:526
  29.3 0.9 %shard_map.104 = (f32[648,128]{1,0:T(8,128)S(1)}, f32[4,256]{1,0:T(4,128)S(1)}, bf16[32,16,256]{2,1,0:T(8,128)(2,1)S(1)}) custom-call(bf16[272,128]{1,0:T(8,128)(2,1)S(1)} %shard_map.103.refs_0_, bf16[272,128]{1,0:T(8,128)(2,1)S(1)} %collective-permute-done.6.refs_1_, bf16[272,128]{1,0:T(8,128)(2,1)S(1)} %collective-permute-done.7.refs_2_, ...), custom_call_target="tpu_custom_call" | custom-call | flops 150994944 | bytes 3850240 | tf_op jit(solution)/shard_map/pallas_call | solution.py:92
  30.3 0.7 %shard_map.105.own = f32[2,576,128]{2,1,0:T(8,128)S(1)} custom-call(bf16[32,16,256]{2,1,0:T(8,128)(2,1)S(1)} %get-tuple-element.38.left_ref, bf16[32,144,256]{2,1,0:T(8,128)(2,1)S(1)} %get-tuple-element.31.particles), custom_call_target="tpu_custom_call" | custom-call | flops 301989888 | bytes 3211264 | tf_op jit(solution)/shard_map/pallas_call | solution.py:92
  31.0 0.9 %collective-permute-done.9.other = f32[648,128]{1,0:T(8,128)S(1)} collective-permute-done((f32[648,128]{1,0:T(8,128)S(1)}, f32[648,128]{1,0:T(8,128)S(1)}, u32[]{:S(2)}, u32[]{:S(2)}) %collective-permute-start.9) | collective-permute-done | bytes 331808 | tf_op jit(solution)/shard_map/ppermute | solution.py:526
  31.9 0.8 %shard_map.106 = (f32[4,256,256]{2,1,0:T(8,128)S(1)}, f32[8,256]{1,0:T(8,128)S(1)}) custom-call(f32[2,576,128]{2,1,0:T(8,128)S(1)} %shard_map.105.own, f32[648,128]{1,0:T(8,128)S(1)} %collective-permute-done.9.other, f32[4,256]{1,0:T(4,128)S(1)} %get-tuple-element.40.energy_ref, f32[256,256]{1,0:T(8,128)S(1)} %shard_map.99.prior_term, ...), custom_call_target="tpu_custom_call" | custom-call | flops 402653184 | bytes 2793472 | tf_op jit(solution)/shard_map/pallas_call | solution.py:92
  32.7 1.6 %collective-permute-start.10 = (f32[8,256]{1,0:T(8,128)S(1)}, f32[8,256]{1,0:T(8,128)S(1)}, u32[]{:S(2)}, u32[]{:S(2)}) collective-permute-start(f32[8,256]{1,0:T(8,128)S(1)} %get-tuple-element.42.here.first), channel_id=1, source_target_pairs={{0,2},{2,0},{1,3},{3,1},{4,6},{6,4},{5,7},{7,5},{8,10},{10,8},{9,1... | collective-permute-start | bytes 24584 | tf_op jit(solution)/shard_map/ppermute | solution.py:526
  34.3 2.2 %collective-permute-done.10.second = f32[8,256]{1,0:T(8,128)S(1)} collective-permute-done((f32[8,256]{1,0:T(8,128)S(1)}, f32[8,256]{1,0:T(8,128)S(1)}, u32[]{:S(2)}, u32[]{:S(2)}) %collective-permute-start.10) | collective-permute-done | bytes 8224 | tf_op jit(solution)/shard_map/ppermute | solution.py:526
  37.0 0.7 %shard_map.108.image = f32[576,128]{1,0:T(8,128)S(1)} custom-call(bf16[4,256,256]{2,1,0:T(8,128)(2,1)S(1)} %get-tuple-element.43.rounded_ref, bf16[512,256]{1,0:T(8,128)(2,1)S(1)} %copy-done.1, bf16[512,256]{1,0:T(8,128)(2,1)S(1)} %copy-done, bf16[32,144,256]{2,1,0:T(8,128)(2,1)S(1)} %get-tuple-element.31.particles), custom_call_target="tpu_custom_call" | custom-call | flops 268435456 | bytes 4292608 | tf_op jit(solution)/shard_map/pallas_call | solution.py:92
  37.7 0.8 %collective-permute-done.11.spectrum = bf16[33,16,144]{2,1,0:T(8,128)(2,1)S(1)} collective-permute-done((bf16[33,16,144]{2,1,0:T(8,128)(2,1)S(1)}, bf16[33,16,144]{2,1,0:T(8,128)(2,1)S(1)}, u32[]{:S(2)}, u32[]{:S(2)}) %collective-permute-start.11) | collective-permute-done | bytes 152096 | tf_op jit(solution)/shard_map/ppermute | solution.py:526
  38.5 0.5 %shard_map.109 = (f32[72,128]{1,0:T(8,128)S(1)}, f32[72,128]{1,0:T(8,128)S(1)}, f32[72,128]{1,0:T(8,128)S(1)}, f32[72,128]{1,0:T(8,128)S(1)}) custom-call(f32[576,128]{1,0:T(8,128)S(1)} %shard_map.108.image, bf16[33,16,144]{2,1,0:T(8,128)(2,1)S(1)} %get-tuple-element.44.mine, bf16[33,16,144]{2,1,0:T(8,128)(2,1)S(1)} %collective-permute-done.11.spectrum, ...), custom_call_target="tpu_custom_call" | custom-call | flops 311427072 | bytes 3653632 | tf_op jit(solution)/shard_map/pallas_call | solution.py:92
  39.0 2.6 %collective-permute-start.12 = (f32[72,128]{1,0:T(8,128)S(1)}, f32[72,128]{1,0:T(8,128)S(1)}, u32[]{:S(2)}, u32[]{:S(2)}) collective-permute-start(f32[72,128]{1,0:T(8,128)S(1)} %get-tuple-element.45), channel_id=1, source_target_pairs={{0,12},{4,8},{8,4},{12,0},{1,13},{5,9},{9,5},{13,1},{2,14},{6,10},... | collective-permute-start | bytes 110600 | tf_op jit(solution)/shard_map/ppermute | solution.py:526
  41.7 1.8 %collective-permute-start.14 = (f32[72,128]{1,0:T(8,128)S(1)}, f32[72,128]{1,0:T(8,128)S(1)}, u32[]{:S(2)}, u32[]{:S(2)}) collective-permute-start(f32[72,128]{1,0:T(8,128)S(1)} %get-tuple-element.47), channel_id=1, source_target_pairs={{0,4},{4,0},{8,12},{12,8},{1,5},{5,1},{9,13},{13,9},{2,6},{6,2},{1... | collective-permute-start | bytes 110600 | tf_op jit(solution)/shard_map/ppermute | solution.py:526
  43.4 1.5 %collective-permute-done.12.refs_0_ = f32[72,128]{1,0:T(8,128)S(1)} collective-permute-done((f32[72,128]{1,0:T(8,128)S(1)}, f32[72,128]{1,0:T(8,128)S(1)}, u32[]{:S(2)}, u32[]{:S(2)}) %collective-permute-start.12) | collective-permute-done | bytes 36896 | tf_op jit(solution)/shard_map/ppermute | solution.py:526
  44.9 1.6 %collective-permute-done.13.refs_1_ = f32[72,128]{1,0:T(8,128)S(1)} collective-permute-done((f32[72,128]{1,0:T(8,128)S(1)}, f32[72,128]{1,0:T(8,128)S(1)}, u32[]{:S(2)}, u32[]{:S(2)}) %collective-permute-start.13) | collective-permute-done | bytes 36896 | tf_op jit(solution)/shard_map/ppermute | solution.py:526
  46.5 0.6 %shard_map.110 = (f32[1,64,128]{2,1,0:T(8,128)}, f32[1,144]{1,0:T(1,128)}) custom-call(f32[72,128]{1,0:T(8,128)S(1)} %collective-permute-done.12.refs_0_, f32[72,128]{1,0:T(8,128)S(1)} %collective-permute-done.13.refs_1_, f32[72,128]{1,0:T(8,128)S(1)} %collective-permute-done.14.refs_2_, f32[72,128]{1,0:T(8,128)S(1)} %get-tuple-element.48.refs_3_, ...), custom_call_target="tpu_custom_call" | custom-call | bytes 229376 | tf_op jit(solution)/shard_map/pallas_call | solution.py:92
  (30 shorter events, 1.4 us)
Async XLA Ops:
  0.6 5.2 %copy-start.4 = (bf16[1,64,128]{2,1,0:T(8,128)(2,1)S(1)}, bf16[1,64,128]{2,1,0:T(8,128)(2,1)}, u32[]{:S(2)}) copy-start(bf16[1,64,128]{2,1,0:T(8,128)(2,1)} %refs_0_) | copy-start | bytes 49156
  0.6 6.3 %copy-start.7 = (bf16[288,64,128]{2,1,0:T(8,128)(2,1)S(1)}, bf16[288,64,128]{2,1,0:T(8,128)(2,1)}, u32[]{:S(2)}) copy-start(bf16[288,64,128]{2,1,0:T(8,128)(2,1)} %particles_ref.1) | copy-start | bytes 14155780
  0.6 7.7 %collective-permute-start.2 = (bf16[1,64,128]{2,1,0:T(8,128)(2,1)}, bf16[1,64,128]{2,1,0:T(8,128)(2,1)S(1)}, u32[]{:S(2)}, u32[]{:S(2)}) collective-permute-start(bf16[1,64,128]{2,1,0:T(8,128)(2,1)} %refs_0_), channel_id=1, source_target_pairs={{0,12},{4,8},{8,4},{12,0},{1,13},{5,9},{9,5},{13,1},{2,14},{6,10},... | collective-permute-start | bytes 49160 | tf_op jit(solution)/shard_map/ppermute | solution.py:526
  5.8 4.7 %copy-start.6 = (f32[64]{0:T(128)S(1)}, f32[64]{0:T(128)}, u32[]{:S(2)}) copy-start(f32[64]{0:T(128)} %param.10) | copy-start | bytes 772
  5.8 4.7 %collective-permute-start.1 = (bf16[1,64,128]{2,1,0:T(8,128)(2,1)S(1)}, bf16[1,64,128]{2,1,0:T(8,128)(2,1)S(1)}, u32[]{:S(2)}, u32[]{:S(2)}) collective-permute-start(bf16[1,64,128]{2,1,0:T(8,128)(2,1)S(1)} %copy-done.4), channel_id=1, source_target_pairs={{0,8},{4,12},{8,0},{12,4},{1,9},{5,13},{9,1},{13,5},{2,10},{6,14},... | collective-permute-start | bytes 49160 | tf_op jit(solution)/shard_map/ppermute | solution.py:526
  5.9 4.6 %collective-permute-start = (bf16[1,64,128]{2,1,0:T(8,128)(2,1)S(1)}, bf16[1,64,128]{2,1,0:T(8,128)(2,1)S(1)}, u32[]{:S(2)}, u32[]{:S(2)}) collective-permute-start(bf16[1,64,128]{2,1,0:T(8,128)(2,1)S(1)} %copy-done.4), channel_id=1, source_target_pairs={{0,4},{4,0},{8,12},{12,8},{1,5},{5,1},{9,13},{13,9},{2,6},{6,2},{1... | collective-permute-start | bytes 49160 | tf_op jit(solution)/shard_map/ppermute | solution.py:526
  8.4 3.2 %copy-start.5 = (s32[288]{0:T(512)S(1)}, s32[288]{0:T(512)}, u32[]{:S(2)}) copy-start(s32[288]{0:T(512)} %prior_ref.1) | copy-start | bytes 3460
  10.5 2.6 %copy-start.2 = (bf16[512,256]{1,0:T(8,128)(2,1)S(1)}, bf16[512,256]{1,0:T(8,128)(2,1)}, u32[]{:S(2)}) copy-start(bf16[512,256]{1,0:T(8,128)(2,1)} %constant.9.clone.inv_lo) | copy-start | bytes 786436
  10.6 2.6 %copy-start.3 = (bf16[512,256]{1,0:T(8,128)(2,1)S(1)}, bf16[512,256]{1,0:T(8,128)(2,1)}, u32[]{:S(2)}) copy-start(bf16[512,256]{1,0:T(8,128)(2,1)} %constant.8.clone.inv_hi) | copy-start | bytes 786436
  11.5 1.6 %collective-permute-start.3 = (f32[648,128]{1,0:T(8,128)S(1)}, f32[648,128]{1,0:T(8,128)S(1)}, u32[]{:S(2)}, u32[]{:S(2)}) collective-permute-start(f32[648,128]{1,0:T(8,128)S(1)} %get-tuple-element.32), channel_id=1, source_target_pairs={{0,1},{1,0},{2,3},{3,2},{4,5},{5,4},{6,7},{7,6},{8,9},{9,8},{10,11... | collective-permute-start | bytes 995336 | tf_op jit(solution)/shard_map/ppermute | solution.py:526
  11.7 6.0 %copy-start = (bf16[512,256]{1,0:T(8,128)(2,1)S(1)}, bf16[512,256]{1,0:T(8,128)(2,1)}, u32[]{:S(2)}) copy-start(bf16[512,256]{1,0:T(8,128)(2,1)} %constant.11.clone.fwd_lo) | copy-start | bytes 786436
  11.7 6.0 %copy-start.1 = (bf16[512,256]{1,0:T(8,128)(2,1)S(1)}, bf16[512,256]{1,0:T(8,128)(2,1)}, u32[]{:S(2)}) copy-start(bf16[512,256]{1,0:T(8,128)(2,1)} %constant.10.clone.fwd_hi) | copy-start | bytes 786436
  14.0 3.7 %collective-permute-start.4 = (f32[8,256]{1,0:T(8,128)S(1)}, f32[8,256]{1,0:T(8,128)S(1)}, u32[]{:S(2)}, u32[]{:S(2)}) collective-permute-start(f32[8,256]{1,0:T(8,128)S(1)} %get-tuple-element.35.here.first), channel_id=1, source_target_pairs={{0,2},{2,0},{1,3},{3,1},{4,6},{6,4},{5,7},{7,5},{8,10},{10,8},{9,1... | collective-permute-start | bytes 24584 | tf_op jit(solution)/shard_map/ppermute | solution.py:526
  18.1 1.6 %collective-permute-start.5 = (bf16[33,16,144]{2,1,0:T(8,128)(2,1)S(1)}, bf16[33,16,144]{2,1,0:T(8,128)(2,1)S(1)}, u32[]{:S(2)}, u32[]{:S(2)}) collective-permute-start(bf16[33,16,144]{2,1,0:T(8,128)(2,1)S(1)} %get-tuple-element.37.mine), channel_id=1, source_target_pairs={{0,1},{1,0},{2,3},{3,2},{4,5},{5,4},{6,7},{7,6},{8,9},{9,8},{10,11... | collective-permute-start | bytes 456200 | tf_op jit(solution)/shard_map/ppermute | solution.py:526
  20.3 6.9 %collective-permute-start.8 = (bf16[272,128]{1,0:T(8,128)(2,1)S(1)}, bf16[272,128]{1,0:T(8,128)(2,1)S(1)}, u32[]{:S(2)}, u32[]{:S(2)}) collective-permute-start(bf16[272,128]{1,0:T(8,128)(2,1)S(1)} %shard_map.103.refs_0_), channel_id=1, source_target_pairs={{0,12},{4,8},{8,4},{12,0},{1,13},{5,9},{9,5},{13,1},{2,14},{6,10},... | collective-permute-start | bytes 208904 | tf_op jit(solution)/shard_map/ppermute | solution.py:526
  21.8 7.6 %collective-permute-start.7 = (bf16[272,128]{1,0:T(8,128)(2,1)S(1)}, bf16[272,128]{1,0:T(8,128)(2,1)S(1)}, u32[]{:S(2)}, u32[]{:S(2)}) collective-permute-start(bf16[272,128]{1,0:T(8,128)(2,1)S(1)} %shard_map.103.refs_0_), channel_id=1, source_target_pairs={{0,8},{4,12},{8,0},{12,4},{1,9},{5,13},{9,1},{13,5},{2,10},{6,14},... | collective-permute-start | bytes 208904 | tf_op jit(solution)/shard_map/ppermute | solution.py:526
  22.4 6.9 %collective-permute-start.6 = (bf16[272,128]{1,0:T(8,128)(2,1)S(1)}, bf16[272,128]{1,0:T(8,128)(2,1)S(1)}, u32[]{:S(2)}, u32[]{:S(2)}) collective-permute-start(bf16[272,128]{1,0:T(8,128)(2,1)S(1)} %shard_map.103.refs_0_), channel_id=1, source_target_pairs={{0,4},{4,0},{8,12},{12,8},{1,5},{5,1},{9,13},{13,9},{2,6},{6,2},{1... | collective-permute-start | bytes 208904 | tf_op jit(solution)/shard_map/ppermute | solution.py:526
  30.2 1.6 %collective-permute-start.9 = (f32[648,128]{1,0:T(8,128)S(1)}, f32[648,128]{1,0:T(8,128)S(1)}, u32[]{:S(2)}, u32[]{:S(2)}) collective-permute-start(f32[648,128]{1,0:T(8,128)S(1)} %get-tuple-element.39), channel_id=1, source_target_pairs={{0,1},{1,0},{2,3},{3,2},{4,5},{5,4},{6,7},{7,6},{8,9},{9,8},{10,11... | collective-permute-start | bytes 995336 | tf_op jit(solution)/shard_map/ppermute | solution.py:526
  32.7 3.7 %collective-permute-start.10 = (f32[8,256]{1,0:T(8,128)S(1)}, f32[8,256]{1,0:T(8,128)S(1)}, u32[]{:S(2)}, u32[]{:S(2)}) collective-permute-start(f32[8,256]{1,0:T(8,128)S(1)} %get-tuple-element.42.here.first), channel_id=1, source_target_pairs={{0,2},{2,0},{1,3},{3,1},{4,6},{6,4},{5,7},{7,5},{8,10},{10,8},{9,1... | collective-permute-start | bytes 24584 | tf_op jit(solution)/shard_map/ppermute | solution.py:526
  36.9 1.6 %collective-permute-start.11 = (bf16[33,16,144]{2,1,0:T(8,128)(2,1)S(1)}, bf16[33,16,144]{2,1,0:T(8,128)(2,1)S(1)}, u32[]{:S(2)}, u32[]{:S(2)}) collective-permute-start(bf16[33,16,144]{2,1,0:T(8,128)(2,1)S(1)} %get-tuple-element.44.mine), channel_id=1, source_target_pairs={{0,1},{1,0},{2,3},{3,2},{4,5},{5,4},{6,7},{7,6},{8,9},{9,8},{10,11... | collective-permute-start | bytes 456200 | tf_op jit(solution)/shard_map/ppermute | solution.py:526
  39.0 5.9 %collective-permute-start.12 = (f32[72,128]{1,0:T(8,128)S(1)}, f32[72,128]{1,0:T(8,128)S(1)}, u32[]{:S(2)}, u32[]{:S(2)}) collective-permute-start(f32[72,128]{1,0:T(8,128)S(1)} %get-tuple-element.45), channel_id=1, source_target_pairs={{0,12},{4,8},{8,4},{12,0},{1,13},{5,9},{9,5},{13,1},{2,14},{6,10},... | collective-permute-start | bytes 110600 | tf_op jit(solution)/shard_map/ppermute | solution.py:526
  41.7 4.9 %collective-permute-start.13 = (f32[72,128]{1,0:T(8,128)S(1)}, f32[72,128]{1,0:T(8,128)S(1)}, u32[]{:S(2)}, u32[]{:S(2)}) collective-permute-start(f32[72,128]{1,0:T(8,128)S(1)} %get-tuple-element.46), channel_id=1, source_target_pairs={{0,8},{4,12},{8,0},{12,4},{1,9},{5,13},{9,1},{13,5},{2,10},{6,14},... | collective-permute-start | bytes 110600 | tf_op jit(solution)/shard_map/ppermute | solution.py:526
  41.7 4.9 %collective-permute-start.14 = (f32[72,128]{1,0:T(8,128)S(1)}, f32[72,128]{1,0:T(8,128)S(1)}, u32[]{:S(2)}, u32[]{:S(2)}) collective-permute-start(f32[72,128]{1,0:T(8,128)S(1)} %get-tuple-element.47), channel_id=1, source_target_pairs={{0,4},{4,0},{8,12},{12,8},{1,5},{5,1},{9,13},{13,9},{2,6},{6,2},{1... | collective-permute-start | bytes 110600 | tf_op jit(solution)/shard_map/ppermute | solution.py:526

commit v11 on v10

--- a/solution.py
+++ b/solution.py
@@ -161,8 +161,8 @@
     return values[0]
 
 
-def weigh_kernel(fresh, count, *refs):
-    sources = refs[:count]
+def weigh_kernel(fresh, turns, count, *refs):
+    sources = [refs[[0, *turns].index(i)] for i in range(count)]
     doubled_ref, particles, out, energy_ref, left_ref, image, *rest = refs[count:]
     pairs, share, twice = particles.shape
     freqs, depth = 2 * pairs, twice // 2
@@ -238,7 +238,7 @@
     return -(-share // 128)
 
 
-def weigh(sources, inverse_noise, particles, fresh):
+def weigh(sources, turns, inverse_noise, particles, fresh):
     pairs, share, twice = particles.shape
     classes = len(sources)
     pitch = 2 * pairs + SPARE
@@ -246,8 +246,8 @@
     assert tiles == 1 or tiles == 2 and 128 % (share - 128) == 0
     packs = -(-2 * classes * (share - 128) // 128) if tiles == 2 else 0
     return call(
-        functools.partial(weigh_kernel, fresh, classes),
-        [*sources, inverse_noise, particles],
+        functools.partial(weigh_kernel, fresh, turns, classes),
+        [*[sources[i] for i in (0, *turns)], inverse_noise, particles],
         [
             (((2 * classes + packs) * pitch, 128), F32),
             ((classes, tiles * 128), F32),
@@ -259,24 +259,46 @@
     )
 
 
-def correlate_kernel(left_ref, particles, out):
+def correlate_kernel(
+    left_ref, particles, energy_ref, prior_term, inv_hi, inv_lo, partial_ref, field
+):
     pairs = left_ref.shape[0]
     classes = left_ref.shape[1] // 4
+    freqs, pitch = 2 * pairs, 2 * pairs + SPARE
+    outs = [field.at[tile] for tile in range(field.shape[0])]
 
     def body(f):
-        outs = [out.at[tile] for tile in range(out.shape[0])]
-        place(outs, f, times(left_ref[f], particles[f]), classes, 2 * pairs + SPARE)
+        place(outs, f, times(left_ref[f], particles[f]), classes, pitch)
 
     loop(pairs, body, 32)
 
-
-def correlate(left, particles):
+    def score(k, carry):
+        value = [across(field, rows((2 * k + part) * pitch, freqs)) for part in range(2)]
+        inner = invert(jnp.concatenate(value, 0), inv_hi, inv_lo, 0)
+        partial_ref[k] = inner - 0.5 * energy_ref[pl.ds(k, 1), :] + prior_term[...]
+        return carry
+
+    each(classes, score, 0)
+
+
+def invert(value, inv_hi, inv_lo, half):
+    high, low = split(value)
+    columns = pl.ds(half * (ANG // 2), ANG // 2)
+    at = table_rows(0, ANG)
+    return dot(inv_hi[at, columns], high) + (
+        dot(inv_hi[at, columns], low) + dot(inv_lo[at, columns], high)
+    )
+
+
+def correlate(left, particles, energy, prior_term, inv_hi, inv_lo):
     pairs, share, twice = particles.shape
-    lines = left.shape[1] // 2 * (2 * pairs + SPARE)
+    classes, lanes = energy.shape
+    lines = 2 * classes * (2 * pairs + SPARE)
     return call(
         correlate_kernel,
-        [left, particles],
-        [((lane_tiles(share), lines, 128), F32)],
+        [left, particles, energy, prior_term, inv_hi, inv_lo],
+        [((classes, ANG, lanes), F32)],
+        [((lanes // 128, lines, 128), F32)],
         flops=2 * left.shape[1] * share * pairs * twice * 8,
     )[0]
 
@@ -289,13 +311,12 @@
     return pl.ds(pl.multiple_of(lax.axis_index("rot") * ANG + base, 128), count)
 
 
-def score_kernel(particles, own, other, energy_ref, prior_term, inv_hi, inv_lo, *refs):
-    weights, peaks = refs
-    classes, share = energy_ref.shape
-    tiles, lines, width = own.shape
-    pitch = lines // (2 * classes)
-    freqs = pitch - SPARE
-    which = table_rows(0, ANG)
+def score_kernel(particles, partial_ref, other, inv_hi, inv_lo, weights, peaks):
+    classes, _, share = partial_ref.shape
+    tiles = share // 128
+    freqs = ANG // 4
+    pitch = freqs + SPARE
+
     def unpacked(group):
         first = other[rows(group * pitch, freqs), :]
         if tiles == 1:
@@ -307,16 +328,10 @@
         return jnp.concatenate([first, pltpu.roll(packed, back, 1)], 1)
 
     def score(k, peak):
-        near = [across(own, rows((2 * k + part) * pitch, freqs)) for part in range(2)]
-        far = [unpacked(2 * k + part) for part in range(2)]
-        value = jnp.concatenate(near + far, 0)
-        high, low = split(value)
-        inner = dot(inv_hi[which, :], high) + (
-            dot(inv_hi[which, :], low) + dot(inv_lo[which, :], high)
-        )
-        far = other[rows(2 * k * pitch + freqs, SPARE), :][:1]
-        energy = energy_ref[pl.ds(k, 1), :] + jnp.concatenate([far] * tiles, 1)
-        scores = inner - 0.5 * energy + prior_term[...]
+        value = jnp.concatenate([unpacked(2 * k + part) for part in range(2)], 0)
+        energy = other[rows(2 * k * pitch + freqs, SPARE), :][:1]
+        inner = invert(value, inv_hi, inv_lo, 1)
+        scores = partial_ref[k] + inner - 0.5 * jnp.concatenate([energy] * tiles, 1)
         weights[k] = scores
         return jnp.maximum(peak, jnp.max(scores, axis=0, keepdims=True))
 
@@ -332,13 +347,13 @@
     peaks[...] = jnp.where(line == 0, peak, total)
 
 
-def scores(own, other, energy, prior_term, inv_hi, inv_lo, particles):
-    classes, share = energy.shape
+def scores(partial, other, inv_hi, inv_lo, particles):
+    classes, _, lanes = partial.shape
     return call(
         functools.partial(score_kernel, particles),
-        [own, other, energy, prior_term, inv_hi, inv_lo],
-        [((classes, ANG, share), F32), ((8, share), F32)],
-        flops=6 * classes * share * ANG * ANG,
+        [partial, other, inv_hi, inv_lo],
+        [(partial.shape, F32), ((8, lanes), F32)],
+        flops=6 * classes * lanes * ANG * ANG,
     )
 
 
@@ -541,22 +556,20 @@
     inv_hi, inv_lo, fwd_hi, fwd_lo = tables(freqs)
     inverse_noise = noise_inv.reshape(1, depth // 2)
     assert blocks & (blocks - 1) == 0
+    turns = sorted(range(1, blocks), key=lambda i: (-i.bit_length(), i))
 
     (permutation,) = call(permutation_kernel, [], [((256, 256), BF16)], flops=1 << 32)
-    first, permutation = lax.optimization_barrier((references, permutation))
     (prior_term,) = call(
         prior_kernel, [prior_rot], [((ANG, lane_tiles(share) * 128), F32)], flops=1 << 26
     )
-    sources = [
-        swap(first if i else references, "blk", blocks, i ^ (blocks - 1)) for i in range(blocks)
-    ][::-1]
+    sources = {i: swap(references, "blk", blocks, i) for i in (*turns, 0)}
     other_images, own_images = prep(particles, permutation, share)
     for step in range(ITERS):
         last = step == ITERS - 1
-        message, energy, left = weigh(sources, inverse_noise, other_images, step == 0)
+        message, energy, left = weigh(sources, turns, inverse_noise, other_images, step == 0)
         message = swap(message, "rot", groups, 1)
-        own = correlate(left, own_images)
-        weights, here = scores(own, message, energy, prior_term, inv_hi, inv_lo, share)
+        partial = correlate(left, own_images, energy, prior_term, inv_hi, inv_lo)
+        weights, here = scores(partial, message, inv_hi, inv_lo, share)
         first = here
         for bit in bits(sides):
             second = swap(first, "cls", sides, bit)
@@ -569,9 +582,9 @@
         image = gather(rounded, fwd_hi, fwd_lo, own_images)
         sums = finish(image, send, message, other_images, last)
         sums = sums if last else sums * blocks
-        sources = [swap(sums[i], "blk", blocks, i) for i in reversed(range(blocks))][::-1]
+        sources = {i: swap(sums[i], "blk", blocks, i) for i in (*turns, 0)}
     means, evidence = call(
-        means_kernel, [*sources[::-1], *evidence], [((1, freqs, depth), F32), ((1, share), F32)]
+        means_kernel, [*[sources[i] for i in turns], sources[0], *evidence], [((1, freqs, depth), F32), ((1, share), F32)]
     )
     return means, evidence.reshape(share)
 

time: 47.3 us -> 47.1 us (level)
  starting transfers between devices: 18.4 us -> 16.1 us
  Pallas kernels: 10.5 us -> 11.7 us
  waiting for transfers between devices: 17.4 us -> 18.3 us
    ppermute x15, starting transfers between devices: 18.4 us -> 16.1 us  [swap(): return lax.ppermute(value, axis, [(i, i ^ bit) for i in range(size)])]
    pallas_call x16, Pallas kernels: 10.5 us -> 11.7 us  [call(): pl.pallas_call(kernel, out_shape=[jax.ShapeDtypeStruct(*x) for x in outs]...]
    ppermute x15, waiting for transfers between devices: 17.4 us -> 18.3 us  [swap(): return lax.ppermute(value, axis, [(i, i ^ bit) for i in range(size)])]
  transfers between devices with their start and end apart: 15 -> 15, of which waited for: 11 -> 13; matrix products, arithmetic and copies ran while one was open for 0% -> 0% of each run, Pallas kernels for 9% -> 12%
where the time goes in v11:
time: 47.1 us; the launch traced here: 47 us
  waiting for transfers between devices  18.3 us (39%)
  starting transfers between devices  16.1 us (34%)
  Pallas kernels  11.7 us (25%)
  between operations  0.84 us (2%)
    ppermute x15, waiting for transfers between devices, swap(): return lax.ppermute(value, axis, [(i, i ^ bit) for i in range(size)])  18.3 us
    ppermute x15, starting transfers between devices, swap(): return lax.ppermute(value, axis, [(i, i ^ bit) for i in range(size)])  16.1 us
    pallas_call x16, Pallas kernels, call(): pl.pallas_call(kernel, out_shape=[jax.ShapeDtypeStruct(*x) for x in outs]...  11.7 us
  transfers between devices with their start and end apart: 15, of which 13 were waited for; matrix products, arithmetic and copies ran while one was open for 0% of the time, Pallas kernels for 12%

profile of v11, /device:TPU:0, one launch (start us, length us, event | category | flops | bytes accessed | tf_op | source)
XLA Modules:
  0.0 47.0 jit_solution(4941707078713420538)
XLA Ops:
  0.6 5.1 %collective-permute-start.1 = (bf16[1,64,128]{2,1,0:T(8,128)(2,1)}, bf16[1,64,128]{2,1,0:T(8,128)(2,1)S(1)}, u32[]{:S(2)}, u32[]{:S(2)}) collective-permute-start(bf16[1,64,128]{2,1,0:T(8,128)(2,1)} %refs_0_.1), channel_id=1, source_target_pairs={{0,12},{4,8},{8,4},{12,0},{1,13},{5,9},{9,5},{13,1},{2,14},{6,10},... | collective-permute-start | bytes 49160 | tf_op jit(solution)/shard_map/ppermute | solution.py:541
  5.8 0.6 %collective-permute-start.2 = (bf16[1,64,128]{2,1,0:T(8,128)(2,1)}, bf16[1,64,128]{2,1,0:T(8,128)(2,1)S(1)}, u32[]{:S(2)}, u32[]{:S(2)}) collective-permute-start(bf16[1,64,128]{2,1,0:T(8,128)(2,1)} %refs_0_.1), channel_id=1, source_target_pairs={{0,4},{4,0},{8,12},{12,8},{1,5},{5,1},{9,13},{13,9},{2,6},{6,2},{1... | collective-permute-start | bytes 49160 | tf_op jit(solution)/shard_map/ppermute | solution.py:541
  6.5 1.4 %shard_map.96 = (bf16[32,144,256]{2,1,0:T(8,128)(2,1)S(1)}, bf16[32,144,256]{2,1,0:T(8,128)(2,1)S(1)}) custom-call(bf16[288,64,128]{2,1,0:T(8,128)(2,1)S(1)} %copy-done.7, bf16[256,256]{1,0:T(8,128)(2,1)S(1)} %shard_map.95.permutation_ref), custom_call_target="tpu_custom_call" | custom-call | flops 2147483648 | bytes 9568256 | tf_op jit(solution)/shard_map/pallas_call | solution.py:92
  7.9 2.7 %collective-permute-done.refs_1_ = bf16[1,64,128]{2,1,0:T(8,128)(2,1)S(1)} collective-permute-done((bf16[1,64,128]{2,1,0:T(8,128)(2,1)}, bf16[1,64,128]{2,1,0:T(8,128)(2,1)S(1)}, u32[]{:S(2)}, u32[]{:S(2)}) %collective-permute-start) | collective-permute-done | bytes 16416 | tf_op jit(solution)/shard_map/ppermute | solution.py:541
  10.6 0.9 %shard_map.97 = (f32[648,128]{1,0:T(8,128)S(1)}, f32[4,256]{1,0:T(4,128)S(1)}, bf16[32,16,256]{2,1,0:T(8,128)(2,1)S(1)}) custom-call(bf16[1,64,128]{2,1,0:T(8,128)(2,1)S(1)} %copy-done.4, bf16[1,64,128]{2,1,0:T(8,128)(2,1)S(1)} %collective-permute-done.refs_1_, bf16[1,64,128]{2,1,0:T(8,128)(2,1)S(1)} %collective-permute-done.1.refs_2_, ...), custom_call_target="tpu_custom_call" | custom-call | flops 150994944 | bytes 3637248 | tf_op jit(solution)/shard_map/pallas_call | solution.py:92
  11.8 1.3 %shard_map.99.partial_ref = f32[4,256,256]{2,1,0:T(8,128)S(1)} custom-call(bf16[32,16,256]{2,1,0:T(8,128)(2,1)S(1)} %get-tuple-element.26.left_ref, bf16[32,144,256]{2,1,0:T(8,128)(2,1)S(1)} %get-tuple-element.27.particles, f32[4,256]{1,0:T(4,128)S(1)} %get-tuple-element.28.energy_ref, f32[256,256]{1,0:T(8,128)S(1)} %shard_map.98.prior_term, ...), custom_call_target="tpu_custom_call" | custom-call | flops 301989888 | bytes 5062656 | tf_op jit(solution)/shard_map/pallas_call | solution.py:92
  13.2 0.8 %shard_map.100 = (f32[4,256,256]{2,1,0:T(8,128)S(1)}, f32[8,256]{1,0:T(8,128)S(1)}) custom-call(f32[4,256,256]{2,1,0:T(8,128)S(1)} %shard_map.99.partial_ref, f32[648,128]{1,0:T(8,128)S(1)} %collective-permute-done.3.other, bf16[512,256]{1,0:T(8,128)(2,1)S(1)} %copy-done.3, bf16[512,256]{1,0:T(8,128)(2,1)S(1)} %copy-done.2), custom_call_target="tpu_custom_call" | custom-call | flops 402653184 | bytes 2973696 | tf_op jit(solution)/shard_map/pallas_call | solution.py:92
  14.0 1.6 %collective-permute-start.4 = (f32[8,256]{1,0:T(8,128)S(1)}, f32[8,256]{1,0:T(8,128)S(1)}, u32[]{:S(2)}, u32[]{:S(2)}) collective-permute-start(f32[8,256]{1,0:T(8,128)S(1)} %get-tuple-element.31.here.first), channel_id=1, source_target_pairs={{0,2},{2,0},{1,3},{3,1},{4,6},{6,4},{5,7},{7,5},{8,10},{10,8},{9,1... | collective-permute-start | bytes 24584 | tf_op jit(solution)/shard_map/ppermute | solution.py:541
  15.6 2.2 %collective-permute-done.4.second = f32[8,256]{1,0:T(8,128)S(1)} collective-permute-done((f32[8,256]{1,0:T(8,128)S(1)}, f32[8,256]{1,0:T(8,128)S(1)}, u32[]{:S(2)}, u32[]{:S(2)}) %collective-permute-start.4) | collective-permute-done | bytes 8224 | tf_op jit(solution)/shard_map/ppermute | solution.py:541
  17.7 0.4 shard_map.101
  18.3 0.7 %shard_map.102.image = f32[576,128]{1,0:T(8,128)S(1)} custom-call(bf16[4,256,256]{2,1,0:T(8,128)(2,1)S(1)} %get-tuple-element.32.rounded_ref, bf16[512,256]{1,0:T(8,128)(2,1)S(1)} %copy-done.1, bf16[512,256]{1,0:T(8,128)(2,1)S(1)} %copy-done, bf16[32,144,256]{2,1,0:T(8,128)(2,1)S(1)} %get-tuple-element.27.particles), custom_call_target="tpu_custom_call" | custom-call | flops 268435456 | bytes 4292608 | tf_op jit(solution)/shard_map/pallas_call | solution.py:92
  19.0 0.8 %collective-permute-done.5.spectrum = bf16[33,16,144]{2,1,0:T(8,128)(2,1)S(1)} collective-permute-done((bf16[33,16,144]{2,1,0:T(8,128)(2,1)S(1)}, bf16[33,16,144]{2,1,0:T(8,128)(2,1)S(1)}, u32[]{:S(2)}, u32[]{:S(2)}) %collective-permute-start.5) | collective-permute-done | bytes 152096 | tf_op jit(solution)/shard_map/ppermute | solution.py:541
  19.8 0.5 %shard_map.103.refs_0_ = bf16[272,128]{1,0:T(8,128)(2,1)S(1)} custom-call(f32[576,128]{1,0:T(8,128)S(1)} %shard_map.102.image, bf16[33,16,144]{2,1,0:T(8,128)(2,1)S(1)} %get-tuple-element.33.mine, bf16[33,16,144]{2,1,0:T(8,128)(2,1)S(1)} %collective-permute-done.5.spectrum, bf16[32,144,256]{2,1,0:T(8,128)(2,1)S(1)} %get-tuple-element.25.refs_5_.particles), custom_call_target="tpu_custom_call" | custom-call | flops 311427072 | bytes 3559424 | tf_op jit(solution)/shard_map/pallas_call | solution.py:92
  20.4 3.5 %collective-permute-start.7 = (bf16[272,128]{1,0:T(8,128)(2,1)S(1)}, bf16[272,128]{1,0:T(8,128)(2,1)S(1)}, u32[]{:S(2)}, u32[]{:S(2)}) collective-permute-start(bf16[272,128]{1,0:T(8,128)(2,1)S(1)} %shard_map.103.refs_0_), channel_id=1, source_target_pairs={{0,12},{4,8},{8,4},{12,0},{1,13},{5,9},{9,5},{13,1},{2,14},{6,10},... | collective-permute-start | bytes 208904 | tf_op jit(solution)/shard_map/ppermute | solution.py:541
  23.8 0.8 %collective-permute-done.8.refs_3_ = bf16[272,128]{1,0:T(8,128)(2,1)S(1)} collective-permute-done((bf16[272,128]{1,0:T(8,128)(2,1)S(1)}, bf16[272,128]{1,0:T(8,128)(2,1)S(1)}, u32[]{:S(2)}, u32[]{:S(2)}) %collective-permute-start.8) | collective-permute-done | bytes 69664 | tf_op jit(solution)/shard_map/ppermute | solution.py:541
  24.7 3.7 %collective-permute-done.7.refs_2_ = bf16[272,128]{1,0:T(8,128)(2,1)S(1)} collective-permute-done((bf16[272,128]{1,0:T(8,128)(2,1)S(1)}, bf16[272,128]{1,0:T(8,128)(2,1)S(1)}, u32[]{:S(2)}, u32[]{:S(2)}) %collective-permute-start.7) | collective-permute-done | bytes 69664 | tf_op jit(solution)/shard_map/ppermute | solution.py:541
  28.4 2.1 %collective-permute-done.6.refs_1_ = bf16[272,128]{1,0:T(8,128)(2,1)S(1)} collective-permute-done((bf16[272,128]{1,0:T(8,128)(2,1)S(1)}, bf16[272,128]{1,0:T(8,128)(2,1)S(1)}, u32[]{:S(2)}, u32[]{:S(2)}) %collective-permute-start.6) | collective-permute-done | bytes 69664 | tf_op jit(solution)/shard_map/ppermute | solution.py:541
  30.5 0.9 %shard_map.104 = (f32[648,128]{1,0:T(8,128)S(1)}, f32[4,256]{1,0:T(4,128)S(1)}, bf16[32,16,256]{2,1,0:T(8,128)(2,1)S(1)}) custom-call(bf16[272,128]{1,0:T(8,128)(2,1)S(1)} %shard_map.103.refs_0_, bf16[272,128]{1,0:T(8,128)(2,1)S(1)} %collective-permute-done.6.refs_1_, bf16[272,128]{1,0:T(8,128)(2,1)S(1)} %collective-permute-done.7.refs_2_, ...), custom_call_target="tpu_custom_call" | custom-call | flops 150994944 | bytes 3850240 | tf_op jit(solution)/shard_map/pallas_call | solution.py:92
  31.5 1.3 %shard_map.105.partial_ref = f32[4,256,256]{2,1,0:T(8,128)S(1)} custom-call(bf16[32,16,256]{2,1,0:T(8,128)(2,1)S(1)} %get-tuple-element.34.left_ref, bf16[32,144,256]{2,1,0:T(8,128)(2,1)S(1)} %get-tuple-element.27.particles, f32[4,256]{1,0:T(4,128)S(1)} %get-tuple-element.35.energy_ref, f32[256,256]{1,0:T(8,128)S(1)} %shard_map.98.prior_term, ...), custom_call_target="tpu_custom_call" | custom-call | flops 301989888 | bytes 5062656 | tf_op jit(solution)/shard_map/pallas_call | solution.py:92
  32.8 0.3 collective-permute-done.9.other
  33.1 0.8 %shard_map.106 = (f32[4,256,256]{2,1,0:T(8,128)S(1)}, f32[8,256]{1,0:T(8,128)S(1)}) custom-call(f32[4,256,256]{2,1,0:T(8,128)S(1)} %shard_map.105.partial_ref, f32[648,128]{1,0:T(8,128)S(1)} %collective-permute-done.9.other, bf16[512,256]{1,0:T(8,128)(2,1)S(1)} %copy-done.3, bf16[512,256]{1,0:T(8,128)(2,1)S(1)} %copy-done.2), custom_call_target="tpu_custom_call" | custom-call | flops 402653184 | bytes 2973696 | tf_op jit(solution)/shard_map/pallas_call | solution.py:92
  33.9 1.5 %collective-permute-start.10 = (f32[8,256]{1,0:T(8,128)S(1)}, f32[8,256]{1,0:T(8,128)S(1)}, u32[]{:S(2)}, u32[]{:S(2)}) collective-permute-start(f32[8,256]{1,0:T(8,128)S(1)} %get-tuple-element.38.here.first), channel_id=1, source_target_pairs={{0,2},{2,0},{1,3},{3,1},{4,6},{6,4},{5,7},{7,5},{8,10},{10,8},{9,1... | collective-permute-start | bytes 24584 | tf_op jit(solution)/shard_map/ppermute | solution.py:541
  35.5 2.2 %collective-permute-done.10.second = f32[8,256]{1,0:T(8,128)S(1)} collective-permute-done((f32[8,256]{1,0:T(8,128)S(1)}, f32[8,256]{1,0:T(8,128)S(1)}, u32[]{:S(2)}, u32[]{:S(2)}) %collective-permute-start.10) | collective-permute-done | bytes 8224 | tf_op jit(solution)/shard_map/ppermute | solution.py:541
  37.6 0.4 shard_map.107
  38.2 0.7 %shard_map.108.image = f32[576,128]{1,0:T(8,128)S(1)} custom-call(bf16[4,256,256]{2,1,0:T(8,128)(2,1)S(1)} %get-tuple-element.39.rounded_ref, bf16[512,256]{1,0:T(8,128)(2,1)S(1)} %copy-done.1, bf16[512,256]{1,0:T(8,128)(2,1)S(1)} %copy-done, bf16[32,144,256]{2,1,0:T(8,128)(2,1)S(1)} %get-tuple-element.27.particles), custom_call_target="tpu_custom_call" | custom-call | flops 268435456 | bytes 4292608 | tf_op jit(solution)/shard_map/pallas_call | solution.py:92
  38.9 0.8 %collective-permute-done.11.spectrum = bf16[33,16,144]{2,1,0:T(8,128)(2,1)S(1)} collective-permute-done((bf16[33,16,144]{2,1,0:T(8,128)(2,1)S(1)}, bf16[33,16,144]{2,1,0:T(8,128)(2,1)S(1)}, u32[]{:S(2)}, u32[]{:S(2)}) %collective-permute-start.11) | collective-permute-done | bytes 152096 | tf_op jit(solution)/shard_map/ppermute | solution.py:541
  39.7 0.5 %shard_map.109 = (f32[72,128]{1,0:T(8,128)S(1)}, f32[72,128]{1,0:T(8,128)S(1)}, f32[72,128]{1,0:T(8,128)S(1)}, f32[72,128]{1,0:T(8,128)S(1)}) custom-call(f32[576,128]{1,0:T(8,128)S(1)} %shard_map.108.image, bf16[33,16,144]{2,1,0:T(8,128)(2,1)S(1)} %get-tuple-element.40.mine, bf16[33,16,144]{2,1,0:T(8,128)(2,1)S(1)} %collective-permute-done.11.spectrum, ...), custom_call_target="tpu_custom_call" | custom-call | flops 311427072 | bytes 3653632 | tf_op jit(solution)/shard_map/pallas_call | solution.py:92
  40.2 1.7 %collective-permute-start.13 = (f32[72,128]{1,0:T(8,128)S(1)}, f32[72,128]{1,0:T(8,128)S(1)}, u32[]{:S(2)}, u32[]{:S(2)}) collective-permute-start(f32[72,128]{1,0:T(8,128)S(1)} %get-tuple-element.42), channel_id=1, source_target_pairs={{0,12},{4,8},{8,4},{12,0},{1,13},{5,9},{9,5},{13,1},{2,14},{6,10},... | collective-permute-start | bytes 110600 | tf_op jit(solution)/shard_map/ppermute | solution.py:541
  41.9 1.8 %collective-permute-start.14 = (f32[72,128]{1,0:T(8,128)S(1)}, f32[72,128]{1,0:T(8,128)S(1)}, u32[]{:S(2)}, u32[]{:S(2)}) collective-permute-start(f32[72,128]{1,0:T(8,128)S(1)} %get-tuple-element.43), channel_id=1, source_target_pairs={{0,4},{4,0},{8,12},{12,8},{1,5},{5,1},{9,13},{13,9},{2,6},{6,2},{1... | collective-permute-start | bytes 110600 | tf_op jit(solution)/shard_map/ppermute | solution.py:541
  43.7 1.8 %collective-permute-done.12.refs_0_ = f32[72,128]{1,0:T(8,128)S(1)} collective-permute-done((f32[72,128]{1,0:T(8,128)S(1)}, f32[72,128]{1,0:T(8,128)S(1)}, u32[]{:S(2)}, u32[]{:S(2)}) %collective-permute-start.12) | collective-permute-done | bytes 36896 | tf_op jit(solution)/shard_map/ppermute | solution.py:541
  45.6 0.7 %collective-permute-done.13.refs_1_ = f32[72,128]{1,0:T(8,128)S(1)} collective-permute-done((f32[72,128]{1,0:T(8,128)S(1)}, f32[72,128]{1,0:T(8,128)S(1)}, u32[]{:S(2)}, u32[]{:S(2)}) %collective-permute-start.13) | collective-permute-done | bytes 36896 | tf_op jit(solution)/shard_map/ppermute | solution.py:541
  46.4 0.6 %shard_map.110 = (f32[1,64,128]{2,1,0:T(8,128)}, f32[1,144]{1,0:T(1,128)}) custom-call(f32[72,128]{1,0:T(8,128)S(1)} %collective-permute-done.12.refs_0_, f32[72,128]{1,0:T(8,128)S(1)} %collective-permute-done.13.refs_1_, f32[72,128]{1,0:T(8,128)S(1)} %collective-permute-done.14.refs_2_, f32[72,128]{1,0:T(8,128)S(1)} %get-tuple-element.44.refs_3_, ...), custom_call_target="tpu_custom_call" | custom-call | bytes 229376 | tf_op jit(solution)/shard_map/pallas_call | solution.py:92
  (30 shorter events, 0.7 us)
Async XLA Ops:
  0.6 5.8 %copy-start.7 = (bf16[288,64,128]{2,1,0:T(8,128)(2,1)S(1)}, bf16[288,64,128]{2,1,0:T(8,128)(2,1)}, u32[]{:S(2)}) copy-start(bf16[288,64,128]{2,1,0:T(8,128)(2,1)} %particles_ref.1) | copy-start | bytes 14155780
  0.6 7.3 %collective-permute-start.1 = (bf16[1,64,128]{2,1,0:T(8,128)(2,1)}, bf16[1,64,128]{2,1,0:T(8,128)(2,1)S(1)}, u32[]{:S(2)}, u32[]{:S(2)}) collective-permute-start(bf16[1,64,128]{2,1,0:T(8,128)(2,1)} %refs_0_.1), channel_id=1, source_target_pairs={{0,12},{4,8},{8,4},{12,0},{1,13},{5,9},{9,5},{13,1},{2,14},{6,10},... | collective-permute-start | bytes 49160 | tf_op jit(solution)/shard_map/ppermute | solution.py:541
  5.8 4.8 %collective-permute-start = (bf16[1,64,128]{2,1,0:T(8,128)(2,1)}, bf16[1,64,128]{2,1,0:T(8,128)(2,1)S(1)}, u32[]{:S(2)}, u32[]{:S(2)}) collective-permute-start(bf16[1,64,128]{2,1,0:T(8,128)(2,1)} %refs_0_.1), channel_id=1, source_target_pairs={{0,8},{4,12},{8,0},{12,4},{1,9},{5,13},{9,1},{13,5},{2,10},{6,14},... | collective-permute-start | bytes 49160 | tf_op jit(solution)/shard_map/ppermute | solution.py:541
  5.8 4.8 %collective-permute-start.2 = (bf16[1,64,128]{2,1,0:T(8,128)(2,1)}, bf16[1,64,128]{2,1,0:T(8,128)(2,1)S(1)}, u32[]{:S(2)}, u32[]{:S(2)}) collective-permute-start(bf16[1,64,128]{2,1,0:T(8,128)(2,1)} %refs_0_.1), channel_id=1, source_target_pairs={{0,4},{4,0},{8,12},{12,8},{1,5},{5,1},{9,13},{13,9},{2,6},{6,2},{1... | collective-permute-start | bytes 49160 | tf_op jit(solution)/shard_map/ppermute | solution.py:541
  6.5 4.1 %copy-start.4 = (bf16[1,64,128]{2,1,0:T(8,128)(2,1)S(1)}, bf16[1,64,128]{2,1,0:T(8,128)(2,1)}, u32[]{:S(2)}) copy-start(bf16[1,64,128]{2,1,0:T(8,128)(2,1)} %refs_0_.1) | copy-start | bytes 49156
  6.5 4.1 %copy-start.6 = (f32[64]{0:T(128)S(1)}, f32[64]{0:T(128)}, u32[]{:S(2)}) copy-start(f32[64]{0:T(128)} %param.10) | copy-start | bytes 772
  7.9 3.7 %copy-start.5 = (s32[288]{0:T(512)S(1)}, s32[288]{0:T(512)}, u32[]{:S(2)}) copy-start(s32[288]{0:T(512)} %prior_ref.1) | copy-start | bytes 3460
  7.9 3.9 %copy-start.2 = (bf16[512,256]{1,0:T(8,128)(2,1)S(1)}, bf16[512,256]{1,0:T(8,128)(2,1)}, u32[]{:S(2)}) copy-start(bf16[512,256]{1,0:T(8,128)(2,1)} %constant.9.clone.inv_lo) | copy-start | bytes 786436
  7.9 3.9 %copy-start.3 = (bf16[512,256]{1,0:T(8,128)(2,1)S(1)}, bf16[512,256]{1,0:T(8,128)(2,1)}, u32[]{:S(2)}) copy-start(bf16[512,256]{1,0:T(8,128)(2,1)} %constant.8.clone.inv_hi) | copy-start | bytes 786436
  11.5 1.6 %collective-permute-start.3 = (f32[648,128]{1,0:T(8,128)S(1)}, f32[648,128]{1,0:T(8,128)S(1)}, u32[]{:S(2)}, u32[]{:S(2)}) collective-permute-start(f32[648,128]{1,0:T(8,128)S(1)} %get-tuple-element.29), channel_id=1, source_target_pairs={{0,1},{1,0},{2,3},{3,2},{4,5},{5,4},{6,7},{7,6},{8,9},{9,8},{10,11... | collective-permute-start | bytes 995336 | tf_op jit(solution)/shard_map/ppermute | solution.py:541
  11.8 5.9 %copy-start = (bf16[512,256]{1,0:T(8,128)(2,1)S(1)}, bf16[512,256]{1,0:T(8,128)(2,1)}, u32[]{:S(2)}) copy-start(bf16[512,256]{1,0:T(8,128)(2,1)} %constant.11.clone.fwd_lo) | copy-start | bytes 786436
  11.8 5.9 %copy-start.1 = (bf16[512,256]{1,0:T(8,128)(2,1)S(1)}, bf16[512,256]{1,0:T(8,128)(2,1)}, u32[]{:S(2)}) copy-start(bf16[512,256]{1,0:T(8,128)(2,1)} %constant.10.clone.fwd_hi) | copy-start | bytes 786436
  14.0 3.7 %collective-permute-start.4 = (f32[8,256]{1,0:T(8,128)S(1)}, f32[8,256]{1,0:T(8,128)S(1)}, u32[]{:S(2)}, u32[]{:S(2)}) collective-permute-start(f32[8,256]{1,0:T(8,128)S(1)} %get-tuple-element.31.here.first), channel_id=1, source_target_pairs={{0,2},{2,0},{1,3},{3,1},{4,6},{6,4},{5,7},{7,5},{8,10},{10,8},{9,1... | collective-permute-start | bytes 24584 | tf_op jit(solution)/shard_map/ppermute | solution.py:541
  18.2 1.6 %collective-permute-start.5 = (bf16[33,16,144]{2,1,0:T(8,128)(2,1)S(1)}, bf16[33,16,144]{2,1,0:T(8,128)(2,1)S(1)}, u32[]{:S(2)}, u32[]{:S(2)}) collective-permute-start(bf16[33,16,144]{2,1,0:T(8,128)(2,1)S(1)} %get-tuple-element.33.mine), channel_id=1, source_target_pairs={{0,1},{1,0},{2,3},{3,2},{4,5},{5,4},{6,7},{7,6},{8,9},{9,8},{10,11... | collective-permute-start | bytes 456200 | tf_op jit(solution)/shard_map/ppermute | solution.py:541
  20.3 4.4 %collective-permute-start.8 = (bf16[272,128]{1,0:T(8,128)(2,1)S(1)}, bf16[272,128]{1,0:T(8,128)(2,1)S(1)}, u32[]{:S(2)}, u32[]{:S(2)}) collective-permute-start(bf16[272,128]{1,0:T(8,128)(2,1)S(1)} %shard_map.103.refs_0_), channel_id=1, source_target_pairs={{0,4},{4,0},{8,12},{12,8},{1,5},{5,1},{9,13},{13,9},{2,6},{6,2},{1... | collective-permute-start | bytes 208904 | tf_op jit(solution)/shard_map/ppermute | solution.py:541
  20.4 8.0 %collective-permute-start.7 = (bf16[272,128]{1,0:T(8,128)(2,1)S(1)}, bf16[272,128]{1,0:T(8,128)(2,1)S(1)}, u32[]{:S(2)}, u32[]{:S(2)}) collective-permute-start(bf16[272,128]{1,0:T(8,128)(2,1)S(1)} %shard_map.103.refs_0_), channel_id=1, source_target_pairs={{0,12},{4,8},{8,4},{12,0},{1,13},{5,9},{9,5},{13,1},{2,14},{6,10},... | collective-permute-start | bytes 208904 | tf_op jit(solution)/shard_map/ppermute | solution.py:541
  23.8 6.7 %collective-permute-start.6 = (bf16[272,128]{1,0:T(8,128)(2,1)S(1)}, bf16[272,128]{1,0:T(8,128)(2,1)S(1)}, u32[]{:S(2)}, u32[]{:S(2)}) collective-permute-start(bf16[272,128]{1,0:T(8,128)(2,1)S(1)} %shard_map.103.refs_0_), channel_id=1, source_target_pairs={{0,8},{4,12},{8,0},{12,4},{1,9},{5,13},{9,1},{13,5},{2,10},{6,14},... | collective-permute-start | bytes 208904 | tf_op jit(solution)/shard_map/ppermute | solution.py:541
  31.4 1.6 %collective-permute-start.9 = (f32[648,128]{1,0:T(8,128)S(1)}, f32[648,128]{1,0:T(8,128)S(1)}, u32[]{:S(2)}, u32[]{:S(2)}) collective-permute-start(f32[648,128]{1,0:T(8,128)S(1)} %get-tuple-element.36), channel_id=1, source_target_pairs={{0,1},{1,0},{2,3},{3,2},{4,5},{5,4},{6,7},{7,6},{8,9},{9,8},{10,11... | collective-permute-start | bytes 995336 | tf_op jit(solution)/shard_map/ppermute | solution.py:541
  33.9 3.7 %collective-permute-start.10 = (f32[8,256]{1,0:T(8,128)S(1)}, f32[8,256]{1,0:T(8,128)S(1)}, u32[]{:S(2)}, u32[]{:S(2)}) collective-permute-start(f32[8,256]{1,0:T(8,128)S(1)} %get-tuple-element.38.here.first), channel_id=1, source_target_pairs={{0,2},{2,0},{1,3},{3,1},{4,6},{6,4},{5,7},{7,5},{8,10},{10,8},{9,1... | collective-permute-start | bytes 24584 | tf_op jit(solution)/shard_map/ppermute | solution.py:541
  38.1 1.6 %collective-permute-start.11 = (bf16[33,16,144]{2,1,0:T(8,128)(2,1)S(1)}, bf16[33,16,144]{2,1,0:T(8,128)(2,1)S(1)}, u32[]{:S(2)}, u32[]{:S(2)}) collective-permute-start(bf16[33,16,144]{2,1,0:T(8,128)(2,1)S(1)} %get-tuple-element.40.mine), channel_id=1, source_target_pairs={{0,1},{1,0},{2,3},{3,2},{4,5},{5,4},{6,7},{7,6},{8,9},{9,8},{10,11... | collective-permute-start | bytes 456200 | tf_op jit(solution)/shard_map/ppermute | solution.py:541
  40.2 5.4 %collective-permute-start.12 = (f32[72,128]{1,0:T(8,128)S(1)}, f32[72,128]{1,0:T(8,128)S(1)}, u32[]{:S(2)}, u32[]{:S(2)}) collective-permute-start(f32[72,128]{1,0:T(8,128)S(1)} %get-tuple-element.41), channel_id=1, source_target_pairs={{0,8},{4,12},{8,0},{12,4},{1,9},{5,13},{9,1},{13,5},{2,10},{6,14},... | collective-permute-start | bytes 110600 | tf_op jit(solution)/shard_map/ppermute | solution.py:541
  40.2 6.0 %collective-permute-start.13 = (f32[72,128]{1,0:T(8,128)S(1)}, f32[72,128]{1,0:T(8,128)S(1)}, u32[]{:S(2)}, u32[]{:S(2)}) collective-permute-start(f32[72,128]{1,0:T(8,128)S(1)} %get-tuple-element.42), channel_id=1, source_target_pairs={{0,12},{4,8},{8,4},{12,0},{1,13},{5,9},{9,5},{13,1},{2,14},{6,10},... | collective-permute-start | bytes 110600 | tf_op jit(solution)/shard_map/ppermute | solution.py:541
  41.9 4.4 %collective-permute-start.14 = (f32[72,128]{1,0:T(8,128)S(1)}, f32[72,128]{1,0:T(8,128)S(1)}, u32[]{:S(2)}, u32[]{:S(2)}) collective-permute-start(f32[72,128]{1,0:T(8,128)S(1)} %get-tuple-element.43), channel_id=1, source_target_pairs={{0,4},{4,0},{8,12},{12,8},{1,5},{5,1},{9,13},{13,9},{2,6},{6,2},{1... | collective-permute-start | bytes 110600 | tf_op jit(solution)/shard_map/ppermute | solution.py:541

commit v12 on v10

--- a/solution.py
+++ b/solution.py
@@ -43,11 +43,12 @@
         inverse.append(np.concatenate([sides[group][0], sides[1 - group][0]], 1))
         forward.append(np.concatenate([sides[1 - group][1], sides[group][1]], 0))
     result = []
-    for table in (inverse, forward):
-        table = np.stack(table).astype(np.float32)
+    for table, kinds in ((inverse, (0, 0, 1)), (forward, (0, 1))):
+        table = np.concatenate(table, 0).astype(np.float32)
         high = table.astype(BF16)
-        result += [high, (table - high.astype(np.float32)).astype(BF16)]
-    return [jnp.asarray(x.reshape(-1, ANG)) for x in result]
+        parts = [high, (table - high.astype(np.float32)).astype(BF16)]
+        result.append(jnp.asarray(np.concatenate([parts[kind] for kind in kinds], 1)))
+    return result
 
 
 def loop(count, body, unroll):
@@ -161,8 +162,8 @@
     return values[0]
 
 
-def weigh_kernel(fresh, count, *refs):
-    sources = refs[:count]
+def weigh_kernel(fresh, order, count, *refs):
+    sources = [refs[order.index(i)] for i in range(count)]
     doubled_ref, particles, out, energy_ref, left_ref, image, *rest = refs[count:]
     pairs, share, twice = particles.shape
     freqs, depth = 2 * pairs, twice // 2
@@ -238,7 +239,7 @@
     return -(-share // 128)
 
 
-def weigh(sources, inverse_noise, particles, fresh):
+def weigh(sources, order, inverse_noise, particles, fresh):
     pairs, share, twice = particles.shape
     classes = len(sources)
     pitch = 2 * pairs + SPARE
@@ -246,8 +247,8 @@
     assert tiles == 1 or tiles == 2 and 128 % (share - 128) == 0
     packs = -(-2 * classes * (share - 128) // 128) if tiles == 2 else 0
     return call(
-        functools.partial(weigh_kernel, fresh, classes),
-        [*sources, inverse_noise, particles],
+        functools.partial(weigh_kernel, fresh, order, classes),
+        [*[sources[i] for i in order], inverse_noise, particles],
         [
             (((2 * classes + packs) * pitch, 128), F32),
             ((classes, tiles * 128), F32),
@@ -289,13 +290,14 @@
     return pl.ds(pl.multiple_of(lax.axis_index("rot") * ANG + base, 128), count)
 
 
-def score_kernel(particles, own, other, energy_ref, prior_term, inv_hi, inv_lo, *refs):
-    weights, peaks = refs
+def score_kernel(particles, own, other, energy_ref, prior_term, inverse, *refs):
+    weights, tops, peaks = refs
     classes, share = energy_ref.shape
     tiles, lines, width = own.shape
     pitch = lines // (2 * classes)
     freqs = pitch - SPARE
     which = table_rows(0, ANG)
+
     def unpacked(group):
         first = other[rows(group * pitch, freqs), :]
         if tiles == 1:
@@ -306,73 +308,70 @@
         back = (bundle - group % bundle) % bundle * width
         return jnp.concatenate([first, pltpu.roll(packed, back, 1)], 1)
 
-    def score(k, peak):
+    def score(k, carry):
         near = [across(own, rows((2 * k + part) * pitch, freqs)) for part in range(2)]
         far = [unpacked(2 * k + part) for part in range(2)]
-        value = jnp.concatenate(near + far, 0)
-        high, low = split(value)
-        inner = dot(inv_hi[which, :], high) + (
-            dot(inv_hi[which, :], low) + dot(inv_lo[which, :], high)
-        )
+        high, low = split(jnp.concatenate(near + far, 0))
+        inner = dot(inverse[which, :], jnp.concatenate([high, low, high], 0))
         far = other[rows(2 * k * pitch + freqs, SPARE), :][:1]
         energy = energy_ref[pl.ds(k, 1), :] + jnp.concatenate([far] * tiles, 1)
         scores = inner - 0.5 * energy + prior_term[...]
-        weights[k] = scores
-        return jnp.maximum(peak, jnp.max(scores, axis=0, keepdims=True))
-
-    peak = each(classes, score, jnp.full((1, share), -jnp.inf, F32))
-
-    def weight(k, total):
-        value = jnp.exp(weights[k] - peak)
+        top = jnp.max(scores, axis=0, keepdims=True)
+        value = jnp.exp(scores - top)
         weights[k] = value
-        return total + jnp.sum(value, axis=0, keepdims=True)
-
-    total = each(classes, weight, jnp.zeros((1, share), F32))
+        total = jnp.sum(value, axis=0, keepdims=True)
+        tops[pl.ds(k, 1), :] = top
+        return merge(carry, (top, total))
+
+    first = (jnp.full((1, share), -jnp.inf, F32), jnp.zeros((1, share), F32))
+    top, total = each(classes, score, first)
     line = lax.broadcasted_iota(jnp.int32, peaks.shape, 0)
-    peaks[...] = jnp.where(line == 0, peak, total)
-
-
-def scores(own, other, energy, prior_term, inv_hi, inv_lo, particles):
-    classes, share = energy.shape
+    peaks[...] = jnp.where(line == 0, top, total)
+
+
+def scores(own, other, energy, prior_term, inverse, particles):
+    classes, lanes = energy.shape
     return call(
         functools.partial(score_kernel, particles),
-        [own, other, energy, prior_term, inv_hi, inv_lo],
-        [((classes, ANG, share), F32), ((8, share), F32)],
-        flops=6 * classes * share * ANG * ANG,
+        [own, other, energy, prior_term, inverse],
+        [((classes, ANG, lanes), F32), ((classes, lanes), F32), ((8, lanes), F32)],
+        flops=6 * classes * lanes * ANG * ANG,
     )
 
 
 def merge(first, second):
-    top = jnp.maximum(first[0:1], second[0:1])
-    total = first[1:2] * jnp.exp(first[0:1] - top) + second[1:2] * jnp.exp(second[0:1] - top)
-    return top, total
+    top = jnp.maximum(first[0], second[0])
+    return top, first[1] * jnp.exp(first[0] - top) + second[1] * jnp.exp(second[0] - top)
+
+
+def two_lines(ref):
+    return ref[0:1, :], ref[1:2, :]
 
 
 def merge_kernel(first, second, out):
-    top, total = merge(first[...], second[...])
+    top, total = merge(two_lines(first), two_lines(second))
     line = lax.broadcasted_iota(jnp.int32, out.shape, 0)
     out[...] = jnp.where(line == 0, top, total)
 
 
-def turn_kernel(share, weights, here, first, second, fwd_hi, fwd_lo, *refs):
+def turn_kernel(share, weights, tops, first, second, forward, *refs):
     rounded_ref, send, *evidence_ref, held = refs
     classes, _, lanes = weights.shape
     pairs = (held.shape[1] // (2 * classes) - SPARE) // 2
-    top, total = merge(first[...], second[...])
+    top, total = merge(two_lines(first), two_lines(second))
     for ref in evidence_ref:
         ref[...] = (top + jnp.log(total))[:, :share]
-    factor = jnp.exp(here[0:1, :] - top) / total
     lane = lax.broadcasted_iota(jnp.int32, (1, lanes), 1)
-    factor = jnp.where(lane < share, factor, 0.0)
+    inverse_total = jnp.where(lane < share, 1.0 / total, 0.0)
     which = table_rows(0, ANG // 2)
     line = lax.broadcasted_iota(jnp.int32, (4 * classes, share), 0)
 
     def body(k, column):
-        value = weights[k] * factor
+        value = weights[k] * (jnp.exp(tops[pl.ds(k, 1), :] - top) * inverse_total)
         count = jnp.sum(jnp.sum(value, axis=0, keepdims=True), axis=1, keepdims=True)
         rounded = value.astype(BF16)
         rounded_ref[k] = rounded
-        spread(held, k, dot(fwd_hi[which, :], rounded) + dot(fwd_lo[which, :], rounded))
+        spread(held, k, dot(forward[which, :], jnp.concatenate([rounded, rounded], 0)))
         high = count.astype(BF16).astype(F32)
         return jnp.where(line == k, high, jnp.where(line == classes + k, count - high, column))
 
@@ -404,11 +403,11 @@
     return jnp.concatenate(parts, 0)[:, :share]
 
 
-def turn(weights, here, first, second, fwd_hi, fwd_lo, freqs, share, last):
+def turn(weights, tops, first, second, forward, freqs, share, last):
     classes, _, lanes = weights.shape
     return call(
         functools.partial(turn_kernel, share),
-        [weights, here, first, second, fwd_hi, fwd_lo],
+        [weights, tops, first, second, forward],
         [
             ((classes, ANG, lanes), BF16),
             ((freqs // 2 + 1, 4 * classes, share), BF16),
@@ -419,14 +418,14 @@
     )
 
 
-def gather_kernel(rounded_ref, fwd_hi, fwd_lo, particles, image, held):
+def gather_kernel(rounded_ref, forward, particles, image, held):
     classes = rounded_ref.shape[0]
     pairs, share, _ = particles.shape
     which = table_rows(ANG // 2, ANG // 2)
 
     def body(k, carry):
         rounded = rounded_ref[k]
-        spread(held, k, dot(fwd_hi[which, :], rounded) + dot(fwd_lo[which, :], rounded))
+        spread(held, k, dot(forward[which, :], jnp.concatenate([rounded, rounded], 0)))
         return carry
 
     each(classes, body, 0)
@@ -437,13 +436,13 @@
     loop(pairs, accumulate, 32)
 
 
-def gather(rounded, fwd_hi, fwd_lo, particles):
+def gather(rounded, forward, particles):
     pairs, share, twice = particles.shape
     classes, _, lanes = rounded.shape
     lines = 2 * classes * (2 * pairs + SPARE)
     return call(
         gather_kernel,
-        [rounded, fwd_hi, fwd_lo, particles],
+        [rounded, forward, particles],
         [((lines, twice // 2), F32)],
         [((lanes // 128, lines, 128), F32)],
         flops=4 * classes * lanes * ANG * ANG,
@@ -538,40 +537,39 @@
     blocks = lax.axis_size("blk")
     assert groups == 2 and 2 * groups * freqs == ANG
     share = batch // groups
-    inv_hi, inv_lo, fwd_hi, fwd_lo = tables(freqs)
+    inverse, forward = tables(freqs)
     inverse_noise = noise_inv.reshape(1, depth // 2)
     assert blocks & (blocks - 1) == 0
+    turns = sorted(range(1, blocks), key=lambda i: (-i.bit_length(), i))
 
     (permutation,) = call(permutation_kernel, [], [((256, 256), BF16)], flops=1 << 32)
-    first, permutation = lax.optimization_barrier((references, permutation))
     (prior_term,) = call(
         prior_kernel, [prior_rot], [((ANG, lane_tiles(share) * 128), F32)], flops=1 << 26
     )
-    sources = [
-        swap(first if i else references, "blk", blocks, i ^ (blocks - 1)) for i in range(blocks)
-    ][::-1]
+    sources = {i: swap(references, "blk", blocks, i) for i in (*turns, 0)}
     other_images, own_images = prep(particles, permutation, share)
     for step in range(ITERS):
         last = step == ITERS - 1
-        message, energy, left = weigh(sources, inverse_noise, other_images, step == 0)
+        order = [0, *(reversed(turns) if step else reversed(range(1, blocks)))]
+        message, energy, left = weigh(sources, order, inverse_noise, other_images, step == 0)
         message = swap(message, "rot", groups, 1)
         own = correlate(left, own_images)
-        weights, here = scores(own, message, energy, prior_term, inv_hi, inv_lo, share)
+        weights, tops, here = scores(own, message, energy, prior_term, inverse, share)
         first = here
         for bit in bits(sides):
             second = swap(first, "cls", sides, bit)
             if 2 * bit < sides:
                 (first,) = call(merge_kernel, [first, second], [(here.shape, F32)])
         rounded, send, *evidence = turn(
-            weights, here, first, second, fwd_hi, fwd_lo, freqs, share, last
+            weights, tops, first, second, forward, freqs, share, last
         )
         message = swap(send, "rot", groups, 1)
-        image = gather(rounded, fwd_hi, fwd_lo, own_images)
+        image = gather(rounded, forward, own_images)
         sums = finish(image, send, message, other_images, last)
         sums = sums if last else sums * blocks
-        sources = [swap(sums[i], "blk", blocks, i) for i in reversed(range(blocks))][::-1]
+        sources = {i: swap(sums[i], "blk", blocks, i) for i in (*turns, 0)}
     means, evidence = call(
-        means_kernel, [*sources[::-1], *evidence], [((1, freqs, depth), F32), ((1, share), F32)]
+        means_kernel, [*[sources[i] for i in turns], sources[0], *evidence], [((1, freqs, depth), F32), ((1, share), F32)]
     )
     return means, evidence.reshape(share)
 

time: 47.3 us -> 47.2 us (level)
  waiting for transfers between devices: 17.4 us -> 19.8 us
  starting transfers between devices: 18.4 us -> 16 us
    ppermute x15, waiting for transfers between devices: 17.4 us -> 19.8 us  [swap(): return lax.ppermute(value, axis, [(i, i ^ bit) for i in range(size)])]
    ppermute x15, starting transfers between devices: 18.4 us -> 16 us  [swap(): return lax.ppermute(value, axis, [(i, i ^ bit) for i in range(size)])]
  transfers between devices with their start and end apart: 15 -> 15, of which waited for: 11 -> 12; matrix products, arithmetic and copies ran while one was open for 0% -> 0% of each run, Pallas kernels for 9% -> 10%
where the time goes in v12:
time: 47.2 us; the launch traced here: 47 us
  waiting for transfers between devices  19.8 us (42%)
  starting transfers between devices  16 us (34%)
  Pallas kernels  10.4 us (22%)
  between operations  0.79 us (2%)
    ppermute x15, waiting for transfers between devices, swap(): return lax.ppermute(value, axis, [(i, i ^ bit) for i in range(size)])  19.8 us
    ppermute x15, starting transfers between devices, swap(): return lax.ppermute(value, axis, [(i, i ^ bit) for i in range(size)])  16 us
    pallas_call x16, Pallas kernels, call(): pl.pallas_call(kernel, out_shape=[jax.ShapeDtypeStruct(*x) for x in outs]...  10.4 us
  transfers between devices with their start and end apart: 15, of which 12 were waited for; matrix products, arithmetic and copies ran while one was open for 0% of the time, Pallas kernels for 10%

profile of v12, /device:TPU:0, one launch (start us, length us, event | category | flops | bytes accessed | tf_op | source)
XLA Modules:
  0.0 47.0 jit_solution(11275074756718571510)
XLA Ops:
  0.6 4.1 %collective-permute-start.1 = (bf16[1,64,128]{2,1,0:T(8,128)(2,1)}, bf16[1,64,128]{2,1,0:T(8,128)(2,1)S(1)}, u32[]{:S(2)}, u32[]{:S(2)}) collective-permute-start(bf16[1,64,128]{2,1,0:T(8,128)(2,1)} %refs_0_.1), channel_id=1, source_target_pairs={{0,8},{4,12},{8,0},{12,4},{1,9},{5,13},{9,1},{13,5},{2,10},{6,14},... | collective-permute-start | bytes 49160 | tf_op jit(solution)/shard_map/ppermute | solution.py:525
  4.7 1.3 %collective-permute-start = (bf16[1,64,128]{2,1,0:T(8,128)(2,1)}, bf16[1,64,128]{2,1,0:T(8,128)(2,1)S(1)}, u32[]{:S(2)}, u32[]{:S(2)}) collective-permute-start(bf16[1,64,128]{2,1,0:T(8,128)(2,1)} %refs_0_.1), channel_id=1, source_target_pairs={{0,12},{4,8},{8,4},{12,0},{1,13},{5,9},{9,5},{13,1},{2,14},{6,10},... | collective-permute-start | bytes 49160 | tf_op jit(solution)/shard_map/ppermute | solution.py:525
  6.4 1.4 %shard_map.78 = (bf16[32,144,256]{2,1,0:T(8,128)(2,1)S(1)}, bf16[32,144,256]{2,1,0:T(8,128)(2,1)S(1)}) custom-call(bf16[288,64,128]{2,1,0:T(8,128)(2,1)S(1)} %copy-done.5, bf16[256,256]{1,0:T(8,128)(2,1)S(1)} %shard_map.77.permutation_ref), custom_call_target="tpu_custom_call" | custom-call | flops 2147483648 | bytes 9568256 | tf_op jit(solution)/shard_map/pallas_call | solution.py:93
  7.8 2.7 %collective-permute-done.refs_1_ = bf16[1,64,128]{2,1,0:T(8,128)(2,1)S(1)} collective-permute-done((bf16[1,64,128]{2,1,0:T(8,128)(2,1)}, bf16[1,64,128]{2,1,0:T(8,128)(2,1)S(1)}, u32[]{:S(2)}, u32[]{:S(2)}) %collective-permute-start) | collective-permute-done | bytes 16416 | tf_op jit(solution)/shard_map/ppermute | solution.py:525
  10.5 0.9 %shard_map.79 = (f32[648,128]{1,0:T(8,128)S(1)}, f32[4,256]{1,0:T(4,128)S(1)}, bf16[32,16,256]{2,1,0:T(8,128)(2,1)S(1)}) custom-call(bf16[1,64,128]{2,1,0:T(8,128)(2,1)S(1)} %copy-done.2, bf16[1,64,128]{2,1,0:T(8,128)(2,1)S(1)} %collective-permute-done.refs_1_, bf16[1,64,128]{2,1,0:T(8,128)(2,1)S(1)} %collective-permute-done.1.refs_2_, ...), custom_call_target="tpu_custom_call" | custom-call | flops 150994944 | bytes 3637248 | tf_op jit(solution)/shard_map/pallas_call | solution.py:93
  11.7 0.7 %shard_map.80.own = f32[2,576,128]{2,1,0:T(8,128)S(1)} custom-call(bf16[32,16,256]{2,1,0:T(8,128)(2,1)S(1)} %get-tuple-element.28.left_ref, bf16[32,144,256]{2,1,0:T(8,128)(2,1)S(1)} %get-tuple-element.29.particles), custom_call_target="tpu_custom_call" | custom-call | flops 301989888 | bytes 3211264 | tf_op jit(solution)/shard_map/pallas_call | solution.py:93
  12.4 0.7 %collective-permute-done.3.other = f32[648,128]{1,0:T(8,128)S(1)} collective-permute-done((f32[648,128]{1,0:T(8,128)S(1)}, f32[648,128]{1,0:T(8,128)S(1)}, u32[]{:S(2)}, u32[]{:S(2)}) %collective-permute-start.3) | collective-permute-done | bytes 331808 | tf_op jit(solution)/shard_map/ppermute | solution.py:525
  13.1 0.8 %shard_map.82 = (f32[4,256,256]{2,1,0:T(8,128)S(1)}, f32[4,256]{1,0:T(4,128)S(1)}, f32[8,256]{1,0:T(8,128)S(1)}) custom-call(f32[2,576,128]{2,1,0:T(8,128)S(1)} %shard_map.80.own, f32[648,128]{1,0:T(8,128)S(1)} %collective-permute-done.3.other, f32[4,256]{1,0:T(4,128)S(1)} %get-tuple-element.31.energy_ref, f32[256,256]{1,0:T(8,128)S(1)} %shard_map.81.prior_term, ...), custom_call_target="tpu_custom_call" | custom-call | flops 402653184 | bytes 3072000 | tf_op jit(solution)/shard_map/pallas_call | solution.py:93
  13.9 1.6 %collective-permute-start.4 = (f32[8,256]{1,0:T(8,128)S(1)}, f32[8,256]{1,0:T(8,128)S(1)}, u32[]{:S(2)}, u32[]{:S(2)}) collective-permute-start(f32[8,256]{1,0:T(8,128)S(1)} %get-tuple-element.34.first), channel_id=1, source_target_pairs={{0,2},{2,0},{1,3},{3,1},{4,6},{6,4},{5,7},{7,5},{8,10},{10,8},{9,1... | collective-permute-start | bytes 24584 | tf_op jit(solution)/shard_map/ppermute | solution.py:525
  15.4 2.1 %collective-permute-done.4.second = f32[8,256]{1,0:T(8,128)S(1)} collective-permute-done((f32[8,256]{1,0:T(8,128)S(1)}, f32[8,256]{1,0:T(8,128)S(1)}, u32[]{:S(2)}, u32[]{:S(2)}) %collective-permute-start.4) | collective-permute-done | bytes 8224 | tf_op jit(solution)/shard_map/ppermute | solution.py:525
  18.1 0.7 %shard_map.84.image = f32[576,128]{1,0:T(8,128)S(1)} custom-call(bf16[4,256,256]{2,1,0:T(8,128)(2,1)S(1)} %get-tuple-element.35.rounded_ref, bf16[512,512]{1,0:T(8,128)(2,1)S(1)} %copy-done, bf16[32,144,256]{2,1,0:T(8,128)(2,1)S(1)} %get-tuple-element.29.particles), custom_call_target="tpu_custom_call" | custom-call | flops 268435456 | bytes 4292608 | tf_op jit(solution)/shard_map/pallas_call | solution.py:93
  18.8 0.8 %collective-permute-done.5.spectrum = bf16[33,16,144]{2,1,0:T(8,128)(2,1)S(1)} collective-permute-done((bf16[33,16,144]{2,1,0:T(8,128)(2,1)S(1)}, bf16[33,16,144]{2,1,0:T(8,128)(2,1)S(1)}, u32[]{:S(2)}, u32[]{:S(2)}) %collective-permute-start.5) | collective-permute-done | bytes 152096 | tf_op jit(solution)/shard_map/ppermute | solution.py:525
  19.6 0.5 %shard_map.85.refs_0_ = bf16[272,128]{1,0:T(8,128)(2,1)S(1)} custom-call(f32[576,128]{1,0:T(8,128)S(1)} %shard_map.84.image, bf16[33,16,144]{2,1,0:T(8,128)(2,1)S(1)} %get-tuple-element.36.mine, bf16[33,16,144]{2,1,0:T(8,128)(2,1)S(1)} %collective-permute-done.5.spectrum, bf16[32,144,256]{2,1,0:T(8,128)(2,1)S(1)} %get-tuple-element.27.refs_5_.particles), custom_call_target="tpu_custom_call" | custom-call | flops 311427072 | bytes 3559424 | tf_op jit(solution)/shard_map/pallas_call | solution.py:93
  20.1 1.3 %collective-permute-start.8 = (bf16[272,128]{1,0:T(8,128)(2,1)S(1)}, bf16[272,128]{1,0:T(8,128)(2,1)S(1)}, u32[]{:S(2)}, u32[]{:S(2)}) collective-permute-start(bf16[272,128]{1,0:T(8,128)(2,1)S(1)} %shard_map.85.refs_0_), channel_id=1, source_target_pairs={{0,8},{4,12},{8,0},{12,4},{1,9},{5,13},{9,1},{13,5},{2,10},{6,14},... | collective-permute-start | bytes 208904 | tf_op jit(solution)/shard_map/ppermute | solution.py:525
  21.4 0.9 %collective-permute-start.7 = (bf16[272,128]{1,0:T(8,128)(2,1)S(1)}, bf16[272,128]{1,0:T(8,128)(2,1)S(1)}, u32[]{:S(2)}, u32[]{:S(2)}) collective-permute-start(bf16[272,128]{1,0:T(8,128)(2,1)S(1)} %shard_map.85.refs_0_), channel_id=1, source_target_pairs={{0,12},{4,8},{8,4},{12,0},{1,13},{5,9},{9,5},{13,1},{2,14},{6,10},... | collective-permute-start | bytes 208904 | tf_op jit(solution)/shard_map/ppermute | solution.py:525
  22.3 1.3 %collective-permute-start.6 = (bf16[272,128]{1,0:T(8,128)(2,1)S(1)}, bf16[272,128]{1,0:T(8,128)(2,1)S(1)}, u32[]{:S(2)}, u32[]{:S(2)}) collective-permute-start(bf16[272,128]{1,0:T(8,128)(2,1)S(1)} %shard_map.85.refs_0_), channel_id=1, source_target_pairs={{0,4},{4,0},{8,12},{12,8},{1,5},{5,1},{9,13},{13,9},{2,6},{6,2},{1... | collective-permute-start | bytes 208904 | tf_op jit(solution)/shard_map/ppermute | solution.py:525
  23.7 3.6 %collective-permute-done.8.refs_3_ = bf16[272,128]{1,0:T(8,128)(2,1)S(1)} collective-permute-done((bf16[272,128]{1,0:T(8,128)(2,1)S(1)}, bf16[272,128]{1,0:T(8,128)(2,1)S(1)}, u32[]{:S(2)}, u32[]{:S(2)}) %collective-permute-start.8) | collective-permute-done | bytes 69664 | tf_op jit(solution)/shard_map/ppermute | solution.py:525
  27.3 0.6 %collective-permute-done.7.refs_2_ = bf16[272,128]{1,0:T(8,128)(2,1)S(1)} collective-permute-done((bf16[272,128]{1,0:T(8,128)(2,1)S(1)}, bf16[272,128]{1,0:T(8,128)(2,1)S(1)}, u32[]{:S(2)}, u32[]{:S(2)}) %collective-permute-start.7) | collective-permute-done | bytes 69664 | tf_op jit(solution)/shard_map/ppermute | solution.py:525
  28.0 1.2 %collective-permute-done.6.refs_1_ = bf16[272,128]{1,0:T(8,128)(2,1)S(1)} collective-permute-done((bf16[272,128]{1,0:T(8,128)(2,1)S(1)}, bf16[272,128]{1,0:T(8,128)(2,1)S(1)}, u32[]{:S(2)}, u32[]{:S(2)}) %collective-permute-start.6) | collective-permute-done | bytes 69664 | tf_op jit(solution)/shard_map/ppermute | solution.py:525
  29.1 0.9 %shard_map.86 = (f32[648,128]{1,0:T(8,128)S(1)}, f32[4,256]{1,0:T(4,128)S(1)}, bf16[32,16,256]{2,1,0:T(8,128)(2,1)S(1)}) custom-call(bf16[272,128]{1,0:T(8,128)(2,1)S(1)} %shard_map.85.refs_0_, bf16[272,128]{1,0:T(8,128)(2,1)S(1)} %collective-permute-done.6.refs_1_, bf16[272,128]{1,0:T(8,128)(2,1)S(1)} %collective-permute-done.7.refs_2_, ...), custom_call_target="tpu_custom_call" | custom-call | flops 150994944 | bytes 3850240 | tf_op jit(solution)/shard_map/pallas_call | solution.py:93
  30.1 0.7 %shard_map.87.own = f32[2,576,128]{2,1,0:T(8,128)S(1)} custom-call(bf16[32,16,256]{2,1,0:T(8,128)(2,1)S(1)} %get-tuple-element.37.left_ref, bf16[32,144,256]{2,1,0:T(8,128)(2,1)S(1)} %get-tuple-element.29.particles), custom_call_target="tpu_custom_call" | custom-call | flops 301989888 | bytes 3211264 | tf_op jit(solution)/shard_map/pallas_call | solution.py:93
  30.8 0.9 %collective-permute-done.9.other = f32[648,128]{1,0:T(8,128)S(1)} collective-permute-done((f32[648,128]{1,0:T(8,128)S(1)}, f32[648,128]{1,0:T(8,128)S(1)}, u32[]{:S(2)}, u32[]{:S(2)}) %collective-permute-start.9) | collective-permute-done | bytes 331808 | tf_op jit(solution)/shard_map/ppermute | solution.py:525
  31.7 0.8 %shard_map.88 = (f32[4,256,256]{2,1,0:T(8,128)S(1)}, f32[4,256]{1,0:T(4,128)S(1)}, f32[8,256]{1,0:T(8,128)S(1)}) custom-call(f32[2,576,128]{2,1,0:T(8,128)S(1)} %shard_map.87.own, f32[648,128]{1,0:T(8,128)S(1)} %collective-permute-done.9.other, f32[4,256]{1,0:T(4,128)S(1)} %get-tuple-element.39.energy_ref, f32[256,256]{1,0:T(8,128)S(1)} %shard_map.81.prior_term, ...), custom_call_target="tpu_custom_call" | custom-call | flops 402653184 | bytes 3072000 | tf_op jit(solution)/shard_map/pallas_call | solution.py:93
  32.5 1.5 %collective-permute-start.10 = (f32[8,256]{1,0:T(8,128)S(1)}, f32[8,256]{1,0:T(8,128)S(1)}, u32[]{:S(2)}, u32[]{:S(2)}) collective-permute-start(f32[8,256]{1,0:T(8,128)S(1)} %get-tuple-element.42.first), channel_id=1, source_target_pairs={{0,2},{2,0},{1,3},{3,1},{4,6},{6,4},{5,7},{7,5},{8,10},{10,8},{9,1... | collective-permute-start | bytes 24584 | tf_op jit(solution)/shard_map/ppermute | solution.py:525
  34.0 2.2 %collective-permute-done.10.second = f32[8,256]{1,0:T(8,128)S(1)} collective-permute-done((f32[8,256]{1,0:T(8,128)S(1)}, f32[8,256]{1,0:T(8,128)S(1)}, u32[]{:S(2)}, u32[]{:S(2)}) %collective-permute-start.10) | collective-permute-done | bytes 8224 | tf_op jit(solution)/shard_map/ppermute | solution.py:525
  36.7 0.7 %shard_map.90.image = f32[576,128]{1,0:T(8,128)S(1)} custom-call(bf16[4,256,256]{2,1,0:T(8,128)(2,1)S(1)} %get-tuple-element.43.rounded_ref, bf16[512,512]{1,0:T(8,128)(2,1)S(1)} %copy-done, bf16[32,144,256]{2,1,0:T(8,128)(2,1)S(1)} %get-tuple-element.29.particles), custom_call_target="tpu_custom_call" | custom-call | flops 268435456 | bytes 4292608 | tf_op jit(solution)/shard_map/pallas_call | solution.py:93
  37.4 0.8 %collective-permute-done.11.spectrum = bf16[33,16,144]{2,1,0:T(8,128)(2,1)S(1)} collective-permute-done((bf16[33,16,144]{2,1,0:T(8,128)(2,1)S(1)}, bf16[33,16,144]{2,1,0:T(8,128)(2,1)S(1)}, u32[]{:S(2)}, u32[]{:S(2)}) %collective-permute-start.11) | collective-permute-done | bytes 152096 | tf_op jit(solution)/shard_map/ppermute | solution.py:525
  38.7 1.9 %collective-permute-start.12 = (f32[72,128]{1,0:T(8,128)S(1)}, f32[72,128]{1,0:T(8,128)S(1)}, u32[]{:S(2)}, u32[]{:S(2)}) collective-permute-start(f32[72,128]{1,0:T(8,128)S(1)} %get-tuple-element.45), channel_id=1, source_target_pairs={{0,8},{4,12},{8,0},{12,4},{1,9},{5,13},{9,1},{13,5},{2,10},{6,14},... | collective-permute-start | bytes 110600 | tf_op jit(solution)/shard_map/ppermute | solution.py:525
  40.6 1.2 %collective-permute-start.13 = (f32[72,128]{1,0:T(8,128)S(1)}, f32[72,128]{1,0:T(8,128)S(1)}, u32[]{:S(2)}, u32[]{:S(2)}) collective-permute-start(f32[72,128]{1,0:T(8,128)S(1)} %get-tuple-element.46), channel_id=1, source_target_pairs={{0,12},{4,8},{8,4},{12,0},{1,13},{5,9},{9,5},{13,1},{2,14},{6,10},... | collective-permute-start | bytes 110600 | tf_op jit(solution)/shard_map/ppermute | solution.py:525
  42.3 2.1 %collective-permute-done.12.refs_0_ = f32[72,128]{1,0:T(8,128)S(1)} collective-permute-done((f32[72,128]{1,0:T(8,128)S(1)}, f32[72,128]{1,0:T(8,128)S(1)}, u32[]{:S(2)}, u32[]{:S(2)}) %collective-permute-start.12) | collective-permute-done | bytes 36896 | tf_op jit(solution)/shard_map/ppermute | solution.py:525
  44.4 2.0 %collective-permute-done.13.refs_1_ = f32[72,128]{1,0:T(8,128)S(1)} collective-permute-done((f32[72,128]{1,0:T(8,128)S(1)}, f32[72,128]{1,0:T(8,128)S(1)}, u32[]{:S(2)}, u32[]{:S(2)}) %collective-permute-start.13) | collective-permute-done | bytes 36896 | tf_op jit(solution)/shard_map/ppermute | solution.py:525
  46.4 0.6 %shard_map.92 = (f32[1,64,128]{2,1,0:T(8,128)}, f32[1,144]{1,0:T(1,128)}) custom-call(f32[72,128]{1,0:T(8,128)S(1)} %collective-permute-done.12.refs_0_, f32[72,128]{1,0:T(8,128)S(1)} %collective-permute-done.13.refs_1_, f32[72,128]{1,0:T(8,128)S(1)} %collective-permute-done.14.refs_2_, f32[72,128]{1,0:T(8,128)S(1)} %get-tuple-element.48.refs_3_, ...), custom_call_target="tpu_custom_call" | custom-call | bytes 229376 | tf_op jit(solution)/shard_map/pallas_call | solution.py:93
  (26 shorter events, 2.6 us)
Async XLA Ops:
  0.6 5.7 %copy-start.5 = (bf16[288,64,128]{2,1,0:T(8,128)(2,1)S(1)}, bf16[288,64,128]{2,1,0:T(8,128)(2,1)}, u32[]{:S(2)}) copy-start(bf16[288,64,128]{2,1,0:T(8,128)(2,1)} %particles_ref.1) | copy-start | bytes 14155780
  0.6 7.2 %collective-permute-start.1 = (bf16[1,64,128]{2,1,0:T(8,128)(2,1)}, bf16[1,64,128]{2,1,0:T(8,128)(2,1)S(1)}, u32[]{:S(2)}, u32[]{:S(2)}) collective-permute-start(bf16[1,64,128]{2,1,0:T(8,128)(2,1)} %refs_0_.1), channel_id=1, source_target_pairs={{0,8},{4,12},{8,0},{12,4},{1,9},{5,13},{9,1},{13,5},{2,10},{6,14},... | collective-permute-start | bytes 49160 | tf_op jit(solution)/shard_map/ppermute | solution.py:525
  4.7 5.7 %collective-permute-start = (bf16[1,64,128]{2,1,0:T(8,128)(2,1)}, bf16[1,64,128]{2,1,0:T(8,128)(2,1)S(1)}, u32[]{:S(2)}, u32[]{:S(2)}) collective-permute-start(bf16[1,64,128]{2,1,0:T(8,128)(2,1)} %refs_0_.1), channel_id=1, source_target_pairs={{0,12},{4,8},{8,4},{12,0},{1,13},{5,9},{9,5},{13,1},{2,14},{6,10},... | collective-permute-start | bytes 49160 | tf_op jit(solution)/shard_map/ppermute | solution.py:525
  6.1 4.4 %collective-permute-start.2 = (bf16[1,64,128]{2,1,0:T(8,128)(2,1)}, bf16[1,64,128]{2,1,0:T(8,128)(2,1)S(1)}, u32[]{:S(2)}, u32[]{:S(2)}) collective-permute-start(bf16[1,64,128]{2,1,0:T(8,128)(2,1)} %refs_0_.1), channel_id=1, source_target_pairs={{0,4},{4,0},{8,12},{12,8},{1,5},{5,1},{9,13},{13,9},{2,6},{6,2},{1... | collective-permute-start | bytes 49160 | tf_op jit(solution)/shard_map/ppermute | solution.py:525
  6.4 4.1 %copy-start.2 = (bf16[1,64,128]{2,1,0:T(8,128)(2,1)S(1)}, bf16[1,64,128]{2,1,0:T(8,128)(2,1)}, u32[]{:S(2)}) copy-start(bf16[1,64,128]{2,1,0:T(8,128)(2,1)} %refs_0_.1) | copy-start | bytes 49156
  6.4 4.1 %copy-start.4 = (f32[64]{0:T(128)S(1)}, f32[64]{0:T(128)}, u32[]{:S(2)}) copy-start(f32[64]{0:T(128)} %param.8) | copy-start | bytes 772
  7.8 3.7 %copy-start.3 = (s32[288]{0:T(512)S(1)}, s32[288]{0:T(512)}, u32[]{:S(2)}) copy-start(s32[288]{0:T(512)} %prior_ref.1) | copy-start | bytes 3460
  10.5 2.6 %copy-start.1 = (bf16[512,768]{1,0:T(8,128)(2,1)S(1)}, bf16[512,768]{1,0:T(8,128)(2,1)}, u32[]{:S(2)}) copy-start(bf16[512,768]{1,0:T(8,128)(2,1)} %constant.4.clone.inverse) | copy-start | bytes 2359300
  11.4 1.6 %collective-permute-start.3 = (f32[648,128]{1,0:T(8,128)S(1)}, f32[648,128]{1,0:T(8,128)S(1)}, u32[]{:S(2)}, u32[]{:S(2)}) collective-permute-start(f32[648,128]{1,0:T(8,128)S(1)} %get-tuple-element.30), channel_id=1, source_target_pairs={{0,1},{1,0},{2,3},{3,2},{4,5},{5,4},{6,7},{7,6},{8,9},{9,8},{10,11... | collective-permute-start | bytes 995336 | tf_op jit(solution)/shard_map/ppermute | solution.py:525
  11.7 5.9 %copy-start = (bf16[512,512]{1,0:T(8,128)(2,1)S(1)}, bf16[512,512]{1,0:T(8,128)(2,1)}, u32[]{:S(2)}) copy-start(bf16[512,512]{1,0:T(8,128)(2,1)} %constant.5.clone.forward) | copy-start | bytes 1572868
  13.9 3.7 %collective-permute-start.4 = (f32[8,256]{1,0:T(8,128)S(1)}, f32[8,256]{1,0:T(8,128)S(1)}, u32[]{:S(2)}, u32[]{:S(2)}) collective-permute-start(f32[8,256]{1,0:T(8,128)S(1)} %get-tuple-element.34.first), channel_id=1, source_target_pairs={{0,2},{2,0},{1,3},{3,1},{4,6},{6,4},{5,7},{7,5},{8,10},{10,8},{9,1... | collective-permute-start | bytes 24584 | tf_op jit(solution)/shard_map/ppermute | solution.py:525
  18.0 1.6 %collective-permute-start.5 = (bf16[33,16,144]{2,1,0:T(8,128)(2,1)S(1)}, bf16[33,16,144]{2,1,0:T(8,128)(2,1)S(1)}, u32[]{:S(2)}, u32[]{:S(2)}) collective-permute-start(bf16[33,16,144]{2,1,0:T(8,128)(2,1)S(1)} %get-tuple-element.36.mine), channel_id=1, source_target_pairs={{0,1},{1,0},{2,3},{3,2},{4,5},{5,4},{6,7},{7,6},{8,9},{9,8},{10,11... | collective-permute-start | bytes 456200 | tf_op jit(solution)/shard_map/ppermute | solution.py:525
  20.1 7.2 %collective-permute-start.8 = (bf16[272,128]{1,0:T(8,128)(2,1)S(1)}, bf16[272,128]{1,0:T(8,128)(2,1)S(1)}, u32[]{:S(2)}, u32[]{:S(2)}) collective-permute-start(bf16[272,128]{1,0:T(8,128)(2,1)S(1)} %shard_map.85.refs_0_), channel_id=1, source_target_pairs={{0,8},{4,12},{8,0},{12,4},{1,9},{5,13},{9,1},{13,5},{2,10},{6,14},... | collective-permute-start | bytes 208904 | tf_op jit(solution)/shard_map/ppermute | solution.py:525
  21.4 6.5 %collective-permute-start.7 = (bf16[272,128]{1,0:T(8,128)(2,1)S(1)}, bf16[272,128]{1,0:T(8,128)(2,1)S(1)}, u32[]{:S(2)}, u32[]{:S(2)}) collective-permute-start(bf16[272,128]{1,0:T(8,128)(2,1)S(1)} %shard_map.85.refs_0_), channel_id=1, source_target_pairs={{0,12},{4,8},{8,4},{12,0},{1,13},{5,9},{9,5},{13,1},{2,14},{6,10},... | collective-permute-start | bytes 208904 | tf_op jit(solution)/shard_map/ppermute | solution.py:525
  22.3 6.8 %collective-permute-start.6 = (bf16[272,128]{1,0:T(8,128)(2,1)S(1)}, bf16[272,128]{1,0:T(8,128)(2,1)S(1)}, u32[]{:S(2)}, u32[]{:S(2)}) collective-permute-start(bf16[272,128]{1,0:T(8,128)(2,1)S(1)} %shard_map.85.refs_0_), channel_id=1, source_target_pairs={{0,4},{4,0},{8,12},{12,8},{1,5},{5,1},{9,13},{13,9},{2,6},{6,2},{1... | collective-permute-start | bytes 208904 | tf_op jit(solution)/shard_map/ppermute | solution.py:525
  30.1 1.6 %collective-permute-start.9 = (f32[648,128]{1,0:T(8,128)S(1)}, f32[648,128]{1,0:T(8,128)S(1)}, u32[]{:S(2)}, u32[]{:S(2)}) collective-permute-start(f32[648,128]{1,0:T(8,128)S(1)} %get-tuple-element.38), channel_id=1, source_target_pairs={{0,1},{1,0},{2,3},{3,2},{4,5},{5,4},{6,7},{7,6},{8,9},{9,8},{10,11... | collective-permute-start | bytes 995336 | tf_op jit(solution)/shard_map/ppermute | solution.py:525
  32.5 3.7 %collective-permute-start.10 = (f32[8,256]{1,0:T(8,128)S(1)}, f32[8,256]{1,0:T(8,128)S(1)}, u32[]{:S(2)}, u32[]{:S(2)}) collective-permute-start(f32[8,256]{1,0:T(8,128)S(1)} %get-tuple-element.42.first), channel_id=1, source_target_pairs={{0,2},{2,0},{1,3},{3,1},{4,6},{6,4},{5,7},{7,5},{8,10},{10,8},{9,1... | collective-permute-start | bytes 24584 | tf_op jit(solution)/shard_map/ppermute | solution.py:525
  36.6 1.6 %collective-permute-start.11 = (bf16[33,16,144]{2,1,0:T(8,128)(2,1)S(1)}, bf16[33,16,144]{2,1,0:T(8,128)(2,1)S(1)}, u32[]{:S(2)}, u32[]{:S(2)}) collective-permute-start(bf16[33,16,144]{2,1,0:T(8,128)(2,1)S(1)} %get-tuple-element.44.mine), channel_id=1, source_target_pairs={{0,1},{1,0},{2,3},{3,2},{4,5},{5,4},{6,7},{7,6},{8,9},{9,8},{10,11... | collective-permute-start | bytes 456200 | tf_op jit(solution)/shard_map/ppermute | solution.py:525
  38.7 5.6 %collective-permute-start.12 = (f32[72,128]{1,0:T(8,128)S(1)}, f32[72,128]{1,0:T(8,128)S(1)}, u32[]{:S(2)}, u32[]{:S(2)}) collective-permute-start(f32[72,128]{1,0:T(8,128)S(1)} %get-tuple-element.45), channel_id=1, source_target_pairs={{0,8},{4,12},{8,0},{12,4},{1,9},{5,13},{9,1},{13,5},{2,10},{6,14},... | collective-permute-start | bytes 110600 | tf_op jit(solution)/shard_map/ppermute | solution.py:525
  40.6 5.8 %collective-permute-start.13 = (f32[72,128]{1,0:T(8,128)S(1)}, f32[72,128]{1,0:T(8,128)S(1)}, u32[]{:S(2)}, u32[]{:S(2)}) collective-permute-start(f32[72,128]{1,0:T(8,128)S(1)} %get-tuple-element.46), channel_id=1, source_target_pairs={{0,12},{4,8},{8,4},{12,0},{1,13},{5,9},{9,5},{13,1},{2,14},{6,10},... | collective-permute-start | bytes 110600 | tf_op jit(solution)/shard_map/ppermute | solution.py:525
  41.8 4.6 %collective-permute-start.14 = (f32[72,128]{1,0:T(8,128)S(1)}, f32[72,128]{1,0:T(8,128)S(1)}, u32[]{:S(2)}, u32[]{:S(2)}) collective-permute-start(f32[72,128]{1,0:T(8,128)S(1)} %get-tuple-element.47), channel_id=1, source_target_pairs={{0,4},{4,0},{8,12},{12,8},{1,5},{5,1},{9,13},{13,9},{2,6},{6,2},{1... | collective-permute-start | bytes 110600 | tf_op jit(solution)/shard_map/ppermute | solution.py:525

commit v13 on v12

--- a/solution.py
+++ b/solution.py
@@ -107,18 +107,37 @@
     out[...] = ((to // 16 == at % 16) & (to % 16 == at // 16)).astype(F32).astype(BF16)
 
 
-def prior_kernel(prior_ref, prior_term):
-    turns = lax.broadcasted_iota(jnp.int32, prior_term.shape, 0)
-    lane = lax.broadcasted_iota(jnp.int32, (1, prior_term.shape[1]), 1)
+def prior_kernel(share, prior_ref, prior_term):
+    turns = lax.broadcasted_iota(jnp.int32, (ANG, 256), 0)
+    lane = lax.broadcasted_iota(jnp.int32, (1, 256), 1)
     priors = prior_ref[...].reshape(1, -1)
-    half = priors.shape[1] // 2
     first, second = [
-        jnp.concatenate([priors[:, i * half : (i + 1) * half], lane[:, half:]], 1)
+        jnp.concatenate([priors[:, i * share : (i + 1) * share], lane[:, share:]], 1)
         for i in range(2)
     ]
     offset = jnp.abs(turns - jnp.where(lax.axis_index("rot") == 0, first, second))
     distance = jnp.minimum(offset, ANG - offset).astype(F32)
-    prior_term[...] = -distance * distance / (2.0 * SIGMA * SIGMA)
+    term = -distance * distance / (2.0 * SIGMA * SIGMA)
+    prior_term[:, :128] = term[:, :128]
+    prior_term[:, 128:] = repeat(term[:, 128:], share - 128, 128 // (share - 128))
+
+
+def turned(value, lanes):
+    return pltpu.roll(value, lanes % 128, 1) if lanes % 128 else value
+
+
+def repeat(value, width, times):
+    lane = lax.broadcasted_iota(jnp.int32, value.shape, 1)
+    value = jnp.where(lane < width, value, 0.0)
+    return sum(turned(value, i * width) for i in range(times))
+
+
+def layout(classes, share):
+    width = share - 128
+    assert 0 < width < 128 and 128 % width == 0 and classes % 2 == 0
+    bundle = min(128 // width, classes)
+    assert classes % bundle == 0
+    return width, bundle, classes // bundle
 
 
 def prep_kernel(share, particles_ref, permutation_ref, other, own):
@@ -164,10 +183,10 @@
 
 def weigh_kernel(fresh, order, count, *refs):
     sources = [refs[order.index(i)] for i in range(count)]
-    doubled_ref, particles, out, energy_ref, left_ref, image, *rest = refs[count:]
+    doubled_ref, particles, out, energy_ref, left_ref, image, rest = refs[count:]
     pairs, share, twice = particles.shape
     freqs, depth = 2 * pairs, twice // 2
-    classes, lanes = energy_ref.shape
+    classes = energy_ref.shape[0]
     pitch = freqs + SPARE
     radii = depth // 2
     lane = lax.broadcasted_iota(jnp.int32, (freqs, depth), 1)
@@ -192,9 +211,9 @@
         image[rows(2 * k * pitch, freqs), :] = weighted
         image[rows((2 * k + 1) * pitch, freqs), :] = sign * pltpu.roll(weighted, radii, 1)
         energy = jnp.sum(plain * plain * scale, axis=0, keepdims=True)
-        energy = jnp.broadcast_to(jnp.sum(energy, axis=1, keepdims=True), (SPARE, lanes))
+        energy = jnp.broadcast_to(jnp.sum(energy, axis=1, keepdims=True), (SPARE, 128))
         energy_ref[pl.ds(k, 1), :] = energy[:1]
-        out[rows(2 * k * pitch + freqs, SPARE), :] = energy[:, : out.shape[1]]
+        out[rows(2 * k * pitch + freqs, SPARE), :] = energy
 
     none = jnp.zeros((2 * classes, depth), BF16)
 
@@ -207,135 +226,178 @@
             [jnp.concatenate([first, none], 1), jnp.concatenate([none, second], 1)], 0
         )
         left_ref[f] = left
-        place([out, *rest], f, times(left, particles[f]), classes, pitch)
+        place(out, rest, f, times(left, particles[f]), classes, pitch)
 
     loop(pairs, correlate, 32)
-    for ref in rest:
-        width = share - 128
-        for pack in range(-(-2 * classes * width // 128)):
-            total = 0.0
-            for i in range(min(128 // width, 2 * classes - pack * (128 // width))):
-                group = ref[rows((pack * (128 // width) + i) * pitch, pitch), :]
-                total = total + (pltpu.roll(group, i * width, 1) if i else group)
-            out[rows((2 * classes + pack) * pitch, pitch), :] = total
+    pack(out, rest, classes, share, pitch)
 
 
 def times(left, particles):
     return lax.dot_general(left, particles, (((1,), (1,)), ((), ())), preferred_element_type=F32)
 
 
-def place(outs, f, value, classes, pitch):
-    spare = jnp.zeros((value.shape[0], len(outs) * 128 - value.shape[1]), F32)
-    value = jnp.concatenate([value, spare], 1) if spare.size else value
+def place(out, rest, f, value, classes, pitch):
+    width = value.shape[1] - 128
+    spare = jnp.zeros((value.shape[0], 128 - width), F32)
+    value = jnp.concatenate([value, spare], 1)
     for part in range(2):
         at = pl.ds(2 * f + part, 2 * classes, stride=pitch)
-        for tile, out in enumerate(outs):
-            out[at, :] = value[
-                part * 2 * classes : (part + 1) * 2 * classes, tile * 128 : (tile + 1) * 128
-            ]
-
-
-def lane_tiles(share):
-    return -(-share // 128)
+        mine = value[part * 2 * classes : (part + 1) * 2 * classes]
+        out[at, :] = mine[:, :128]
+        rest[at, :] = mine[:, 128:]
+
+
+def pack(out, rest, classes, share, pitch):
+    width = share - 128
+    each_pack = 128 // width
+    for first in range(0, 2 * classes, each_pack):
+        total = 0.0
+        for group in range(first, min(first + each_pack, 2 * classes)):
+            part, k = divmod(group, classes)
+            value = rest[rows((2 * k + part) * pitch, pitch), :]
+            total = total + turned(value, (group - first) * width)
+        out[rows((2 * classes + first // each_pack) * pitch, pitch), :] = total
+
+
+def unpack(ref, unit, part, classes, share, pitch, freqs):
+    width, bundle, _ = layout(classes, share)
+    group = part * classes + unit * bundle
+    each_pack = 128 // width
+    value = ref[rows((2 * classes + group // each_pack) * pitch, freqs), :]
+    return turned(value, -(group % each_pack) * width)
+
+
+def corr_lines(classes, share, pitch):
+    return (2 * classes + -(-2 * classes * (share - 128) // 128)) * pitch
 
 
 def weigh(sources, order, inverse_noise, particles, fresh):
     pairs, share, twice = particles.shape
     classes = len(sources)
     pitch = 2 * pairs + SPARE
-    tiles = lane_tiles(share)
-    assert tiles == 1 or tiles == 2 and 128 % (share - 128) == 0
-    packs = -(-2 * classes * (share - 128) // 128) if tiles == 2 else 0
     return call(
         functools.partial(weigh_kernel, fresh, order, classes),
         [*[sources[i] for i in order], inverse_noise, particles],
         [
-            (((2 * classes + packs) * pitch, 128), F32),
-            ((classes, tiles * 128), F32),
+            ((corr_lines(classes, share, pitch), 128), F32),
+            ((classes, 128), F32),
             ((pairs, 4 * classes, twice), BF16),
         ],
-        [((2 * classes * pitch, twice // 2), F32)]
-        + [((2 * classes * pitch, 128), F32)] * (tiles - 1),
+        [((2 * classes * pitch, twice // 2), F32), ((2 * classes * pitch, 128), F32)],
         flops=8 * classes * share * pairs * twice * 4,
     )
 
 
-def correlate_kernel(left_ref, particles, out):
-    pairs = left_ref.shape[0]
+def correlate_kernel(left_ref, particles, out, rest):
+    pairs, share, _ = particles.shape
     classes = left_ref.shape[1] // 4
+    pitch = 2 * pairs + SPARE
 
     def body(f):
-        outs = [out.at[tile] for tile in range(out.shape[0])]
-        place(outs, f, times(left_ref[f], particles[f]), classes, 2 * pairs + SPARE)
+        place(out, rest, f, times(left_ref[f], particles[f]), classes, pitch)
 
     loop(pairs, body, 32)
+    pack(out, rest, classes, share, pitch)
 
 
 def correlate(left, particles):
     pairs, share, twice = particles.shape
-    lines = left.shape[1] // 2 * (2 * pairs + SPARE)
+    classes = left.shape[1] // 4
+    pitch = 2 * pairs + SPARE
     return call(
         correlate_kernel,
         [left, particles],
-        [((lane_tiles(share), lines, 128), F32)],
+        [((corr_lines(classes, share, pitch), 128), F32)],
+        [((2 * classes * pitch, 128), F32)],
         flops=2 * left.shape[1] * share * pairs * twice * 8,
     )[0]
 
 
-def across(ref, at):
-    return jnp.concatenate([ref[tile, at, :] for tile in range(ref.shape[0])], 1)
-
-
 def table_rows(base, count):
     return pl.ds(pl.multiple_of(lax.axis_index("rot") * ANG + base, 128), count)
 
 
-def score_kernel(particles, own, other, energy_ref, prior_term, inverse, *refs):
-    weights, tops, peaks = refs
-    classes, share = energy_ref.shape
-    tiles, lines, width = own.shape
-    pitch = lines // (2 * classes)
-    freqs = pitch - SPARE
-    which = table_rows(0, ANG)
-
-    def unpacked(group):
-        first = other[rows(group * pitch, freqs), :]
-        if tiles == 1:
-            return first
-        width = particles - 128
-        bundle = 128 // width
-        packed = other[rows((2 * classes + group // bundle) * pitch, freqs), :]
-        back = (bundle - group % bundle) % bundle * width
-        return jnp.concatenate([first, pltpu.roll(packed, back, 1)], 1)
-
-    def score(k, carry):
-        near = [across(own, rows((2 * k + part) * pitch, freqs)) for part in range(2)]
-        far = [unpacked(2 * k + part) for part in range(2)]
-        high, low = split(jnp.concatenate(near + far, 0))
-        inner = dot(inverse[which, :], jnp.concatenate([high, low, high], 0))
-        far = other[rows(2 * k * pitch + freqs, SPARE), :][:1]
-        energy = energy_ref[pl.ds(k, 1), :] + jnp.concatenate([far] * tiles, 1)
-        scores = inner - 0.5 * energy + prior_term[...]
+def score_kernel(share, own, other, energy_ref, prior_term, inverse, *refs):
+    weights, more, tops, more_tops, peaks = refs
+    classes = energy_ref.shape[0]
+    width, bundle, units = layout(classes, share)
+    freqs = ANG // 4
+    pitch = freqs + SPARE
+    at = table_rows(0, ANG)
+    lane = lax.broadcasted_iota(jnp.int32, (1, 128), 1)
+
+    def exponentials(value, energy, prior):
+        high, low = split(value)
+        inner = dot(inverse[at, :], jnp.concatenate([high, low, high], 0))
+        scores = inner - 0.5 * energy + prior
         top = jnp.max(scores, axis=0, keepdims=True)
         value = jnp.exp(scores - top)
-        weights[k] = value
-        total = jnp.sum(value, axis=0, keepdims=True)
-        tops[pl.ds(k, 1), :] = top
-        return merge(carry, (top, total))
-
-    first = (jnp.full((1, share), -jnp.inf, F32), jnp.zeros((1, share), F32))
-    top, total = each(classes, score, first)
+        return value, top, jnp.sum(value, axis=0, keepdims=True)
+
+    def energy_of(k):
+        return energy_ref[pl.ds(k, 1), :] + other[rows(2 * k * pitch + freqs, SPARE), :][:1]
+
+    def slab(i, carry):
+        value = jnp.concatenate(
+            [
+                jnp.concatenate(
+                    [ref[rows((4 * i + 2 * j + part) * pitch, freqs), :] for j in range(2)], 1
+                )
+                for ref in (own, other)
+                for part in range(2)
+            ],
+            0,
+        )
+        energy = jnp.concatenate([energy_of(2 * i), energy_of(2 * i + 1)], 1)
+        prior = jnp.concatenate([prior_term[:, :128]] * 2, 1)
+        weights[i], top, total = exponentials(value, energy, prior)
+        tops[pl.ds(i, 1), :] = top
+        for j in (0, 128):
+            carry = merge(carry, (top[:, j : j + 128], total[:, j : j + 128]))
+        return carry
+
+    empty = (jnp.full((1, 128), -jnp.inf, F32), jnp.zeros((1, 128), F32))
+    top, total = each(classes // 2, slab, empty)
+    rest = empty
+    for unit in range(units):
+        value = jnp.concatenate(
+            [
+                unpack(ref, unit, part, classes, share, pitch, freqs)
+                for ref in (own, other)
+                for part in range(2)
+            ],
+            0,
+        )
+        energy = sum(
+            jnp.where(lane // width == j, energy_of(unit * bundle + j), 0.0)
+            for j in range(bundle)
+        )
+        more[unit], more_top, more_total = exponentials(value, energy, prior_term[:, 128:])
+        more_tops[pl.ds(unit, 1), :] = more_top
+        for j in range(bundle):
+            rest = merge(rest, (turned(more_top, -j * width), turned(more_total, -j * width)))
     line = lax.broadcasted_iota(jnp.int32, peaks.shape, 0)
-    peaks[...] = jnp.where(line == 0, top, total)
-
-
-def scores(own, other, energy, prior_term, inverse, particles):
-    classes, lanes = energy.shape
+    peaks[...] = jnp.where(
+        line == 0,
+        jnp.concatenate([top, rest[0]], 1),
+        jnp.concatenate([total, rest[1]], 1),
+    )
+
+
+def scores(own, other, energy, prior_term, inverse, share):
+    classes = energy.shape[0]
+    units = layout(classes, share)[2]
     return call(
-        functools.partial(score_kernel, particles),
+        functools.partial(score_kernel, share),
         [own, other, energy, prior_term, inverse],
-        [((classes, ANG, lanes), F32), ((classes, lanes), F32), ((8, lanes), F32)],
-        flops=6 * classes * lanes * ANG * ANG,
+        [
+            ((classes // 2, ANG, 256), F32),
+            ((units, ANG, 128), F32),
+            ((classes // 2, 256), F32),
+            ((units, 128), F32),
+            ((8, 256), F32),
+        ],
+        flops=6 * classes * 256 * ANG * ANG,
     )
 
 
@@ -354,98 +416,152 @@
     out[...] = jnp.where(line == 0, top, total)
 
 
-def turn_kernel(share, weights, tops, first, second, forward, *refs):
-    rounded_ref, send, *evidence_ref, held = refs
-    classes, _, lanes = weights.shape
-    pairs = (held.shape[1] // (2 * classes) - SPARE) // 2
+def turn_kernel(share, weights, more, tops, more_tops, first, second, forward, *refs):
+    rounded_ref, rounded_more, send, *evidence_ref, held = refs
+    classes = 2 * weights.shape[0]
+    width, bundle, units = layout(classes, share)
+    pairs = (held.shape[0] // (2 * classes) - SPARE) // 2
     top, total = merge(two_lines(first), two_lines(second))
     for ref in evidence_ref:
         ref[...] = (top + jnp.log(total))[:, :share]
-    lane = lax.broadcasted_iota(jnp.int32, (1, lanes), 1)
-    inverse_total = jnp.where(lane < share, 1.0 / total, 0.0)
-    which = table_rows(0, ANG // 2)
-    line = lax.broadcasted_iota(jnp.int32, (4 * classes, share), 0)
-
-    def body(k, column):
-        value = weights[k] * (jnp.exp(tops[pl.ds(k, 1), :] - top) * inverse_total)
-        count = jnp.sum(jnp.sum(value, axis=0, keepdims=True), axis=1, keepdims=True)
-        rounded = value.astype(BF16)
-        rounded_ref[k] = rounded
-        spread(held, k, dot(forward[which, :], jnp.concatenate([rounded, rounded], 0)))
+    scale = 1.0 / total
+    at = table_rows(0, ANG // 2)
+    lane = lax.broadcasted_iota(jnp.int32, (1, 128), 1)
+    line = lax.broadcasted_iota(jnp.int32, (4 * classes, 128), 0)
+
+    def put(column, k, count):
         high = count.astype(BF16).astype(F32)
         return jnp.where(line == k, high, jnp.where(line == classes + k, count - high, column))
 
-    column = each(classes, body, jnp.zeros((4 * classes, share), F32))
-    send[pairs] = column.astype(BF16)
+    more_counts = []
+    for unit in range(units):
+        factor = jnp.exp(
+            more_tops[pl.ds(unit, 1), :] - repeat(top[:, 128:], width, bundle)
+        ) * repeat(scale[:, 128:], width, bundle)
+        value = more[unit] * jnp.where(lane < bundle * width, factor, 0.0)
+        count = jnp.sum(value, axis=0, keepdims=True)
+        for j in range(bundle):
+            mine = jnp.where(lane // width == j, count, 0.0)
+            more_counts.append(jnp.sum(mine, axis=1, keepdims=True))
+        rounded = value.astype(BF16)
+        rounded_more[unit] = rounded
+        spectrum = dot(forward[at, :], jnp.concatenate([rounded, rounded], 0)).astype(BF16)
+        step = 4 * classes
+        entries = spectrum.shape[0] // step
+        for i in range(entries):
+            send[pairs + unit * entries + i] = spectrum[i * step : (i + 1) * step]
+
+    tops_here = jnp.concatenate([top[:, :128]] * 2, 1)
+    scale_here = jnp.concatenate([scale[:, :128]] * 2, 1)
+
+    def body(i, column):
+        value = weights[i] * (jnp.exp(tops[pl.ds(i, 1), :] - tops_here) * scale_here)
+        rounded = value.astype(BF16)
+        rounded_ref[i] = rounded
+        spread(held, i, dot(forward[at, :], jnp.concatenate([rounded, rounded], 0)))
+        count = jnp.sum(value, axis=0, keepdims=True)
+        for j in range(2):
+            mine = jnp.sum(count[:, j * 128 : (j + 1) * 128], axis=1, keepdims=True)
+            column = put(column, 2 * i + j, mine)
+        return column
+
+    column = each(classes // 2, body, jnp.zeros((4 * classes, 128), F32))
+    extra = jnp.zeros((4 * classes, 128), F32)
+    for k, count in enumerate(more_counts):
+        extra = put(extra, k, count)
+    send[send.shape[0] - 2] = column.astype(BF16)
+    send[send.shape[0] - 1] = extra.astype(BF16)
 
     def rearrange(f):
-        send[f] = pick(held, f, classes, share)
+        send[f] = pick(held, f, classes).astype(BF16)
 
     loop(pairs, rearrange, 32)
 
 
-def spread(held, k, value):
-    tiles, lines, width = held.shape
+def spread(held, i, value):
     freqs = value.shape[0] // 2
-    for part in range(2):
-        for tile in range(tiles):
-            held[tile, rows((2 * k + part) * (freqs + SPARE), freqs), :] = value[
-                part * freqs : (part + 1) * freqs, tile * width : (tile + 1) * width
+    for j in range(2):
+        for part in range(2):
+            held[rows((4 * i + 2 * j + part) * (freqs + SPARE), freqs), :] = value[
+                part * freqs : (part + 1) * freqs, j * 128 : (j + 1) * 128
             ]
 
 
-def pick(held, f, classes, share):
-    pitch = held.shape[1] // (2 * classes)
-    parts = [
-        across(held, pl.ds(2 * f + part, 2 * classes, stride=pitch)).astype(BF16)
-        for part in range(2)
-    ]
-    return jnp.concatenate(parts, 0)[:, :share]
-
-
-def turn(weights, tops, first, second, forward, freqs, share, last):
-    classes, _, lanes = weights.shape
+def spread_more(held, unit, value, classes, share):
+    width, bundle, _ = layout(classes, share)
+    freqs = value.shape[0] // 2
+    for j in range(bundle):
+        shifted = turned(value, -j * width)
+        for part in range(2):
+            k = unit * bundle + j
+            held[rows((2 * k + part) * (freqs + SPARE), freqs), :] = shifted[
+                part * freqs : (part + 1) * freqs
+            ]
+
+
+def pick(held, f, classes):
+    pitch = held.shape[0] // (2 * classes)
+    return jnp.concatenate(
+        [held[pl.ds(2 * f + part, 2 * classes, stride=pitch), :] for part in range(2)], 0
+    )
+
+
+def message_shape(classes, pairs, units):
+    return (pairs + units * (ANG // 2) // (4 * classes) + 2, 4 * classes, 128)
+
+
+def turn(weights, more, tops, more_tops, first, second, forward, freqs, share, last):
+    classes = 2 * weights.shape[0]
+    units = more.shape[0]
     return call(
         functools.partial(turn_kernel, share),
-        [weights, tops, first, second, forward],
+        [weights, more, tops, more_tops, first, second, forward],
         [
-            ((classes, ANG, lanes), BF16),
-            ((freqs // 2 + 1, 4 * classes, share), BF16),
+            (weights.shape, BF16),
+            (more.shape, BF16),
+            (message_shape(classes, freqs // 2, units), BF16),
             *([((1, share), F32)] if last else []),
         ],
-        [((lanes // 128, 2 * classes * (freqs + SPARE), 128), F32)],
-        flops=4 * classes * lanes * ANG * ANG,
-    )
-
-
-def gather_kernel(rounded_ref, forward, particles, image, held):
-    classes = rounded_ref.shape[0]
+        [((2 * classes * (freqs + SPARE), 128), F32)],
+        flops=4 * classes * 256 * ANG * ANG,
+    )
+
+
+def gather_kernel(rounded_ref, rounded_more, forward, particles, image, held, held_more):
+    classes = 2 * rounded_ref.shape[0]
     pairs, share, _ = particles.shape
-    which = table_rows(ANG // 2, ANG // 2)
-
-    def body(k, carry):
-        rounded = rounded_ref[k]
-        spread(held, k, dot(forward[which, :], jnp.concatenate([rounded, rounded], 0)))
+    at = table_rows(ANG // 2, ANG // 2)
+
+    for unit in range(rounded_more.shape[0]):
+        rounded = rounded_more[unit]
+        value = dot(forward[at, :], jnp.concatenate([rounded, rounded], 0))
+        spread_more(held_more, unit, value, classes, share)
+
+    def body(i, carry):
+        rounded = rounded_ref[i]
+        spread(held, i, dot(forward[at, :], jnp.concatenate([rounded, rounded], 0)))
         return carry
 
-    each(classes, body, 0)
+    each(classes // 2, body, 0)
 
     def accumulate(f):
-        take_in(image, f, dot(pick(held, f, classes, share), particles[f]), classes)
+        left = [pick(ref, f, classes).astype(BF16) for ref in (held, held_more)]
+        left = jnp.concatenate(left, 1)[:, :share]
+        take_in(image, f, dot(left, particles[f]), classes)
 
     loop(pairs, accumulate, 32)
 
 
-def gather(rounded, forward, particles):
+def gather(rounded, rounded_more, forward, particles):
     pairs, share, twice = particles.shape
-    classes, _, lanes = rounded.shape
+    classes = 2 * rounded.shape[0]
     lines = 2 * classes * (2 * pairs + SPARE)
     return call(
         gather_kernel,
-        [rounded, forward, particles],
+        [rounded, rounded_more, forward, particles],
         [((lines, twice // 2), F32)],
-        [((lanes // 128, lines, 128), F32)],
-        flops=4 * classes * lanes * ANG * ANG,
+        [((lines, 128), F32)] * 2,
+        flops=4 * classes * 256 * ANG * ANG,
     )[0]
 
 
@@ -459,18 +575,27 @@
 
 
 def finish_kernel(image, mine, spectrum, particles, *refs):
-    outs, held = refs[:-1], refs[-1]
-    pairs, _, twice = particles.shape
+    *outs, held, held_more = refs
+    pairs, share, twice = particles.shape
     classes = spectrum.shape[1] // 4
     freqs, depth = 2 * pairs, twice // 2
     radii = depth // 2
     pitch = freqs + SPARE
 
+    units = layout(classes, share)[2]
+    entries = ANG // 2 // (4 * classes)
+    for unit in range(units):
+        first = pairs + unit * entries
+        value = jnp.concatenate([spectrum[first + i] for i in range(entries)], 0)
+        spread_more(held_more, unit, value.astype(F32), classes, share)
+
     def body(f):
-        take_in(held, f, dot(spectrum[f], particles[f]), classes)
+        left = jnp.concatenate([spectrum[f], pick(held_more, f, classes).astype(BF16)], 1)
+        take_in(held, f, dot(left[:, :share], particles[f]), classes)
 
     loop(pairs, body, 32)
-    counts = (mine[pairs].astype(F32) + spectrum[pairs].astype(F32))[:, :depth]
+    end = spectrum.shape[0]
+    counts = sum(ref[i].astype(F32) for ref in (mine, spectrum) for i in (end - 2, end - 1))
     counts = counts[:classes] + counts[classes : 2 * classes]
     lane = lax.broadcasted_iota(jnp.int32, (freqs, depth), 1)
     sign = jnp.where(lane < radii, -1.0, 1.0).astype(F32)
@@ -506,7 +631,7 @@
         finish_kernel,
         [image, mine, spectrum, particles],
         outs,
-        [(image.shape, F32)],
+        [(image.shape, F32)] * 2,
         flops=2 * math.prod(spectrum.shape) * twice * 8,
     )
 
@@ -544,7 +669,7 @@
 
     (permutation,) = call(permutation_kernel, [], [((256, 256), BF16)], flops=1 << 32)
     (prior_term,) = call(
-        prior_kernel, [prior_rot], [((ANG, lane_tiles(share) * 128), F32)], flops=1 << 26
+        functools.partial(prior_kernel, share), [prior_rot], [((ANG, 256), F32)], flops=1 << 26
     )
     sources = {i: swap(references, "blk", blocks, i) for i in (*turns, 0)}
     other_images, own_images = prep(particles, permutation, share)
@@ -554,17 +679,17 @@
         message, energy, left = weigh(sources, order, inverse_noise, other_images, step == 0)
         message = swap(message, "rot", groups, 1)
         own = correlate(left, own_images)
-        weights, tops, here = scores(own, message, energy, prior_term, inverse, share)
+        *weights, here = scores(own, message, energy, prior_term, inverse, share)
         first = here
         for bit in bits(sides):
             second = swap(first, "cls", sides, bit)
             if 2 * bit < sides:
                 (first,) = call(merge_kernel, [first, second], [(here.shape, F32)])
-        rounded, send, *evidence = turn(
-            weights, tops, first, second, forward, freqs, share, last
+        rounded, more, send, *evidence = turn(
+            *weights, first, second, forward, freqs, share, last
         )
         message = swap(send, "rot", groups, 1)
-        image = gather(rounded, forward, own_images)
+        image = gather(rounded, more, forward, own_images)
         sums = finish(image, send, message, other_images, last)
         sums = sums if last else sums * blocks
         sources = {i: swap(sums[i], "blk", blocks, i) for i in (*turns, 0)}

time: 47.2 us -> 46.6 us (0.987)
  waiting for transfers between devices: 19.8 us -> 19.1 us
    ppermute x15, waiting for transfers between devices: 19.8 us -> 19.1 us  [swap(): return lax.ppermute(value, axis, [(i, i ^ bit) for i in range(size)])]
where the time goes in v13:
time: 46.6 us; the launch traced here: 46.5 us
  waiting for transfers between devices  19.1 us (41%)
  starting transfers between devices  16 us (34%)
  Pallas kernels  10.5 us (23%)
  between operations  0.79 us (2%)
    ppermute x15, waiting for transfers between devices, swap(): return lax.ppermute(value, axis, [(i, i ^ bit) for i in range(size)])  19.1 us
    ppermute x15, starting transfers between devices, swap(): return lax.ppermute(value, axis, [(i, i ^ bit) for i in range(size)])  16 us
    pallas_call x16, Pallas kernels, call(): pl.pallas_call(kernel, out_shape=[jax.ShapeDtypeStruct(*x) for x in outs]...  10.5 us
  transfers between devices with their start and end apart: 15, of which 12 were waited for; matrix products, arithmetic and copies ran while one was open for 0% of the time, Pallas kernels for 10%

profile of v13, /device:TPU:0, one launch (start us, length us, event | category | flops | bytes accessed | tf_op | source)
XLA Modules:
  0.0 46.5 jit_solution(15237731949441943417)
XLA Ops:
  0.6 4.1 %collective-permute-start.1 = (bf16[1,64,128]{2,1,0:T(8,128)(2,1)}, bf16[1,64,128]{2,1,0:T(8,128)(2,1)S(1)}, u32[]{:S(2)}, u32[]{:S(2)}) collective-permute-start(bf16[1,64,128]{2,1,0:T(8,128)(2,1)} %refs_0_.1), channel_id=1, source_target_pairs={{0,8},{4,12},{8,0},{12,4},{1,9},{5,13},{9,1},{13,5},{2,10},{6,14},... | collective-permute-start | bytes 49160 | tf_op jit(solution)/shard_map/ppermute | solution.py:650
  4.7 1.3 %collective-permute-start = (bf16[1,64,128]{2,1,0:T(8,128)(2,1)}, bf16[1,64,128]{2,1,0:T(8,128)(2,1)S(1)}, u32[]{:S(2)}, u32[]{:S(2)}) collective-permute-start(bf16[1,64,128]{2,1,0:T(8,128)(2,1)} %refs_0_.1), channel_id=1, source_target_pairs={{0,12},{4,8},{8,4},{12,0},{1,13},{5,9},{9,5},{13,1},{2,14},{6,10},... | collective-permute-start | bytes 49160 | tf_op jit(solution)/shard_map/ppermute | solution.py:650
  6.4 1.4 %shard_map.78 = (bf16[32,144,256]{2,1,0:T(8,128)(2,1)S(1)}, bf16[32,144,256]{2,1,0:T(8,128)(2,1)S(1)}) custom-call(bf16[288,64,128]{2,1,0:T(8,128)(2,1)S(1)} %copy-done.5, bf16[256,256]{1,0:T(8,128)(2,1)S(1)} %shard_map.77.permutation_ref), custom_call_target="tpu_custom_call" | custom-call | flops 2147483648 | bytes 9568256 | tf_op jit(solution)/shard_map/pallas_call | solution.py:93
  7.8 2.7 %collective-permute-done.refs_1_ = bf16[1,64,128]{2,1,0:T(8,128)(2,1)S(1)} collective-permute-done((bf16[1,64,128]{2,1,0:T(8,128)(2,1)}, bf16[1,64,128]{2,1,0:T(8,128)(2,1)S(1)}, u32[]{:S(2)}, u32[]{:S(2)}) %collective-permute-start) | collective-permute-done | bytes 16416 | tf_op jit(solution)/shard_map/ppermute | solution.py:650
  10.5 0.9 %shard_map.79 = (f32[648,128]{1,0:T(8,128)S(1)}, f32[4,128]{1,0:T(4,128)S(1)}, bf16[32,16,256]{2,1,0:T(8,128)(2,1)S(1)}) custom-call(bf16[1,64,128]{2,1,0:T(8,128)(2,1)S(1)} %copy-done.2, bf16[1,64,128]{2,1,0:T(8,128)(2,1)S(1)} %collective-permute-done.refs_1_, bf16[1,64,128]{2,1,0:T(8,128)(2,1)S(1)} %collective-permute-done.1.refs_2_, ...), custom_call_target="tpu_custom_call" | custom-call | flops 150994944 | bytes 3629056 | tf_op jit(solution)/shard_map/pallas_call | solution.py:93
  11.9 0.8 %shard_map.80.own = f32[648,128]{1,0:T(8,128)S(1)} custom-call(bf16[32,16,256]{2,1,0:T(8,128)(2,1)S(1)} %get-tuple-element.34.left_ref, bf16[32,144,256]{2,1,0:T(8,128)(2,1)S(1)} %get-tuple-element.35.particles), custom_call_target="tpu_custom_call" | custom-call | flops 301989888 | bytes 3252224 | tf_op jit(solution)/shard_map/pallas_call | solution.py:93
  13.1 0.6 %shard_map.82 = (f32[2,256,256]{2,1,0:T(8,128)S(1)}, f32[1,256,128]{2,1,0:T(8,128)S(1)}, f32[2,256]{1,0:T(2,128)S(1)}, f32[1,128]{1,0:T(1,128)S(1)}, f32[8,256]{1,0:T(8,128)S(1)}) custom-call(f32[648,128]{1,0:T(8,128)S(1)} %shard_map.80.own, f32[648,128]{1,0:T(8,128)S(1)} %collective-permute-done.3.other, f32[4,128]{1,0:T(4,128)S(1)} %get-tuple-element.37.energy_ref, ...), custom_call_target="tpu_custom_call" | custom-call | flops 402653184 | bytes 2424832 | tf_op jit(solution)/shard_map/pallas_call | solution.py:93
  13.7 1.5 %collective-permute-start.4 = (f32[8,256]{1,0:T(8,128)S(1)}, f32[8,256]{1,0:T(8,128)S(1)}, u32[]{:S(2)}, u32[]{:S(2)}) collective-permute-start(f32[8,256]{1,0:T(8,128)S(1)} %get-tuple-element.42.first), channel_id=1, source_target_pairs={{0,2},{2,0},{1,3},{3,1},{4,6},{6,4},{5,7},{7,5},{8,10},{10,8},{9,1... | collective-permute-start | bytes 24584 | tf_op jit(solution)/shard_map/ppermute | solution.py:650
  15.3 2.2 %collective-permute-done.4.second = f32[8,256]{1,0:T(8,128)S(1)} collective-permute-done((f32[8,256]{1,0:T(8,128)S(1)}, f32[8,256]{1,0:T(8,128)S(1)}, u32[]{:S(2)}, u32[]{:S(2)}) %collective-permute-start.4) | collective-permute-done | bytes 8224 | tf_op jit(solution)/shard_map/ppermute | solution.py:650
  17.9 0.7 %shard_map.84.image = f32[576,128]{1,0:T(8,128)S(1)} custom-call(bf16[2,256,256]{2,1,0:T(8,128)(2,1)S(1)} %get-tuple-element.43.rounded_ref, bf16[1,256,128]{2,1,0:T(8,128)(2,1)S(1)} %get-tuple-element.44.rounded_more, bf16[512,512]{1,0:T(8,128)(2,1)S(1)} %copy-done, bf16[32,144,256]{2,1,0:T(8,128)(2,1)S(1)} %get-tuple-element.35.particles), custom_call_target="tpu_custom_call" | custom-call | flops 268435456 | bytes 4096000 | tf_op jit(solution)/shard_map/pallas_call | solution.py:93
  18.6 0.7 %collective-permute-done.5.spectrum = bf16[42,16,128]{2,1,0:T(8,128)(2,1)S(1)} collective-permute-done((bf16[42,16,128]{2,1,0:T(8,128)(2,1)S(1)}, bf16[42,16,128]{2,1,0:T(8,128)(2,1)S(1)}, u32[]{:S(2)}, u32[]{:S(2)}) %collective-permute-start.5) | collective-permute-done | bytes 172064 | tf_op jit(solution)/shard_map/ppermute | solution.py:650
  19.3 0.6 %shard_map.85.refs_0_ = bf16[272,128]{1,0:T(8,128)(2,1)S(1)} custom-call(f32[576,128]{1,0:T(8,128)S(1)} %shard_map.84.image, bf16[42,16,128]{2,1,0:T(8,128)(2,1)S(1)} %get-tuple-element.45.mine, bf16[42,16,128]{2,1,0:T(8,128)(2,1)S(1)} %collective-permute-done.5.spectrum, bf16[32,144,256]{2,1,0:T(8,128)(2,1)S(1)} %get-tuple-element.33.refs_5_.particles), custom_call_target="tpu_custom_call" | custom-call | flops 352321536 | bytes 3657728 | tf_op jit(solution)/shard_map/pallas_call | solution.py:93
  19.9 1.3 %collective-permute-start.8 = (bf16[272,128]{1,0:T(8,128)(2,1)S(1)}, bf16[272,128]{1,0:T(8,128)(2,1)S(1)}, u32[]{:S(2)}, u32[]{:S(2)}) collective-permute-start(bf16[272,128]{1,0:T(8,128)(2,1)S(1)} %shard_map.85.refs_0_), channel_id=1, source_target_pairs={{0,8},{4,12},{8,0},{12,4},{1,9},{5,13},{9,1},{13,5},{2,10},{6,14},... | collective-permute-start | bytes 208904 | tf_op jit(solution)/shard_map/ppermute | solution.py:650
  21.1 0.9 %collective-permute-start.7 = (bf16[272,128]{1,0:T(8,128)(2,1)S(1)}, bf16[272,128]{1,0:T(8,128)(2,1)S(1)}, u32[]{:S(2)}, u32[]{:S(2)}) collective-permute-start(bf16[272,128]{1,0:T(8,128)(2,1)S(1)} %shard_map.85.refs_0_), channel_id=1, source_target_pairs={{0,12},{4,8},{8,4},{12,0},{1,13},{5,9},{9,5},{13,1},{2,14},{6,10},... | collective-permute-start | bytes 208904 | tf_op jit(solution)/shard_map/ppermute | solution.py:650
  22.1 1.4 %collective-permute-start.6 = (bf16[272,128]{1,0:T(8,128)(2,1)S(1)}, bf16[272,128]{1,0:T(8,128)(2,1)S(1)}, u32[]{:S(2)}, u32[]{:S(2)}) collective-permute-start(bf16[272,128]{1,0:T(8,128)(2,1)S(1)} %shard_map.85.refs_0_), channel_id=1, source_target_pairs={{0,4},{4,0},{8,12},{12,8},{1,5},{5,1},{9,13},{13,9},{2,6},{6,2},{1... | collective-permute-start | bytes 208904 | tf_op jit(solution)/shard_map/ppermute | solution.py:650
  23.4 3.6 %collective-permute-done.8.refs_3_ = bf16[272,128]{1,0:T(8,128)(2,1)S(1)} collective-permute-done((bf16[272,128]{1,0:T(8,128)(2,1)S(1)}, bf16[272,128]{1,0:T(8,128)(2,1)S(1)}, u32[]{:S(2)}, u32[]{:S(2)}) %collective-permute-start.8) | collective-permute-done | bytes 69664 | tf_op jit(solution)/shard_map/ppermute | solution.py:650
  27.0 0.6 %collective-permute-done.7.refs_2_ = bf16[272,128]{1,0:T(8,128)(2,1)S(1)} collective-permute-done((bf16[272,128]{1,0:T(8,128)(2,1)S(1)}, bf16[272,128]{1,0:T(8,128)(2,1)S(1)}, u32[]{:S(2)}, u32[]{:S(2)}) %collective-permute-start.7) | collective-permute-done | bytes 69664 | tf_op jit(solution)/shard_map/ppermute | solution.py:650
  27.7 1.2 %collective-permute-done.6.refs_1_ = bf16[272,128]{1,0:T(8,128)(2,1)S(1)} collective-permute-done((bf16[272,128]{1,0:T(8,128)(2,1)S(1)}, bf16[272,128]{1,0:T(8,128)(2,1)S(1)}, u32[]{:S(2)}, u32[]{:S(2)}) %collective-permute-start.6) | collective-permute-done | bytes 69664 | tf_op jit(solution)/shard_map/ppermute | solution.py:650
  28.9 0.9 %shard_map.86 = (f32[648,128]{1,0:T(8,128)S(1)}, f32[4,128]{1,0:T(4,128)S(1)}, bf16[32,16,256]{2,1,0:T(8,128)(2,1)S(1)}) custom-call(bf16[272,128]{1,0:T(8,128)(2,1)S(1)} %shard_map.85.refs_0_, bf16[272,128]{1,0:T(8,128)(2,1)S(1)} %collective-permute-done.6.refs_1_, bf16[272,128]{1,0:T(8,128)(2,1)S(1)} %collective-permute-done.7.refs_2_, ...), custom_call_target="tpu_custom_call" | custom-call | flops 150994944 | bytes 3842048 | tf_op jit(solution)/shard_map/pallas_call | solution.py:93
  29.8 0.8 %shard_map.87.own = f32[648,128]{1,0:T(8,128)S(1)} custom-call(bf16[32,16,256]{2,1,0:T(8,128)(2,1)S(1)} %get-tuple-element.46.left_ref, bf16[32,144,256]{2,1,0:T(8,128)(2,1)S(1)} %get-tuple-element.35.particles), custom_call_target="tpu_custom_call" | custom-call | flops 301989888 | bytes 3252224 | tf_op jit(solution)/shard_map/pallas_call | solution.py:93
  30.6 0.8 %collective-permute-done.9.other = f32[648,128]{1,0:T(8,128)S(1)} collective-permute-done((f32[648,128]{1,0:T(8,128)S(1)}, f32[648,128]{1,0:T(8,128)S(1)}, u32[]{:S(2)}, u32[]{:S(2)}) %collective-permute-start.9) | collective-permute-done | bytes 331808 | tf_op jit(solution)/shard_map/ppermute | solution.py:650
  31.4 0.7 %shard_map.88 = (f32[2,256,256]{2,1,0:T(8,128)S(1)}, f32[1,256,128]{2,1,0:T(8,128)S(1)}, f32[2,256]{1,0:T(2,128)S(1)}, f32[1,128]{1,0:T(1,128)S(1)}, f32[8,256]{1,0:T(8,128)S(1)}) custom-call(f32[648,128]{1,0:T(8,128)S(1)} %shard_map.87.own, f32[648,128]{1,0:T(8,128)S(1)} %collective-permute-done.9.other, f32[4,128]{1,0:T(4,128)S(1)} %get-tuple-element.48.energy_ref, ...), custom_call_target="tpu_custom_call" | custom-call | flops 402653184 | bytes 2424832 | tf_op jit(solution)/shard_map/pallas_call | solution.py:93
  32.1 1.5 %collective-permute-start.10 = (f32[8,256]{1,0:T(8,128)S(1)}, f32[8,256]{1,0:T(8,128)S(1)}, u32[]{:S(2)}, u32[]{:S(2)}) collective-permute-start(f32[8,256]{1,0:T(8,128)S(1)} %get-tuple-element.53.first), channel_id=1, source_target_pairs={{0,2},{2,0},{1,3},{3,1},{4,6},{6,4},{5,7},{7,5},{8,10},{10,8},{9,1... | collective-permute-start | bytes 24584 | tf_op jit(solution)/shard_map/ppermute | solution.py:650
  33.6 2.2 %collective-permute-done.10.second = f32[8,256]{1,0:T(8,128)S(1)} collective-permute-done((f32[8,256]{1,0:T(8,128)S(1)}, f32[8,256]{1,0:T(8,128)S(1)}, u32[]{:S(2)}, u32[]{:S(2)}) %collective-permute-start.10) | collective-permute-done | bytes 8224 | tf_op jit(solution)/shard_map/ppermute | solution.py:650
  36.2 0.7 %shard_map.90.image = f32[576,128]{1,0:T(8,128)S(1)} custom-call(bf16[2,256,256]{2,1,0:T(8,128)(2,1)S(1)} %get-tuple-element.54.rounded_ref, bf16[1,256,128]{2,1,0:T(8,128)(2,1)S(1)} %get-tuple-element.55.rounded_more, bf16[512,512]{1,0:T(8,128)(2,1)S(1)} %copy-done, bf16[32,144,256]{2,1,0:T(8,128)(2,1)S(1)} %get-tuple-element.35.particles), custom_call_target="tpu_custom_call" | custom-call | flops 268435456 | bytes 4096000 | tf_op jit(solution)/shard_map/pallas_call | solution.py:93
  36.9 0.7 %collective-permute-done.11.spectrum = bf16[42,16,128]{2,1,0:T(8,128)(2,1)S(1)} collective-permute-done((bf16[42,16,128]{2,1,0:T(8,128)(2,1)S(1)}, bf16[42,16,128]{2,1,0:T(8,128)(2,1)S(1)}, u32[]{:S(2)}, u32[]{:S(2)}) %collective-permute-start.11) | collective-permute-done | bytes 172064 | tf_op jit(solution)/shard_map/ppermute | solution.py:650
  37.6 0.6 %shard_map.91 = (f32[72,128]{1,0:T(8,128)S(1)}, f32[72,128]{1,0:T(8,128)S(1)}, f32[72,128]{1,0:T(8,128)S(1)}, f32[72,128]{1,0:T(8,128)S(1)}) custom-call(f32[576,128]{1,0:T(8,128)S(1)} %shard_map.90.image, bf16[42,16,128]{2,1,0:T(8,128)(2,1)S(1)} %get-tuple-element.56.mine, bf16[42,16,128]{2,1,0:T(8,128)(2,1)S(1)} %collective-permute-done.11.spectrum, ...), custom_call_target="tpu_custom_call" | custom-call | flops 352321536 | bytes 3751936 | tf_op jit(solution)/shard_map/pallas_call | solution.py:93
  38.2 1.9 %collective-permute-start.12 = (f32[72,128]{1,0:T(8,128)S(1)}, f32[72,128]{1,0:T(8,128)S(1)}, u32[]{:S(2)}, u32[]{:S(2)}) collective-permute-start(f32[72,128]{1,0:T(8,128)S(1)} %get-tuple-element.57), channel_id=1, source_target_pairs={{0,8},{4,12},{8,0},{12,4},{1,9},{5,13},{9,1},{13,5},{2,10},{6,14},... | collective-permute-start | bytes 110600 | tf_op jit(solution)/shard_map/ppermute | solution.py:650
  40.1 1.2 %collective-permute-start.13 = (f32[72,128]{1,0:T(8,128)S(1)}, f32[72,128]{1,0:T(8,128)S(1)}, u32[]{:S(2)}, u32[]{:S(2)}) collective-permute-start(f32[72,128]{1,0:T(8,128)S(1)} %get-tuple-element.58), channel_id=1, source_target_pairs={{0,12},{4,8},{8,4},{12,0},{1,13},{5,9},{9,5},{13,1},{2,14},{6,10},... | collective-permute-start | bytes 110600 | tf_op jit(solution)/shard_map/ppermute | solution.py:650
  41.8 2.1 %collective-permute-done.12.refs_0_ = f32[72,128]{1,0:T(8,128)S(1)} collective-permute-done((f32[72,128]{1,0:T(8,128)S(1)}, f32[72,128]{1,0:T(8,128)S(1)}, u32[]{:S(2)}, u32[]{:S(2)}) %collective-permute-start.12) | collective-permute-done | bytes 36896 | tf_op jit(solution)/shard_map/ppermute | solution.py:650
  43.8 2.0 %collective-permute-done.13.refs_1_ = f32[72,128]{1,0:T(8,128)S(1)} collective-permute-done((f32[72,128]{1,0:T(8,128)S(1)}, f32[72,128]{1,0:T(8,128)S(1)}, u32[]{:S(2)}, u32[]{:S(2)}) %collective-permute-start.13) | collective-permute-done | bytes 36896 | tf_op jit(solution)/shard_map/ppermute | solution.py:650
  45.8 0.6 %shard_map.92 = (f32[1,64,128]{2,1,0:T(8,128)}, f32[1,144]{1,0:T(1,128)}) custom-call(f32[72,128]{1,0:T(8,128)S(1)} %collective-permute-done.12.refs_0_, f32[72,128]{1,0:T(8,128)S(1)} %collective-permute-done.13.refs_1_, f32[72,128]{1,0:T(8,128)S(1)} %collective-permute-done.14.refs_2_, f32[72,128]{1,0:T(8,128)S(1)} %get-tuple-element.60.refs_3_, ...), custom_call_target="tpu_custom_call" | custom-call | bytes 229376 | tf_op jit(solution)/shard_map/pallas_call | solution.py:93
  (26 shorter events, 2.5 us)
Async XLA Ops:
  0.6 5.7 %copy-start.5 = (bf16[288,64,128]{2,1,0:T(8,128)(2,1)S(1)}, bf16[288,64,128]{2,1,0:T(8,128)(2,1)}, u32[]{:S(2)}) copy-start(bf16[288,64,128]{2,1,0:T(8,128)(2,1)} %particles_ref.1) | copy-start | bytes 14155780
  0.6 7.2 %collective-permute-start.1 = (bf16[1,64,128]{2,1,0:T(8,128)(2,1)}, bf16[1,64,128]{2,1,0:T(8,128)(2,1)S(1)}, u32[]{:S(2)}, u32[]{:S(2)}) collective-permute-start(bf16[1,64,128]{2,1,0:T(8,128)(2,1)} %refs_0_.1), channel_id=1, source_target_pairs={{0,8},{4,12},{8,0},{12,4},{1,9},{5,13},{9,1},{13,5},{2,10},{6,14},... | collective-permute-start | bytes 49160 | tf_op jit(solution)/shard_map/ppermute | solution.py:650
  4.7 5.7 %collective-permute-start = (bf16[1,64,128]{2,1,0:T(8,128)(2,1)}, bf16[1,64,128]{2,1,0:T(8,128)(2,1)S(1)}, u32[]{:S(2)}, u32[]{:S(2)}) collective-permute-start(bf16[1,64,128]{2,1,0:T(8,128)(2,1)} %refs_0_.1), channel_id=1, source_target_pairs={{0,12},{4,8},{8,4},{12,0},{1,13},{5,9},{9,5},{13,1},{2,14},{6,10},... | collective-permute-start | bytes 49160 | tf_op jit(solution)/shard_map/ppermute | solution.py:650
  6.1 4.4 %collective-permute-start.2 = (bf16[1,64,128]{2,1,0:T(8,128)(2,1)}, bf16[1,64,128]{2,1,0:T(8,128)(2,1)S(1)}, u32[]{:S(2)}, u32[]{:S(2)}) collective-permute-start(bf16[1,64,128]{2,1,0:T(8,128)(2,1)} %refs_0_.1), channel_id=1, source_target_pairs={{0,4},{4,0},{8,12},{12,8},{1,5},{5,1},{9,13},{13,9},{2,6},{6,2},{1... | collective-permute-start | bytes 49160 | tf_op jit(solution)/shard_map/ppermute | solution.py:650
  6.4 4.1 %copy-start.2 = (bf16[1,64,128]{2,1,0:T(8,128)(2,1)S(1)}, bf16[1,64,128]{2,1,0:T(8,128)(2,1)}, u32[]{:S(2)}) copy-start(bf16[1,64,128]{2,1,0:T(8,128)(2,1)} %refs_0_.1) | copy-start | bytes 49156
  6.4 4.1 %copy-start.4 = (f32[64]{0:T(128)S(1)}, f32[64]{0:T(128)}, u32[]{:S(2)}) copy-start(f32[64]{0:T(128)} %param.8) | copy-start | bytes 772
  7.8 3.7 %copy-start.3 = (s32[288]{0:T(512)S(1)}, s32[288]{0:T(512)}, u32[]{:S(2)}) copy-start(s32[288]{0:T(512)} %prior_ref.1) | copy-start | bytes 3460
  10.5 2.6 %copy-start.1 = (bf16[512,768]{1,0:T(8,128)(2,1)S(1)}, bf16[512,768]{1,0:T(8,128)(2,1)}, u32[]{:S(2)}) copy-start(bf16[512,768]{1,0:T(8,128)(2,1)} %constant.4.clone.inverse) | copy-start | bytes 2359300
  11.4 1.6 %collective-permute-start.3 = (f32[648,128]{1,0:T(8,128)S(1)}, f32[648,128]{1,0:T(8,128)S(1)}, u32[]{:S(2)}, u32[]{:S(2)}) collective-permute-start(f32[648,128]{1,0:T(8,128)S(1)} %get-tuple-element.36), channel_id=1, source_target_pairs={{0,1},{1,0},{2,3},{3,2},{4,5},{5,4},{6,7},{7,6},{8,9},{9,8},{10,11... | collective-permute-start | bytes 995336 | tf_op jit(solution)/shard_map/ppermute | solution.py:650
  11.9 5.5 %copy-start = (bf16[512,512]{1,0:T(8,128)(2,1)S(1)}, bf16[512,512]{1,0:T(8,128)(2,1)}, u32[]{:S(2)}) copy-start(bf16[512,512]{1,0:T(8,128)(2,1)} %constant.5.clone.forward) | copy-start | bytes 1572868
  13.7 3.7 %collective-permute-start.4 = (f32[8,256]{1,0:T(8,128)S(1)}, f32[8,256]{1,0:T(8,128)S(1)}, u32[]{:S(2)}, u32[]{:S(2)}) collective-permute-start(f32[8,256]{1,0:T(8,128)S(1)} %get-tuple-element.42.first), channel_id=1, source_target_pairs={{0,2},{2,0},{1,3},{3,1},{4,6},{6,4},{5,7},{7,5},{8,10},{10,8},{9,1... | collective-permute-start | bytes 24584 | tf_op jit(solution)/shard_map/ppermute | solution.py:650
  17.8 1.5 %collective-permute-start.5 = (bf16[42,16,128]{2,1,0:T(8,128)(2,1)S(1)}, bf16[42,16,128]{2,1,0:T(8,128)(2,1)S(1)}, u32[]{:S(2)}, u32[]{:S(2)}) collective-permute-start(bf16[42,16,128]{2,1,0:T(8,128)(2,1)S(1)} %get-tuple-element.45.mine), channel_id=1, source_target_pairs={{0,1},{1,0},{2,3},{3,2},{4,5},{5,4},{6,7},{7,6},{8,9},{9,8},{10,11... | collective-permute-start | bytes 516104 | tf_op jit(solution)/shard_map/ppermute | solution.py:650
  19.9 7.2 %collective-permute-start.8 = (bf16[272,128]{1,0:T(8,128)(2,1)S(1)}, bf16[272,128]{1,0:T(8,128)(2,1)S(1)}, u32[]{:S(2)}, u32[]{:S(2)}) collective-permute-start(bf16[272,128]{1,0:T(8,128)(2,1)S(1)} %shard_map.85.refs_0_), channel_id=1, source_target_pairs={{0,8},{4,12},{8,0},{12,4},{1,9},{5,13},{9,1},{13,5},{2,10},{6,14},... | collective-permute-start | bytes 208904 | tf_op jit(solution)/shard_map/ppermute | solution.py:650
  21.1 6.5 %collective-permute-start.7 = (bf16[272,128]{1,0:T(8,128)(2,1)S(1)}, bf16[272,128]{1,0:T(8,128)(2,1)S(1)}, u32[]{:S(2)}, u32[]{:S(2)}) collective-permute-start(bf16[272,128]{1,0:T(8,128)(2,1)S(1)} %shard_map.85.refs_0_), channel_id=1, source_target_pairs={{0,12},{4,8},{8,4},{12,0},{1,13},{5,9},{9,5},{13,1},{2,14},{6,10},... | collective-permute-start | bytes 208904 | tf_op jit(solution)/shard_map/ppermute | solution.py:650
  22.1 6.8 %collective-permute-start.6 = (bf16[272,128]{1,0:T(8,128)(2,1)S(1)}, bf16[272,128]{1,0:T(8,128)(2,1)S(1)}, u32[]{:S(2)}, u32[]{:S(2)}) collective-permute-start(bf16[272,128]{1,0:T(8,128)(2,1)S(1)} %shard_map.85.refs_0_), channel_id=1, source_target_pairs={{0,4},{4,0},{8,12},{12,8},{1,5},{5,1},{9,13},{13,9},{2,6},{6,2},{1... | collective-permute-start | bytes 208904 | tf_op jit(solution)/shard_map/ppermute | solution.py:650
  29.8 1.6 %collective-permute-start.9 = (f32[648,128]{1,0:T(8,128)S(1)}, f32[648,128]{1,0:T(8,128)S(1)}, u32[]{:S(2)}, u32[]{:S(2)}) collective-permute-start(f32[648,128]{1,0:T(8,128)S(1)} %get-tuple-element.47), channel_id=1, source_target_pairs={{0,1},{1,0},{2,3},{3,2},{4,5},{5,4},{6,7},{7,6},{8,9},{9,8},{10,11... | collective-permute-start | bytes 995336 | tf_op jit(solution)/shard_map/ppermute | solution.py:650
  32.1 3.7 %collective-permute-start.10 = (f32[8,256]{1,0:T(8,128)S(1)}, f32[8,256]{1,0:T(8,128)S(1)}, u32[]{:S(2)}, u32[]{:S(2)}) collective-permute-start(f32[8,256]{1,0:T(8,128)S(1)} %get-tuple-element.53.first), channel_id=1, source_target_pairs={{0,2},{2,0},{1,3},{3,1},{4,6},{6,4},{5,7},{7,5},{8,10},{10,8},{9,1... | collective-permute-start | bytes 24584 | tf_op jit(solution)/shard_map/ppermute | solution.py:650
  36.2 1.5 %collective-permute-start.11 = (bf16[42,16,128]{2,1,0:T(8,128)(2,1)S(1)}, bf16[42,16,128]{2,1,0:T(8,128)(2,1)S(1)}, u32[]{:S(2)}, u32[]{:S(2)}) collective-permute-start(bf16[42,16,128]{2,1,0:T(8,128)(2,1)S(1)} %get-tuple-element.56.mine), channel_id=1, source_target_pairs={{0,1},{1,0},{2,3},{3,2},{4,5},{5,4},{6,7},{7,6},{8,9},{9,8},{10,11... | collective-permute-start | bytes 516104 | tf_op jit(solution)/shard_map/ppermute | solution.py:650
  38.2 5.6 %collective-permute-start.12 = (f32[72,128]{1,0:T(8,128)S(1)}, f32[72,128]{1,0:T(8,128)S(1)}, u32[]{:S(2)}, u32[]{:S(2)}) collective-permute-start(f32[72,128]{1,0:T(8,128)S(1)} %get-tuple-element.57), channel_id=1, source_target_pairs={{0,8},{4,12},{8,0},{12,4},{1,9},{5,13},{9,1},{13,5},{2,10},{6,14},... | collective-permute-start | bytes 110600 | tf_op jit(solution)/shard_map/ppermute | solution.py:650
  40.1 5.8 %collective-permute-start.13 = (f32[72,128]{1,0:T(8,128)S(1)}, f32[72,128]{1,0:T(8,128)S(1)}, u32[]{:S(2)}, u32[]{:S(2)}) collective-permute-start(f32[72,128]{1,0:T(8,128)S(1)} %get-tuple-element.58), channel_id=1, source_target_pairs={{0,12},{4,8},{8,4},{12,0},{1,13},{5,9},{9,5},{13,1},{2,14},{6,10},... | collective-permute-start | bytes 110600 | tf_op jit(solution)/shard_map/ppermute | solution.py:650
  41.3 4.6 %collective-permute-start.14 = (f32[72,128]{1,0:T(8,128)S(1)}, f32[72,128]{1,0:T(8,128)S(1)}, u32[]{:S(2)}, u32[]{:S(2)}) collective-permute-start(f32[72,128]{1,0:T(8,128)S(1)} %get-tuple-element.59), channel_id=1, source_target_pairs={{0,4},{4,0},{8,12},{12,8},{1,5},{5,1},{9,13},{13,9},{2,6},{6,2},{1... | collective-permute-start | bytes 110600 | tf_op jit(solution)/shard_map/ppermute | solution.py:650

commit v14 on v13

--- a/solution.py
+++ b/solution.py
@@ -107,6 +107,10 @@
     out[...] = ((to // 16 == at % 16) & (to % 16 == at // 16)).astype(F32).astype(BF16)
 
 
+def half_index():
+    return lax.rem(lax.axis_index("rot") + lax.axis_index("cls"), 2)
+
+
 def prior_kernel(share, prior_ref, prior_term):
     turns = lax.broadcasted_iota(jnp.int32, (ANG, 256), 0)
     lane = lax.broadcasted_iota(jnp.int32, (1, 256), 1)
@@ -115,7 +119,7 @@
         jnp.concatenate([priors[:, i * share : (i + 1) * share], lane[:, share:]], 1)
         for i in range(2)
     ]
-    offset = jnp.abs(turns - jnp.where(lax.axis_index("rot") == 0, first, second))
+    offset = jnp.abs(turns - jnp.where(half_index() == 0, first, second))
     distance = jnp.minimum(offset, ANG - offset).astype(F32)
     term = -distance * distance / (2.0 * SIGMA * SIGMA)
     prior_term[:, :128] = term[:, :128]
@@ -142,17 +146,17 @@
 
 def prep_kernel(share, particles_ref, permutation_ref, other, own):
     freqs, depth = particles_ref.shape[1:]
-    group = lax.axis_index("rot")
+    half = half_index()
     permutation = permutation_ref[...]
-    for out, first in ((other, (1 - group) * share), (own, group * share)):
+    for out, first in ((other, (1 - half) * share), (own, half * share)):
         for p in range(0, share, 16):
             for f in range(0, freqs, 32):
                 blocks = [
                     jnp.concatenate(
-                        [particles_ref[first + p + j, pl.ds(f + half, 16), :] for j in range(16)],
+                        [particles_ref[first + p + j, pl.ds(f + second, 16), :] for j in range(16)],
                         0,
                     )
-                    for half in (0, 16)
+                    for second in (0, 16)
                 ]
                 turned = dot(permutation, jnp.concatenate(blocks, 1)).astype(BF16)
                 for half in range(2):
@@ -417,13 +421,12 @@
 
 
 def turn_kernel(share, weights, more, tops, more_tops, first, second, forward, *refs):
-    rounded_ref, rounded_more, send, *evidence_ref, held = refs
+    rounded_ref, rounded_more, send, *last, held = refs
     classes = 2 * weights.shape[0]
     width, bundle, units = layout(classes, share)
     pairs = (held.shape[0] // (2 * classes) - SPARE) // 2
     top, total = merge(two_lines(first), two_lines(second))
-    for ref in evidence_ref:
-        ref[...] = (top + jnp.log(total))[:, :share]
+    evidence = top + jnp.log(total)
     scale = 1.0 / total
     at = table_rows(0, ANG // 2)
     lane = lax.broadcasted_iota(jnp.int32, (1, 128), 1)
@@ -469,6 +472,14 @@
     extra = jnp.zeros((4 * classes, 128), F32)
     for k, count in enumerate(more_counts):
         extra = put(extra, k, count)
+    for ref in last:
+        ref[...] = evidence[:, :share]
+        high = evidence.astype(BF16).astype(F32)
+        middle = (evidence - high).astype(BF16).astype(F32)
+        for i, value in enumerate((high, middle, evidence - high - middle)):
+            for j in range(2):
+                mine = value[:, j * 128 : (j + 1) * 128]
+                extra = jnp.where(line == 2 * classes + 2 * i + j, mine, extra)
     send[send.shape[0] - 2] = column.astype(BF16)
     send[send.shape[0] - 1] = extra.astype(BF16)
 
@@ -576,6 +587,7 @@
 
 def finish_kernel(image, mine, spectrum, particles, *refs):
     *outs, held, held_more = refs
+    evidence_ref = outs.pop() if len(outs) > 1 else None
     pairs, share, twice = particles.shape
     classes = spectrum.shape[1] // 4
     freqs, depth = 2 * pairs, twice // 2
@@ -596,6 +608,10 @@
     loop(pairs, body, 32)
     end = spectrum.shape[0]
     counts = sum(ref[i].astype(F32) for ref in (mine, spectrum) for i in (end - 2, end - 1))
+    if evidence_ref is not None:
+        parts = spectrum[end - 1].astype(F32)[2 * classes :]
+        parts = [jnp.concatenate([parts[i : i + 1], parts[i + 1 : i + 2]], 1) for i in (0, 2, 4)]
+        evidence_ref[...] = (parts[0] + (parts[1] + parts[2]))[:, :share]
     counts = counts[:classes] + counts[classes : 2 * classes]
     lane = lax.broadcasted_iota(jnp.int32, (freqs, depth), 1)
     sign = jnp.where(lane < radii, -1.0, 1.0).astype(F32)
@@ -624,7 +640,7 @@
     classes = spectrum.shape[1] // 4
     freqs, depth = 2 * pairs, twice // 2
     if last:
-        outs = [((freqs + SPARE, depth), F32)] * classes
+        outs = [((freqs + SPARE, depth), F32)] * classes + [((1, particles.shape[1]), F32)]
     else:
         outs = [((classes * freqs + -(-2 * classes // 16) * 16, depth), BF16)]
     return call(
@@ -637,8 +653,9 @@
 
 
 def means_kernel(*refs):
-    *parts, evidence_ref, out, last_ref = refs
-    last_ref[...] = evidence_ref[...]
+    *parts, own, other, out, evidence_ref = refs
+    odd = lax.rem(lax.axis_index("cls"), 2)
+    evidence_ref[...] = jnp.where(odd == 0, own[...], other[...])
     freqs = out.shape[1]
     total = tree(ref[...] for ref in parts)
     out[0] = total[:freqs, :] / (total[freqs : freqs + 1, :] + shrinkage)
@@ -682,7 +699,7 @@
         *weights, here = scores(own, message, energy, prior_term, inverse, share)
         first = here
         for bit in bits(sides):
-            second = swap(first, "cls", sides, bit)
+            second = swap(first, ("cls", "rot"), sides * groups, groups * bit + (bit == 1))
             if 2 * bit < sides:
                 (first,) = call(merge_kernel, [first, second], [(here.shape, F32)])
         rounded, more, send, *evidence = turn(
@@ -691,10 +708,10 @@
         message = swap(send, "rot", groups, 1)
         image = gather(rounded, more, forward, own_images)
         sums = finish(image, send, message, other_images, last)
-        sums = sums if last else sums * blocks
+        sums, others = (sums[:blocks], sums[blocks:]) if last else (sums * blocks, [])
         sources = {i: swap(sums[i], "blk", blocks, i) for i in (*turns, 0)}
     means, evidence = call(
-        means_kernel, [*[sources[i] for i in turns], sources[0], *evidence], [((1, freqs, depth), F32), ((1, share), F32)]
+        means_kernel, [*[sources[i] for i in turns], sources[0], *evidence, *others], [((1, freqs, depth), F32), ((1, share), F32)]
     )
     return means, evidence.reshape(share)
 

time: 46.6 us -> 45.5 us (0.976)
  waiting for transfers between devices: 19.1 us -> 18.2 us
    ppermute x15, waiting for transfers between devices: 19.1 us -> 18.2 us  [swap(): return lax.ppermute(value, axis, [(i, i ^ bit) for i in range(size)])]
  transfers between devices with their start and end apart: 15 -> 15, of which waited for: 12 -> 12; matrix products, arithmetic and copies ran while one was open for 0% -> 0% of each run, Pallas kernels for 10% -> 11%
where the time goes in v14:
time: 45.5 us; the launch traced here: 45.4 us
  waiting for transfers between devices  18.2 us (40%)
  starting transfers between devices  15.8 us (35%)
  Pallas kernels  10.5 us (23%)
  between operations  0.77 us (2%)
    ppermute x15, waiting for transfers between devices, swap(): return lax.ppermute(value, axis, [(i, i ^ bit) for i in range(size)])  18.2 us
    ppermute x15, starting transfers between devices, swap(): return lax.ppermute(value, axis, [(i, i ^ bit) for i in range(size)])  15.8 us
    pallas_call x16, Pallas kernels, call(): pl.pallas_call(kernel, out_shape=[jax.ShapeDtypeStruct(*x) for x in outs]...  10.5 us
  transfers between devices with their start and end apart: 15, of which 12 were waited for; matrix products, arithmetic and copies ran while one was open for 0% of the time, Pallas kernels for 11%

profile of v14, /device:TPU:0, one launch (start us, length us, event | category | flops | bytes accessed | tf_op | source)
XLA Modules:
  0.0 45.4 jit_solution(3790621372561698239)
XLA Ops:
  0.6 4.1 %collective-permute-start.1 = (bf16[1,64,128]{2,1,0:T(8,128)(2,1)}, bf16[1,64,128]{2,1,0:T(8,128)(2,1)S(1)}, u32[]{:S(2)}, u32[]{:S(2)}) collective-permute-start(bf16[1,64,128]{2,1,0:T(8,128)(2,1)} %refs_0_.1), channel_id=1, source_target_pairs={{0,8},{4,12},{8,0},{12,4},{1,9},{5,13},{9,1},{13,5},{2,10},{6,14},... | collective-permute-start | bytes 49160 | tf_op jit(solution)/shard_map/ppermute | solution.py:667
  4.7 1.3 %collective-permute-start = (bf16[1,64,128]{2,1,0:T(8,128)(2,1)}, bf16[1,64,128]{2,1,0:T(8,128)(2,1)S(1)}, u32[]{:S(2)}, u32[]{:S(2)}) collective-permute-start(bf16[1,64,128]{2,1,0:T(8,128)(2,1)} %refs_0_.1), channel_id=1, source_target_pairs={{0,12},{4,8},{8,4},{12,0},{1,13},{5,9},{9,5},{13,1},{2,14},{6,10},... | collective-permute-start | bytes 49160 | tf_op jit(solution)/shard_map/ppermute | solution.py:667
  6.4 1.4 %shard_map.78 = (bf16[32,144,256]{2,1,0:T(8,128)(2,1)S(1)}, bf16[32,144,256]{2,1,0:T(8,128)(2,1)S(1)}) custom-call(bf16[288,64,128]{2,1,0:T(8,128)(2,1)S(1)} %copy-done.5, bf16[256,256]{1,0:T(8,128)(2,1)S(1)} %shard_map.77.permutation_ref), custom_call_target="tpu_custom_call" | custom-call | flops 2147483648 | bytes 9568256 | tf_op jit(solution)/shard_map/pallas_call | solution.py:93
  7.8 2.6 %collective-permute-done.refs_1_ = bf16[1,64,128]{2,1,0:T(8,128)(2,1)S(1)} collective-permute-done((bf16[1,64,128]{2,1,0:T(8,128)(2,1)}, bf16[1,64,128]{2,1,0:T(8,128)(2,1)S(1)}, u32[]{:S(2)}, u32[]{:S(2)}) %collective-permute-start) | collective-permute-done | bytes 16416 | tf_op jit(solution)/shard_map/ppermute | solution.py:667
  10.5 0.9 %shard_map.79 = (f32[648,128]{1,0:T(8,128)S(1)}, f32[4,128]{1,0:T(4,128)S(1)}, bf16[32,16,256]{2,1,0:T(8,128)(2,1)S(1)}) custom-call(bf16[1,64,128]{2,1,0:T(8,128)(2,1)S(1)} %copy-done.2, bf16[1,64,128]{2,1,0:T(8,128)(2,1)S(1)} %collective-permute-done.refs_1_, bf16[1,64,128]{2,1,0:T(8,128)(2,1)S(1)} %collective-permute-done.1.refs_2_, ...), custom_call_target="tpu_custom_call" | custom-call | flops 150994944 | bytes 3629056 | tf_op jit(solution)/shard_map/pallas_call | solution.py:93
  11.9 0.8 %shard_map.80.own = f32[648,128]{1,0:T(8,128)S(1)} custom-call(bf16[32,16,256]{2,1,0:T(8,128)(2,1)S(1)} %get-tuple-element.35.left_ref, bf16[32,144,256]{2,1,0:T(8,128)(2,1)S(1)} %get-tuple-element.36.particles), custom_call_target="tpu_custom_call" | custom-call | flops 301989888 | bytes 3252224 | tf_op jit(solution)/shard_map/pallas_call | solution.py:93
  13.1 0.6 %shard_map.82 = (f32[2,256,256]{2,1,0:T(8,128)S(1)}, f32[1,256,128]{2,1,0:T(8,128)S(1)}, f32[2,256]{1,0:T(2,128)S(1)}, f32[1,128]{1,0:T(1,128)S(1)}, f32[8,256]{1,0:T(8,128)S(1)}) custom-call(f32[648,128]{1,0:T(8,128)S(1)} %shard_map.80.own, f32[648,128]{1,0:T(8,128)S(1)} %collective-permute-done.3.other, f32[4,128]{1,0:T(4,128)S(1)} %get-tuple-element.38.energy_ref, ...), custom_call_target="tpu_custom_call" | custom-call | flops 402653184 | bytes 2424832 | tf_op jit(solution)/shard_map/pallas_call | solution.py:93
  13.7 1.3 %collective-permute-start.4 = (f32[8,256]{1,0:T(8,128)S(1)}, f32[8,256]{1,0:T(8,128)S(1)}, u32[]{:S(2)}, u32[]{:S(2)}) collective-permute-start(f32[8,256]{1,0:T(8,128)S(1)} %get-tuple-element.43.first), channel_id=1, source_target_pairs={{0,3},{1,2},{2,1},{3,0},{4,7},{5,6},{6,5},{7,4},{8,11},{9,10},{10,... | collective-permute-start | bytes 24584 | tf_op jit(solution)/shard_map/ppermute | solution.py:667
  15.0 1.8 %collective-permute-done.4.second = f32[8,256]{1,0:T(8,128)S(1)} collective-permute-done((f32[8,256]{1,0:T(8,128)S(1)}, f32[8,256]{1,0:T(8,128)S(1)}, u32[]{:S(2)}, u32[]{:S(2)}) %collective-permute-start.4) | collective-permute-done | bytes 8224 | tf_op jit(solution)/shard_map/ppermute | solution.py:667
  17.5 0.7 %shard_map.84.image = f32[576,128]{1,0:T(8,128)S(1)} custom-call(bf16[2,256,256]{2,1,0:T(8,128)(2,1)S(1)} %get-tuple-element.44.rounded_ref, bf16[1,256,128]{2,1,0:T(8,128)(2,1)S(1)} %get-tuple-element.45.rounded_more, bf16[512,512]{1,0:T(8,128)(2,1)S(1)} %copy-done, bf16[32,144,256]{2,1,0:T(8,128)(2,1)S(1)} %get-tuple-element.36.particles), custom_call_target="tpu_custom_call" | custom-call | flops 268435456 | bytes 4096000 | tf_op jit(solution)/shard_map/pallas_call | solution.py:93
  18.1 0.6 %collective-permute-done.5.spectrum = bf16[42,16,128]{2,1,0:T(8,128)(2,1)S(1)} collective-permute-done((bf16[42,16,128]{2,1,0:T(8,128)(2,1)S(1)}, bf16[42,16,128]{2,1,0:T(8,128)(2,1)S(1)}, u32[]{:S(2)}, u32[]{:S(2)}) %collective-permute-start.5) | collective-permute-done | bytes 172064 | tf_op jit(solution)/shard_map/ppermute | solution.py:667
  18.7 0.6 %shard_map.85.refs_0_ = bf16[272,128]{1,0:T(8,128)(2,1)S(1)} custom-call(f32[576,128]{1,0:T(8,128)S(1)} %shard_map.84.image, bf16[42,16,128]{2,1,0:T(8,128)(2,1)S(1)} %get-tuple-element.46.mine, bf16[42,16,128]{2,1,0:T(8,128)(2,1)S(1)} %collective-permute-done.5.spectrum, bf16[32,144,256]{2,1,0:T(8,128)(2,1)S(1)} %get-tuple-element.34.refs_5_.particles), custom_call_target="tpu_custom_call" | custom-call | flops 352321536 | bytes 3657728 | tf_op jit(solution)/shard_map/pallas_call | solution.py:93
  19.3 1.3 %collective-permute-start.8 = (bf16[272,128]{1,0:T(8,128)(2,1)S(1)}, bf16[272,128]{1,0:T(8,128)(2,1)S(1)}, u32[]{:S(2)}, u32[]{:S(2)}) collective-permute-start(bf16[272,128]{1,0:T(8,128)(2,1)S(1)} %shard_map.85.refs_0_), channel_id=1, source_target_pairs={{0,8},{4,12},{8,0},{12,4},{1,9},{5,13},{9,1},{13,5},{2,10},{6,14},... | collective-permute-start | bytes 208904 | tf_op jit(solution)/shard_map/ppermute | solution.py:667
  20.6 0.9 %collective-permute-start.7 = (bf16[272,128]{1,0:T(8,128)(2,1)S(1)}, bf16[272,128]{1,0:T(8,128)(2,1)S(1)}, u32[]{:S(2)}, u32[]{:S(2)}) collective-permute-start(bf16[272,128]{1,0:T(8,128)(2,1)S(1)} %shard_map.85.refs_0_), channel_id=1, source_target_pairs={{0,12},{4,8},{8,4},{12,0},{1,13},{5,9},{9,5},{13,1},{2,14},{6,10},... | collective-permute-start | bytes 208904 | tf_op jit(solution)/shard_map/ppermute | solution.py:667
  21.5 1.4 %collective-permute-start.6 = (bf16[272,128]{1,0:T(8,128)(2,1)S(1)}, bf16[272,128]{1,0:T(8,128)(2,1)S(1)}, u32[]{:S(2)}, u32[]{:S(2)}) collective-permute-start(bf16[272,128]{1,0:T(8,128)(2,1)S(1)} %shard_map.85.refs_0_), channel_id=1, source_target_pairs={{0,4},{4,0},{8,12},{12,8},{1,5},{5,1},{9,13},{13,9},{2,6},{6,2},{1... | collective-permute-start | bytes 208904 | tf_op jit(solution)/shard_map/ppermute | solution.py:667
  22.8 3.7 %collective-permute-done.8.refs_3_ = bf16[272,128]{1,0:T(8,128)(2,1)S(1)} collective-permute-done((bf16[272,128]{1,0:T(8,128)(2,1)S(1)}, bf16[272,128]{1,0:T(8,128)(2,1)S(1)}, u32[]{:S(2)}, u32[]{:S(2)}) %collective-permute-start.8) | collective-permute-done | bytes 69664 | tf_op jit(solution)/shard_map/ppermute | solution.py:667
  26.5 0.6 %collective-permute-done.7.refs_2_ = bf16[272,128]{1,0:T(8,128)(2,1)S(1)} collective-permute-done((bf16[272,128]{1,0:T(8,128)(2,1)S(1)}, bf16[272,128]{1,0:T(8,128)(2,1)S(1)}, u32[]{:S(2)}, u32[]{:S(2)}) %collective-permute-start.7) | collective-permute-done | bytes 69664 | tf_op jit(solution)/shard_map/ppermute | solution.py:667
  27.1 1.2 %collective-permute-done.6.refs_1_ = bf16[272,128]{1,0:T(8,128)(2,1)S(1)} collective-permute-done((bf16[272,128]{1,0:T(8,128)(2,1)S(1)}, bf16[272,128]{1,0:T(8,128)(2,1)S(1)}, u32[]{:S(2)}, u32[]{:S(2)}) %collective-permute-start.6) | collective-permute-done | bytes 69664 | tf_op jit(solution)/shard_map/ppermute | solution.py:667
  28.3 0.9 %shard_map.86 = (f32[648,128]{1,0:T(8,128)S(1)}, f32[4,128]{1,0:T(4,128)S(1)}, bf16[32,16,256]{2,1,0:T(8,128)(2,1)S(1)}) custom-call(bf16[272,128]{1,0:T(8,128)(2,1)S(1)} %shard_map.85.refs_0_, bf16[272,128]{1,0:T(8,128)(2,1)S(1)} %collective-permute-done.6.refs_1_, bf16[272,128]{1,0:T(8,128)(2,1)S(1)} %collective-permute-done.7.refs_2_, ...), custom_call_target="tpu_custom_call" | custom-call | flops 150994944 | bytes 3842048 | tf_op jit(solution)/shard_map/pallas_call | solution.py:93
  29.3 0.8 %shard_map.87.own = f32[648,128]{1,0:T(8,128)S(1)} custom-call(bf16[32,16,256]{2,1,0:T(8,128)(2,1)S(1)} %get-tuple-element.47.left_ref, bf16[32,144,256]{2,1,0:T(8,128)(2,1)S(1)} %get-tuple-element.36.particles), custom_call_target="tpu_custom_call" | custom-call | flops 301989888 | bytes 3252224 | tf_op jit(solution)/shard_map/pallas_call | solution.py:93
  30.1 0.8 %collective-permute-done.9.other = f32[648,128]{1,0:T(8,128)S(1)} collective-permute-done((f32[648,128]{1,0:T(8,128)S(1)}, f32[648,128]{1,0:T(8,128)S(1)}, u32[]{:S(2)}, u32[]{:S(2)}) %collective-permute-start.9) | collective-permute-done | bytes 331808 | tf_op jit(solution)/shard_map/ppermute | solution.py:667
  30.9 0.7 %shard_map.88 = (f32[2,256,256]{2,1,0:T(8,128)S(1)}, f32[1,256,128]{2,1,0:T(8,128)S(1)}, f32[2,256]{1,0:T(2,128)S(1)}, f32[1,128]{1,0:T(1,128)S(1)}, f32[8,256]{1,0:T(8,128)S(1)}) custom-call(f32[648,128]{1,0:T(8,128)S(1)} %shard_map.87.own, f32[648,128]{1,0:T(8,128)S(1)} %collective-permute-done.9.other, f32[4,128]{1,0:T(4,128)S(1)} %get-tuple-element.49.energy_ref, ...), custom_call_target="tpu_custom_call" | custom-call | flops 402653184 | bytes 2424832 | tf_op jit(solution)/shard_map/pallas_call | solution.py:93
  31.5 1.3 %collective-permute-start.10 = (f32[8,256]{1,0:T(8,128)S(1)}, f32[8,256]{1,0:T(8,128)S(1)}, u32[]{:S(2)}, u32[]{:S(2)}) collective-permute-start(f32[8,256]{1,0:T(8,128)S(1)} %get-tuple-element.54.first), channel_id=1, source_target_pairs={{0,3},{1,2},{2,1},{3,0},{4,7},{5,6},{6,5},{7,4},{8,11},{9,10},{10,... | collective-permute-start | bytes 24584 | tf_op jit(solution)/shard_map/ppermute | solution.py:667
  32.8 1.8 %collective-permute-done.10.second = f32[8,256]{1,0:T(8,128)S(1)} collective-permute-done((f32[8,256]{1,0:T(8,128)S(1)}, f32[8,256]{1,0:T(8,128)S(1)}, u32[]{:S(2)}, u32[]{:S(2)}) %collective-permute-start.10) | collective-permute-done | bytes 8224 | tf_op jit(solution)/shard_map/ppermute | solution.py:667
  35.2 0.7 %shard_map.90.image = f32[576,128]{1,0:T(8,128)S(1)} custom-call(bf16[2,256,256]{2,1,0:T(8,128)(2,1)S(1)} %get-tuple-element.55.rounded_ref, bf16[1,256,128]{2,1,0:T(8,128)(2,1)S(1)} %get-tuple-element.56.rounded_more, bf16[512,512]{1,0:T(8,128)(2,1)S(1)} %copy-done, bf16[32,144,256]{2,1,0:T(8,128)(2,1)S(1)} %get-tuple-element.36.particles), custom_call_target="tpu_custom_call" | custom-call | flops 268435456 | bytes 4096000 | tf_op jit(solution)/shard_map/pallas_call | solution.py:93
  35.9 0.6 %collective-permute-done.11.spectrum = bf16[42,16,128]{2,1,0:T(8,128)(2,1)S(1)} collective-permute-done((bf16[42,16,128]{2,1,0:T(8,128)(2,1)S(1)}, bf16[42,16,128]{2,1,0:T(8,128)(2,1)S(1)}, u32[]{:S(2)}, u32[]{:S(2)}) %collective-permute-start.11) | collective-permute-done | bytes 172064 | tf_op jit(solution)/shard_map/ppermute | solution.py:667
  36.5 0.6 %shard_map.91 = (f32[72,128]{1,0:T(8,128)S(1)}, f32[72,128]{1,0:T(8,128)S(1)}, f32[72,128]{1,0:T(8,128)S(1)}, f32[72,128]{1,0:T(8,128)S(1)}, f32[1,144]{1,0:T(1,128)S(1)}) custom-call(f32[576,128]{1,0:T(8,128)S(1)} %shard_map.90.image, bf16[42,16,128]{2,1,0:T(8,128)(2,1)S(1)} %get-tuple-element.57.mine, ...), custom_call_target="tpu_custom_call" | custom-call | flops 352321536 | bytes 3768320 | tf_op jit(solution)/shard_map/pallas_call | solution.py:93
  37.1 1.9 %collective-permute-start.12 = (f32[72,128]{1,0:T(8,128)S(1)}, f32[72,128]{1,0:T(8,128)S(1)}, u32[]{:S(2)}, u32[]{:S(2)}) collective-permute-start(f32[72,128]{1,0:T(8,128)S(1)} %get-tuple-element.58), channel_id=1, source_target_pairs={{0,8},{4,12},{8,0},{12,4},{1,9},{5,13},{9,1},{13,5},{2,10},{6,14},... | collective-permute-start | bytes 110600 | tf_op jit(solution)/shard_map/ppermute | solution.py:667
  39.0 1.2 %collective-permute-start.13 = (f32[72,128]{1,0:T(8,128)S(1)}, f32[72,128]{1,0:T(8,128)S(1)}, u32[]{:S(2)}, u32[]{:S(2)}) collective-permute-start(f32[72,128]{1,0:T(8,128)S(1)} %get-tuple-element.59), channel_id=1, source_target_pairs={{0,12},{4,8},{8,4},{12,0},{1,13},{5,9},{9,5},{13,1},{2,14},{6,10},... | collective-permute-start | bytes 110600 | tf_op jit(solution)/shard_map/ppermute | solution.py:667
  40.6 2.1 %collective-permute-done.12.refs_0_ = f32[72,128]{1,0:T(8,128)S(1)} collective-permute-done((f32[72,128]{1,0:T(8,128)S(1)}, f32[72,128]{1,0:T(8,128)S(1)}, u32[]{:S(2)}, u32[]{:S(2)}) %collective-permute-start.12) | collective-permute-done | bytes 36896 | tf_op jit(solution)/shard_map/ppermute | solution.py:667
  42.7 2.0 %collective-permute-done.13.refs_1_ = f32[72,128]{1,0:T(8,128)S(1)} collective-permute-done((f32[72,128]{1,0:T(8,128)S(1)}, f32[72,128]{1,0:T(8,128)S(1)}, u32[]{:S(2)}, u32[]{:S(2)}) %collective-permute-start.13) | collective-permute-done | bytes 36896 | tf_op jit(solution)/shard_map/ppermute | solution.py:667
  44.7 0.6 %shard_map.92 = (f32[1,64,128]{2,1,0:T(8,128)}, f32[1,144]{1,0:T(1,128)}) custom-call(f32[72,128]{1,0:T(8,128)S(1)} %collective-permute-done.12.refs_0_, f32[72,128]{1,0:T(8,128)S(1)} %collective-permute-done.13.refs_1_, f32[72,128]{1,0:T(8,128)S(1)} %collective-permute-done.14.refs_2_, f32[72,128]{1,0:T(8,128)S(1)} %get-tuple-element.61.refs_3_, ...), custom_call_target="tpu_custom_call" | custom-call | bytes 245760 | tf_op jit(solution)/shard_map/pallas_call | solution.py:93
  (26 shorter events, 2.8 us)
Async XLA Ops:
  0.6 5.7 %copy-start.5 = (bf16[288,64,128]{2,1,0:T(8,128)(2,1)S(1)}, bf16[288,64,128]{2,1,0:T(8,128)(2,1)}, u32[]{:S(2)}) copy-start(bf16[288,64,128]{2,1,0:T(8,128)(2,1)} %particles_ref.1) | copy-start | bytes 14155780
  0.6 7.2 %collective-permute-start.1 = (bf16[1,64,128]{2,1,0:T(8,128)(2,1)}, bf16[1,64,128]{2,1,0:T(8,128)(2,1)S(1)}, u32[]{:S(2)}, u32[]{:S(2)}) collective-permute-start(bf16[1,64,128]{2,1,0:T(8,128)(2,1)} %refs_0_.1), channel_id=1, source_target_pairs={{0,8},{4,12},{8,0},{12,4},{1,9},{5,13},{9,1},{13,5},{2,10},{6,14},... | collective-permute-start | bytes 49160 | tf_op jit(solution)/shard_map/ppermute | solution.py:667
  4.7 5.7 %collective-permute-start = (bf16[1,64,128]{2,1,0:T(8,128)(2,1)}, bf16[1,64,128]{2,1,0:T(8,128)(2,1)S(1)}, u32[]{:S(2)}, u32[]{:S(2)}) collective-permute-start(bf16[1,64,128]{2,1,0:T(8,128)(2,1)} %refs_0_.1), channel_id=1, source_target_pairs={{0,12},{4,8},{8,4},{12,0},{1,13},{5,9},{9,5},{13,1},{2,14},{6,10},... | collective-permute-start | bytes 49160 | tf_op jit(solution)/shard_map/ppermute | solution.py:667
  6.1 4.4 %collective-permute-start.2 = (bf16[1,64,128]{2,1,0:T(8,128)(2,1)}, bf16[1,64,128]{2,1,0:T(8,128)(2,1)S(1)}, u32[]{:S(2)}, u32[]{:S(2)}) collective-permute-start(bf16[1,64,128]{2,1,0:T(8,128)(2,1)} %refs_0_.1), channel_id=1, source_target_pairs={{0,4},{4,0},{8,12},{12,8},{1,5},{5,1},{9,13},{13,9},{2,6},{6,2},{1... | collective-permute-start | bytes 49160 | tf_op jit(solution)/shard_map/ppermute | solution.py:667
  6.4 4.1 %copy-start.2 = (bf16[1,64,128]{2,1,0:T(8,128)(2,1)S(1)}, bf16[1,64,128]{2,1,0:T(8,128)(2,1)}, u32[]{:S(2)}) copy-start(bf16[1,64,128]{2,1,0:T(8,128)(2,1)} %refs_0_.1) | copy-start | bytes 49156
  6.4 4.1 %copy-start.4 = (f32[64]{0:T(128)S(1)}, f32[64]{0:T(128)}, u32[]{:S(2)}) copy-start(f32[64]{0:T(128)} %param.8) | copy-start | bytes 772
  7.8 3.7 %copy-start.3 = (s32[288]{0:T(512)S(1)}, s32[288]{0:T(512)}, u32[]{:S(2)}) copy-start(s32[288]{0:T(512)} %prior_ref.1) | copy-start | bytes 3460
  10.5 2.6 %copy-start.1 = (bf16[512,768]{1,0:T(8,128)(2,1)S(1)}, bf16[512,768]{1,0:T(8,128)(2,1)}, u32[]{:S(2)}) copy-start(bf16[512,768]{1,0:T(8,128)(2,1)} %constant.4.clone.inverse) | copy-start | bytes 2359300
  11.4 1.6 %collective-permute-start.3 = (f32[648,128]{1,0:T(8,128)S(1)}, f32[648,128]{1,0:T(8,128)S(1)}, u32[]{:S(2)}, u32[]{:S(2)}) collective-permute-start(f32[648,128]{1,0:T(8,128)S(1)} %get-tuple-element.37), channel_id=1, source_target_pairs={{0,1},{1,0},{2,3},{3,2},{4,5},{5,4},{6,7},{7,6},{8,9},{9,8},{10,11... | collective-permute-start | bytes 995336 | tf_op jit(solution)/shard_map/ppermute | solution.py:667
  11.9 4.9 %copy-start = (bf16[512,512]{1,0:T(8,128)(2,1)S(1)}, bf16[512,512]{1,0:T(8,128)(2,1)}, u32[]{:S(2)}) copy-start(bf16[512,512]{1,0:T(8,128)(2,1)} %constant.5.clone.forward) | copy-start | bytes 1572868
  13.7 3.1 %collective-permute-start.4 = (f32[8,256]{1,0:T(8,128)S(1)}, f32[8,256]{1,0:T(8,128)S(1)}, u32[]{:S(2)}, u32[]{:S(2)}) collective-permute-start(f32[8,256]{1,0:T(8,128)S(1)} %get-tuple-element.43.first), channel_id=1, source_target_pairs={{0,3},{1,2},{2,1},{3,0},{4,7},{5,6},{6,5},{7,4},{8,11},{9,10},{10,... | collective-permute-start | bytes 24584 | tf_op jit(solution)/shard_map/ppermute | solution.py:667
  17.3 1.5 %collective-permute-start.5 = (bf16[42,16,128]{2,1,0:T(8,128)(2,1)S(1)}, bf16[42,16,128]{2,1,0:T(8,128)(2,1)S(1)}, u32[]{:S(2)}, u32[]{:S(2)}) collective-permute-start(bf16[42,16,128]{2,1,0:T(8,128)(2,1)S(1)} %get-tuple-element.46.mine), channel_id=1, source_target_pairs={{0,1},{1,0},{2,3},{3,2},{4,5},{5,4},{6,7},{7,6},{8,9},{9,8},{10,11... | collective-permute-start | bytes 516104 | tf_op jit(solution)/shard_map/ppermute | solution.py:667
  19.3 7.2 %collective-permute-start.8 = (bf16[272,128]{1,0:T(8,128)(2,1)S(1)}, bf16[272,128]{1,0:T(8,128)(2,1)S(1)}, u32[]{:S(2)}, u32[]{:S(2)}) collective-permute-start(bf16[272,128]{1,0:T(8,128)(2,1)S(1)} %shard_map.85.refs_0_), channel_id=1, source_target_pairs={{0,8},{4,12},{8,0},{12,4},{1,9},{5,13},{9,1},{13,5},{2,10},{6,14},... | collective-permute-start | bytes 208904 | tf_op jit(solution)/shard_map/ppermute | solution.py:667
  20.6 6.6 %collective-permute-start.7 = (bf16[272,128]{1,0:T(8,128)(2,1)S(1)}, bf16[272,128]{1,0:T(8,128)(2,1)S(1)}, u32[]{:S(2)}, u32[]{:S(2)}) collective-permute-start(bf16[272,128]{1,0:T(8,128)(2,1)S(1)} %shard_map.85.refs_0_), channel_id=1, source_target_pairs={{0,12},{4,8},{8,4},{12,0},{1,13},{5,9},{9,5},{13,1},{2,14},{6,10},... | collective-permute-start | bytes 208904 | tf_op jit(solution)/shard_map/ppermute | solution.py:667
  21.5 6.8 %collective-permute-start.6 = (bf16[272,128]{1,0:T(8,128)(2,1)S(1)}, bf16[272,128]{1,0:T(8,128)(2,1)S(1)}, u32[]{:S(2)}, u32[]{:S(2)}) collective-permute-start(bf16[272,128]{1,0:T(8,128)(2,1)S(1)} %shard_map.85.refs_0_), channel_id=1, source_target_pairs={{0,4},{4,0},{8,12},{12,8},{1,5},{5,1},{9,13},{13,9},{2,6},{6,2},{1... | collective-permute-start | bytes 208904 | tf_op jit(solution)/shard_map/ppermute | solution.py:667
  29.2 1.6 %collective-permute-start.9 = (f32[648,128]{1,0:T(8,128)S(1)}, f32[648,128]{1,0:T(8,128)S(1)}, u32[]{:S(2)}, u32[]{:S(2)}) collective-permute-start(f32[648,128]{1,0:T(8,128)S(1)} %get-tuple-element.48), channel_id=1, source_target_pairs={{0,1},{1,0},{2,3},{3,2},{4,5},{5,4},{6,7},{7,6},{8,9},{9,8},{10,11... | collective-permute-start | bytes 995336 | tf_op jit(solution)/shard_map/ppermute | solution.py:667
  31.5 3.1 %collective-permute-start.10 = (f32[8,256]{1,0:T(8,128)S(1)}, f32[8,256]{1,0:T(8,128)S(1)}, u32[]{:S(2)}, u32[]{:S(2)}) collective-permute-start(f32[8,256]{1,0:T(8,128)S(1)} %get-tuple-element.54.first), channel_id=1, source_target_pairs={{0,3},{1,2},{2,1},{3,0},{4,7},{5,6},{6,5},{7,4},{8,11},{9,10},{10,... | collective-permute-start | bytes 24584 | tf_op jit(solution)/shard_map/ppermute | solution.py:667
  35.0 1.5 %collective-permute-start.11 = (bf16[42,16,128]{2,1,0:T(8,128)(2,1)S(1)}, bf16[42,16,128]{2,1,0:T(8,128)(2,1)S(1)}, u32[]{:S(2)}, u32[]{:S(2)}) collective-permute-start(bf16[42,16,128]{2,1,0:T(8,128)(2,1)S(1)} %get-tuple-element.57.mine), channel_id=1, source_target_pairs={{0,1},{1,0},{2,3},{3,2},{4,5},{5,4},{6,7},{7,6},{8,9},{9,8},{10,11... | collective-permute-start | bytes 516104 | tf_op jit(solution)/shard_map/ppermute | solution.py:667
  37.1 5.6 %collective-permute-start.12 = (f32[72,128]{1,0:T(8,128)S(1)}, f32[72,128]{1,0:T(8,128)S(1)}, u32[]{:S(2)}, u32[]{:S(2)}) collective-permute-start(f32[72,128]{1,0:T(8,128)S(1)} %get-tuple-element.58), channel_id=1, source_target_pairs={{0,8},{4,12},{8,0},{12,4},{1,9},{5,13},{9,1},{13,5},{2,10},{6,14},... | collective-permute-start | bytes 110600 | tf_op jit(solution)/shard_map/ppermute | solution.py:667
  39.0 5.8 %collective-permute-start.13 = (f32[72,128]{1,0:T(8,128)S(1)}, f32[72,128]{1,0:T(8,128)S(1)}, u32[]{:S(2)}, u32[]{:S(2)}) collective-permute-start(f32[72,128]{1,0:T(8,128)S(1)} %get-tuple-element.59), channel_id=1, source_target_pairs={{0,12},{4,8},{8,4},{12,0},{1,13},{5,9},{9,5},{13,1},{2,14},{6,10},... | collective-permute-start | bytes 110600 | tf_op jit(solution)/shard_map/ppermute | solution.py:667
  40.2 4.6 %collective-permute-start.14 = (f32[72,128]{1,0:T(8,128)S(1)}, f32[72,128]{1,0:T(8,128)S(1)}, u32[]{:S(2)}, u32[]{:S(2)}) collective-permute-start(f32[72,128]{1,0:T(8,128)S(1)} %get-tuple-element.60), channel_id=1, source_target_pairs={{0,4},{4,0},{8,12},{12,8},{1,5},{5,1},{9,13},{13,9},{2,6},{6,2},{1... | collective-permute-start | bytes 110600 | tf_op jit(solution)/shard_map/ppermute | solution.py:667

commit v15 on v14

--- a/solution.py
+++ b/solution.py
@@ -625,8 +625,11 @@
         if len(outs) == 1:
             outs[0][pl.ds(k * freqs, freqs), :] = value.astype(BF16)
         else:
-            outs[k][pl.ds(0, freqs), :] = value
-            outs[k][pl.ds(freqs, SPARE), :] = jnp.broadcast_to(counts[k : k + 1], (SPARE, depth))
+            high = counts[k : k + 1].astype(BF16).astype(F32)
+            line = lax.broadcasted_iota(jnp.int32, (outs[k].shape[0] - freqs, depth), 0)
+            tail = jnp.where(line == 0, high, jnp.where(line == 1, counts[k : k + 1] - high, 0.0))
+            outs[k][pl.ds(0, freqs), :] = value.astype(outs[k].dtype)
+            outs[k][pl.ds(freqs, tail.shape[0]), :] = tail.astype(outs[k].dtype)
     if len(outs) == 1:
         end = outs[0].shape[0] - classes * freqs
         high, low = split(counts)
@@ -640,7 +643,9 @@
     classes = spectrum.shape[1] // 4
     freqs, depth = 2 * pairs, twice // 2
     if last:
-        outs = [((freqs + SPARE, depth), F32)] * classes + [((1, particles.shape[1]), F32)]
+        near, far = ((freqs + SPARE, depth), F32), ((freqs + 16, depth), BF16)
+        outs = [near if k < 2 else far for k in range(classes)]
+        outs.append(((1, particles.shape[1]), F32))
     else:
         outs = [((classes * freqs + -(-2 * classes // 16) * 16, depth), BF16)]
     return call(
@@ -657,8 +662,9 @@
     odd = lax.rem(lax.axis_index("cls"), 2)
     evidence_ref[...] = jnp.where(odd == 0, own[...], other[...])
     freqs = out.shape[1]
-    total = tree(ref[...] for ref in parts)
-    out[0] = total[:freqs, :] / (total[freqs : freqs + 1, :] + shrinkage)
+    total = tree(ref[...].astype(F32)[: freqs + 2] for ref in parts)
+    counts = total[freqs : freqs + 1, :] + total[freqs + 1 : freqs + 2, :]
+    out[0] = total[:freqs, :] / (counts + shrinkage)
 
 
 def swap(value, axis, size, bit):

time: 45.5 us -> 46.3 us (1.018)
  starting transfers between devices: 15.8 us -> 16.7 us
    ppermute x15, starting transfers between devices: 15.8 us -> 16.7 us  [swap(): return lax.ppermute(value, axis, [(i, i ^ bit) for i in range(size)])]
  transfers between devices with their start and end apart: 15 -> 15, of which waited for: 12 -> 12; matrix products, arithmetic and copies ran while one was open for 0% -> 0% of each run, Pallas kernels for 11% -> 10%
where the time goes in v15:
time: 46.3 us; the launch traced here: 46.2 us
  waiting for transfers between devices  18.1 us (39%)
  starting transfers between devices  16.7 us (36%)
  Pallas kernels  10.5 us (23%)
  between operations  0.77 us (2%)
    ppermute x15, waiting for transfers between devices, swap(): return lax.ppermute(value, axis, [(i, i ^ bit) for i in range(size)])  18.1 us
    ppermute x15, starting transfers between devices, swap(): return lax.ppermute(value, axis, [(i, i ^ bit) for i in range(size)])  16.7 us
    pallas_call x16, Pallas kernels, call(): pl.pallas_call(kernel, out_shape=[jax.ShapeDtypeStruct(*x) for x in outs]...  10.5 us
  transfers between devices with their start and end apart: 15, of which 12 were waited for; matrix products, arithmetic and copies ran while one was open for 0% of the time, Pallas kernels for 10%

profile of v15, /device:TPU:0, one launch (start us, length us, event | category | flops | bytes accessed | tf_op | source)
XLA Modules:
  0.0 46.2 jit_solution(5506823914120420667)
XLA Ops:
  0.6 4.1 %collective-permute-start.1 = (bf16[1,64,128]{2,1,0:T(8,128)(2,1)}, bf16[1,64,128]{2,1,0:T(8,128)(2,1)S(1)}, u32[]{:S(2)}, u32[]{:S(2)}) collective-permute-start(bf16[1,64,128]{2,1,0:T(8,128)(2,1)} %refs_0_.1), channel_id=1, source_target_pairs={{0,8},{4,12},{8,0},{12,4},{1,9},{5,13},{9,1},{13,5},{2,10},{6,14},... | collective-permute-start | bytes 49160 | tf_op jit(solution)/shard_map/ppermute | solution.py:673
  4.7 1.3 %collective-permute-start = (bf16[1,64,128]{2,1,0:T(8,128)(2,1)}, bf16[1,64,128]{2,1,0:T(8,128)(2,1)S(1)}, u32[]{:S(2)}, u32[]{:S(2)}) collective-permute-start(bf16[1,64,128]{2,1,0:T(8,128)(2,1)} %refs_0_.1), channel_id=1, source_target_pairs={{0,12},{4,8},{8,4},{12,0},{1,13},{5,9},{9,5},{13,1},{2,14},{6,10},... | collective-permute-start | bytes 49160 | tf_op jit(solution)/shard_map/ppermute | solution.py:673
  6.4 1.4 %shard_map.78 = (bf16[32,144,256]{2,1,0:T(8,128)(2,1)S(1)}, bf16[32,144,256]{2,1,0:T(8,128)(2,1)S(1)}) custom-call(bf16[288,64,128]{2,1,0:T(8,128)(2,1)S(1)} %copy-done.5, bf16[256,256]{1,0:T(8,128)(2,1)S(1)} %shard_map.77.permutation_ref), custom_call_target="tpu_custom_call" | custom-call | flops 2147483648 | bytes 9568256 | tf_op jit(solution)/shard_map/pallas_call | solution.py:93
  7.8 2.6 %collective-permute-done.refs_1_ = bf16[1,64,128]{2,1,0:T(8,128)(2,1)S(1)} collective-permute-done((bf16[1,64,128]{2,1,0:T(8,128)(2,1)}, bf16[1,64,128]{2,1,0:T(8,128)(2,1)S(1)}, u32[]{:S(2)}, u32[]{:S(2)}) %collective-permute-start) | collective-permute-done | bytes 16416 | tf_op jit(solution)/shard_map/ppermute | solution.py:673
  10.5 0.9 %shard_map.79 = (f32[648,128]{1,0:T(8,128)S(1)}, f32[4,128]{1,0:T(4,128)S(1)}, bf16[32,16,256]{2,1,0:T(8,128)(2,1)S(1)}) custom-call(bf16[1,64,128]{2,1,0:T(8,128)(2,1)S(1)} %copy-done.2, bf16[1,64,128]{2,1,0:T(8,128)(2,1)S(1)} %collective-permute-done.refs_1_, bf16[1,64,128]{2,1,0:T(8,128)(2,1)S(1)} %collective-permute-done.1.refs_2_, ...), custom_call_target="tpu_custom_call" | custom-call | flops 150994944 | bytes 3629056 | tf_op jit(solution)/shard_map/pallas_call | solution.py:93
  11.9 0.8 %shard_map.80.own = f32[648,128]{1,0:T(8,128)S(1)} custom-call(bf16[32,16,256]{2,1,0:T(8,128)(2,1)S(1)} %get-tuple-element.35.left_ref, bf16[32,144,256]{2,1,0:T(8,128)(2,1)S(1)} %get-tuple-element.36.particles), custom_call_target="tpu_custom_call" | custom-call | flops 301989888 | bytes 3252224 | tf_op jit(solution)/shard_map/pallas_call | solution.py:93
  13.1 0.6 %shard_map.82 = (f32[2,256,256]{2,1,0:T(8,128)S(1)}, f32[1,256,128]{2,1,0:T(8,128)S(1)}, f32[2,256]{1,0:T(2,128)S(1)}, f32[1,128]{1,0:T(1,128)S(1)}, f32[8,256]{1,0:T(8,128)S(1)}) custom-call(f32[648,128]{1,0:T(8,128)S(1)} %shard_map.80.own, f32[648,128]{1,0:T(8,128)S(1)} %collective-permute-done.3.other, f32[4,128]{1,0:T(4,128)S(1)} %get-tuple-element.38.energy_ref, ...), custom_call_target="tpu_custom_call" | custom-call | flops 402653184 | bytes 2424832 | tf_op jit(solution)/shard_map/pallas_call | solution.py:93
  13.7 1.3 %collective-permute-start.4 = (f32[8,256]{1,0:T(8,128)S(1)}, f32[8,256]{1,0:T(8,128)S(1)}, u32[]{:S(2)}, u32[]{:S(2)}) collective-permute-start(f32[8,256]{1,0:T(8,128)S(1)} %get-tuple-element.43.first), channel_id=1, source_target_pairs={{0,3},{1,2},{2,1},{3,0},{4,7},{5,6},{6,5},{7,4},{8,11},{9,10},{10,... | collective-permute-start | bytes 24584 | tf_op jit(solution)/shard_map/ppermute | solution.py:673
  15.0 1.8 %collective-permute-done.4.second = f32[8,256]{1,0:T(8,128)S(1)} collective-permute-done((f32[8,256]{1,0:T(8,128)S(1)}, f32[8,256]{1,0:T(8,128)S(1)}, u32[]{:S(2)}, u32[]{:S(2)}) %collective-permute-start.4) | collective-permute-done | bytes 8224 | tf_op jit(solution)/shard_map/ppermute | solution.py:673
  17.5 0.7 %shard_map.84.image = f32[576,128]{1,0:T(8,128)S(1)} custom-call(bf16[2,256,256]{2,1,0:T(8,128)(2,1)S(1)} %get-tuple-element.44.rounded_ref, bf16[1,256,128]{2,1,0:T(8,128)(2,1)S(1)} %get-tuple-element.45.rounded_more, bf16[512,512]{1,0:T(8,128)(2,1)S(1)} %copy-done, bf16[32,144,256]{2,1,0:T(8,128)(2,1)S(1)} %get-tuple-element.36.particles), custom_call_target="tpu_custom_call" | custom-call | flops 268435456 | bytes 4096000 | tf_op jit(solution)/shard_map/pallas_call | solution.py:93
  18.1 0.6 %collective-permute-done.5.spectrum = bf16[42,16,128]{2,1,0:T(8,128)(2,1)S(1)} collective-permute-done((bf16[42,16,128]{2,1,0:T(8,128)(2,1)S(1)}, bf16[42,16,128]{2,1,0:T(8,128)(2,1)S(1)}, u32[]{:S(2)}, u32[]{:S(2)}) %collective-permute-start.5) | collective-permute-done | bytes 172064 | tf_op jit(solution)/shard_map/ppermute | solution.py:673
  18.7 0.6 %shard_map.85.refs_0_ = bf16[272,128]{1,0:T(8,128)(2,1)S(1)} custom-call(f32[576,128]{1,0:T(8,128)S(1)} %shard_map.84.image, bf16[42,16,128]{2,1,0:T(8,128)(2,1)S(1)} %get-tuple-element.46.mine, bf16[42,16,128]{2,1,0:T(8,128)(2,1)S(1)} %collective-permute-done.5.spectrum, bf16[32,144,256]{2,1,0:T(8,128)(2,1)S(1)} %get-tuple-element.34.refs_5_.particles), custom_call_target="tpu_custom_call" | custom-call | flops 352321536 | bytes 3657728 | tf_op jit(solution)/shard_map/pallas_call | solution.py:93
  19.3 1.3 %collective-permute-start.8 = (bf16[272,128]{1,0:T(8,128)(2,1)S(1)}, bf16[272,128]{1,0:T(8,128)(2,1)S(1)}, u32[]{:S(2)}, u32[]{:S(2)}) collective-permute-start(bf16[272,128]{1,0:T(8,128)(2,1)S(1)} %shard_map.85.refs_0_), channel_id=1, source_target_pairs={{0,8},{4,12},{8,0},{12,4},{1,9},{5,13},{9,1},{13,5},{2,10},{6,14},... | collective-permute-start | bytes 208904 | tf_op jit(solution)/shard_map/ppermute | solution.py:673
  20.6 0.9 %collective-permute-start.7 = (bf16[272,128]{1,0:T(8,128)(2,1)S(1)}, bf16[272,128]{1,0:T(8,128)(2,1)S(1)}, u32[]{:S(2)}, u32[]{:S(2)}) collective-permute-start(bf16[272,128]{1,0:T(8,128)(2,1)S(1)} %shard_map.85.refs_0_), channel_id=1, source_target_pairs={{0,12},{4,8},{8,4},{12,0},{1,13},{5,9},{9,5},{13,1},{2,14},{6,10},... | collective-permute-start | bytes 208904 | tf_op jit(solution)/shard_map/ppermute | solution.py:673
  21.5 1.4 %collective-permute-start.6 = (bf16[272,128]{1,0:T(8,128)(2,1)S(1)}, bf16[272,128]{1,0:T(8,128)(2,1)S(1)}, u32[]{:S(2)}, u32[]{:S(2)}) collective-permute-start(bf16[272,128]{1,0:T(8,128)(2,1)S(1)} %shard_map.85.refs_0_), channel_id=1, source_target_pairs={{0,4},{4,0},{8,12},{12,8},{1,5},{5,1},{9,13},{13,9},{2,6},{6,2},{1... | collective-permute-start | bytes 208904 | tf_op jit(solution)/shard_map/ppermute | solution.py:673
  22.8 3.7 %collective-permute-done.8.refs_3_ = bf16[272,128]{1,0:T(8,128)(2,1)S(1)} collective-permute-done((bf16[272,128]{1,0:T(8,128)(2,1)S(1)}, bf16[272,128]{1,0:T(8,128)(2,1)S(1)}, u32[]{:S(2)}, u32[]{:S(2)}) %collective-permute-start.8) | collective-permute-done | bytes 69664 | tf_op jit(solution)/shard_map/ppermute | solution.py:673
  26.5 0.6 %collective-permute-done.7.refs_2_ = bf16[272,128]{1,0:T(8,128)(2,1)S(1)} collective-permute-done((bf16[272,128]{1,0:T(8,128)(2,1)S(1)}, bf16[272,128]{1,0:T(8,128)(2,1)S(1)}, u32[]{:S(2)}, u32[]{:S(2)}) %collective-permute-start.7) | collective-permute-done | bytes 69664 | tf_op jit(solution)/shard_map/ppermute | solution.py:673
  27.1 1.2 %collective-permute-done.6.refs_1_ = bf16[272,128]{1,0:T(8,128)(2,1)S(1)} collective-permute-done((bf16[272,128]{1,0:T(8,128)(2,1)S(1)}, bf16[272,128]{1,0:T(8,128)(2,1)S(1)}, u32[]{:S(2)}, u32[]{:S(2)}) %collective-permute-start.6) | collective-permute-done | bytes 69664 | tf_op jit(solution)/shard_map/ppermute | solution.py:673
  28.3 0.9 %shard_map.86 = (f32[648,128]{1,0:T(8,128)S(1)}, f32[4,128]{1,0:T(4,128)S(1)}, bf16[32,16,256]{2,1,0:T(8,128)(2,1)S(1)}) custom-call(bf16[272,128]{1,0:T(8,128)(2,1)S(1)} %shard_map.85.refs_0_, bf16[272,128]{1,0:T(8,128)(2,1)S(1)} %collective-permute-done.6.refs_1_, bf16[272,128]{1,0:T(8,128)(2,1)S(1)} %collective-permute-done.7.refs_2_, ...), custom_call_target="tpu_custom_call" | custom-call | flops 150994944 | bytes 3842048 | tf_op jit(solution)/shard_map/pallas_call | solution.py:93
  29.3 0.8 %shard_map.87.own = f32[648,128]{1,0:T(8,128)S(1)} custom-call(bf16[32,16,256]{2,1,0:T(8,128)(2,1)S(1)} %get-tuple-element.47.left_ref, bf16[32,144,256]{2,1,0:T(8,128)(2,1)S(1)} %get-tuple-element.36.particles), custom_call_target="tpu_custom_call" | custom-call | flops 301989888 | bytes 3252224 | tf_op jit(solution)/shard_map/pallas_call | solution.py:93
  30.1 0.8 %collective-permute-done.9.other = f32[648,128]{1,0:T(8,128)S(1)} collective-permute-done((f32[648,128]{1,0:T(8,128)S(1)}, f32[648,128]{1,0:T(8,128)S(1)}, u32[]{:S(2)}, u32[]{:S(2)}) %collective-permute-start.9) | collective-permute-done | bytes 331808 | tf_op jit(solution)/shard_map/ppermute | solution.py:673
  30.9 0.7 %shard_map.88 = (f32[2,256,256]{2,1,0:T(8,128)S(1)}, f32[1,256,128]{2,1,0:T(8,128)S(1)}, f32[2,256]{1,0:T(2,128)S(1)}, f32[1,128]{1,0:T(1,128)S(1)}, f32[8,256]{1,0:T(8,128)S(1)}) custom-call(f32[648,128]{1,0:T(8,128)S(1)} %shard_map.87.own, f32[648,128]{1,0:T(8,128)S(1)} %collective-permute-done.9.other, f32[4,128]{1,0:T(4,128)S(1)} %get-tuple-element.49.energy_ref, ...), custom_call_target="tpu_custom_call" | custom-call | flops 402653184 | bytes 2424832 | tf_op jit(solution)/shard_map/pallas_call | solution.py:93
  31.5 1.3 %collective-permute-start.10 = (f32[8,256]{1,0:T(8,128)S(1)}, f32[8,256]{1,0:T(8,128)S(1)}, u32[]{:S(2)}, u32[]{:S(2)}) collective-permute-start(f32[8,256]{1,0:T(8,128)S(1)} %get-tuple-element.54.first), channel_id=1, source_target_pairs={{0,3},{1,2},{2,1},{3,0},{4,7},{5,6},{6,5},{7,4},{8,11},{9,10},{10,... | collective-permute-start | bytes 24584 | tf_op jit(solution)/shard_map/ppermute | solution.py:673
  32.8 1.8 %collective-permute-done.10.second = f32[8,256]{1,0:T(8,128)S(1)} collective-permute-done((f32[8,256]{1,0:T(8,128)S(1)}, f32[8,256]{1,0:T(8,128)S(1)}, u32[]{:S(2)}, u32[]{:S(2)}) %collective-permute-start.10) | collective-permute-done | bytes 8224 | tf_op jit(solution)/shard_map/ppermute | solution.py:673
  35.2 0.7 %shard_map.90.image = f32[576,128]{1,0:T(8,128)S(1)} custom-call(bf16[2,256,256]{2,1,0:T(8,128)(2,1)S(1)} %get-tuple-element.55.rounded_ref, bf16[1,256,128]{2,1,0:T(8,128)(2,1)S(1)} %get-tuple-element.56.rounded_more, bf16[512,512]{1,0:T(8,128)(2,1)S(1)} %copy-done, bf16[32,144,256]{2,1,0:T(8,128)(2,1)S(1)} %get-tuple-element.36.particles), custom_call_target="tpu_custom_call" | custom-call | flops 268435456 | bytes 4096000 | tf_op jit(solution)/shard_map/pallas_call | solution.py:93
  35.9 0.6 %collective-permute-done.11.spectrum = bf16[42,16,128]{2,1,0:T(8,128)(2,1)S(1)} collective-permute-done((bf16[42,16,128]{2,1,0:T(8,128)(2,1)S(1)}, bf16[42,16,128]{2,1,0:T(8,128)(2,1)S(1)}, u32[]{:S(2)}, u32[]{:S(2)}) %collective-permute-start.11) | collective-permute-done | bytes 172064 | tf_op jit(solution)/shard_map/ppermute | solution.py:673
  37.1 0.7 %collective-permute-start.14 = (f32[72,128]{1,0:T(8,128)S(1)}, f32[72,128]{1,0:T(8,128)S(1)}, u32[]{:S(2)}, u32[]{:S(2)}) collective-permute-start(f32[72,128]{1,0:T(8,128)S(1)} %get-tuple-element.60), channel_id=1, source_target_pairs={{0,4},{4,0},{8,12},{12,8},{1,5},{5,1},{9,13},{13,9},{2,6},{6,2},{1... | collective-permute-start | bytes 110600 | tf_op jit(solution)/shard_map/ppermute | solution.py:673
  37.8 2.2 %collective-permute-start.12 = (bf16[80,128]{1,0:T(8,128)(2,1)S(1)}, bf16[80,128]{1,0:T(8,128)(2,1)S(1)}, u32[]{:S(2)}, u32[]{:S(2)}) collective-permute-start(bf16[80,128]{1,0:T(8,128)(2,1)S(1)} %get-tuple-element.58), channel_id=1, source_target_pairs={{0,8},{4,12},{8,0},{12,4},{1,9},{5,13},{9,1},{13,5},{2,10},{6,14},... | collective-permute-start | bytes 61448 | tf_op jit(solution)/shard_map/ppermute | solution.py:673
  40.0 1.5 %collective-permute-start.13 = (bf16[80,128]{1,0:T(8,128)(2,1)S(1)}, bf16[80,128]{1,0:T(8,128)(2,1)S(1)}, u32[]{:S(2)}, u32[]{:S(2)}) collective-permute-start(bf16[80,128]{1,0:T(8,128)(2,1)S(1)} %get-tuple-element.59), channel_id=1, source_target_pairs={{0,12},{4,8},{8,4},{12,0},{1,13},{5,9},{9,5},{13,1},{2,14},{6,10},... | collective-permute-start | bytes 61448 | tf_op jit(solution)/shard_map/ppermute | solution.py:673
  41.5 1.0 %collective-permute-done.12.refs_0_ = bf16[80,128]{1,0:T(8,128)(2,1)S(1)} collective-permute-done((bf16[80,128]{1,0:T(8,128)(2,1)S(1)}, bf16[80,128]{1,0:T(8,128)(2,1)S(1)}, u32[]{:S(2)}, u32[]{:S(2)}) %collective-permute-start.12) | collective-permute-done | bytes 20512 | tf_op jit(solution)/shard_map/ppermute | solution.py:673
  42.5 3.0 %collective-permute-done.13.refs_1_ = bf16[80,128]{1,0:T(8,128)(2,1)S(1)} collective-permute-done((bf16[80,128]{1,0:T(8,128)(2,1)S(1)}, bf16[80,128]{1,0:T(8,128)(2,1)S(1)}, u32[]{:S(2)}, u32[]{:S(2)}) %collective-permute-start.13) | collective-permute-done | bytes 20512 | tf_op jit(solution)/shard_map/ppermute | solution.py:673
  45.6 0.6 %shard_map.92 = (f32[1,64,128]{2,1,0:T(8,128)}, f32[1,144]{1,0:T(1,128)}) custom-call(bf16[80,128]{1,0:T(8,128)(2,1)S(1)} %collective-permute-done.12.refs_0_, bf16[80,128]{1,0:T(8,128)(2,1)S(1)} %collective-permute-done.13.refs_1_, f32[72,128]{1,0:T(8,128)S(1)} %collective-permute-done.14.refs_2_, f32[72,128]{1,0:T(8,128)S(1)} %get-tuple-element.61.refs_3_, ...), custom_call_target="tpu_custom_call" | custom-call | bytes 204800 | tf_op jit(solution)/shard_map/pallas_call | solution.py:93
  (26 shorter events, 2.9 us)
Async XLA Ops:
  0.6 5.7 %copy-start.5 = (bf16[288,64,128]{2,1,0:T(8,128)(2,1)S(1)}, bf16[288,64,128]{2,1,0:T(8,128)(2,1)}, u32[]{:S(2)}) copy-start(bf16[288,64,128]{2,1,0:T(8,128)(2,1)} %particles_ref.1) | copy-start | bytes 14155780
  0.6 7.2 %collective-permute-start.1 = (bf16[1,64,128]{2,1,0:T(8,128)(2,1)}, bf16[1,64,128]{2,1,0:T(8,128)(2,1)S(1)}, u32[]{:S(2)}, u32[]{:S(2)}) collective-permute-start(bf16[1,64,128]{2,1,0:T(8,128)(2,1)} %refs_0_.1), channel_id=1, source_target_pairs={{0,8},{4,12},{8,0},{12,4},{1,9},{5,13},{9,1},{13,5},{2,10},{6,14},... | collective-permute-start | bytes 49160 | tf_op jit(solution)/shard_map/ppermute | solution.py:673
  4.7 5.7 %collective-permute-start = (bf16[1,64,128]{2,1,0:T(8,128)(2,1)}, bf16[1,64,128]{2,1,0:T(8,128)(2,1)S(1)}, u32[]{:S(2)}, u32[]{:S(2)}) collective-permute-start(bf16[1,64,128]{2,1,0:T(8,128)(2,1)} %refs_0_.1), channel_id=1, source_target_pairs={{0,12},{4,8},{8,4},{12,0},{1,13},{5,9},{9,5},{13,1},{2,14},{6,10},... | collective-permute-start | bytes 49160 | tf_op jit(solution)/shard_map/ppermute | solution.py:673
  6.1 4.4 %collective-permute-start.2 = (bf16[1,64,128]{2,1,0:T(8,128)(2,1)}, bf16[1,64,128]{2,1,0:T(8,128)(2,1)S(1)}, u32[]{:S(2)}, u32[]{:S(2)}) collective-permute-start(bf16[1,64,128]{2,1,0:T(8,128)(2,1)} %refs_0_.1), channel_id=1, source_target_pairs={{0,4},{4,0},{8,12},{12,8},{1,5},{5,1},{9,13},{13,9},{2,6},{6,2},{1... | collective-permute-start | bytes 49160 | tf_op jit(solution)/shard_map/ppermute | solution.py:673
  6.4 4.1 %copy-start.2 = (bf16[1,64,128]{2,1,0:T(8,128)(2,1)S(1)}, bf16[1,64,128]{2,1,0:T(8,128)(2,1)}, u32[]{:S(2)}) copy-start(bf16[1,64,128]{2,1,0:T(8,128)(2,1)} %refs_0_.1) | copy-start | bytes 49156
  6.4 4.1 %copy-start.4 = (f32[64]{0:T(128)S(1)}, f32[64]{0:T(128)}, u32[]{:S(2)}) copy-start(f32[64]{0:T(128)} %param.8) | copy-start | bytes 772
  7.8 3.7 %copy-start.3 = (s32[288]{0:T(512)S(1)}, s32[288]{0:T(512)}, u32[]{:S(2)}) copy-start(s32[288]{0:T(512)} %prior_ref.1) | copy-start | bytes 3460
  10.5 2.6 %copy-start.1 = (bf16[512,768]{1,0:T(8,128)(2,1)S(1)}, bf16[512,768]{1,0:T(8,128)(2,1)}, u32[]{:S(2)}) copy-start(bf16[512,768]{1,0:T(8,128)(2,1)} %constant.4.clone.inverse) | copy-start | bytes 2359300
  11.4 1.6 %collective-permute-start.3 = (f32[648,128]{1,0:T(8,128)S(1)}, f32[648,128]{1,0:T(8,128)S(1)}, u32[]{:S(2)}, u32[]{:S(2)}) collective-permute-start(f32[648,128]{1,0:T(8,128)S(1)} %get-tuple-element.37), channel_id=1, source_target_pairs={{0,1},{1,0},{2,3},{3,2},{4,5},{5,4},{6,7},{7,6},{8,9},{9,8},{10,11... | collective-permute-start | bytes 995336 | tf_op jit(solution)/shard_map/ppermute | solution.py:673
  11.9 4.9 %copy-start = (bf16[512,512]{1,0:T(8,128)(2,1)S(1)}, bf16[512,512]{1,0:T(8,128)(2,1)}, u32[]{:S(2)}) copy-start(bf16[512,512]{1,0:T(8,128)(2,1)} %constant.5.clone.forward) | copy-start | bytes 1572868
  13.7 3.1 %collective-permute-start.4 = (f32[8,256]{1,0:T(8,128)S(1)}, f32[8,256]{1,0:T(8,128)S(1)}, u32[]{:S(2)}, u32[]{:S(2)}) collective-permute-start(f32[8,256]{1,0:T(8,128)S(1)} %get-tuple-element.43.first), channel_id=1, source_target_pairs={{0,3},{1,2},{2,1},{3,0},{4,7},{5,6},{6,5},{7,4},{8,11},{9,10},{10,... | collective-permute-start | bytes 24584 | tf_op jit(solution)/shard_map/ppermute | solution.py:673
  17.3 1.5 %collective-permute-start.5 = (bf16[42,16,128]{2,1,0:T(8,128)(2,1)S(1)}, bf16[42,16,128]{2,1,0:T(8,128)(2,1)S(1)}, u32[]{:S(2)}, u32[]{:S(2)}) collective-permute-start(bf16[42,16,128]{2,1,0:T(8,128)(2,1)S(1)} %get-tuple-element.46.mine), channel_id=1, source_target_pairs={{0,1},{1,0},{2,3},{3,2},{4,5},{5,4},{6,7},{7,6},{8,9},{9,8},{10,11... | collective-permute-start | bytes 516104 | tf_op jit(solution)/shard_map/ppermute | solution.py:673
  19.3 7.2 %collective-permute-start.8 = (bf16[272,128]{1,0:T(8,128)(2,1)S(1)}, bf16[272,128]{1,0:T(8,128)(2,1)S(1)}, u32[]{:S(2)}, u32[]{:S(2)}) collective-permute-start(bf16[272,128]{1,0:T(8,128)(2,1)S(1)} %shard_map.85.refs_0_), channel_id=1, source_target_pairs={{0,8},{4,12},{8,0},{12,4},{1,9},{5,13},{9,1},{13,5},{2,10},{6,14},... | collective-permute-start | bytes 208904 | tf_op jit(solution)/shard_map/ppermute | solution.py:673
  20.6 6.6 %collective-permute-start.7 = (bf16[272,128]{1,0:T(8,128)(2,1)S(1)}, bf16[272,128]{1,0:T(8,128)(2,1)S(1)}, u32[]{:S(2)}, u32[]{:S(2)}) collective-permute-start(bf16[272,128]{1,0:T(8,128)(2,1)S(1)} %shard_map.85.refs_0_), channel_id=1, source_target_pairs={{0,12},{4,8},{8,4},{12,0},{1,13},{5,9},{9,5},{13,1},{2,14},{6,10},... | collective-permute-start | bytes 208904 | tf_op jit(solution)/shard_map/ppermute | solution.py:673
  21.5 6.8 %collective-permute-start.6 = (bf16[272,128]{1,0:T(8,128)(2,1)S(1)}, bf16[272,128]{1,0:T(8,128)(2,1)S(1)}, u32[]{:S(2)}, u32[]{:S(2)}) collective-permute-start(bf16[272,128]{1,0:T(8,128)(2,1)S(1)} %shard_map.85.refs_0_), channel_id=1, source_target_pairs={{0,4},{4,0},{8,12},{12,8},{1,5},{5,1},{9,13},{13,9},{2,6},{6,2},{1... | collective-permute-start | bytes 208904 | tf_op jit(solution)/shard_map/ppermute | solution.py:673
  29.2 1.6 %collective-permute-start.9 = (f32[648,128]{1,0:T(8,128)S(1)}, f32[648,128]{1,0:T(8,128)S(1)}, u32[]{:S(2)}, u32[]{:S(2)}) collective-permute-start(f32[648,128]{1,0:T(8,128)S(1)} %get-tuple-element.48), channel_id=1, source_target_pairs={{0,1},{1,0},{2,3},{3,2},{4,5},{5,4},{6,7},{7,6},{8,9},{9,8},{10,11... | collective-permute-start | bytes 995336 | tf_op jit(solution)/shard_map/ppermute | solution.py:673
  31.5 3.1 %collective-permute-start.10 = (f32[8,256]{1,0:T(8,128)S(1)}, f32[8,256]{1,0:T(8,128)S(1)}, u32[]{:S(2)}, u32[]{:S(2)}) collective-permute-start(f32[8,256]{1,0:T(8,128)S(1)} %get-tuple-element.54.first), channel_id=1, source_target_pairs={{0,3},{1,2},{2,1},{3,0},{4,7},{5,6},{6,5},{7,4},{8,11},{9,10},{10,... | collective-permute-start | bytes 24584 | tf_op jit(solution)/shard_map/ppermute | solution.py:673
  35.0 1.5 %collective-permute-start.11 = (bf16[42,16,128]{2,1,0:T(8,128)(2,1)S(1)}, bf16[42,16,128]{2,1,0:T(8,128)(2,1)S(1)}, u32[]{:S(2)}, u32[]{:S(2)}) collective-permute-start(bf16[42,16,128]{2,1,0:T(8,128)(2,1)S(1)} %get-tuple-element.57.mine), channel_id=1, source_target_pairs={{0,1},{1,0},{2,3},{3,2},{4,5},{5,4},{6,7},{7,6},{8,9},{9,8},{10,11... | collective-permute-start | bytes 516104 | tf_op jit(solution)/shard_map/ppermute | solution.py:673
  37.1 8.5 %collective-permute-start.14 = (f32[72,128]{1,0:T(8,128)S(1)}, f32[72,128]{1,0:T(8,128)S(1)}, u32[]{:S(2)}, u32[]{:S(2)}) collective-permute-start(f32[72,128]{1,0:T(8,128)S(1)} %get-tuple-element.60), channel_id=1, source_target_pairs={{0,4},{4,0},{8,12},{12,8},{1,5},{5,1},{9,13},{13,9},{2,6},{6,2},{1... | collective-permute-start | bytes 110600 | tf_op jit(solution)/shard_map/ppermute | solution.py:673
  37.8 4.7 %collective-permute-start.12 = (bf16[80,128]{1,0:T(8,128)(2,1)S(1)}, bf16[80,128]{1,0:T(8,128)(2,1)S(1)}, u32[]{:S(2)}, u32[]{:S(2)}) collective-permute-start(bf16[80,128]{1,0:T(8,128)(2,1)S(1)} %get-tuple-element.58), channel_id=1, source_target_pairs={{0,8},{4,12},{8,0},{12,4},{1,9},{5,13},{9,1},{13,5},{2,10},{6,14},... | collective-permute-start | bytes 61448 | tf_op jit(solution)/shard_map/ppermute | solution.py:673
  40.0 5.6 %collective-permute-start.13 = (bf16[80,128]{1,0:T(8,128)(2,1)S(1)}, bf16[80,128]{1,0:T(8,128)(2,1)S(1)}, u32[]{:S(2)}, u32[]{:S(2)}) collective-permute-start(bf16[80,128]{1,0:T(8,128)(2,1)S(1)} %get-tuple-element.59), channel_id=1, source_target_pairs={{0,12},{4,8},{8,4},{12,0},{1,13},{5,9},{9,5},{13,1},{2,14},{6,10},... | collective-permute-start | bytes 61448 | tf_op jit(solution)/shard_map/ppermute | solution.py:673

commit v16 on v14

--- a/solution.py
+++ b/solution.py
@@ -186,8 +186,8 @@
 
 
 def weigh_kernel(fresh, order, count, *refs):
-    sources = [refs[order.index(i)] for i in range(count)]
-    doubled_ref, particles, out, energy_ref, left_ref, image, rest = refs[count:]
+    sources = [[ref for ref, at in zip(refs, order) if at == i] for i in range(count)]
+    doubled_ref, particles, out, energy_ref, left_ref, image, rest = refs[len(order) :]
     pairs, share, twice = particles.shape
     freqs, depth = 2 * pairs, twice // 2
     classes = energy_ref.shape[0]
@@ -201,12 +201,12 @@
 
     for k in range(classes):
         if fresh:
-            plain = sources[k][0].astype(F32)
+            plain = sum(source[0].astype(F32) for source in sources[k])
         else:
             sums, highs, lows = [
                 tree(
                     source[pl.ds(base + (k ^ i) * step, step), :].astype(F32)
-                    for i, source in enumerate(sources)
+                    for i, (source,) in enumerate(sources)
                 )
                 for base, step in ((0, freqs), (classes * freqs, 1), (classes * (freqs + 1), 1))
             ]
@@ -278,10 +278,11 @@
 def weigh(sources, order, inverse_noise, particles, fresh):
     pairs, share, twice = particles.shape
     classes = len(sources)
+    operands = [sources[i][order[:at].count(i)] for at, i in enumerate(order)]
     pitch = 2 * pairs + SPARE
     return call(
         functools.partial(weigh_kernel, fresh, order, classes),
-        [*[sources[i] for i in order], inverse_noise, particles],
+        [*operands, inverse_noise, particles],
         [
             ((corr_lines(classes, share, pitch), 128), F32),
             ((classes, 128), F32),
@@ -688,11 +689,18 @@
     (prior_term,) = call(
         functools.partial(prior_kernel, share), [prior_rot], [((ANG, 256), F32)], flops=1 << 26
     )
-    sources = {i: swap(references, "blk", blocks, i) for i in (*turns, 0)}
+    sources = {i: [swap(references, "blk", blocks, i)] for i in (*turns[1:], 0)}
+    ways = [(i, i ^ turns[0]) for i in range(blocks)]
+    sources[turns[0]] = [
+        lax.ppermute(references, "blk", [(i, j) for i, j in ways if (i < j) == up])
+        for up in (True, False)
+    ]
     other_images, own_images = prep(particles, permutation, share)
     for step in range(ITERS):
         last = step == ITERS - 1
-        order = [0, *(reversed(turns) if step else reversed(range(1, blocks)))]
+        order = [0, *reversed(turns)]
+        if not step:
+            order = [0, turns[0], *turns[1:-1], turns[0], turns[-1]]
         message, energy, left = weigh(sources, order, inverse_noise, other_images, step == 0)
         message = swap(message, "rot", groups, 1)
         own = correlate(left, own_images)
@@ -709,9 +717,9 @@
         image = gather(rounded, more, forward, own_images)
         sums = finish(image, send, message, other_images, last)
         sums, others = (sums[:blocks], sums[blocks:]) if last else (sums * blocks, [])
-        sources = {i: swap(sums[i], "blk", blocks, i) for i in (*turns, 0)}
+        sources = {i: [swap(sums[i], "blk", blocks, i)] for i in (*turns, 0)}
     means, evidence = call(
-        means_kernel, [*[sources[i] for i in turns], sources[0], *evidence, *others], [((1, freqs, depth), F32), ((1, share), F32)]
+        means_kernel, [*[sources[i][0] for i in reversed(range(blocks))], *evidence, *others], [((1, freqs, depth), F32), ((1, share), F32)]
     )
     return means, evidence.reshape(share)
 

time: 45.5 us -> 48.4 us (1.064)
  starting transfers between devices: 15.8 us -> 21.3 us
  waiting for transfers between devices: 18.2 us -> 15.6 us
    ppermute x0 -> x2, starting transfers between devices: none -> 2.84 us  [shards(): lax.ppermute(references, 'blk', [(i, j) for i, j in ways if (i < j) == up])]
    ppermute x15 -> x14, waiting for transfers between devices: 18.2 us -> 15.6 us  [swap(): return lax.ppermute(value, axis, [(i, i ^ bit) for i in range(size)])]
    ppermute x15 -> x14, starting transfers between devices: 15.8 us -> 18.4 us  [swap(): return lax.ppermute(value, axis, [(i, i ^ bit) for i in range(size)])]
  transfers between devices with their start and end apart: 15 -> 16, of which waited for: 12 -> 12; matrix products, arithmetic and copies ran while one was open for 0% -> 0% of each run, Pallas kernels for 11% -> 10%
where the time goes in v16:
time: 48.4 us; the launch traced here: 48.2 us
  starting transfers between devices  21.3 us (44%)
  waiting for transfers between devices  15.6 us (32%)
  Pallas kernels  10.5 us (22%)
  between operations  0.79 us (2%)
    ppermute x14, starting transfers between devices, swap(): return lax.ppermute(value, axis, [(i, i ^ bit) for i in range(size)])  18.4 us
    ppermute x14, waiting for transfers between devices, swap(): return lax.ppermute(value, axis, [(i, i ^ bit) for i in range(size)])  15.6 us
    pallas_call x16, Pallas kernels, call(): pl.pallas_call(kernel, out_shape=[jax.ShapeDtypeStruct(*x) for x in outs]...  10.5 us
    ppermute x2, starting transfers between devices, shards(): lax.ppermute(references, 'blk', [(i, j) for i, j in ways if (i < j) == up])  2.84 us
  transfers between devices with their start and end apart: 16, of which 12 were waited for; matrix products, arithmetic and copies ran while one was open for 0% of the time, Pallas kernels for 10%

profile of v16, /device:TPU:0, one launch (start us, length us, event | category | flops | bytes accessed | tf_op | source)
XLA Modules:
  0.0 48.2 jit_solution(10541999739104899494)
XLA Ops:
  0.6 1.6 %collective-permute-start.2 = (bf16[1,64,128]{2,1,0:T(8,128)(2,1)}, bf16[1,64,128]{2,1,0:T(8,128)(2,1)S(1)}, u32[]{:S(2)}, u32[]{:S(2)}) collective-permute-start(bf16[1,64,128]{2,1,0:T(8,128)(2,1)} %refs_0_.1), channel_id=1, source_target_pairs={{8,0},{12,4},{9,1},{13,5},{10,2},{14,6},{11,3},{15,7},{24,16},{28,... | collective-permute-start | bytes 49160 | tf_op jit(solution)/shard_map/ppermute | solution.py:695
  2.2 6.1 %collective-permute-start.1 = (bf16[1,64,128]{2,1,0:T(8,128)(2,1)}, bf16[1,64,128]{2,1,0:T(8,128)(2,1)S(1)}, u32[]{:S(2)}, u32[]{:S(2)}) collective-permute-start(bf16[1,64,128]{2,1,0:T(8,128)(2,1)} %refs_0_.1), channel_id=1, source_target_pairs={{0,12},{4,8},{8,4},{12,0},{1,13},{5,9},{9,5},{13,1},{2,14},{6,10},... | collective-permute-start | bytes 49160 | tf_op jit(solution)/shard_map/ppermute | solution.py:668
  8.3 1.3 %collective-permute-start = (bf16[1,64,128]{2,1,0:T(8,128)(2,1)}, bf16[1,64,128]{2,1,0:T(8,128)(2,1)S(1)}, u32[]{:S(2)}, u32[]{:S(2)}) collective-permute-start(bf16[1,64,128]{2,1,0:T(8,128)(2,1)} %refs_0_.1), channel_id=1, source_target_pairs={{0,8},{4,12},{1,9},{5,13},{2,10},{6,14},{3,11},{7,15},{16,24},{20,... | collective-permute-start | bytes 49160 | tf_op jit(solution)/shard_map/ppermute | solution.py:695
  9.6 1.3 %collective-permute-start.3 = (bf16[1,64,128]{2,1,0:T(8,128)(2,1)}, bf16[1,64,128]{2,1,0:T(8,128)(2,1)S(1)}, u32[]{:S(2)}, u32[]{:S(2)}) collective-permute-start(bf16[1,64,128]{2,1,0:T(8,128)(2,1)} %refs_0_.1), channel_id=1, source_target_pairs={{0,4},{4,0},{8,12},{12,8},{1,5},{5,1},{9,13},{13,9},{2,6},{6,2},{1... | collective-permute-start | bytes 49160 | tf_op jit(solution)/shard_map/ppermute | solution.py:668
  10.9 1.4 %shard_map.78 = (bf16[32,144,256]{2,1,0:T(8,128)(2,1)S(1)}, bf16[32,144,256]{2,1,0:T(8,128)(2,1)S(1)}) custom-call(bf16[288,64,128]{2,1,0:T(8,128)(2,1)S(1)} %copy-done.5, bf16[256,256]{1,0:T(8,128)(2,1)S(1)} %shard_map.77.permutation_ref), custom_call_target="tpu_custom_call" | custom-call | flops 2147483648 | bytes 9568256 | tf_op jit(solution)/shard_map/pallas_call | solution.py:93
  12.4 1.2 %collective-permute-done.3.refs_4_ = bf16[1,64,128]{2,1,0:T(8,128)(2,1)S(1)} collective-permute-done((bf16[1,64,128]{2,1,0:T(8,128)(2,1)}, bf16[1,64,128]{2,1,0:T(8,128)(2,1)S(1)}, u32[]{:S(2)}, u32[]{:S(2)}) %collective-permute-start.3) | collective-permute-done | bytes 16416 | tf_op jit(solution)/shard_map/ppermute | solution.py:668
  13.6 0.9 %shard_map.79 = (f32[648,128]{1,0:T(8,128)S(1)}, f32[4,128]{1,0:T(4,128)S(1)}, bf16[32,16,256]{2,1,0:T(8,128)(2,1)S(1)}) custom-call(bf16[1,64,128]{2,1,0:T(8,128)(2,1)S(1)} %copy-done.2, bf16[1,64,128]{2,1,0:T(8,128)(2,1)S(1)} %collective-permute-done.refs_1_, bf16[1,64,128]{2,1,0:T(8,128)(2,1)S(1)} %collective-permute-done.1.refs_2_, ...), custom_call_target="tpu_custom_call" | custom-call | flops 150994944 | bytes 3645440 | tf_op jit(solution)/shard_map/pallas_call | solution.py:93
  15.0 0.8 %shard_map.80.own = f32[648,128]{1,0:T(8,128)S(1)} custom-call(bf16[32,16,256]{2,1,0:T(8,128)(2,1)S(1)} %get-tuple-element.35.left_ref, bf16[32,144,256]{2,1,0:T(8,128)(2,1)S(1)} %get-tuple-element.36.particles), custom_call_target="tpu_custom_call" | custom-call | flops 301989888 | bytes 3252224 | tf_op jit(solution)/shard_map/pallas_call | solution.py:93
  16.2 0.6 %shard_map.82 = (f32[2,256,256]{2,1,0:T(8,128)S(1)}, f32[1,256,128]{2,1,0:T(8,128)S(1)}, f32[2,256]{1,0:T(2,128)S(1)}, f32[1,128]{1,0:T(1,128)S(1)}, f32[8,256]{1,0:T(8,128)S(1)}) custom-call(f32[648,128]{1,0:T(8,128)S(1)} %shard_map.80.own, f32[648,128]{1,0:T(8,128)S(1)} %collective-permute-done.4.other, f32[4,128]{1,0:T(4,128)S(1)} %get-tuple-element.38.energy_ref, ...), custom_call_target="tpu_custom_call" | custom-call | flops 402653184 | bytes 2424832 | tf_op jit(solution)/shard_map/pallas_call | solution.py:93
  16.8 1.3 %collective-permute-start.5 = (f32[8,256]{1,0:T(8,128)S(1)}, f32[8,256]{1,0:T(8,128)S(1)}, u32[]{:S(2)}, u32[]{:S(2)}) collective-permute-start(f32[8,256]{1,0:T(8,128)S(1)} %get-tuple-element.43.first), channel_id=1, source_target_pairs={{0,3},{1,2},{2,1},{3,0},{4,7},{5,6},{6,5},{7,4},{8,11},{9,10},{10,... | collective-permute-start | bytes 24584 | tf_op jit(solution)/shard_map/ppermute | solution.py:668
  18.1 1.8 %collective-permute-done.5.second = f32[8,256]{1,0:T(8,128)S(1)} collective-permute-done((f32[8,256]{1,0:T(8,128)S(1)}, f32[8,256]{1,0:T(8,128)S(1)}, u32[]{:S(2)}, u32[]{:S(2)}) %collective-permute-start.5) | collective-permute-done | bytes 8224 | tf_op jit(solution)/shard_map/ppermute | solution.py:668
  20.6 0.7 %shard_map.84.image = f32[576,128]{1,0:T(8,128)S(1)} custom-call(bf16[2,256,256]{2,1,0:T(8,128)(2,1)S(1)} %get-tuple-element.44.rounded_ref, bf16[1,256,128]{2,1,0:T(8,128)(2,1)S(1)} %get-tuple-element.45.rounded_more, bf16[512,512]{1,0:T(8,128)(2,1)S(1)} %copy-done, bf16[32,144,256]{2,1,0:T(8,128)(2,1)S(1)} %get-tuple-element.36.particles), custom_call_target="tpu_custom_call" | custom-call | flops 268435456 | bytes 4096000 | tf_op jit(solution)/shard_map/pallas_call | solution.py:93
  21.2 0.6 %collective-permute-done.6.spectrum = bf16[42,16,128]{2,1,0:T(8,128)(2,1)S(1)} collective-permute-done((bf16[42,16,128]{2,1,0:T(8,128)(2,1)S(1)}, bf16[42,16,128]{2,1,0:T(8,128)(2,1)S(1)}, u32[]{:S(2)}, u32[]{:S(2)}) %collective-permute-start.6) | collective-permute-done | bytes 172064 | tf_op jit(solution)/shard_map/ppermute | solution.py:668
  21.8 0.6 %shard_map.85.refs_0_ = bf16[272,128]{1,0:T(8,128)(2,1)S(1)} custom-call(f32[576,128]{1,0:T(8,128)S(1)} %shard_map.84.image, bf16[42,16,128]{2,1,0:T(8,128)(2,1)S(1)} %get-tuple-element.46.mine, bf16[42,16,128]{2,1,0:T(8,128)(2,1)S(1)} %collective-permute-done.6.spectrum, bf16[32,144,256]{2,1,0:T(8,128)(2,1)S(1)} %get-tuple-element.34.refs_6_.particles.refs_5_), custom_call_target="tpu_custom_call" | custom-call | flops 352321536 | bytes 3657728 | tf_op jit(solution)/shard_map/pallas_call | solution.py:93
  22.4 0.9 %collective-permute-start.9 = (bf16[272,128]{1,0:T(8,128)(2,1)S(1)}, bf16[272,128]{1,0:T(8,128)(2,1)S(1)}, u32[]{:S(2)}, u32[]{:S(2)}) collective-permute-start(bf16[272,128]{1,0:T(8,128)(2,1)S(1)} %shard_map.85.refs_0_), channel_id=1, source_target_pairs={{0,8},{4,12},{8,0},{12,4},{1,9},{5,13},{9,1},{13,5},{2,10},{6,14},... | collective-permute-start | bytes 208904 | tf_op jit(solution)/shard_map/ppermute | solution.py:668
  23.2 2.7 %collective-permute-start.8 = (bf16[272,128]{1,0:T(8,128)(2,1)S(1)}, bf16[272,128]{1,0:T(8,128)(2,1)S(1)}, u32[]{:S(2)}, u32[]{:S(2)}) collective-permute-start(bf16[272,128]{1,0:T(8,128)(2,1)S(1)} %shard_map.85.refs_0_), channel_id=1, source_target_pairs={{0,12},{4,8},{8,4},{12,0},{1,13},{5,9},{9,5},{13,1},{2,14},{6,10},... | collective-permute-start | bytes 208904 | tf_op jit(solution)/shard_map/ppermute | solution.py:668
  26.0 5.3 %collective-permute-done.9.refs_3_ = bf16[272,128]{1,0:T(8,128)(2,1)S(1)} collective-permute-done((bf16[272,128]{1,0:T(8,128)(2,1)S(1)}, bf16[272,128]{1,0:T(8,128)(2,1)S(1)}, u32[]{:S(2)}, u32[]{:S(2)}) %collective-permute-start.9) | collective-permute-done | bytes 69664 | tf_op jit(solution)/shard_map/ppermute | solution.py:668
  31.6 0.9 %shard_map.86 = (f32[648,128]{1,0:T(8,128)S(1)}, f32[4,128]{1,0:T(4,128)S(1)}, bf16[32,16,256]{2,1,0:T(8,128)(2,1)S(1)}) custom-call(bf16[272,128]{1,0:T(8,128)(2,1)S(1)} %shard_map.85.refs_0_, bf16[272,128]{1,0:T(8,128)(2,1)S(1)} %collective-permute-done.7.refs_1_, bf16[272,128]{1,0:T(8,128)(2,1)S(1)} %collective-permute-done.8.refs_2_, ...), custom_call_target="tpu_custom_call" | custom-call | flops 150994944 | bytes 3842048 | tf_op jit(solution)/shard_map/pallas_call | solution.py:93
  32.6 0.8 %shard_map.87.own = f32[648,128]{1,0:T(8,128)S(1)} custom-call(bf16[32,16,256]{2,1,0:T(8,128)(2,1)S(1)} %get-tuple-element.47.left_ref, bf16[32,144,256]{2,1,0:T(8,128)(2,1)S(1)} %get-tuple-element.36.particles), custom_call_target="tpu_custom_call" | custom-call | flops 301989888 | bytes 3252224 | tf_op jit(solution)/shard_map/pallas_call | solution.py:93
  33.4 0.8 %collective-permute-done.10.other = f32[648,128]{1,0:T(8,128)S(1)} collective-permute-done((f32[648,128]{1,0:T(8,128)S(1)}, f32[648,128]{1,0:T(8,128)S(1)}, u32[]{:S(2)}, u32[]{:S(2)}) %collective-permute-start.10) | collective-permute-done | bytes 331808 | tf_op jit(solution)/shard_map/ppermute | solution.py:668
  34.2 0.7 %shard_map.88 = (f32[2,256,256]{2,1,0:T(8,128)S(1)}, f32[1,256,128]{2,1,0:T(8,128)S(1)}, f32[2,256]{1,0:T(2,128)S(1)}, f32[1,128]{1,0:T(1,128)S(1)}, f32[8,256]{1,0:T(8,128)S(1)}) custom-call(f32[648,128]{1,0:T(8,128)S(1)} %shard_map.87.own, f32[648,128]{1,0:T(8,128)S(1)} %collective-permute-done.10.other, f32[4,128]{1,0:T(4,128)S(1)} %get-tuple-element.49.energy_ref, ...), custom_call_target="tpu_custom_call" | custom-call | flops 402653184 | bytes 2424832 | tf_op jit(solution)/shard_map/pallas_call | solution.py:93
  34.8 1.3 %collective-permute-start.11 = (f32[8,256]{1,0:T(8,128)S(1)}, f32[8,256]{1,0:T(8,128)S(1)}, u32[]{:S(2)}, u32[]{:S(2)}) collective-permute-start(f32[8,256]{1,0:T(8,128)S(1)} %get-tuple-element.54.first), channel_id=1, source_target_pairs={{0,3},{1,2},{2,1},{3,0},{4,7},{5,6},{6,5},{7,4},{8,11},{9,10},{10,... | collective-permute-start | bytes 24584 | tf_op jit(solution)/shard_map/ppermute | solution.py:668
  36.1 1.8 %collective-permute-done.11.second = f32[8,256]{1,0:T(8,128)S(1)} collective-permute-done((f32[8,256]{1,0:T(8,128)S(1)}, f32[8,256]{1,0:T(8,128)S(1)}, u32[]{:S(2)}, u32[]{:S(2)}) %collective-permute-start.11) | collective-permute-done | bytes 8224 | tf_op jit(solution)/shard_map/ppermute | solution.py:668
  38.6 0.7 %shard_map.90.image = f32[576,128]{1,0:T(8,128)S(1)} custom-call(bf16[2,256,256]{2,1,0:T(8,128)(2,1)S(1)} %get-tuple-element.55.rounded_ref, bf16[1,256,128]{2,1,0:T(8,128)(2,1)S(1)} %get-tuple-element.56.rounded_more, bf16[512,512]{1,0:T(8,128)(2,1)S(1)} %copy-done, bf16[32,144,256]{2,1,0:T(8,128)(2,1)S(1)} %get-tuple-element.36.particles), custom_call_target="tpu_custom_call" | custom-call | flops 268435456 | bytes 4096000 | tf_op jit(solution)/shard_map/pallas_call | solution.py:93
  39.2 0.6 %collective-permute-done.12.spectrum = bf16[42,16,128]{2,1,0:T(8,128)(2,1)S(1)} collective-permute-done((bf16[42,16,128]{2,1,0:T(8,128)(2,1)S(1)}, bf16[42,16,128]{2,1,0:T(8,128)(2,1)S(1)}, u32[]{:S(2)}, u32[]{:S(2)}) %collective-permute-start.12) | collective-permute-done | bytes 172064 | tf_op jit(solution)/shard_map/ppermute | solution.py:668
  39.8 0.6 %shard_map.91 = (f32[72,128]{1,0:T(8,128)S(1)}, f32[72,128]{1,0:T(8,128)S(1)}, f32[72,128]{1,0:T(8,128)S(1)}, f32[72,128]{1,0:T(8,128)S(1)}, f32[1,144]{1,0:T(1,128)S(1)}) custom-call(f32[576,128]{1,0:T(8,128)S(1)} %shard_map.90.image, bf16[42,16,128]{2,1,0:T(8,128)(2,1)S(1)} %get-tuple-element.57.mine, ...), custom_call_target="tpu_custom_call" | custom-call | flops 352321536 | bytes 3768320 | tf_op jit(solution)/shard_map/pallas_call | solution.py:93
  40.4 1.8 %collective-permute-start.13 = (f32[72,128]{1,0:T(8,128)S(1)}, f32[72,128]{1,0:T(8,128)S(1)}, u32[]{:S(2)}, u32[]{:S(2)}) collective-permute-start(f32[72,128]{1,0:T(8,128)S(1)} %get-tuple-element.58), channel_id=1, source_target_pairs={{0,12},{4,8},{8,4},{12,0},{1,13},{5,9},{9,5},{13,1},{2,14},{6,10},... | collective-permute-start | bytes 110600 | tf_op jit(solution)/shard_map/ppermute | solution.py:668
  42.2 0.7 %collective-permute-start.14 = (f32[72,128]{1,0:T(8,128)S(1)}, f32[72,128]{1,0:T(8,128)S(1)}, u32[]{:S(2)}, u32[]{:S(2)}) collective-permute-start(f32[72,128]{1,0:T(8,128)S(1)} %get-tuple-element.59), channel_id=1, source_target_pairs={{0,8},{4,12},{8,0},{12,4},{1,9},{5,13},{9,1},{13,5},{2,10},{6,14},... | collective-permute-start | bytes 110600 | tf_op jit(solution)/shard_map/ppermute | solution.py:668
  42.9 1.9 %collective-permute-start.15 = (f32[72,128]{1,0:T(8,128)S(1)}, f32[72,128]{1,0:T(8,128)S(1)}, u32[]{:S(2)}, u32[]{:S(2)}) collective-permute-start(f32[72,128]{1,0:T(8,128)S(1)} %get-tuple-element.60), channel_id=1, source_target_pairs={{0,4},{4,0},{8,12},{12,8},{1,5},{5,1},{9,13},{13,9},{2,6},{6,2},{1... | collective-permute-start | bytes 110600 | tf_op jit(solution)/shard_map/ppermute | solution.py:668
  44.8 1.4 %collective-permute-done.13.refs_0_ = f32[72,128]{1,0:T(8,128)S(1)} collective-permute-done((f32[72,128]{1,0:T(8,128)S(1)}, f32[72,128]{1,0:T(8,128)S(1)}, u32[]{:S(2)}, u32[]{:S(2)}) %collective-permute-start.13) | collective-permute-done | bytes 36896 | tf_op jit(solution)/shard_map/ppermute | solution.py:668
  46.2 1.2 %collective-permute-done.14.refs_1_ = f32[72,128]{1,0:T(8,128)S(1)} collective-permute-done((f32[72,128]{1,0:T(8,128)S(1)}, f32[72,128]{1,0:T(8,128)S(1)}, u32[]{:S(2)}, u32[]{:S(2)}) %collective-permute-start.14) | collective-permute-done | bytes 36896 | tf_op jit(solution)/shard_map/ppermute | solution.py:668
  47.6 0.6 %shard_map.92 = (f32[1,64,128]{2,1,0:T(8,128)}, f32[1,144]{1,0:T(1,128)}) custom-call(f32[72,128]{1,0:T(8,128)S(1)} %collective-permute-done.13.refs_0_, f32[72,128]{1,0:T(8,128)S(1)} %collective-permute-done.14.refs_1_, f32[72,128]{1,0:T(8,128)S(1)} %collective-permute-done.15.refs_2_, f32[72,128]{1,0:T(8,128)S(1)} %get-tuple-element.61.refs_3_, ...), custom_call_target="tpu_custom_call" | custom-call | bytes 245760 | tf_op jit(solution)/shard_map/pallas_call | solution.py:93
  (28 shorter events, 2.6 us)
Async XLA Ops:
  0.6 10.3 %copy-start.5 = (bf16[288,64,128]{2,1,0:T(8,128)(2,1)S(1)}, bf16[288,64,128]{2,1,0:T(8,128)(2,1)}, u32[]{:S(2)}) copy-start(bf16[288,64,128]{2,1,0:T(8,128)(2,1)} %particles_ref.1) | copy-start | bytes 14155780
  0.6 11.7 %collective-permute-start.2 = (bf16[1,64,128]{2,1,0:T(8,128)(2,1)}, bf16[1,64,128]{2,1,0:T(8,128)(2,1)S(1)}, u32[]{:S(2)}, u32[]{:S(2)}) collective-permute-start(bf16[1,64,128]{2,1,0:T(8,128)(2,1)} %refs_0_.1), channel_id=1, source_target_pairs={{8,0},{12,4},{9,1},{13,5},{10,2},{14,6},{11,3},{15,7},{24,16},{28,... | collective-permute-start | bytes 49160 | tf_op jit(solution)/shard_map/ppermute | solution.py:695
  2.2 10.1 %collective-permute-start.1 = (bf16[1,64,128]{2,1,0:T(8,128)(2,1)}, bf16[1,64,128]{2,1,0:T(8,128)(2,1)S(1)}, u32[]{:S(2)}, u32[]{:S(2)}) collective-permute-start(bf16[1,64,128]{2,1,0:T(8,128)(2,1)} %refs_0_.1), channel_id=1, source_target_pairs={{0,12},{4,8},{8,4},{12,0},{1,13},{5,9},{9,5},{13,1},{2,14},{6,10},... | collective-permute-start | bytes 49160 | tf_op jit(solution)/shard_map/ppermute | solution.py:668
  8.3 4.1 %collective-permute-start = (bf16[1,64,128]{2,1,0:T(8,128)(2,1)}, bf16[1,64,128]{2,1,0:T(8,128)(2,1)S(1)}, u32[]{:S(2)}, u32[]{:S(2)}) collective-permute-start(bf16[1,64,128]{2,1,0:T(8,128)(2,1)} %refs_0_.1), channel_id=1, source_target_pairs={{0,8},{4,12},{1,9},{5,13},{2,10},{6,14},{3,11},{7,15},{16,24},{20,... | collective-permute-start | bytes 49160 | tf_op jit(solution)/shard_map/ppermute | solution.py:695
  9.6 4.0 %collective-permute-start.3 = (bf16[1,64,128]{2,1,0:T(8,128)(2,1)}, bf16[1,64,128]{2,1,0:T(8,128)(2,1)S(1)}, u32[]{:S(2)}, u32[]{:S(2)}) collective-permute-start(bf16[1,64,128]{2,1,0:T(8,128)(2,1)} %refs_0_.1), channel_id=1, source_target_pairs={{0,4},{4,0},{8,12},{12,8},{1,5},{5,1},{9,13},{13,9},{2,6},{6,2},{1... | collective-permute-start | bytes 49160 | tf_op jit(solution)/shard_map/ppermute | solution.py:668
  10.9 2.7 %copy-start.2 = (bf16[1,64,128]{2,1,0:T(8,128)(2,1)S(1)}, bf16[1,64,128]{2,1,0:T(8,128)(2,1)}, u32[]{:S(2)}) copy-start(bf16[1,64,128]{2,1,0:T(8,128)(2,1)} %refs_0_.1) | copy-start | bytes 49156
  10.9 2.7 %copy-start.4 = (f32[64]{0:T(128)S(1)}, f32[64]{0:T(128)}, u32[]{:S(2)}) copy-start(f32[64]{0:T(128)} %param.8) | copy-start | bytes 772
  12.3 2.2 %copy-start.3 = (s32[288]{0:T(512)S(1)}, s32[288]{0:T(512)}, u32[]{:S(2)}) copy-start(s32[288]{0:T(512)} %prior_ref.1) | copy-start | bytes 3460
  13.6 2.6 %copy-start.1 = (bf16[512,768]{1,0:T(8,128)(2,1)S(1)}, bf16[512,768]{1,0:T(8,128)(2,1)}, u32[]{:S(2)}) copy-start(bf16[512,768]{1,0:T(8,128)(2,1)} %constant.4.clone.inverse) | copy-start | bytes 2359300
  14.5 1.6 %collective-permute-start.4 = (f32[648,128]{1,0:T(8,128)S(1)}, f32[648,128]{1,0:T(8,128)S(1)}, u32[]{:S(2)}, u32[]{:S(2)}) collective-permute-start(f32[648,128]{1,0:T(8,128)S(1)} %get-tuple-element.37), channel_id=1, source_target_pairs={{0,1},{1,0},{2,3},{3,2},{4,5},{5,4},{6,7},{7,6},{8,9},{9,8},{10,11... | collective-permute-start | bytes 995336 | tf_op jit(solution)/shard_map/ppermute | solution.py:668
  15.0 4.9 %copy-start = (bf16[512,512]{1,0:T(8,128)(2,1)S(1)}, bf16[512,512]{1,0:T(8,128)(2,1)}, u32[]{:S(2)}) copy-start(bf16[512,512]{1,0:T(8,128)(2,1)} %constant.5.clone.forward) | copy-start | bytes 1572868
  16.8 3.1 %collective-permute-start.5 = (f32[8,256]{1,0:T(8,128)S(1)}, f32[8,256]{1,0:T(8,128)S(1)}, u32[]{:S(2)}, u32[]{:S(2)}) collective-permute-start(f32[8,256]{1,0:T(8,128)S(1)} %get-tuple-element.43.first), channel_id=1, source_target_pairs={{0,3},{1,2},{2,1},{3,0},{4,7},{5,6},{6,5},{7,4},{8,11},{9,10},{10,... | collective-permute-start | bytes 24584 | tf_op jit(solution)/shard_map/ppermute | solution.py:668
  20.3 1.5 %collective-permute-start.6 = (bf16[42,16,128]{2,1,0:T(8,128)(2,1)S(1)}, bf16[42,16,128]{2,1,0:T(8,128)(2,1)S(1)}, u32[]{:S(2)}, u32[]{:S(2)}) collective-permute-start(bf16[42,16,128]{2,1,0:T(8,128)(2,1)S(1)} %get-tuple-element.46.mine), channel_id=1, source_target_pairs={{0,1},{1,0},{2,3},{3,2},{4,5},{5,4},{6,7},{7,6},{8,9},{9,8},{10,11... | collective-permute-start | bytes 516104 | tf_op jit(solution)/shard_map/ppermute | solution.py:668
  22.4 8.9 %collective-permute-start.9 = (bf16[272,128]{1,0:T(8,128)(2,1)S(1)}, bf16[272,128]{1,0:T(8,128)(2,1)S(1)}, u32[]{:S(2)}, u32[]{:S(2)}) collective-permute-start(bf16[272,128]{1,0:T(8,128)(2,1)S(1)} %shard_map.85.refs_0_), channel_id=1, source_target_pairs={{0,8},{4,12},{8,0},{12,4},{1,9},{5,13},{9,1},{13,5},{2,10},{6,14},... | collective-permute-start | bytes 208904 | tf_op jit(solution)/shard_map/ppermute | solution.py:668
  23.2 8.0 %collective-permute-start.8 = (bf16[272,128]{1,0:T(8,128)(2,1)S(1)}, bf16[272,128]{1,0:T(8,128)(2,1)S(1)}, u32[]{:S(2)}, u32[]{:S(2)}) collective-permute-start(bf16[272,128]{1,0:T(8,128)(2,1)S(1)} %shard_map.85.refs_0_), channel_id=1, source_target_pairs={{0,12},{4,8},{8,4},{12,0},{1,13},{5,9},{9,5},{13,1},{2,14},{6,10},... | collective-permute-start | bytes 208904 | tf_op jit(solution)/shard_map/ppermute | solution.py:668
  26.0 5.6 %collective-permute-start.7 = (bf16[272,128]{1,0:T(8,128)(2,1)S(1)}, bf16[272,128]{1,0:T(8,128)(2,1)S(1)}, u32[]{:S(2)}, u32[]{:S(2)}) collective-permute-start(bf16[272,128]{1,0:T(8,128)(2,1)S(1)} %shard_map.85.refs_0_), channel_id=1, source_target_pairs={{0,4},{4,0},{8,12},{12,8},{1,5},{5,1},{9,13},{13,9},{2,6},{6,2},{1... | collective-permute-start | bytes 208904 | tf_op jit(solution)/shard_map/ppermute | solution.py:668
  32.5 1.6 %collective-permute-start.10 = (f32[648,128]{1,0:T(8,128)S(1)}, f32[648,128]{1,0:T(8,128)S(1)}, u32[]{:S(2)}, u32[]{:S(2)}) collective-permute-start(f32[648,128]{1,0:T(8,128)S(1)} %get-tuple-element.48), channel_id=1, source_target_pairs={{0,1},{1,0},{2,3},{3,2},{4,5},{5,4},{6,7},{7,6},{8,9},{9,8},{10,11... | collective-permute-start | bytes 995336 | tf_op jit(solution)/shard_map/ppermute | solution.py:668
  34.8 3.1 %collective-permute-start.11 = (f32[8,256]{1,0:T(8,128)S(1)}, f32[8,256]{1,0:T(8,128)S(1)}, u32[]{:S(2)}, u32[]{:S(2)}) collective-permute-start(f32[8,256]{1,0:T(8,128)S(1)} %get-tuple-element.54.first), channel_id=1, source_target_pairs={{0,3},{1,2},{2,1},{3,0},{4,7},{5,6},{6,5},{7,4},{8,11},{9,10},{10,... | collective-permute-start | bytes 24584 | tf_op jit(solution)/shard_map/ppermute | solution.py:668
  38.4 1.5 %collective-permute-start.12 = (bf16[42,16,128]{2,1,0:T(8,128)(2,1)S(1)}, bf16[42,16,128]{2,1,0:T(8,128)(2,1)S(1)}, u32[]{:S(2)}, u32[]{:S(2)}) collective-permute-start(bf16[42,16,128]{2,1,0:T(8,128)(2,1)S(1)} %get-tuple-element.57.mine), channel_id=1, source_target_pairs={{0,1},{1,0},{2,3},{3,2},{4,5},{5,4},{6,7},{7,6},{8,9},{9,8},{10,11... | collective-permute-start | bytes 516104 | tf_op jit(solution)/shard_map/ppermute | solution.py:668
  40.4 5.8 %collective-permute-start.13 = (f32[72,128]{1,0:T(8,128)S(1)}, f32[72,128]{1,0:T(8,128)S(1)}, u32[]{:S(2)}, u32[]{:S(2)}) collective-permute-start(f32[72,128]{1,0:T(8,128)S(1)} %get-tuple-element.58), channel_id=1, source_target_pairs={{0,12},{4,8},{8,4},{12,0},{1,13},{5,9},{9,5},{13,1},{2,14},{6,10},... | collective-permute-start | bytes 110600 | tf_op jit(solution)/shard_map/ppermute | solution.py:668
  42.2 5.2 %collective-permute-start.14 = (f32[72,128]{1,0:T(8,128)S(1)}, f32[72,128]{1,0:T(8,128)S(1)}, u32[]{:S(2)}, u32[]{:S(2)}) collective-permute-start(f32[72,128]{1,0:T(8,128)S(1)} %get-tuple-element.59), channel_id=1, source_target_pairs={{0,8},{4,12},{8,0},{12,4},{1,9},{5,13},{9,1},{13,5},{2,10},{6,14},... | collective-permute-start | bytes 110600 | tf_op jit(solution)/shard_map/ppermute | solution.py:668
  42.9 4.6 %collective-permute-start.15 = (f32[72,128]{1,0:T(8,128)S(1)}, f32[72,128]{1,0:T(8,128)S(1)}, u32[]{:S(2)}, u32[]{:S(2)}) collective-permute-start(f32[72,128]{1,0:T(8,128)S(1)} %get-tuple-element.60), channel_id=1, source_target_pairs={{0,4},{4,0},{8,12},{12,8},{1,5},{5,1},{9,13},{13,9},{2,6},{6,2},{1... | collective-permute-start | bytes 110600 | tf_op jit(solution)/shard_map/ppermute | solution.py:668

commit v17 on v14

--- a/solution.py
+++ b/solution.py
@@ -711,7 +711,7 @@
         sums, others = (sums[:blocks], sums[blocks:]) if last else (sums * blocks, [])
         sources = {i: swap(sums[i], "blk", blocks, i) for i in (*turns, 0)}
     means, evidence = call(
-        means_kernel, [*[sources[i] for i in turns], sources[0], *evidence, *others], [((1, freqs, depth), F32), ((1, share), F32)]
+        means_kernel, [*[sources[i] for i in reversed(range(blocks))], *evidence, *others], [((1, freqs, depth), F32), ((1, share), F32)]
     )
     return means, evidence.reshape(share)
 

time: 45.5 us -> 45.1 us (level)
  waiting for transfers between devices: 18.2 us -> 16.9 us
  starting transfers between devices: 15.8 us -> 16.7 us
    ppermute x15, waiting for transfers between devices: 18.2 us -> 16.9 us  [swap(): return lax.ppermute(value, axis, [(i, i ^ bit) for i in range(size)])]
    ppermute x15, starting transfers between devices: 15.8 us -> 16.7 us  [swap(): return lax.ppermute(value, axis, [(i, i ^ bit) for i in range(size)])]
where the time goes in v17:
time: 45.1 us; the launch traced here: 44.9 us
  waiting for transfers between devices  16.9 us (37%)
  starting transfers between devices  16.7 us (37%)
  Pallas kernels  10.5 us (23%)
  between operations  0.77 us (2%)
    ppermute x15, waiting for transfers between devices, swap(): return lax.ppermute(value, axis, [(i, i ^ bit) for i in range(size)])  16.9 us
    ppermute x15, starting transfers between devices, swap(): return lax.ppermute(value, axis, [(i, i ^ bit) for i in range(size)])  16.7 us
    pallas_call x16, Pallas kernels, call(): pl.pallas_call(kernel, out_shape=[jax.ShapeDtypeStruct(*x) for x in outs]...  10.5 us
  transfers between devices with their start and end apart: 15, of which 12 were waited for; matrix products, arithmetic and copies ran while one was open for 0% of the time, Pallas kernels for 11%

profile of v17, /device:TPU:0, one launch (start us, length us, event | category | flops | bytes accessed | tf_op | source)
XLA Modules:
  0.0 44.9 jit_solution(13810935865485592806)
XLA Ops:
  0.6 4.1 %collective-permute-start.1 = (bf16[1,64,128]{2,1,0:T(8,128)(2,1)}, bf16[1,64,128]{2,1,0:T(8,128)(2,1)S(1)}, u32[]{:S(2)}, u32[]{:S(2)}) collective-permute-start(bf16[1,64,128]{2,1,0:T(8,128)(2,1)} %refs_0_.1), channel_id=1, source_target_pairs={{0,8},{4,12},{8,0},{12,4},{1,9},{5,13},{9,1},{13,5},{2,10},{6,14},... | collective-permute-start | bytes 49160 | tf_op jit(solution)/shard_map/ppermute | solution.py:667
  4.7 1.3 %collective-permute-start = (bf16[1,64,128]{2,1,0:T(8,128)(2,1)}, bf16[1,64,128]{2,1,0:T(8,128)(2,1)S(1)}, u32[]{:S(2)}, u32[]{:S(2)}) collective-permute-start(bf16[1,64,128]{2,1,0:T(8,128)(2,1)} %refs_0_.1), channel_id=1, source_target_pairs={{0,12},{4,8},{8,4},{12,0},{1,13},{5,9},{9,5},{13,1},{2,14},{6,10},... | collective-permute-start | bytes 49160 | tf_op jit(solution)/shard_map/ppermute | solution.py:667
  6.4 1.4 %shard_map.78 = (bf16[32,144,256]{2,1,0:T(8,128)(2,1)S(1)}, bf16[32,144,256]{2,1,0:T(8,128)(2,1)S(1)}) custom-call(bf16[288,64,128]{2,1,0:T(8,128)(2,1)S(1)} %copy-done.5, bf16[256,256]{1,0:T(8,128)(2,1)S(1)} %shard_map.77.permutation_ref), custom_call_target="tpu_custom_call" | custom-call | flops 2147483648 | bytes 9568256 | tf_op jit(solution)/shard_map/pallas_call | solution.py:93
  7.8 2.6 %collective-permute-done.refs_1_ = bf16[1,64,128]{2,1,0:T(8,128)(2,1)S(1)} collective-permute-done((bf16[1,64,128]{2,1,0:T(8,128)(2,1)}, bf16[1,64,128]{2,1,0:T(8,128)(2,1)S(1)}, u32[]{:S(2)}, u32[]{:S(2)}) %collective-permute-start) | collective-permute-done | bytes 16416 | tf_op jit(solution)/shard_map/ppermute | solution.py:667
  10.5 0.9 %shard_map.79 = (f32[648,128]{1,0:T(8,128)S(1)}, f32[4,128]{1,0:T(4,128)S(1)}, bf16[32,16,256]{2,1,0:T(8,128)(2,1)S(1)}) custom-call(bf16[1,64,128]{2,1,0:T(8,128)(2,1)S(1)} %copy-done.2, bf16[1,64,128]{2,1,0:T(8,128)(2,1)S(1)} %collective-permute-done.refs_1_, bf16[1,64,128]{2,1,0:T(8,128)(2,1)S(1)} %collective-permute-done.1.refs_2_, ...), custom_call_target="tpu_custom_call" | custom-call | flops 150994944 | bytes 3629056 | tf_op jit(solution)/shard_map/pallas_call | solution.py:93
  11.9 0.8 %shard_map.80.own = f32[648,128]{1,0:T(8,128)S(1)} custom-call(bf16[32,16,256]{2,1,0:T(8,128)(2,1)S(1)} %get-tuple-element.35.left_ref, bf16[32,144,256]{2,1,0:T(8,128)(2,1)S(1)} %get-tuple-element.36.particles), custom_call_target="tpu_custom_call" | custom-call | flops 301989888 | bytes 3252224 | tf_op jit(solution)/shard_map/pallas_call | solution.py:93
  13.1 0.6 %shard_map.82 = (f32[2,256,256]{2,1,0:T(8,128)S(1)}, f32[1,256,128]{2,1,0:T(8,128)S(1)}, f32[2,256]{1,0:T(2,128)S(1)}, f32[1,128]{1,0:T(1,128)S(1)}, f32[8,256]{1,0:T(8,128)S(1)}) custom-call(f32[648,128]{1,0:T(8,128)S(1)} %shard_map.80.own, f32[648,128]{1,0:T(8,128)S(1)} %collective-permute-done.3.other, f32[4,128]{1,0:T(4,128)S(1)} %get-tuple-element.38.energy_ref, ...), custom_call_target="tpu_custom_call" | custom-call | flops 402653184 | bytes 2424832 | tf_op jit(solution)/shard_map/pallas_call | solution.py:93
  13.7 1.3 %collective-permute-start.4 = (f32[8,256]{1,0:T(8,128)S(1)}, f32[8,256]{1,0:T(8,128)S(1)}, u32[]{:S(2)}, u32[]{:S(2)}) collective-permute-start(f32[8,256]{1,0:T(8,128)S(1)} %get-tuple-element.43.first), channel_id=1, source_target_pairs={{0,3},{1,2},{2,1},{3,0},{4,7},{5,6},{6,5},{7,4},{8,11},{9,10},{10,... | collective-permute-start | bytes 24584 | tf_op jit(solution)/shard_map/ppermute | solution.py:667
  15.0 1.8 %collective-permute-done.4.second = f32[8,256]{1,0:T(8,128)S(1)} collective-permute-done((f32[8,256]{1,0:T(8,128)S(1)}, f32[8,256]{1,0:T(8,128)S(1)}, u32[]{:S(2)}, u32[]{:S(2)}) %collective-permute-start.4) | collective-permute-done | bytes 8224 | tf_op jit(solution)/shard_map/ppermute | solution.py:667
  17.5 0.7 %shard_map.84.image = f32[576,128]{1,0:T(8,128)S(1)} custom-call(bf16[2,256,256]{2,1,0:T(8,128)(2,1)S(1)} %get-tuple-element.44.rounded_ref, bf16[1,256,128]{2,1,0:T(8,128)(2,1)S(1)} %get-tuple-element.45.rounded_more, bf16[512,512]{1,0:T(8,128)(2,1)S(1)} %copy-done, bf16[32,144,256]{2,1,0:T(8,128)(2,1)S(1)} %get-tuple-element.36.particles), custom_call_target="tpu_custom_call" | custom-call | flops 268435456 | bytes 4096000 | tf_op jit(solution)/shard_map/pallas_call | solution.py:93
  18.1 0.6 %collective-permute-done.5.spectrum = bf16[42,16,128]{2,1,0:T(8,128)(2,1)S(1)} collective-permute-done((bf16[42,16,128]{2,1,0:T(8,128)(2,1)S(1)}, bf16[42,16,128]{2,1,0:T(8,128)(2,1)S(1)}, u32[]{:S(2)}, u32[]{:S(2)}) %collective-permute-start.5) | collective-permute-done | bytes 172064 | tf_op jit(solution)/shard_map/ppermute | solution.py:667
  18.7 0.6 %shard_map.85.refs_0_ = bf16[272,128]{1,0:T(8,128)(2,1)S(1)} custom-call(f32[576,128]{1,0:T(8,128)S(1)} %shard_map.84.image, bf16[42,16,128]{2,1,0:T(8,128)(2,1)S(1)} %get-tuple-element.46.mine, bf16[42,16,128]{2,1,0:T(8,128)(2,1)S(1)} %collective-permute-done.5.spectrum, bf16[32,144,256]{2,1,0:T(8,128)(2,1)S(1)} %get-tuple-element.34.refs_5_.particles), custom_call_target="tpu_custom_call" | custom-call | flops 352321536 | bytes 3657728 | tf_op jit(solution)/shard_map/pallas_call | solution.py:93
  19.3 1.3 %collective-permute-start.8 = (bf16[272,128]{1,0:T(8,128)(2,1)S(1)}, bf16[272,128]{1,0:T(8,128)(2,1)S(1)}, u32[]{:S(2)}, u32[]{:S(2)}) collective-permute-start(bf16[272,128]{1,0:T(8,128)(2,1)S(1)} %shard_map.85.refs_0_), channel_id=1, source_target_pairs={{0,8},{4,12},{8,0},{12,4},{1,9},{5,13},{9,1},{13,5},{2,10},{6,14},... | collective-permute-start | bytes 208904 | tf_op jit(solution)/shard_map/ppermute | solution.py:667
  20.6 0.9 %collective-permute-start.7 = (bf16[272,128]{1,0:T(8,128)(2,1)S(1)}, bf16[272,128]{1,0:T(8,128)(2,1)S(1)}, u32[]{:S(2)}, u32[]{:S(2)}) collective-permute-start(bf16[272,128]{1,0:T(8,128)(2,1)S(1)} %shard_map.85.refs_0_), channel_id=1, source_target_pairs={{0,12},{4,8},{8,4},{12,0},{1,13},{5,9},{9,5},{13,1},{2,14},{6,10},... | collective-permute-start | bytes 208904 | tf_op jit(solution)/shard_map/ppermute | solution.py:667
  21.5 1.4 %collective-permute-start.6 = (bf16[272,128]{1,0:T(8,128)(2,1)S(1)}, bf16[272,128]{1,0:T(8,128)(2,1)S(1)}, u32[]{:S(2)}, u32[]{:S(2)}) collective-permute-start(bf16[272,128]{1,0:T(8,128)(2,1)S(1)} %shard_map.85.refs_0_), channel_id=1, source_target_pairs={{0,4},{4,0},{8,12},{12,8},{1,5},{5,1},{9,13},{13,9},{2,6},{6,2},{1... | collective-permute-start | bytes 208904 | tf_op jit(solution)/shard_map/ppermute | solution.py:667
  22.8 3.7 %collective-permute-done.8.refs_3_ = bf16[272,128]{1,0:T(8,128)(2,1)S(1)} collective-permute-done((bf16[272,128]{1,0:T(8,128)(2,1)S(1)}, bf16[272,128]{1,0:T(8,128)(2,1)S(1)}, u32[]{:S(2)}, u32[]{:S(2)}) %collective-permute-start.8) | collective-permute-done | bytes 69664 | tf_op jit(solution)/shard_map/ppermute | solution.py:667
  26.5 0.6 %collective-permute-done.7.refs_2_ = bf16[272,128]{1,0:T(8,128)(2,1)S(1)} collective-permute-done((bf16[272,128]{1,0:T(8,128)(2,1)S(1)}, bf16[272,128]{1,0:T(8,128)(2,1)S(1)}, u32[]{:S(2)}, u32[]{:S(2)}) %collective-permute-start.7) | collective-permute-done | bytes 69664 | tf_op jit(solution)/shard_map/ppermute | solution.py:667
  27.1 1.2 %collective-permute-done.6.refs_1_ = bf16[272,128]{1,0:T(8,128)(2,1)S(1)} collective-permute-done((bf16[272,128]{1,0:T(8,128)(2,1)S(1)}, bf16[272,128]{1,0:T(8,128)(2,1)S(1)}, u32[]{:S(2)}, u32[]{:S(2)}) %collective-permute-start.6) | collective-permute-done | bytes 69664 | tf_op jit(solution)/shard_map/ppermute | solution.py:667
  28.3 0.9 %shard_map.86 = (f32[648,128]{1,0:T(8,128)S(1)}, f32[4,128]{1,0:T(4,128)S(1)}, bf16[32,16,256]{2,1,0:T(8,128)(2,1)S(1)}) custom-call(bf16[272,128]{1,0:T(8,128)(2,1)S(1)} %shard_map.85.refs_0_, bf16[272,128]{1,0:T(8,128)(2,1)S(1)} %collective-permute-done.6.refs_1_, bf16[272,128]{1,0:T(8,128)(2,1)S(1)} %collective-permute-done.7.refs_2_, ...), custom_call_target="tpu_custom_call" | custom-call | flops 150994944 | bytes 3842048 | tf_op jit(solution)/shard_map/pallas_call | solution.py:93
  29.3 0.8 %shard_map.87.own = f32[648,128]{1,0:T(8,128)S(1)} custom-call(bf16[32,16,256]{2,1,0:T(8,128)(2,1)S(1)} %get-tuple-element.47.left_ref, bf16[32,144,256]{2,1,0:T(8,128)(2,1)S(1)} %get-tuple-element.36.particles), custom_call_target="tpu_custom_call" | custom-call | flops 301989888 | bytes 3252224 | tf_op jit(solution)/shard_map/pallas_call | solution.py:93
  30.1 0.8 %collective-permute-done.9.other = f32[648,128]{1,0:T(8,128)S(1)} collective-permute-done((f32[648,128]{1,0:T(8,128)S(1)}, f32[648,128]{1,0:T(8,128)S(1)}, u32[]{:S(2)}, u32[]{:S(2)}) %collective-permute-start.9) | collective-permute-done | bytes 331808 | tf_op jit(solution)/shard_map/ppermute | solution.py:667
  30.9 0.7 %shard_map.88 = (f32[2,256,256]{2,1,0:T(8,128)S(1)}, f32[1,256,128]{2,1,0:T(8,128)S(1)}, f32[2,256]{1,0:T(2,128)S(1)}, f32[1,128]{1,0:T(1,128)S(1)}, f32[8,256]{1,0:T(8,128)S(1)}) custom-call(f32[648,128]{1,0:T(8,128)S(1)} %shard_map.87.own, f32[648,128]{1,0:T(8,128)S(1)} %collective-permute-done.9.other, f32[4,128]{1,0:T(4,128)S(1)} %get-tuple-element.49.energy_ref, ...), custom_call_target="tpu_custom_call" | custom-call | flops 402653184 | bytes 2424832 | tf_op jit(solution)/shard_map/pallas_call | solution.py:93
  31.5 1.3 %collective-permute-start.10 = (f32[8,256]{1,0:T(8,128)S(1)}, f32[8,256]{1,0:T(8,128)S(1)}, u32[]{:S(2)}, u32[]{:S(2)}) collective-permute-start(f32[8,256]{1,0:T(8,128)S(1)} %get-tuple-element.54.first), channel_id=1, source_target_pairs={{0,3},{1,2},{2,1},{3,0},{4,7},{5,6},{6,5},{7,4},{8,11},{9,10},{10,... | collective-permute-start | bytes 24584 | tf_op jit(solution)/shard_map/ppermute | solution.py:667
  32.8 1.8 %collective-permute-done.10.second = f32[8,256]{1,0:T(8,128)S(1)} collective-permute-done((f32[8,256]{1,0:T(8,128)S(1)}, f32[8,256]{1,0:T(8,128)S(1)}, u32[]{:S(2)}, u32[]{:S(2)}) %collective-permute-start.10) | collective-permute-done | bytes 8224 | tf_op jit(solution)/shard_map/ppermute | solution.py:667
  35.2 0.7 %shard_map.90.image = f32[576,128]{1,0:T(8,128)S(1)} custom-call(bf16[2,256,256]{2,1,0:T(8,128)(2,1)S(1)} %get-tuple-element.55.rounded_ref, bf16[1,256,128]{2,1,0:T(8,128)(2,1)S(1)} %get-tuple-element.56.rounded_more, bf16[512,512]{1,0:T(8,128)(2,1)S(1)} %copy-done, bf16[32,144,256]{2,1,0:T(8,128)(2,1)S(1)} %get-tuple-element.36.particles), custom_call_target="tpu_custom_call" | custom-call | flops 268435456 | bytes 4096000 | tf_op jit(solution)/shard_map/pallas_call | solution.py:93
  35.9 0.6 %collective-permute-done.11.spectrum = bf16[42,16,128]{2,1,0:T(8,128)(2,1)S(1)} collective-permute-done((bf16[42,16,128]{2,1,0:T(8,128)(2,1)S(1)}, bf16[42,16,128]{2,1,0:T(8,128)(2,1)S(1)}, u32[]{:S(2)}, u32[]{:S(2)}) %collective-permute-start.11) | collective-permute-done | bytes 172064 | tf_op jit(solution)/shard_map/ppermute | solution.py:667
  36.5 0.6 %shard_map.91 = (f32[72,128]{1,0:T(8,128)S(1)}, f32[72,128]{1,0:T(8,128)S(1)}, f32[72,128]{1,0:T(8,128)S(1)}, f32[72,128]{1,0:T(8,128)S(1)}, f32[1,144]{1,0:T(1,128)S(1)}) custom-call(f32[576,128]{1,0:T(8,128)S(1)} %shard_map.90.image, bf16[42,16,128]{2,1,0:T(8,128)(2,1)S(1)} %get-tuple-element.57.mine, ...), custom_call_target="tpu_custom_call" | custom-call | flops 352321536 | bytes 3768320 | tf_op jit(solution)/shard_map/pallas_call | solution.py:93
  37.1 2.3 %collective-permute-start.12 = (f32[72,128]{1,0:T(8,128)S(1)}, f32[72,128]{1,0:T(8,128)S(1)}, u32[]{:S(2)}, u32[]{:S(2)}) collective-permute-start(f32[72,128]{1,0:T(8,128)S(1)} %get-tuple-element.58), channel_id=1, source_target_pairs={{0,12},{4,8},{8,4},{12,0},{1,13},{5,9},{9,5},{13,1},{2,14},{6,10},... | collective-permute-start | bytes 110600 | tf_op jit(solution)/shard_map/ppermute | solution.py:667
  39.4 2.1 %collective-permute-start.14 = (f32[72,128]{1,0:T(8,128)S(1)}, f32[72,128]{1,0:T(8,128)S(1)}, u32[]{:S(2)}, u32[]{:S(2)}) collective-permute-start(f32[72,128]{1,0:T(8,128)S(1)} %get-tuple-element.60), channel_id=1, source_target_pairs={{0,4},{4,0},{8,12},{12,8},{1,5},{5,1},{9,13},{13,9},{2,6},{6,2},{1... | collective-permute-start | bytes 110600 | tf_op jit(solution)/shard_map/ppermute | solution.py:667
  41.5 1.6 %collective-permute-done.12.refs_0_ = f32[72,128]{1,0:T(8,128)S(1)} collective-permute-done((f32[72,128]{1,0:T(8,128)S(1)}, f32[72,128]{1,0:T(8,128)S(1)}, u32[]{:S(2)}, u32[]{:S(2)}) %collective-permute-start.12) | collective-permute-done | bytes 36896 | tf_op jit(solution)/shard_map/ppermute | solution.py:667
  43.1 1.1 %collective-permute-done.13.refs_1_ = f32[72,128]{1,0:T(8,128)S(1)} collective-permute-done((f32[72,128]{1,0:T(8,128)S(1)}, f32[72,128]{1,0:T(8,128)S(1)}, u32[]{:S(2)}, u32[]{:S(2)}) %collective-permute-start.13) | collective-permute-done | bytes 36896 | tf_op jit(solution)/shard_map/ppermute | solution.py:667
  44.3 0.6 %shard_map.92 = (f32[1,64,128]{2,1,0:T(8,128)}, f32[1,144]{1,0:T(1,128)}) custom-call(f32[72,128]{1,0:T(8,128)S(1)} %collective-permute-done.12.refs_0_, f32[72,128]{1,0:T(8,128)S(1)} %collective-permute-done.13.refs_1_, f32[72,128]{1,0:T(8,128)S(1)} %collective-permute-done.14.refs_2_, f32[72,128]{1,0:T(8,128)S(1)} %get-tuple-element.61.refs_3_, ...), custom_call_target="tpu_custom_call" | custom-call | bytes 245760 | tf_op jit(solution)/shard_map/pallas_call | solution.py:93
  (26 shorter events, 2.4 us)
Async XLA Ops:
  0.6 5.7 %copy-start.5 = (bf16[288,64,128]{2,1,0:T(8,128)(2,1)S(1)}, bf16[288,64,128]{2,1,0:T(8,128)(2,1)}, u32[]{:S(2)}) copy-start(bf16[288,64,128]{2,1,0:T(8,128)(2,1)} %particles_ref.1) | copy-start | bytes 14155780
  0.6 7.2 %collective-permute-start.1 = (bf16[1,64,128]{2,1,0:T(8,128)(2,1)}, bf16[1,64,128]{2,1,0:T(8,128)(2,1)S(1)}, u32[]{:S(2)}, u32[]{:S(2)}) collective-permute-start(bf16[1,64,128]{2,1,0:T(8,128)(2,1)} %refs_0_.1), channel_id=1, source_target_pairs={{0,8},{4,12},{8,0},{12,4},{1,9},{5,13},{9,1},{13,5},{2,10},{6,14},... | collective-permute-start | bytes 49160 | tf_op jit(solution)/shard_map/ppermute | solution.py:667
  4.7 5.7 %collective-permute-start = (bf16[1,64,128]{2,1,0:T(8,128)(2,1)}, bf16[1,64,128]{2,1,0:T(8,128)(2,1)S(1)}, u32[]{:S(2)}, u32[]{:S(2)}) collective-permute-start(bf16[1,64,128]{2,1,0:T(8,128)(2,1)} %refs_0_.1), channel_id=1, source_target_pairs={{0,12},{4,8},{8,4},{12,0},{1,13},{5,9},{9,5},{13,1},{2,14},{6,10},... | collective-permute-start | bytes 49160 | tf_op jit(solution)/shard_map/ppermute | solution.py:667
  6.1 4.4 %collective-permute-start.2 = (bf16[1,64,128]{2,1,0:T(8,128)(2,1)}, bf16[1,64,128]{2,1,0:T(8,128)(2,1)S(1)}, u32[]{:S(2)}, u32[]{:S(2)}) collective-permute-start(bf16[1,64,128]{2,1,0:T(8,128)(2,1)} %refs_0_.1), channel_id=1, source_target_pairs={{0,4},{4,0},{8,12},{12,8},{1,5},{5,1},{9,13},{13,9},{2,6},{6,2},{1... | collective-permute-start | bytes 49160 | tf_op jit(solution)/shard_map/ppermute | solution.py:667
  6.4 4.1 %copy-start.2 = (bf16[1,64,128]{2,1,0:T(8,128)(2,1)S(1)}, bf16[1,64,128]{2,1,0:T(8,128)(2,1)}, u32[]{:S(2)}) copy-start(bf16[1,64,128]{2,1,0:T(8,128)(2,1)} %refs_0_.1) | copy-start | bytes 49156
  6.4 4.1 %copy-start.4 = (f32[64]{0:T(128)S(1)}, f32[64]{0:T(128)}, u32[]{:S(2)}) copy-start(f32[64]{0:T(128)} %param.8) | copy-start | bytes 772
  7.8 3.7 %copy-start.3 = (s32[288]{0:T(512)S(1)}, s32[288]{0:T(512)}, u32[]{:S(2)}) copy-start(s32[288]{0:T(512)} %prior_ref.1) | copy-start | bytes 3460
  10.5 2.6 %copy-start.1 = (bf16[512,768]{1,0:T(8,128)(2,1)S(1)}, bf16[512,768]{1,0:T(8,128)(2,1)}, u32[]{:S(2)}) copy-start(bf16[512,768]{1,0:T(8,128)(2,1)} %constant.4.clone.inverse) | copy-start | bytes 2359300
  11.4 1.6 %collective-permute-start.3 = (f32[648,128]{1,0:T(8,128)S(1)}, f32[648,128]{1,0:T(8,128)S(1)}, u32[]{:S(2)}, u32[]{:S(2)}) collective-permute-start(f32[648,128]{1,0:T(8,128)S(1)} %get-tuple-element.37), channel_id=1, source_target_pairs={{0,1},{1,0},{2,3},{3,2},{4,5},{5,4},{6,7},{7,6},{8,9},{9,8},{10,11... | collective-permute-start | bytes 995336 | tf_op jit(solution)/shard_map/ppermute | solution.py:667
  11.9 4.9 %copy-start = (bf16[512,512]{1,0:T(8,128)(2,1)S(1)}, bf16[512,512]{1,0:T(8,128)(2,1)}, u32[]{:S(2)}) copy-start(bf16[512,512]{1,0:T(8,128)(2,1)} %constant.5.clone.forward) | copy-start | bytes 1572868
  13.7 3.1 %collective-permute-start.4 = (f32[8,256]{1,0:T(8,128)S(1)}, f32[8,256]{1,0:T(8,128)S(1)}, u32[]{:S(2)}, u32[]{:S(2)}) collective-permute-start(f32[8,256]{1,0:T(8,128)S(1)} %get-tuple-element.43.first), channel_id=1, source_target_pairs={{0,3},{1,2},{2,1},{3,0},{4,7},{5,6},{6,5},{7,4},{8,11},{9,10},{10,... | collective-permute-start | bytes 24584 | tf_op jit(solution)/shard_map/ppermute | solution.py:667
  17.3 1.5 %collective-permute-start.5 = (bf16[42,16,128]{2,1,0:T(8,128)(2,1)S(1)}, bf16[42,16,128]{2,1,0:T(8,128)(2,1)S(1)}, u32[]{:S(2)}, u32[]{:S(2)}) collective-permute-start(bf16[42,16,128]{2,1,0:T(8,128)(2,1)S(1)} %get-tuple-element.46.mine), channel_id=1, source_target_pairs={{0,1},{1,0},{2,3},{3,2},{4,5},{5,4},{6,7},{7,6},{8,9},{9,8},{10,11... | collective-permute-start | bytes 516104 | tf_op jit(solution)/shard_map/ppermute | solution.py:667
  19.3 7.2 %collective-permute-start.8 = (bf16[272,128]{1,0:T(8,128)(2,1)S(1)}, bf16[272,128]{1,0:T(8,128)(2,1)S(1)}, u32[]{:S(2)}, u32[]{:S(2)}) collective-permute-start(bf16[272,128]{1,0:T(8,128)(2,1)S(1)} %shard_map.85.refs_0_), channel_id=1, source_target_pairs={{0,8},{4,12},{8,0},{12,4},{1,9},{5,13},{9,1},{13,5},{2,10},{6,14},... | collective-permute-start | bytes 208904 | tf_op jit(solution)/shard_map/ppermute | solution.py:667
  20.6 6.6 %collective-permute-start.7 = (bf16[272,128]{1,0:T(8,128)(2,1)S(1)}, bf16[272,128]{1,0:T(8,128)(2,1)S(1)}, u32[]{:S(2)}, u32[]{:S(2)}) collective-permute-start(bf16[272,128]{1,0:T(8,128)(2,1)S(1)} %shard_map.85.refs_0_), channel_id=1, source_target_pairs={{0,12},{4,8},{8,4},{12,0},{1,13},{5,9},{9,5},{13,1},{2,14},{6,10},... | collective-permute-start | bytes 208904 | tf_op jit(solution)/shard_map/ppermute | solution.py:667
  21.5 6.8 %collective-permute-start.6 = (bf16[272,128]{1,0:T(8,128)(2,1)S(1)}, bf16[272,128]{1,0:T(8,128)(2,1)S(1)}, u32[]{:S(2)}, u32[]{:S(2)}) collective-permute-start(bf16[272,128]{1,0:T(8,128)(2,1)S(1)} %shard_map.85.refs_0_), channel_id=1, source_target_pairs={{0,4},{4,0},{8,12},{12,8},{1,5},{5,1},{9,13},{13,9},{2,6},{6,2},{1... | collective-permute-start | bytes 208904 | tf_op jit(solution)/shard_map/ppermute | solution.py:667
  29.2 1.6 %collective-permute-start.9 = (f32[648,128]{1,0:T(8,128)S(1)}, f32[648,128]{1,0:T(8,128)S(1)}, u32[]{:S(2)}, u32[]{:S(2)}) collective-permute-start(f32[648,128]{1,0:T(8,128)S(1)} %get-tuple-element.48), channel_id=1, source_target_pairs={{0,1},{1,0},{2,3},{3,2},{4,5},{5,4},{6,7},{7,6},{8,9},{9,8},{10,11... | collective-permute-start | bytes 995336 | tf_op jit(solution)/shard_map/ppermute | solution.py:667
  31.5 3.1 %collective-permute-start.10 = (f32[8,256]{1,0:T(8,128)S(1)}, f32[8,256]{1,0:T(8,128)S(1)}, u32[]{:S(2)}, u32[]{:S(2)}) collective-permute-start(f32[8,256]{1,0:T(8,128)S(1)} %get-tuple-element.54.first), channel_id=1, source_target_pairs={{0,3},{1,2},{2,1},{3,0},{4,7},{5,6},{6,5},{7,4},{8,11},{9,10},{10,... | collective-permute-start | bytes 24584 | tf_op jit(solution)/shard_map/ppermute | solution.py:667
  35.0 1.5 %collective-permute-start.11 = (bf16[42,16,128]{2,1,0:T(8,128)(2,1)S(1)}, bf16[42,16,128]{2,1,0:T(8,128)(2,1)S(1)}, u32[]{:S(2)}, u32[]{:S(2)}) collective-permute-start(bf16[42,16,128]{2,1,0:T(8,128)(2,1)S(1)} %get-tuple-element.57.mine), channel_id=1, source_target_pairs={{0,1},{1,0},{2,3},{3,2},{4,5},{5,4},{6,7},{7,6},{8,9},{9,8},{10,11... | collective-permute-start | bytes 516104 | tf_op jit(solution)/shard_map/ppermute | solution.py:667
  37.1 6.1 %collective-permute-start.12 = (f32[72,128]{1,0:T(8,128)S(1)}, f32[72,128]{1,0:T(8,128)S(1)}, u32[]{:S(2)}, u32[]{:S(2)}) collective-permute-start(f32[72,128]{1,0:T(8,128)S(1)} %get-tuple-element.58), channel_id=1, source_target_pairs={{0,12},{4,8},{8,4},{12,0},{1,13},{5,9},{9,5},{13,1},{2,14},{6,10},... | collective-permute-start | bytes 110600 | tf_op jit(solution)/shard_map/ppermute | solution.py:667
  39.4 4.9 %collective-permute-start.13 = (f32[72,128]{1,0:T(8,128)S(1)}, f32[72,128]{1,0:T(8,128)S(1)}, u32[]{:S(2)}, u32[]{:S(2)}) collective-permute-start(f32[72,128]{1,0:T(8,128)S(1)} %get-tuple-element.59), channel_id=1, source_target_pairs={{0,8},{4,12},{8,0},{12,4},{1,9},{5,13},{9,1},{13,5},{2,10},{6,14},... | collective-permute-start | bytes 110600 | tf_op jit(solution)/shard_map/ppermute | solution.py:667
  39.4 4.9 %collective-permute-start.14 = (f32[72,128]{1,0:T(8,128)S(1)}, f32[72,128]{1,0:T(8,128)S(1)}, u32[]{:S(2)}, u32[]{:S(2)}) collective-permute-start(f32[72,128]{1,0:T(8,128)S(1)} %get-tuple-element.60), channel_id=1, source_target_pairs={{0,4},{4,0},{8,12},{12,8},{1,5},{5,1},{9,13},{13,9},{2,6},{6,2},{1... | collective-permute-start | bytes 110600 | tf_op jit(solution)/shard_map/ppermute | solution.py:667

commit v18 on v17

--- a/solution.py
+++ b/solution.py
@@ -29,7 +29,7 @@
 
 def tables(half_freq):
     turn = np.arange(ANG)
-    inverse, forward = [], []
+    inverse, far, forward = [], [], []
     for group in range(2):
         sides = {}
         for which in range(2):
@@ -40,10 +40,11 @@
                 np.concatenate([scale * np.cos(angle), -scale * np.sin(angle)], 1),
                 np.concatenate([np.cos(angle), np.sin(angle)], 1).T,
             )
-        inverse.append(np.concatenate([sides[group][0], sides[1 - group][0]], 1))
+        inverse.append(sides[group][0])
+        far.append(sides[1 - group][0])
         forward.append(np.concatenate([sides[1 - group][1], sides[group][1]], 0))
     result = []
-    for table, kinds in ((inverse, (0, 0, 1)), (forward, (0, 1))):
+    for table, kinds in ((inverse, (0, 0, 1)), (far, (0, 0, 1)), (forward, (0, 1))):
         table = np.concatenate(table, 0).astype(np.float32)
         high = table.astype(BF16)
         parts = [high, (table - high.astype(np.float32)).astype(BF16)]
@@ -187,7 +188,7 @@
 
 def weigh_kernel(fresh, order, count, *refs):
     sources = [refs[order.index(i)] for i in range(count)]
-    doubled_ref, particles, out, energy_ref, left_ref, image, rest = refs[count:]
+    doubled_ref, particles, out, rest, energy_ref, left_ref, image = refs[count:]
     pairs, share, twice = particles.shape
     freqs, depth = 2 * pairs, twice // 2
     classes = energy_ref.shape[0]
@@ -233,7 +234,6 @@
         place(out, rest, f, times(left, particles[f]), classes, pitch)
 
     loop(pairs, correlate, 32)
-    pack(out, rest, classes, share, pitch)
 
 
 def times(left, particles):
@@ -260,19 +260,23 @@
             part, k = divmod(group, classes)
             value = rest[rows((2 * k + part) * pitch, pitch), :]
             total = total + turned(value, (group - first) * width)
-        out[rows((2 * classes + first // each_pack) * pitch, pitch), :] = total
+        out[rows(first // each_pack * pitch, pitch), :] = total
+
+
+def pack_kernel(classes, share, pitch, rest, out):
+    pack(out, rest, classes, share, pitch)
 
 
 def unpack(ref, unit, part, classes, share, pitch, freqs):
     width, bundle, _ = layout(classes, share)
     group = part * classes + unit * bundle
     each_pack = 128 // width
-    value = ref[rows((2 * classes + group // each_pack) * pitch, freqs), :]
+    value = ref[rows(group // each_pack * pitch, freqs), :]
     return turned(value, -(group % each_pack) * width)
 
 
-def corr_lines(classes, share, pitch):
-    return (2 * classes + -(-2 * classes * (share - 128) // 128)) * pitch
+def packed_lines(classes, share, pitch):
+    return -(-2 * classes * (share - 128) // 128) * pitch
 
 
 def weigh(sources, order, inverse_noise, particles, fresh):
@@ -283,78 +287,116 @@
         functools.partial(weigh_kernel, fresh, order, classes),
         [*[sources[i] for i in order], inverse_noise, particles],
         [
-            ((corr_lines(classes, share, pitch), 128), F32),
+            ((2 * classes * pitch, 128), F32),
+            ((2 * classes * pitch, 128), F32),
             ((classes, 128), F32),
             ((pairs, 4 * classes, twice), BF16),
         ],
-        [((2 * classes * pitch, twice // 2), F32), ((2 * classes * pitch, 128), F32)],
+        [((2 * classes * pitch, twice // 2), F32)],
         flops=8 * classes * share * pairs * twice * 4,
     )
 
 
-def correlate_kernel(left_ref, particles, out, rest):
-    pairs, share, _ = particles.shape
+def correlate_kernel(share, left_ref, particles, energy_ref, prior_term, table, *refs):
+    partial, partial_more, main, rest, packed = refs
+    pairs = particles.shape[0]
     classes = left_ref.shape[1] // 4
-    pitch = 2 * pairs + SPARE
+    freqs, pitch = 2 * pairs, 2 * pairs + SPARE
+    _, bundle, units = layout(classes, share)
 
     def body(f):
-        place(out, rest, f, times(left_ref[f], particles[f]), classes, pitch)
+        place(main, rest, f, times(left_ref[f], particles[f]), classes, pitch)
 
     loop(pairs, body, 32)
-    pack(out, rest, classes, share, pitch)
-
-
-def correlate(left, particles):
+    pack(packed, rest, classes, share, pitch)
+
+    def energy_of(k):
+        return energy_ref[pl.ds(k, 1), :]
+
+    def slab(i, carry):
+        prior = jnp.concatenate([prior_term[:, :128]] * 2, 1)
+        energy = jnp.concatenate([energy_of(2 * i), energy_of(2 * i + 1)], 1)
+        partial[i] = invert(table, two_classes(main, i, pitch, freqs)) - 0.5 * energy + prior
+        return carry
+
+    for unit in range(units):
+        energy = beside(energy_of, unit, classes, share)
+        value = several_classes(packed, unit, classes, share, pitch, freqs)
+        partial_more[unit] = invert(table, value) - 0.5 * energy + prior_term[:, 128:]
+    each(classes // 2, slab, 0)
+
+
+def two_classes(main, i, pitch, freqs):
+    return jnp.concatenate(
+        [
+            jnp.concatenate(
+                [main[rows((4 * i + 2 * j + part) * pitch, freqs), :] for j in range(2)], 1
+            )
+            for part in range(2)
+        ],
+        0,
+    )
+
+
+def several_classes(packed, unit, classes, share, pitch, freqs):
+    return jnp.concatenate(
+        [unpack(packed, unit, part, classes, share, pitch, freqs) for part in range(2)], 0
+    )
+
+
+def beside(value_of, unit, classes, share):
+    width, bundle, _ = layout(classes, share)
+    lane = lax.broadcasted_iota(jnp.int32, (1, 128), 1)
+    return sum(
+        jnp.where(lane // width == j, value_of(unit * bundle + j), 0.0) for j in range(bundle)
+    )
+
+
+def invert(table, value):
+    high, low = split(value)
+    return dot(table[table_rows(0, ANG), :], jnp.concatenate([high, low, high], 0))
+
+
+def correlate(left, particles, energy, prior_term, table):
     pairs, share, twice = particles.shape
     classes = left.shape[1] // 4
     pitch = 2 * pairs + SPARE
     return call(
-        correlate_kernel,
-        [left, particles],
-        [((corr_lines(classes, share, pitch), 128), F32)],
-        [((2 * classes * pitch, 128), F32)],
+        functools.partial(correlate_kernel, share),
+        [left, particles, energy, prior_term, table],
+        [((classes // 2, ANG, 256), F32), ((layout(classes, share)[2], ANG, 128), F32)],
+        [
+            ((2 * classes * pitch, 128), F32),
+            ((2 * classes * pitch, 128), F32),
+            ((packed_lines(classes, share, pitch), 128), F32),
+        ],
         flops=2 * left.shape[1] * share * pairs * twice * 8,
-    )[0]
+    )
 
 
 def table_rows(base, count):
     return pl.ds(pl.multiple_of(lax.axis_index("rot") * ANG + base, 128), count)
 
 
-def score_kernel(share, own, other, energy_ref, prior_term, inverse, *refs):
+def score_kernel(share, partial, partial_more, other, other_more, table, *refs):
     weights, more, tops, more_tops, peaks = refs
-    classes = energy_ref.shape[0]
+    classes = 2 * partial.shape[0]
     width, bundle, units = layout(classes, share)
     freqs = ANG // 4
     pitch = freqs + SPARE
-    at = table_rows(0, ANG)
-    lane = lax.broadcasted_iota(jnp.int32, (1, 128), 1)
-
-    def exponentials(value, energy, prior):
-        high, low = split(value)
-        inner = dot(inverse[at, :], jnp.concatenate([high, low, high], 0))
-        scores = inner - 0.5 * energy + prior
+
+    def exponentials(scores):
         top = jnp.max(scores, axis=0, keepdims=True)
         value = jnp.exp(scores - top)
         return value, top, jnp.sum(value, axis=0, keepdims=True)
 
     def energy_of(k):
-        return energy_ref[pl.ds(k, 1), :] + other[rows(2 * k * pitch + freqs, SPARE), :][:1]
+        return other[rows(2 * k * pitch + freqs, SPARE), :][:1]
 
     def slab(i, carry):
-        value = jnp.concatenate(
-            [
-                jnp.concatenate(
-                    [ref[rows((4 * i + 2 * j + part) * pitch, freqs), :] for j in range(2)], 1
-                )
-                for ref in (own, other)
-                for part in range(2)
-            ],
-            0,
-        )
         energy = jnp.concatenate([energy_of(2 * i), energy_of(2 * i + 1)], 1)
-        prior = jnp.concatenate([prior_term[:, :128]] * 2, 1)
-        weights[i], top, total = exponentials(value, energy, prior)
+        inner = invert(table, two_classes(other, i, pitch, freqs))
+        weights[i], top, total = exponentials(inner + (partial[i] - 0.5 * energy))
         tops[pl.ds(i, 1), :] = top
         for j in (0, 128):
             carry = merge(carry, (top[:, j : j + 128], total[:, j : j + 128]))
@@ -364,19 +406,9 @@
     top, total = each(classes // 2, slab, empty)
     rest = empty
     for unit in range(units):
-        value = jnp.concatenate(
-            [
-                unpack(ref, unit, part, classes, share, pitch, freqs)
-                for ref in (own, other)
-                for part in range(2)
-            ],
-            0,
-        )
-        energy = sum(
-            jnp.where(lane // width == j, energy_of(unit * bundle + j), 0.0)
-            for j in range(bundle)
-        )
-        more[unit], more_top, more_total = exponentials(value, energy, prior_term[:, 128:])
+        energy = beside(energy_of, unit, classes, share)
+        inner = invert(table, several_classes(other_more, unit, classes, share, pitch, freqs))
+        more[unit], more_top, more_total = exponentials(inner + (partial_more[unit] - 0.5 * energy))
         more_tops[pl.ds(unit, 1), :] = more_top
         for j in range(bundle):
             rest = merge(rest, (turned(more_top, -j * width), turned(more_total, -j * width)))
@@ -388,12 +420,12 @@
     )
 
 
-def scores(own, other, energy, prior_term, inverse, share):
-    classes = energy.shape[0]
+def scores(partial, partial_more, other, other_more, table, share):
+    classes = 2 * partial.shape[0]
     units = layout(classes, share)[2]
     return call(
         functools.partial(score_kernel, share),
-        [own, other, energy, prior_term, inverse],
+        [partial, partial_more, other, other_more, table],
         [
             ((classes // 2, ANG, 256), F32),
             ((units, ANG, 128), F32),
@@ -679,7 +711,7 @@
     blocks = lax.axis_size("blk")
     assert groups == 2 and 2 * groups * freqs == ANG
     share = batch // groups
-    inverse, forward = tables(freqs)
+    near, far, forward = tables(freqs)
     inverse_noise = noise_inv.reshape(1, depth // 2)
     assert blocks & (blocks - 1) == 0
     turns = sorted(range(1, blocks), key=lambda i: (-i.bit_length(), i))
@@ -692,11 +724,20 @@
     other_images, own_images = prep(particles, permutation, share)
     for step in range(ITERS):
         last = step == ITERS - 1
-        order = [0, *(reversed(turns) if step else reversed(range(1, blocks)))]
-        message, energy, left = weigh(sources, order, inverse_noise, other_images, step == 0)
+        order = [0, *turns]
+        message, rest, energy, left = weigh(
+            sources, order, inverse_noise, other_images, step == 0
+        )
+        pitch = freqs + SPARE
+        (packed,) = call(
+            functools.partial(pack_kernel, blocks, share, pitch),
+            [rest],
+            [((packed_lines(blocks, share, pitch), 128), F32)],
+        )
         message = swap(message, "rot", groups, 1)
-        own = correlate(left, own_images)
-        *weights, here = scores(own, message, energy, prior_term, inverse, share)
+        packed = swap(packed, "rot", groups, 1)
+        partial = correlate(left, own_images, energy, prior_term, near)
+        *weights, here = scores(*partial, message, packed, far, share)
         first = here
         for bit in bits(sides):
             second = swap(first, ("cls", "rot"), sides * groups, groups * bit + (bit == 1))

time: 45.1 us -> 47.1 us (1.044)
  starting transfers between devices: 16.7 us -> 17.6 us
  Pallas kernels: 10.5 us -> 11.2 us
    ppermute x15 -> x17, starting transfers between devices: 16.7 us -> 17.6 us  [swap(): return lax.ppermute(value, axis, [(i, i ^ bit) for i in range(size)])]
    pallas_call x16 -> x18, Pallas kernels: 10.5 us -> 11.2 us  [call(): pl.pallas_call(kernel, out_shape=[jax.ShapeDtypeStruct(*x) for x in outs]...]
    ppermute x15 -> x17, waiting for transfers between devices: 16.9 us -> 17.2 us  [swap(): return lax.ppermute(value, axis, [(i, i ^ bit) for i in range(size)])]
  transfers between devices with their start and end apart: 15 -> 17, of which waited for: 12 -> 11; matrix products, arithmetic and copies ran while one was open for 0% -> 0% of each run, Pallas kernels for 11% -> 13%
where the time goes in v18:
time: 47.1 us; the launch traced here: 46.9 us
  starting transfers between devices  17.6 us (37%)
  waiting for transfers between devices  17.2 us (37%)
  Pallas kernels  11.2 us (24%)
  between operations  0.84 us (2%)
    ppermute x17, starting transfers between devices, swap(): return lax.ppermute(value, axis, [(i, i ^ bit) for i in range(size)])  17.6 us
    ppermute x17, waiting for transfers between devices, swap(): return lax.ppermute(value, axis, [(i, i ^ bit) for i in range(size)])  17.2 us
    pallas_call x18, Pallas kernels, call(): pl.pallas_call(kernel, out_shape=[jax.ShapeDtypeStruct(*x) for x in outs]...  11.2 us
  transfers between devices with their start and end apart: 17, of which 11 were waited for; matrix products, arithmetic and copies ran while one was open for 0% of the time, Pallas kernels for 13%

profile of v18, /device:TPU:0, one launch (start us, length us, event | category | flops | bytes accessed | tf_op | source)
XLA Modules:
  0.0 46.9 jit_solution(15892309209919474264)
XLA Ops:
  0.6 5.1 %collective-permute-start.1 = (bf16[1,64,128]{2,1,0:T(8,128)(2,1)}, bf16[1,64,128]{2,1,0:T(8,128)(2,1)S(1)}, u32[]{:S(2)}, u32[]{:S(2)}) collective-permute-start(bf16[1,64,128]{2,1,0:T(8,128)(2,1)} %refs_0_.1), channel_id=1, source_target_pairs={{0,12},{4,8},{8,4},{12,0},{1,13},{5,9},{9,5},{13,1},{2,14},{6,10},... | collective-permute-start | bytes 49160 | tf_op jit(solution)/shard_map/ppermute | solution.py:699
  5.8 0.6 %collective-permute-start.2 = (bf16[1,64,128]{2,1,0:T(8,128)(2,1)}, bf16[1,64,128]{2,1,0:T(8,128)(2,1)S(1)}, u32[]{:S(2)}, u32[]{:S(2)}) collective-permute-start(bf16[1,64,128]{2,1,0:T(8,128)(2,1)} %refs_0_.1), channel_id=1, source_target_pairs={{0,4},{4,0},{8,12},{12,8},{1,5},{5,1},{9,13},{13,9},{2,6},{6,2},{1... | collective-permute-start | bytes 49160 | tf_op jit(solution)/shard_map/ppermute | solution.py:699
  6.5 1.4 %shard_map.87 = (bf16[32,144,256]{2,1,0:T(8,128)(2,1)S(1)}, bf16[32,144,256]{2,1,0:T(8,128)(2,1)S(1)}) custom-call(bf16[288,64,128]{2,1,0:T(8,128)(2,1)S(1)} %copy-done.5, bf16[256,256]{1,0:T(8,128)(2,1)S(1)} %shard_map.86.permutation_ref), custom_call_target="tpu_custom_call" | custom-call | flops 2147483648 | bytes 9568256 | tf_op jit(solution)/shard_map/pallas_call | solution.py:94
  7.9 2.7 %collective-permute-done.refs_1_ = bf16[1,64,128]{2,1,0:T(8,128)(2,1)S(1)} collective-permute-done((bf16[1,64,128]{2,1,0:T(8,128)(2,1)}, bf16[1,64,128]{2,1,0:T(8,128)(2,1)S(1)}, u32[]{:S(2)}, u32[]{:S(2)}) %collective-permute-start) | collective-permute-done | bytes 16416 | tf_op jit(solution)/shard_map/ppermute | solution.py:699
  10.6 0.8 %shard_map.88 = (f32[576,128]{1,0:T(8,128)S(1)}, f32[576,128]{1,0:T(8,128)S(1)}, f32[4,128]{1,0:T(4,128)S(1)}, bf16[32,16,256]{2,1,0:T(8,128)(2,1)S(1)}) custom-call(bf16[1,64,128]{2,1,0:T(8,128)(2,1)S(1)} %copy-done.2, bf16[1,64,128]{2,1,0:T(8,128)(2,1)S(1)} %collective-permute-done.refs_1_, bf16[1,64,128]{2,1,0:T(8,128)(2,1)S(1)} %collective-permute-done.1.refs_2_, ...), custom_call_target="tpu_custom_call" | custom-call | flops 150994944 | bytes 3588096 | tf_op jit(solution)/shard_map/pallas_call | solution.py:94
  11.7 0.6 %collective-permute-start.4 = (f32[72,128]{1,0:T(8,128)S(1)}, f32[72,128]{1,0:T(8,128)S(1)}, u32[]{:S(2)}, u32[]{:S(2)}) collective-permute-start(f32[72,128]{1,0:T(8,128)S(1)} %shard_map.91), channel_id=1, source_target_pairs={{0,1},{1,0},{2,3},{3,2},{4,5},{5,4},{6,7},{7,6},{8,9},{9,8},{10,11... | collective-permute-start | bytes 110600 | tf_op jit(solution)/shard_map/ppermute | solution.py:699
  12.2 0.4 shard_map.89.prior_term
  12.7 1.2 %shard_map.90 = (f32[2,256,256]{2,1,0:T(8,128)S(1)}, f32[1,256,128]{2,1,0:T(8,128)S(1)}) custom-call(bf16[32,16,256]{2,1,0:T(8,128)(2,1)S(1)} %get-tuple-element.41.left_ref, bf16[32,144,256]{2,1,0:T(8,128)(2,1)S(1)} %get-tuple-element.42.particles, f32[4,128]{1,0:T(4,128)S(1)} %get-tuple-element.43.energy_ref, f32[256,256]{1,0:T(8,128)S(1)} %shard_map.89.prior_term, ...), custom_call_target="tpu_custom_call" | custom-call | flops 301989888 | bytes 4571136 | tf_op jit(solution)/shard_map/pallas_call | solution.py:94
  14.0 0.5 %shard_map.92 = (f32[2,256,256]{2,1,0:T(8,128)S(1)}, f32[1,256,128]{2,1,0:T(8,128)S(1)}, f32[2,256]{1,0:T(2,128)S(1)}, f32[1,128]{1,0:T(1,128)S(1)}, f32[8,256]{1,0:T(8,128)S(1)}) custom-call(f32[2,256,256]{2,1,0:T(8,128)S(1)} %get-tuple-element.44.partial, f32[1,256,128]{2,1,0:T(8,128)S(1)} %get-tuple-element.45.partial_more, ...), custom_call_target="tpu_custom_call" | custom-call | flops 402653184 | bytes 2080768 | tf_op jit(solution)/shard_map/pallas_call | solution.py:94
  14.5 1.1 %collective-permute-start.5 = (f32[8,256]{1,0:T(8,128)S(1)}, f32[8,256]{1,0:T(8,128)S(1)}, u32[]{:S(2)}, u32[]{:S(2)}) collective-permute-start(f32[8,256]{1,0:T(8,128)S(1)} %get-tuple-element.52.first), channel_id=1, source_target_pairs={{0,3},{1,2},{2,1},{3,0},{4,7},{5,6},{6,5},{7,4},{8,11},{9,10},{10,... | collective-permute-start | bytes 24584 | tf_op jit(solution)/shard_map/ppermute | solution.py:699
  15.7 2.0 %collective-permute-done.5.second = f32[8,256]{1,0:T(8,128)S(1)} collective-permute-done((f32[8,256]{1,0:T(8,128)S(1)}, f32[8,256]{1,0:T(8,128)S(1)}, u32[]{:S(2)}, u32[]{:S(2)}) %collective-permute-start.5) | collective-permute-done | bytes 8224 | tf_op jit(solution)/shard_map/ppermute | solution.py:699
  18.2 0.7 %shard_map.94.image = f32[576,128]{1,0:T(8,128)S(1)} custom-call(bf16[2,256,256]{2,1,0:T(8,128)(2,1)S(1)} %get-tuple-element.53.rounded_ref, bf16[1,256,128]{2,1,0:T(8,128)(2,1)S(1)} %get-tuple-element.54.rounded_more, bf16[512,512]{1,0:T(8,128)(2,1)S(1)} %copy-done, bf16[32,144,256]{2,1,0:T(8,128)(2,1)S(1)} %get-tuple-element.42.particles), custom_call_target="tpu_custom_call" | custom-call | flops 268435456 | bytes 4096000 | tf_op jit(solution)/shard_map/pallas_call | solution.py:94
  18.9 0.6 %collective-permute-done.6.spectrum = bf16[42,16,128]{2,1,0:T(8,128)(2,1)S(1)} collective-permute-done((bf16[42,16,128]{2,1,0:T(8,128)(2,1)S(1)}, bf16[42,16,128]{2,1,0:T(8,128)(2,1)S(1)}, u32[]{:S(2)}, u32[]{:S(2)}) %collective-permute-start.6) | collective-permute-done | bytes 172064 | tf_op jit(solution)/shard_map/ppermute | solution.py:699
  19.5 0.6 %shard_map.95.refs_0_ = bf16[272,128]{1,0:T(8,128)(2,1)S(1)} custom-call(f32[576,128]{1,0:T(8,128)S(1)} %shard_map.94.image, bf16[42,16,128]{2,1,0:T(8,128)(2,1)S(1)} %get-tuple-element.55.mine, bf16[42,16,128]{2,1,0:T(8,128)(2,1)S(1)} %collective-permute-done.6.spectrum, bf16[32,144,256]{2,1,0:T(8,128)(2,1)S(1)} %get-tuple-element.40.refs_5_.particles), custom_call_target="tpu_custom_call" | custom-call | flops 352321536 | bytes 3657728 | tf_op jit(solution)/shard_map/pallas_call | solution.py:94
  20.1 3.5 %collective-permute-start.8 = (bf16[272,128]{1,0:T(8,128)(2,1)S(1)}, bf16[272,128]{1,0:T(8,128)(2,1)S(1)}, u32[]{:S(2)}, u32[]{:S(2)}) collective-permute-start(bf16[272,128]{1,0:T(8,128)(2,1)S(1)} %shard_map.95.refs_0_), channel_id=1, source_target_pairs={{0,12},{4,8},{8,4},{12,0},{1,13},{5,9},{9,5},{13,1},{2,14},{6,10},... | collective-permute-start | bytes 208904 | tf_op jit(solution)/shard_map/ppermute | solution.py:699
  23.6 0.8 %collective-permute-done.9.refs_3_ = bf16[272,128]{1,0:T(8,128)(2,1)S(1)} collective-permute-done((bf16[272,128]{1,0:T(8,128)(2,1)S(1)}, bf16[272,128]{1,0:T(8,128)(2,1)S(1)}, u32[]{:S(2)}, u32[]{:S(2)}) %collective-permute-start.9) | collective-permute-done | bytes 69664 | tf_op jit(solution)/shard_map/ppermute | solution.py:699
  24.4 3.7 %collective-permute-done.8.refs_2_ = bf16[272,128]{1,0:T(8,128)(2,1)S(1)} collective-permute-done((bf16[272,128]{1,0:T(8,128)(2,1)S(1)}, bf16[272,128]{1,0:T(8,128)(2,1)S(1)}, u32[]{:S(2)}, u32[]{:S(2)}) %collective-permute-start.8) | collective-permute-done | bytes 69664 | tf_op jit(solution)/shard_map/ppermute | solution.py:699
  28.1 2.1 %collective-permute-done.7.refs_1_ = bf16[272,128]{1,0:T(8,128)(2,1)S(1)} collective-permute-done((bf16[272,128]{1,0:T(8,128)(2,1)S(1)}, bf16[272,128]{1,0:T(8,128)(2,1)S(1)}, u32[]{:S(2)}, u32[]{:S(2)}) %collective-permute-start.7) | collective-permute-done | bytes 69664 | tf_op jit(solution)/shard_map/ppermute | solution.py:699
  30.3 0.8 %shard_map.96 = (f32[576,128]{1,0:T(8,128)S(1)}, f32[576,128]{1,0:T(8,128)S(1)}, f32[4,128]{1,0:T(4,128)S(1)}, bf16[32,16,256]{2,1,0:T(8,128)(2,1)S(1)}) custom-call(bf16[272,128]{1,0:T(8,128)(2,1)S(1)} %shard_map.95.refs_0_, bf16[272,128]{1,0:T(8,128)(2,1)S(1)} %collective-permute-done.7.refs_1_, bf16[272,128]{1,0:T(8,128)(2,1)S(1)} %collective-permute-done.8.refs_2_, ...), custom_call_target="tpu_custom_call" | custom-call | flops 150994944 | bytes 3801088 | tf_op jit(solution)/shard_map/pallas_call | solution.py:94
  31.3 0.5 %collective-permute-start.11 = (f32[72,128]{1,0:T(8,128)S(1)}, f32[72,128]{1,0:T(8,128)S(1)}, u32[]{:S(2)}, u32[]{:S(2)}) collective-permute-start(f32[72,128]{1,0:T(8,128)S(1)} %shard_map.98), channel_id=1, source_target_pairs={{0,1},{1,0},{2,3},{3,2},{4,5},{5,4},{6,7},{7,6},{8,9},{9,8},{10,11... | collective-permute-start | bytes 110600 | tf_op jit(solution)/shard_map/ppermute | solution.py:699
  31.9 1.2 %shard_map.97 = (f32[2,256,256]{2,1,0:T(8,128)S(1)}, f32[1,256,128]{2,1,0:T(8,128)S(1)}) custom-call(bf16[32,16,256]{2,1,0:T(8,128)(2,1)S(1)} %get-tuple-element.56.left_ref, bf16[32,144,256]{2,1,0:T(8,128)(2,1)S(1)} %get-tuple-element.42.particles, f32[4,128]{1,0:T(4,128)S(1)} %get-tuple-element.57.energy_ref, f32[256,256]{1,0:T(8,128)S(1)} %shard_map.89.prior_term, ...), custom_call_target="tpu_custom_call" | custom-call | flops 301989888 | bytes 4571136 | tf_op jit(solution)/shard_map/pallas_call | solution.py:94
  33.1 0.5 %shard_map.99 = (f32[2,256,256]{2,1,0:T(8,128)S(1)}, f32[1,256,128]{2,1,0:T(8,128)S(1)}, f32[2,256]{1,0:T(2,128)S(1)}, f32[1,128]{1,0:T(1,128)S(1)}, f32[8,256]{1,0:T(8,128)S(1)}) custom-call(f32[2,256,256]{2,1,0:T(8,128)S(1)} %get-tuple-element.58.partial, f32[1,256,128]{2,1,0:T(8,128)S(1)} %get-tuple-element.59.partial_more, ...), custom_call_target="tpu_custom_call" | custom-call | flops 402653184 | bytes 2080768 | tf_op jit(solution)/shard_map/pallas_call | solution.py:94
  33.7 1.1 %collective-permute-start.12 = (f32[8,256]{1,0:T(8,128)S(1)}, f32[8,256]{1,0:T(8,128)S(1)}, u32[]{:S(2)}, u32[]{:S(2)}) collective-permute-start(f32[8,256]{1,0:T(8,128)S(1)} %get-tuple-element.66.first), channel_id=1, source_target_pairs={{0,3},{1,2},{2,1},{3,0},{4,7},{5,6},{6,5},{7,4},{8,11},{9,10},{10,... | collective-permute-start | bytes 24584 | tf_op jit(solution)/shard_map/ppermute | solution.py:699
  34.8 2.0 %collective-permute-done.12.second = f32[8,256]{1,0:T(8,128)S(1)} collective-permute-done((f32[8,256]{1,0:T(8,128)S(1)}, f32[8,256]{1,0:T(8,128)S(1)}, u32[]{:S(2)}, u32[]{:S(2)}) %collective-permute-start.12) | collective-permute-done | bytes 8224 | tf_op jit(solution)/shard_map/ppermute | solution.py:699
  37.4 0.7 %shard_map.101.image = f32[576,128]{1,0:T(8,128)S(1)} custom-call(bf16[2,256,256]{2,1,0:T(8,128)(2,1)S(1)} %get-tuple-element.67.rounded_ref, bf16[1,256,128]{2,1,0:T(8,128)(2,1)S(1)} %get-tuple-element.68.rounded_more, bf16[512,512]{1,0:T(8,128)(2,1)S(1)} %copy-done, bf16[32,144,256]{2,1,0:T(8,128)(2,1)S(1)} %get-tuple-element.42.particles), custom_call_target="tpu_custom_call" | custom-call | flops 268435456 | bytes 4096000 | tf_op jit(solution)/shard_map/pallas_call | solution.py:94
  38.0 0.6 %collective-permute-done.13.spectrum = bf16[42,16,128]{2,1,0:T(8,128)(2,1)S(1)} collective-permute-done((bf16[42,16,128]{2,1,0:T(8,128)(2,1)S(1)}, bf16[42,16,128]{2,1,0:T(8,128)(2,1)S(1)}, u32[]{:S(2)}, u32[]{:S(2)}) %collective-permute-start.13) | collective-permute-done | bytes 172064 | tf_op jit(solution)/shard_map/ppermute | solution.py:699
  38.7 0.6 %shard_map.102 = (f32[72,128]{1,0:T(8,128)S(1)}, f32[72,128]{1,0:T(8,128)S(1)}, f32[72,128]{1,0:T(8,128)S(1)}, f32[72,128]{1,0:T(8,128)S(1)}, f32[1,144]{1,0:T(1,128)S(1)}) custom-call(f32[576,128]{1,0:T(8,128)S(1)} %shard_map.101.image, bf16[42,16,128]{2,1,0:T(8,128)(2,1)S(1)} %get-tuple-element.69.mine, ...), custom_call_target="tpu_custom_call" | custom-call | flops 352321536 | bytes 3768320 | tf_op jit(solution)/shard_map/pallas_call | solution.py:94
  39.2 1.7 %collective-permute-start.14 = (f32[72,128]{1,0:T(8,128)S(1)}, f32[72,128]{1,0:T(8,128)S(1)}, u32[]{:S(2)}, u32[]{:S(2)}) collective-permute-start(f32[72,128]{1,0:T(8,128)S(1)} %get-tuple-element.70), channel_id=1, source_target_pairs={{0,12},{4,8},{8,4},{12,0},{1,13},{5,9},{9,5},{13,1},{2,14},{6,10},... | collective-permute-start | bytes 110600 | tf_op jit(solution)/shard_map/ppermute | solution.py:699
  40.9 2.8 %collective-permute-start.16 = (f32[72,128]{1,0:T(8,128)S(1)}, f32[72,128]{1,0:T(8,128)S(1)}, u32[]{:S(2)}, u32[]{:S(2)}) collective-permute-start(f32[72,128]{1,0:T(8,128)S(1)} %get-tuple-element.72), channel_id=1, source_target_pairs={{0,4},{4,0},{8,12},{12,8},{1,5},{5,1},{9,13},{13,9},{2,6},{6,2},{1... | collective-permute-start | bytes 110600 | tf_op jit(solution)/shard_map/ppermute | solution.py:699
  43.7 1.4 %collective-permute-done.14.refs_0_ = f32[72,128]{1,0:T(8,128)S(1)} collective-permute-done((f32[72,128]{1,0:T(8,128)S(1)}, f32[72,128]{1,0:T(8,128)S(1)}, u32[]{:S(2)}, u32[]{:S(2)}) %collective-permute-start.14) | collective-permute-done | bytes 36896 | tf_op jit(solution)/shard_map/ppermute | solution.py:699
  45.1 1.2 %collective-permute-done.15.refs_1_ = f32[72,128]{1,0:T(8,128)S(1)} collective-permute-done((f32[72,128]{1,0:T(8,128)S(1)}, f32[72,128]{1,0:T(8,128)S(1)}, u32[]{:S(2)}, u32[]{:S(2)}) %collective-permute-start.15) | collective-permute-done | bytes 36896 | tf_op jit(solution)/shard_map/ppermute | solution.py:699
  46.3 0.6 %shard_map.103 = (f32[1,64,128]{2,1,0:T(8,128)}, f32[1,144]{1,0:T(1,128)}) custom-call(f32[72,128]{1,0:T(8,128)S(1)} %collective-permute-done.14.refs_0_, f32[72,128]{1,0:T(8,128)S(1)} %collective-permute-done.15.refs_1_, f32[72,128]{1,0:T(8,128)S(1)} %collective-permute-done.16.refs_2_, f32[72,128]{1,0:T(8,128)S(1)} %get-tuple-element.73.refs_3_, ...), custom_call_target="tpu_custom_call" | custom-call | bytes 245760 | tf_op jit(solution)/shard_map/pallas_call | solution.py:94
  (34 shorter events, 1.8 us)
Async XLA Ops:
  0.6 5.8 %copy-start.5 = (bf16[288,64,128]{2,1,0:T(8,128)(2,1)S(1)}, bf16[288,64,128]{2,1,0:T(8,128)(2,1)}, u32[]{:S(2)}) copy-start(bf16[288,64,128]{2,1,0:T(8,128)(2,1)} %particles_ref.1) | copy-start | bytes 14155780
  0.6 7.3 %collective-permute-start.1 = (bf16[1,64,128]{2,1,0:T(8,128)(2,1)}, bf16[1,64,128]{2,1,0:T(8,128)(2,1)S(1)}, u32[]{:S(2)}, u32[]{:S(2)}) collective-permute-start(bf16[1,64,128]{2,1,0:T(8,128)(2,1)} %refs_0_.1), channel_id=1, source_target_pairs={{0,12},{4,8},{8,4},{12,0},{1,13},{5,9},{9,5},{13,1},{2,14},{6,10},... | collective-permute-start | bytes 49160 | tf_op jit(solution)/shard_map/ppermute | solution.py:699
  5.8 4.8 %collective-permute-start = (bf16[1,64,128]{2,1,0:T(8,128)(2,1)}, bf16[1,64,128]{2,1,0:T(8,128)(2,1)S(1)}, u32[]{:S(2)}, u32[]{:S(2)}) collective-permute-start(bf16[1,64,128]{2,1,0:T(8,128)(2,1)} %refs_0_.1), channel_id=1, source_target_pairs={{0,8},{4,12},{8,0},{12,4},{1,9},{5,13},{9,1},{13,5},{2,10},{6,14},... | collective-permute-start | bytes 49160 | tf_op jit(solution)/shard_map/ppermute | solution.py:699
  5.8 4.8 %collective-permute-start.2 = (bf16[1,64,128]{2,1,0:T(8,128)(2,1)}, bf16[1,64,128]{2,1,0:T(8,128)(2,1)S(1)}, u32[]{:S(2)}, u32[]{:S(2)}) collective-permute-start(bf16[1,64,128]{2,1,0:T(8,128)(2,1)} %refs_0_.1), channel_id=1, source_target_pairs={{0,4},{4,0},{8,12},{12,8},{1,5},{5,1},{9,13},{13,9},{2,6},{6,2},{1... | collective-permute-start | bytes 49160 | tf_op jit(solution)/shard_map/ppermute | solution.py:699
  6.5 4.1 %copy-start.2 = (bf16[1,64,128]{2,1,0:T(8,128)(2,1)S(1)}, bf16[1,64,128]{2,1,0:T(8,128)(2,1)}, u32[]{:S(2)}) copy-start(bf16[1,64,128]{2,1,0:T(8,128)(2,1)} %refs_0_.1) | copy-start | bytes 49156
  6.5 4.1 %copy-start.4 = (f32[64]{0:T(128)S(1)}, f32[64]{0:T(128)}, u32[]{:S(2)}) copy-start(f32[64]{0:T(128)} %param.9) | copy-start | bytes 772
  7.9 4.3 %copy-start.3 = (s32[288]{0:T(512)S(1)}, s32[288]{0:T(512)}, u32[]{:S(2)}) copy-start(s32[288]{0:T(512)} %prior_ref.1) | copy-start | bytes 3460
  7.9 4.8 %copy-start.1 = (bf16[512,384]{1,0:T(8,128)(2,1)S(1)}, bf16[512,384]{1,0:T(8,128)(2,1)}, u32[]{:S(2)}) copy-start(bf16[512,384]{1,0:T(8,128)(2,1)} %constant.6.clone.table) | copy-start | bytes 1179652
  11.5 2.5 %copy-start.6 = (bf16[512,384]{1,0:T(8,128)(2,1)S(1)}, bf16[512,384]{1,0:T(8,128)(2,1)}, u32[]{:S(2)}) copy-start(bf16[512,384]{1,0:T(8,128)(2,1)} %constant.7.clone.table) | copy-start | bytes 1179652
  11.5 2.5 %collective-permute-start.3 = (f32[576,128]{1,0:T(8,128)S(1)}, f32[576,128]{1,0:T(8,128)S(1)}, u32[]{:S(2)}, u32[]{:S(2)}) collective-permute-start(f32[576,128]{1,0:T(8,128)S(1)} %get-tuple-element.46), channel_id=1, source_target_pairs={{0,1},{1,0},{2,3},{3,2},{4,5},{5,4},{6,7},{7,6},{8,9},{9,8},{10,11... | collective-permute-start | bytes 884744 | tf_op jit(solution)/shard_map/ppermute | solution.py:699
  11.7 2.3 %collective-permute-start.4 = (f32[72,128]{1,0:T(8,128)S(1)}, f32[72,128]{1,0:T(8,128)S(1)}, u32[]{:S(2)}, u32[]{:S(2)}) collective-permute-start(f32[72,128]{1,0:T(8,128)S(1)} %shard_map.91), channel_id=1, source_target_pairs={{0,1},{1,0},{2,3},{3,2},{4,5},{5,4},{6,7},{7,6},{8,9},{9,8},{10,11... | collective-permute-start | bytes 110600 | tf_op jit(solution)/shard_map/ppermute | solution.py:699
  12.7 4.9 %copy-start = (bf16[512,512]{1,0:T(8,128)(2,1)S(1)}, bf16[512,512]{1,0:T(8,128)(2,1)}, u32[]{:S(2)}) copy-start(bf16[512,512]{1,0:T(8,128)(2,1)} %constant.8.clone.forward) | copy-start | bytes 1572868
  14.5 3.1 %collective-permute-start.5 = (f32[8,256]{1,0:T(8,128)S(1)}, f32[8,256]{1,0:T(8,128)S(1)}, u32[]{:S(2)}, u32[]{:S(2)}) collective-permute-start(f32[8,256]{1,0:T(8,128)S(1)} %get-tuple-element.52.first), channel_id=1, source_target_pairs={{0,3},{1,2},{2,1},{3,0},{4,7},{5,6},{6,5},{7,4},{8,11},{9,10},{10,... | collective-permute-start | bytes 24584 | tf_op jit(solution)/shard_map/ppermute | solution.py:699
  18.0 1.5 %collective-permute-start.6 = (bf16[42,16,128]{2,1,0:T(8,128)(2,1)S(1)}, bf16[42,16,128]{2,1,0:T(8,128)(2,1)S(1)}, u32[]{:S(2)}, u32[]{:S(2)}) collective-permute-start(bf16[42,16,128]{2,1,0:T(8,128)(2,1)S(1)} %get-tuple-element.55.mine), channel_id=1, source_target_pairs={{0,1},{1,0},{2,3},{3,2},{4,5},{5,4},{6,7},{7,6},{8,9},{9,8},{10,11... | collective-permute-start | bytes 516104 | tf_op jit(solution)/shard_map/ppermute | solution.py:699
  20.1 4.4 %collective-permute-start.9 = (bf16[272,128]{1,0:T(8,128)(2,1)S(1)}, bf16[272,128]{1,0:T(8,128)(2,1)S(1)}, u32[]{:S(2)}, u32[]{:S(2)}) collective-permute-start(bf16[272,128]{1,0:T(8,128)(2,1)S(1)} %shard_map.95.refs_0_), channel_id=1, source_target_pairs={{0,4},{4,0},{8,12},{12,8},{1,5},{5,1},{9,13},{13,9},{2,6},{6,2},{1... | collective-permute-start | bytes 208904 | tf_op jit(solution)/shard_map/ppermute | solution.py:699
  20.1 8.0 %collective-permute-start.8 = (bf16[272,128]{1,0:T(8,128)(2,1)S(1)}, bf16[272,128]{1,0:T(8,128)(2,1)S(1)}, u32[]{:S(2)}, u32[]{:S(2)}) collective-permute-start(bf16[272,128]{1,0:T(8,128)(2,1)S(1)} %shard_map.95.refs_0_), channel_id=1, source_target_pairs={{0,12},{4,8},{8,4},{12,0},{1,13},{5,9},{9,5},{13,1},{2,14},{6,10},... | collective-permute-start | bytes 208904 | tf_op jit(solution)/shard_map/ppermute | solution.py:699
  23.6 6.7 %collective-permute-start.7 = (bf16[272,128]{1,0:T(8,128)(2,1)S(1)}, bf16[272,128]{1,0:T(8,128)(2,1)S(1)}, u32[]{:S(2)}, u32[]{:S(2)}) collective-permute-start(bf16[272,128]{1,0:T(8,128)(2,1)S(1)} %shard_map.95.refs_0_), channel_id=1, source_target_pairs={{0,8},{4,12},{8,0},{12,4},{1,9},{5,13},{9,1},{13,5},{2,10},{6,14},... | collective-permute-start | bytes 208904 | tf_op jit(solution)/shard_map/ppermute | solution.py:699
  31.1 2.0 %collective-permute-start.10 = (f32[576,128]{1,0:T(8,128)S(1)}, f32[576,128]{1,0:T(8,128)S(1)}, u32[]{:S(2)}, u32[]{:S(2)}) collective-permute-start(f32[576,128]{1,0:T(8,128)S(1)} %get-tuple-element.60), channel_id=1, source_target_pairs={{0,1},{1,0},{2,3},{3,2},{4,5},{5,4},{6,7},{7,6},{8,9},{9,8},{10,11... | collective-permute-start | bytes 884744 | tf_op jit(solution)/shard_map/ppermute | solution.py:699
  31.3 1.8 %collective-permute-start.11 = (f32[72,128]{1,0:T(8,128)S(1)}, f32[72,128]{1,0:T(8,128)S(1)}, u32[]{:S(2)}, u32[]{:S(2)}) collective-permute-start(f32[72,128]{1,0:T(8,128)S(1)} %shard_map.98), channel_id=1, source_target_pairs={{0,1},{1,0},{2,3},{3,2},{4,5},{5,4},{6,7},{7,6},{8,9},{9,8},{10,11... | collective-permute-start | bytes 110600 | tf_op jit(solution)/shard_map/ppermute | solution.py:699
  33.7 3.1 %collective-permute-start.12 = (f32[8,256]{1,0:T(8,128)S(1)}, f32[8,256]{1,0:T(8,128)S(1)}, u32[]{:S(2)}, u32[]{:S(2)}) collective-permute-start(f32[8,256]{1,0:T(8,128)S(1)} %get-tuple-element.66.first), channel_id=1, source_target_pairs={{0,3},{1,2},{2,1},{3,0},{4,7},{5,6},{6,5},{7,4},{8,11},{9,10},{10,... | collective-permute-start | bytes 24584 | tf_op jit(solution)/shard_map/ppermute | solution.py:699
  37.2 1.5 %collective-permute-start.13 = (bf16[42,16,128]{2,1,0:T(8,128)(2,1)S(1)}, bf16[42,16,128]{2,1,0:T(8,128)(2,1)S(1)}, u32[]{:S(2)}, u32[]{:S(2)}) collective-permute-start(bf16[42,16,128]{2,1,0:T(8,128)(2,1)S(1)} %get-tuple-element.69.mine), channel_id=1, source_target_pairs={{0,1},{1,0},{2,3},{3,2},{4,5},{5,4},{6,7},{7,6},{8,9},{9,8},{10,11... | collective-permute-start | bytes 516104 | tf_op jit(solution)/shard_map/ppermute | solution.py:699
  39.2 5.8 %collective-permute-start.14 = (f32[72,128]{1,0:T(8,128)S(1)}, f32[72,128]{1,0:T(8,128)S(1)}, u32[]{:S(2)}, u32[]{:S(2)}) collective-permute-start(f32[72,128]{1,0:T(8,128)S(1)} %get-tuple-element.70), channel_id=1, source_target_pairs={{0,12},{4,8},{8,4},{12,0},{1,13},{5,9},{9,5},{13,1},{2,14},{6,10},... | collective-permute-start | bytes 110600 | tf_op jit(solution)/shard_map/ppermute | solution.py:699
  40.9 5.3 %collective-permute-start.15 = (f32[72,128]{1,0:T(8,128)S(1)}, f32[72,128]{1,0:T(8,128)S(1)}, u32[]{:S(2)}, u32[]{:S(2)}) collective-permute-start(f32[72,128]{1,0:T(8,128)S(1)} %get-tuple-element.71), channel_id=1, source_target_pairs={{0,8},{4,12},{8,0},{12,4},{1,9},{5,13},{9,1},{13,5},{2,10},{6,14},... | collective-permute-start | bytes 110600 | tf_op jit(solution)/shard_map/ppermute | solution.py:699
  40.9 5.4 %collective-permute-start.16 = (f32[72,128]{1,0:T(8,128)S(1)}, f32[72,128]{1,0:T(8,128)S(1)}, u32[]{:S(2)}, u32[]{:S(2)}) collective-permute-start(f32[72,128]{1,0:T(8,128)S(1)} %get-tuple-element.72), channel_id=1, source_target_pairs={{0,4},{4,0},{8,12},{12,8},{1,5},{5,1},{9,13},{13,9},{2,6},{6,2},{1... | collective-permute-start | bytes 110600 | tf_op jit(solution)/shard_map/ppermute | solution.py:699

commit v19 on v17

--- a/solution.py
+++ b/solution.py
@@ -222,17 +222,18 @@
     none = jnp.zeros((2 * classes, depth), BF16)
 
     def correlate(f):
-        first, second = [
-            image[pl.ds(2 * f + part, 2 * classes, stride=pitch), :].astype(BF16)
-            for part in range(2)
-        ]
-        left = jnp.concatenate(
-            [jnp.concatenate([first, none], 1), jnp.concatenate([none, second], 1)], 0
-        )
-        left_ref[f] = left
-        place(out, rest, f, times(left, particles[f]), classes, pitch)
-
-    loop(pairs, correlate, 32)
+        lefts = []
+        for first, second in pick(image, f, classes):
+            first, second = first.astype(BF16), second.astype(BF16)
+            left = jnp.concatenate(
+                [jnp.concatenate([first, none], 1), jnp.concatenate([none, second], 1)], 0
+            )
+            left_ref[f + len(lefts)] = left
+            lefts.append(left)
+        values = [times(left, particles[f + i]) for i, left in enumerate(lefts)]
+        place(out, rest, f, values, classes, pitch)
+
+    every(pairs, correlate)
     pack(out, rest, classes, share, pitch)
 
 
@@ -240,15 +241,35 @@
     return lax.dot_general(left, particles, (((1,), (1,)), ((), ())), preferred_element_type=F32)
 
 
-def place(out, rest, f, value, classes, pitch):
-    width = value.shape[1] - 128
-    spare = jnp.zeros((value.shape[0], 128 - width), F32)
-    value = jnp.concatenate([value, spare], 1)
-    for part in range(2):
-        at = pl.ds(2 * f + part, 2 * classes, stride=pitch)
-        mine = value[part * 2 * classes : (part + 1) * 2 * classes]
-        out[at, :] = mine[:, :128]
-        rest[at, :] = mine[:, 128:]
+GROUP = 4
+
+
+def every(pairs, body):
+    for f in range(0, pairs, GROUP):
+        body(f)
+
+
+def put(ref, f, blocks, pitch):
+    turned_blocks = jnp.swapaxes(jnp.stack(blocks, 0), 0, 1)
+    for i in range(blocks[0].shape[0]):
+        ref[pl.ds(i * pitch + 2 * f, 2 * GROUP), :] = turned_blocks[i]
+
+
+def pick(ref, f, classes):
+    pitch = ref.shape[0] // (2 * classes)
+    blocks = [ref[pl.ds(i * pitch + 2 * f, 2 * GROUP), :] for i in range(2 * classes)]
+    blocks = jnp.swapaxes(jnp.stack(blocks, 0), 0, 1)
+    return [(blocks[2 * i], blocks[2 * i + 1]) for i in range(GROUP)]
+
+
+def place(out, rest, f, values, classes, pitch):
+    width = values[0].shape[1] - 128
+    spare = jnp.zeros((2 * classes, 128 - width), F32)
+    parts = [
+        value[part * 2 * classes : (part + 1) * 2 * classes] for value in values for part in range(2)
+    ]
+    put(out, f, [part[:, :128] for part in parts], pitch)
+    put(rest, f, [jnp.concatenate([part[:, 128:], spare], 1) for part in parts], pitch)
 
 
 def pack(out, rest, classes, share, pitch):
@@ -298,9 +319,10 @@
     pitch = 2 * pairs + SPARE
 
     def body(f):
-        place(out, rest, f, times(left_ref[f], particles[f]), classes, pitch)
-
-    loop(pairs, body, 32)
+        values = [times(left_ref[f + i], particles[f + i]) for i in range(GROUP)]
+        place(out, rest, f, values, classes, pitch)
+
+    every(pairs, body)
     pack(out, rest, classes, share, pitch)
 
 
@@ -432,7 +454,7 @@
     lane = lax.broadcasted_iota(jnp.int32, (1, 128), 1)
     line = lax.broadcasted_iota(jnp.int32, (4 * classes, 128), 0)
 
-    def put(column, k, count):
+    def with_count(column, k, count):
         high = count.astype(BF16).astype(F32)
         return jnp.where(line == k, high, jnp.where(line == classes + k, count - high, column))
 
@@ -465,13 +487,13 @@
         count = jnp.sum(value, axis=0, keepdims=True)
         for j in range(2):
             mine = jnp.sum(count[:, j * 128 : (j + 1) * 128], axis=1, keepdims=True)
-            column = put(column, 2 * i + j, mine)
+            column = with_count(column, 2 * i + j, mine)
         return column
 
     column = each(classes // 2, body, jnp.zeros((4 * classes, 128), F32))
     extra = jnp.zeros((4 * classes, 128), F32)
     for k, count in enumerate(more_counts):
-        extra = put(extra, k, count)
+        extra = with_count(extra, k, count)
     for ref in last:
         ref[...] = evidence[:, :share]
         high = evidence.astype(BF16).astype(F32)
@@ -484,9 +506,10 @@
     send[send.shape[0] - 1] = extra.astype(BF16)
 
     def rearrange(f):
-        send[f] = pick(held, f, classes).astype(BF16)
-
-    loop(pairs, rearrange, 32)
+        for i, parts in enumerate(pick(held, f, classes)):
+            send[f + i] = jnp.concatenate(parts, 0).astype(BF16)
+
+    every(pairs, rearrange)
 
 
 def spread(held, i, value):
@@ -508,13 +531,6 @@
             held[rows((2 * k + part) * (freqs + SPARE), freqs), :] = shifted[
                 part * freqs : (part + 1) * freqs
             ]
-
-
-def pick(held, f, classes):
-    pitch = held.shape[0] // (2 * classes)
-    return jnp.concatenate(
-        [held[pl.ds(2 * f + part, 2 * classes, stride=pitch), :] for part in range(2)], 0
-    )
 
 
 def message_shape(classes, pairs, units):
@@ -556,11 +572,13 @@
     each(classes // 2, body, 0)
 
     def accumulate(f):
-        left = [pick(ref, f, classes).astype(BF16) for ref in (held, held_more)]
-        left = jnp.concatenate(left, 1)[:, :share]
-        take_in(image, f, dot(left, particles[f]), classes)
-
-    loop(pairs, accumulate, 32)
+        values = []
+        for i, both in enumerate(zip(pick(held, f, classes), pick(held_more, f, classes))):
+            left = [jnp.concatenate(parts, 0).astype(BF16) for parts in both]
+            values.append(dot(jnp.concatenate(left, 1)[:, :share], particles[f + i]))
+        take_in(image, f, values, classes)
+
+    every(pairs, accumulate)
 
 
 def gather(rounded, rounded_more, forward, particles):
@@ -576,13 +594,14 @@
     )[0]
 
 
-def take_in(image, f, value, classes):
+def take_in(image, f, values, classes):
     lines, depth = image.shape
-    for part in range(2):
-        at = pl.ds(2 * f + part, 2 * classes, stride=lines // (2 * classes))
-        image[at, :] = value[
-            part * 2 * classes : (part + 1) * 2 * classes, part * depth : (part + 1) * depth
-        ]
+    blocks = [
+        value[part * 2 * classes : (part + 1) * 2 * classes, part * depth : (part + 1) * depth]
+        for value in values
+        for part in range(2)
+    ]
+    put(image, f, blocks, lines // (2 * classes))
 
 
 def finish_kernel(image, mine, spectrum, particles, *refs):
@@ -602,10 +621,14 @@
         spread_more(held_more, unit, value.astype(F32), classes, share)
 
     def body(f):
-        left = jnp.concatenate([spectrum[f], pick(held_more, f, classes).astype(BF16)], 1)
-        take_in(held, f, dot(left[:, :share], particles[f]), classes)
-
-    loop(pairs, body, 32)
+        values = []
+        for i, parts in enumerate(pick(held_more, f, classes)):
+            left = jnp.concatenate(parts, 0).astype(BF16)
+            left = jnp.concatenate([spectrum[f + i], left], 1)[:, :share]
+            values.append(dot(left, particles[f + i]))
+        take_in(held, f, values, classes)
+
+    every(pairs, body)
     end = spectrum.shape[0]
     counts = sum(ref[i].astype(F32) for ref in (mine, spectrum) for i in (end - 2, end - 1))
     if evidence_ref is not None:

time: 45.1 us -> 45 us (level)
  no operation moved by 1% of the time
where the time goes in v19:
time: 45 us; the launch traced here: 44.9 us
  waiting for transfers between devices  16.9 us (38%)
  starting transfers between devices  16.7 us (37%)
  Pallas kernels  10.5 us (23%)
  between operations  0.78 us (2%)
    ppermute x15, waiting for transfers between devices, swap(): return lax.ppermute(value, axis, [(i, i ^ bit) for i in range(size)])  16.9 us
    ppermute x15, starting transfers between devices, swap(): return lax.ppermute(value, axis, [(i, i ^ bit) for i in range(size)])  16.7 us
    pallas_call x16, Pallas kernels, call(): pl.pallas_call(kernel, out_shape=[jax.ShapeDtypeStruct(*x) for x in outs]...  10.5 us
  transfers between devices with their start and end apart: 15, of which 12 were waited for; matrix products, arithmetic and copies ran while one was open for 0% of the time, Pallas kernels for 11%

profile of v19, /device:TPU:0, one launch (start us, length us, event | category | flops | bytes accessed | tf_op | source)
XLA Modules:
  0.0 44.9 jit_solution(16192832800143347474)
XLA Ops:
  0.6 4.1 %collective-permute-start.1 = (bf16[1,64,128]{2,1,0:T(8,128)(2,1)}, bf16[1,64,128]{2,1,0:T(8,128)(2,1)S(1)}, u32[]{:S(2)}, u32[]{:S(2)}) collective-permute-start(bf16[1,64,128]{2,1,0:T(8,128)(2,1)} %refs_0_.1), channel_id=1, source_target_pairs={{0,8},{4,12},{8,0},{12,4},{1,9},{5,13},{9,1},{13,5},{2,10},{6,14},... | collective-permute-start | bytes 49160 | tf_op jit(solution)/shard_map/ppermute | solution.py:690
  4.7 1.3 %collective-permute-start = (bf16[1,64,128]{2,1,0:T(8,128)(2,1)}, bf16[1,64,128]{2,1,0:T(8,128)(2,1)S(1)}, u32[]{:S(2)}, u32[]{:S(2)}) collective-permute-start(bf16[1,64,128]{2,1,0:T(8,128)(2,1)} %refs_0_.1), channel_id=1, source_target_pairs={{0,12},{4,8},{8,4},{12,0},{1,13},{5,9},{9,5},{13,1},{2,14},{6,10},... | collective-permute-start | bytes 49160 | tf_op jit(solution)/shard_map/ppermute | solution.py:690
  6.4 1.4 %shard_map.78 = (bf16[32,144,256]{2,1,0:T(8,128)(2,1)S(1)}, bf16[32,144,256]{2,1,0:T(8,128)(2,1)S(1)}) custom-call(bf16[288,64,128]{2,1,0:T(8,128)(2,1)S(1)} %copy-done.5, bf16[256,256]{1,0:T(8,128)(2,1)S(1)} %shard_map.77.permutation_ref), custom_call_target="tpu_custom_call" | custom-call | flops 2147483648 | bytes 9568256 | tf_op jit(solution)/shard_map/pallas_call | solution.py:93
  7.8 2.6 %collective-permute-done.refs_1_ = bf16[1,64,128]{2,1,0:T(8,128)(2,1)S(1)} collective-permute-done((bf16[1,64,128]{2,1,0:T(8,128)(2,1)}, bf16[1,64,128]{2,1,0:T(8,128)(2,1)S(1)}, u32[]{:S(2)}, u32[]{:S(2)}) %collective-permute-start) | collective-permute-done | bytes 16416 | tf_op jit(solution)/shard_map/ppermute | solution.py:690
  10.5 0.9 %shard_map.79 = (f32[648,128]{1,0:T(8,128)S(1)}, f32[4,128]{1,0:T(4,128)S(1)}, bf16[32,16,256]{2,1,0:T(8,128)(2,1)S(1)}) custom-call(bf16[1,64,128]{2,1,0:T(8,128)(2,1)S(1)} %copy-done.2, bf16[1,64,128]{2,1,0:T(8,128)(2,1)S(1)} %collective-permute-done.refs_1_, bf16[1,64,128]{2,1,0:T(8,128)(2,1)S(1)} %collective-permute-done.1.refs_2_, ...), custom_call_target="tpu_custom_call" | custom-call | flops 150994944 | bytes 3629056 | tf_op jit(solution)/shard_map/pallas_call | solution.py:93
  11.9 0.8 %shard_map.80.own = f32[648,128]{1,0:T(8,128)S(1)} custom-call(bf16[32,16,256]{2,1,0:T(8,128)(2,1)S(1)} %get-tuple-element.35.left_ref, bf16[32,144,256]{2,1,0:T(8,128)(2,1)S(1)} %get-tuple-element.36.particles), custom_call_target="tpu_custom_call" | custom-call | flops 301989888 | bytes 3252224 | tf_op jit(solution)/shard_map/pallas_call | solution.py:93
  13.1 0.6 %shard_map.82 = (f32[2,256,256]{2,1,0:T(8,128)S(1)}, f32[1,256,128]{2,1,0:T(8,128)S(1)}, f32[2,256]{1,0:T(2,128)S(1)}, f32[1,128]{1,0:T(1,128)S(1)}, f32[8,256]{1,0:T(8,128)S(1)}) custom-call(f32[648,128]{1,0:T(8,128)S(1)} %shard_map.80.own, f32[648,128]{1,0:T(8,128)S(1)} %collective-permute-done.3.other, f32[4,128]{1,0:T(4,128)S(1)} %get-tuple-element.38.energy_ref, ...), custom_call_target="tpu_custom_call" | custom-call | flops 402653184 | bytes 2424832 | tf_op jit(solution)/shard_map/pallas_call | solution.py:93
  13.7 1.3 %collective-permute-start.4 = (f32[8,256]{1,0:T(8,128)S(1)}, f32[8,256]{1,0:T(8,128)S(1)}, u32[]{:S(2)}, u32[]{:S(2)}) collective-permute-start(f32[8,256]{1,0:T(8,128)S(1)} %get-tuple-element.43.first), channel_id=1, source_target_pairs={{0,3},{1,2},{2,1},{3,0},{4,7},{5,6},{6,5},{7,4},{8,11},{9,10},{10,... | collective-permute-start | bytes 24584 | tf_op jit(solution)/shard_map/ppermute | solution.py:690
  15.0 1.8 %collective-permute-done.4.second = f32[8,256]{1,0:T(8,128)S(1)} collective-permute-done((f32[8,256]{1,0:T(8,128)S(1)}, f32[8,256]{1,0:T(8,128)S(1)}, u32[]{:S(2)}, u32[]{:S(2)}) %collective-permute-start.4) | collective-permute-done | bytes 8224 | tf_op jit(solution)/shard_map/ppermute | solution.py:690
  17.5 0.7 %shard_map.84.image = f32[576,128]{1,0:T(8,128)S(1)} custom-call(bf16[2,256,256]{2,1,0:T(8,128)(2,1)S(1)} %get-tuple-element.44.rounded_ref, bf16[1,256,128]{2,1,0:T(8,128)(2,1)S(1)} %get-tuple-element.45.rounded_more, bf16[512,512]{1,0:T(8,128)(2,1)S(1)} %copy-done, bf16[32,144,256]{2,1,0:T(8,128)(2,1)S(1)} %get-tuple-element.36.particles), custom_call_target="tpu_custom_call" | custom-call | flops 268435456 | bytes 4096000 | tf_op jit(solution)/shard_map/pallas_call | solution.py:93
  18.1 0.6 %collective-permute-done.5.spectrum = bf16[42,16,128]{2,1,0:T(8,128)(2,1)S(1)} collective-permute-done((bf16[42,16,128]{2,1,0:T(8,128)(2,1)S(1)}, bf16[42,16,128]{2,1,0:T(8,128)(2,1)S(1)}, u32[]{:S(2)}, u32[]{:S(2)}) %collective-permute-start.5) | collective-permute-done | bytes 172064 | tf_op jit(solution)/shard_map/ppermute | solution.py:690
  18.7 0.6 %shard_map.85.refs_0_ = bf16[272,128]{1,0:T(8,128)(2,1)S(1)} custom-call(f32[576,128]{1,0:T(8,128)S(1)} %shard_map.84.image, bf16[42,16,128]{2,1,0:T(8,128)(2,1)S(1)} %get-tuple-element.46.mine, bf16[42,16,128]{2,1,0:T(8,128)(2,1)S(1)} %collective-permute-done.5.spectrum, bf16[32,144,256]{2,1,0:T(8,128)(2,1)S(1)} %get-tuple-element.34.refs_5_.particles), custom_call_target="tpu_custom_call" | custom-call | flops 352321536 | bytes 3657728 | tf_op jit(solution)/shard_map/pallas_call | solution.py:93
  19.3 1.3 %collective-permute-start.8 = (bf16[272,128]{1,0:T(8,128)(2,1)S(1)}, bf16[272,128]{1,0:T(8,128)(2,1)S(1)}, u32[]{:S(2)}, u32[]{:S(2)}) collective-permute-start(bf16[272,128]{1,0:T(8,128)(2,1)S(1)} %shard_map.85.refs_0_), channel_id=1, source_target_pairs={{0,8},{4,12},{8,0},{12,4},{1,9},{5,13},{9,1},{13,5},{2,10},{6,14},... | collective-permute-start | bytes 208904 | tf_op jit(solution)/shard_map/ppermute | solution.py:690
  20.5 0.9 %collective-permute-start.7 = (bf16[272,128]{1,0:T(8,128)(2,1)S(1)}, bf16[272,128]{1,0:T(8,128)(2,1)S(1)}, u32[]{:S(2)}, u32[]{:S(2)}) collective-permute-start(bf16[272,128]{1,0:T(8,128)(2,1)S(1)} %shard_map.85.refs_0_), channel_id=1, source_target_pairs={{0,12},{4,8},{8,4},{12,0},{1,13},{5,9},{9,5},{13,1},{2,14},{6,10},... | collective-permute-start | bytes 208904 | tf_op jit(solution)/shard_map/ppermute | solution.py:690
  21.5 1.3 %collective-permute-start.6 = (bf16[272,128]{1,0:T(8,128)(2,1)S(1)}, bf16[272,128]{1,0:T(8,128)(2,1)S(1)}, u32[]{:S(2)}, u32[]{:S(2)}) collective-permute-start(bf16[272,128]{1,0:T(8,128)(2,1)S(1)} %shard_map.85.refs_0_), channel_id=1, source_target_pairs={{0,4},{4,0},{8,12},{12,8},{1,5},{5,1},{9,13},{13,9},{2,6},{6,2},{1... | collective-permute-start | bytes 208904 | tf_op jit(solution)/shard_map/ppermute | solution.py:690
  22.8 3.7 %collective-permute-done.8.refs_3_ = bf16[272,128]{1,0:T(8,128)(2,1)S(1)} collective-permute-done((bf16[272,128]{1,0:T(8,128)(2,1)S(1)}, bf16[272,128]{1,0:T(8,128)(2,1)S(1)}, u32[]{:S(2)}, u32[]{:S(2)}) %collective-permute-start.8) | collective-permute-done | bytes 69664 | tf_op jit(solution)/shard_map/ppermute | solution.py:690
  26.5 0.6 %collective-permute-done.7.refs_2_ = bf16[272,128]{1,0:T(8,128)(2,1)S(1)} collective-permute-done((bf16[272,128]{1,0:T(8,128)(2,1)S(1)}, bf16[272,128]{1,0:T(8,128)(2,1)S(1)}, u32[]{:S(2)}, u32[]{:S(2)}) %collective-permute-start.7) | collective-permute-done | bytes 69664 | tf_op jit(solution)/shard_map/ppermute | solution.py:690
  27.1 1.2 %collective-permute-done.6.refs_1_ = bf16[272,128]{1,0:T(8,128)(2,1)S(1)} collective-permute-done((bf16[272,128]{1,0:T(8,128)(2,1)S(1)}, bf16[272,128]{1,0:T(8,128)(2,1)S(1)}, u32[]{:S(2)}, u32[]{:S(2)}) %collective-permute-start.6) | collective-permute-done | bytes 69664 | tf_op jit(solution)/shard_map/ppermute | solution.py:690
  28.3 0.9 %shard_map.86 = (f32[648,128]{1,0:T(8,128)S(1)}, f32[4,128]{1,0:T(4,128)S(1)}, bf16[32,16,256]{2,1,0:T(8,128)(2,1)S(1)}) custom-call(bf16[272,128]{1,0:T(8,128)(2,1)S(1)} %shard_map.85.refs_0_, bf16[272,128]{1,0:T(8,128)(2,1)S(1)} %collective-permute-done.6.refs_1_, bf16[272,128]{1,0:T(8,128)(2,1)S(1)} %collective-permute-done.7.refs_2_, ...), custom_call_target="tpu_custom_call" | custom-call | flops 150994944 | bytes 3842048 | tf_op jit(solution)/shard_map/pallas_call | solution.py:93
  29.2 0.8 %shard_map.87.own = f32[648,128]{1,0:T(8,128)S(1)} custom-call(bf16[32,16,256]{2,1,0:T(8,128)(2,1)S(1)} %get-tuple-element.47.left_ref, bf16[32,144,256]{2,1,0:T(8,128)(2,1)S(1)} %get-tuple-element.36.particles), custom_call_target="tpu_custom_call" | custom-call | flops 301989888 | bytes 3252224 | tf_op jit(solution)/shard_map/pallas_call | solution.py:93
  30.0 0.8 %collective-permute-done.9.other = f32[648,128]{1,0:T(8,128)S(1)} collective-permute-done((f32[648,128]{1,0:T(8,128)S(1)}, f32[648,128]{1,0:T(8,128)S(1)}, u32[]{:S(2)}, u32[]{:S(2)}) %collective-permute-start.9) | collective-permute-done | bytes 331808 | tf_op jit(solution)/shard_map/ppermute | solution.py:690
  30.9 0.7 %shard_map.88 = (f32[2,256,256]{2,1,0:T(8,128)S(1)}, f32[1,256,128]{2,1,0:T(8,128)S(1)}, f32[2,256]{1,0:T(2,128)S(1)}, f32[1,128]{1,0:T(1,128)S(1)}, f32[8,256]{1,0:T(8,128)S(1)}) custom-call(f32[648,128]{1,0:T(8,128)S(1)} %shard_map.87.own, f32[648,128]{1,0:T(8,128)S(1)} %collective-permute-done.9.other, f32[4,128]{1,0:T(4,128)S(1)} %get-tuple-element.49.energy_ref, ...), custom_call_target="tpu_custom_call" | custom-call | flops 402653184 | bytes 2424832 | tf_op jit(solution)/shard_map/pallas_call | solution.py:93
  31.5 1.3 %collective-permute-start.10 = (f32[8,256]{1,0:T(8,128)S(1)}, f32[8,256]{1,0:T(8,128)S(1)}, u32[]{:S(2)}, u32[]{:S(2)}) collective-permute-start(f32[8,256]{1,0:T(8,128)S(1)} %get-tuple-element.54.first), channel_id=1, source_target_pairs={{0,3},{1,2},{2,1},{3,0},{4,7},{5,6},{6,5},{7,4},{8,11},{9,10},{10,... | collective-permute-start | bytes 24584 | tf_op jit(solution)/shard_map/ppermute | solution.py:690
  32.8 1.8 %collective-permute-done.10.second = f32[8,256]{1,0:T(8,128)S(1)} collective-permute-done((f32[8,256]{1,0:T(8,128)S(1)}, f32[8,256]{1,0:T(8,128)S(1)}, u32[]{:S(2)}, u32[]{:S(2)}) %collective-permute-start.10) | collective-permute-done | bytes 8224 | tf_op jit(solution)/shard_map/ppermute | solution.py:690
  35.2 0.7 %shard_map.90.image = f32[576,128]{1,0:T(8,128)S(1)} custom-call(bf16[2,256,256]{2,1,0:T(8,128)(2,1)S(1)} %get-tuple-element.55.rounded_ref, bf16[1,256,128]{2,1,0:T(8,128)(2,1)S(1)} %get-tuple-element.56.rounded_more, bf16[512,512]{1,0:T(8,128)(2,1)S(1)} %copy-done, bf16[32,144,256]{2,1,0:T(8,128)(2,1)S(1)} %get-tuple-element.36.particles), custom_call_target="tpu_custom_call" | custom-call | flops 268435456 | bytes 4096000 | tf_op jit(solution)/shard_map/pallas_call | solution.py:93
  35.9 0.6 %collective-permute-done.11.spectrum = bf16[42,16,128]{2,1,0:T(8,128)(2,1)S(1)} collective-permute-done((bf16[42,16,128]{2,1,0:T(8,128)(2,1)S(1)}, bf16[42,16,128]{2,1,0:T(8,128)(2,1)S(1)}, u32[]{:S(2)}, u32[]{:S(2)}) %collective-permute-start.11) | collective-permute-done | bytes 172064 | tf_op jit(solution)/shard_map/ppermute | solution.py:690
  36.5 0.6 %shard_map.91 = (f32[72,128]{1,0:T(8,128)S(1)}, f32[72,128]{1,0:T(8,128)S(1)}, f32[72,128]{1,0:T(8,128)S(1)}, f32[72,128]{1,0:T(8,128)S(1)}, f32[1,144]{1,0:T(1,128)S(1)}) custom-call(f32[576,128]{1,0:T(8,128)S(1)} %shard_map.90.image, bf16[42,16,128]{2,1,0:T(8,128)(2,1)S(1)} %get-tuple-element.57.mine, ...), custom_call_target="tpu_custom_call" | custom-call | flops 352321536 | bytes 3768320 | tf_op jit(solution)/shard_map/pallas_call | solution.py:93
  37.0 2.3 %collective-permute-start.12 = (f32[72,128]{1,0:T(8,128)S(1)}, f32[72,128]{1,0:T(8,128)S(1)}, u32[]{:S(2)}, u32[]{:S(2)}) collective-permute-start(f32[72,128]{1,0:T(8,128)S(1)} %get-tuple-element.58), channel_id=1, source_target_pairs={{0,12},{4,8},{8,4},{12,0},{1,13},{5,9},{9,5},{13,1},{2,14},{6,10},... | collective-permute-start | bytes 110600 | tf_op jit(solution)/shard_map/ppermute | solution.py:690
  39.4 2.1 %collective-permute-start.14 = (f32[72,128]{1,0:T(8,128)S(1)}, f32[72,128]{1,0:T(8,128)S(1)}, u32[]{:S(2)}, u32[]{:S(2)}) collective-permute-start(f32[72,128]{1,0:T(8,128)S(1)} %get-tuple-element.60), channel_id=1, source_target_pairs={{0,4},{4,0},{8,12},{12,8},{1,5},{5,1},{9,13},{13,9},{2,6},{6,2},{1... | collective-permute-start | bytes 110600 | tf_op jit(solution)/shard_map/ppermute | solution.py:690
  41.5 1.6 %collective-permute-done.12.refs_0_ = f32[72,128]{1,0:T(8,128)S(1)} collective-permute-done((f32[72,128]{1,0:T(8,128)S(1)}, f32[72,128]{1,0:T(8,128)S(1)}, u32[]{:S(2)}, u32[]{:S(2)}) %collective-permute-start.12) | collective-permute-done | bytes 36896 | tf_op jit(solution)/shard_map/ppermute | solution.py:690
  43.1 1.1 %collective-permute-done.13.refs_1_ = f32[72,128]{1,0:T(8,128)S(1)} collective-permute-done((f32[72,128]{1,0:T(8,128)S(1)}, f32[72,128]{1,0:T(8,128)S(1)}, u32[]{:S(2)}, u32[]{:S(2)}) %collective-permute-start.13) | collective-permute-done | bytes 36896 | tf_op jit(solution)/shard_map/ppermute | solution.py:690
  44.2 0.6 %shard_map.92 = (f32[1,64,128]{2,1,0:T(8,128)}, f32[1,144]{1,0:T(1,128)}) custom-call(f32[72,128]{1,0:T(8,128)S(1)} %collective-permute-done.12.refs_0_, f32[72,128]{1,0:T(8,128)S(1)} %collective-permute-done.13.refs_1_, f32[72,128]{1,0:T(8,128)S(1)} %collective-permute-done.14.refs_2_, f32[72,128]{1,0:T(8,128)S(1)} %get-tuple-element.61.refs_3_, ...), custom_call_target="tpu_custom_call" | custom-call | bytes 245760 | tf_op jit(solution)/shard_map/pallas_call | solution.py:93
  (26 shorter events, 2.3 us)
Async XLA Ops:
  0.6 5.7 %copy-start.5 = (bf16[288,64,128]{2,1,0:T(8,128)(2,1)S(1)}, bf16[288,64,128]{2,1,0:T(8,128)(2,1)}, u32[]{:S(2)}) copy-start(bf16[288,64,128]{2,1,0:T(8,128)(2,1)} %particles_ref.1) | copy-start | bytes 14155780
  0.6 7.2 %collective-permute-start.1 = (bf16[1,64,128]{2,1,0:T(8,128)(2,1)}, bf16[1,64,128]{2,1,0:T(8,128)(2,1)S(1)}, u32[]{:S(2)}, u32[]{:S(2)}) collective-permute-start(bf16[1,64,128]{2,1,0:T(8,128)(2,1)} %refs_0_.1), channel_id=1, source_target_pairs={{0,8},{4,12},{8,0},{12,4},{1,9},{5,13},{9,1},{13,5},{2,10},{6,14},... | collective-permute-start | bytes 49160 | tf_op jit(solution)/shard_map/ppermute | solution.py:690
  4.7 5.7 %collective-permute-start = (bf16[1,64,128]{2,1,0:T(8,128)(2,1)}, bf16[1,64,128]{2,1,0:T(8,128)(2,1)S(1)}, u32[]{:S(2)}, u32[]{:S(2)}) collective-permute-start(bf16[1,64,128]{2,1,0:T(8,128)(2,1)} %refs_0_.1), channel_id=1, source_target_pairs={{0,12},{4,8},{8,4},{12,0},{1,13},{5,9},{9,5},{13,1},{2,14},{6,10},... | collective-permute-start | bytes 49160 | tf_op jit(solution)/shard_map/ppermute | solution.py:690
  6.1 4.4 %collective-permute-start.2 = (bf16[1,64,128]{2,1,0:T(8,128)(2,1)}, bf16[1,64,128]{2,1,0:T(8,128)(2,1)S(1)}, u32[]{:S(2)}, u32[]{:S(2)}) collective-permute-start(bf16[1,64,128]{2,1,0:T(8,128)(2,1)} %refs_0_.1), channel_id=1, source_target_pairs={{0,4},{4,0},{8,12},{12,8},{1,5},{5,1},{9,13},{13,9},{2,6},{6,2},{1... | collective-permute-start | bytes 49160 | tf_op jit(solution)/shard_map/ppermute | solution.py:690
  6.4 4.1 %copy-start.2 = (bf16[1,64,128]{2,1,0:T(8,128)(2,1)S(1)}, bf16[1,64,128]{2,1,0:T(8,128)(2,1)}, u32[]{:S(2)}) copy-start(bf16[1,64,128]{2,1,0:T(8,128)(2,1)} %refs_0_.1) | copy-start | bytes 49156
  6.4 4.1 %copy-start.4 = (f32[64]{0:T(128)S(1)}, f32[64]{0:T(128)}, u32[]{:S(2)}) copy-start(f32[64]{0:T(128)} %param.8) | copy-start | bytes 772
  7.8 3.7 %copy-start.3 = (s32[288]{0:T(512)S(1)}, s32[288]{0:T(512)}, u32[]{:S(2)}) copy-start(s32[288]{0:T(512)} %prior_ref.1) | copy-start | bytes 3460
  10.5 2.6 %copy-start.1 = (bf16[512,768]{1,0:T(8,128)(2,1)S(1)}, bf16[512,768]{1,0:T(8,128)(2,1)}, u32[]{:S(2)}) copy-start(bf16[512,768]{1,0:T(8,128)(2,1)} %constant.4.clone.inverse) | copy-start | bytes 2359300
  11.4 1.6 %collective-permute-start.3 = (f32[648,128]{1,0:T(8,128)S(1)}, f32[648,128]{1,0:T(8,128)S(1)}, u32[]{:S(2)}, u32[]{:S(2)}) collective-permute-start(f32[648,128]{1,0:T(8,128)S(1)} %get-tuple-element.37), channel_id=1, source_target_pairs={{0,1},{1,0},{2,3},{3,2},{4,5},{5,4},{6,7},{7,6},{8,9},{9,8},{10,11... | collective-permute-start | bytes 995336 | tf_op jit(solution)/shard_map/ppermute | solution.py:690
  11.9 4.9 %copy-start = (bf16[512,512]{1,0:T(8,128)(2,1)S(1)}, bf16[512,512]{1,0:T(8,128)(2,1)}, u32[]{:S(2)}) copy-start(bf16[512,512]{1,0:T(8,128)(2,1)} %constant.5.clone.forward) | copy-start | bytes 1572868
  13.7 3.1 %collective-permute-start.4 = (f32[8,256]{1,0:T(8,128)S(1)}, f32[8,256]{1,0:T(8,128)S(1)}, u32[]{:S(2)}, u32[]{:S(2)}) collective-permute-start(f32[8,256]{1,0:T(8,128)S(1)} %get-tuple-element.43.first), channel_id=1, source_target_pairs={{0,3},{1,2},{2,1},{3,0},{4,7},{5,6},{6,5},{7,4},{8,11},{9,10},{10,... | collective-permute-start | bytes 24584 | tf_op jit(solution)/shard_map/ppermute | solution.py:690
  17.2 1.5 %collective-permute-start.5 = (bf16[42,16,128]{2,1,0:T(8,128)(2,1)S(1)}, bf16[42,16,128]{2,1,0:T(8,128)(2,1)S(1)}, u32[]{:S(2)}, u32[]{:S(2)}) collective-permute-start(bf16[42,16,128]{2,1,0:T(8,128)(2,1)S(1)} %get-tuple-element.46.mine), channel_id=1, source_target_pairs={{0,1},{1,0},{2,3},{3,2},{4,5},{5,4},{6,7},{7,6},{8,9},{9,8},{10,11... | collective-permute-start | bytes 516104 | tf_op jit(solution)/shard_map/ppermute | solution.py:690
  19.3 7.2 %collective-permute-start.8 = (bf16[272,128]{1,0:T(8,128)(2,1)S(1)}, bf16[272,128]{1,0:T(8,128)(2,1)S(1)}, u32[]{:S(2)}, u32[]{:S(2)}) collective-permute-start(bf16[272,128]{1,0:T(8,128)(2,1)S(1)} %shard_map.85.refs_0_), channel_id=1, source_target_pairs={{0,8},{4,12},{8,0},{12,4},{1,9},{5,13},{9,1},{13,5},{2,10},{6,14},... | collective-permute-start | bytes 208904 | tf_op jit(solution)/shard_map/ppermute | solution.py:690
  20.5 6.6 %collective-permute-start.7 = (bf16[272,128]{1,0:T(8,128)(2,1)S(1)}, bf16[272,128]{1,0:T(8,128)(2,1)S(1)}, u32[]{:S(2)}, u32[]{:S(2)}) collective-permute-start(bf16[272,128]{1,0:T(8,128)(2,1)S(1)} %shard_map.85.refs_0_), channel_id=1, source_target_pairs={{0,12},{4,8},{8,4},{12,0},{1,13},{5,9},{9,5},{13,1},{2,14},{6,10},... | collective-permute-start | bytes 208904 | tf_op jit(solution)/shard_map/ppermute | solution.py:690
  21.5 6.8 %collective-permute-start.6 = (bf16[272,128]{1,0:T(8,128)(2,1)S(1)}, bf16[272,128]{1,0:T(8,128)(2,1)S(1)}, u32[]{:S(2)}, u32[]{:S(2)}) collective-permute-start(bf16[272,128]{1,0:T(8,128)(2,1)S(1)} %shard_map.85.refs_0_), channel_id=1, source_target_pairs={{0,4},{4,0},{8,12},{12,8},{1,5},{5,1},{9,13},{13,9},{2,6},{6,2},{1... | collective-permute-start | bytes 208904 | tf_op jit(solution)/shard_map/ppermute | solution.py:690
  29.2 1.6 %collective-permute-start.9 = (f32[648,128]{1,0:T(8,128)S(1)}, f32[648,128]{1,0:T(8,128)S(1)}, u32[]{:S(2)}, u32[]{:S(2)}) collective-permute-start(f32[648,128]{1,0:T(8,128)S(1)} %get-tuple-element.48), channel_id=1, source_target_pairs={{0,1},{1,0},{2,3},{3,2},{4,5},{5,4},{6,7},{7,6},{8,9},{9,8},{10,11... | collective-permute-start | bytes 995336 | tf_op jit(solution)/shard_map/ppermute | solution.py:690
  31.5 3.1 %collective-permute-start.10 = (f32[8,256]{1,0:T(8,128)S(1)}, f32[8,256]{1,0:T(8,128)S(1)}, u32[]{:S(2)}, u32[]{:S(2)}) collective-permute-start(f32[8,256]{1,0:T(8,128)S(1)} %get-tuple-element.54.first), channel_id=1, source_target_pairs={{0,3},{1,2},{2,1},{3,0},{4,7},{5,6},{6,5},{7,4},{8,11},{9,10},{10,... | collective-permute-start | bytes 24584 | tf_op jit(solution)/shard_map/ppermute | solution.py:690
  35.0 1.5 %collective-permute-start.11 = (bf16[42,16,128]{2,1,0:T(8,128)(2,1)S(1)}, bf16[42,16,128]{2,1,0:T(8,128)(2,1)S(1)}, u32[]{:S(2)}, u32[]{:S(2)}) collective-permute-start(bf16[42,16,128]{2,1,0:T(8,128)(2,1)S(1)} %get-tuple-element.57.mine), channel_id=1, source_target_pairs={{0,1},{1,0},{2,3},{3,2},{4,5},{5,4},{6,7},{7,6},{8,9},{9,8},{10,11... | collective-permute-start | bytes 516104 | tf_op jit(solution)/shard_map/ppermute | solution.py:690
  37.0 6.1 %collective-permute-start.12 = (f32[72,128]{1,0:T(8,128)S(1)}, f32[72,128]{1,0:T(8,128)S(1)}, u32[]{:S(2)}, u32[]{:S(2)}) collective-permute-start(f32[72,128]{1,0:T(8,128)S(1)} %get-tuple-element.58), channel_id=1, source_target_pairs={{0,12},{4,8},{8,4},{12,0},{1,13},{5,9},{9,5},{13,1},{2,14},{6,10},... | collective-permute-start | bytes 110600 | tf_op jit(solution)/shard_map/ppermute | solution.py:690
  39.4 4.9 %collective-permute-start.13 = (f32[72,128]{1,0:T(8,128)S(1)}, f32[72,128]{1,0:T(8,128)S(1)}, u32[]{:S(2)}, u32[]{:S(2)}) collective-permute-start(f32[72,128]{1,0:T(8,128)S(1)} %get-tuple-element.59), channel_id=1, source_target_pairs={{0,8},{4,12},{8,0},{12,4},{1,9},{5,13},{9,1},{13,5},{2,10},{6,14},... | collective-permute-start | bytes 110600 | tf_op jit(solution)/shard_map/ppermute | solution.py:690
  39.4 4.9 %collective-permute-start.14 = (f32[72,128]{1,0:T(8,128)S(1)}, f32[72,128]{1,0:T(8,128)S(1)}, u32[]{:S(2)}, u32[]{:S(2)}) collective-permute-start(f32[72,128]{1,0:T(8,128)S(1)} %get-tuple-element.60), channel_id=1, source_target_pairs={{0,4},{4,0},{8,12},{12,8},{1,5},{5,1},{9,13},{13,9},{2,6},{6,2},{1... | collective-permute-start | bytes 110600 | tf_op jit(solution)/shard_map/ppermute | solution.py:690

commit v20 on v19

--- a/solution.py
+++ b/solution.py
@@ -51,22 +51,6 @@
     return result
 
 
-def loop(count, body, unroll):
-    while count % unroll:
-        unroll -= 1
-    if unroll == count:
-        for i in range(count):
-            body(i)
-        return
-
-    def step(outer, carry):
-        for inner in range(unroll):
-            body(outer * unroll + inner)
-        return carry
-
-    lax.fori_loop(0, count // unroll, step, 0)
-
-
 def each(count, body, init):
     if count <= 8:
         for k in range(count):
@@ -187,7 +171,7 @@
 
 def weigh_kernel(fresh, order, count, *refs):
     sources = [refs[order.index(i)] for i in range(count)]
-    doubled_ref, particles, out, energy_ref, left_ref, image, rest = refs[count:]
+    doubled_ref, particles, out, energy_ref, left_ref, image = refs[count:]
     pairs, share, twice = particles.shape
     freqs, depth = 2 * pairs, twice // 2
     classes = energy_ref.shape[0]
@@ -199,16 +183,22 @@
     row = lax.broadcasted_iota(jnp.int32, (freqs, depth), 0) + lax.axis_index("rot") * freqs
     scale = jnp.where(row == 0, 1.0 / ANG, 2.0 / ANG).astype(F32) * doubled
 
+    tails = []
+    if not fresh:
+        end = sources[0].shape[0] - classes * freqs
+        tails = [source[pl.ds(classes * freqs, end), :].astype(F32) for source in sources]
+
     for k in range(classes):
         if fresh:
             plain = sources[k][0].astype(F32)
         else:
-            sums, highs, lows = [
-                tree(
-                    source[pl.ds(base + (k ^ i) * step, step), :].astype(F32)
-                    for i, source in enumerate(sources)
-                )
-                for base, step in ((0, freqs), (classes * freqs, 1), (classes * (freqs + 1), 1))
+            sums = tree(
+                source[pl.ds((k ^ i) * freqs, freqs), :].astype(F32)
+                for i, source in enumerate(sources)
+            )
+            highs, lows = [
+                tree(tail[base + (k ^ i) : base + (k ^ i) + 1] for i, tail in enumerate(tails))
+                for base in (0, classes)
             ]
             plain = (sums / (highs + lows + shrinkage)).astype(BF16).astype(F32)
         weighted = (plain * doubled).astype(BF16).astype(F32)
@@ -231,10 +221,9 @@
             left_ref[f + len(lefts)] = left
             lefts.append(left)
         values = [times(left, particles[f + i]) for i, left in enumerate(lefts)]
-        place(out, rest, f, values, classes, pitch)
+        place(out, f, values, classes, pitch)
 
     every(pairs, correlate)
-    pack(out, rest, classes, share, pitch)
 
 
 def times(left, particles):
@@ -262,26 +251,23 @@
     return [(blocks[2 * i], blocks[2 * i + 1]) for i in range(GROUP)]
 
 
-def place(out, rest, f, values, classes, pitch):
+def place(out, f, values, classes, pitch):
     width = values[0].shape[1] - 128
+    each_pack = 128 // width
     spare = jnp.zeros((2 * classes, 128 - width), F32)
     parts = [
         value[part * 2 * classes : (part + 1) * 2 * classes] for value in values for part in range(2)
     ]
     put(out, f, [part[:, :128] for part in parts], pitch)
-    put(rest, f, [jnp.concatenate([part[:, 128:], spare], 1) for part in parts], pitch)
-
-
-def pack(out, rest, classes, share, pitch):
-    width = share - 128
-    each_pack = 128 // width
+    more = [jnp.concatenate([part[:, 128:], spare], 1) for part in parts]
+    more = jnp.swapaxes(jnp.stack(more, 0), 0, 1)
     for first in range(0, 2 * classes, each_pack):
         total = 0.0
         for group in range(first, min(first + each_pack, 2 * classes)):
             part, k = divmod(group, classes)
-            value = rest[rows((2 * k + part) * pitch, pitch), :]
-            total = total + turned(value, (group - first) * width)
-        out[rows((2 * classes + first // each_pack) * pitch, pitch), :] = total
+            total = total + turned(more[2 * k + part], (group - first) * width)
+        at = (2 * classes + first // each_pack) * pitch + 2 * f
+        out[pl.ds(at, 2 * GROUP), :] = total
 
 
 def unpack(ref, unit, part, classes, share, pitch, freqs):
@@ -308,22 +294,21 @@
             ((classes, 128), F32),
             ((pairs, 4 * classes, twice), BF16),
         ],
-        [((2 * classes * pitch, twice // 2), F32), ((2 * classes * pitch, 128), F32)],
+        [((2 * classes * pitch, twice // 2), F32)],
         flops=8 * classes * share * pairs * twice * 4,
     )
 
 
-def correlate_kernel(left_ref, particles, out, rest):
+def correlate_kernel(left_ref, particles, out):
     pairs, share, _ = particles.shape
     classes = left_ref.shape[1] // 4
     pitch = 2 * pairs + SPARE
 
     def body(f):
         values = [times(left_ref[f + i], particles[f + i]) for i in range(GROUP)]
-        place(out, rest, f, values, classes, pitch)
+        place(out, f, values, classes, pitch)
 
     every(pairs, body)
-    pack(out, rest, classes, share, pitch)
 
 
 def correlate(left, particles):
@@ -334,7 +319,6 @@
         correlate_kernel,
         [left, particles],
         [((corr_lines(classes, share, pitch), 128), F32)],
-        [((2 * classes * pitch, 128), F32)],
         flops=2 * left.shape[1] * share * pairs * twice * 8,
     )[0]
 
@@ -605,7 +589,7 @@
 
 
 def finish_kernel(image, mine, spectrum, particles, *refs):
-    *outs, held, held_more = refs
+    *outs, held = refs
     evidence_ref = outs.pop() if len(outs) > 1 else None
     pairs, share, twice = particles.shape
     classes = spectrum.shape[1] // 4
@@ -613,16 +597,24 @@
     radii = depth // 2
     pitch = freqs + SPARE
 
-    units = layout(classes, share)[2]
-    entries = ANG // 2 // (4 * classes)
-    for unit in range(units):
-        first = pairs + unit * entries
-        value = jnp.concatenate([spectrum[first + i] for i in range(entries)], 0)
-        spread_more(held_more, unit, value.astype(F32), classes, share)
+    width, bundle, units = layout(classes, share)
+    step = 4 * classes
+    entries = ANG // 2 // step
+
+    def received(f):
+        blocks = []
+        for k in range(classes):
+            unit, j = divmod(k, bundle)
+            for part in range(2):
+                entry, first = divmod(part * freqs + 2 * f, step)
+                value = spectrum[pairs + unit * entries + entry].astype(F32)
+                blocks.append(turned(value[first : first + 2 * GROUP], -j * width))
+        blocks = jnp.swapaxes(jnp.stack(blocks, 0), 0, 1)
+        return [(blocks[2 * i], blocks[2 * i + 1]) for i in range(GROUP)]
 
     def body(f):
         values = []
-        for i, parts in enumerate(pick(held_more, f, classes)):
+        for i, parts in enumerate(received(f)):
             left = jnp.concatenate(parts, 0).astype(BF16)
             left = jnp.concatenate([spectrum[f + i], left], 1)[:, :share]
             values.append(dot(left, particles[f + i]))
@@ -639,12 +631,12 @@
     lane = lax.broadcasted_iota(jnp.int32, (freqs, depth), 1)
     sign = jnp.where(lane < radii, -1.0, 1.0).astype(F32)
     for k in range(classes):
-        plain, turned = [
+        plain, crossed = [
             image[rows((2 * k + part) * pitch, freqs), :]
             + held[rows((2 * k + part) * pitch, freqs), :]
             for part in range(2)
         ]
-        value = plain + sign * pltpu.roll(turned, radii, 1)
+        value = plain + sign * pltpu.roll(crossed, radii, 1)
         if len(outs) == 1:
             outs[0][pl.ds(k * freqs, freqs), :] = value.astype(BF16)
         else:
@@ -670,7 +662,7 @@
         finish_kernel,
         [image, mine, spectrum, particles],
         outs,
-        [(image.shape, F32)] * 2,
+        [(image.shape, F32)],
         flops=2 * math.prod(spectrum.shape) * twice * 8,
     )
 

time: 45 us -> 45 us (level)
  no operation moved by 1% of the time
where the time goes in v20:
time: 45 us; the launch traced here: 44.9 us
  waiting for transfers between devices  16.9 us (38%)
  starting transfers between devices  16.7 us (37%)
  Pallas kernels  10.5 us (23%)
  between operations  0.79 us (2%)
    ppermute x15, waiting for transfers between devices, swap(): return lax.ppermute(value, axis, [(i, i ^ bit) for i in range(size)])  16.9 us
    ppermute x15, starting transfers between devices, swap(): return lax.ppermute(value, axis, [(i, i ^ bit) for i in range(size)])  16.7 us
    pallas_call x16, Pallas kernels, call(): pl.pallas_call(kernel, out_shape=[jax.ShapeDtypeStruct(*x) for x in outs]...  10.5 us
  transfers between devices with their start and end apart: 15, of which 12 were waited for; matrix products, arithmetic and copies ran while one was open for 0% of the time, Pallas kernels for 11%

profile of v20, /device:TPU:0, one launch (start us, length us, event | category | flops | bytes accessed | tf_op | source)
XLA Modules:
  0.0 44.9 jit_solution(7004251178218313252)
XLA Ops:
  0.6 4.1 %collective-permute-start.1 = (bf16[1,64,128]{2,1,0:T(8,128)(2,1)}, bf16[1,64,128]{2,1,0:T(8,128)(2,1)S(1)}, u32[]{:S(2)}, u32[]{:S(2)}) collective-permute-start(bf16[1,64,128]{2,1,0:T(8,128)(2,1)} %refs_0_.1), channel_id=1, source_target_pairs={{0,8},{4,12},{8,0},{12,4},{1,9},{5,13},{9,1},{13,5},{2,10},{6,14},... | collective-permute-start | bytes 49160 | tf_op jit(solution)/shard_map/ppermute | solution.py:682
  4.7 1.3 %collective-permute-start = (bf16[1,64,128]{2,1,0:T(8,128)(2,1)}, bf16[1,64,128]{2,1,0:T(8,128)(2,1)S(1)}, u32[]{:S(2)}, u32[]{:S(2)}) collective-permute-start(bf16[1,64,128]{2,1,0:T(8,128)(2,1)} %refs_0_.1), channel_id=1, source_target_pairs={{0,12},{4,8},{8,4},{12,0},{1,13},{5,9},{9,5},{13,1},{2,14},{6,10},... | collective-permute-start | bytes 49160 | tf_op jit(solution)/shard_map/ppermute | solution.py:682
  6.4 1.4 %shard_map.78 = (bf16[32,144,256]{2,1,0:T(8,128)(2,1)S(1)}, bf16[32,144,256]{2,1,0:T(8,128)(2,1)S(1)}) custom-call(bf16[288,64,128]{2,1,0:T(8,128)(2,1)S(1)} %copy-done.5, bf16[256,256]{1,0:T(8,128)(2,1)S(1)} %shard_map.77.permutation_ref), custom_call_target="tpu_custom_call" | custom-call | flops 2147483648 | bytes 9568256 | tf_op jit(solution)/shard_map/pallas_call | solution.py:77
  7.8 2.6 %collective-permute-done.refs_1_ = bf16[1,64,128]{2,1,0:T(8,128)(2,1)S(1)} collective-permute-done((bf16[1,64,128]{2,1,0:T(8,128)(2,1)}, bf16[1,64,128]{2,1,0:T(8,128)(2,1)S(1)}, u32[]{:S(2)}, u32[]{:S(2)}) %collective-permute-start) | collective-permute-done | bytes 16416 | tf_op jit(solution)/shard_map/ppermute | solution.py:682
  10.5 0.9 %shard_map.79 = (f32[648,128]{1,0:T(8,128)S(1)}, f32[4,128]{1,0:T(4,128)S(1)}, bf16[32,16,256]{2,1,0:T(8,128)(2,1)S(1)}) custom-call(bf16[1,64,128]{2,1,0:T(8,128)(2,1)S(1)} %copy-done.2, bf16[1,64,128]{2,1,0:T(8,128)(2,1)S(1)} %collective-permute-done.refs_1_, bf16[1,64,128]{2,1,0:T(8,128)(2,1)S(1)} %collective-permute-done.1.refs_2_, ...), custom_call_target="tpu_custom_call" | custom-call | flops 150994944 | bytes 3334144 | tf_op jit(solution)/shard_map/pallas_call | solution.py:77
  11.9 0.8 %shard_map.80.own = f32[648,128]{1,0:T(8,128)S(1)} custom-call(bf16[32,16,256]{2,1,0:T(8,128)(2,1)S(1)} %get-tuple-element.35.left_ref, bf16[32,144,256]{2,1,0:T(8,128)(2,1)S(1)} %get-tuple-element.36.particles), custom_call_target="tpu_custom_call" | custom-call | flops 301989888 | bytes 2957312 | tf_op jit(solution)/shard_map/pallas_call | solution.py:77
  13.1 0.6 %shard_map.82 = (f32[2,256,256]{2,1,0:T(8,128)S(1)}, f32[1,256,128]{2,1,0:T(8,128)S(1)}, f32[2,256]{1,0:T(2,128)S(1)}, f32[1,128]{1,0:T(1,128)S(1)}, f32[8,256]{1,0:T(8,128)S(1)}) custom-call(f32[648,128]{1,0:T(8,128)S(1)} %shard_map.80.own, f32[648,128]{1,0:T(8,128)S(1)} %collective-permute-done.3.other, f32[4,128]{1,0:T(4,128)S(1)} %get-tuple-element.38.energy_ref, ...), custom_call_target="tpu_custom_call" | custom-call | flops 402653184 | bytes 2424832 | tf_op jit(solution)/shard_map/pallas_call | solution.py:77
  13.7 1.3 %collective-permute-start.4 = (f32[8,256]{1,0:T(8,128)S(1)}, f32[8,256]{1,0:T(8,128)S(1)}, u32[]{:S(2)}, u32[]{:S(2)}) collective-permute-start(f32[8,256]{1,0:T(8,128)S(1)} %get-tuple-element.43.first), channel_id=1, source_target_pairs={{0,3},{1,2},{2,1},{3,0},{4,7},{5,6},{6,5},{7,4},{8,11},{9,10},{10,... | collective-permute-start | bytes 24584 | tf_op jit(solution)/shard_map/ppermute | solution.py:682
  15.0 1.8 %collective-permute-done.4.second = f32[8,256]{1,0:T(8,128)S(1)} collective-permute-done((f32[8,256]{1,0:T(8,128)S(1)}, f32[8,256]{1,0:T(8,128)S(1)}, u32[]{:S(2)}, u32[]{:S(2)}) %collective-permute-start.4) | collective-permute-done | bytes 8224 | tf_op jit(solution)/shard_map/ppermute | solution.py:682
  17.5 0.7 %shard_map.84.image = f32[576,128]{1,0:T(8,128)S(1)} custom-call(bf16[2,256,256]{2,1,0:T(8,128)(2,1)S(1)} %get-tuple-element.44.rounded_ref, bf16[1,256,128]{2,1,0:T(8,128)(2,1)S(1)} %get-tuple-element.45.rounded_more, bf16[512,512]{1,0:T(8,128)(2,1)S(1)} %copy-done, bf16[32,144,256]{2,1,0:T(8,128)(2,1)S(1)} %get-tuple-element.36.particles), custom_call_target="tpu_custom_call" | custom-call | flops 268435456 | bytes 4096000 | tf_op jit(solution)/shard_map/pallas_call | solution.py:77
  18.1 0.6 %collective-permute-done.5.spectrum = bf16[42,16,128]{2,1,0:T(8,128)(2,1)S(1)} collective-permute-done((bf16[42,16,128]{2,1,0:T(8,128)(2,1)S(1)}, bf16[42,16,128]{2,1,0:T(8,128)(2,1)S(1)}, u32[]{:S(2)}, u32[]{:S(2)}) %collective-permute-start.5) | collective-permute-done | bytes 172064 | tf_op jit(solution)/shard_map/ppermute | solution.py:682
  18.7 0.6 %shard_map.85.refs_0_ = bf16[272,128]{1,0:T(8,128)(2,1)S(1)} custom-call(f32[576,128]{1,0:T(8,128)S(1)} %shard_map.84.image, bf16[42,16,128]{2,1,0:T(8,128)(2,1)S(1)} %get-tuple-element.46.mine, bf16[42,16,128]{2,1,0:T(8,128)(2,1)S(1)} %collective-permute-done.5.spectrum, bf16[32,144,256]{2,1,0:T(8,128)(2,1)S(1)} %get-tuple-element.34.refs_5_.particles), custom_call_target="tpu_custom_call" | custom-call | flops 352321536 | bytes 3362816 | tf_op jit(solution)/shard_map/pallas_call | solution.py:77
  19.3 1.3 %collective-permute-start.8 = (bf16[272,128]{1,0:T(8,128)(2,1)S(1)}, bf16[272,128]{1,0:T(8,128)(2,1)S(1)}, u32[]{:S(2)}, u32[]{:S(2)}) collective-permute-start(bf16[272,128]{1,0:T(8,128)(2,1)S(1)} %shard_map.85.refs_0_), channel_id=1, source_target_pairs={{0,8},{4,12},{8,0},{12,4},{1,9},{5,13},{9,1},{13,5},{2,10},{6,14},... | collective-permute-start | bytes 208904 | tf_op jit(solution)/shard_map/ppermute | solution.py:682
  20.5 0.9 %collective-permute-start.7 = (bf16[272,128]{1,0:T(8,128)(2,1)S(1)}, bf16[272,128]{1,0:T(8,128)(2,1)S(1)}, u32[]{:S(2)}, u32[]{:S(2)}) collective-permute-start(bf16[272,128]{1,0:T(8,128)(2,1)S(1)} %shard_map.85.refs_0_), channel_id=1, source_target_pairs={{0,12},{4,8},{8,4},{12,0},{1,13},{5,9},{9,5},{13,1},{2,14},{6,10},... | collective-permute-start | bytes 208904 | tf_op jit(solution)/shard_map/ppermute | solution.py:682
  21.5 1.4 %collective-permute-start.6 = (bf16[272,128]{1,0:T(8,128)(2,1)S(1)}, bf16[272,128]{1,0:T(8,128)(2,1)S(1)}, u32[]{:S(2)}, u32[]{:S(2)}) collective-permute-start(bf16[272,128]{1,0:T(8,128)(2,1)S(1)} %shard_map.85.refs_0_), channel_id=1, source_target_pairs={{0,4},{4,0},{8,12},{12,8},{1,5},{5,1},{9,13},{13,9},{2,6},{6,2},{1... | collective-permute-start | bytes 208904 | tf_op jit(solution)/shard_map/ppermute | solution.py:682
  22.8 3.7 %collective-permute-done.8.refs_3_ = bf16[272,128]{1,0:T(8,128)(2,1)S(1)} collective-permute-done((bf16[272,128]{1,0:T(8,128)(2,1)S(1)}, bf16[272,128]{1,0:T(8,128)(2,1)S(1)}, u32[]{:S(2)}, u32[]{:S(2)}) %collective-permute-start.8) | collective-permute-done | bytes 69664 | tf_op jit(solution)/shard_map/ppermute | solution.py:682
  26.5 0.6 %collective-permute-done.7.refs_2_ = bf16[272,128]{1,0:T(8,128)(2,1)S(1)} collective-permute-done((bf16[272,128]{1,0:T(8,128)(2,1)S(1)}, bf16[272,128]{1,0:T(8,128)(2,1)S(1)}, u32[]{:S(2)}, u32[]{:S(2)}) %collective-permute-start.7) | collective-permute-done | bytes 69664 | tf_op jit(solution)/shard_map/ppermute | solution.py:682
  27.1 1.2 %collective-permute-done.6.refs_1_ = bf16[272,128]{1,0:T(8,128)(2,1)S(1)} collective-permute-done((bf16[272,128]{1,0:T(8,128)(2,1)S(1)}, bf16[272,128]{1,0:T(8,128)(2,1)S(1)}, u32[]{:S(2)}, u32[]{:S(2)}) %collective-permute-start.6) | collective-permute-done | bytes 69664 | tf_op jit(solution)/shard_map/ppermute | solution.py:682
  28.3 0.9 %shard_map.86 = (f32[648,128]{1,0:T(8,128)S(1)}, f32[4,128]{1,0:T(4,128)S(1)}, bf16[32,16,256]{2,1,0:T(8,128)(2,1)S(1)}) custom-call(bf16[272,128]{1,0:T(8,128)(2,1)S(1)} %shard_map.85.refs_0_, bf16[272,128]{1,0:T(8,128)(2,1)S(1)} %collective-permute-done.6.refs_1_, bf16[272,128]{1,0:T(8,128)(2,1)S(1)} %collective-permute-done.7.refs_2_, ...), custom_call_target="tpu_custom_call" | custom-call | flops 150994944 | bytes 3547136 | tf_op jit(solution)/shard_map/pallas_call | solution.py:77
  29.2 0.8 %shard_map.87.own = f32[648,128]{1,0:T(8,128)S(1)} custom-call(bf16[32,16,256]{2,1,0:T(8,128)(2,1)S(1)} %get-tuple-element.47.left_ref, bf16[32,144,256]{2,1,0:T(8,128)(2,1)S(1)} %get-tuple-element.36.particles), custom_call_target="tpu_custom_call" | custom-call | flops 301989888 | bytes 2957312 | tf_op jit(solution)/shard_map/pallas_call | solution.py:77
  30.1 0.8 %collective-permute-done.9.other = f32[648,128]{1,0:T(8,128)S(1)} collective-permute-done((f32[648,128]{1,0:T(8,128)S(1)}, f32[648,128]{1,0:T(8,128)S(1)}, u32[]{:S(2)}, u32[]{:S(2)}) %collective-permute-start.9) | collective-permute-done | bytes 331808 | tf_op jit(solution)/shard_map/ppermute | solution.py:682
  30.9 0.7 %shard_map.88 = (f32[2,256,256]{2,1,0:T(8,128)S(1)}, f32[1,256,128]{2,1,0:T(8,128)S(1)}, f32[2,256]{1,0:T(2,128)S(1)}, f32[1,128]{1,0:T(1,128)S(1)}, f32[8,256]{1,0:T(8,128)S(1)}) custom-call(f32[648,128]{1,0:T(8,128)S(1)} %shard_map.87.own, f32[648,128]{1,0:T(8,128)S(1)} %collective-permute-done.9.other, f32[4,128]{1,0:T(4,128)S(1)} %get-tuple-element.49.energy_ref, ...), custom_call_target="tpu_custom_call" | custom-call | flops 402653184 | bytes 2424832 | tf_op jit(solution)/shard_map/pallas_call | solution.py:77
  31.5 1.3 %collective-permute-start.10 = (f32[8,256]{1,0:T(8,128)S(1)}, f32[8,256]{1,0:T(8,128)S(1)}, u32[]{:S(2)}, u32[]{:S(2)}) collective-permute-start(f32[8,256]{1,0:T(8,128)S(1)} %get-tuple-element.54.first), channel_id=1, source_target_pairs={{0,3},{1,2},{2,1},{3,0},{4,7},{5,6},{6,5},{7,4},{8,11},{9,10},{10,... | collective-permute-start | bytes 24584 | tf_op jit(solution)/shard_map/ppermute | solution.py:682
  32.8 1.8 %collective-permute-done.10.second = f32[8,256]{1,0:T(8,128)S(1)} collective-permute-done((f32[8,256]{1,0:T(8,128)S(1)}, f32[8,256]{1,0:T(8,128)S(1)}, u32[]{:S(2)}, u32[]{:S(2)}) %collective-permute-start.10) | collective-permute-done | bytes 8224 | tf_op jit(solution)/shard_map/ppermute | solution.py:682
  35.2 0.7 %shard_map.90.image = f32[576,128]{1,0:T(8,128)S(1)} custom-call(bf16[2,256,256]{2,1,0:T(8,128)(2,1)S(1)} %get-tuple-element.55.rounded_ref, bf16[1,256,128]{2,1,0:T(8,128)(2,1)S(1)} %get-tuple-element.56.rounded_more, bf16[512,512]{1,0:T(8,128)(2,1)S(1)} %copy-done, bf16[32,144,256]{2,1,0:T(8,128)(2,1)S(1)} %get-tuple-element.36.particles), custom_call_target="tpu_custom_call" | custom-call | flops 268435456 | bytes 4096000 | tf_op jit(solution)/shard_map/pallas_call | solution.py:77
  35.9 0.6 %collective-permute-done.11.spectrum = bf16[42,16,128]{2,1,0:T(8,128)(2,1)S(1)} collective-permute-done((bf16[42,16,128]{2,1,0:T(8,128)(2,1)S(1)}, bf16[42,16,128]{2,1,0:T(8,128)(2,1)S(1)}, u32[]{:S(2)}, u32[]{:S(2)}) %collective-permute-start.11) | collective-permute-done | bytes 172064 | tf_op jit(solution)/shard_map/ppermute | solution.py:682
  36.5 0.6 %shard_map.91 = (f32[72,128]{1,0:T(8,128)S(1)}, f32[72,128]{1,0:T(8,128)S(1)}, f32[72,128]{1,0:T(8,128)S(1)}, f32[72,128]{1,0:T(8,128)S(1)}, f32[1,144]{1,0:T(1,128)S(1)}) custom-call(f32[576,128]{1,0:T(8,128)S(1)} %shard_map.90.image, bf16[42,16,128]{2,1,0:T(8,128)(2,1)S(1)} %get-tuple-element.57.mine, ...), custom_call_target="tpu_custom_call" | custom-call | flops 352321536 | bytes 3473408 | tf_op jit(solution)/shard_map/pallas_call | solution.py:77
  37.0 2.3 %collective-permute-start.12 = (f32[72,128]{1,0:T(8,128)S(1)}, f32[72,128]{1,0:T(8,128)S(1)}, u32[]{:S(2)}, u32[]{:S(2)}) collective-permute-start(f32[72,128]{1,0:T(8,128)S(1)} %get-tuple-element.58), channel_id=1, source_target_pairs={{0,12},{4,8},{8,4},{12,0},{1,13},{5,9},{9,5},{13,1},{2,14},{6,10},... | collective-permute-start | bytes 110600 | tf_op jit(solution)/shard_map/ppermute | solution.py:682
  39.4 2.1 %collective-permute-start.14 = (f32[72,128]{1,0:T(8,128)S(1)}, f32[72,128]{1,0:T(8,128)S(1)}, u32[]{:S(2)}, u32[]{:S(2)}) collective-permute-start(f32[72,128]{1,0:T(8,128)S(1)} %get-tuple-element.60), channel_id=1, source_target_pairs={{0,4},{4,0},{8,12},{12,8},{1,5},{5,1},{9,13},{13,9},{2,6},{6,2},{1... | collective-permute-start | bytes 110600 | tf_op jit(solution)/shard_map/ppermute | solution.py:682
  41.5 1.6 %collective-permute-done.12.refs_0_ = f32[72,128]{1,0:T(8,128)S(1)} collective-permute-done((f32[72,128]{1,0:T(8,128)S(1)}, f32[72,128]{1,0:T(8,128)S(1)}, u32[]{:S(2)}, u32[]{:S(2)}) %collective-permute-start.12) | collective-permute-done | bytes 36896 | tf_op jit(solution)/shard_map/ppermute | solution.py:682
  43.1 1.1 %collective-permute-done.13.refs_1_ = f32[72,128]{1,0:T(8,128)S(1)} collective-permute-done((f32[72,128]{1,0:T(8,128)S(1)}, f32[72,128]{1,0:T(8,128)S(1)}, u32[]{:S(2)}, u32[]{:S(2)}) %collective-permute-start.13) | collective-permute-done | bytes 36896 | tf_op jit(solution)/shard_map/ppermute | solution.py:682
  44.3 0.6 %shard_map.92 = (f32[1,64,128]{2,1,0:T(8,128)}, f32[1,144]{1,0:T(1,128)}) custom-call(f32[72,128]{1,0:T(8,128)S(1)} %collective-permute-done.12.refs_0_, f32[72,128]{1,0:T(8,128)S(1)} %collective-permute-done.13.refs_1_, f32[72,128]{1,0:T(8,128)S(1)} %collective-permute-done.14.refs_2_, f32[72,128]{1,0:T(8,128)S(1)} %get-tuple-element.61.refs_3_, ...), custom_call_target="tpu_custom_call" | custom-call | bytes 245760 | tf_op jit(solution)/shard_map/pallas_call | solution.py:77
  (26 shorter events, 2.3 us)
Async XLA Ops:
  0.6 5.7 %copy-start.5 = (bf16[288,64,128]{2,1,0:T(8,128)(2,1)S(1)}, bf16[288,64,128]{2,1,0:T(8,128)(2,1)}, u32[]{:S(2)}) copy-start(bf16[288,64,128]{2,1,0:T(8,128)(2,1)} %particles_ref.1) | copy-start | bytes 14155780
  0.6 7.2 %collective-permute-start.1 = (bf16[1,64,128]{2,1,0:T(8,128)(2,1)}, bf16[1,64,128]{2,1,0:T(8,128)(2,1)S(1)}, u32[]{:S(2)}, u32[]{:S(2)}) collective-permute-start(bf16[1,64,128]{2,1,0:T(8,128)(2,1)} %refs_0_.1), channel_id=1, source_target_pairs={{0,8},{4,12},{8,0},{12,4},{1,9},{5,13},{9,1},{13,5},{2,10},{6,14},... | collective-permute-start | bytes 49160 | tf_op jit(solution)/shard_map/ppermute | solution.py:682
  4.7 5.7 %collective-permute-start = (bf16[1,64,128]{2,1,0:T(8,128)(2,1)}, bf16[1,64,128]{2,1,0:T(8,128)(2,1)S(1)}, u32[]{:S(2)}, u32[]{:S(2)}) collective-permute-start(bf16[1,64,128]{2,1,0:T(8,128)(2,1)} %refs_0_.1), channel_id=1, source_target_pairs={{0,12},{4,8},{8,4},{12,0},{1,13},{5,9},{9,5},{13,1},{2,14},{6,10},... | collective-permute-start | bytes 49160 | tf_op jit(solution)/shard_map/ppermute | solution.py:682
  6.1 4.4 %collective-permute-start.2 = (bf16[1,64,128]{2,1,0:T(8,128)(2,1)}, bf16[1,64,128]{2,1,0:T(8,128)(2,1)S(1)}, u32[]{:S(2)}, u32[]{:S(2)}) collective-permute-start(bf16[1,64,128]{2,1,0:T(8,128)(2,1)} %refs_0_.1), channel_id=1, source_target_pairs={{0,4},{4,0},{8,12},{12,8},{1,5},{5,1},{9,13},{13,9},{2,6},{6,2},{1... | collective-permute-start | bytes 49160 | tf_op jit(solution)/shard_map/ppermute | solution.py:682
  6.4 4.1 %copy-start.2 = (bf16[1,64,128]{2,1,0:T(8,128)(2,1)S(1)}, bf16[1,64,128]{2,1,0:T(8,128)(2,1)}, u32[]{:S(2)}) copy-start(bf16[1,64,128]{2,1,0:T(8,128)(2,1)} %refs_0_.1) | copy-start | bytes 49156
  6.4 4.1 %copy-start.4 = (f32[64]{0:T(128)S(1)}, f32[64]{0:T(128)}, u32[]{:S(2)}) copy-start(f32[64]{0:T(128)} %param.8) | copy-start | bytes 772
  7.8 3.7 %copy-start.3 = (s32[288]{0:T(512)S(1)}, s32[288]{0:T(512)}, u32[]{:S(2)}) copy-start(s32[288]{0:T(512)} %prior_ref.1) | copy-start | bytes 3460
  10.5 2.6 %copy-start.1 = (bf16[512,768]{1,0:T(8,128)(2,1)S(1)}, bf16[512,768]{1,0:T(8,128)(2,1)}, u32[]{:S(2)}) copy-start(bf16[512,768]{1,0:T(8,128)(2,1)} %constant.4.clone.inverse) | copy-start | bytes 2359300
  11.4 1.6 %collective-permute-start.3 = (f32[648,128]{1,0:T(8,128)S(1)}, f32[648,128]{1,0:T(8,128)S(1)}, u32[]{:S(2)}, u32[]{:S(2)}) collective-permute-start(f32[648,128]{1,0:T(8,128)S(1)} %get-tuple-element.37), channel_id=1, source_target_pairs={{0,1},{1,0},{2,3},{3,2},{4,5},{5,4},{6,7},{7,6},{8,9},{9,8},{10,11... | collective-permute-start | bytes 995336 | tf_op jit(solution)/shard_map/ppermute | solution.py:682
  11.9 4.9 %copy-start = (bf16[512,512]{1,0:T(8,128)(2,1)S(1)}, bf16[512,512]{1,0:T(8,128)(2,1)}, u32[]{:S(2)}) copy-start(bf16[512,512]{1,0:T(8,128)(2,1)} %constant.5.clone.forward) | copy-start | bytes 1572868
  13.7 3.1 %collective-permute-start.4 = (f32[8,256]{1,0:T(8,128)S(1)}, f32[8,256]{1,0:T(8,128)S(1)}, u32[]{:S(2)}, u32[]{:S(2)}) collective-permute-start(f32[8,256]{1,0:T(8,128)S(1)} %get-tuple-element.43.first), channel_id=1, source_target_pairs={{0,3},{1,2},{2,1},{3,0},{4,7},{5,6},{6,5},{7,4},{8,11},{9,10},{10,... | collective-permute-start | bytes 24584 | tf_op jit(solution)/shard_map/ppermute | solution.py:682
  17.2 1.5 %collective-permute-start.5 = (bf16[42,16,128]{2,1,0:T(8,128)(2,1)S(1)}, bf16[42,16,128]{2,1,0:T(8,128)(2,1)S(1)}, u32[]{:S(2)}, u32[]{:S(2)}) collective-permute-start(bf16[42,16,128]{2,1,0:T(8,128)(2,1)S(1)} %get-tuple-element.46.mine), channel_id=1, source_target_pairs={{0,1},{1,0},{2,3},{3,2},{4,5},{5,4},{6,7},{7,6},{8,9},{9,8},{10,11... | collective-permute-start | bytes 516104 | tf_op jit(solution)/shard_map/ppermute | solution.py:682
  19.3 7.2 %collective-permute-start.8 = (bf16[272,128]{1,0:T(8,128)(2,1)S(1)}, bf16[272,128]{1,0:T(8,128)(2,1)S(1)}, u32[]{:S(2)}, u32[]{:S(2)}) collective-permute-start(bf16[272,128]{1,0:T(8,128)(2,1)S(1)} %shard_map.85.refs_0_), channel_id=1, source_target_pairs={{0,8},{4,12},{8,0},{12,4},{1,9},{5,13},{9,1},{13,5},{2,10},{6,14},... | collective-permute-start | bytes 208904 | tf_op jit(solution)/shard_map/ppermute | solution.py:682
  20.5 6.6 %collective-permute-start.7 = (bf16[272,128]{1,0:T(8,128)(2,1)S(1)}, bf16[272,128]{1,0:T(8,128)(2,1)S(1)}, u32[]{:S(2)}, u32[]{:S(2)}) collective-permute-start(bf16[272,128]{1,0:T(8,128)(2,1)S(1)} %shard_map.85.refs_0_), channel_id=1, source_target_pairs={{0,12},{4,8},{8,4},{12,0},{1,13},{5,9},{9,5},{13,1},{2,14},{6,10},... | collective-permute-start | bytes 208904 | tf_op jit(solution)/shard_map/ppermute | solution.py:682
  21.5 6.8 %collective-permute-start.6 = (bf16[272,128]{1,0:T(8,128)(2,1)S(1)}, bf16[272,128]{1,0:T(8,128)(2,1)S(1)}, u32[]{:S(2)}, u32[]{:S(2)}) collective-permute-start(bf16[272,128]{1,0:T(8,128)(2,1)S(1)} %shard_map.85.refs_0_), channel_id=1, source_target_pairs={{0,4},{4,0},{8,12},{12,8},{1,5},{5,1},{9,13},{13,9},{2,6},{6,2},{1... | collective-permute-start | bytes 208904 | tf_op jit(solution)/shard_map/ppermute | solution.py:682
  29.2 1.6 %collective-permute-start.9 = (f32[648,128]{1,0:T(8,128)S(1)}, f32[648,128]{1,0:T(8,128)S(1)}, u32[]{:S(2)}, u32[]{:S(2)}) collective-permute-start(f32[648,128]{1,0:T(8,128)S(1)} %get-tuple-element.48), channel_id=1, source_target_pairs={{0,1},{1,0},{2,3},{3,2},{4,5},{5,4},{6,7},{7,6},{8,9},{9,8},{10,11... | collective-permute-start | bytes 995336 | tf_op jit(solution)/shard_map/ppermute | solution.py:682
  31.5 3.1 %collective-permute-start.10 = (f32[8,256]{1,0:T(8,128)S(1)}, f32[8,256]{1,0:T(8,128)S(1)}, u32[]{:S(2)}, u32[]{:S(2)}) collective-permute-start(f32[8,256]{1,0:T(8,128)S(1)} %get-tuple-element.54.first), channel_id=1, source_target_pairs={{0,3},{1,2},{2,1},{3,0},{4,7},{5,6},{6,5},{7,4},{8,11},{9,10},{10,... | collective-permute-start | bytes 24584 | tf_op jit(solution)/shard_map/ppermute | solution.py:682
  35.0 1.5 %collective-permute-start.11 = (bf16[42,16,128]{2,1,0:T(8,128)(2,1)S(1)}, bf16[42,16,128]{2,1,0:T(8,128)(2,1)S(1)}, u32[]{:S(2)}, u32[]{:S(2)}) collective-permute-start(bf16[42,16,128]{2,1,0:T(8,128)(2,1)S(1)} %get-tuple-element.57.mine), channel_id=1, source_target_pairs={{0,1},{1,0},{2,3},{3,2},{4,5},{5,4},{6,7},{7,6},{8,9},{9,8},{10,11... | collective-permute-start | bytes 516104 | tf_op jit(solution)/shard_map/ppermute | solution.py:682
  37.0 6.1 %collective-permute-start.12 = (f32[72,128]{1,0:T(8,128)S(1)}, f32[72,128]{1,0:T(8,128)S(1)}, u32[]{:S(2)}, u32[]{:S(2)}) collective-permute-start(f32[72,128]{1,0:T(8,128)S(1)} %get-tuple-element.58), channel_id=1, source_target_pairs={{0,12},{4,8},{8,4},{12,0},{1,13},{5,9},{9,5},{13,1},{2,14},{6,10},... | collective-permute-start | bytes 110600 | tf_op jit(solution)/shard_map/ppermute | solution.py:682
  39.4 4.9 %collective-permute-start.13 = (f32[72,128]{1,0:T(8,128)S(1)}, f32[72,128]{1,0:T(8,128)S(1)}, u32[]{:S(2)}, u32[]{:S(2)}) collective-permute-start(f32[72,128]{1,0:T(8,128)S(1)} %get-tuple-element.59), channel_id=1, source_target_pairs={{0,8},{4,12},{8,0},{12,4},{1,9},{5,13},{9,1},{13,5},{2,10},{6,14},... | collective-permute-start | bytes 110600 | tf_op jit(solution)/shard_map/ppermute | solution.py:682
  39.4 4.9 %collective-permute-start.14 = (f32[72,128]{1,0:T(8,128)S(1)}, f32[72,128]{1,0:T(8,128)S(1)}, u32[]{:S(2)}, u32[]{:S(2)}) collective-permute-start(f32[72,128]{1,0:T(8,128)S(1)} %get-tuple-element.60), channel_id=1, source_target_pairs={{0,4},{4,0},{8,12},{12,8},{1,5},{5,1},{9,13},{13,9},{2,6},{6,2},{1... | collective-permute-start | bytes 110600 | tf_op jit(solution)/shard_map/ppermute | solution.py:682

commit v21 on v20

--- a/solution.py
+++ b/solution.py
@@ -707,7 +707,7 @@
     other_images, own_images = prep(particles, permutation, share)
     for step in range(ITERS):
         last = step == ITERS - 1
-        order = [0, *(reversed(turns) if step else reversed(range(1, blocks)))]
+        order = list(range(blocks)) if step else [0, *reversed(range(1, blocks))]
         message, energy, left = weigh(sources, order, inverse_noise, other_images, step == 0)
         message = swap(message, "rot", groups, 1)
         own = correlate(left, own_images)

time: 45 us -> 45 us (level)
  waiting for transfers between devices: 16.9 us -> 15.9 us
  starting transfers between devices: 16.7 us -> 17.6 us
    ppermute x15, waiting for transfers between devices: 16.9 us -> 15.9 us  [swap(): return lax.ppermute(value, axis, [(i, i ^ bit) for i in range(size)])]
    ppermute x15, starting transfers between devices: 16.7 us -> 17.6 us  [swap(): return lax.ppermute(value, axis, [(i, i ^ bit) for i in range(size)])]
  transfers between devices with their start and end apart: 15 -> 15, of which waited for: 12 -> 11; matrix products, arithmetic and copies ran while one was open for 0% -> 0% of each run, Pallas kernels for 11% -> 11%
where the time goes in v21:
time: 45 us; the launch traced here: 44.8 us
  starting transfers between devices  17.6 us (39%)
  waiting for transfers between devices  15.9 us (35%)
  Pallas kernels  10.5 us (23%)
  between operations  0.78 us (2%)
    ppermute x15, starting transfers between devices, swap(): return lax.ppermute(value, axis, [(i, i ^ bit) for i in range(size)])  17.6 us
    ppermute x15, waiting for transfers between devices, swap(): return lax.ppermute(value, axis, [(i, i ^ bit) for i in range(size)])  15.9 us
    pallas_call x16, Pallas kernels, call(): pl.pallas_call(kernel, out_shape=[jax.ShapeDtypeStruct(*x) for x in outs]...  10.5 us
  transfers between devices with their start and end apart: 15, of which 11 were waited for; matrix products, arithmetic and copies ran while one was open for 0% of the time, Pallas kernels for 11%

profile of v21, /device:TPU:0, one launch (start us, length us, event | category | flops | bytes accessed | tf_op | source)
XLA Modules:
  0.0 44.8 jit_solution(11093275138219364386)
XLA Ops:
  0.6 4.1 %collective-permute-start.1 = (bf16[1,64,128]{2,1,0:T(8,128)(2,1)}, bf16[1,64,128]{2,1,0:T(8,128)(2,1)S(1)}, u32[]{:S(2)}, u32[]{:S(2)}) collective-permute-start(bf16[1,64,128]{2,1,0:T(8,128)(2,1)} %refs_0_.1), channel_id=1, source_target_pairs={{0,8},{4,12},{8,0},{12,4},{1,9},{5,13},{9,1},{13,5},{2,10},{6,14},... | collective-permute-start | bytes 49160 | tf_op jit(solution)/shard_map/ppermute | solution.py:682
  4.7 1.3 %collective-permute-start = (bf16[1,64,128]{2,1,0:T(8,128)(2,1)}, bf16[1,64,128]{2,1,0:T(8,128)(2,1)S(1)}, u32[]{:S(2)}, u32[]{:S(2)}) collective-permute-start(bf16[1,64,128]{2,1,0:T(8,128)(2,1)} %refs_0_.1), channel_id=1, source_target_pairs={{0,12},{4,8},{8,4},{12,0},{1,13},{5,9},{9,5},{13,1},{2,14},{6,10},... | collective-permute-start | bytes 49160 | tf_op jit(solution)/shard_map/ppermute | solution.py:682
  6.4 1.4 %shard_map.78 = (bf16[32,144,256]{2,1,0:T(8,128)(2,1)S(1)}, bf16[32,144,256]{2,1,0:T(8,128)(2,1)S(1)}) custom-call(bf16[288,64,128]{2,1,0:T(8,128)(2,1)S(1)} %copy-done.5, bf16[256,256]{1,0:T(8,128)(2,1)S(1)} %shard_map.77.permutation_ref), custom_call_target="tpu_custom_call" | custom-call | flops 2147483648 | bytes 9568256 | tf_op jit(solution)/shard_map/pallas_call | solution.py:77
  7.8 2.6 %collective-permute-done.refs_1_ = bf16[1,64,128]{2,1,0:T(8,128)(2,1)S(1)} collective-permute-done((bf16[1,64,128]{2,1,0:T(8,128)(2,1)}, bf16[1,64,128]{2,1,0:T(8,128)(2,1)S(1)}, u32[]{:S(2)}, u32[]{:S(2)}) %collective-permute-start) | collective-permute-done | bytes 16416 | tf_op jit(solution)/shard_map/ppermute | solution.py:682
  10.5 0.9 %shard_map.79 = (f32[648,128]{1,0:T(8,128)S(1)}, f32[4,128]{1,0:T(4,128)S(1)}, bf16[32,16,256]{2,1,0:T(8,128)(2,1)S(1)}) custom-call(bf16[1,64,128]{2,1,0:T(8,128)(2,1)S(1)} %copy-done.2, bf16[1,64,128]{2,1,0:T(8,128)(2,1)S(1)} %collective-permute-done.refs_1_, bf16[1,64,128]{2,1,0:T(8,128)(2,1)S(1)} %collective-permute-done.1.refs_2_, ...), custom_call_target="tpu_custom_call" | custom-call | flops 150994944 | bytes 3334144 | tf_op jit(solution)/shard_map/pallas_call | solution.py:77
  11.5 0.4 shard_map.81.prior_term
  11.9 0.8 %shard_map.80.own = f32[648,128]{1,0:T(8,128)S(1)} custom-call(bf16[32,16,256]{2,1,0:T(8,128)(2,1)S(1)} %get-tuple-element.35.left_ref, bf16[32,144,256]{2,1,0:T(8,128)(2,1)S(1)} %get-tuple-element.36.particles), custom_call_target="tpu_custom_call" | custom-call | flops 301989888 | bytes 2957312 | tf_op jit(solution)/shard_map/pallas_call | solution.py:77
  13.1 0.6 %shard_map.82 = (f32[2,256,256]{2,1,0:T(8,128)S(1)}, f32[1,256,128]{2,1,0:T(8,128)S(1)}, f32[2,256]{1,0:T(2,128)S(1)}, f32[1,128]{1,0:T(1,128)S(1)}, f32[8,256]{1,0:T(8,128)S(1)}) custom-call(f32[648,128]{1,0:T(8,128)S(1)} %shard_map.80.own, f32[648,128]{1,0:T(8,128)S(1)} %collective-permute-done.3.other, f32[4,128]{1,0:T(4,128)S(1)} %get-tuple-element.38.energy_ref, ...), custom_call_target="tpu_custom_call" | custom-call | flops 402653184 | bytes 2424832 | tf_op jit(solution)/shard_map/pallas_call | solution.py:77
  13.7 1.3 %collective-permute-start.4 = (f32[8,256]{1,0:T(8,128)S(1)}, f32[8,256]{1,0:T(8,128)S(1)}, u32[]{:S(2)}, u32[]{:S(2)}) collective-permute-start(f32[8,256]{1,0:T(8,128)S(1)} %get-tuple-element.43.first), channel_id=1, source_target_pairs={{0,3},{1,2},{2,1},{3,0},{4,7},{5,6},{6,5},{7,4},{8,11},{9,10},{10,... | collective-permute-start | bytes 24584 | tf_op jit(solution)/shard_map/ppermute | solution.py:682
  15.0 1.8 %collective-permute-done.4.second = f32[8,256]{1,0:T(8,128)S(1)} collective-permute-done((f32[8,256]{1,0:T(8,128)S(1)}, f32[8,256]{1,0:T(8,128)S(1)}, u32[]{:S(2)}, u32[]{:S(2)}) %collective-permute-start.4) | collective-permute-done | bytes 8224 | tf_op jit(solution)/shard_map/ppermute | solution.py:682
  17.5 0.7 %shard_map.84.image = f32[576,128]{1,0:T(8,128)S(1)} custom-call(bf16[2,256,256]{2,1,0:T(8,128)(2,1)S(1)} %get-tuple-element.44.rounded_ref, bf16[1,256,128]{2,1,0:T(8,128)(2,1)S(1)} %get-tuple-element.45.rounded_more, bf16[512,512]{1,0:T(8,128)(2,1)S(1)} %copy-done, bf16[32,144,256]{2,1,0:T(8,128)(2,1)S(1)} %get-tuple-element.36.particles), custom_call_target="tpu_custom_call" | custom-call | flops 268435456 | bytes 4096000 | tf_op jit(solution)/shard_map/pallas_call | solution.py:77
  18.1 0.6 %collective-permute-done.5.spectrum = bf16[42,16,128]{2,1,0:T(8,128)(2,1)S(1)} collective-permute-done((bf16[42,16,128]{2,1,0:T(8,128)(2,1)S(1)}, bf16[42,16,128]{2,1,0:T(8,128)(2,1)S(1)}, u32[]{:S(2)}, u32[]{:S(2)}) %collective-permute-start.5) | collective-permute-done | bytes 172064 | tf_op jit(solution)/shard_map/ppermute | solution.py:682
  18.7 0.6 %shard_map.85.refs_0_ = bf16[272,128]{1,0:T(8,128)(2,1)S(1)} custom-call(f32[576,128]{1,0:T(8,128)S(1)} %shard_map.84.image, bf16[42,16,128]{2,1,0:T(8,128)(2,1)S(1)} %get-tuple-element.46.mine, bf16[42,16,128]{2,1,0:T(8,128)(2,1)S(1)} %collective-permute-done.5.spectrum, bf16[32,144,256]{2,1,0:T(8,128)(2,1)S(1)} %get-tuple-element.34.refs_5_.particles), custom_call_target="tpu_custom_call" | custom-call | flops 352321536 | bytes 3362816 | tf_op jit(solution)/shard_map/pallas_call | solution.py:77
  19.3 2.0 %collective-permute-start.8 = (bf16[272,128]{1,0:T(8,128)(2,1)S(1)}, bf16[272,128]{1,0:T(8,128)(2,1)S(1)}, u32[]{:S(2)}, u32[]{:S(2)}) collective-permute-start(bf16[272,128]{1,0:T(8,128)(2,1)S(1)} %shard_map.85.refs_0_), channel_id=1, source_target_pairs={{0,12},{4,8},{8,4},{12,0},{1,13},{5,9},{9,5},{13,1},{2,14},{6,10},... | collective-permute-start | bytes 208904 | tf_op jit(solution)/shard_map/ppermute | solution.py:682
  21.3 2.4 %collective-permute-start.6 = (bf16[272,128]{1,0:T(8,128)(2,1)S(1)}, bf16[272,128]{1,0:T(8,128)(2,1)S(1)}, u32[]{:S(2)}, u32[]{:S(2)}) collective-permute-start(bf16[272,128]{1,0:T(8,128)(2,1)S(1)} %shard_map.85.refs_0_), channel_id=1, source_target_pairs={{0,4},{4,0},{8,12},{12,8},{1,5},{5,1},{9,13},{13,9},{2,6},{6,2},{1... | collective-permute-start | bytes 208904 | tf_op jit(solution)/shard_map/ppermute | solution.py:682
  23.7 2.5 %collective-permute-done.8.refs_3_ = bf16[272,128]{1,0:T(8,128)(2,1)S(1)} collective-permute-done((bf16[272,128]{1,0:T(8,128)(2,1)S(1)}, bf16[272,128]{1,0:T(8,128)(2,1)S(1)}, u32[]{:S(2)}, u32[]{:S(2)}) %collective-permute-start.8) | collective-permute-done | bytes 69664 | tf_op jit(solution)/shard_map/ppermute | solution.py:682
  26.2 2.1 %collective-permute-done.7.refs_2_ = bf16[272,128]{1,0:T(8,128)(2,1)S(1)} collective-permute-done((bf16[272,128]{1,0:T(8,128)(2,1)S(1)}, bf16[272,128]{1,0:T(8,128)(2,1)S(1)}, u32[]{:S(2)}, u32[]{:S(2)}) %collective-permute-start.7) | collective-permute-done | bytes 69664 | tf_op jit(solution)/shard_map/ppermute | solution.py:682
  28.4 0.9 %shard_map.86 = (f32[648,128]{1,0:T(8,128)S(1)}, f32[4,128]{1,0:T(4,128)S(1)}, bf16[32,16,256]{2,1,0:T(8,128)(2,1)S(1)}) custom-call(bf16[272,128]{1,0:T(8,128)(2,1)S(1)} %shard_map.85.refs_0_, bf16[272,128]{1,0:T(8,128)(2,1)S(1)} %collective-permute-done.6.refs_1_, bf16[272,128]{1,0:T(8,128)(2,1)S(1)} %collective-permute-done.7.refs_2_, ...), custom_call_target="tpu_custom_call" | custom-call | flops 150994944 | bytes 3547136 | tf_op jit(solution)/shard_map/pallas_call | solution.py:77
  29.3 0.8 %shard_map.87.own = f32[648,128]{1,0:T(8,128)S(1)} custom-call(bf16[32,16,256]{2,1,0:T(8,128)(2,1)S(1)} %get-tuple-element.47.left_ref, bf16[32,144,256]{2,1,0:T(8,128)(2,1)S(1)} %get-tuple-element.36.particles), custom_call_target="tpu_custom_call" | custom-call | flops 301989888 | bytes 2957312 | tf_op jit(solution)/shard_map/pallas_call | solution.py:77
  30.1 0.8 %collective-permute-done.9.other = f32[648,128]{1,0:T(8,128)S(1)} collective-permute-done((f32[648,128]{1,0:T(8,128)S(1)}, f32[648,128]{1,0:T(8,128)S(1)}, u32[]{:S(2)}, u32[]{:S(2)}) %collective-permute-start.9) | collective-permute-done | bytes 331808 | tf_op jit(solution)/shard_map/ppermute | solution.py:682
  30.9 0.7 %shard_map.88 = (f32[2,256,256]{2,1,0:T(8,128)S(1)}, f32[1,256,128]{2,1,0:T(8,128)S(1)}, f32[2,256]{1,0:T(2,128)S(1)}, f32[1,128]{1,0:T(1,128)S(1)}, f32[8,256]{1,0:T(8,128)S(1)}) custom-call(f32[648,128]{1,0:T(8,128)S(1)} %shard_map.87.own, f32[648,128]{1,0:T(8,128)S(1)} %collective-permute-done.9.other, f32[4,128]{1,0:T(4,128)S(1)} %get-tuple-element.49.energy_ref, ...), custom_call_target="tpu_custom_call" | custom-call | flops 402653184 | bytes 2424832 | tf_op jit(solution)/shard_map/pallas_call | solution.py:77
  31.6 1.3 %collective-permute-start.10 = (f32[8,256]{1,0:T(8,128)S(1)}, f32[8,256]{1,0:T(8,128)S(1)}, u32[]{:S(2)}, u32[]{:S(2)}) collective-permute-start(f32[8,256]{1,0:T(8,128)S(1)} %get-tuple-element.54.first), channel_id=1, source_target_pairs={{0,3},{1,2},{2,1},{3,0},{4,7},{5,6},{6,5},{7,4},{8,11},{9,10},{10,... | collective-permute-start | bytes 24584 | tf_op jit(solution)/shard_map/ppermute | solution.py:682
  32.9 1.8 %collective-permute-done.10.second = f32[8,256]{1,0:T(8,128)S(1)} collective-permute-done((f32[8,256]{1,0:T(8,128)S(1)}, f32[8,256]{1,0:T(8,128)S(1)}, u32[]{:S(2)}, u32[]{:S(2)}) %collective-permute-start.10) | collective-permute-done | bytes 8224 | tf_op jit(solution)/shard_map/ppermute | solution.py:682
  34.7 0.4 shard_map.89
  35.3 0.7 %shard_map.90.image = f32[576,128]{1,0:T(8,128)S(1)} custom-call(bf16[2,256,256]{2,1,0:T(8,128)(2,1)S(1)} %get-tuple-element.55.rounded_ref, bf16[1,256,128]{2,1,0:T(8,128)(2,1)S(1)} %get-tuple-element.56.rounded_more, bf16[512,512]{1,0:T(8,128)(2,1)S(1)} %copy-done, bf16[32,144,256]{2,1,0:T(8,128)(2,1)S(1)} %get-tuple-element.36.particles), custom_call_target="tpu_custom_call" | custom-call | flops 268435456 | bytes 4096000 | tf_op jit(solution)/shard_map/pallas_call | solution.py:77
  36.0 0.6 %collective-permute-done.11.spectrum = bf16[42,16,128]{2,1,0:T(8,128)(2,1)S(1)} collective-permute-done((bf16[42,16,128]{2,1,0:T(8,128)(2,1)S(1)}, bf16[42,16,128]{2,1,0:T(8,128)(2,1)S(1)}, u32[]{:S(2)}, u32[]{:S(2)}) %collective-permute-start.11) | collective-permute-done | bytes 172064 | tf_op jit(solution)/shard_map/ppermute | solution.py:682
  36.6 0.6 %shard_map.91 = (f32[72,128]{1,0:T(8,128)S(1)}, f32[72,128]{1,0:T(8,128)S(1)}, f32[72,128]{1,0:T(8,128)S(1)}, f32[72,128]{1,0:T(8,128)S(1)}, f32[1,144]{1,0:T(1,128)S(1)}) custom-call(f32[576,128]{1,0:T(8,128)S(1)} %shard_map.90.image, bf16[42,16,128]{2,1,0:T(8,128)(2,1)S(1)} %get-tuple-element.57.mine, ...), custom_call_target="tpu_custom_call" | custom-call | flops 352321536 | bytes 3473408 | tf_op jit(solution)/shard_map/pallas_call | solution.py:77
  37.1 2.0 %collective-permute-start.12 = (f32[72,128]{1,0:T(8,128)S(1)}, f32[72,128]{1,0:T(8,128)S(1)}, u32[]{:S(2)}, u32[]{:S(2)}) collective-permute-start(f32[72,128]{1,0:T(8,128)S(1)} %get-tuple-element.58), channel_id=1, source_target_pairs={{0,12},{4,8},{8,4},{12,0},{1,13},{5,9},{9,5},{13,1},{2,14},{6,10},... | collective-permute-start | bytes 110600 | tf_op jit(solution)/shard_map/ppermute | solution.py:682
  39.2 2.4 %collective-permute-start.14 = (f32[72,128]{1,0:T(8,128)S(1)}, f32[72,128]{1,0:T(8,128)S(1)}, u32[]{:S(2)}, u32[]{:S(2)}) collective-permute-start(f32[72,128]{1,0:T(8,128)S(1)} %get-tuple-element.60), channel_id=1, source_target_pairs={{0,4},{4,0},{8,12},{12,8},{1,5},{5,1},{9,13},{13,9},{2,6},{6,2},{1... | collective-permute-start | bytes 110600 | tf_op jit(solution)/shard_map/ppermute | solution.py:682
  41.6 1.5 %collective-permute-done.12.refs_0_ = f32[72,128]{1,0:T(8,128)S(1)} collective-permute-done((f32[72,128]{1,0:T(8,128)S(1)}, f32[72,128]{1,0:T(8,128)S(1)}, u32[]{:S(2)}, u32[]{:S(2)}) %collective-permute-start.12) | collective-permute-done | bytes 36896 | tf_op jit(solution)/shard_map/ppermute | solution.py:682
  43.0 1.1 %collective-permute-done.13.refs_1_ = f32[72,128]{1,0:T(8,128)S(1)} collective-permute-done((f32[72,128]{1,0:T(8,128)S(1)}, f32[72,128]{1,0:T(8,128)S(1)}, u32[]{:S(2)}, u32[]{:S(2)}) %collective-permute-start.13) | collective-permute-done | bytes 36896 | tf_op jit(solution)/shard_map/ppermute | solution.py:682
  44.2 0.6 %shard_map.92 = (f32[1,64,128]{2,1,0:T(8,128)}, f32[1,144]{1,0:T(1,128)}) custom-call(f32[72,128]{1,0:T(8,128)S(1)} %collective-permute-done.12.refs_0_, f32[72,128]{1,0:T(8,128)S(1)} %collective-permute-done.13.refs_1_, f32[72,128]{1,0:T(8,128)S(1)} %collective-permute-done.14.refs_2_, f32[72,128]{1,0:T(8,128)S(1)} %get-tuple-element.61.refs_3_, ...), custom_call_target="tpu_custom_call" | custom-call | bytes 245760 | tf_op jit(solution)/shard_map/pallas_call | solution.py:77
  (26 shorter events, 1.5 us)
Async XLA Ops:
  0.6 5.7 %copy-start.5 = (bf16[288,64,128]{2,1,0:T(8,128)(2,1)S(1)}, bf16[288,64,128]{2,1,0:T(8,128)(2,1)}, u32[]{:S(2)}) copy-start(bf16[288,64,128]{2,1,0:T(8,128)(2,1)} %particles_ref.1) | copy-start | bytes 14155780
  0.6 7.2 %collective-permute-start.1 = (bf16[1,64,128]{2,1,0:T(8,128)(2,1)}, bf16[1,64,128]{2,1,0:T(8,128)(2,1)S(1)}, u32[]{:S(2)}, u32[]{:S(2)}) collective-permute-start(bf16[1,64,128]{2,1,0:T(8,128)(2,1)} %refs_0_.1), channel_id=1, source_target_pairs={{0,8},{4,12},{8,0},{12,4},{1,9},{5,13},{9,1},{13,5},{2,10},{6,14},... | collective-permute-start | bytes 49160 | tf_op jit(solution)/shard_map/ppermute | solution.py:682
  4.7 5.7 %collective-permute-start = (bf16[1,64,128]{2,1,0:T(8,128)(2,1)}, bf16[1,64,128]{2,1,0:T(8,128)(2,1)S(1)}, u32[]{:S(2)}, u32[]{:S(2)}) collective-permute-start(bf16[1,64,128]{2,1,0:T(8,128)(2,1)} %refs_0_.1), channel_id=1, source_target_pairs={{0,12},{4,8},{8,4},{12,0},{1,13},{5,9},{9,5},{13,1},{2,14},{6,10},... | collective-permute-start | bytes 49160 | tf_op jit(solution)/shard_map/ppermute | solution.py:682
  6.1 4.4 %collective-permute-start.2 = (bf16[1,64,128]{2,1,0:T(8,128)(2,1)}, bf16[1,64,128]{2,1,0:T(8,128)(2,1)S(1)}, u32[]{:S(2)}, u32[]{:S(2)}) collective-permute-start(bf16[1,64,128]{2,1,0:T(8,128)(2,1)} %refs_0_.1), channel_id=1, source_target_pairs={{0,4},{4,0},{8,12},{12,8},{1,5},{5,1},{9,13},{13,9},{2,6},{6,2},{1... | collective-permute-start | bytes 49160 | tf_op jit(solution)/shard_map/ppermute | solution.py:682
  6.4 4.1 %copy-start.2 = (bf16[1,64,128]{2,1,0:T(8,128)(2,1)S(1)}, bf16[1,64,128]{2,1,0:T(8,128)(2,1)}, u32[]{:S(2)}) copy-start(bf16[1,64,128]{2,1,0:T(8,128)(2,1)} %refs_0_.1) | copy-start | bytes 49156
  6.4 4.1 %copy-start.4 = (f32[64]{0:T(128)S(1)}, f32[64]{0:T(128)}, u32[]{:S(2)}) copy-start(f32[64]{0:T(128)} %param.8) | copy-start | bytes 772
  7.8 3.7 %copy-start.3 = (s32[288]{0:T(512)S(1)}, s32[288]{0:T(512)}, u32[]{:S(2)}) copy-start(s32[288]{0:T(512)} %prior_ref.1) | copy-start | bytes 3460
  10.5 2.6 %copy-start.1 = (bf16[512,768]{1,0:T(8,128)(2,1)S(1)}, bf16[512,768]{1,0:T(8,128)(2,1)}, u32[]{:S(2)}) copy-start(bf16[512,768]{1,0:T(8,128)(2,1)} %constant.4.clone.inverse) | copy-start | bytes 2359300
  11.4 1.6 %collective-permute-start.3 = (f32[648,128]{1,0:T(8,128)S(1)}, f32[648,128]{1,0:T(8,128)S(1)}, u32[]{:S(2)}, u32[]{:S(2)}) collective-permute-start(f32[648,128]{1,0:T(8,128)S(1)} %get-tuple-element.37), channel_id=1, source_target_pairs={{0,1},{1,0},{2,3},{3,2},{4,5},{5,4},{6,7},{7,6},{8,9},{9,8},{10,11... | collective-permute-start | bytes 995336 | tf_op jit(solution)/shard_map/ppermute | solution.py:682
  11.9 4.9 %copy-start = (bf16[512,512]{1,0:T(8,128)(2,1)S(1)}, bf16[512,512]{1,0:T(8,128)(2,1)}, u32[]{:S(2)}) copy-start(bf16[512,512]{1,0:T(8,128)(2,1)} %constant.5.clone.forward) | copy-start | bytes 1572868
  13.7 3.1 %collective-permute-start.4 = (f32[8,256]{1,0:T(8,128)S(1)}, f32[8,256]{1,0:T(8,128)S(1)}, u32[]{:S(2)}, u32[]{:S(2)}) collective-permute-start(f32[8,256]{1,0:T(8,128)S(1)} %get-tuple-element.43.first), channel_id=1, source_target_pairs={{0,3},{1,2},{2,1},{3,0},{4,7},{5,6},{6,5},{7,4},{8,11},{9,10},{10,... | collective-permute-start | bytes 24584 | tf_op jit(solution)/shard_map/ppermute | solution.py:682
  17.2 1.5 %collective-permute-start.5 = (bf16[42,16,128]{2,1,0:T(8,128)(2,1)S(1)}, bf16[42,16,128]{2,1,0:T(8,128)(2,1)S(1)}, u32[]{:S(2)}, u32[]{:S(2)}) collective-permute-start(bf16[42,16,128]{2,1,0:T(8,128)(2,1)S(1)} %get-tuple-element.46.mine), channel_id=1, source_target_pairs={{0,1},{1,0},{2,3},{3,2},{4,5},{5,4},{6,7},{7,6},{8,9},{9,8},{10,11... | collective-permute-start | bytes 516104 | tf_op jit(solution)/shard_map/ppermute | solution.py:682
  19.3 6.9 %collective-permute-start.8 = (bf16[272,128]{1,0:T(8,128)(2,1)S(1)}, bf16[272,128]{1,0:T(8,128)(2,1)S(1)}, u32[]{:S(2)}, u32[]{:S(2)}) collective-permute-start(bf16[272,128]{1,0:T(8,128)(2,1)S(1)} %shard_map.85.refs_0_), channel_id=1, source_target_pairs={{0,12},{4,8},{8,4},{12,0},{1,13},{5,9},{9,5},{13,1},{2,14},{6,10},... | collective-permute-start | bytes 208904 | tf_op jit(solution)/shard_map/ppermute | solution.py:682
  21.3 7.0 %collective-permute-start.7 = (bf16[272,128]{1,0:T(8,128)(2,1)S(1)}, bf16[272,128]{1,0:T(8,128)(2,1)S(1)}, u32[]{:S(2)}, u32[]{:S(2)}) collective-permute-start(bf16[272,128]{1,0:T(8,128)(2,1)S(1)} %shard_map.85.refs_0_), channel_id=1, source_target_pairs={{0,8},{4,12},{8,0},{12,4},{1,9},{5,13},{9,1},{13,5},{2,10},{6,14},... | collective-permute-start | bytes 208904 | tf_op jit(solution)/shard_map/ppermute | solution.py:682
  21.3 7.0 %collective-permute-start.6 = (bf16[272,128]{1,0:T(8,128)(2,1)S(1)}, bf16[272,128]{1,0:T(8,128)(2,1)S(1)}, u32[]{:S(2)}, u32[]{:S(2)}) collective-permute-start(bf16[272,128]{1,0:T(8,128)(2,1)S(1)} %shard_map.85.refs_0_), channel_id=1, source_target_pairs={{0,4},{4,0},{8,12},{12,8},{1,5},{5,1},{9,13},{13,9},{2,6},{6,2},{1... | collective-permute-start | bytes 208904 | tf_op jit(solution)/shard_map/ppermute | solution.py:682
  29.3 1.6 %collective-permute-start.9 = (f32[648,128]{1,0:T(8,128)S(1)}, f32[648,128]{1,0:T(8,128)S(1)}, u32[]{:S(2)}, u32[]{:S(2)}) collective-permute-start(f32[648,128]{1,0:T(8,128)S(1)} %get-tuple-element.48), channel_id=1, source_target_pairs={{0,1},{1,0},{2,3},{3,2},{4,5},{5,4},{6,7},{7,6},{8,9},{9,8},{10,11... | collective-permute-start | bytes 995336 | tf_op jit(solution)/shard_map/ppermute | solution.py:682
  31.6 3.1 %collective-permute-start.10 = (f32[8,256]{1,0:T(8,128)S(1)}, f32[8,256]{1,0:T(8,128)S(1)}, u32[]{:S(2)}, u32[]{:S(2)}) collective-permute-start(f32[8,256]{1,0:T(8,128)S(1)} %get-tuple-element.54.first), channel_id=1, source_target_pairs={{0,3},{1,2},{2,1},{3,0},{4,7},{5,6},{6,5},{7,4},{8,11},{9,10},{10,... | collective-permute-start | bytes 24584 | tf_op jit(solution)/shard_map/ppermute | solution.py:682
  35.1 1.5 %collective-permute-start.11 = (bf16[42,16,128]{2,1,0:T(8,128)(2,1)S(1)}, bf16[42,16,128]{2,1,0:T(8,128)(2,1)S(1)}, u32[]{:S(2)}, u32[]{:S(2)}) collective-permute-start(bf16[42,16,128]{2,1,0:T(8,128)(2,1)S(1)} %get-tuple-element.57.mine), channel_id=1, source_target_pairs={{0,1},{1,0},{2,3},{3,2},{4,5},{5,4},{6,7},{7,6},{8,9},{9,8},{10,11... | collective-permute-start | bytes 516104 | tf_op jit(solution)/shard_map/ppermute | solution.py:682
  37.1 5.9 %collective-permute-start.12 = (f32[72,128]{1,0:T(8,128)S(1)}, f32[72,128]{1,0:T(8,128)S(1)}, u32[]{:S(2)}, u32[]{:S(2)}) collective-permute-start(f32[72,128]{1,0:T(8,128)S(1)} %get-tuple-element.58), channel_id=1, source_target_pairs={{0,12},{4,8},{8,4},{12,0},{1,13},{5,9},{9,5},{13,1},{2,14},{6,10},... | collective-permute-start | bytes 110600 | tf_op jit(solution)/shard_map/ppermute | solution.py:682
  39.2 5.0 %collective-permute-start.13 = (f32[72,128]{1,0:T(8,128)S(1)}, f32[72,128]{1,0:T(8,128)S(1)}, u32[]{:S(2)}, u32[]{:S(2)}) collective-permute-start(f32[72,128]{1,0:T(8,128)S(1)} %get-tuple-element.59), channel_id=1, source_target_pairs={{0,8},{4,12},{8,0},{12,4},{1,9},{5,13},{9,1},{13,5},{2,10},{6,14},... | collective-permute-start | bytes 110600 | tf_op jit(solution)/shard_map/ppermute | solution.py:682
  39.2 5.0 %collective-permute-start.14 = (f32[72,128]{1,0:T(8,128)S(1)}, f32[72,128]{1,0:T(8,128)S(1)}, u32[]{:S(2)}, u32[]{:S(2)}) collective-permute-start(f32[72,128]{1,0:T(8,128)S(1)} %get-tuple-element.60), channel_id=1, source_target_pairs={{0,4},{4,0},{8,12},{12,8},{1,5},{5,1},{9,13},{13,9},{2,6},{6,2},{1... | collective-permute-start | bytes 110600 | tf_op jit(solution)/shard_map/ppermute | solution.py:682

commit v22 on v20

--- a/solution.py
+++ b/solution.py
@@ -29,7 +29,7 @@
 
 def tables(half_freq):
     turn = np.arange(ANG)
-    inverse, forward = [], []
+    near, far, forward = [], [], []
     for group in range(2):
         sides = {}
         for which in range(2):
@@ -40,10 +40,11 @@
                 np.concatenate([scale * np.cos(angle), -scale * np.sin(angle)], 1),
                 np.concatenate([np.cos(angle), np.sin(angle)], 1).T,
             )
-        inverse.append(np.concatenate([sides[group][0], sides[1 - group][0]], 1))
+        near.append(sides[group][0])
+        far.append(sides[1 - group][0])
         forward.append(np.concatenate([sides[1 - group][1], sides[group][1]], 0))
     result = []
-    for table, kinds in ((inverse, (0, 0, 1)), (forward, (0, 1))):
+    for table, kinds in ((near, (0, 0, 1)), (far, (0, 0, 1)), (forward, (0, 1))):
         table = np.concatenate(table, 0).astype(np.float32)
         high = table.astype(BF16)
         parts = [high, (table - high.astype(np.float32)).astype(BF16)]
@@ -299,68 +300,97 @@
     )
 
 
-def correlate_kernel(left_ref, particles, out):
+def correlate_kernel(left_ref, particles, energy_ref, prior_term, table, *refs):
+    partial, partial_more, field = refs
     pairs, share, _ = particles.shape
     classes = left_ref.shape[1] // 4
-    pitch = 2 * pairs + SPARE
+    freqs, pitch = 2 * pairs, 2 * pairs + SPARE
 
     def body(f):
         values = [times(left_ref[f + i], particles[f + i]) for i in range(GROUP)]
-        place(out, f, values, classes, pitch)
+        place(field, f, values, classes, pitch)
 
     every(pairs, body)
 
-
-def correlate(left, particles):
+    def energy_of(k):
+        return energy_ref[pl.ds(k, 1), :]
+
+    def slab(i, carry):
+        prior = jnp.concatenate([prior_term[:, :128]] * 2, 1)
+        energy = jnp.concatenate([energy_of(2 * i), energy_of(2 * i + 1)], 1)
+        partial[i] = invert(table, two_classes(field, i, pitch, freqs)) - 0.5 * energy + prior
+        return carry
+
+    each(classes // 2, slab, 0)
+    for unit in range(partial_more.shape[0]):
+        energy = beside(energy_of, unit, classes, share)
+        value = several_classes(field, unit, classes, share, pitch, freqs)
+        partial_more[unit] = invert(table, value) - 0.5 * energy + prior_term[:, 128:]
+
+
+def two_classes(field, i, pitch, freqs):
+    parts = [
+        [field[rows((4 * i + 2 * j + part) * pitch, freqs), :] for j in range(2)]
+        for part in range(2)
+    ]
+    return jnp.concatenate([jnp.concatenate(part, 1) for part in parts], 0)
+
+
+def several_classes(field, unit, classes, share, pitch, freqs):
+    return jnp.concatenate(
+        [unpack(field, unit, part, classes, share, pitch, freqs) for part in range(2)], 0
+    )
+
+
+def beside(value_of, unit, classes, share):
+    width, bundle, _ = layout(classes, share)
+    lane = lax.broadcasted_iota(jnp.int32, (1, 128), 1)
+    return sum(
+        jnp.where(lane // width == j, value_of(unit * bundle + j), 0.0) for j in range(bundle)
+    )
+
+
+def invert(table, value):
+    high, low = split(value)
+    return dot(table[table_rows(0, ANG), :], jnp.concatenate([high, low, high], 0))
+
+
+def correlate(left, particles, energy, prior_term, table):
     pairs, share, twice = particles.shape
     classes = left.shape[1] // 4
     pitch = 2 * pairs + SPARE
     return call(
         correlate_kernel,
-        [left, particles],
+        [left, particles, energy, prior_term, table],
+        [((classes // 2, ANG, 256), F32), ((layout(classes, share)[2], ANG, 128), F32)],
         [((corr_lines(classes, share, pitch), 128), F32)],
         flops=2 * left.shape[1] * share * pairs * twice * 8,
-    )[0]
+    )
 
 
 def table_rows(base, count):
     return pl.ds(pl.multiple_of(lax.axis_index("rot") * ANG + base, 128), count)
 
 
-def score_kernel(share, own, other, energy_ref, prior_term, inverse, *refs):
+def score_kernel(share, partial, partial_more, other, table, *refs):
     weights, more, tops, more_tops, peaks = refs
-    classes = energy_ref.shape[0]
+    classes = 2 * partial.shape[0]
     width, bundle, units = layout(classes, share)
     freqs = ANG // 4
     pitch = freqs + SPARE
-    at = table_rows(0, ANG)
-    lane = lax.broadcasted_iota(jnp.int32, (1, 128), 1)
-
-    def exponentials(value, energy, prior):
-        high, low = split(value)
-        inner = dot(inverse[at, :], jnp.concatenate([high, low, high], 0))
-        scores = inner - 0.5 * energy + prior
+
+    def exponentials(scores):
         top = jnp.max(scores, axis=0, keepdims=True)
         value = jnp.exp(scores - top)
         return value, top, jnp.sum(value, axis=0, keepdims=True)
 
     def energy_of(k):
-        return energy_ref[pl.ds(k, 1), :] + other[rows(2 * k * pitch + freqs, SPARE), :][:1]
+        return other[rows(2 * k * pitch + freqs, SPARE), :][:1]
 
     def slab(i, carry):
-        value = jnp.concatenate(
-            [
-                jnp.concatenate(
-                    [ref[rows((4 * i + 2 * j + part) * pitch, freqs), :] for j in range(2)], 1
-                )
-                for ref in (own, other)
-                for part in range(2)
-            ],
-            0,
-        )
         energy = jnp.concatenate([energy_of(2 * i), energy_of(2 * i + 1)], 1)
-        prior = jnp.concatenate([prior_term[:, :128]] * 2, 1)
-        weights[i], top, total = exponentials(value, energy, prior)
+        inner = invert(table, two_classes(other, i, pitch, freqs))
+        weights[i], top, total = exponentials(inner + (partial[i] - 0.5 * energy))
         tops[pl.ds(i, 1), :] = top
         for j in (0, 128):
             carry = merge(carry, (top[:, j : j + 128], total[:, j : j + 128]))
@@ -370,19 +400,9 @@
     top, total = each(classes // 2, slab, empty)
     rest = empty
     for unit in range(units):
-        value = jnp.concatenate(
-            [
-                unpack(ref, unit, part, classes, share, pitch, freqs)
-                for ref in (own, other)
-                for part in range(2)
-            ],
-            0,
-        )
-        energy = sum(
-            jnp.where(lane // width == j, energy_of(unit * bundle + j), 0.0)
-            for j in range(bundle)
-        )
-        more[unit], more_top, more_total = exponentials(value, energy, prior_term[:, 128:])
+        energy = beside(energy_of, unit, classes, share)
+        inner = invert(table, several_classes(other, unit, classes, share, pitch, freqs))
+        more[unit], more_top, more_total = exponentials(inner + (partial_more[unit] - 0.5 * energy))
         more_tops[pl.ds(unit, 1), :] = more_top
         for j in range(bundle):
             rest = merge(rest, (turned(more_top, -j * width), turned(more_total, -j * width)))
@@ -394,12 +414,12 @@
     )
 
 
-def scores(own, other, energy, prior_term, inverse, share):
-    classes = energy.shape[0]
+def scores(partial, partial_more, other, table, share):
+    classes = 2 * partial.shape[0]
     units = layout(classes, share)[2]
     return call(
         functools.partial(score_kernel, share),
-        [own, other, energy, prior_term, inverse],
+        [partial, partial_more, other, table],
         [
             ((classes // 2, ANG, 256), F32),
             ((units, ANG, 128), F32),
@@ -694,7 +714,7 @@
     blocks = lax.axis_size("blk")
     assert groups == 2 and 2 * groups * freqs == ANG
     share = batch // groups
-    inverse, forward = tables(freqs)
+    near, far, forward = tables(freqs)
     inverse_noise = noise_inv.reshape(1, depth // 2)
     assert blocks & (blocks - 1) == 0
     turns = sorted(range(1, blocks), key=lambda i: (-i.bit_length(), i))
@@ -710,8 +730,8 @@
         order = [0, *(reversed(turns) if step else reversed(range(1, blocks)))]
         message, energy, left = weigh(sources, order, inverse_noise, other_images, step == 0)
         message = swap(message, "rot", groups, 1)
-        own = correlate(left, own_images)
-        *weights, here = scores(own, message, energy, prior_term, inverse, share)
+        partial = correlate(left, own_images, energy, prior_term, near)
+        *weights, here = scores(*partial, message, far, share)
         first = here
         for bit in bits(sides):
             second = swap(first, ("cls", "rot"), sides * groups, groups * bit + (bit == 1))

time: 45 us -> 45.2 us (level)
  waiting for transfers between devices: 16.9 us -> 16 us
  starting transfers between devices: 16.7 us -> 17.3 us
    ppermute x15, waiting for transfers between devices: 16.9 us -> 16 us  [swap(): return lax.ppermute(value, axis, [(i, i ^ bit) for i in range(size)])]
    ppermute x15, starting transfers between devices: 16.7 us -> 17.3 us  [swap(): return lax.ppermute(value, axis, [(i, i ^ bit) for i in range(size)])]
  transfers between devices with their start and end apart: 15 -> 15, of which waited for: 12 -> 12; matrix products, arithmetic and copies ran while one was open for 0% -> 0% of each run, Pallas kernels for 11% -> 12%
where the time goes in v22:
time: 45.2 us; the launch traced here: 45 us
  starting transfers between devices  17.3 us (38%)
  waiting for transfers between devices  16 us (35%)
  Pallas kernels  10.9 us (24%)
  between operations  0.8 us (2%)
    ppermute x15, starting transfers between devices, swap(): return lax.ppermute(value, axis, [(i, i ^ bit) for i in range(size)])  17.3 us
    ppermute x15, waiting for transfers between devices, swap(): return lax.ppermute(value, axis, [(i, i ^ bit) for i in range(size)])  16 us
    pallas_call x16, Pallas kernels, call(): pl.pallas_call(kernel, out_shape=[jax.ShapeDtypeStruct(*x) for x in outs]...  10.9 us
  transfers between devices with their start and end apart: 15, of which 12 were waited for; matrix products, arithmetic and copies ran while one was open for 0% of the time, Pallas kernels for 12%

profile of v22, /device:TPU:0, one launch (start us, length us, event | category | flops | bytes accessed | tf_op | source)
XLA Modules:
  0.0 45.0 jit_solution(11843957315270824578)
XLA Ops:
  0.6 4.1 %collective-permute-start.1 = (bf16[1,64,128]{2,1,0:T(8,128)(2,1)}, bf16[1,64,128]{2,1,0:T(8,128)(2,1)S(1)}, u32[]{:S(2)}, u32[]{:S(2)}) collective-permute-start(bf16[1,64,128]{2,1,0:T(8,128)(2,1)} %refs_0_.1), channel_id=1, source_target_pairs={{0,8},{4,12},{8,0},{12,4},{1,9},{5,13},{9,1},{13,5},{2,10},{6,14},... | collective-permute-start | bytes 49160 | tf_op jit(solution)/shard_map/ppermute | solution.py:702
  4.7 1.3 %collective-permute-start = (bf16[1,64,128]{2,1,0:T(8,128)(2,1)}, bf16[1,64,128]{2,1,0:T(8,128)(2,1)S(1)}, u32[]{:S(2)}, u32[]{:S(2)}) collective-permute-start(bf16[1,64,128]{2,1,0:T(8,128)(2,1)} %refs_0_.1), channel_id=1, source_target_pairs={{0,12},{4,8},{8,4},{12,0},{1,13},{5,9},{9,5},{13,1},{2,14},{6,10},... | collective-permute-start | bytes 49160 | tf_op jit(solution)/shard_map/ppermute | solution.py:702
  6.4 1.4 %shard_map.87 = (bf16[32,144,256]{2,1,0:T(8,128)(2,1)S(1)}, bf16[32,144,256]{2,1,0:T(8,128)(2,1)S(1)}) custom-call(bf16[288,64,128]{2,1,0:T(8,128)(2,1)S(1)} %copy-done.5, bf16[256,256]{1,0:T(8,128)(2,1)S(1)} %shard_map.86.permutation_ref), custom_call_target="tpu_custom_call" | custom-call | flops 2147483648 | bytes 9568256 | tf_op jit(solution)/shard_map/pallas_call | solution.py:78
  7.9 2.6 %collective-permute-done.refs_1_ = bf16[1,64,128]{2,1,0:T(8,128)(2,1)S(1)} collective-permute-done((bf16[1,64,128]{2,1,0:T(8,128)(2,1)}, bf16[1,64,128]{2,1,0:T(8,128)(2,1)S(1)}, u32[]{:S(2)}, u32[]{:S(2)}) %collective-permute-start) | collective-permute-done | bytes 16416 | tf_op jit(solution)/shard_map/ppermute | solution.py:702
  10.5 0.9 %shard_map.88 = (f32[648,128]{1,0:T(8,128)S(1)}, f32[4,128]{1,0:T(4,128)S(1)}, bf16[32,16,256]{2,1,0:T(8,128)(2,1)S(1)}) custom-call(bf16[1,64,128]{2,1,0:T(8,128)(2,1)S(1)} %copy-done.2, bf16[1,64,128]{2,1,0:T(8,128)(2,1)S(1)} %collective-permute-done.refs_1_, bf16[1,64,128]{2,1,0:T(8,128)(2,1)S(1)} %collective-permute-done.1.refs_2_, ...), custom_call_target="tpu_custom_call" | custom-call | flops 150994944 | bytes 3334144 | tf_op jit(solution)/shard_map/pallas_call | solution.py:78
  11.5 0.4 shard_map.89.prior_term
  12.0 1.1 %shard_map.90 = (f32[2,256,256]{2,1,0:T(8,128)S(1)}, f32[1,256,128]{2,1,0:T(8,128)S(1)}) custom-call(bf16[32,16,256]{2,1,0:T(8,128)(2,1)S(1)} %get-tuple-element.39.left_ref, bf16[32,144,256]{2,1,0:T(8,128)(2,1)S(1)} %get-tuple-element.40.particles, f32[4,128]{1,0:T(4,128)S(1)} %get-tuple-element.41.energy_ref, f32[256,256]{1,0:T(8,128)S(1)} %shard_map.89.prior_term, ...), custom_call_target="tpu_custom_call" | custom-call | flops 301989888 | bytes 4276224 | tf_op jit(solution)/shard_map/pallas_call | solution.py:78
  13.1 0.6 %shard_map.91 = (f32[2,256,256]{2,1,0:T(8,128)S(1)}, f32[1,256,128]{2,1,0:T(8,128)S(1)}, f32[2,256]{1,0:T(2,128)S(1)}, f32[1,128]{1,0:T(1,128)S(1)}, f32[8,256]{1,0:T(8,128)S(1)}) custom-call(f32[2,256,256]{2,1,0:T(8,128)S(1)} %get-tuple-element.42.partial, f32[1,256,128]{2,1,0:T(8,128)S(1)} %get-tuple-element.43.partial_more, ...), custom_call_target="tpu_custom_call" | custom-call | flops 402653184 | bytes 2080768 | tf_op jit(solution)/shard_map/pallas_call | solution.py:78
  13.7 1.6 %collective-permute-start.4 = (f32[8,256]{1,0:T(8,128)S(1)}, f32[8,256]{1,0:T(8,128)S(1)}, u32[]{:S(2)}, u32[]{:S(2)}) collective-permute-start(f32[8,256]{1,0:T(8,128)S(1)} %get-tuple-element.49.first), channel_id=1, source_target_pairs={{0,3},{1,2},{2,1},{3,0},{4,7},{5,6},{6,5},{7,4},{8,11},{9,10},{10,... | collective-permute-start | bytes 24584 | tf_op jit(solution)/shard_map/ppermute | solution.py:702
  15.3 1.5 %collective-permute-done.4.second = f32[8,256]{1,0:T(8,128)S(1)} collective-permute-done((f32[8,256]{1,0:T(8,128)S(1)}, f32[8,256]{1,0:T(8,128)S(1)}, u32[]{:S(2)}, u32[]{:S(2)}) %collective-permute-start.4) | collective-permute-done | bytes 8224 | tf_op jit(solution)/shard_map/ppermute | solution.py:702
  17.2 0.5 %collective-permute-start.5 = (bf16[42,16,128]{2,1,0:T(8,128)(2,1)S(1)}, bf16[42,16,128]{2,1,0:T(8,128)(2,1)S(1)}, u32[]{:S(2)}, u32[]{:S(2)}) collective-permute-start(bf16[42,16,128]{2,1,0:T(8,128)(2,1)S(1)} %get-tuple-element.52.mine), channel_id=1, source_target_pairs={{0,1},{1,0},{2,3},{3,2},{4,5},{5,4},{6,7},{7,6},{8,9},{9,8},{10,11... | collective-permute-start | bytes 516104 | tf_op jit(solution)/shard_map/ppermute | solution.py:702
  17.7 0.7 %shard_map.93.image = f32[576,128]{1,0:T(8,128)S(1)} custom-call(bf16[2,256,256]{2,1,0:T(8,128)(2,1)S(1)} %get-tuple-element.50.rounded_ref, bf16[1,256,128]{2,1,0:T(8,128)(2,1)S(1)} %get-tuple-element.51.rounded_more, bf16[512,512]{1,0:T(8,128)(2,1)S(1)} %copy-done, bf16[32,144,256]{2,1,0:T(8,128)(2,1)S(1)} %get-tuple-element.40.particles), custom_call_target="tpu_custom_call" | custom-call | flops 268435456 | bytes 4096000 | tf_op jit(solution)/shard_map/pallas_call | solution.py:78
  18.7 0.6 %shard_map.94.refs_0_ = bf16[272,128]{1,0:T(8,128)(2,1)S(1)} custom-call(f32[576,128]{1,0:T(8,128)S(1)} %shard_map.93.image, bf16[42,16,128]{2,1,0:T(8,128)(2,1)S(1)} %get-tuple-element.52.mine, bf16[42,16,128]{2,1,0:T(8,128)(2,1)S(1)} %collective-permute-done.5.spectrum, bf16[32,144,256]{2,1,0:T(8,128)(2,1)S(1)} %get-tuple-element.38.refs_5_.particles), custom_call_target="tpu_custom_call" | custom-call | flops 352321536 | bytes 3362816 | tf_op jit(solution)/shard_map/pallas_call | solution.py:78
  19.3 1.3 %collective-permute-start.8 = (bf16[272,128]{1,0:T(8,128)(2,1)S(1)}, bf16[272,128]{1,0:T(8,128)(2,1)S(1)}, u32[]{:S(2)}, u32[]{:S(2)}) collective-permute-start(bf16[272,128]{1,0:T(8,128)(2,1)S(1)} %shard_map.94.refs_0_), channel_id=1, source_target_pairs={{0,8},{4,12},{8,0},{12,4},{1,9},{5,13},{9,1},{13,5},{2,10},{6,14},... | collective-permute-start | bytes 208904 | tf_op jit(solution)/shard_map/ppermute | solution.py:702
  20.6 0.9 %collective-permute-start.7 = (bf16[272,128]{1,0:T(8,128)(2,1)S(1)}, bf16[272,128]{1,0:T(8,128)(2,1)S(1)}, u32[]{:S(2)}, u32[]{:S(2)}) collective-permute-start(bf16[272,128]{1,0:T(8,128)(2,1)S(1)} %shard_map.94.refs_0_), channel_id=1, source_target_pairs={{0,12},{4,8},{8,4},{12,0},{1,13},{5,9},{9,5},{13,1},{2,14},{6,10},... | collective-permute-start | bytes 208904 | tf_op jit(solution)/shard_map/ppermute | solution.py:702
  21.5 1.3 %collective-permute-start.6 = (bf16[272,128]{1,0:T(8,128)(2,1)S(1)}, bf16[272,128]{1,0:T(8,128)(2,1)S(1)}, u32[]{:S(2)}, u32[]{:S(2)}) collective-permute-start(bf16[272,128]{1,0:T(8,128)(2,1)S(1)} %shard_map.94.refs_0_), channel_id=1, source_target_pairs={{0,4},{4,0},{8,12},{12,8},{1,5},{5,1},{9,13},{13,9},{2,6},{6,2},{1... | collective-permute-start | bytes 208904 | tf_op jit(solution)/shard_map/ppermute | solution.py:702
  22.8 4.1 %collective-permute-done.8.refs_3_ = bf16[272,128]{1,0:T(8,128)(2,1)S(1)} collective-permute-done((bf16[272,128]{1,0:T(8,128)(2,1)S(1)}, bf16[272,128]{1,0:T(8,128)(2,1)S(1)}, u32[]{:S(2)}, u32[]{:S(2)}) %collective-permute-start.8) | collective-permute-done | bytes 69664 | tf_op jit(solution)/shard_map/ppermute | solution.py:702
  27.3 1.2 %collective-permute-done.6.refs_1_ = bf16[272,128]{1,0:T(8,128)(2,1)S(1)} collective-permute-done((bf16[272,128]{1,0:T(8,128)(2,1)S(1)}, bf16[272,128]{1,0:T(8,128)(2,1)S(1)}, u32[]{:S(2)}, u32[]{:S(2)}) %collective-permute-start.6) | collective-permute-done | bytes 69664 | tf_op jit(solution)/shard_map/ppermute | solution.py:702
  28.5 0.9 %shard_map.95 = (f32[648,128]{1,0:T(8,128)S(1)}, f32[4,128]{1,0:T(4,128)S(1)}, bf16[32,16,256]{2,1,0:T(8,128)(2,1)S(1)}) custom-call(bf16[272,128]{1,0:T(8,128)(2,1)S(1)} %shard_map.94.refs_0_, bf16[272,128]{1,0:T(8,128)(2,1)S(1)} %collective-permute-done.6.refs_1_, bf16[272,128]{1,0:T(8,128)(2,1)S(1)} %collective-permute-done.7.refs_2_, ...), custom_call_target="tpu_custom_call" | custom-call | flops 150994944 | bytes 3547136 | tf_op jit(solution)/shard_map/pallas_call | solution.py:78
  29.5 1.1 %shard_map.96 = (f32[2,256,256]{2,1,0:T(8,128)S(1)}, f32[1,256,128]{2,1,0:T(8,128)S(1)}) custom-call(bf16[32,16,256]{2,1,0:T(8,128)(2,1)S(1)} %get-tuple-element.53.left_ref, bf16[32,144,256]{2,1,0:T(8,128)(2,1)S(1)} %get-tuple-element.40.particles, f32[4,128]{1,0:T(4,128)S(1)} %get-tuple-element.54.energy_ref, f32[256,256]{1,0:T(8,128)S(1)} %shard_map.89.prior_term, ...), custom_call_target="tpu_custom_call" | custom-call | flops 301989888 | bytes 4276224 | tf_op jit(solution)/shard_map/pallas_call | solution.py:78
  30.6 0.5 %collective-permute-done.9.other = f32[648,128]{1,0:T(8,128)S(1)} collective-permute-done((f32[648,128]{1,0:T(8,128)S(1)}, f32[648,128]{1,0:T(8,128)S(1)}, u32[]{:S(2)}, u32[]{:S(2)}) %collective-permute-start.9) | collective-permute-done | bytes 331808 | tf_op jit(solution)/shard_map/ppermute | solution.py:702
  31.1 0.5 %shard_map.97 = (f32[2,256,256]{2,1,0:T(8,128)S(1)}, f32[1,256,128]{2,1,0:T(8,128)S(1)}, f32[2,256]{1,0:T(2,128)S(1)}, f32[1,128]{1,0:T(1,128)S(1)}, f32[8,256]{1,0:T(8,128)S(1)}) custom-call(f32[2,256,256]{2,1,0:T(8,128)S(1)} %get-tuple-element.55.partial, f32[1,256,128]{2,1,0:T(8,128)S(1)} %get-tuple-element.56.partial_more, ...), custom_call_target="tpu_custom_call" | custom-call | flops 402653184 | bytes 2080768 | tf_op jit(solution)/shard_map/pallas_call | solution.py:78
  31.6 1.3 %collective-permute-start.10 = (f32[8,256]{1,0:T(8,128)S(1)}, f32[8,256]{1,0:T(8,128)S(1)}, u32[]{:S(2)}, u32[]{:S(2)}) collective-permute-start(f32[8,256]{1,0:T(8,128)S(1)} %get-tuple-element.62.first), channel_id=1, source_target_pairs={{0,3},{1,2},{2,1},{3,0},{4,7},{5,6},{6,5},{7,4},{8,11},{9,10},{10,... | collective-permute-start | bytes 24584 | tf_op jit(solution)/shard_map/ppermute | solution.py:702
  32.9 1.8 %collective-permute-done.10.second = f32[8,256]{1,0:T(8,128)S(1)} collective-permute-done((f32[8,256]{1,0:T(8,128)S(1)}, f32[8,256]{1,0:T(8,128)S(1)}, u32[]{:S(2)}, u32[]{:S(2)}) %collective-permute-start.10) | collective-permute-done | bytes 8224 | tf_op jit(solution)/shard_map/ppermute | solution.py:702
  35.3 0.7 %shard_map.99.image = f32[576,128]{1,0:T(8,128)S(1)} custom-call(bf16[2,256,256]{2,1,0:T(8,128)(2,1)S(1)} %get-tuple-element.63.rounded_ref, bf16[1,256,128]{2,1,0:T(8,128)(2,1)S(1)} %get-tuple-element.64.rounded_more, bf16[512,512]{1,0:T(8,128)(2,1)S(1)} %copy-done, bf16[32,144,256]{2,1,0:T(8,128)(2,1)S(1)} %get-tuple-element.40.particles), custom_call_target="tpu_custom_call" | custom-call | flops 268435456 | bytes 4096000 | tf_op jit(solution)/shard_map/pallas_call | solution.py:78
  36.0 0.6 %collective-permute-done.11.spectrum = bf16[42,16,128]{2,1,0:T(8,128)(2,1)S(1)} collective-permute-done((bf16[42,16,128]{2,1,0:T(8,128)(2,1)S(1)}, bf16[42,16,128]{2,1,0:T(8,128)(2,1)S(1)}, u32[]{:S(2)}, u32[]{:S(2)}) %collective-permute-start.11) | collective-permute-done | bytes 172064 | tf_op jit(solution)/shard_map/ppermute | solution.py:702
  36.6 0.6 %shard_map.100 = (f32[72,128]{1,0:T(8,128)S(1)}, f32[72,128]{1,0:T(8,128)S(1)}, f32[72,128]{1,0:T(8,128)S(1)}, f32[72,128]{1,0:T(8,128)S(1)}, f32[1,144]{1,0:T(1,128)S(1)}) custom-call(f32[576,128]{1,0:T(8,128)S(1)} %shard_map.99.image, bf16[42,16,128]{2,1,0:T(8,128)(2,1)S(1)} %get-tuple-element.65.mine, ...), custom_call_target="tpu_custom_call" | custom-call | flops 352321536 | bytes 3473408 | tf_op jit(solution)/shard_map/pallas_call | solution.py:78
  37.2 2.4 %collective-permute-start.12 = (f32[72,128]{1,0:T(8,128)S(1)}, f32[72,128]{1,0:T(8,128)S(1)}, u32[]{:S(2)}, u32[]{:S(2)}) collective-permute-start(f32[72,128]{1,0:T(8,128)S(1)} %get-tuple-element.66), channel_id=1, source_target_pairs={{0,12},{4,8},{8,4},{12,0},{1,13},{5,9},{9,5},{13,1},{2,14},{6,10},... | collective-permute-start | bytes 110600 | tf_op jit(solution)/shard_map/ppermute | solution.py:702
  39.5 2.0 %collective-permute-start.14 = (f32[72,128]{1,0:T(8,128)S(1)}, f32[72,128]{1,0:T(8,128)S(1)}, u32[]{:S(2)}, u32[]{:S(2)}) collective-permute-start(f32[72,128]{1,0:T(8,128)S(1)} %get-tuple-element.68), channel_id=1, source_target_pairs={{0,4},{4,0},{8,12},{12,8},{1,5},{5,1},{9,13},{13,9},{2,6},{6,2},{1... | collective-permute-start | bytes 110600 | tf_op jit(solution)/shard_map/ppermute | solution.py:702
  41.6 1.6 %collective-permute-done.12.refs_0_ = f32[72,128]{1,0:T(8,128)S(1)} collective-permute-done((f32[72,128]{1,0:T(8,128)S(1)}, f32[72,128]{1,0:T(8,128)S(1)}, u32[]{:S(2)}, u32[]{:S(2)}) %collective-permute-start.12) | collective-permute-done | bytes 36896 | tf_op jit(solution)/shard_map/ppermute | solution.py:702
  43.2 1.2 %collective-permute-done.13.refs_1_ = f32[72,128]{1,0:T(8,128)S(1)} collective-permute-done((f32[72,128]{1,0:T(8,128)S(1)}, f32[72,128]{1,0:T(8,128)S(1)}, u32[]{:S(2)}, u32[]{:S(2)}) %collective-permute-start.13) | collective-permute-done | bytes 36896 | tf_op jit(solution)/shard_map/ppermute | solution.py:702
  44.4 0.6 %shard_map.101 = (f32[1,64,128]{2,1,0:T(8,128)}, f32[1,144]{1,0:T(1,128)}) custom-call(f32[72,128]{1,0:T(8,128)S(1)} %collective-permute-done.12.refs_0_, f32[72,128]{1,0:T(8,128)S(1)} %collective-permute-done.13.refs_1_, f32[72,128]{1,0:T(8,128)S(1)} %collective-permute-done.14.refs_2_, f32[72,128]{1,0:T(8,128)S(1)} %get-tuple-element.69.refs_3_, ...), custom_call_target="tpu_custom_call" | custom-call | bytes 245760 | tf_op jit(solution)/shard_map/pallas_call | solution.py:78
  (28 shorter events, 2.2 us)
Async XLA Ops:
  0.6 5.7 %copy-start.5 = (bf16[288,64,128]{2,1,0:T(8,128)(2,1)S(1)}, bf16[288,64,128]{2,1,0:T(8,128)(2,1)}, u32[]{:S(2)}) copy-start(bf16[288,64,128]{2,1,0:T(8,128)(2,1)} %particles_ref.1) | copy-start | bytes 14155780
  0.6 7.2 %collective-permute-start.1 = (bf16[1,64,128]{2,1,0:T(8,128)(2,1)}, bf16[1,64,128]{2,1,0:T(8,128)(2,1)S(1)}, u32[]{:S(2)}, u32[]{:S(2)}) collective-permute-start(bf16[1,64,128]{2,1,0:T(8,128)(2,1)} %refs_0_.1), channel_id=1, source_target_pairs={{0,8},{4,12},{8,0},{12,4},{1,9},{5,13},{9,1},{13,5},{2,10},{6,14},... | collective-permute-start | bytes 49160 | tf_op jit(solution)/shard_map/ppermute | solution.py:702
  4.7 5.7 %collective-permute-start = (bf16[1,64,128]{2,1,0:T(8,128)(2,1)}, bf16[1,64,128]{2,1,0:T(8,128)(2,1)S(1)}, u32[]{:S(2)}, u32[]{:S(2)}) collective-permute-start(bf16[1,64,128]{2,1,0:T(8,128)(2,1)} %refs_0_.1), channel_id=1, source_target_pairs={{0,12},{4,8},{8,4},{12,0},{1,13},{5,9},{9,5},{13,1},{2,14},{6,10},... | collective-permute-start | bytes 49160 | tf_op jit(solution)/shard_map/ppermute | solution.py:702
  6.1 4.4 %collective-permute-start.2 = (bf16[1,64,128]{2,1,0:T(8,128)(2,1)}, bf16[1,64,128]{2,1,0:T(8,128)(2,1)S(1)}, u32[]{:S(2)}, u32[]{:S(2)}) collective-permute-start(bf16[1,64,128]{2,1,0:T(8,128)(2,1)} %refs_0_.1), channel_id=1, source_target_pairs={{0,4},{4,0},{8,12},{12,8},{1,5},{5,1},{9,13},{13,9},{2,6},{6,2},{1... | collective-permute-start | bytes 49160 | tf_op jit(solution)/shard_map/ppermute | solution.py:702
  6.4 4.1 %copy-start.2 = (bf16[1,64,128]{2,1,0:T(8,128)(2,1)S(1)}, bf16[1,64,128]{2,1,0:T(8,128)(2,1)}, u32[]{:S(2)}) copy-start(bf16[1,64,128]{2,1,0:T(8,128)(2,1)} %refs_0_.1) | copy-start | bytes 49156
  6.4 4.1 %copy-start.4 = (f32[64]{0:T(128)S(1)}, f32[64]{0:T(128)}, u32[]{:S(2)}) copy-start(f32[64]{0:T(128)} %param.9) | copy-start | bytes 772
  7.8 3.7 %copy-start.3 = (s32[288]{0:T(512)S(1)}, s32[288]{0:T(512)}, u32[]{:S(2)}) copy-start(s32[288]{0:T(512)} %prior_ref.1) | copy-start | bytes 3460
  7.8 4.1 %copy-start.1 = (bf16[512,384]{1,0:T(8,128)(2,1)S(1)}, bf16[512,384]{1,0:T(8,128)(2,1)}, u32[]{:S(2)}) copy-start(bf16[512,384]{1,0:T(8,128)(2,1)} %constant.6.clone.table) | copy-start | bytes 1179652
  11.4 1.7 %copy-start.6 = (bf16[512,384]{1,0:T(8,128)(2,1)S(1)}, bf16[512,384]{1,0:T(8,128)(2,1)}, u32[]{:S(2)}) copy-start(bf16[512,384]{1,0:T(8,128)(2,1)} %constant.7.clone.table) | copy-start | bytes 1179652
  11.4 1.7 %collective-permute-start.3 = (f32[648,128]{1,0:T(8,128)S(1)}, f32[648,128]{1,0:T(8,128)S(1)}, u32[]{:S(2)}, u32[]{:S(2)}) collective-permute-start(f32[648,128]{1,0:T(8,128)S(1)} %get-tuple-element.44), channel_id=1, source_target_pairs={{0,1},{1,0},{2,3},{3,2},{4,5},{5,4},{6,7},{7,6},{8,9},{9,8},{10,11... | collective-permute-start | bytes 995336 | tf_op jit(solution)/shard_map/ppermute | solution.py:702
  12.0 4.8 %copy-start = (bf16[512,512]{1,0:T(8,128)(2,1)S(1)}, bf16[512,512]{1,0:T(8,128)(2,1)}, u32[]{:S(2)}) copy-start(bf16[512,512]{1,0:T(8,128)(2,1)} %constant.8.clone.forward) | copy-start | bytes 1572868
  13.7 3.1 %collective-permute-start.4 = (f32[8,256]{1,0:T(8,128)S(1)}, f32[8,256]{1,0:T(8,128)S(1)}, u32[]{:S(2)}, u32[]{:S(2)}) collective-permute-start(f32[8,256]{1,0:T(8,128)S(1)} %get-tuple-element.49.first), channel_id=1, source_target_pairs={{0,3},{1,2},{2,1},{3,0},{4,7},{5,6},{6,5},{7,4},{8,11},{9,10},{10,... | collective-permute-start | bytes 24584 | tf_op jit(solution)/shard_map/ppermute | solution.py:702
  17.2 1.6 %collective-permute-start.5 = (bf16[42,16,128]{2,1,0:T(8,128)(2,1)S(1)}, bf16[42,16,128]{2,1,0:T(8,128)(2,1)S(1)}, u32[]{:S(2)}, u32[]{:S(2)}) collective-permute-start(bf16[42,16,128]{2,1,0:T(8,128)(2,1)S(1)} %get-tuple-element.52.mine), channel_id=1, source_target_pairs={{0,1},{1,0},{2,3},{3,2},{4,5},{5,4},{6,7},{7,6},{8,9},{9,8},{10,11... | collective-permute-start | bytes 516104 | tf_op jit(solution)/shard_map/ppermute | solution.py:702
  19.3 7.6 %collective-permute-start.8 = (bf16[272,128]{1,0:T(8,128)(2,1)S(1)}, bf16[272,128]{1,0:T(8,128)(2,1)S(1)}, u32[]{:S(2)}, u32[]{:S(2)}) collective-permute-start(bf16[272,128]{1,0:T(8,128)(2,1)S(1)} %shard_map.94.refs_0_), channel_id=1, source_target_pairs={{0,8},{4,12},{8,0},{12,4},{1,9},{5,13},{9,1},{13,5},{2,10},{6,14},... | collective-permute-start | bytes 208904 | tf_op jit(solution)/shard_map/ppermute | solution.py:702
  20.6 6.7 %collective-permute-start.7 = (bf16[272,128]{1,0:T(8,128)(2,1)S(1)}, bf16[272,128]{1,0:T(8,128)(2,1)S(1)}, u32[]{:S(2)}, u32[]{:S(2)}) collective-permute-start(bf16[272,128]{1,0:T(8,128)(2,1)S(1)} %shard_map.94.refs_0_), channel_id=1, source_target_pairs={{0,12},{4,8},{8,4},{12,0},{1,13},{5,9},{9,5},{13,1},{2,14},{6,10},... | collective-permute-start | bytes 208904 | tf_op jit(solution)/shard_map/ppermute | solution.py:702
  21.5 7.0 %collective-permute-start.6 = (bf16[272,128]{1,0:T(8,128)(2,1)S(1)}, bf16[272,128]{1,0:T(8,128)(2,1)S(1)}, u32[]{:S(2)}, u32[]{:S(2)}) collective-permute-start(bf16[272,128]{1,0:T(8,128)(2,1)S(1)} %shard_map.94.refs_0_), channel_id=1, source_target_pairs={{0,4},{4,0},{8,12},{12,8},{1,5},{5,1},{9,13},{13,9},{2,6},{6,2},{1... | collective-permute-start | bytes 208904 | tf_op jit(solution)/shard_map/ppermute | solution.py:702
  29.4 1.6 %collective-permute-start.9 = (f32[648,128]{1,0:T(8,128)S(1)}, f32[648,128]{1,0:T(8,128)S(1)}, u32[]{:S(2)}, u32[]{:S(2)}) collective-permute-start(f32[648,128]{1,0:T(8,128)S(1)} %get-tuple-element.57), channel_id=1, source_target_pairs={{0,1},{1,0},{2,3},{3,2},{4,5},{5,4},{6,7},{7,6},{8,9},{9,8},{10,11... | collective-permute-start | bytes 995336 | tf_op jit(solution)/shard_map/ppermute | solution.py:702
  31.6 3.1 %collective-permute-start.10 = (f32[8,256]{1,0:T(8,128)S(1)}, f32[8,256]{1,0:T(8,128)S(1)}, u32[]{:S(2)}, u32[]{:S(2)}) collective-permute-start(f32[8,256]{1,0:T(8,128)S(1)} %get-tuple-element.62.first), channel_id=1, source_target_pairs={{0,3},{1,2},{2,1},{3,0},{4,7},{5,6},{6,5},{7,4},{8,11},{9,10},{10,... | collective-permute-start | bytes 24584 | tf_op jit(solution)/shard_map/ppermute | solution.py:702
  35.1 1.5 %collective-permute-start.11 = (bf16[42,16,128]{2,1,0:T(8,128)(2,1)S(1)}, bf16[42,16,128]{2,1,0:T(8,128)(2,1)S(1)}, u32[]{:S(2)}, u32[]{:S(2)}) collective-permute-start(bf16[42,16,128]{2,1,0:T(8,128)(2,1)S(1)} %get-tuple-element.65.mine), channel_id=1, source_target_pairs={{0,1},{1,0},{2,3},{3,2},{4,5},{5,4},{6,7},{7,6},{8,9},{9,8},{10,11... | collective-permute-start | bytes 516104 | tf_op jit(solution)/shard_map/ppermute | solution.py:702
  37.2 6.0 %collective-permute-start.12 = (f32[72,128]{1,0:T(8,128)S(1)}, f32[72,128]{1,0:T(8,128)S(1)}, u32[]{:S(2)}, u32[]{:S(2)}) collective-permute-start(f32[72,128]{1,0:T(8,128)S(1)} %get-tuple-element.66), channel_id=1, source_target_pairs={{0,12},{4,8},{8,4},{12,0},{1,13},{5,9},{9,5},{13,1},{2,14},{6,10},... | collective-permute-start | bytes 110600 | tf_op jit(solution)/shard_map/ppermute | solution.py:702
  39.5 4.9 %collective-permute-start.13 = (f32[72,128]{1,0:T(8,128)S(1)}, f32[72,128]{1,0:T(8,128)S(1)}, u32[]{:S(2)}, u32[]{:S(2)}) collective-permute-start(f32[72,128]{1,0:T(8,128)S(1)} %get-tuple-element.67), channel_id=1, source_target_pairs={{0,8},{4,12},{8,0},{12,4},{1,9},{5,13},{9,1},{13,5},{2,10},{6,14},... | collective-permute-start | bytes 110600 | tf_op jit(solution)/shard_map/ppermute | solution.py:702
  39.5 4.9 %collective-permute-start.14 = (f32[72,128]{1,0:T(8,128)S(1)}, f32[72,128]{1,0:T(8,128)S(1)}, u32[]{:S(2)}, u32[]{:S(2)}) collective-permute-start(f32[72,128]{1,0:T(8,128)S(1)} %get-tuple-element.68), channel_id=1, source_target_pairs={{0,4},{4,0},{8,12},{12,8},{1,5},{5,1},{9,13},{13,9},{2,6},{6,2},{1... | collective-permute-start | bytes 110600 | tf_op jit(solution)/shard_map/ppermute | solution.py:702

commit v23 on v22

--- a/solution.py
+++ b/solution.py
@@ -129,9 +129,10 @@
     return width, bundle, classes // bundle
 
 
-def prep_kernel(share, particles_ref, permutation_ref, other, own):
+def prep_kernel(share, particles_ref, permutation_ref, prior_ref, other, own, prior_term):
     freqs, depth = particles_ref.shape[1:]
     half = half_index()
+    prior_kernel(share, prior_ref, prior_term)
     permutation = permutation_ref[...]
     for out, first in ((other, (1 - half) * share), (own, half * share)):
         for p in range(0, share, 16):
@@ -152,13 +153,13 @@
                         ]
 
 
-def prep(particles, permutation, share):
+def prep(particles, permutation, prior_rot, share):
     _, freqs, depth = particles.shape
     assert share % 16 == 0 and freqs % 32 == 0
     return call(
         functools.partial(prep_kernel, share),
-        [particles, permutation],
-        [((freqs // 2, share, 2 * depth), BF16)] * 2,
+        [particles, permutation, prior_rot],
+        [((freqs // 2, share, 2 * depth), BF16)] * 2 + [((ANG, 256), F32)],
         flops=1 << 31,
     )
 
@@ -720,11 +721,8 @@
     turns = sorted(range(1, blocks), key=lambda i: (-i.bit_length(), i))
 
     (permutation,) = call(permutation_kernel, [], [((256, 256), BF16)], flops=1 << 32)
-    (prior_term,) = call(
-        functools.partial(prior_kernel, share), [prior_rot], [((ANG, 256), F32)], flops=1 << 26
-    )
     sources = {i: swap(references, "blk", blocks, i) for i in (*turns, 0)}
-    other_images, own_images = prep(particles, permutation, share)
+    other_images, own_images, prior_term = prep(particles, permutation, prior_rot, share)
     for step in range(ITERS):
         last = step == ITERS - 1
         order = [0, *(reversed(turns) if step else reversed(range(1, blocks)))]

time: 45.2 us -> 44.8 us (level)
  waiting for transfers between devices: 16 us -> 16.8 us
  starting transfers between devices: 17.3 us -> 16.6 us
    ppermute x15, waiting for transfers between devices: 16 us -> 16.8 us  [swap(): return lax.ppermute(value, axis, [(i, i ^ bit) for i in range(size)])]
    ppermute x15, starting transfers between devices: 17.3 us -> 16.6 us  [swap(): return lax.ppermute(value, axis, [(i, i ^ bit) for i in range(size)])]
    pallas_call x16 -> x15, Pallas kernels: 10.9 us -> 10.5 us  [call(): pl.pallas_call(kernel, out_shape=[jax.ShapeDtypeStruct(*x) for x in outs]...]
  transfers between devices with their start and end apart: 15 -> 15, of which waited for: 12 -> 12; matrix products, arithmetic and copies ran while one was open for 0% -> 0% of each run, Pallas kernels for 12% -> 11%
where the time goes in v23:
time: 44.8 us; the launch traced here: 44.7 us
  waiting for transfers between devices  16.8 us (38%)
  starting transfers between devices  16.6 us (37%)
  Pallas kernels  10.5 us (23%)
  between operations  0.8 us (2%)
    ppermute x15, waiting for transfers between devices, swap(): return lax.ppermute(value, axis, [(i, i ^ bit) for i in range(size)])  16.8 us
    ppermute x15, starting transfers between devices, swap(): return lax.ppermute(value, axis, [(i, i ^ bit) for i in range(size)])  16.6 us
    pallas_call x15, Pallas kernels, call(): pl.pallas_call(kernel, out_shape=[jax.ShapeDtypeStruct(*x) for x in outs]...  10.5 us
  transfers between devices with their start and end apart: 15, of which 12 were waited for; matrix products, arithmetic and copies ran while one was open for 0% of the time, Pallas kernels for 11%

profile of v23, /device:TPU:0, one launch (start us, length us, event | category | flops | bytes accessed | tf_op | source)
XLA Modules:
  0.0 44.7 jit_solution(5542312160355099291)
XLA Ops:
  0.6 4.1 %collective-permute-start.1 = (bf16[1,64,128]{2,1,0:T(8,128)(2,1)}, bf16[1,64,128]{2,1,0:T(8,128)(2,1)S(1)}, u32[]{:S(2)}, u32[]{:S(2)}) collective-permute-start(bf16[1,64,128]{2,1,0:T(8,128)(2,1)} %refs_0_.1), channel_id=1, source_target_pairs={{0,8},{4,12},{8,0},{12,4},{1,9},{5,13},{9,1},{13,5},{2,10},{6,14},... | collective-permute-start | bytes 49160 | tf_op jit(solution)/shard_map/ppermute | solution.py:703
  4.8 1.3 %collective-permute-start = (bf16[1,64,128]{2,1,0:T(8,128)(2,1)}, bf16[1,64,128]{2,1,0:T(8,128)(2,1)S(1)}, u32[]{:S(2)}, u32[]{:S(2)}) collective-permute-start(bf16[1,64,128]{2,1,0:T(8,128)(2,1)} %refs_0_.1), channel_id=1, source_target_pairs={{0,12},{4,8},{8,4},{12,0},{1,13},{5,9},{9,5},{13,1},{2,14},{6,10},... | collective-permute-start | bytes 49160 | tf_op jit(solution)/shard_map/ppermute | solution.py:703
  6.4 1.4 %shard_map.87 = (bf16[32,144,256]{2,1,0:T(8,128)(2,1)S(1)}, bf16[32,144,256]{2,1,0:T(8,128)(2,1)S(1)}, f32[256,256]{1,0:T(8,128)S(1)}) custom-call(bf16[288,64,128]{2,1,0:T(8,128)(2,1)S(1)} %copy-done.4, bf16[256,256]{1,0:T(8,128)(2,1)S(1)} %shard_map.86.permutation_ref, s32[288]{0:T(512)S(1)} %copy-done.5), custom_call_target="tpu_custom_call" | custom-call | flops 2147483648 | bytes 9854976 | tf_op jit(solution)/shard_map/pallas_call | solution.py:78
  7.9 2.6 %collective-permute-done.refs_1_ = bf16[1,64,128]{2,1,0:T(8,128)(2,1)S(1)} collective-permute-done((bf16[1,64,128]{2,1,0:T(8,128)(2,1)}, bf16[1,64,128]{2,1,0:T(8,128)(2,1)S(1)}, u32[]{:S(2)}, u32[]{:S(2)}) %collective-permute-start) | collective-permute-done | bytes 16416 | tf_op jit(solution)/shard_map/ppermute | solution.py:703
  10.5 0.9 %shard_map.88 = (f32[648,128]{1,0:T(8,128)S(1)}, f32[4,128]{1,0:T(4,128)S(1)}, bf16[32,16,256]{2,1,0:T(8,128)(2,1)S(1)}) custom-call(bf16[1,64,128]{2,1,0:T(8,128)(2,1)S(1)} %copy-done.2, bf16[1,64,128]{2,1,0:T(8,128)(2,1)S(1)} %collective-permute-done.refs_1_, bf16[1,64,128]{2,1,0:T(8,128)(2,1)S(1)} %collective-permute-done.1.refs_2_, ...), custom_call_target="tpu_custom_call" | custom-call | flops 150994944 | bytes 3334144 | tf_op jit(solution)/shard_map/pallas_call | solution.py:78
  11.5 1.1 %shard_map.89 = (f32[2,256,256]{2,1,0:T(8,128)S(1)}, f32[1,256,128]{2,1,0:T(8,128)S(1)}) custom-call(bf16[32,16,256]{2,1,0:T(8,128)(2,1)S(1)} %get-tuple-element.40.left_ref, bf16[32,144,256]{2,1,0:T(8,128)(2,1)S(1)} %get-tuple-element.41.particles, f32[4,128]{1,0:T(4,128)S(1)} %get-tuple-element.42.energy_ref, f32[256,256]{1,0:T(8,128)S(1)} %get-tuple-element.43.prior_term, ...), custom_call_target="tpu_custom_call" | custom-call | flops 301989888 | bytes 4276224 | tf_op jit(solution)/shard_map/pallas_call | solution.py:78
  13.1 0.6 %shard_map.90 = (f32[2,256,256]{2,1,0:T(8,128)S(1)}, f32[1,256,128]{2,1,0:T(8,128)S(1)}, f32[2,256]{1,0:T(2,128)S(1)}, f32[1,128]{1,0:T(1,128)S(1)}, f32[8,256]{1,0:T(8,128)S(1)}) custom-call(f32[2,256,256]{2,1,0:T(8,128)S(1)} %get-tuple-element.44.partial, f32[1,256,128]{2,1,0:T(8,128)S(1)} %get-tuple-element.45.partial_more, ...), custom_call_target="tpu_custom_call" | custom-call | flops 402653184 | bytes 2080768 | tf_op jit(solution)/shard_map/pallas_call | solution.py:78
  13.7 1.3 %collective-permute-start.4 = (f32[8,256]{1,0:T(8,128)S(1)}, f32[8,256]{1,0:T(8,128)S(1)}, u32[]{:S(2)}, u32[]{:S(2)}) collective-permute-start(f32[8,256]{1,0:T(8,128)S(1)} %get-tuple-element.51.first), channel_id=1, source_target_pairs={{0,3},{1,2},{2,1},{3,0},{4,7},{5,6},{6,5},{7,4},{8,11},{9,10},{10,... | collective-permute-start | bytes 24584 | tf_op jit(solution)/shard_map/ppermute | solution.py:703
  14.9 1.8 %collective-permute-done.4.second = f32[8,256]{1,0:T(8,128)S(1)} collective-permute-done((f32[8,256]{1,0:T(8,128)S(1)}, f32[8,256]{1,0:T(8,128)S(1)}, u32[]{:S(2)}, u32[]{:S(2)}) %collective-permute-start.4) | collective-permute-done | bytes 8224 | tf_op jit(solution)/shard_map/ppermute | solution.py:703
  17.4 0.7 %shard_map.92.image = f32[576,128]{1,0:T(8,128)S(1)} custom-call(bf16[2,256,256]{2,1,0:T(8,128)(2,1)S(1)} %get-tuple-element.52.rounded_ref, bf16[1,256,128]{2,1,0:T(8,128)(2,1)S(1)} %get-tuple-element.53.rounded_more, bf16[512,512]{1,0:T(8,128)(2,1)S(1)} %copy-done, bf16[32,144,256]{2,1,0:T(8,128)(2,1)S(1)} %get-tuple-element.41.particles), custom_call_target="tpu_custom_call" | custom-call | flops 268435456 | bytes 4096000 | tf_op jit(solution)/shard_map/pallas_call | solution.py:78
  18.0 0.6 %collective-permute-done.5.spectrum = bf16[42,16,128]{2,1,0:T(8,128)(2,1)S(1)} collective-permute-done((bf16[42,16,128]{2,1,0:T(8,128)(2,1)S(1)}, bf16[42,16,128]{2,1,0:T(8,128)(2,1)S(1)}, u32[]{:S(2)}, u32[]{:S(2)}) %collective-permute-start.5) | collective-permute-done | bytes 172064 | tf_op jit(solution)/shard_map/ppermute | solution.py:703
  18.6 0.6 %shard_map.93.refs_0_ = bf16[272,128]{1,0:T(8,128)(2,1)S(1)} custom-call(f32[576,128]{1,0:T(8,128)S(1)} %shard_map.92.image, bf16[42,16,128]{2,1,0:T(8,128)(2,1)S(1)} %get-tuple-element.54.mine, bf16[42,16,128]{2,1,0:T(8,128)(2,1)S(1)} %collective-permute-done.5.spectrum, bf16[32,144,256]{2,1,0:T(8,128)(2,1)S(1)} %get-tuple-element.39.refs_5_.particles), custom_call_target="tpu_custom_call" | custom-call | flops 352321536 | bytes 3362816 | tf_op jit(solution)/shard_map/pallas_call | solution.py:78
  19.2 1.3 %collective-permute-start.8 = (bf16[272,128]{1,0:T(8,128)(2,1)S(1)}, bf16[272,128]{1,0:T(8,128)(2,1)S(1)}, u32[]{:S(2)}, u32[]{:S(2)}) collective-permute-start(bf16[272,128]{1,0:T(8,128)(2,1)S(1)} %shard_map.93.refs_0_), channel_id=1, source_target_pairs={{0,8},{4,12},{8,0},{12,4},{1,9},{5,13},{9,1},{13,5},{2,10},{6,14},... | collective-permute-start | bytes 208904 | tf_op jit(solution)/shard_map/ppermute | solution.py:703
  20.5 0.9 %collective-permute-start.7 = (bf16[272,128]{1,0:T(8,128)(2,1)S(1)}, bf16[272,128]{1,0:T(8,128)(2,1)S(1)}, u32[]{:S(2)}, u32[]{:S(2)}) collective-permute-start(bf16[272,128]{1,0:T(8,128)(2,1)S(1)} %shard_map.93.refs_0_), channel_id=1, source_target_pairs={{0,12},{4,8},{8,4},{12,0},{1,13},{5,9},{9,5},{13,1},{2,14},{6,10},... | collective-permute-start | bytes 208904 | tf_op jit(solution)/shard_map/ppermute | solution.py:703
  21.4 1.4 %collective-permute-start.6 = (bf16[272,128]{1,0:T(8,128)(2,1)S(1)}, bf16[272,128]{1,0:T(8,128)(2,1)S(1)}, u32[]{:S(2)}, u32[]{:S(2)}) collective-permute-start(bf16[272,128]{1,0:T(8,128)(2,1)S(1)} %shard_map.93.refs_0_), channel_id=1, source_target_pairs={{0,4},{4,0},{8,12},{12,8},{1,5},{5,1},{9,13},{13,9},{2,6},{6,2},{1... | collective-permute-start | bytes 208904 | tf_op jit(solution)/shard_map/ppermute | solution.py:703
  22.7 3.6 %collective-permute-done.8.refs_3_ = bf16[272,128]{1,0:T(8,128)(2,1)S(1)} collective-permute-done((bf16[272,128]{1,0:T(8,128)(2,1)S(1)}, bf16[272,128]{1,0:T(8,128)(2,1)S(1)}, u32[]{:S(2)}, u32[]{:S(2)}) %collective-permute-start.8) | collective-permute-done | bytes 69664 | tf_op jit(solution)/shard_map/ppermute | solution.py:703
  26.4 0.6 %collective-permute-done.7.refs_2_ = bf16[272,128]{1,0:T(8,128)(2,1)S(1)} collective-permute-done((bf16[272,128]{1,0:T(8,128)(2,1)S(1)}, bf16[272,128]{1,0:T(8,128)(2,1)S(1)}, u32[]{:S(2)}, u32[]{:S(2)}) %collective-permute-start.7) | collective-permute-done | bytes 69664 | tf_op jit(solution)/shard_map/ppermute | solution.py:703
  27.0 1.2 %collective-permute-done.6.refs_1_ = bf16[272,128]{1,0:T(8,128)(2,1)S(1)} collective-permute-done((bf16[272,128]{1,0:T(8,128)(2,1)S(1)}, bf16[272,128]{1,0:T(8,128)(2,1)S(1)}, u32[]{:S(2)}, u32[]{:S(2)}) %collective-permute-start.6) | collective-permute-done | bytes 69664 | tf_op jit(solution)/shard_map/ppermute | solution.py:703
  28.2 0.9 %shard_map.94 = (f32[648,128]{1,0:T(8,128)S(1)}, f32[4,128]{1,0:T(4,128)S(1)}, bf16[32,16,256]{2,1,0:T(8,128)(2,1)S(1)}) custom-call(bf16[272,128]{1,0:T(8,128)(2,1)S(1)} %shard_map.93.refs_0_, bf16[272,128]{1,0:T(8,128)(2,1)S(1)} %collective-permute-done.6.refs_1_, bf16[272,128]{1,0:T(8,128)(2,1)S(1)} %collective-permute-done.7.refs_2_, ...), custom_call_target="tpu_custom_call" | custom-call | flops 150994944 | bytes 3547136 | tf_op jit(solution)/shard_map/pallas_call | solution.py:78
  29.1 1.1 %shard_map.95 = (f32[2,256,256]{2,1,0:T(8,128)S(1)}, f32[1,256,128]{2,1,0:T(8,128)S(1)}) custom-call(bf16[32,16,256]{2,1,0:T(8,128)(2,1)S(1)} %get-tuple-element.55.left_ref, bf16[32,144,256]{2,1,0:T(8,128)(2,1)S(1)} %get-tuple-element.41.particles, f32[4,128]{1,0:T(4,128)S(1)} %get-tuple-element.56.energy_ref, f32[256,256]{1,0:T(8,128)S(1)} %get-tuple-element.43.prior_term, ...), custom_call_target="tpu_custom_call" | custom-call | flops 301989888 | bytes 4276224 | tf_op jit(solution)/shard_map/pallas_call | solution.py:78
  30.2 0.5 %collective-permute-done.9.other = f32[648,128]{1,0:T(8,128)S(1)} collective-permute-done((f32[648,128]{1,0:T(8,128)S(1)}, f32[648,128]{1,0:T(8,128)S(1)}, u32[]{:S(2)}, u32[]{:S(2)}) %collective-permute-start.9) | collective-permute-done | bytes 331808 | tf_op jit(solution)/shard_map/ppermute | solution.py:703
  30.7 0.5 %shard_map.96 = (f32[2,256,256]{2,1,0:T(8,128)S(1)}, f32[1,256,128]{2,1,0:T(8,128)S(1)}, f32[2,256]{1,0:T(2,128)S(1)}, f32[1,128]{1,0:T(1,128)S(1)}, f32[8,256]{1,0:T(8,128)S(1)}) custom-call(f32[2,256,256]{2,1,0:T(8,128)S(1)} %get-tuple-element.57.partial, f32[1,256,128]{2,1,0:T(8,128)S(1)} %get-tuple-element.58.partial_more, ...), custom_call_target="tpu_custom_call" | custom-call | flops 402653184 | bytes 2080768 | tf_op jit(solution)/shard_map/pallas_call | solution.py:78
  31.3 1.3 %collective-permute-start.10 = (f32[8,256]{1,0:T(8,128)S(1)}, f32[8,256]{1,0:T(8,128)S(1)}, u32[]{:S(2)}, u32[]{:S(2)}) collective-permute-start(f32[8,256]{1,0:T(8,128)S(1)} %get-tuple-element.64.first), channel_id=1, source_target_pairs={{0,3},{1,2},{2,1},{3,0},{4,7},{5,6},{6,5},{7,4},{8,11},{9,10},{10,... | collective-permute-start | bytes 24584 | tf_op jit(solution)/shard_map/ppermute | solution.py:703
  32.6 1.8 %collective-permute-done.10.second = f32[8,256]{1,0:T(8,128)S(1)} collective-permute-done((f32[8,256]{1,0:T(8,128)S(1)}, f32[8,256]{1,0:T(8,128)S(1)}, u32[]{:S(2)}, u32[]{:S(2)}) %collective-permute-start.10) | collective-permute-done | bytes 8224 | tf_op jit(solution)/shard_map/ppermute | solution.py:703
  35.0 0.7 %shard_map.98.image = f32[576,128]{1,0:T(8,128)S(1)} custom-call(bf16[2,256,256]{2,1,0:T(8,128)(2,1)S(1)} %get-tuple-element.65.rounded_ref, bf16[1,256,128]{2,1,0:T(8,128)(2,1)S(1)} %get-tuple-element.66.rounded_more, bf16[512,512]{1,0:T(8,128)(2,1)S(1)} %copy-done, bf16[32,144,256]{2,1,0:T(8,128)(2,1)S(1)} %get-tuple-element.41.particles), custom_call_target="tpu_custom_call" | custom-call | flops 268435456 | bytes 4096000 | tf_op jit(solution)/shard_map/pallas_call | solution.py:78
  35.7 0.6 %collective-permute-done.11.spectrum = bf16[42,16,128]{2,1,0:T(8,128)(2,1)S(1)} collective-permute-done((bf16[42,16,128]{2,1,0:T(8,128)(2,1)S(1)}, bf16[42,16,128]{2,1,0:T(8,128)(2,1)S(1)}, u32[]{:S(2)}, u32[]{:S(2)}) %collective-permute-start.11) | collective-permute-done | bytes 172064 | tf_op jit(solution)/shard_map/ppermute | solution.py:703
  36.3 0.6 %shard_map.99 = (f32[72,128]{1,0:T(8,128)S(1)}, f32[72,128]{1,0:T(8,128)S(1)}, f32[72,128]{1,0:T(8,128)S(1)}, f32[72,128]{1,0:T(8,128)S(1)}, f32[1,144]{1,0:T(1,128)S(1)}) custom-call(f32[576,128]{1,0:T(8,128)S(1)} %shard_map.98.image, bf16[42,16,128]{2,1,0:T(8,128)(2,1)S(1)} %get-tuple-element.67.mine, ...), custom_call_target="tpu_custom_call" | custom-call | flops 352321536 | bytes 3473408 | tf_op jit(solution)/shard_map/pallas_call | solution.py:78
  36.8 2.3 %collective-permute-start.12 = (f32[72,128]{1,0:T(8,128)S(1)}, f32[72,128]{1,0:T(8,128)S(1)}, u32[]{:S(2)}, u32[]{:S(2)}) collective-permute-start(f32[72,128]{1,0:T(8,128)S(1)} %get-tuple-element.68), channel_id=1, source_target_pairs={{0,12},{4,8},{8,4},{12,0},{1,13},{5,9},{9,5},{13,1},{2,14},{6,10},... | collective-permute-start | bytes 110600 | tf_op jit(solution)/shard_map/ppermute | solution.py:703
  39.1 2.1 %collective-permute-start.14 = (f32[72,128]{1,0:T(8,128)S(1)}, f32[72,128]{1,0:T(8,128)S(1)}, u32[]{:S(2)}, u32[]{:S(2)}) collective-permute-start(f32[72,128]{1,0:T(8,128)S(1)} %get-tuple-element.70), channel_id=1, source_target_pairs={{0,4},{4,0},{8,12},{12,8},{1,5},{5,1},{9,13},{13,9},{2,6},{6,2},{1... | collective-permute-start | bytes 110600 | tf_op jit(solution)/shard_map/ppermute | solution.py:703
  41.3 1.6 %collective-permute-done.12.refs_0_ = f32[72,128]{1,0:T(8,128)S(1)} collective-permute-done((f32[72,128]{1,0:T(8,128)S(1)}, f32[72,128]{1,0:T(8,128)S(1)}, u32[]{:S(2)}, u32[]{:S(2)}) %collective-permute-start.12) | collective-permute-done | bytes 36896 | tf_op jit(solution)/shard_map/ppermute | solution.py:703
  42.9 1.1 %collective-permute-done.13.refs_1_ = f32[72,128]{1,0:T(8,128)S(1)} collective-permute-done((f32[72,128]{1,0:T(8,128)S(1)}, f32[72,128]{1,0:T(8,128)S(1)}, u32[]{:S(2)}, u32[]{:S(2)}) %collective-permute-start.13) | collective-permute-done | bytes 36896 | tf_op jit(solution)/shard_map/ppermute | solution.py:703
  44.0 0.6 %shard_map.100 = (f32[1,64,128]{2,1,0:T(8,128)}, f32[1,144]{1,0:T(1,128)}) custom-call(f32[72,128]{1,0:T(8,128)S(1)} %collective-permute-done.12.refs_0_, f32[72,128]{1,0:T(8,128)S(1)} %collective-permute-done.13.refs_1_, f32[72,128]{1,0:T(8,128)S(1)} %collective-permute-done.14.refs_2_, f32[72,128]{1,0:T(8,128)S(1)} %get-tuple-element.71.refs_3_, ...), custom_call_target="tpu_custom_call" | custom-call | bytes 245760 | tf_op jit(solution)/shard_map/pallas_call | solution.py:78
  (27 shorter events, 2.0 us)
Async XLA Ops:
  0.6 5.8 %copy-start.5 = (s32[288]{0:T(512)S(1)}, s32[288]{0:T(512)}, u32[]{:S(2)}) copy-start(s32[288]{0:T(512)} %prior_ref.1) | copy-start | bytes 3460
  0.6 5.8 %copy-start.4 = (bf16[288,64,128]{2,1,0:T(8,128)(2,1)S(1)}, bf16[288,64,128]{2,1,0:T(8,128)(2,1)}, u32[]{:S(2)}) copy-start(bf16[288,64,128]{2,1,0:T(8,128)(2,1)} %particles_ref.1) | copy-start | bytes 14155780
  0.6 7.2 %collective-permute-start.1 = (bf16[1,64,128]{2,1,0:T(8,128)(2,1)}, bf16[1,64,128]{2,1,0:T(8,128)(2,1)S(1)}, u32[]{:S(2)}, u32[]{:S(2)}) collective-permute-start(bf16[1,64,128]{2,1,0:T(8,128)(2,1)} %refs_0_.1), channel_id=1, source_target_pairs={{0,8},{4,12},{8,0},{12,4},{1,9},{5,13},{9,1},{13,5},{2,10},{6,14},... | collective-permute-start | bytes 49160 | tf_op jit(solution)/shard_map/ppermute | solution.py:703
  4.8 5.7 %collective-permute-start = (bf16[1,64,128]{2,1,0:T(8,128)(2,1)}, bf16[1,64,128]{2,1,0:T(8,128)(2,1)S(1)}, u32[]{:S(2)}, u32[]{:S(2)}) collective-permute-start(bf16[1,64,128]{2,1,0:T(8,128)(2,1)} %refs_0_.1), channel_id=1, source_target_pairs={{0,12},{4,8},{8,4},{12,0},{1,13},{5,9},{9,5},{13,1},{2,14},{6,10},... | collective-permute-start | bytes 49160 | tf_op jit(solution)/shard_map/ppermute | solution.py:703
  6.1 4.4 %collective-permute-start.2 = (bf16[1,64,128]{2,1,0:T(8,128)(2,1)}, bf16[1,64,128]{2,1,0:T(8,128)(2,1)S(1)}, u32[]{:S(2)}, u32[]{:S(2)}) collective-permute-start(bf16[1,64,128]{2,1,0:T(8,128)(2,1)} %refs_0_.1), channel_id=1, source_target_pairs={{0,4},{4,0},{8,12},{12,8},{1,5},{5,1},{9,13},{13,9},{2,6},{6,2},{1... | collective-permute-start | bytes 49160 | tf_op jit(solution)/shard_map/ppermute | solution.py:703
  6.4 4.1 %copy-start.2 = (bf16[1,64,128]{2,1,0:T(8,128)(2,1)S(1)}, bf16[1,64,128]{2,1,0:T(8,128)(2,1)}, u32[]{:S(2)}) copy-start(bf16[1,64,128]{2,1,0:T(8,128)(2,1)} %refs_0_.1) | copy-start | bytes 49156
  6.4 4.1 %copy-start.3 = (f32[64]{0:T(128)S(1)}, f32[64]{0:T(128)}, u32[]{:S(2)}) copy-start(f32[64]{0:T(128)} %param.9) | copy-start | bytes 772
  7.9 3.6 %copy-start.1 = (bf16[512,384]{1,0:T(8,128)(2,1)S(1)}, bf16[512,384]{1,0:T(8,128)(2,1)}, u32[]{:S(2)}) copy-start(bf16[512,384]{1,0:T(8,128)(2,1)} %constant.6.clone.table) | copy-start | bytes 1179652
  10.5 2.6 %copy-start.6 = (bf16[512,384]{1,0:T(8,128)(2,1)S(1)}, bf16[512,384]{1,0:T(8,128)(2,1)}, u32[]{:S(2)}) copy-start(bf16[512,384]{1,0:T(8,128)(2,1)} %constant.7.clone.table) | copy-start | bytes 1179652
  11.5 1.6 %collective-permute-start.3 = (f32[648,128]{1,0:T(8,128)S(1)}, f32[648,128]{1,0:T(8,128)S(1)}, u32[]{:S(2)}, u32[]{:S(2)}) collective-permute-start(f32[648,128]{1,0:T(8,128)S(1)} %get-tuple-element.46), channel_id=1, source_target_pairs={{0,1},{1,0},{2,3},{3,2},{4,5},{5,4},{6,7},{7,6},{8,9},{9,8},{10,11... | collective-permute-start | bytes 995336 | tf_op jit(solution)/shard_map/ppermute | solution.py:703
  11.5 5.3 %copy-start = (bf16[512,512]{1,0:T(8,128)(2,1)S(1)}, bf16[512,512]{1,0:T(8,128)(2,1)}, u32[]{:S(2)}) copy-start(bf16[512,512]{1,0:T(8,128)(2,1)} %constant.8.clone.forward) | copy-start | bytes 1572868
  13.7 3.1 %collective-permute-start.4 = (f32[8,256]{1,0:T(8,128)S(1)}, f32[8,256]{1,0:T(8,128)S(1)}, u32[]{:S(2)}, u32[]{:S(2)}) collective-permute-start(f32[8,256]{1,0:T(8,128)S(1)} %get-tuple-element.51.first), channel_id=1, source_target_pairs={{0,3},{1,2},{2,1},{3,0},{4,7},{5,6},{6,5},{7,4},{8,11},{9,10},{10,... | collective-permute-start | bytes 24584 | tf_op jit(solution)/shard_map/ppermute | solution.py:703
  17.2 1.5 %collective-permute-start.5 = (bf16[42,16,128]{2,1,0:T(8,128)(2,1)S(1)}, bf16[42,16,128]{2,1,0:T(8,128)(2,1)S(1)}, u32[]{:S(2)}, u32[]{:S(2)}) collective-permute-start(bf16[42,16,128]{2,1,0:T(8,128)(2,1)S(1)} %get-tuple-element.54.mine), channel_id=1, source_target_pairs={{0,1},{1,0},{2,3},{3,2},{4,5},{5,4},{6,7},{7,6},{8,9},{9,8},{10,11... | collective-permute-start | bytes 516104 | tf_op jit(solution)/shard_map/ppermute | solution.py:703
  19.2 7.2 %collective-permute-start.8 = (bf16[272,128]{1,0:T(8,128)(2,1)S(1)}, bf16[272,128]{1,0:T(8,128)(2,1)S(1)}, u32[]{:S(2)}, u32[]{:S(2)}) collective-permute-start(bf16[272,128]{1,0:T(8,128)(2,1)S(1)} %shard_map.93.refs_0_), channel_id=1, source_target_pairs={{0,8},{4,12},{8,0},{12,4},{1,9},{5,13},{9,1},{13,5},{2,10},{6,14},... | collective-permute-start | bytes 208904 | tf_op jit(solution)/shard_map/ppermute | solution.py:703
  20.5 6.5 %collective-permute-start.7 = (bf16[272,128]{1,0:T(8,128)(2,1)S(1)}, bf16[272,128]{1,0:T(8,128)(2,1)S(1)}, u32[]{:S(2)}, u32[]{:S(2)}) collective-permute-start(bf16[272,128]{1,0:T(8,128)(2,1)S(1)} %shard_map.93.refs_0_), channel_id=1, source_target_pairs={{0,12},{4,8},{8,4},{12,0},{1,13},{5,9},{9,5},{13,1},{2,14},{6,10},... | collective-permute-start | bytes 208904 | tf_op jit(solution)/shard_map/ppermute | solution.py:703
  21.4 6.8 %collective-permute-start.6 = (bf16[272,128]{1,0:T(8,128)(2,1)S(1)}, bf16[272,128]{1,0:T(8,128)(2,1)S(1)}, u32[]{:S(2)}, u32[]{:S(2)}) collective-permute-start(bf16[272,128]{1,0:T(8,128)(2,1)S(1)} %shard_map.93.refs_0_), channel_id=1, source_target_pairs={{0,4},{4,0},{8,12},{12,8},{1,5},{5,1},{9,13},{13,9},{2,6},{6,2},{1... | collective-permute-start | bytes 208904 | tf_op jit(solution)/shard_map/ppermute | solution.py:703
  29.1 1.6 %collective-permute-start.9 = (f32[648,128]{1,0:T(8,128)S(1)}, f32[648,128]{1,0:T(8,128)S(1)}, u32[]{:S(2)}, u32[]{:S(2)}) collective-permute-start(f32[648,128]{1,0:T(8,128)S(1)} %get-tuple-element.59), channel_id=1, source_target_pairs={{0,1},{1,0},{2,3},{3,2},{4,5},{5,4},{6,7},{7,6},{8,9},{9,8},{10,11... | collective-permute-start | bytes 995336 | tf_op jit(solution)/shard_map/ppermute | solution.py:703
  31.3 3.1 %collective-permute-start.10 = (f32[8,256]{1,0:T(8,128)S(1)}, f32[8,256]{1,0:T(8,128)S(1)}, u32[]{:S(2)}, u32[]{:S(2)}) collective-permute-start(f32[8,256]{1,0:T(8,128)S(1)} %get-tuple-element.64.first), channel_id=1, source_target_pairs={{0,3},{1,2},{2,1},{3,0},{4,7},{5,6},{6,5},{7,4},{8,11},{9,10},{10,... | collective-permute-start | bytes 24584 | tf_op jit(solution)/shard_map/ppermute | solution.py:703
  34.8 1.5 %collective-permute-start.11 = (bf16[42,16,128]{2,1,0:T(8,128)(2,1)S(1)}, bf16[42,16,128]{2,1,0:T(8,128)(2,1)S(1)}, u32[]{:S(2)}, u32[]{:S(2)}) collective-permute-start(bf16[42,16,128]{2,1,0:T(8,128)(2,1)S(1)} %get-tuple-element.67.mine), channel_id=1, source_target_pairs={{0,1},{1,0},{2,3},{3,2},{4,5},{5,4},{6,7},{7,6},{8,9},{9,8},{10,11... | collective-permute-start | bytes 516104 | tf_op jit(solution)/shard_map/ppermute | solution.py:703
  36.8 6.1 %collective-permute-start.12 = (f32[72,128]{1,0:T(8,128)S(1)}, f32[72,128]{1,0:T(8,128)S(1)}, u32[]{:S(2)}, u32[]{:S(2)}) collective-permute-start(f32[72,128]{1,0:T(8,128)S(1)} %get-tuple-element.68), channel_id=1, source_target_pairs={{0,12},{4,8},{8,4},{12,0},{1,13},{5,9},{9,5},{13,1},{2,14},{6,10},... | collective-permute-start | bytes 110600 | tf_op jit(solution)/shard_map/ppermute | solution.py:703
  39.1 4.9 %collective-permute-start.13 = (f32[72,128]{1,0:T(8,128)S(1)}, f32[72,128]{1,0:T(8,128)S(1)}, u32[]{:S(2)}, u32[]{:S(2)}) collective-permute-start(f32[72,128]{1,0:T(8,128)S(1)} %get-tuple-element.69), channel_id=1, source_target_pairs={{0,8},{4,12},{8,0},{12,4},{1,9},{5,13},{9,1},{13,5},{2,10},{6,14},... | collective-permute-start | bytes 110600 | tf_op jit(solution)/shard_map/ppermute | solution.py:703
  39.1 4.9 %collective-permute-start.14 = (f32[72,128]{1,0:T(8,128)S(1)}, f32[72,128]{1,0:T(8,128)S(1)}, u32[]{:S(2)}, u32[]{:S(2)}) collective-permute-start(f32[72,128]{1,0:T(8,128)S(1)} %get-tuple-element.70), channel_id=1, source_target_pairs={{0,4},{4,0},{8,12},{12,8},{1,5},{5,1},{9,13},{13,9},{2,6},{6,2},{1... | collective-permute-start | bytes 110600 | tf_op jit(solution)/shard_map/ppermute | solution.py:703

commit v24 on v23

--- a/solution.py
+++ b/solution.py
@@ -177,7 +177,7 @@
     pairs, share, twice = particles.shape
     freqs, depth = 2 * pairs, twice // 2
     classes = energy_ref.shape[0]
-    pitch = freqs + SPARE
+    pitch = freqs
     radii = depth // 2
     lane = lax.broadcasted_iota(jnp.int32, (freqs, depth), 1)
     sign = jnp.where(lane < radii, -1.0, 1.0).astype(F32)
@@ -190,6 +190,7 @@
         end = sources[0].shape[0] - classes * freqs
         tails = [source[pl.ds(classes * freqs, end), :].astype(F32) for source in sources]
 
+    energies = [jnp.zeros((SPARE, 128), F32)] * -(-classes // SPARE)
     for k in range(classes):
         if fresh:
             plain = sources[k][0].astype(F32)
@@ -208,9 +209,12 @@
         image[rows((2 * k + 1) * pitch, freqs), :] = sign * pltpu.roll(weighted, radii, 1)
         energy = jnp.sum(plain * plain * scale, axis=0, keepdims=True)
         energy = jnp.broadcast_to(jnp.sum(energy, axis=1, keepdims=True), (SPARE, 128))
+        line = lax.broadcasted_iota(jnp.int32, (SPARE, 128), 0)
+        energies[k // SPARE] = jnp.where(line == k % SPARE, energy, energies[k // SPARE])
         energy_ref[pl.ds(k, 1), :] = energy[:1]
-        out[rows(2 * k * pitch + freqs, SPARE), :] = energy
-
+
+    for i, energy in enumerate(energies):
+        out[pl.ds(out.shape[0] - (len(energies) - i) * SPARE, SPARE), :] = energy
     none = jnp.zeros((2 * classes, depth), BF16)
 
     def correlate(f):
@@ -281,13 +285,14 @@
 
 
 def corr_lines(classes, share, pitch):
-    return (2 * classes + -(-2 * classes * (share - 128) // 128)) * pitch
+    packs = -(-2 * classes * (share - 128) // 128)
+    return (2 * classes + packs) * pitch + -(-classes // SPARE) * SPARE
 
 
 def weigh(sources, order, inverse_noise, particles, fresh):
     pairs, share, twice = particles.shape
     classes = len(sources)
-    pitch = 2 * pairs + SPARE
+    pitch = 2 * pairs
     return call(
         functools.partial(weigh_kernel, fresh, order, classes),
         [*[sources[i] for i in order], inverse_noise, particles],
@@ -305,7 +310,7 @@
     partial, partial_more, field = refs
     pairs, share, _ = particles.shape
     classes = left_ref.shape[1] // 4
-    freqs, pitch = 2 * pairs, 2 * pairs + SPARE
+    freqs = pitch = 2 * pairs
 
     def body(f):
         values = [times(left_ref[f + i], particles[f + i]) for i in range(GROUP)]
@@ -359,7 +364,7 @@
 def correlate(left, particles, energy, prior_term, table):
     pairs, share, twice = particles.shape
     classes = left.shape[1] // 4
-    pitch = 2 * pairs + SPARE
+    pitch = 2 * pairs
     return call(
         correlate_kernel,
         [left, particles, energy, prior_term, table],
@@ -378,7 +383,7 @@
     classes = 2 * partial.shape[0]
     width, bundle, units = layout(classes, share)
     freqs = ANG // 4
-    pitch = freqs + SPARE
+    pitch = freqs
 
     def exponentials(scores):
         top = jnp.max(scores, axis=0, keepdims=True)
@@ -386,7 +391,7 @@
         return value, top, jnp.sum(value, axis=0, keepdims=True)
 
     def energy_of(k):
-        return other[rows(2 * k * pitch + freqs, SPARE), :][:1]
+        return other[pl.ds(other.shape[0] - -(-classes // SPARE) * SPARE + k, 1), :]
 
     def slab(i, carry):
         energy = jnp.concatenate([energy_of(2 * i), energy_of(2 * i + 1)], 1)
@@ -451,7 +456,7 @@
     rounded_ref, rounded_more, send, *last, held = refs
     classes = 2 * weights.shape[0]
     width, bundle, units = layout(classes, share)
-    pairs = (held.shape[0] // (2 * classes) - SPARE) // 2
+    pairs = held.shape[0] // (2 * classes) // 2
     top, total = merge(two_lines(first), two_lines(second))
     evidence = top + jnp.log(total)
     scale = 1.0 / total
@@ -521,7 +526,7 @@
     freqs = value.shape[0] // 2
     for j in range(2):
         for part in range(2):
-            held[rows((4 * i + 2 * j + part) * (freqs + SPARE), freqs), :] = value[
+            held[rows((4 * i + 2 * j + part) * freqs, freqs), :] = value[
                 part * freqs : (part + 1) * freqs, j * 128 : (j + 1) * 128
             ]
 
@@ -533,7 +538,7 @@
         shifted = turned(value, -j * width)
         for part in range(2):
             k = unit * bundle + j
-            held[rows((2 * k + part) * (freqs + SPARE), freqs), :] = shifted[
+            held[rows((2 * k + part) * freqs, freqs), :] = shifted[
                 part * freqs : (part + 1) * freqs
             ]
 
@@ -554,7 +559,7 @@
             (message_shape(classes, freqs // 2, units), BF16),
             *([((1, share), F32)] if last else []),
         ],
-        [((2 * classes * (freqs + SPARE), 128), F32)],
+        [((2 * classes * freqs, 128), F32)],
         flops=4 * classes * 256 * ANG * ANG,
     )
 
@@ -589,7 +594,7 @@
 def gather(rounded, rounded_more, forward, particles):
     pairs, share, twice = particles.shape
     classes = 2 * rounded.shape[0]
-    lines = 2 * classes * (2 * pairs + SPARE)
+    lines = 2 * classes * 2 * pairs
     return call(
         gather_kernel,
         [rounded, rounded_more, forward, particles],
@@ -616,7 +621,7 @@
     classes = spectrum.shape[1] // 4
     freqs, depth = 2 * pairs, twice // 2
     radii = depth // 2
-    pitch = freqs + SPARE
+    pitch = freqs
 
     width, bundle, units = layout(classes, share)
     step = 4 * classes

time: 44.8 us -> 44.7 us (level)
  no operation moved by 1% of the time
where the time goes in v24:
time: 44.7 us; the launch traced here: 44.6 us
  waiting for transfers between devices  16.7 us (37%)
  starting transfers between devices  16.6 us (37%)
  Pallas kernels  10.5 us (23%)
  between operations  0.8 us (2%)
    ppermute x15, waiting for transfers between devices, swap(): return lax.ppermute(value, axis, [(i, i ^ bit) for i in range(size)])  16.7 us
    ppermute x15, starting transfers between devices, swap(): return lax.ppermute(value, axis, [(i, i ^ bit) for i in range(size)])  16.6 us
    pallas_call x15, Pallas kernels, call(): pl.pallas_call(kernel, out_shape=[jax.ShapeDtypeStruct(*x) for x in outs]...  10.5 us
  transfers between devices with their start and end apart: 15, of which 12 were waited for; matrix products, arithmetic and copies ran while one was open for 0% of the time, Pallas kernels for 11%

profile of v24, /device:TPU:0, one launch (start us, length us, event | category | flops | bytes accessed | tf_op | source)
XLA Modules:
  0.0 44.6 jit_solution(16871446659557812322)
XLA Ops:
  0.6 4.1 %collective-permute-start.1 = (bf16[1,64,128]{2,1,0:T(8,128)(2,1)}, bf16[1,64,128]{2,1,0:T(8,128)(2,1)S(1)}, u32[]{:S(2)}, u32[]{:S(2)}) collective-permute-start(bf16[1,64,128]{2,1,0:T(8,128)(2,1)} %refs_0_.1), channel_id=1, source_target_pairs={{0,8},{4,12},{8,0},{12,4},{1,9},{5,13},{9,1},{13,5},{2,10},{6,14},... | collective-permute-start | bytes 49160 | tf_op jit(solution)/shard_map/ppermute | solution.py:708
  4.8 1.3 %collective-permute-start = (bf16[1,64,128]{2,1,0:T(8,128)(2,1)}, bf16[1,64,128]{2,1,0:T(8,128)(2,1)S(1)}, u32[]{:S(2)}, u32[]{:S(2)}) collective-permute-start(bf16[1,64,128]{2,1,0:T(8,128)(2,1)} %refs_0_.1), channel_id=1, source_target_pairs={{0,12},{4,8},{8,4},{12,0},{1,13},{5,9},{9,5},{13,1},{2,14},{6,10},... | collective-permute-start | bytes 49160 | tf_op jit(solution)/shard_map/ppermute | solution.py:708
  6.4 1.4 %shard_map.87 = (bf16[32,144,256]{2,1,0:T(8,128)(2,1)S(1)}, bf16[32,144,256]{2,1,0:T(8,128)(2,1)S(1)}, f32[256,256]{1,0:T(8,128)S(1)}) custom-call(bf16[288,64,128]{2,1,0:T(8,128)(2,1)S(1)} %copy-done.4, bf16[256,256]{1,0:T(8,128)(2,1)S(1)} %shard_map.86.permutation_ref, s32[288]{0:T(512)S(1)} %copy-done.5), custom_call_target="tpu_custom_call" | custom-call | flops 2147483648 | bytes 9854976 | tf_op jit(solution)/shard_map/pallas_call | solution.py:78
  7.9 2.6 %collective-permute-done.refs_1_ = bf16[1,64,128]{2,1,0:T(8,128)(2,1)S(1)} collective-permute-done((bf16[1,64,128]{2,1,0:T(8,128)(2,1)}, bf16[1,64,128]{2,1,0:T(8,128)(2,1)S(1)}, u32[]{:S(2)}, u32[]{:S(2)}) %collective-permute-start) | collective-permute-done | bytes 16416 | tf_op jit(solution)/shard_map/ppermute | solution.py:708
  10.5 0.9 %shard_map.88 = (f32[584,128]{1,0:T(8,128)S(1)}, f32[4,128]{1,0:T(4,128)S(1)}, bf16[32,16,256]{2,1,0:T(8,128)(2,1)S(1)}) custom-call(bf16[1,64,128]{2,1,0:T(8,128)(2,1)S(1)} %copy-done.2, bf16[1,64,128]{2,1,0:T(8,128)(2,1)S(1)} %collective-permute-done.refs_1_, bf16[1,64,128]{2,1,0:T(8,128)(2,1)S(1)} %collective-permute-done.1.refs_2_, ...), custom_call_target="tpu_custom_call" | custom-call | flops 150994944 | bytes 3268608 | tf_op jit(solution)/shard_map/pallas_call | solution.py:78
  11.5 1.1 %shard_map.89 = (f32[2,256,256]{2,1,0:T(8,128)S(1)}, f32[1,256,128]{2,1,0:T(8,128)S(1)}) custom-call(bf16[32,16,256]{2,1,0:T(8,128)(2,1)S(1)} %get-tuple-element.40.left_ref, bf16[32,144,256]{2,1,0:T(8,128)(2,1)S(1)} %get-tuple-element.41.particles, f32[4,128]{1,0:T(4,128)S(1)} %get-tuple-element.42.energy_ref, f32[256,256]{1,0:T(8,128)S(1)} %get-tuple-element.43.prior_term, ...), custom_call_target="tpu_custom_call" | custom-call | flops 301989888 | bytes 4243456 | tf_op jit(solution)/shard_map/pallas_call | solution.py:78
  13.1 0.5 %shard_map.90 = (f32[2,256,256]{2,1,0:T(8,128)S(1)}, f32[1,256,128]{2,1,0:T(8,128)S(1)}, f32[2,256]{1,0:T(2,128)S(1)}, f32[1,128]{1,0:T(1,128)S(1)}, f32[8,256]{1,0:T(8,128)S(1)}) custom-call(f32[2,256,256]{2,1,0:T(8,128)S(1)} %get-tuple-element.44.partial, f32[1,256,128]{2,1,0:T(8,128)S(1)} %get-tuple-element.45.partial_more, ...), custom_call_target="tpu_custom_call" | custom-call | flops 402653184 | bytes 2048000 | tf_op jit(solution)/shard_map/pallas_call | solution.py:78
  13.6 1.3 %collective-permute-start.4 = (f32[8,256]{1,0:T(8,128)S(1)}, f32[8,256]{1,0:T(8,128)S(1)}, u32[]{:S(2)}, u32[]{:S(2)}) collective-permute-start(f32[8,256]{1,0:T(8,128)S(1)} %get-tuple-element.51.first), channel_id=1, source_target_pairs={{0,3},{1,2},{2,1},{3,0},{4,7},{5,6},{6,5},{7,4},{8,11},{9,10},{10,... | collective-permute-start | bytes 24584 | tf_op jit(solution)/shard_map/ppermute | solution.py:708
  14.9 1.8 %collective-permute-done.4.second = f32[8,256]{1,0:T(8,128)S(1)} collective-permute-done((f32[8,256]{1,0:T(8,128)S(1)}, f32[8,256]{1,0:T(8,128)S(1)}, u32[]{:S(2)}, u32[]{:S(2)}) %collective-permute-start.4) | collective-permute-done | bytes 8224 | tf_op jit(solution)/shard_map/ppermute | solution.py:708
  17.3 0.7 %shard_map.92.image = f32[512,128]{1,0:T(8,128)S(1)} custom-call(bf16[2,256,256]{2,1,0:T(8,128)(2,1)S(1)} %get-tuple-element.52.rounded_ref, bf16[1,256,128]{2,1,0:T(8,128)(2,1)S(1)} %get-tuple-element.53.rounded_more, bf16[512,512]{1,0:T(8,128)(2,1)S(1)} %copy-done, bf16[32,144,256]{2,1,0:T(8,128)(2,1)S(1)} %get-tuple-element.41.particles), custom_call_target="tpu_custom_call" | custom-call | flops 268435456 | bytes 3997696 | tf_op jit(solution)/shard_map/pallas_call | solution.py:78
  18.0 0.6 %collective-permute-done.5.spectrum = bf16[42,16,128]{2,1,0:T(8,128)(2,1)S(1)} collective-permute-done((bf16[42,16,128]{2,1,0:T(8,128)(2,1)S(1)}, bf16[42,16,128]{2,1,0:T(8,128)(2,1)S(1)}, u32[]{:S(2)}, u32[]{:S(2)}) %collective-permute-start.5) | collective-permute-done | bytes 172064 | tf_op jit(solution)/shard_map/ppermute | solution.py:708
  18.6 0.6 %shard_map.93.refs_0_ = bf16[272,128]{1,0:T(8,128)(2,1)S(1)} custom-call(f32[512,128]{1,0:T(8,128)S(1)} %shard_map.92.image, bf16[42,16,128]{2,1,0:T(8,128)(2,1)S(1)} %get-tuple-element.54.mine, bf16[42,16,128]{2,1,0:T(8,128)(2,1)S(1)} %collective-permute-done.5.spectrum, bf16[32,144,256]{2,1,0:T(8,128)(2,1)S(1)} %get-tuple-element.39.refs_5_.particles), custom_call_target="tpu_custom_call" | custom-call | flops 352321536 | bytes 3297280 | tf_op jit(solution)/shard_map/pallas_call | solution.py:78
  19.1 1.3 %collective-permute-start.8 = (bf16[272,128]{1,0:T(8,128)(2,1)S(1)}, bf16[272,128]{1,0:T(8,128)(2,1)S(1)}, u32[]{:S(2)}, u32[]{:S(2)}) collective-permute-start(bf16[272,128]{1,0:T(8,128)(2,1)S(1)} %shard_map.93.refs_0_), channel_id=1, source_target_pairs={{0,8},{4,12},{8,0},{12,4},{1,9},{5,13},{9,1},{13,5},{2,10},{6,14},... | collective-permute-start | bytes 208904 | tf_op jit(solution)/shard_map/ppermute | solution.py:708
  20.4 0.9 %collective-permute-start.7 = (bf16[272,128]{1,0:T(8,128)(2,1)S(1)}, bf16[272,128]{1,0:T(8,128)(2,1)S(1)}, u32[]{:S(2)}, u32[]{:S(2)}) collective-permute-start(bf16[272,128]{1,0:T(8,128)(2,1)S(1)} %shard_map.93.refs_0_), channel_id=1, source_target_pairs={{0,12},{4,8},{8,4},{12,0},{1,13},{5,9},{9,5},{13,1},{2,14},{6,10},... | collective-permute-start | bytes 208904 | tf_op jit(solution)/shard_map/ppermute | solution.py:708
  21.3 1.3 %collective-permute-start.6 = (bf16[272,128]{1,0:T(8,128)(2,1)S(1)}, bf16[272,128]{1,0:T(8,128)(2,1)S(1)}, u32[]{:S(2)}, u32[]{:S(2)}) collective-permute-start(bf16[272,128]{1,0:T(8,128)(2,1)S(1)} %shard_map.93.refs_0_), channel_id=1, source_target_pairs={{0,4},{4,0},{8,12},{12,8},{1,5},{5,1},{9,13},{13,9},{2,6},{6,2},{1... | collective-permute-start | bytes 208904 | tf_op jit(solution)/shard_map/ppermute | solution.py:708
  22.7 3.6 %collective-permute-done.8.refs_3_ = bf16[272,128]{1,0:T(8,128)(2,1)S(1)} collective-permute-done((bf16[272,128]{1,0:T(8,128)(2,1)S(1)}, bf16[272,128]{1,0:T(8,128)(2,1)S(1)}, u32[]{:S(2)}, u32[]{:S(2)}) %collective-permute-start.8) | collective-permute-done | bytes 69664 | tf_op jit(solution)/shard_map/ppermute | solution.py:708
  26.3 0.6 %collective-permute-done.7.refs_2_ = bf16[272,128]{1,0:T(8,128)(2,1)S(1)} collective-permute-done((bf16[272,128]{1,0:T(8,128)(2,1)S(1)}, bf16[272,128]{1,0:T(8,128)(2,1)S(1)}, u32[]{:S(2)}, u32[]{:S(2)}) %collective-permute-start.7) | collective-permute-done | bytes 69664 | tf_op jit(solution)/shard_map/ppermute | solution.py:708
  27.0 1.2 %collective-permute-done.6.refs_1_ = bf16[272,128]{1,0:T(8,128)(2,1)S(1)} collective-permute-done((bf16[272,128]{1,0:T(8,128)(2,1)S(1)}, bf16[272,128]{1,0:T(8,128)(2,1)S(1)}, u32[]{:S(2)}, u32[]{:S(2)}) %collective-permute-start.6) | collective-permute-done | bytes 69664 | tf_op jit(solution)/shard_map/ppermute | solution.py:708
  28.1 0.9 %shard_map.94 = (f32[584,128]{1,0:T(8,128)S(1)}, f32[4,128]{1,0:T(4,128)S(1)}, bf16[32,16,256]{2,1,0:T(8,128)(2,1)S(1)}) custom-call(bf16[272,128]{1,0:T(8,128)(2,1)S(1)} %shard_map.93.refs_0_, bf16[272,128]{1,0:T(8,128)(2,1)S(1)} %collective-permute-done.6.refs_1_, bf16[272,128]{1,0:T(8,128)(2,1)S(1)} %collective-permute-done.7.refs_2_, ...), custom_call_target="tpu_custom_call" | custom-call | flops 150994944 | bytes 3481600 | tf_op jit(solution)/shard_map/pallas_call | solution.py:78
  29.1 1.1 %shard_map.95 = (f32[2,256,256]{2,1,0:T(8,128)S(1)}, f32[1,256,128]{2,1,0:T(8,128)S(1)}) custom-call(bf16[32,16,256]{2,1,0:T(8,128)(2,1)S(1)} %get-tuple-element.55.left_ref, bf16[32,144,256]{2,1,0:T(8,128)(2,1)S(1)} %get-tuple-element.41.particles, f32[4,128]{1,0:T(4,128)S(1)} %get-tuple-element.56.energy_ref, f32[256,256]{1,0:T(8,128)S(1)} %get-tuple-element.43.prior_term, ...), custom_call_target="tpu_custom_call" | custom-call | flops 301989888 | bytes 4243456 | tf_op jit(solution)/shard_map/pallas_call | solution.py:78
  30.2 0.5 %collective-permute-done.9.other = f32[584,128]{1,0:T(8,128)S(1)} collective-permute-done((f32[584,128]{1,0:T(8,128)S(1)}, f32[584,128]{1,0:T(8,128)S(1)}, u32[]{:S(2)}, u32[]{:S(2)}) %collective-permute-start.9) | collective-permute-done | bytes 299040 | tf_op jit(solution)/shard_map/ppermute | solution.py:708
  30.7 0.5 %shard_map.96 = (f32[2,256,256]{2,1,0:T(8,128)S(1)}, f32[1,256,128]{2,1,0:T(8,128)S(1)}, f32[2,256]{1,0:T(2,128)S(1)}, f32[1,128]{1,0:T(1,128)S(1)}, f32[8,256]{1,0:T(8,128)S(1)}) custom-call(f32[2,256,256]{2,1,0:T(8,128)S(1)} %get-tuple-element.57.partial, f32[1,256,128]{2,1,0:T(8,128)S(1)} %get-tuple-element.58.partial_more, ...), custom_call_target="tpu_custom_call" | custom-call | flops 402653184 | bytes 2048000 | tf_op jit(solution)/shard_map/pallas_call | solution.py:78
  31.2 1.3 %collective-permute-start.10 = (f32[8,256]{1,0:T(8,128)S(1)}, f32[8,256]{1,0:T(8,128)S(1)}, u32[]{:S(2)}, u32[]{:S(2)}) collective-permute-start(f32[8,256]{1,0:T(8,128)S(1)} %get-tuple-element.64.first), channel_id=1, source_target_pairs={{0,3},{1,2},{2,1},{3,0},{4,7},{5,6},{6,5},{7,4},{8,11},{9,10},{10,... | collective-permute-start | bytes 24584 | tf_op jit(solution)/shard_map/ppermute | solution.py:708
  32.5 1.8 %collective-permute-done.10.second = f32[8,256]{1,0:T(8,128)S(1)} collective-permute-done((f32[8,256]{1,0:T(8,128)S(1)}, f32[8,256]{1,0:T(8,128)S(1)}, u32[]{:S(2)}, u32[]{:S(2)}) %collective-permute-start.10) | collective-permute-done | bytes 8224 | tf_op jit(solution)/shard_map/ppermute | solution.py:708
  34.9 0.7 %shard_map.98.image = f32[512,128]{1,0:T(8,128)S(1)} custom-call(bf16[2,256,256]{2,1,0:T(8,128)(2,1)S(1)} %get-tuple-element.65.rounded_ref, bf16[1,256,128]{2,1,0:T(8,128)(2,1)S(1)} %get-tuple-element.66.rounded_more, bf16[512,512]{1,0:T(8,128)(2,1)S(1)} %copy-done, bf16[32,144,256]{2,1,0:T(8,128)(2,1)S(1)} %get-tuple-element.41.particles), custom_call_target="tpu_custom_call" | custom-call | flops 268435456 | bytes 3997696 | tf_op jit(solution)/shard_map/pallas_call | solution.py:78
  35.6 0.6 %collective-permute-done.11.spectrum = bf16[42,16,128]{2,1,0:T(8,128)(2,1)S(1)} collective-permute-done((bf16[42,16,128]{2,1,0:T(8,128)(2,1)S(1)}, bf16[42,16,128]{2,1,0:T(8,128)(2,1)S(1)}, u32[]{:S(2)}, u32[]{:S(2)}) %collective-permute-start.11) | collective-permute-done | bytes 172064 | tf_op jit(solution)/shard_map/ppermute | solution.py:708
  36.2 0.6 %shard_map.99 = (f32[72,128]{1,0:T(8,128)S(1)}, f32[72,128]{1,0:T(8,128)S(1)}, f32[72,128]{1,0:T(8,128)S(1)}, f32[72,128]{1,0:T(8,128)S(1)}, f32[1,144]{1,0:T(1,128)S(1)}) custom-call(f32[512,128]{1,0:T(8,128)S(1)} %shard_map.98.image, bf16[42,16,128]{2,1,0:T(8,128)(2,1)S(1)} %get-tuple-element.67.mine, ...), custom_call_target="tpu_custom_call" | custom-call | flops 352321536 | bytes 3407872 | tf_op jit(solution)/shard_map/pallas_call | solution.py:78
  36.7 2.3 %collective-permute-start.12 = (f32[72,128]{1,0:T(8,128)S(1)}, f32[72,128]{1,0:T(8,128)S(1)}, u32[]{:S(2)}, u32[]{:S(2)}) collective-permute-start(f32[72,128]{1,0:T(8,128)S(1)} %get-tuple-element.68), channel_id=1, source_target_pairs={{0,12},{4,8},{8,4},{12,0},{1,13},{5,9},{9,5},{13,1},{2,14},{6,10},... | collective-permute-start | bytes 110600 | tf_op jit(solution)/shard_map/ppermute | solution.py:708
  39.1 2.1 %collective-permute-start.14 = (f32[72,128]{1,0:T(8,128)S(1)}, f32[72,128]{1,0:T(8,128)S(1)}, u32[]{:S(2)}, u32[]{:S(2)}) collective-permute-start(f32[72,128]{1,0:T(8,128)S(1)} %get-tuple-element.70), channel_id=1, source_target_pairs={{0,4},{4,0},{8,12},{12,8},{1,5},{5,1},{9,13},{13,9},{2,6},{6,2},{1... | collective-permute-start | bytes 110600 | tf_op jit(solution)/shard_map/ppermute | solution.py:708
  41.2 1.6 %collective-permute-done.12.refs_0_ = f32[72,128]{1,0:T(8,128)S(1)} collective-permute-done((f32[72,128]{1,0:T(8,128)S(1)}, f32[72,128]{1,0:T(8,128)S(1)}, u32[]{:S(2)}, u32[]{:S(2)}) %collective-permute-start.12) | collective-permute-done | bytes 36896 | tf_op jit(solution)/shard_map/ppermute | solution.py:708
  42.8 1.1 %collective-permute-done.13.refs_1_ = f32[72,128]{1,0:T(8,128)S(1)} collective-permute-done((f32[72,128]{1,0:T(8,128)S(1)}, f32[72,128]{1,0:T(8,128)S(1)}, u32[]{:S(2)}, u32[]{:S(2)}) %collective-permute-start.13) | collective-permute-done | bytes 36896 | tf_op jit(solution)/shard_map/ppermute | solution.py:708
  44.0 0.6 %shard_map.100 = (f32[1,64,128]{2,1,0:T(8,128)}, f32[1,144]{1,0:T(1,128)}) custom-call(f32[72,128]{1,0:T(8,128)S(1)} %collective-permute-done.12.refs_0_, f32[72,128]{1,0:T(8,128)S(1)} %collective-permute-done.13.refs_1_, f32[72,128]{1,0:T(8,128)S(1)} %collective-permute-done.14.refs_2_, f32[72,128]{1,0:T(8,128)S(1)} %get-tuple-element.71.refs_3_, ...), custom_call_target="tpu_custom_call" | custom-call | bytes 245760 | tf_op jit(solution)/shard_map/pallas_call | solution.py:78
  (27 shorter events, 2.0 us)
Async XLA Ops:
  0.6 5.8 %copy-start.5 = (s32[288]{0:T(512)S(1)}, s32[288]{0:T(512)}, u32[]{:S(2)}) copy-start(s32[288]{0:T(512)} %prior_ref.1) | copy-start | bytes 3460
  0.6 5.8 %copy-start.4 = (bf16[288,64,128]{2,1,0:T(8,128)(2,1)S(1)}, bf16[288,64,128]{2,1,0:T(8,128)(2,1)}, u32[]{:S(2)}) copy-start(bf16[288,64,128]{2,1,0:T(8,128)(2,1)} %particles_ref.1) | copy-start | bytes 14155780
  0.6 7.2 %collective-permute-start.1 = (bf16[1,64,128]{2,1,0:T(8,128)(2,1)}, bf16[1,64,128]{2,1,0:T(8,128)(2,1)S(1)}, u32[]{:S(2)}, u32[]{:S(2)}) collective-permute-start(bf16[1,64,128]{2,1,0:T(8,128)(2,1)} %refs_0_.1), channel_id=1, source_target_pairs={{0,8},{4,12},{8,0},{12,4},{1,9},{5,13},{9,1},{13,5},{2,10},{6,14},... | collective-permute-start | bytes 49160 | tf_op jit(solution)/shard_map/ppermute | solution.py:708
  4.8 5.7 %collective-permute-start = (bf16[1,64,128]{2,1,0:T(8,128)(2,1)}, bf16[1,64,128]{2,1,0:T(8,128)(2,1)S(1)}, u32[]{:S(2)}, u32[]{:S(2)}) collective-permute-start(bf16[1,64,128]{2,1,0:T(8,128)(2,1)} %refs_0_.1), channel_id=1, source_target_pairs={{0,12},{4,8},{8,4},{12,0},{1,13},{5,9},{9,5},{13,1},{2,14},{6,10},... | collective-permute-start | bytes 49160 | tf_op jit(solution)/shard_map/ppermute | solution.py:708
  6.1 4.4 %collective-permute-start.2 = (bf16[1,64,128]{2,1,0:T(8,128)(2,1)}, bf16[1,64,128]{2,1,0:T(8,128)(2,1)S(1)}, u32[]{:S(2)}, u32[]{:S(2)}) collective-permute-start(bf16[1,64,128]{2,1,0:T(8,128)(2,1)} %refs_0_.1), channel_id=1, source_target_pairs={{0,4},{4,0},{8,12},{12,8},{1,5},{5,1},{9,13},{13,9},{2,6},{6,2},{1... | collective-permute-start | bytes 49160 | tf_op jit(solution)/shard_map/ppermute | solution.py:708
  6.4 4.1 %copy-start.2 = (bf16[1,64,128]{2,1,0:T(8,128)(2,1)S(1)}, bf16[1,64,128]{2,1,0:T(8,128)(2,1)}, u32[]{:S(2)}) copy-start(bf16[1,64,128]{2,1,0:T(8,128)(2,1)} %refs_0_.1) | copy-start | bytes 49156
  6.4 4.1 %copy-start.3 = (f32[64]{0:T(128)S(1)}, f32[64]{0:T(128)}, u32[]{:S(2)}) copy-start(f32[64]{0:T(128)} %param.9) | copy-start | bytes 772
  7.9 3.6 %copy-start.1 = (bf16[512,384]{1,0:T(8,128)(2,1)S(1)}, bf16[512,384]{1,0:T(8,128)(2,1)}, u32[]{:S(2)}) copy-start(bf16[512,384]{1,0:T(8,128)(2,1)} %constant.6.clone.table) | copy-start | bytes 1179652
  10.5 2.6 %copy-start.6 = (bf16[512,384]{1,0:T(8,128)(2,1)S(1)}, bf16[512,384]{1,0:T(8,128)(2,1)}, u32[]{:S(2)}) copy-start(bf16[512,384]{1,0:T(8,128)(2,1)} %constant.7.clone.table) | copy-start | bytes 1179652
  11.5 1.6 %collective-permute-start.3 = (f32[584,128]{1,0:T(8,128)S(1)}, f32[584,128]{1,0:T(8,128)S(1)}, u32[]{:S(2)}, u32[]{:S(2)}) collective-permute-start(f32[584,128]{1,0:T(8,128)S(1)} %get-tuple-element.46), channel_id=1, source_target_pairs={{0,1},{1,0},{2,3},{3,2},{4,5},{5,4},{6,7},{7,6},{8,9},{9,8},{10,11... | collective-permute-start | bytes 897032 | tf_op jit(solution)/shard_map/ppermute | solution.py:708
  11.5 5.2 %copy-start = (bf16[512,512]{1,0:T(8,128)(2,1)S(1)}, bf16[512,512]{1,0:T(8,128)(2,1)}, u32[]{:S(2)}) copy-start(bf16[512,512]{1,0:T(8,128)(2,1)} %constant.8.clone.forward) | copy-start | bytes 1572868
  13.6 3.1 %collective-permute-start.4 = (f32[8,256]{1,0:T(8,128)S(1)}, f32[8,256]{1,0:T(8,128)S(1)}, u32[]{:S(2)}, u32[]{:S(2)}) collective-permute-start(f32[8,256]{1,0:T(8,128)S(1)} %get-tuple-element.51.first), channel_id=1, source_target_pairs={{0,3},{1,2},{2,1},{3,0},{4,7},{5,6},{6,5},{7,4},{8,11},{9,10},{10,... | collective-permute-start | bytes 24584 | tf_op jit(solution)/shard_map/ppermute | solution.py:708
  17.1 1.5 %collective-permute-start.5 = (bf16[42,16,128]{2,1,0:T(8,128)(2,1)S(1)}, bf16[42,16,128]{2,1,0:T(8,128)(2,1)S(1)}, u32[]{:S(2)}, u32[]{:S(2)}) collective-permute-start(bf16[42,16,128]{2,1,0:T(8,128)(2,1)S(1)} %get-tuple-element.54.mine), channel_id=1, source_target_pairs={{0,1},{1,0},{2,3},{3,2},{4,5},{5,4},{6,7},{7,6},{8,9},{9,8},{10,11... | collective-permute-start | bytes 516104 | tf_op jit(solution)/shard_map/ppermute | solution.py:708
  19.1 7.2 %collective-permute-start.8 = (bf16[272,128]{1,0:T(8,128)(2,1)S(1)}, bf16[272,128]{1,0:T(8,128)(2,1)S(1)}, u32[]{:S(2)}, u32[]{:S(2)}) collective-permute-start(bf16[272,128]{1,0:T(8,128)(2,1)S(1)} %shard_map.93.refs_0_), channel_id=1, source_target_pairs={{0,8},{4,12},{8,0},{12,4},{1,9},{5,13},{9,1},{13,5},{2,10},{6,14},... | collective-permute-start | bytes 208904 | tf_op jit(solution)/shard_map/ppermute | solution.py:708
  20.4 6.5 %collective-permute-start.7 = (bf16[272,128]{1,0:T(8,128)(2,1)S(1)}, bf16[272,128]{1,0:T(8,128)(2,1)S(1)}, u32[]{:S(2)}, u32[]{:S(2)}) collective-permute-start(bf16[272,128]{1,0:T(8,128)(2,1)S(1)} %shard_map.93.refs_0_), channel_id=1, source_target_pairs={{0,12},{4,8},{8,4},{12,0},{1,13},{5,9},{9,5},{13,1},{2,14},{6,10},... | collective-permute-start | bytes 208904 | tf_op jit(solution)/shard_map/ppermute | solution.py:708
  21.3 6.8 %collective-permute-start.6 = (bf16[272,128]{1,0:T(8,128)(2,1)S(1)}, bf16[272,128]{1,0:T(8,128)(2,1)S(1)}, u32[]{:S(2)}, u32[]{:S(2)}) collective-permute-start(bf16[272,128]{1,0:T(8,128)(2,1)S(1)} %shard_map.93.refs_0_), channel_id=1, source_target_pairs={{0,4},{4,0},{8,12},{12,8},{1,5},{5,1},{9,13},{13,9},{2,6},{6,2},{1... | collective-permute-start | bytes 208904 | tf_op jit(solution)/shard_map/ppermute | solution.py:708
  29.1 1.6 %collective-permute-start.9 = (f32[584,128]{1,0:T(8,128)S(1)}, f32[584,128]{1,0:T(8,128)S(1)}, u32[]{:S(2)}, u32[]{:S(2)}) collective-permute-start(f32[584,128]{1,0:T(8,128)S(1)} %get-tuple-element.59), channel_id=1, source_target_pairs={{0,1},{1,0},{2,3},{3,2},{4,5},{5,4},{6,7},{7,6},{8,9},{9,8},{10,11... | collective-permute-start | bytes 897032 | tf_op jit(solution)/shard_map/ppermute | solution.py:708
  31.2 3.1 %collective-permute-start.10 = (f32[8,256]{1,0:T(8,128)S(1)}, f32[8,256]{1,0:T(8,128)S(1)}, u32[]{:S(2)}, u32[]{:S(2)}) collective-permute-start(f32[8,256]{1,0:T(8,128)S(1)} %get-tuple-element.64.first), channel_id=1, source_target_pairs={{0,3},{1,2},{2,1},{3,0},{4,7},{5,6},{6,5},{7,4},{8,11},{9,10},{10,... | collective-permute-start | bytes 24584 | tf_op jit(solution)/shard_map/ppermute | solution.py:708
  34.7 1.5 %collective-permute-start.11 = (bf16[42,16,128]{2,1,0:T(8,128)(2,1)S(1)}, bf16[42,16,128]{2,1,0:T(8,128)(2,1)S(1)}, u32[]{:S(2)}, u32[]{:S(2)}) collective-permute-start(bf16[42,16,128]{2,1,0:T(8,128)(2,1)S(1)} %get-tuple-element.67.mine), channel_id=1, source_target_pairs={{0,1},{1,0},{2,3},{3,2},{4,5},{5,4},{6,7},{7,6},{8,9},{9,8},{10,11... | collective-permute-start | bytes 516104 | tf_op jit(solution)/shard_map/ppermute | solution.py:708
  36.7 6.1 %collective-permute-start.12 = (f32[72,128]{1,0:T(8,128)S(1)}, f32[72,128]{1,0:T(8,128)S(1)}, u32[]{:S(2)}, u32[]{:S(2)}) collective-permute-start(f32[72,128]{1,0:T(8,128)S(1)} %get-tuple-element.68), channel_id=1, source_target_pairs={{0,12},{4,8},{8,4},{12,0},{1,13},{5,9},{9,5},{13,1},{2,14},{6,10},... | collective-permute-start | bytes 110600 | tf_op jit(solution)/shard_map/ppermute | solution.py:708
  39.0 4.9 %collective-permute-start.13 = (f32[72,128]{1,0:T(8,128)S(1)}, f32[72,128]{1,0:T(8,128)S(1)}, u32[]{:S(2)}, u32[]{:S(2)}) collective-permute-start(f32[72,128]{1,0:T(8,128)S(1)} %get-tuple-element.69), channel_id=1, source_target_pairs={{0,8},{4,12},{8,0},{12,4},{1,9},{5,13},{9,1},{13,5},{2,10},{6,14},... | collective-permute-start | bytes 110600 | tf_op jit(solution)/shard_map/ppermute | solution.py:708
  39.1 4.9 %collective-permute-start.14 = (f32[72,128]{1,0:T(8,128)S(1)}, f32[72,128]{1,0:T(8,128)S(1)}, u32[]{:S(2)}, u32[]{:S(2)}) collective-permute-start(f32[72,128]{1,0:T(8,128)S(1)} %get-tuple-element.70), channel_id=1, source_target_pairs={{0,4},{4,0},{8,12},{12,8},{1,5},{5,1},{9,13},{13,9},{2,6},{6,2},{1... | collective-permute-start | bytes 110600 | tf_op jit(solution)/shard_map/ppermute | solution.py:708

commit v25 on v24

--- a/solution.py
+++ b/solution.py
@@ -203,7 +203,7 @@
                 tree(tail[base + (k ^ i) : base + (k ^ i) + 1] for i, tail in enumerate(tails))
                 for base in (0, classes)
             ]
-            plain = (sums / (highs + lows + shrinkage)).astype(BF16).astype(F32)
+            plain = (sums * (1.0 / (highs + lows + shrinkage))).astype(BF16).astype(F32)
         weighted = (plain * doubled).astype(BF16).astype(F32)
         image[rows(2 * k * pitch, freqs), :] = weighted
         image[rows((2 * k + 1) * pitch, freqs), :] = sign * pltpu.roll(weighted, radii, 1)

time: 44.7 us -> 44.7 us (level)
  no operation moved by 1% of the time
where the time goes in v25:
time: 44.7 us; the launch traced here: 44.6 us
  waiting for transfers between devices  16.7 us (37%)
  starting transfers between devices  16.6 us (37%)
  Pallas kernels  10.5 us (23%)
  between operations  0.8 us (2%)
    ppermute x15, waiting for transfers between devices, swap(): return lax.ppermute(value, axis, [(i, i ^ bit) for i in range(size)])  16.7 us
    ppermute x15, starting transfers between devices, swap(): return lax.ppermute(value, axis, [(i, i ^ bit) for i in range(size)])  16.6 us
    pallas_call x15, Pallas kernels, call(): pl.pallas_call(kernel, out_shape=[jax.ShapeDtypeStruct(*x) for x in outs]...  10.5 us
  transfers between devices with their start and end apart: 15, of which 12 were waited for; matrix products, arithmetic and copies ran while one was open for 0% of the time, Pallas kernels for 11%

profile of v25, /device:TPU:0, one launch (start us, length us, event | category | flops | bytes accessed | tf_op | source)
XLA Modules:
  0.0 44.6 jit_solution(1580965312762184015)
XLA Ops:
  0.6 4.1 %collective-permute-start.1 = (bf16[1,64,128]{2,1,0:T(8,128)(2,1)}, bf16[1,64,128]{2,1,0:T(8,128)(2,1)S(1)}, u32[]{:S(2)}, u32[]{:S(2)}) collective-permute-start(bf16[1,64,128]{2,1,0:T(8,128)(2,1)} %refs_0_.1), channel_id=1, source_target_pairs={{0,8},{4,12},{8,0},{12,4},{1,9},{5,13},{9,1},{13,5},{2,10},{6,14},... | collective-permute-start | bytes 49160 | tf_op jit(solution)/shard_map/ppermute | solution.py:708
  4.8 1.3 %collective-permute-start = (bf16[1,64,128]{2,1,0:T(8,128)(2,1)}, bf16[1,64,128]{2,1,0:T(8,128)(2,1)S(1)}, u32[]{:S(2)}, u32[]{:S(2)}) collective-permute-start(bf16[1,64,128]{2,1,0:T(8,128)(2,1)} %refs_0_.1), channel_id=1, source_target_pairs={{0,12},{4,8},{8,4},{12,0},{1,13},{5,9},{9,5},{13,1},{2,14},{6,10},... | collective-permute-start | bytes 49160 | tf_op jit(solution)/shard_map/ppermute | solution.py:708
  6.4 1.4 %shard_map.87 = (bf16[32,144,256]{2,1,0:T(8,128)(2,1)S(1)}, bf16[32,144,256]{2,1,0:T(8,128)(2,1)S(1)}, f32[256,256]{1,0:T(8,128)S(1)}) custom-call(bf16[288,64,128]{2,1,0:T(8,128)(2,1)S(1)} %copy-done.4, bf16[256,256]{1,0:T(8,128)(2,1)S(1)} %shard_map.86.permutation_ref, s32[288]{0:T(512)S(1)} %copy-done.5), custom_call_target="tpu_custom_call" | custom-call | flops 2147483648 | bytes 9854976 | tf_op jit(solution)/shard_map/pallas_call | solution.py:78
  7.9 2.6 %collective-permute-done.refs_1_ = bf16[1,64,128]{2,1,0:T(8,128)(2,1)S(1)} collective-permute-done((bf16[1,64,128]{2,1,0:T(8,128)(2,1)}, bf16[1,64,128]{2,1,0:T(8,128)(2,1)S(1)}, u32[]{:S(2)}, u32[]{:S(2)}) %collective-permute-start) | collective-permute-done | bytes 16416 | tf_op jit(solution)/shard_map/ppermute | solution.py:708
  10.5 0.9 %shard_map.88 = (f32[584,128]{1,0:T(8,128)S(1)}, f32[4,128]{1,0:T(4,128)S(1)}, bf16[32,16,256]{2,1,0:T(8,128)(2,1)S(1)}) custom-call(bf16[1,64,128]{2,1,0:T(8,128)(2,1)S(1)} %copy-done.2, bf16[1,64,128]{2,1,0:T(8,128)(2,1)S(1)} %collective-permute-done.refs_1_, bf16[1,64,128]{2,1,0:T(8,128)(2,1)S(1)} %collective-permute-done.1.refs_2_, ...), custom_call_target="tpu_custom_call" | custom-call | flops 150994944 | bytes 3268608 | tf_op jit(solution)/shard_map/pallas_call | solution.py:78
  11.5 1.1 %shard_map.89 = (f32[2,256,256]{2,1,0:T(8,128)S(1)}, f32[1,256,128]{2,1,0:T(8,128)S(1)}) custom-call(bf16[32,16,256]{2,1,0:T(8,128)(2,1)S(1)} %get-tuple-element.40.left_ref, bf16[32,144,256]{2,1,0:T(8,128)(2,1)S(1)} %get-tuple-element.41.particles, f32[4,128]{1,0:T(4,128)S(1)} %get-tuple-element.42.energy_ref, f32[256,256]{1,0:T(8,128)S(1)} %get-tuple-element.43.prior_term, ...), custom_call_target="tpu_custom_call" | custom-call | flops 301989888 | bytes 4243456 | tf_op jit(solution)/shard_map/pallas_call | solution.py:78
  13.1 0.5 %shard_map.90 = (f32[2,256,256]{2,1,0:T(8,128)S(1)}, f32[1,256,128]{2,1,0:T(8,128)S(1)}, f32[2,256]{1,0:T(2,128)S(1)}, f32[1,128]{1,0:T(1,128)S(1)}, f32[8,256]{1,0:T(8,128)S(1)}) custom-call(f32[2,256,256]{2,1,0:T(8,128)S(1)} %get-tuple-element.44.partial, f32[1,256,128]{2,1,0:T(8,128)S(1)} %get-tuple-element.45.partial_more, ...), custom_call_target="tpu_custom_call" | custom-call | flops 402653184 | bytes 2048000 | tf_op jit(solution)/shard_map/pallas_call | solution.py:78
  13.6 1.3 %collective-permute-start.4 = (f32[8,256]{1,0:T(8,128)S(1)}, f32[8,256]{1,0:T(8,128)S(1)}, u32[]{:S(2)}, u32[]{:S(2)}) collective-permute-start(f32[8,256]{1,0:T(8,128)S(1)} %get-tuple-element.51.first), channel_id=1, source_target_pairs={{0,3},{1,2},{2,1},{3,0},{4,7},{5,6},{6,5},{7,4},{8,11},{9,10},{10,... | collective-permute-start | bytes 24584 | tf_op jit(solution)/shard_map/ppermute | solution.py:708
  14.9 1.8 %collective-permute-done.4.second = f32[8,256]{1,0:T(8,128)S(1)} collective-permute-done((f32[8,256]{1,0:T(8,128)S(1)}, f32[8,256]{1,0:T(8,128)S(1)}, u32[]{:S(2)}, u32[]{:S(2)}) %collective-permute-start.4) | collective-permute-done | bytes 8224 | tf_op jit(solution)/shard_map/ppermute | solution.py:708
  17.3 0.7 %shard_map.92.image = f32[512,128]{1,0:T(8,128)S(1)} custom-call(bf16[2,256,256]{2,1,0:T(8,128)(2,1)S(1)} %get-tuple-element.52.rounded_ref, bf16[1,256,128]{2,1,0:T(8,128)(2,1)S(1)} %get-tuple-element.53.rounded_more, bf16[512,512]{1,0:T(8,128)(2,1)S(1)} %copy-done, bf16[32,144,256]{2,1,0:T(8,128)(2,1)S(1)} %get-tuple-element.41.particles), custom_call_target="tpu_custom_call" | custom-call | flops 268435456 | bytes 3997696 | tf_op jit(solution)/shard_map/pallas_call | solution.py:78
  18.0 0.6 %collective-permute-done.5.spectrum = bf16[42,16,128]{2,1,0:T(8,128)(2,1)S(1)} collective-permute-done((bf16[42,16,128]{2,1,0:T(8,128)(2,1)S(1)}, bf16[42,16,128]{2,1,0:T(8,128)(2,1)S(1)}, u32[]{:S(2)}, u32[]{:S(2)}) %collective-permute-start.5) | collective-permute-done | bytes 172064 | tf_op jit(solution)/shard_map/ppermute | solution.py:708
  18.6 0.6 %shard_map.93.refs_0_ = bf16[272,128]{1,0:T(8,128)(2,1)S(1)} custom-call(f32[512,128]{1,0:T(8,128)S(1)} %shard_map.92.image, bf16[42,16,128]{2,1,0:T(8,128)(2,1)S(1)} %get-tuple-element.54.mine, bf16[42,16,128]{2,1,0:T(8,128)(2,1)S(1)} %collective-permute-done.5.spectrum, bf16[32,144,256]{2,1,0:T(8,128)(2,1)S(1)} %get-tuple-element.39.refs_5_.particles), custom_call_target="tpu_custom_call" | custom-call | flops 352321536 | bytes 3297280 | tf_op jit(solution)/shard_map/pallas_call | solution.py:78
  19.1 1.3 %collective-permute-start.8 = (bf16[272,128]{1,0:T(8,128)(2,1)S(1)}, bf16[272,128]{1,0:T(8,128)(2,1)S(1)}, u32[]{:S(2)}, u32[]{:S(2)}) collective-permute-start(bf16[272,128]{1,0:T(8,128)(2,1)S(1)} %shard_map.93.refs_0_), channel_id=1, source_target_pairs={{0,8},{4,12},{8,0},{12,4},{1,9},{5,13},{9,1},{13,5},{2,10},{6,14},... | collective-permute-start | bytes 208904 | tf_op jit(solution)/shard_map/ppermute | solution.py:708
  20.4 0.9 %collective-permute-start.7 = (bf16[272,128]{1,0:T(8,128)(2,1)S(1)}, bf16[272,128]{1,0:T(8,128)(2,1)S(1)}, u32[]{:S(2)}, u32[]{:S(2)}) collective-permute-start(bf16[272,128]{1,0:T(8,128)(2,1)S(1)} %shard_map.93.refs_0_), channel_id=1, source_target_pairs={{0,12},{4,8},{8,4},{12,0},{1,13},{5,9},{9,5},{13,1},{2,14},{6,10},... | collective-permute-start | bytes 208904 | tf_op jit(solution)/shard_map/ppermute | solution.py:708
  21.3 1.3 %collective-permute-start.6 = (bf16[272,128]{1,0:T(8,128)(2,1)S(1)}, bf16[272,128]{1,0:T(8,128)(2,1)S(1)}, u32[]{:S(2)}, u32[]{:S(2)}) collective-permute-start(bf16[272,128]{1,0:T(8,128)(2,1)S(1)} %shard_map.93.refs_0_), channel_id=1, source_target_pairs={{0,4},{4,0},{8,12},{12,8},{1,5},{5,1},{9,13},{13,9},{2,6},{6,2},{1... | collective-permute-start | bytes 208904 | tf_op jit(solution)/shard_map/ppermute | solution.py:708
  22.7 3.6 %collective-permute-done.8.refs_3_ = bf16[272,128]{1,0:T(8,128)(2,1)S(1)} collective-permute-done((bf16[272,128]{1,0:T(8,128)(2,1)S(1)}, bf16[272,128]{1,0:T(8,128)(2,1)S(1)}, u32[]{:S(2)}, u32[]{:S(2)}) %collective-permute-start.8) | collective-permute-done | bytes 69664 | tf_op jit(solution)/shard_map/ppermute | solution.py:708
  26.3 0.6 %collective-permute-done.7.refs_2_ = bf16[272,128]{1,0:T(8,128)(2,1)S(1)} collective-permute-done((bf16[272,128]{1,0:T(8,128)(2,1)S(1)}, bf16[272,128]{1,0:T(8,128)(2,1)S(1)}, u32[]{:S(2)}, u32[]{:S(2)}) %collective-permute-start.7) | collective-permute-done | bytes 69664 | tf_op jit(solution)/shard_map/ppermute | solution.py:708
  27.0 1.2 %collective-permute-done.6.refs_1_ = bf16[272,128]{1,0:T(8,128)(2,1)S(1)} collective-permute-done((bf16[272,128]{1,0:T(8,128)(2,1)S(1)}, bf16[272,128]{1,0:T(8,128)(2,1)S(1)}, u32[]{:S(2)}, u32[]{:S(2)}) %collective-permute-start.6) | collective-permute-done | bytes 69664 | tf_op jit(solution)/shard_map/ppermute | solution.py:708
  28.1 0.9 %shard_map.94 = (f32[584,128]{1,0:T(8,128)S(1)}, f32[4,128]{1,0:T(4,128)S(1)}, bf16[32,16,256]{2,1,0:T(8,128)(2,1)S(1)}) custom-call(bf16[272,128]{1,0:T(8,128)(2,1)S(1)} %shard_map.93.refs_0_, bf16[272,128]{1,0:T(8,128)(2,1)S(1)} %collective-permute-done.6.refs_1_, bf16[272,128]{1,0:T(8,128)(2,1)S(1)} %collective-permute-done.7.refs_2_, ...), custom_call_target="tpu_custom_call" | custom-call | flops 150994944 | bytes 3481600 | tf_op jit(solution)/shard_map/pallas_call | solution.py:78
  29.1 1.1 %shard_map.95 = (f32[2,256,256]{2,1,0:T(8,128)S(1)}, f32[1,256,128]{2,1,0:T(8,128)S(1)}) custom-call(bf16[32,16,256]{2,1,0:T(8,128)(2,1)S(1)} %get-tuple-element.55.left_ref, bf16[32,144,256]{2,1,0:T(8,128)(2,1)S(1)} %get-tuple-element.41.particles, f32[4,128]{1,0:T(4,128)S(1)} %get-tuple-element.56.energy_ref, f32[256,256]{1,0:T(8,128)S(1)} %get-tuple-element.43.prior_term, ...), custom_call_target="tpu_custom_call" | custom-call | flops 301989888 | bytes 4243456 | tf_op jit(solution)/shard_map/pallas_call | solution.py:78
  30.2 0.5 %collective-permute-done.9.other = f32[584,128]{1,0:T(8,128)S(1)} collective-permute-done((f32[584,128]{1,0:T(8,128)S(1)}, f32[584,128]{1,0:T(8,128)S(1)}, u32[]{:S(2)}, u32[]{:S(2)}) %collective-permute-start.9) | collective-permute-done | bytes 299040 | tf_op jit(solution)/shard_map/ppermute | solution.py:708
  30.7 0.5 %shard_map.96 = (f32[2,256,256]{2,1,0:T(8,128)S(1)}, f32[1,256,128]{2,1,0:T(8,128)S(1)}, f32[2,256]{1,0:T(2,128)S(1)}, f32[1,128]{1,0:T(1,128)S(1)}, f32[8,256]{1,0:T(8,128)S(1)}) custom-call(f32[2,256,256]{2,1,0:T(8,128)S(1)} %get-tuple-element.57.partial, f32[1,256,128]{2,1,0:T(8,128)S(1)} %get-tuple-element.58.partial_more, ...), custom_call_target="tpu_custom_call" | custom-call | flops 402653184 | bytes 2048000 | tf_op jit(solution)/shard_map/pallas_call | solution.py:78
  31.2 1.3 %collective-permute-start.10 = (f32[8,256]{1,0:T(8,128)S(1)}, f32[8,256]{1,0:T(8,128)S(1)}, u32[]{:S(2)}, u32[]{:S(2)}) collective-permute-start(f32[8,256]{1,0:T(8,128)S(1)} %get-tuple-element.64.first), channel_id=1, source_target_pairs={{0,3},{1,2},{2,1},{3,0},{4,7},{5,6},{6,5},{7,4},{8,11},{9,10},{10,... | collective-permute-start | bytes 24584 | tf_op jit(solution)/shard_map/ppermute | solution.py:708
  32.5 1.8 %collective-permute-done.10.second = f32[8,256]{1,0:T(8,128)S(1)} collective-permute-done((f32[8,256]{1,0:T(8,128)S(1)}, f32[8,256]{1,0:T(8,128)S(1)}, u32[]{:S(2)}, u32[]{:S(2)}) %collective-permute-start.10) | collective-permute-done | bytes 8224 | tf_op jit(solution)/shard_map/ppermute | solution.py:708
  34.9 0.7 %shard_map.98.image = f32[512,128]{1,0:T(8,128)S(1)} custom-call(bf16[2,256,256]{2,1,0:T(8,128)(2,1)S(1)} %get-tuple-element.65.rounded_ref, bf16[1,256,128]{2,1,0:T(8,128)(2,1)S(1)} %get-tuple-element.66.rounded_more, bf16[512,512]{1,0:T(8,128)(2,1)S(1)} %copy-done, bf16[32,144,256]{2,1,0:T(8,128)(2,1)S(1)} %get-tuple-element.41.particles), custom_call_target="tpu_custom_call" | custom-call | flops 268435456 | bytes 3997696 | tf_op jit(solution)/shard_map/pallas_call | solution.py:78
  35.6 0.6 %collective-permute-done.11.spectrum = bf16[42,16,128]{2,1,0:T(8,128)(2,1)S(1)} collective-permute-done((bf16[42,16,128]{2,1,0:T(8,128)(2,1)S(1)}, bf16[42,16,128]{2,1,0:T(8,128)(2,1)S(1)}, u32[]{:S(2)}, u32[]{:S(2)}) %collective-permute-start.11) | collective-permute-done | bytes 172064 | tf_op jit(solution)/shard_map/ppermute | solution.py:708
  36.2 0.6 %shard_map.99 = (f32[72,128]{1,0:T(8,128)S(1)}, f32[72,128]{1,0:T(8,128)S(1)}, f32[72,128]{1,0:T(8,128)S(1)}, f32[72,128]{1,0:T(8,128)S(1)}, f32[1,144]{1,0:T(1,128)S(1)}) custom-call(f32[512,128]{1,0:T(8,128)S(1)} %shard_map.98.image, bf16[42,16,128]{2,1,0:T(8,128)(2,1)S(1)} %get-tuple-element.67.mine, ...), custom_call_target="tpu_custom_call" | custom-call | flops 352321536 | bytes 3407872 | tf_op jit(solution)/shard_map/pallas_call | solution.py:78
  36.7 2.3 %collective-permute-start.12 = (f32[72,128]{1,0:T(8,128)S(1)}, f32[72,128]{1,0:T(8,128)S(1)}, u32[]{:S(2)}, u32[]{:S(2)}) collective-permute-start(f32[72,128]{1,0:T(8,128)S(1)} %get-tuple-element.68), channel_id=1, source_target_pairs={{0,12},{4,8},{8,4},{12,0},{1,13},{5,9},{9,5},{13,1},{2,14},{6,10},... | collective-permute-start | bytes 110600 | tf_op jit(solution)/shard_map/ppermute | solution.py:708
  39.1 2.1 %collective-permute-start.14 = (f32[72,128]{1,0:T(8,128)S(1)}, f32[72,128]{1,0:T(8,128)S(1)}, u32[]{:S(2)}, u32[]{:S(2)}) collective-permute-start(f32[72,128]{1,0:T(8,128)S(1)} %get-tuple-element.70), channel_id=1, source_target_pairs={{0,4},{4,0},{8,12},{12,8},{1,5},{5,1},{9,13},{13,9},{2,6},{6,2},{1... | collective-permute-start | bytes 110600 | tf_op jit(solution)/shard_map/ppermute | solution.py:708
  41.2 1.6 %collective-permute-done.12.refs_0_ = f32[72,128]{1,0:T(8,128)S(1)} collective-permute-done((f32[72,128]{1,0:T(8,128)S(1)}, f32[72,128]{1,0:T(8,128)S(1)}, u32[]{:S(2)}, u32[]{:S(2)}) %collective-permute-start.12) | collective-permute-done | bytes 36896 | tf_op jit(solution)/shard_map/ppermute | solution.py:708
  42.8 1.1 %collective-permute-done.13.refs_1_ = f32[72,128]{1,0:T(8,128)S(1)} collective-permute-done((f32[72,128]{1,0:T(8,128)S(1)}, f32[72,128]{1,0:T(8,128)S(1)}, u32[]{:S(2)}, u32[]{:S(2)}) %collective-permute-start.13) | collective-permute-done | bytes 36896 | tf_op jit(solution)/shard_map/ppermute | solution.py:708
  44.0 0.6 %shard_map.100 = (f32[1,64,128]{2,1,0:T(8,128)}, f32[1,144]{1,0:T(1,128)}) custom-call(f32[72,128]{1,0:T(8,128)S(1)} %collective-permute-done.12.refs_0_, f32[72,128]{1,0:T(8,128)S(1)} %collective-permute-done.13.refs_1_, f32[72,128]{1,0:T(8,128)S(1)} %collective-permute-done.14.refs_2_, f32[72,128]{1,0:T(8,128)S(1)} %get-tuple-element.71.refs_3_, ...), custom_call_target="tpu_custom_call" | custom-call | bytes 245760 | tf_op jit(solution)/shard_map/pallas_call | solution.py:78
  (27 shorter events, 2.0 us)
Async XLA Ops:
  0.6 5.8 %copy-start.5 = (s32[288]{0:T(512)S(1)}, s32[288]{0:T(512)}, u32[]{:S(2)}) copy-start(s32[288]{0:T(512)} %prior_ref.1) | copy-start | bytes 3460
  0.6 5.8 %copy-start.4 = (bf16[288,64,128]{2,1,0:T(8,128)(2,1)S(1)}, bf16[288,64,128]{2,1,0:T(8,128)(2,1)}, u32[]{:S(2)}) copy-start(bf16[288,64,128]{2,1,0:T(8,128)(2,1)} %particles_ref.1) | copy-start | bytes 14155780
  0.6 7.2 %collective-permute-start.1 = (bf16[1,64,128]{2,1,0:T(8,128)(2,1)}, bf16[1,64,128]{2,1,0:T(8,128)(2,1)S(1)}, u32[]{:S(2)}, u32[]{:S(2)}) collective-permute-start(bf16[1,64,128]{2,1,0:T(8,128)(2,1)} %refs_0_.1), channel_id=1, source_target_pairs={{0,8},{4,12},{8,0},{12,4},{1,9},{5,13},{9,1},{13,5},{2,10},{6,14},... | collective-permute-start | bytes 49160 | tf_op jit(solution)/shard_map/ppermute | solution.py:708
  4.8 5.7 %collective-permute-start = (bf16[1,64,128]{2,1,0:T(8,128)(2,1)}, bf16[1,64,128]{2,1,0:T(8,128)(2,1)S(1)}, u32[]{:S(2)}, u32[]{:S(2)}) collective-permute-start(bf16[1,64,128]{2,1,0:T(8,128)(2,1)} %refs_0_.1), channel_id=1, source_target_pairs={{0,12},{4,8},{8,4},{12,0},{1,13},{5,9},{9,5},{13,1},{2,14},{6,10},... | collective-permute-start | bytes 49160 | tf_op jit(solution)/shard_map/ppermute | solution.py:708
  6.1 4.4 %collective-permute-start.2 = (bf16[1,64,128]{2,1,0:T(8,128)(2,1)}, bf16[1,64,128]{2,1,0:T(8,128)(2,1)S(1)}, u32[]{:S(2)}, u32[]{:S(2)}) collective-permute-start(bf16[1,64,128]{2,1,0:T(8,128)(2,1)} %refs_0_.1), channel_id=1, source_target_pairs={{0,4},{4,0},{8,12},{12,8},{1,5},{5,1},{9,13},{13,9},{2,6},{6,2},{1... | collective-permute-start | bytes 49160 | tf_op jit(solution)/shard_map/ppermute | solution.py:708
  6.4 4.1 %copy-start.2 = (bf16[1,64,128]{2,1,0:T(8,128)(2,1)S(1)}, bf16[1,64,128]{2,1,0:T(8,128)(2,1)}, u32[]{:S(2)}) copy-start(bf16[1,64,128]{2,1,0:T(8,128)(2,1)} %refs_0_.1) | copy-start | bytes 49156
  6.4 4.1 %copy-start.3 = (f32[64]{0:T(128)S(1)}, f32[64]{0:T(128)}, u32[]{:S(2)}) copy-start(f32[64]{0:T(128)} %param.9) | copy-start | bytes 772
  7.9 3.6 %copy-start.1 = (bf16[512,384]{1,0:T(8,128)(2,1)S(1)}, bf16[512,384]{1,0:T(8,128)(2,1)}, u32[]{:S(2)}) copy-start(bf16[512,384]{1,0:T(8,128)(2,1)} %constant.6.clone.table) | copy-start | bytes 1179652
  10.5 2.6 %copy-start.6 = (bf16[512,384]{1,0:T(8,128)(2,1)S(1)}, bf16[512,384]{1,0:T(8,128)(2,1)}, u32[]{:S(2)}) copy-start(bf16[512,384]{1,0:T(8,128)(2,1)} %constant.7.clone.table) | copy-start | bytes 1179652
  11.5 1.6 %collective-permute-start.3 = (f32[584,128]{1,0:T(8,128)S(1)}, f32[584,128]{1,0:T(8,128)S(1)}, u32[]{:S(2)}, u32[]{:S(2)}) collective-permute-start(f32[584,128]{1,0:T(8,128)S(1)} %get-tuple-element.46), channel_id=1, source_target_pairs={{0,1},{1,0},{2,3},{3,2},{4,5},{5,4},{6,7},{7,6},{8,9},{9,8},{10,11... | collective-permute-start | bytes 897032 | tf_op jit(solution)/shard_map/ppermute | solution.py:708
  11.5 5.2 %copy-start = (bf16[512,512]{1,0:T(8,128)(2,1)S(1)}, bf16[512,512]{1,0:T(8,128)(2,1)}, u32[]{:S(2)}) copy-start(bf16[512,512]{1,0:T(8,128)(2,1)} %constant.8.clone.forward) | copy-start | bytes 1572868
  13.6 3.1 %collective-permute-start.4 = (f32[8,256]{1,0:T(8,128)S(1)}, f32[8,256]{1,0:T(8,128)S(1)}, u32[]{:S(2)}, u32[]{:S(2)}) collective-permute-start(f32[8,256]{1,0:T(8,128)S(1)} %get-tuple-element.51.first), channel_id=1, source_target_pairs={{0,3},{1,2},{2,1},{3,0},{4,7},{5,6},{6,5},{7,4},{8,11},{9,10},{10,... | collective-permute-start | bytes 24584 | tf_op jit(solution)/shard_map/ppermute | solution.py:708
  17.1 1.5 %collective-permute-start.5 = (bf16[42,16,128]{2,1,0:T(8,128)(2,1)S(1)}, bf16[42,16,128]{2,1,0:T(8,128)(2,1)S(1)}, u32[]{:S(2)}, u32[]{:S(2)}) collective-permute-start(bf16[42,16,128]{2,1,0:T(8,128)(2,1)S(1)} %get-tuple-element.54.mine), channel_id=1, source_target_pairs={{0,1},{1,0},{2,3},{3,2},{4,5},{5,4},{6,7},{7,6},{8,9},{9,8},{10,11... | collective-permute-start | bytes 516104 | tf_op jit(solution)/shard_map/ppermute | solution.py:708
  19.1 7.2 %collective-permute-start.8 = (bf16[272,128]{1,0:T(8,128)(2,1)S(1)}, bf16[272,128]{1,0:T(8,128)(2,1)S(1)}, u32[]{:S(2)}, u32[]{:S(2)}) collective-permute-start(bf16[272,128]{1,0:T(8,128)(2,1)S(1)} %shard_map.93.refs_0_), channel_id=1, source_target_pairs={{0,8},{4,12},{8,0},{12,4},{1,9},{5,13},{9,1},{13,5},{2,10},{6,14},... | collective-permute-start | bytes 208904 | tf_op jit(solution)/shard_map/ppermute | solution.py:708
  20.4 6.5 %collective-permute-start.7 = (bf16[272,128]{1,0:T(8,128)(2,1)S(1)}, bf16[272,128]{1,0:T(8,128)(2,1)S(1)}, u32[]{:S(2)}, u32[]{:S(2)}) collective-permute-start(bf16[272,128]{1,0:T(8,128)(2,1)S(1)} %shard_map.93.refs_0_), channel_id=1, source_target_pairs={{0,12},{4,8},{8,4},{12,0},{1,13},{5,9},{9,5},{13,1},{2,14},{6,10},... | collective-permute-start | bytes 208904 | tf_op jit(solution)/shard_map/ppermute | solution.py:708
  21.3 6.8 %collective-permute-start.6 = (bf16[272,128]{1,0:T(8,128)(2,1)S(1)}, bf16[272,128]{1,0:T(8,128)(2,1)S(1)}, u32[]{:S(2)}, u32[]{:S(2)}) collective-permute-start(bf16[272,128]{1,0:T(8,128)(2,1)S(1)} %shard_map.93.refs_0_), channel_id=1, source_target_pairs={{0,4},{4,0},{8,12},{12,8},{1,5},{5,1},{9,13},{13,9},{2,6},{6,2},{1... | collective-permute-start | bytes 208904 | tf_op jit(solution)/shard_map/ppermute | solution.py:708
  29.1 1.6 %collective-permute-start.9 = (f32[584,128]{1,0:T(8,128)S(1)}, f32[584,128]{1,0:T(8,128)S(1)}, u32[]{:S(2)}, u32[]{:S(2)}) collective-permute-start(f32[584,128]{1,0:T(8,128)S(1)} %get-tuple-element.59), channel_id=1, source_target_pairs={{0,1},{1,0},{2,3},{3,2},{4,5},{5,4},{6,7},{7,6},{8,9},{9,8},{10,11... | collective-permute-start | bytes 897032 | tf_op jit(solution)/shard_map/ppermute | solution.py:708
  31.2 3.1 %collective-permute-start.10 = (f32[8,256]{1,0:T(8,128)S(1)}, f32[8,256]{1,0:T(8,128)S(1)}, u32[]{:S(2)}, u32[]{:S(2)}) collective-permute-start(f32[8,256]{1,0:T(8,128)S(1)} %get-tuple-element.64.first), channel_id=1, source_target_pairs={{0,3},{1,2},{2,1},{3,0},{4,7},{5,6},{6,5},{7,4},{8,11},{9,10},{10,... | collective-permute-start | bytes 24584 | tf_op jit(solution)/shard_map/ppermute | solution.py:708
  34.7 1.5 %collective-permute-start.11 = (bf16[42,16,128]{2,1,0:T(8,128)(2,1)S(1)}, bf16[42,16,128]{2,1,0:T(8,128)(2,1)S(1)}, u32[]{:S(2)}, u32[]{:S(2)}) collective-permute-start(bf16[42,16,128]{2,1,0:T(8,128)(2,1)S(1)} %get-tuple-element.67.mine), channel_id=1, source_target_pairs={{0,1},{1,0},{2,3},{3,2},{4,5},{5,4},{6,7},{7,6},{8,9},{9,8},{10,11... | collective-permute-start | bytes 516104 | tf_op jit(solution)/shard_map/ppermute | solution.py:708
  36.7 6.1 %collective-permute-start.12 = (f32[72,128]{1,0:T(8,128)S(1)}, f32[72,128]{1,0:T(8,128)S(1)}, u32[]{:S(2)}, u32[]{:S(2)}) collective-permute-start(f32[72,128]{1,0:T(8,128)S(1)} %get-tuple-element.68), channel_id=1, source_target_pairs={{0,12},{4,8},{8,4},{12,0},{1,13},{5,9},{9,5},{13,1},{2,14},{6,10},... | collective-permute-start | bytes 110600 | tf_op jit(solution)/shard_map/ppermute | solution.py:708
  39.0 4.9 %collective-permute-start.13 = (f32[72,128]{1,0:T(8,128)S(1)}, f32[72,128]{1,0:T(8,128)S(1)}, u32[]{:S(2)}, u32[]{:S(2)}) collective-permute-start(f32[72,128]{1,0:T(8,128)S(1)} %get-tuple-element.69), channel_id=1, source_target_pairs={{0,8},{4,12},{8,0},{12,4},{1,9},{5,13},{9,1},{13,5},{2,10},{6,14},... | collective-permute-start | bytes 110600 | tf_op jit(solution)/shard_map/ppermute | solution.py:708
  39.1 4.9 %collective-permute-start.14 = (f32[72,128]{1,0:T(8,128)S(1)}, f32[72,128]{1,0:T(8,128)S(1)}, u32[]{:S(2)}, u32[]{:S(2)}) collective-permute-start(f32[72,128]{1,0:T(8,128)S(1)} %get-tuple-element.70), channel_id=1, source_target_pairs={{0,4},{4,0},{8,12},{12,8},{1,5},{5,1},{9,13},{13,9},{2,6},{6,2},{1... | collective-permute-start | bytes 110600 | tf_op jit(solution)/shard_map/ppermute | solution.py:708
